TPU v7x, 512 devices: a whole 4x8x8 slice. The times are simulated.
512 devices in a mesh: dp: 32 (over y_hi, x, core), blk: 16 (over z, y_lo).
Axes of the slice: x: 4, y: 8 (y_hi: 4, y_lo: 2; y = y_hi * 2 + y_lo), z: 8, core: 2. Of those that a mesh axis runs over, the one named last changes fastest.
Arguments:
- tokens: bfloat16 [6144, 4096], P(('dp', 'blk')), may hold values from -6 to 6
- sequence_labels: int32 [512, 12], P(('dp', 'blk')), may hold values from 0 to 3, never falling along the last dimension, each value on 1 to 6 neighbouring positions
- response_mask: int32 [512, 12], P(('dp', 'blk')), may hold values 0 or 1
- frozen_gate_up: bfloat16 [2, 4096, 14336], P(None, 'dp', 'blk'), may hold values from -0.09375 to 0.09375
- adapter_down_maps: bfloat16 [4096, 32], replicated, may hold values from -0.09375 to 0.09375
- adapter_up_maps: bfloat16 [32, 14336], P(None, 'blk'), may hold values from -0.59765625 to 0.59765625
- readout: bfloat16 [14336], P('blk'), may hold values from -0.046875 to 0.046875
Outputs:
- dpo_loss: float32 [], replicated
- grad_a: float32 [4096, 32], P('dp')
- grad_b: float32 [32, 14336], P('dp', 'blk')
Inputs may be any that keep to these rules, and one draw needn't show every extreme that they name: `sequence_labels`: within each block the sequence numbers never fall; every number of 0 to 3 covers 1 to 6 rows, one exactly 6.
All inputs are finite; a program needn't handle non-finite values. No bound on the sum of `response_mask` on one device may be relied on, other than what follows from the above.
Results may differ from a plain program's by a relative error of at most 0.0033.
Values may be sent and summed in bfloat16 or wider, within the bound.
No kernel may reach another device: no remote copies, remote signals or barrier semaphores. Data moves between devices by JAX's collectives and lax.ppermute only.
A program may use at most 64 MiB of HBM per device.

v0:
```python
import jax
import jax.numpy as jnp
from jax import lax
from jax.sharding import PartitionSpec as P

SEQS = 4


dpo_beta = 0.1
loss_scale = 1024.0
highest = lax.Precision.HIGHEST


def finish_terms(gate_ref, up_ref, low_part, gate_adapter_up, up_adapter_rows, readout_f):
    low_rank_output = gate_adapter_up.shape[0]
    gate_pol = gate_ref + jnp.dot(
        low_part[:, :low_rank_output], gate_adapter_up, preferred_element_type=jnp.float32
    )
    up_pol = up_ref + jnp.dot(
        low_part[:, low_rank_output:], up_adapter_rows, preferred_element_type=jnp.float32
    )
    sig_ref = jax.nn.sigmoid(gate_ref)
    sig_pol = jax.nn.sigmoid(gate_pol)
    score_ref = jnp.dot(gate_ref * sig_ref * up_ref, readout_f, precision=highest)
    score_pol = jnp.dot(gate_pol * sig_pol * up_pol, readout_f, precision=highest)
    k_gate = readout_f * sig_pol * (1.0 + gate_pol * (1.0 - sig_pol)) * up_pol
    k_up = readout_f * gate_pol * sig_pol
    mixed_terms = jnp.concatenate(
        [
            jnp.dot(k_gate, gate_adapter_up.astype(jnp.float32).T, precision=highest),
            jnp.dot(k_up, up_adapter_rows.astype(jnp.float32).T, precision=highest),
        ],
        axis=1,
    )
    return (jnp.stack([score_ref, score_pol], axis=1), mixed_terms, k_gate, k_up)


def pair_margins(scores, sequence_labels, response_mask):
    block_total, row_count = sequence_labels.shape
    onehot = (
        (sequence_labels[:, :, None] == jnp.arange(SEQS, dtype=jnp.int32)[None, None, :])
        & (response_mask[:, :, None] > 0)
    ).astype(jnp.float32)
    seq_sums = jnp.einsum(
        "brs,brk->bsk", onehot, scores.reshape(block_total, row_count, 2), precision=highest
    )
    filled = jnp.sum(onehot, axis=1)
    change = seq_sums[:, :, 1] - seq_sums[:, :, 0]
    margin_gap = change[:, 0::2] - change[:, 1::2]
    pair_valid = ((filled[:, 0::2] > 0.5) & (filled[:, 1::2] > 0.5)).astype(jnp.float32)
    return (margin_gap, pair_valid, onehot)


def row_cotangents(scaled, onehot):
    block_total = scaled.shape[0]
    signed = jnp.stack([scaled, -scaled], axis=2).reshape(block_total, -1)
    return jnp.einsum("brs,bs->br", onehot, signed, precision=highest)


def close_pairs(margin_gap, pair_valid, total_sum):
    logit_arg = dpo_beta * margin_gap
    count_sum, log_total = total_sum(
        jnp.sum(pair_valid), jnp.sum(pair_valid * jax.nn.log_sigmoid(logit_arg))
    )
    pair_total = jnp.maximum(count_sum, 1.0)
    dpo_loss = -log_total / pair_total
    scaled = -loss_scale * dpo_beta * pair_valid * jax.nn.sigmoid(-logit_arg) / pair_total
    return (dpo_loss, scaled)


def wide_total(left_term, right_term):
    return lax.psum((left_term, right_term), ("dp", "blk"))


def on_device(
    tokens,
    sequence_labels,
    response_mask,
    frozen_gate_up,
    adapter_down_maps,
    adapter_up_maps,
    readout,
):
    low_rank_output = adapter_down_maps.shape[1] // 2
    input_low_rank = jnp.dot(tokens, adapter_down_maps, preferred_element_type=jnp.float32).astype(
        jnp.bfloat16
    )
    gate_adapter_up = adapter_up_maps[:low_rank_output]
    up_adapter_rows = adapter_up_maps[low_rank_output:]
    readout_f = readout.astype(jnp.float32)
    group_tokens, low_all = (
        lax.all_gather(tokens, "blk", axis=0, tiled=True),
        lax.all_gather(input_low_rank, "blk", axis=0, tiled=True),
    )
    piece = lax.all_gather(frozen_gate_up, "dp", axis=1, tiled=True)
    gate_acc = jnp.dot(group_tokens, piece[0], preferred_element_type=jnp.float32)
    up_acc = jnp.dot(group_tokens, piece[1], preferred_element_type=jnp.float32)
    scores, mixed_terms, gate_all, up_all = finish_terms(
        gate_acc, up_acc, low_all, gate_adapter_up, up_adapter_rows, readout_f
    )
    scores_own, own_mixed = (
        lax.psum_scatter(scores, "blk", scatter_dimension=0, tiled=True),
        lax.psum_scatter(mixed_terms, "blk", scatter_dimension=0, tiled=True),
    )
    margin_gap, pair_valid, onehot = pair_margins(scores_own, sequence_labels, response_mask)
    dpo_loss, scaled = close_pairs(margin_gap, pair_valid, wide_total)
    cotangent = row_cotangents(scaled, onehot)[0]
    cot_all = lax.all_gather(cotangent, "blk", axis=0, tiled=True)
    weighted = low_all.astype(jnp.float32) * cot_all[:, None]
    grad_b_part = jnp.concatenate(
        [
            jnp.dot(weighted[:, :low_rank_output].T, gate_all, precision=highest),
            jnp.dot(weighted[:, low_rank_output:].T, up_all, precision=highest),
        ],
        axis=0,
    )
    projected = (cotangent[:, None] * own_mixed).astype(jnp.bfloat16)
    grad_a_part = jnp.dot(tokens.T, projected, preferred_element_type=jnp.float32)
    grad_a_rows = lax.psum_scatter(grad_a_part, "dp", scatter_dimension=0, tiled=True)
    grad_a = lax.psum(grad_a_rows, "blk")
    grad_b = lax.psum_scatter(grad_b_part, "dp", scatter_dimension=0, tiled=True)
    return (dpo_loss, grad_a, grad_b)


def solution(mesh):
    in_specs = (
        P(("dp", "blk"), None),
        P(("dp", "blk"), None),
        P(("dp", "blk"), None),
        P(None, "dp", "blk"),
        P(),
        P(None, "blk"),
        P("blk"),
    )
    out_specs = (P(), P("dp", None), P("dp", "blk"))
    return jax.shard_map(
        on_device, mesh=mesh, in_specs=in_specs, out_specs=out_specs, check_vma=False
    )
```

profile of v0, /device:TPU:1, one launch (start us, length us, event | category | flops | bytes accessed | tf_op | source)
XLA Modules:
  0.0 831.9 jit_solution(15246500416958862492)
XLA Ops:
  7.2 0.7 all-gather.7.cloned.1.call-update
  8.0 0.7 all-gather.5.cloned.1.call-update
  8.7 0.7 compare_bitcast_fusion
  9.4 0.8 convert_reduce_fusion
  10.3 0.7 reshape.217
  11.0 0.7 convert_element_type.31
  11.7 1.1 fusion.3
  12.8 34.7 %all-gather.1 = bf16[16,12,32]{2,1,0:T(8,128)(2,1)S(1)} all-gather(bf16[1,12,32]{2,1,0:T(8,128)(2,1)S(1)} %fusion.3), channel_id=1, replica_groups=mesh['dp'=32,'blk'=16] {'blk'}, dimensions={0}, use_global_device_ids=true | all-gather | bytes 13056 | tf_op jit(solution)/shard_map/all_gather | solution.py:93
  47.5 1.4 fusion.51
  50.2 35.2 %all-gather.7.cloned.1.call-done = bf16[16,12,4096]{2,1,0:T(8,128)(2,1)} async-done(((bf16[1,12,4096]{2,1,0:T(8,128)(2,1)}), bf16[16,12,4096]{2,1,0:T(8,128)(2,1)}) %all-gather.7.cloned.1.call-update) | async-done | bytes 1572880 | tf_op jit(solution)/shard_map/all_gather | solution.py:92
  85.4 2.5 reshape.212
  87.9 122.3 %all-gather.5.cloned.1.call-done = bf16[2,4096,896]{2,1,0:T(8,128)(2,1)} async-done(((bf16[2,128,896]{2,1,0:T(8,128)(2,1)}), bf16[2,4096,896]{2,1,0:T(8,128)(2,1)}) %all-gather.5.cloned.1.call-update) | async-done | bytes 14680080 | tf_op jit(solution)/shard_map/all_gather | solution.py:95
  210.2 5.0 fusion.2
  216.0 1.4 copy-done.3
  217.4 1.8 fusion.1
  220.3 0.6 convolution_bitcast_fusion.2
  221.0 28.7 %all-reduce.1 = f32[192,2]{0,1:T(2,128)S(1)} all-reduce(f32[192,2]{0,1:T(2,128)S(1)} %pad_maximum_fusion.2), channel_id=2, replica_groups=mesh['dp'=32,'blk'=16] {'blk'}, use_global_device_ids=true, to_apply=%region_1.0.clone | all-reduce | flops 384 | bytes 3072
  250.7 25.7 %fusion = f32[16,32]{1,0:T(8,128)S(1)} fusion(f32[192,32]{1,0:T(8,128)S(1)} %copy.15), kind=kCustom, calls=%all-reduce-scatter | all-reduce-scatter fusion | flops 8193 | bytes 28672
  276.4 1.3 collective-permute-start.2
  277.7 2.7 collective-permute-start.1
  280.3 3.5 collective-permute-start
  284.4 113.4 %all-reduce.5 = (f32[]{:T(128)}, f32[]{:T(128)}) all-reduce(f32[]{:T(128)} %get-tuple-element.4, f32[]{:T(128)} %get-tuple-element.3), channel_id=1, replica_groups=mesh['dp'=32,'blk'=16] {'dp','blk'}, use_global_device_ids=true, to_apply=%region_3.0 | all-reduce | flops 2 | bytes 16 | tf_op jit(solution)/shard_map/psum | solution.py:72
  398.7 1.9 collective-permute-start.3
  400.7 0.7 collective-permute-done.3
  401.9 1.1 convolution_bitcast_fusion
  403.9 91.7 %reduce-scatter.5.cloned.1.call-done = f32[128,32]{0,1:T(8,128)} async-done(((f32[4096,32]{0,1:T(8,128)}), f32[128,32]{0,1:T(8,128)}) %reduce-scatter.5.cloned.1.call-update) | async-done | bytes 16400 | tf_op jit(solution)/shard_map/reduce_scatter | solution.py:119
  495.6 49.8 %all-reduce.6 = (f32[128,32]{0,1:T(8,128)}, f32[192]{0:T(256)S(1)}) all-reduce(f32[128,32]{0,1:T(8,128)} %reduce-scatter.5.cloned.1.call-done, f32[192]{0:T(256)S(1)} %dynamic-update-slice), channel_id=1, replica_groups=mesh['dp'=32,'blk'=16] {'blk'}, use_global_device_ids=true, to_apply=%region_8.9 | all-reduce | flops 4288 | bytes 34304 | tf_op jit(solution)/shard_map/psum | solution.py:120
  545.5 0.7 fusion.14
  546.7 0.7 pad_maximum_fusion
  547.4 1.3 dynamic-slice.5
  549.4 272.9 %all-reduce.9.cloned.1.call-done = f32[32,896]{1,0:T(8,128)} async-done(((f32[32,896]{1,0:T(8,128)}), f32[32,896]{1,0:T(8,128)}) %all-reduce.9.cloned.1.call-update) | async-done | bytes 114704
  822.3 2.0 constant_dynamic-slice_fusion
  (45 shorter events, 5.5 us)
Async XLA Ops:
  7.2 4.6 copy-start
  7.2 78.2 %all-gather.7.cloned.1.call-start = ((), (), s32[]{:S(2)}) async-start(), calls=%async_computation.3 | async-start | bytes 2228224 | tf_op jit(solution)/shard_map/all_gather | solution.py:92
  7.9 202.3 %all-gather.5.cloned.1.call-start = ((), (), s32[]{:S(2)}) async-start(), calls=%async_computation.1 | async-start | bytes 15138816 | tf_op jit(solution)/shard_map/all_gather | solution.py:95
  8.7 486.9 %reduce-scatter.5.cloned.1.call-start = ((), (), s32[]{:S(2)}) async-start(), calls=%async_computation.2 | async-start | bytes 540672 | tf_op jit(solution)/shard_map/reduce_scatter | solution.py:119
  87.9 127.4 %copy-start.2 = (bf16[32,896]{1,0:T(8,128)(2,1)S(1)}, bf16[32,896]{1,0:T(8,128)(2,1)}, u32[]{:S(2)}) copy-start(bf16[32,896]{1,0:T(8,128)(2,1)} %param.12) | copy-start | bytes 172036
  210.2 7.3 copy-start.3
  219.3 30.4 %copy-start.4 = (s32[1,12]{1,0:T(1,128)S(1)}, s32[1,12]{1,0:T(1,128)}, u32[]{:S(2)}) copy-start(s32[1,12]{1,0:T(1,128)} %param.8) | copy-start | bytes 148
  219.3 182.5 %copy-start.1 = (bf16[12,4096]{1,0:T(8,128)(2,1)S(1)}, bf16[12,4096]{1,0:T(8,128)(2,1)}, u32[]{:S(2)}) copy-start(bf16[12,4096]{1,0:T(8,128)(2,1)} %param.7) | copy-start | bytes 294916
  276.4 125.0 %collective-permute-start.2 = (f32[16,32]{1,0:T(8,128)S(1)}, f32[16,32]{1,0:T(8,128)S(1)}, u32[]{:S(2)}, u32[]{:S(2)}) collective-permute-start(f32[16,32]{1,0:T(8,128)S(1)} %fusion), channel_id=1, source_target_pairs={{0,3},{1,4},{2,5},{3,6},{4,7},{5,8},{6,9},{7,10},{8,11},{9,12},{10... | collective-permute-start | bytes 6152
  277.7 123.7 %collective-permute-start.1 = (f32[16,32]{1,0:T(8,128)S(1)}, f32[16,32]{1,0:T(8,128)S(1)}, u32[]{:S(2)}, u32[]{:S(2)}) collective-permute-start(f32[16,32]{1,0:T(8,128)S(1)} %fusion), channel_id=1, source_target_pairs={{0,2},{1,3},{2,4},{3,5},{4,6},{5,7},{6,8},{7,9},{8,10},{9,11},{10,... | collective-permute-start | bytes 6152
  280.3 121.0 %collective-permute-start = (f32[16,32]{1,0:T(8,128)S(1)}, f32[16,32]{1,0:T(8,128)S(1)}, u32[]{:S(2)}, u32[]{:S(2)}) collective-permute-start(f32[16,32]{1,0:T(8,128)S(1)} %fusion), channel_id=1, source_target_pairs={{0,1},{1,2},{2,3},{3,4},{4,5},{5,6},{6,7},{7,8},{8,9},{9,10},{10,1... | collective-permute-start | bytes 6152
  398.7 2.6 collective-permute-start.3
  403.0 419.3 %all-reduce.9.cloned.1.call-start = ((), (), s32[]{:S(2)}) async-start(), calls=%async_computation.4 | async-start | bytes 229376
Sparse Core Ops, SparseCore 0:
  10.1 75.2 all-gather.6
  88.6 121.5 all-gather.4
  403.1 92.4 reduce-scatter.4
  547.5 274.7 all-reduce.8
where the time goes:
time: 834 us; the launch traced here: 832 us
  waiting for transfers between devices  524 us (63%)
  blocking collectives  252 us (30%)
  between operations  18.4 us (2%)
  matrix products  13.4 us (2%)
  local copies, waits for them, and re-layouts  10.6 us (1%)
  starting transfers between devices  9.42 us (1%)
    unnamed x9, waiting for transfers between devices  275 us
    all_gather x1, waiting for transfers between devices, on_device(): piece = lax.all_gather(frozen_gate_up, 'dp', axis=1, tiled=True)  122 us
    psum x1, blocking collectives, wide_total(): return lax.psum((left_term, right_term), ('dp', 'blk'))  113 us
    reduce_scatter x1, waiting for transfers between devices, on_device(): lax.psum_scatter(grad_a_part, 'dp', scatter_dimension=0, tiled=True)  91.7 us
    unnamed x2, blocking collectives  54.4 us
    psum x1, blocking collectives, on_device(): grad_a = lax.psum(grad_a_rows, 'blk')  49.8 us
    all_gather x1, waiting for transfers between devices, on_device(): lax.all_gather(tokens, 'blk', axis=0, tiled=True)  35.2 us
    all_gather x1, blocking collectives, on_device(): lax.all_gather(input_low_rank, 'blk', axis=0, tiled=True)  34.7 us
  transfers between devices with their start and end apart: 8, of which 5 were waited for; matrix products, arithmetic and copies ran while one was open for 1% of the time, Pallas kernels for 0%

commit v1 on v0

v1 whole, which is shorter than its diff:
```python
import jax
import jax.numpy as jnp
from jax import lax
from jax.sharding import Mesh, PartitionSpec as P

SEQS = 4
ROWS = 12
RANK = 16
WIDTH = 4096
DPO_BETA = 0.1
LOSS_SCALE = 1024.0
HIGHEST = lax.Precision.HIGHEST
F32 = jnp.float32
BF16 = jnp.bfloat16

AXES = ("yh", "x", "c", "z", "yl")
SIZES = (4, 4, 2, 8, 2)
DP = ("yh", "x", "c")
BLK = ("z", "yl")
SWAP = [(0, 1), (1, 0)]


def split_terms(value):
    high = value.astype(BF16)
    low = (value - high.astype(F32)).astype(BF16)
    return high, low


def on_device(tokens, sequence_labels, response_mask, frozen, down, up, readout):
    n_blk, n_dp = 16, 32
    core = lax.axis_index("c")
    units = frozen.shape[2]

    own = lax.all_to_all(frozen, "c", split_axis=0, concat_axis=0)
    weights = lax.all_gather(own.reshape(-1, units), ("yh", "x"), axis=0, tiled=True)

    code = jnp.where(response_mask > 0, sequence_labels, SEQS).astype(BF16)
    block = jnp.concatenate(
        [tokens, jnp.pad(code, ((0, 3), (0, WIDTH - ROWS)))], axis=0
    )
    everyone = lax.all_to_all(
        jnp.broadcast_to(block[None], (n_blk,) + block.shape), BLK, split_axis=0, concat_axis=0
    )
    codes = everyone[:, ROWS, :ROWS].astype(jnp.int32)
    mine = everyone[:, :ROWS].reshape(n_blk * ROWS, WIDTH)
    theirs = lax.ppermute(mine, "c", SWAP)

    low = jnp.dot(mine, down, preferred_element_type=F32).astype(BF16)
    far_half = jnp.dot(theirs, weights, preferred_element_type=F32)
    from_partner = lax.ppermute(far_half, "c", SWAP)
    near_half = jnp.dot(mine, weights, preferred_element_type=F32)
    gate_ref = jnp.where(core == 0, near_half, from_partner)
    up_ref = jnp.where(core == 0, from_partner, near_half)

    b_gate, b_up = up[:RANK], up[RANK:]
    readout_f = readout.astype(F32)
    gate_pol = gate_ref + jnp.dot(low[:, :RANK], b_gate, preferred_element_type=F32)
    up_pol = up_ref + jnp.dot(low[:, RANK:], b_up, preferred_element_type=F32)
    sig_ref = jax.nn.sigmoid(gate_ref)
    sig_pol = jax.nn.sigmoid(gate_pol)
    act_pol = gate_pol * sig_pol
    change = jnp.sum((act_pol * up_pol - gate_ref * sig_ref * up_ref) * readout_f, axis=1)
    k_gate = readout_f * sig_pol * (1.0 + gate_pol * (1.0 - sig_pol)) * up_pol
    k_up = readout_f * act_pol
    contract_last = (((1,), (1,)), ((), ()))
    mixed = jnp.concatenate(
        [
            lax.dot_general(k_gate, b_gate.astype(F32), contract_last, precision=HIGHEST),
            lax.dot_general(k_up, b_up.astype(F32), contract_last, precision=HIGHEST),
        ],
        axis=1,
    )

    pairs = jnp.arange(SEQS // 2, dtype=jnp.int32)
    chosen = (codes[:, :, None] == 2 * pairs).astype(F32)
    rejected = (codes[:, :, None] == 2 * pairs + 1).astype(F32)
    signs = chosen - rejected
    valid = (jnp.max(chosen, axis=1) * jnp.max(rejected, axis=1)).reshape(-1)
    gap_part = jnp.sum(signs * change.reshape(n_blk, ROWS, 1), axis=1).reshape(-1)

    per_peer = mixed.reshape(-1, n_blk, 2).transpose(1, 2, 0).reshape(n_blk, -1)
    gaps_out = jnp.broadcast_to(jnp.pad(gap_part, (0, 96))[None], (n_blk, 128))
    arrived = lax.all_to_all(
        jnp.concatenate([per_peer, gaps_out], axis=1), BLK, split_axis=0, concat_axis=0, tiled=True
    )
    total = jnp.sum(arrived, axis=0)
    columns = total[: 2 * n_blk * ROWS].reshape(2, -1)
    logit = DPO_BETA * total[2 * n_blk * ROWS : 2 * n_blk * ROWS + 2 * n_blk]
    log_sum = jnp.sum(valid * jax.nn.log_sigmoid(logit))
    scaled = -LOSS_SCALE * DPO_BETA * valid * jax.nn.sigmoid(-logit)
    cotangent = jnp.sum(signs * scaled.reshape(n_blk, 1, -1), axis=2).reshape(-1)

    weighted = low.astype(F32) * cotangent[:, None]
    contract_first = (((0,), (0,)), ((), ()))
    grad_b_part = jnp.concatenate(
        [
            lax.dot_general(weighted[:, :RANK], k_gate, contract_first, precision=HIGHEST),
            lax.dot_general(weighted[:, RANK:], k_up, contract_first, precision=HIGHEST),
        ],
        axis=0,
    )
    projected = columns * cotangent[None]
    terms = jnp.dot(
        jnp.concatenate(split_terms(projected), axis=0), mine, preferred_element_type=F32
    )
    grad_a_part = terms[:2] + terms[2:]

    scalars = jnp.concatenate([log_sum[None], jnp.sum(valid)[None], jnp.zeros((126,), F32)])
    outgoing = jnp.concatenate(
        [
            grad_b_part,
            grad_a_part.reshape(2, n_dp, -1).transpose(1, 0, 2).reshape(n_dp, -1),
            jnp.broadcast_to(scalars[None], (n_dp, 128)),
        ],
        axis=1,
    )
    summed = jnp.sum(
        lax.all_to_all(outgoing, DP, split_axis=0, concat_axis=0, tiled=True), axis=0
    )
    rows_a = WIDTH // n_dp
    log_total, count = summed[units + 2 * rows_a], summed[units + 2 * rows_a + 1]
    pair_total = jnp.maximum(count, 1.0)
    grad_b = (summed[:units] / pair_total)[None]
    two = (summed[units : units + 2 * rows_a] / pair_total).reshape(1, 2, rows_a)
    grad_a = lax.all_to_all(
        jnp.broadcast_to(two, (n_blk, 2, rows_a)), BLK, split_axis=0, concat_axis=0
    )
    return -log_total / pair_total, grad_a.reshape(2 * n_blk, rows_a).T, grad_b


def solution(mesh):
    fine = Mesh(mesh.devices.reshape(SIZES), AXES)
    in_specs = (
        P(AXES, None),
        P(AXES, None),
        P(AXES, None),
        P(None, DP, BLK),
        P(),
        P(None, BLK),
        P(BLK),
    )
    out_specs = (P(), P(DP, None), P(DP, BLK))
    return jax.shard_map(
        on_device, mesh=fine, in_specs=in_specs, out_specs=out_specs, check_vma=False
    )
```

time: 834 us -> 217 us (0.26)
  waiting for transfers between devices: 524 us -> 59.9 us
  blocking collectives: 252 us -> 102 us
    unnamed x9 -> x1, waiting for transfers between devices: 275 us -> 0.02 us
    psum x2 -> x0, blocking collectives: 163 us -> none  [the longest x1 113 us: wide_total(): return lax.psum((left_term, right_term), ('dp', 'blk'))]
    all_gather x2 -> x1, waiting for transfers between devices: 157 us -> 51.4 us  [on_device(): lax.all_gather(own.reshape(-1, units), ('yh', 'x'), axis=0, tiled=True)]
    all_to_all x0 -> x4, blocking collectives: none -> 102 us  [the longest x1 54.3 us: on_device(): lax.all_to_all(jnp.broadcast_to(block[None], (n_blk,) + block.shape), BLK...]
    reduce_scatter x1 -> x0, waiting for transfers between devices: 91.7 us -> none  [on_device(): lax.psum_scatter(grad_a_part, 'dp', scatter_dimension=0, tiled=True)]
    unnamed x2 -> x0, blocking collectives: 54.4 us -> none
    all_gather x1 -> x0, blocking collectives: 34.7 us -> none  [on_device(): lax.all_gather(input_low_rank, 'blk', axis=0, tiled=True)]
    unnamed x5 -> x0, starting transfers between devices: 9.31 us -> none
  transfers between devices with their start and end apart: 8 -> 4, of which waited for: 5 -> 3; matrix products, arithmetic and copies ran while one was open for 1% -> 5% of each run, Pallas kernels for 0% -> 0%
where the time goes in v1:
time: 217 us; the launch traced here: 216 us
  blocking collectives  102 us (47%)
  waiting for transfers between devices  59.9 us (28%)
  between operations  16.8 us (8%)
  matrix products  15.9 us (7%)
  starting transfers between devices  9.76 us (4%)
  local copies, waits for them, and re-layouts  6.98 us (3%)
  other arithmetic  4.87 us (2%)
    all_to_all x1, blocking collectives, on_device(): lax.all_to_all(jnp.broadcast_to(block[None], (n_blk,) + block.shape), BLK...  54.3 us
    all_gather x1, waiting for transfers between devices, on_device(): lax.all_gather(own.reshape(-1, units), ('yh', 'x'), axis=0, tiled=True)  51.4 us
    all_to_all x1, blocking collectives, on_device(): lax.all_to_all(outgoing, DP, split_axis=0, concat_axis=0, tiled=True)  19.5 us
    all_to_all x1, blocking collectives, on_device(): lax.all_to_all(jnp.concatenate([per_peer, gaps_out], axis=1), BLK, split_...  15.4 us
    all_to_all x1, blocking collectives, on_device(): own = lax.all_to_all(frozen, 'c', split_axis=0, concat_axis=0)  12.7 us
    all_to_all x1, waiting for transfers between devices, on_device(): lax.all_to_all(jnp.broadcast_to(two, (n_blk, 2, rows_a)), BLK, split_axis...  6.05 us
    dot_general x1, matrix products, on_device(): far_half = jnp.dot(theirs, weights, preferred_element_type=F32)  5.77 us
    dot_general x1, matrix products, on_device(): near_half = jnp.dot(mine, weights, preferred_element_type=F32)  4.89 us
  transfers between devices with their start and end apart: 4, of which 3 were waited for; matrix products, arithmetic and copies ran while one was open for 5% of the time, Pallas kernels for 0%

profile of v1, /device:TPU:1, one launch (start us, length us, event | category | flops | bytes accessed | tf_op | source)
XLA Modules:
  0.0 216.1 jit_solution(17535964041169395196)
XLA Ops:
  7.2 12.7 %all_to_all.33 = bf16[2,128,896]{2,1,0:T(8,128)(2,1)} all-to-all(bf16[2,128,896]{2,1,0:T(8,128)(2,1)} %param.10), channel_id=1, replica_groups=mesh['yh'=4,'x'=4,'c'=2,'z'=8,'yl'=2] {'c'}, dimensions={0} | all-to-all | bytes 917504 | tf_op jit(solution)/shard_map/all_to_all | solution.py:34
  19.9 0.7 fusion.30
  20.6 0.9 fusion.8
  21.5 0.2 broadcast_in_dim.21
  21.7 54.3 %all_to_all.34 = bf16[16,16,4096]{2,1,0:T(8,128)(2,1)} all-to-all(bf16[16,16,4096]{2,1,0:T(8,128)(2,1)S(1)} %broadcast_in_dim.21), channel_id=1, replica_groups=mesh['yh'=4,'x'=4,'c'=2,'z'=8,'yl'=2] {'z','yl'}, dimensions={0} | all-to-all | bytes 4194304 | tf_op jit(solution)/shard_map/all_to_all | solution.py:41
  76.0 2.5 %reshape.110 = bf16[192,4096]{1,0:T(8,128)(2,1)S(1)} reshape(bf16[16,12,4096]{2,1,0:T(8,128)(2,1)} %bitcast.34) | data formatting | bytes 3145728 | tf_op jit(solution)/shard_map/reshape | solution.py:45
  78.5 3.7 %collective-permute-start = (bf16[192,4096]{1,0:T(8,128)(2,1)S(1)}, bf16[192,4096]{1,0:T(8,128)(2,1)S(1)}, u32[]{:S(2)}, u32[]{:S(2)}) collective-permute-start(bf16[192,4096]{1,0:T(8,128)(2,1)S(1)} %reshape.110), channel_id=1, source_target_pairs={{0,16},{16,0},{1,17},{17,1},{2,18},{18,2},{3,19},{19,3},{4,20},{20... | collective-permute-start | bytes 4718600 | tf_op jit(solution)/shard_map/ppermute | solution.py:46
  82.2 0.6 convolution_convert_fusion
  82.8 2.4 %collective-permute-done = bf16[192,4096]{1,0:T(8,128)(2,1)S(1)} collective-permute-done((bf16[192,4096]{1,0:T(8,128)(2,1)S(1)}, bf16[192,4096]{1,0:T(8,128)(2,1)S(1)}, u32[]{:S(2)}, u32[]{:S(2)}) %collective-permute-start) | collective-permute-done | bytes 1572896 | tf_op jit(solution)/shard_map/ppermute | solution.py:46
  85.2 51.4 %all-gather.2.cloned.1.call-done = bf16[4096,896]{1,0:T(8,128)(2,1)} async-done(((bf16[256,896]{1,0:T(8,128)(2,1)}), bf16[4096,896]{1,0:T(8,128)(2,1)}) %all-gather.2.cloned.1.call-update) | async-done | bytes 7340048 | tf_op jit(solution)/shard_map/all_gather | solution.py:35
  136.6 5.8 %fusion.37 = f32[192,896]{1,0:T(8,128)} fusion(bf16[192,4096]{1,0:T(8,128)(2,1)S(1)} %collective-permute-done, bf16[4096,896]{1,0:T(8,128)(2,1)} %all-gather.2.cloned.1.call-done), kind=kOutput, calls=%fused_computation.71 | convolution fusion | flops 1409286144 | bytes 9601024 | tf_op jit(solution)/shard_map/dot_general | solution.py:49
  142.4 2.6 %collective-permute-start.1 = (f32[192,896]{1,0:T(8,128)}, f32[192,896]{1,0:T(8,128)S(1)}, u32[]{:S(2)}, u32[]{:S(2)}) collective-permute-start(f32[192,896]{1,0:T(8,128)} %fusion.37), channel_id=1, source_target_pairs={{0,16},{16,0},{1,17},{17,1},{2,18},{18,2},{3,19},{19,3},{4,20},{20... | collective-permute-start | bytes 2064392 | tf_op jit(solution)/shard_map/ppermute | solution.py:50
  144.9 0.8 slice_convert_fusion
  145.8 4.9 %fusion.36 = f32[192,896]{1,0:T(8,128)S(1)} fusion(bf16[192,4096]{1,0:T(8,128)(2,1)S(1)} %reshape.110, bf16[4096,896]{1,0:T(8,128)(2,1)} %all-gather.2.cloned.1.call-done), kind=kOutput, calls=%fused_computation.70 | convolution fusion | flops 1409286144 | bytes 9601024 | tf_op jit(solution)/shard_map/dot_general | solution.py:51
  150.7 0.3 convolution_add_fusion.1
  151.0 0.6 copy-done.1
  151.6 0.6 fusion.3
  152.2 2.0 multiply_reduce_fusion
  154.6 0.4 fusion.11
  155.2 15.4 %all_to_all.35 = f32[16,1,512]{2,1,0:T(1,128)S(1)} all-to-all(f32[16,1,512]{2,1,0:T(1,128)S(1)} %all_to_all.23), channel_id=1, replica_groups=mesh['yh'=4,'x'=4,'c'=2,'z'=8,'yl'=2] {'z','yl'}, dimensions={0} | all-to-all | bytes 65536 | tf_op jit(solution)/shard_map/all_to_all | solution.py:83
  171.1 0.6 fusion.29
  172.0 0.6 fusion.1
  172.6 0.5 fusion.15
  173.2 0.3 fusion.22
  173.6 1.4 pad_maximum_fusion.2
  175.1 19.5 %all_to_all.36 = f32[32,1,1280]{2,1,0:T(1,128)S(1)} all-to-all(f32[32,1,1280]{2,1,0:T(1,128)S(1)} %copy.35), channel_id=1, replica_groups=mesh['yh'=4,'x'=4,'c'=2,'z'=8,'yl'=2] {'yh','x','c'}, dimensions={0} | all-to-all | bytes 327680 | tf_op jit(solution)/shard_map/all_to_all | solution.py:118
  194.8 0.6 fusion.35
  196.0 0.6 broadcast_in_dim.27
  196.6 3.5 %all-to-all-start.4 = ((f32[16,2,128]{2,1,0:T(2,128)}), f32[16,2,128]{2,1,0:T(2,128)S(1)}, u32[]{:S(2)}, u32[]{:S(2)}) async-start(f32[16,2,128]{2,1,0:T(2,128)} %broadcast_in_dim.27), calls=%async_computation.4 | async-start | bytes 32768 | tf_op jit(solution)/shard_map/all_to_all | solution.py:125
  200.8 0.6 broadcast_in_dim.54
  201.4 6.0 %all-to-all-done.4 = f32[16,2,128]{2,1,0:T(2,128)S(1)} async-done(((f32[16,2,128]{2,1,0:T(2,128)}), f32[16,2,128]{2,1,0:T(2,128)S(1)}, u32[]{:S(2)}, u32[]{:S(2)}) %all-to-all-start.4) | async-done | bytes 16416 | tf_op jit(solution)/shard_map/all_to_all | solution.py:125
  207.5 0.6 copy.40
  (44 shorter events, 1.9 us)
Async XLA Ops:
  7.2 75.1 %copy-start = (bf16[4096,32]{0,1:T(8,128)(2,1)S(1)}, bf16[4096,32]{0,1:T(8,128)(2,1)}, u32[]{:S(2)}) copy-start(bf16[4096,32]{0,1:T(8,128)(2,1)} %param.11) | copy-start | bytes 786436
  7.2 129.4 %all-gather.2.cloned.1.call-start = ((), (), s32[]{:S(2)}) async-start(), calls=%async_computation.5 | async-start | bytes 7798784 | tf_op jit(solution)/shard_map/all_gather | solution.py:35
  76.0 6.2 %copy-start.3 = (bf16[896]{0:T(1024)(128)(2,1)S(1)}, bf16[896]{0:T(1024)(128)(2,1)}, u32[]{:S(2)}) copy-start(bf16[896]{0:T(1024)(128)(2,1)} %param.13) | copy-start | bytes 5380
  78.5 6.7 %collective-permute-start = (bf16[192,4096]{1,0:T(8,128)(2,1)S(1)}, bf16[192,4096]{1,0:T(8,128)(2,1)S(1)}, u32[]{:S(2)}, u32[]{:S(2)}) collective-permute-start(bf16[192,4096]{1,0:T(8,128)(2,1)S(1)} %reshape.110), channel_id=1, source_target_pairs={{0,16},{16,0},{1,17},{17,1},{2,18},{18,2},{3,19},{19,3},{4,20},{20... | collective-permute-start | bytes 4718600 | tf_op jit(solution)/shard_map/ppermute | solution.py:46
  142.4 8.3 %collective-permute-start.1 = (f32[192,896]{1,0:T(8,128)}, f32[192,896]{1,0:T(8,128)S(1)}, u32[]{:S(2)}, u32[]{:S(2)}) collective-permute-start(f32[192,896]{1,0:T(8,128)} %fusion.37), channel_id=1, source_target_pairs={{0,16},{16,0},{1,17},{17,1},{2,18},{18,2},{3,19},{19,3},{4,20},{20... | collective-permute-start | bytes 2064392 | tf_op jit(solution)/shard_map/ppermute | solution.py:50
  145.8 4.9 %copy-start.2 = (bf16[32,896]{1,0:T(8,128)(2,1)S(1)}, bf16[32,896]{1,0:T(8,128)(2,1)}, u32[]{:S(2)}) copy-start(bf16[32,896]{1,0:T(8,128)(2,1)} %param.12) | copy-start | bytes 172036
  150.7 0.9 copy-start.1
  196.6 10.8 %all-to-all-start.4 = ((f32[16,2,128]{2,1,0:T(2,128)}), f32[16,2,128]{2,1,0:T(2,128)S(1)}, u32[]{:S(2)}, u32[]{:S(2)}) async-start(f32[16,2,128]{2,1,0:T(2,128)} %broadcast_in_dim.27), calls=%async_computation.4 | async-start | bytes 32768 | tf_op jit(solution)/shard_map/all_to_all | solution.py:125
Sparse Core Ops, SparseCore 0:
  20.0 116.5 all-gather.1

commit v2 on v1

v2 whole, which is shorter than its diff:
```python
import jax
import jax.numpy as jnp
from jax import lax
from jax.experimental import pallas as pl
from jax.experimental.pallas import tpu as pltpu
from jax.sharding import Mesh, PartitionSpec as P

SEQS = 4
ROWS = 12
RANK = 16
WIDTH = 4096
DPO_BETA = 0.1
LOSS_SCALE = 1024.0
HIGHEST = lax.Precision.HIGHEST
F32 = jnp.float32
BF16 = jnp.bfloat16

AXES = ("s", "t", "x", "c", "z", "yl")
SIZES = (2, 2, 4, 2, 8, 2)
DP = ("s", "t", "x", "c")
BLK = ("z", "yl")
YH = ("s", "t")
SWAP = [(0, 1), (1, 0)]

SLICE = 128
HALF = WIDTH // 2
LANES = 128
COLS = 512
SKIP = 384
GROUP = 384
BLOCKS = GROUP // ROWS
WIDE = 2 * COLS + LANES


def fetch(value, axes, size, k):
    return lax.ppermute(value, axes, [((i + k) % size, i) for i in range(size)])


def products(place, tok, own, own1, own3, own2g, own2u, rest, rest1, rest3, rest2a, rest2b, down, count,
             far, near_x, near_code, w, far_x):
    yh, x, core = place[0], place[1], place[2]
    row_of = {1: 0, 3: 2 * SLICE, 2: 4 * SLICE}

    def piece(k, j, part):
        begin = part * SLICE if k == 0 else row_of[k] + part * SLICE
        if k == 0:
            if j == 2:
                return (own2g, own2u)[part][...]
            return {0: own, 1: own1, 3: own3}[j][pl.ds(begin, SLICE), :]
        if j == 2:
            if begin < 3 * SLICE:
                return rest2a[pl.ds(begin, SLICE), :]
            return rest2b[pl.ds(begin - 3 * SLICE, SLICE), :]
        return {0: rest, 1: rest1, 3: rest3}[j][pl.ds(begin, SLICE), :]

    for k in range(4):
        for j in range(4):
            place_k = (k * 4 + j) * SLICE
            rows = pl.ds(place_k, SLICE)
            w[rows, 0:COLS] = piece(k, j, 0)
            w[rows, COLS : 2 * COLS] = piece(k, j, 1)
            source = lax.rem(yh + k, 4) * 4 + lax.rem(x + j, 4)
            w[rows, 2 * COLS : WIDE] = down[pl.ds(pl.multiple_of((source * 2 + core) * SLICE, SLICE), SLICE), :]
            columns = pl.ds(pl.multiple_of(source * SLICE, SLICE), SLICE)
            for z in range(8):
                lines = pl.ds(z * 48, 48)
                near_x[lines, place_k : place_k + SLICE] = tok[z, core, :, columns]
                far_x[lines, place_k : place_k + SLICE] = tok[z, 1 - core, :, columns]
    for z in range(8):
        near_code[pl.ds(z * 48, 48), :] = tok[z, core, :, HALF : HALF + LANES]
    for n in range(3):
        part = slice(n * GROUP, (n + 1) * GROUP)
        far[:, part] = jnp.dot(far_x[...], w[:, part], preferred_element_type=F32)
    far[:, 2 * COLS : WIDE] = far[:, 2 * COLS : WIDE] + count[...]


def on_device(tokens, sequence_labels, response_mask, frozen, down, up, readout):
    s, t, x, core = (lax.axis_index(a) for a in ("s", "t", "x", "c"))
    code = jnp.where(response_mask > 0, sequence_labels, SEQS)

    by_core = tokens.reshape(ROWS, WIDTH // (2 * SLICE), 2, SLICE).transpose(2, 0, 1, 3)
    code_lanes = jnp.pad(code.reshape(ROWS, 1).astype(BF16), ((0, 0), (0, LANES - 1)))
    message = jnp.concatenate(
        [by_core.reshape(2, ROWS, HALF), jnp.broadcast_to(code_lanes[None], (2, ROWS, LANES))], axis=2
    )
    message = jnp.broadcast_to(message[:, None], (2, 4, ROWS, HALF + LANES))
    eight = lax.all_to_all(
        message.reshape(8, ROWS, HALF + LANES), ("c", "t", "yl"), split_axis=0, concat_axis=0
    )
    eight, frozen, sequence_labels = lax.optimization_barrier((eight, frozen, sequence_labels))
    tok = lax.all_gather(eight.reshape(8 * ROWS, HALF + LANES), "z", axis=0, tiled=True)
    tok = tok.reshape(8, 2, 4 * ROWS, HALF + LANES)

    has = [jnp.max((code == q).astype(F32)) for q in range(SEQS)]
    count = has[0] * has[1] + has[2] * has[3]

    low_half, high_half = frozen[:, :, :COLS], frozen[:, :, SKIP:]
    mine = jnp.where(t == 0, low_half, high_half).reshape(2 * SLICE, COLS)
    other = jnp.where(t == 0, high_half, low_half).reshape(2 * SLICE, COLS)
    count_rows = jnp.broadcast_to(count.astype(BF16), (16, COLS))
    y1 = fetch(other, YH, 4, 1)
    y3 = fetch(other, YH, 4, 3)
    y2 = fetch(jnp.concatenate([mine, count_rows], axis=0), YH, 4, 2)
    own1 = fetch(mine, "x", 4, 1)
    own3 = fetch(mine, "x", 4, 3)
    own2g = fetch(own3[:SLICE], "x", 4, 3)
    own2u = fetch(own1[SLICE:], "x", 4, 1)
    pair_rows = y2[2 * SLICE :] + count_rows
    rest = jnp.concatenate([y1, y3, y2[: 2 * SLICE], pair_rows], axis=0)
    rest1 = fetch(rest, "x", 4, 1)
    rest3 = fetch(rest, "x", 4, 3)
    rest2a = fetch(rest3[: 3 * SLICE], "x", 4, 3)
    rest2b = fetch(rest1[3 * SLICE :], "x", 4, 1)
    count = sum(p[-1, 0].astype(F32) for p in (rest, rest1, rest3, rest2b))
    count_lanes = jnp.where(jnp.arange(LANES) == 2 * RANK, count, 0.0).reshape(1, LANES)

    vmem = pl.BlockSpec(memory_space=pltpu.VMEM)
    smem = pl.BlockSpec(memory_space=pltpu.SMEM)
    far, near_x, near_code, w = pl.pallas_call(
        products,
        out_shape=(
            jax.ShapeDtypeStruct((GROUP, WIDE), F32),
            jax.ShapeDtypeStruct((GROUP, HALF), BF16),
            jax.ShapeDtypeStruct((GROUP, LANES), BF16),
            jax.ShapeDtypeStruct((HALF, WIDE), BF16),
        ),
        in_specs=[smem] + [vmem] * 13,
        out_specs=(vmem,) * 4,
        scratch_shapes=[pltpu.VMEM((GROUP, HALF), BF16)],
        compiler_params=pltpu.CompilerParams(vmem_limit_bytes=40 * 1024 * 1024),
        cost_estimate=pl.CostEstimate(flops=2 * GROUP * HALF * WIDE, bytes_accessed=20_000_000, transcendentals=0),
    )(
        jnp.stack([2 * s + t, x, core]).astype(jnp.int32), tok, mine, own1, own3, own2g, own2u,
        rest, rest1, rest3, rest2a, rest2b, jnp.pad(down, ((0, 0), (0, LANES - 2 * RANK))), count_lanes,
    )
    from_partner = lax.ppermute(far, "c", SWAP)
    both = jnp.dot(near_x, w, preferred_element_type=F32) + from_partner
    gate_ref, up_ref = both[:, :COLS], both[:, COLS : 2 * COLS]
    low = both[:, 2 * COLS : 2 * COLS + 2 * RANK].astype(BF16)
    count = count + from_partner[0, 2 * COLS + 2 * RANK]

    units = jnp.where(t == 0, up[:, :COLS], up[:, SKIP:])
    b_gate, b_up = units[:RANK], units[RANK:]
    shared = jnp.where(jnp.arange(COLS) < 2 * COLS - readout.shape[0], 0.0, 1.0)
    readout_f = jnp.where(t == 0, readout[:COLS].astype(F32), readout[SKIP:].astype(F32) * shared)
    gate_pol = gate_ref + jnp.dot(low[:, :RANK], b_gate, preferred_element_type=F32)
    up_pol = up_ref + jnp.dot(low[:, RANK:], b_up, preferred_element_type=F32)
    sig_ref = jax.nn.sigmoid(gate_ref)
    sig_pol = jax.nn.sigmoid(gate_pol)
    act_pol = gate_pol * sig_pol
    change = jnp.sum((act_pol * up_pol - gate_ref * sig_ref * up_ref) * readout_f, axis=1)
    k_gate = readout_f * sig_pol * (1.0 + gate_pol * (1.0 - sig_pol)) * up_pol
    k_up = readout_f * act_pol
    contract_last = (((1,), (1,)), ((), ()))
    mixed = jnp.concatenate(
        [
            lax.dot_general(b_gate.astype(F32), k_gate, contract_last, precision=HIGHEST),
            lax.dot_general(b_up.astype(F32), k_up, contract_last, precision=HIGHEST),
        ],
        axis=0,
    )

    codes = near_code[:, 0].astype(jnp.int32).reshape(BLOCKS, ROWS)
    pairs = jnp.arange(SEQS // 2, dtype=jnp.int32)
    chosen = (codes[:, :, None] == 2 * pairs).astype(F32)
    rejected = (codes[:, :, None] == 2 * pairs + 1).astype(F32)
    signs = chosen - rejected
    valid = (jnp.max(chosen, axis=1) * jnp.max(rejected, axis=1)).reshape(-1)
    gap_part = jnp.sum(signs * change.reshape(BLOCKS, ROWS, 1), axis=1).reshape(-1)

    for_all = jnp.concatenate([gap_part, count[None], jnp.zeros((63,), F32)])
    arrived = lax.all_to_all(
        jnp.concatenate([mixed, jnp.broadcast_to(for_all[None], (32, LANES))], axis=1),
        ("t", "z", "yl"), split_axis=0, concat_axis=0, tiled=True,
    )
    total = jnp.sum(arrived, axis=0)
    pair_total = jnp.maximum(total[GROUP + 64], 1.0)
    logit = DPO_BETA * total[GROUP : GROUP + 64]
    log_sum = jnp.sum(valid * jax.nn.log_sigmoid(logit))
    scaled = -LOSS_SCALE * DPO_BETA * valid * jax.nn.sigmoid(-logit) / pair_total
    cotangent = jnp.sum(signs * scaled.reshape(BLOCKS, 1, -1), axis=2).reshape(-1)

    projected = (total[:GROUP] * cotangent).astype(BF16)[None]
    partner_projected = lax.ppermute(projected, "c", SWAP)
    weighted = low.astype(F32) * cotangent[:, None]
    contract_first = (((0,), (0,)), ((), ()))
    grad_b_part = jnp.concatenate(
        [
            lax.dot_general(weighted[:, :RANK], k_gate, contract_first, precision=HIGHEST),
            lax.dot_general(weighted[:, RANK:], k_up, contract_first, precision=HIGHEST),
        ],
        axis=0,
    )
    first = jnp.where(core == 0, projected, partner_projected).reshape(1, 8, 1, 48)
    second = jnp.where(core == 0, partner_projected, projected).reshape(1, 8, 1, 48)
    all_projected = jnp.concatenate([first, second], axis=2).reshape(1, 2 * GROUP)
    grad_a_part = jnp.dot(
        all_projected, tok.reshape(2 * GROUP, -1)[:, :HALF], preferred_element_type=F32
    )

    mine_a = jnp.where(jnp.arange(2) == core, 1.0, 0.0).reshape(1, 2, 1)
    slices = (grad_a_part.reshape(16, 1, SLICE) * mine_a).reshape(32, SLICE)
    outgoing = jnp.concatenate(
        [grad_b_part, slices, jnp.broadcast_to(log_sum, (32, LANES))], axis=1
    )
    arrived = lax.all_to_all(outgoing, DP, split_axis=0, concat_axis=0, tiled=True)
    summed = jnp.sum(arrived.reshape(2, 2, 8, -1), axis=(0, 2))
    spare = readout.shape[0] - COLS
    grad_b = jnp.pad(summed[0, :COLS], (0, spare)) + jnp.pad(summed[1, :COLS], (spare, 0))
    columns = summed[:, COLS : COLS + SLICE]
    log_total = summed[0, COLS + SLICE]
    grad_a = lax.all_to_all(
        jnp.broadcast_to(columns[None], (16, 2, SLICE)), BLK, split_axis=0, concat_axis=0
    )
    grad_a = grad_a.transpose(2, 1, 0).reshape(SLICE, 2 * RANK)
    return -log_total / pair_total, grad_a, grad_b[None]


def solution(mesh):
    fine = Mesh(mesh.devices.reshape(SIZES), AXES)
    in_specs = (
        P(AXES, None),
        P(AXES, None),
        P(AXES, None),
        P(None, DP, BLK),
        P(),
        P(None, BLK),
        P(BLK),
    )
    out_specs = (P(), P(DP, None), P(DP, BLK))
    return jax.shard_map(
        on_device, mesh=fine, in_specs=in_specs, out_specs=out_specs, check_vma=False
    )
```

time: 217 us -> 220 us (1.014)
  blocking collectives: 102 us -> 39.6 us
  starting transfers between devices: 9.76 us -> 60.3 us
  local copies, waits for them, and re-layouts: 6.98 us -> 23.8 us
  waiting for transfers between devices: 59.9 us -> 51.4 us
  Pallas kernels: 0 us -> 6.79 us
  between operations: 16.8 us -> 23.1 us
  matrix products: 15.9 us -> 10.7 us
    all_to_all x3 -> x1, blocking collectives: 82.4 us -> 25 us  [on_device(): lax.all_to_all(message.reshape(8, ROWS, HALF + LANES), ('c', 't', 'yl'),...]
    all_gather x1, waiting for transfers between devices: 51.4 us -> 0.02 us  [on_device(): lax.all_gather(eight.reshape(8 * ROWS, HALF + LANES), 'z', axis=0, tiled=...]
    ppermute x2 -> x13, starting transfers between devices: 6.23 us -> 44.4 us  [the longest x11 36.4 us: fetch(): return lax.ppermute(value, axes, [((i + k) % size, i) for i in range(size)])]
    ppermute x2 -> x13, waiting for transfers between devices: 2.39 us -> 36.9 us  [the longest x11 33.6 us: fetch(): return lax.ppermute(value, axes, [((i + k) % size, i) for i in range(size)])]
    all_to_all x1 -> x2, starting transfers between devices: 3.49 us -> 15.9 us  [the longest x1 12.4 us: on_device(): lax.all_to_all(jnp.concatenate([mixed, jnp.broadcast_to(for_all[None], (3...]
    all_to_all x1 -> x2, waiting for transfers between devices: 6.05 us -> 14.5 us  [the longest x1 9.1 us: on_device(): lax.all_to_all(jnp.concatenate([mixed, jnp.broadcast_to(for_all[None], (3...]
    slice x1 -> x14, local copies, waits for them, and re-layouts: 0.59 us -> 8.89 us  [the longest x4 3.41 us: on_device(): count = sum((p[-1, 0].astype(F32) for p in (rest, rest1, rest3, rest2b)))]
    pallas_call x0 -> x1, Pallas kernels: none -> 6.79 us  [on_device(): pl.pallas_call(products, out_shape=(jax.ShapeDtypeStruct((GROUP, WIDE), F...]
  transfers between devices with their start and end apart: 4 -> 16, of which waited for: 3 -> 7; matrix products, arithmetic and copies ran while one was open for 5% -> 6% of each run, Pallas kernels for 0% -> 0%
where the time goes in v2:
time: 220 us; the launch traced here: 219 us
  starting transfers between devices  60.3 us (27%)
  waiting for transfers between devices  51.4 us (23%)
  blocking collectives  39.6 us (18%)
  local copies, waits for them, and re-layouts  23.8 us (11%)
  between operations  23.1 us (10%)
  matrix products  10.7 us (5%)
  Pallas kernels  6.79 us (3%)
  other arithmetic  3.12 us (1%)
    ppermute x11, starting transfers between devices, fetch(): return lax.ppermute(value, axes, [((i + k) % size, i) for i in range(size)])  36.4 us
    ppermute x11, waiting for transfers between devices, fetch(): return lax.ppermute(value, axes, [((i + k) % size, i) for i in range(size)])  33.6 us
    all_to_all x1, blocking collectives, on_device(): lax.all_to_all(message.reshape(8, ROWS, HALF + LANES), ('c', 't', 'yl'),...  25 us
    all_to_all x1, blocking collectives, on_device(): lax.all_to_all(outgoing, DP, split_axis=0, concat_axis=0, tiled=True)  14.6 us
    all_to_all x1, starting transfers between devices, on_device(): lax.all_to_all(jnp.concatenate([mixed, jnp.broadcast_to(for_all[None], (3...  12.4 us
    all_to_all x1, waiting for transfers between devices, on_device(): lax.all_to_all(jnp.concatenate([mixed, jnp.broadcast_to(for_all[None], (3...  9.1 us
    pallas_call x1, Pallas kernels, on_device(): pl.pallas_call(products, out_shape=(jax.ShapeDtypeStruct((GROUP, WIDE), F...  6.79 us
    unnamed x27, local copies, waits for them, and re-layouts  6.75 us
  transfers between devices with their start and end apart: 16, of which 7 were waited for; matrix products, arithmetic and copies ran while one was open for 6% of the time, Pallas kernels for 0%

profile of v2, /device:TPU:1, one launch (start us, length us, event | category | flops | bytes accessed | tf_op | source)
XLA Modules:
  0.0 218.9 jit_solution(4827636274940486699)
XLA Ops:
  7.2 1.4 fusion.31
  9.9 25.0 %all_to_all.28 = bf16[8,12,2176]{2,1,0:T(8,128)(2,1)S(1)} all-to-all(bf16[8,12,2176]{2,1,0:T(8,128)(2,1)S(1)} %bitcast.52), channel_id=1, replica_groups=mesh['s'=2,'t'=2,'x'=4,'c'=2,'z'=8,'yl'=2] {'c','t','yl'}, dimensions={0} | all-to-all | bytes 835584 | tf_op jit(solution)/shard_map/all_to_all | solution.py:87
  38.6 2.1 collective-permute-start.6
  40.6 5.1 %collective-permute-start.4 = (bf16[256,512]{1,0:T(8,128)(2,1)S(1)}, bf16[256,512]{1,0:T(8,128)(2,1)S(1)}, u32[]{:S(2)}, u32[]{:S(2)}) collective-permute-start(bf16[256,512]{1,0:T(8,128)(2,1)S(1)} %bitcast.55), channel_id=1, source_target_pairs={{128,0},{256,128},{384,256},{0,384},{129,1},{257,129},{385,257},{1... | collective-permute-start | bytes 786440 | tf_op jit(solution)/shard_map/ppermute | solution.py:36
  45.7 1.9 collective-permute-start.5
  47.6 6.9 %collective-permute-done.6 = bf16[272,512]{1,0:T(8,128)(2,1)S(1)} collective-permute-done((bf16[272,512]{1,0:T(8,128)(2,1)S(1)}, bf16[272,512]{1,0:T(8,128)(2,1)S(1)}, u32[]{:S(2)}, u32[]{:S(2)}) %collective-permute-start.6) | collective-permute-done | bytes 278560 | tf_op jit(solution)/shard_map/ppermute | solution.py:36
  54.6 11.3 %collective-permute-done.4 = bf16[256,512]{1,0:T(8,128)(2,1)S(1)} collective-permute-done((bf16[256,512]{1,0:T(8,128)(2,1)S(1)}, bf16[256,512]{1,0:T(8,128)(2,1)S(1)}, u32[]{:S(2)}, u32[]{:S(2)}) %collective-permute-start.4) | collective-permute-done | bytes 262176 | tf_op jit(solution)/shard_map/ppermute | solution.py:36
  65.9 4.5 %collective-permute-start.7 = (bf16[784,512]{1,0:T(8,128)(2,1)S(1)}, bf16[784,512]{1,0:T(8,128)(2,1)S(1)}, u32[]{:S(2)}, u32[]{:S(2)}) collective-permute-start(bf16[784,512]{1,0:T(8,128)(2,1)S(1)} %pad_maximum_fusion.rest), channel_id=1, source_target_pairs={{32,0},{64,32},{96,64},{0,96},{33,1},{65,33},{97,65},{1,97},{34,2}... | collective-permute-start | bytes 2408456 | tf_op jit(solution)/shard_map/ppermute | solution.py:36
  70.4 1.9 collective-permute-start.8
  72.4 14.9 %collective-permute-done.7.rest1 = bf16[784,512]{1,0:T(8,128)(2,1)S(1)} collective-permute-done((bf16[784,512]{1,0:T(8,128)(2,1)S(1)}, bf16[784,512]{1,0:T(8,128)(2,1)S(1)}, u32[]{:S(2)}, u32[]{:S(2)}) %collective-permute-start.7) | collective-permute-done | bytes 802848 | tf_op jit(solution)/shard_map/ppermute | solution.py:36
  88.1 5.3 %collective-permute-start.10 = (bf16[400,512]{1,0:T(8,128)(2,1)}, bf16[400,512]{1,0:T(8,128)(2,1)}, u32[]{:S(2)}, u32[]{:S(2)}) collective-permute-start(bf16[400,512]{1,0:T(8,128)(2,1)} %slice.160), channel_id=1, source_target_pairs={{32,0},{64,32},{96,64},{0,96},{33,1},{65,33},{97,65},{1,97},{34,2}... | collective-permute-start | bytes 1228808 | tf_op jit(solution)/shard_map/ppermute | solution.py:36
  93.4 1.9 collective-permute-start.1
  95.4 4.6 %collective-permute-start = (bf16[256,512]{1,0:T(8,128)(2,1)S(1)}, bf16[256,512]{1,0:T(8,128)(2,1)S(1)}, u32[]{:S(2)}, u32[]{:S(2)}) collective-permute-start(bf16[256,512]{1,0:T(8,128)(2,1)S(1)} %bitcast.50), channel_id=1, source_target_pairs={{32,0},{64,32},{96,64},{0,96},{33,1},{65,33},{97,65},{1,97},{34,2}... | collective-permute-start | bytes 786440 | tf_op jit(solution)/shard_map/ppermute | solution.py:36
  101.7 1.9 collective-permute-start.9
  104.3 1.9 collective-permute-start.2
  107.4 5.3 %collective-permute-start.3 = (bf16[128,512]{1,0:T(8,128)(2,1)}, bf16[128,512]{1,0:T(8,128)(2,1)}, u32[]{:S(2)}, u32[]{:S(2)}) collective-permute-start(bf16[128,512]{1,0:T(8,128)(2,1)} %slice.156), channel_id=1, source_target_pairs={{32,0},{64,32},{96,64},{0,96},{33,1},{65,33},{97,65},{1,97},{34,2}... | collective-permute-start | bytes 393224 | tf_op jit(solution)/shard_map/ppermute | solution.py:36
  112.8 1.3 copy.39
  114.2 1.4 pad.18.down
  121.7 1.9 copy-done
  124.8 6.8 %shard_map.94 = (f32[384,1152]{1,0:T(8,128)}, bf16[384,2048]{1,0:T(8,128)(2,1)S(1)}, bf16[384,128]{1,0:T(8,128)(2,1)S(1)}, bf16[2048,1152]{1,0:T(8,128)(2,1)}) custom-call(s32[3]{0:T(128)S(1)} %pad_add_fusion.1.place, bf16[8,2,48,2176]{3,2,1,0:T(8,128)(2,1)S(1)} %bitcast.47, bf16[256,512]{1,0:T(8,128)(2,1)S(1)} %bitcast.51, ...), custom_call_target="tpu_custom_call" | custom-call | flops 1811939328 | bytes 20000000 | tf_op jit(solution)/shard_map/pallas_call | solution.py:119
  131.6 1.2 copy-done.4
  132.8 4.3 %collective-permute-start.11 = (f32[384,1152]{1,0:T(8,128)}, f32[384,1152]{1,0:T(8,128)}, u32[]{:S(2)}, u32[]{:S(2)}) collective-permute-start(f32[384,1152]{1,0:T(8,128)} %get-tuple-element.13), channel_id=1, source_target_pairs={{0,16},{16,0},{1,17},{17,1},{2,18},{18,2},{3,19},{19,3},{4,20},{20... | collective-permute-start | bytes 5308424 | tf_op jit(solution)/shard_map/ppermute | solution.py:136
  137.5 3.2 %collective-permute-done.11 = f32[384,1152]{1,0:T(8,128)} collective-permute-done((f32[384,1152]{1,0:T(8,128)}, f32[384,1152]{1,0:T(8,128)}, u32[]{:S(2)}, u32[]{:S(2)}) %collective-permute-start.11) | collective-permute-done | bytes 1769504 | tf_op jit(solution)/shard_map/ppermute | solution.py:136
  140.8 5.6 %fusion.36 = (bf16[384,1152]{1,0:T(8,128)(2,1)S(1)}, f32[384,1152]{1,0:T(8,128)S(1)}) fusion(f32[384,1152]{1,0:T(8,128)} %collective-permute-done.11, bf16[384,2048]{1,0:T(8,128)(2,1)} %copy-done.4, bf16[2048,1152]{1,0:T(8,128)(2,1)} %get-tuple-element.12), kind=kOutput, calls=%fused_computation.81 | convolution fusion | flops 1812824064 | bytes 10715136 | tf_op jit(solution)/shard_map/dot_general | solution.py:137
  148.7 1.3 slice.172
  151.9 12.4 %all-to-all-start.1 = ((f32[32,1,512]{2,1,0:T(1,128)}), f32[32,1,512]{2,1,0:T(1,128)S(1)}, u32[]{:S(2)}, u32[]{:S(2)}) async-start(f32[32,1,512]{2,1,0:T(1,128)} %copy.43), calls=%async_computation.1 | async-start | bytes 131072 | tf_op jit(solution)/shard_map/all_to_all | solution.py:172
  164.3 9.1 %all-to-all-done.1 = f32[32,1,512]{2,1,0:T(1,128)S(1)} async-done(((f32[32,1,512]{2,1,0:T(1,128)}), f32[32,1,512]{2,1,0:T(1,128)S(1)}, u32[]{:S(2)}, u32[]{:S(2)}) %all-to-all-start.1) | async-done | bytes 65568 | tf_op jit(solution)/shard_map/all_to_all | solution.py:172
  176.2 2.0 fusion.4
  178.2 3.7 %collective-permute-start.12 = (bf16[1,384]{1,0:T(2,128)(2,1)S(1)}, bf16[1,384]{1,0:T(2,128)(2,1)S(1)}, u32[]{:S(2)}, u32[]{:S(2)}) collective-permute-start(bf16[1,384]{1,0:T(2,128)(2,1)S(1)} %broadcast_in_dim.86), channel_id=1, source_target_pairs={{0,16},{16,0},{1,17},{17,1},{2,18},{18,2},{3,19},{19,3},{4,20},{20... | collective-permute-start | bytes 2312 | tf_op jit(solution)/shard_map/ppermute | solution.py:184
  184.2 14.6 %all_to_all.29 = f32[32,1,768]{2,1,0:T(1,128)S(1)} all-to-all(f32[32,1,768]{2,1,0:T(1,128)S(1)} %copy.52), channel_id=1, replica_groups=mesh['s'=2,'t'=2,'x'=4,'c'=2,'z'=8,'yl'=2] {'s','t','x','c'}, dimensions={0} | all-to-all | bytes 196608 | tf_op jit(solution)/shard_map/all_to_all | solution.py:206
  199.5 3.5 %all-to-all-start.3 = ((f32[16,2,128]{2,1,0:T(2,128)}), f32[16,2,128]{2,1,0:T(2,128)S(1)}, u32[]{:S(2)}, u32[]{:S(2)}) async-start(f32[16,2,128]{2,1,0:T(2,128)} %broadcast_in_dim.90), calls=%async_computation.3 | async-start | bytes 32768 | tf_op jit(solution)/shard_map/all_to_all | solution.py:212
  204.9 5.4 %all-to-all-done.3 = f32[16,2,128]{2,1,0:T(2,128)S(1)} async-done(((f32[16,2,128]{2,1,0:T(2,128)}), f32[16,2,128]{2,1,0:T(2,128)S(1)}, u32[]{:S(2)}, u32[]{:S(2)}) %all-to-all-start.3) | async-done | bytes 16416 | tf_op jit(solution)/shard_map/all_to_all | solution.py:212
  (119 shorter events, 22.2 us)
Async XLA Ops:
  7.2 114.5 %all-gather.2.cloned.1.call-start = ((), (), s32[]{:S(2)}) async-start(), calls=%async_computation.4 | async-start | bytes 3760128 | tf_op jit(solution)/shard_map/all_gather | solution.py:91
  9.9 28.6 %copy-start.8 = (bf16[2,128,896]{2,1,0:T(8,128)(2,1)S(1)}, bf16[2,128,896]{2,1,0:T(8,128)(2,1)}, u32[]{:S(2)}) copy-start(bf16[2,128,896]{2,1,0:T(8,128)(2,1)} %param.10) | copy-start | bytes 1376260
  38.6 16.0 %collective-permute-start.6 = (bf16[272,512]{1,0:T(8,128)(2,1)S(1)}, bf16[272,512]{1,0:T(8,128)(2,1)S(1)}, u32[]{:S(2)}, u32[]{:S(2)}) collective-permute-start(bf16[272,512]{1,0:T(8,128)(2,1)S(1)} %concatenate.28), channel_id=1, source_target_pairs={{256,0},{384,128},{0,256},{128,384},{257,1},{385,129},{1,257},{129... | collective-permute-start | bytes 835592 | tf_op jit(solution)/shard_map/ppermute | solution.py:36
  40.6 25.2 %collective-permute-start.4 = (bf16[256,512]{1,0:T(8,128)(2,1)S(1)}, bf16[256,512]{1,0:T(8,128)(2,1)S(1)}, u32[]{:S(2)}, u32[]{:S(2)}) collective-permute-start(bf16[256,512]{1,0:T(8,128)(2,1)S(1)} %bitcast.55), channel_id=1, source_target_pairs={{128,0},{256,128},{384,256},{0,384},{129,1},{257,129},{385,257},{1... | collective-permute-start | bytes 786440 | tf_op jit(solution)/shard_map/ppermute | solution.py:36
  45.7 20.1 %collective-permute-start.5 = (bf16[256,512]{1,0:T(8,128)(2,1)S(1)}, bf16[256,512]{1,0:T(8,128)(2,1)S(1)}, u32[]{:S(2)}, u32[]{:S(2)}) collective-permute-start(bf16[256,512]{1,0:T(8,128)(2,1)S(1)} %bitcast.56), channel_id=1, source_target_pairs={{384,0},{0,128},{128,256},{256,384},{385,1},{1,129},{129,257},{257... | collective-permute-start | bytes 786440 | tf_op jit(solution)/shard_map/ppermute | solution.py:36
  54.6 58.3 %copy-start.9 = (bf16[4096,32]{0,1:T(8,128)(2,1)S(1)}, bf16[4096,32]{0,1:T(8,128)(2,1)}, u32[]{:S(2)}) copy-start(bf16[4096,32]{0,1:T(8,128)(2,1)} %param.11) | copy-start | bytes 786436
  65.9 21.4 %collective-permute-start.7 = (bf16[784,512]{1,0:T(8,128)(2,1)S(1)}, bf16[784,512]{1,0:T(8,128)(2,1)S(1)}, u32[]{:S(2)}, u32[]{:S(2)}) collective-permute-start(bf16[784,512]{1,0:T(8,128)(2,1)S(1)} %pad_maximum_fusion.rest), channel_id=1, source_target_pairs={{32,0},{64,32},{96,64},{0,96},{33,1},{65,33},{97,65},{1,97},{34,2}... | collective-permute-start | bytes 2408456 | tf_op jit(solution)/shard_map/ppermute | solution.py:36
  70.4 29.5 %collective-permute-start.8 = (bf16[784,512]{1,0:T(8,128)(2,1)S(1)}, bf16[784,512]{1,0:T(8,128)(2,1)S(1)}, u32[]{:S(2)}, u32[]{:S(2)}) collective-permute-start(bf16[784,512]{1,0:T(8,128)(2,1)S(1)} %pad_maximum_fusion.rest), channel_id=1, source_target_pairs={{96,0},{0,32},{32,64},{64,96},{97,1},{1,33},{33,65},{65,97},{98,2}... | collective-permute-start | bytes 2408456 | tf_op jit(solution)/shard_map/ppermute | solution.py:36
  88.1 31.7 %collective-permute-start.10 = (bf16[400,512]{1,0:T(8,128)(2,1)}, bf16[400,512]{1,0:T(8,128)(2,1)}, u32[]{:S(2)}, u32[]{:S(2)}) collective-permute-start(bf16[400,512]{1,0:T(8,128)(2,1)} %slice.160), channel_id=1, source_target_pairs={{32,0},{64,32},{96,64},{0,96},{33,1},{65,33},{97,65},{1,97},{34,2}... | collective-permute-start | bytes 1228808 | tf_op jit(solution)/shard_map/ppermute | solution.py:36
  93.4 10.2 %collective-permute-start.1 = (bf16[256,512]{1,0:T(8,128)(2,1)S(1)}, bf16[256,512]{1,0:T(8,128)(2,1)S(1)}, u32[]{:S(2)}, u32[]{:S(2)}) collective-permute-start(bf16[256,512]{1,0:T(8,128)(2,1)S(1)} %bitcast.49), channel_id=1, source_target_pairs={{96,0},{0,32},{32,64},{64,96},{97,1},{1,33},{33,65},{65,97},{98,2}... | collective-permute-start | bytes 786440 | tf_op jit(solution)/shard_map/ppermute | solution.py:36
  95.4 11.4 %collective-permute-start = (bf16[256,512]{1,0:T(8,128)(2,1)S(1)}, bf16[256,512]{1,0:T(8,128)(2,1)S(1)}, u32[]{:S(2)}, u32[]{:S(2)}) collective-permute-start(bf16[256,512]{1,0:T(8,128)(2,1)S(1)} %bitcast.50), channel_id=1, source_target_pairs={{32,0},{64,32},{96,64},{0,96},{33,1},{65,33},{97,65},{1,97},{34,2}... | collective-permute-start | bytes 786440 | tf_op jit(solution)/shard_map/ppermute | solution.py:36
  100.0 0.9 copy-start.2
  101.7 20.0 %collective-permute-start.9 = (bf16[384,512]{1,0:T(8,128)(2,1)}, bf16[384,512]{1,0:T(8,128)(2,1)}, u32[]{:S(2)}, u32[]{:S(2)}) collective-permute-start(bf16[384,512]{1,0:T(8,128)(2,1)} %slice.159), channel_id=1, source_target_pairs={{96,0},{0,32},{32,64},{64,96},{97,1},{1,33},{33,65},{65,97},{98,2}... | collective-permute-start | bytes 1179656 | tf_op jit(solution)/shard_map/ppermute | solution.py:36
  104.3 17.3 %collective-permute-start.2 = (bf16[128,512]{1,0:T(8,128)(2,1)}, bf16[128,512]{1,0:T(8,128)(2,1)}, u32[]{:S(2)}, u32[]{:S(2)}) collective-permute-start(bf16[128,512]{1,0:T(8,128)(2,1)} %slice.155), channel_id=1, source_target_pairs={{96,0},{0,32},{32,64},{64,96},{97,1},{1,33},{33,65},{65,97},{98,2}... | collective-permute-start | bytes 393224 | tf_op jit(solution)/shard_map/ppermute | solution.py:36
  107.4 14.2 %collective-permute-start.3 = (bf16[128,512]{1,0:T(8,128)(2,1)}, bf16[128,512]{1,0:T(8,128)(2,1)}, u32[]{:S(2)}, u32[]{:S(2)}) collective-permute-start(bf16[128,512]{1,0:T(8,128)(2,1)} %slice.156), channel_id=1, source_target_pairs={{32,0},{64,32},{96,64},{0,96},{33,1},{65,33},{97,65},{1,97},{34,2}... | collective-permute-start | bytes 393224 | tf_op jit(solution)/shard_map/ppermute | solution.py:36
  121.7 1.9 copy-start
  123.7 1.1 copy-start.3
  124.8 12.3 %copy-start.11 = (bf16[896]{0:T(1024)(128)(2,1)S(1)}, bf16[896]{0:T(1024)(128)(2,1)}, u32[]{:S(2)}) copy-start(bf16[896]{0:T(1024)(128)(2,1)} %param.13) | copy-start | bytes 5380
  124.8 12.4 %copy-start.10 = (bf16[32,896]{1,0:T(8,128)(2,1)S(1)}, bf16[32,896]{1,0:T(8,128)(2,1)}, u32[]{:S(2)}) copy-start(bf16[32,896]{1,0:T(8,128)(2,1)} %param.12) | copy-start | bytes 172036
  131.6 1.2 copy-start.4
  132.8 8.0 %collective-permute-start.11 = (f32[384,1152]{1,0:T(8,128)}, f32[384,1152]{1,0:T(8,128)}, u32[]{:S(2)}, u32[]{:S(2)}) collective-permute-start(f32[384,1152]{1,0:T(8,128)} %get-tuple-element.13), channel_id=1, source_target_pairs={{0,16},{16,0},{1,17},{17,1},{2,18},{18,2},{3,19},{19,3},{4,20},{20... | collective-permute-start | bytes 5308424 | tf_op jit(solution)/shard_map/ppermute | solution.py:136
  146.6 1.0 copy-start.7
  147.6 3.0 %copy-start.5 = (f32[384,512]{1,0:T(8,128)}, f32[384,512]{1,0:T(8,128)S(1)}, u32[]{:S(2)}) copy-start(f32[384,512]{1,0:T(8,128)S(1)} %get-tuple-element.26) | copy-start | bytes 2359300
  151.9 21.6 %all-to-all-start.1 = ((f32[32,1,512]{2,1,0:T(1,128)}), f32[32,1,512]{2,1,0:T(1,128)S(1)}, u32[]{:S(2)}, u32[]{:S(2)}) async-start(f32[32,1,512]{2,1,0:T(1,128)} %copy.43), calls=%async_computation.1 | async-start | bytes 131072 | tf_op jit(solution)/shard_map/all_to_all | solution.py:172
  176.1 5.9 %copy-start.6 = (f32[384,512]{1,0:T(8,128)S(1)}, f32[384,512]{1,0:T(8,128)}, u32[]{:S(2)}) copy-start(f32[384,512]{1,0:T(8,128)} %copy-done.5) | copy-start | bytes 2359300
  176.2 7.2 %copy-start.1 = (bf16[768,2176]{1,0:T(8,128)(2,1)S(1)}, bf16[768,2176]{1,0:T(8,128)(2,1)}, u32[]{:S(2)}) copy-start(bf16[768,2176]{1,0:T(8,128)(2,1)} %all-gather.2.cloned.1.call-done) | copy-start | bytes 10027012
  178.2 4.9 %collective-permute-start.12 = (bf16[1,384]{1,0:T(2,128)(2,1)S(1)}, bf16[1,384]{1,0:T(2,128)(2,1)S(1)}, u32[]{:S(2)}, u32[]{:S(2)}) collective-permute-start(bf16[1,384]{1,0:T(2,128)(2,1)S(1)} %broadcast_in_dim.86), channel_id=1, source_target_pairs={{0,16},{16,0},{1,17},{17,1},{2,18},{18,2},{3,19},{19,3},{4,20},{20... | collective-permute-start | bytes 2312 | tf_op jit(solution)/shard_map/ppermute | solution.py:184
  199.5 10.8 %all-to-all-start.3 = ((f32[16,2,128]{2,1,0:T(2,128)}), f32[16,2,128]{2,1,0:T(2,128)S(1)}, u32[]{:S(2)}, u32[]{:S(2)}) async-start(f32[16,2,128]{2,1,0:T(2,128)} %broadcast_in_dim.90), calls=%async_computation.3 | async-start | bytes 32768 | tf_op jit(solution)/shard_map/all_to_all | solution.py:212
Sparse Core Ops, SparseCore 0:
  35.9 49.2 all-gather.1

commit v3 on v2

v3 whole, which is shorter than its diff:
```python
import functools

import jax
import jax.numpy as jnp
from jax import lax
from jax.experimental import pallas as pl
from jax.experimental.pallas import tpu as pltpu
from jax.sharding import Mesh, PartitionSpec as P

SEQS = 4
ROWS = 12
RANK = 16
WIDTH = 4096
DPO_BETA = 0.1
LOSS_SCALE = 1024.0
F32 = jnp.float32
BF16 = jnp.bfloat16

AXES = ("s", "t", "x", "c", "z", "yl")
SIZES = (2, 2, 4, 2, 8, 2)
DP = ("s", "t", "x", "c")
BLK = ("z", "yl")
YH = ("s", "t")
SWAP = [(0, 1), (1, 0)]

SLICE = 128
HALF = WIDTH // 2
LANES = 128
COLS = 512
SKIP = 384
GROUP = 384
BLOCKS = GROUP // ROWS
WIDE = 2 * COLS + LANES
CONTRACT_LAST = (((1,), (1,)), ((), ()))


def fetch(value, axes, size, k):
    return lax.ppermute(value, axes, [((i + k) % size, i) for i in range(size)])


def swapped(value, axis, index):
    far = lax.ppermute(value, axis, SWAP)
    return jnp.where(index == 0, jnp.stack([value, far]), jnp.stack([far, value]))


def split(value, terms):
    parts = []
    for _ in range(terms):
        parts.append(value.astype(BF16))
        value = value - parts[-1].astype(F32)
    return parts


def dot(a, b, dims=(((1,), (0,)), ((), ()))):
    return lax.dot_general(a, b, dims, preferred_element_type=F32)


def source_of(place, k, j):
    return lax.rem(place[0] + k, 4) * 4 + lax.rem(place[1] + j, 4)


def down_rows(down, place, source):
    return down[pl.ds(pl.multiple_of((source * 2 + place[2]) * SLICE, SLICE), SLICE), :]


def columns_of(source):
    return pl.ds(pl.multiple_of(source * SLICE, SLICE), SLICE)


def early_products(place, tok, own, own1, own3, own2g, own2u, rest, rest1, rest3, down, acc, w, lined):
    pieces = []
    for j, ref in ((0, own), (1, own1), (3, own3)):
        pieces.append((0, j, ref[0:SLICE, :], ref[SLICE : 2 * SLICE, :]))
    pieces.append((0, 2, own2g[...], own2u[...]))
    for j, ref in ((0, rest), (1, rest1), (3, rest3)):
        for at, k in enumerate((1, 3, 2)):
            begin = 2 * at * SLICE
            pieces.append((k, j, ref[begin : begin + SLICE, :], ref[begin + SLICE : begin + 2 * SLICE, :]))
    for at, (k, j, gate, up) in enumerate(pieces):
        source = source_of(place, k, j)
        w[at * SLICE : (at + 1) * SLICE, 0:COLS] = gate
        w[at * SLICE : (at + 1) * SLICE, COLS : 2 * COLS] = up
        w[at * SLICE : (at + 1) * SLICE, 2 * COLS : WIDE] = down_rows(down, place, source)
        lined[:, at * SLICE : (at + 1) * SLICE] = tok[:, columns_of(source)]
    for n in range(3):
        part = slice(n * GROUP, (n + 1) * GROUP)
        acc[:, part] = dot(lined[...], w[:, part])


def late_products(far, place, tok, acc, rest2a, rest2b, down, out, w, lined):
    core = place[2]
    half = 1 - core if far else core
    rows = pl.ds(pl.multiple_of(half * GROUP, GROUP), GROUP)
    pieces = (
        (1, rest2a[0:SLICE, :], rest2a[SLICE : 2 * SLICE, :]),
        (3, rest2a[2 * SLICE : 3 * SLICE, :], rest2b[0:SLICE, :]),
        (2, rest2b[SLICE : 2 * SLICE, :], rest2b[2 * SLICE : 3 * SLICE, :]),
    )
    for at, (k, gate, up) in enumerate(pieces):
        source = source_of(place, k, 2)
        w[at * SLICE : (at + 1) * SLICE, 0:COLS] = gate
        w[at * SLICE : (at + 1) * SLICE, COLS : 2 * COLS] = up
        w[at * SLICE : (at + 1) * SLICE, 2 * COLS : WIDE] = down_rows(down, place, source)
        lined[:, at * SLICE : (at + 1) * SLICE] = tok[rows, columns_of(source)]
    for n in range(3):
        part = slice(n * GROUP, (n + 1) * GROUP)
        out[:, part] = acc[rows, part] + dot(lined[...], w[:, part])


def score(place, near, partner, b_gate, b_up, readout, signs, count, message, gate_high, gate_low, up_high,
          up_low, low_t):
    low = near[:, 2 * COLS : WIDE] + partner[:, 2 * COLS : WIDE]
    low_b = low.astype(BF16)
    gate_ref = near[:, 0:COLS] + partner[:, 0:COLS]
    up_ref = near[:, COLS : 2 * COLS] + partner[:, COLS : 2 * COLS]
    gate_pol = gate_ref + dot(low_b, b_gate[...])
    up_pol = up_ref + dot(low_b, b_up[...])
    sig_ref = jax.nn.sigmoid(gate_ref)
    sig_pol = jax.nn.sigmoid(gate_pol)
    act_pol = gate_pol * sig_pol
    read = readout[...].astype(F32)
    change = act_pol * up_pol - gate_ref * sig_ref * up_ref
    k_gate = read * sig_pol * (1.0 + gate_pol * (1.0 - sig_pol)) * up_pol
    k_up = read * act_pol
    read_b = jnp.broadcast_to(readout[...], (8, COLS))
    change_row = sum(dot(read_b, part, CONTRACT_LAST) for part in split(change, 3))
    sign = signs[place[2]]
    gaps = sum(dot(part, sign, CONTRACT_LAST) for part in split(change_row, 3))
    message[:, GROUP : GROUP + LANES] = jnp.broadcast_to(gaps[0:1, :] + count[...], (2 * RANK, LANES))
    high, rest = split(k_gate, 2)
    gate_high[...], gate_low[...] = high, rest
    mixed = dot(b_gate[0 : 2 * RANK, :], high, CONTRACT_LAST) + dot(b_gate[0 : 2 * RANK, :], rest, CONTRACT_LAST)
    high, rest = split(k_up, 2)
    up_high[...], up_low[...] = high, rest
    mixed_up = dot(b_up[0 : 2 * RANK, :], high, CONTRACT_LAST) + dot(b_up[0 : 2 * RANK, :], rest, CONTRACT_LAST)
    message[:, 0:GROUP] = mixed + mixed_up
    low_t[...] = low_b.astype(F32).T[0 : 2 * RANK, :]


def close(place, arrived, signs, valid, low_t, gate_high, gate_low, up_high, up_low, tok, out, total_out):
    core = place[2]
    totals = [jnp.sum(arrived[h], axis=0, keepdims=True) for h in range(2)]
    tails = [total[:, GROUP : GROUP + LANES] for total in totals]
    pair_total = jnp.maximum(tails[0][:, 64:65] + tails[1][:, 64:65], 1.0)
    logs, cotangents, terms = 0.0, [], []
    for h in range(2):
        logit = DPO_BETA * tails[h]
        logs = logs + jnp.sum(
            valid[h] * (jnp.minimum(logit, 0.0) - jnp.log1p(jnp.exp(-jnp.abs(logit)))), axis=1, keepdims=True
        )
        scaled = -LOSS_SCALE * DPO_BETA * valid[h] * jax.nn.sigmoid(-logit) / pair_total
        scaled = jnp.broadcast_to(scaled, (8, LANES))
        cotangent = sum(dot(part, signs[h]) for part in split(scaled, 3))
        cotangents.append(cotangent[0:1, :])
        projected = jnp.broadcast_to(totals[h][:, 0:GROUP], (8, GROUP)) * cotangent
        terms.append(dot(projected.astype(BF16), tok[h * GROUP : (h + 1) * GROUP, 0:HALF]))
    grad_a = (terms[0] + terms[1])[0:1, :]
    own = jnp.where(core == 0, cotangents[0], cotangents[1])
    high, rest = split(low_t[...] * own, 2)
    gate = dot(high[0:RANK], gate_high[...]) + dot(high[0:RANK], gate_low[...]) + dot(rest[0:RANK], gate_high[...])
    up = dot(high[RANK:], up_high[...]) + dot(high[RANK:], up_low[...]) + dot(rest[RANK:], up_high[...])
    out[0:RANK, 0:COLS] = gate
    out[RANK : 2 * RANK, 0:COLS] = up
    line = lax.broadcasted_iota(jnp.int32, (2 * RANK, SLICE), 0)
    slices = jnp.zeros((2 * RANK, SLICE), F32)
    for i in range(RANK):
        here = jnp.broadcast_to(grad_a[:, i * SLICE : (i + 1) * SLICE], (2 * RANK, SLICE))
        slices = jnp.where(line == 2 * i + core, here, slices)
    out[:, COLS : COLS + SLICE] = slices
    out[:, COLS + SLICE :] = jnp.broadcast_to(0.5 * logs, (2 * RANK, LANES))
    total_out[...] = jnp.broadcast_to(pair_total, (8, LANES))


def kernel(function, shapes, scratch, arguments, flops):
    vmem = pl.BlockSpec(memory_space=pltpu.VMEM)
    smem = pl.BlockSpec(memory_space=pltpu.SMEM)
    return pl.pallas_call(
        function,
        out_shape=tuple(jax.ShapeDtypeStruct(*s) for s in shapes),
        in_specs=[smem] + [vmem] * (len(arguments) - 1),
        out_specs=(vmem,) * len(shapes),
        scratch_shapes=[pltpu.VMEM(*s) for s in scratch],
        compiler_params=pltpu.CompilerParams(vmem_limit_bytes=48 * 1024 * 1024),
        cost_estimate=pl.CostEstimate(flops=flops, bytes_accessed=10_000_000, transcendentals=0),
    )(*arguments)


def on_device(tokens, sequence_labels, response_mask, frozen, down, up, readout):
    s, t, x, core, yl = (lax.axis_index(a) for a in ("s", "t", "x", "c", "yl"))
    code = jnp.where(response_mask > 0, sequence_labels, SEQS)

    by_core = tokens.reshape(ROWS, WIDTH // (2 * SLICE), 2, SLICE).transpose(2, 0, 1, 3).reshape(2, ROWS, HALF)
    code_lanes = jnp.pad(code.reshape(ROWS, 1).astype(BF16), ((0, 0), (0, LANES - 1)))
    keep = jnp.concatenate([jnp.where(core == 0, by_core[0], by_core[1]), code_lanes], axis=1)
    give = jnp.concatenate([jnp.where(core == 0, by_core[1], by_core[0]), code_lanes], axis=1)
    take = lax.ppermute(give, "c", SWAP)
    pair = jnp.where(
        core == 0, jnp.concatenate([keep, take], axis=0), jnp.concatenate([take, keep], axis=0)
    )
    eight = swapped(swapped(pair, "yl", yl), "t", t)
    tok = lax.all_gather(eight.reshape(8 * ROWS, HALF + LANES), "z", axis=0, tiled=True)

    has = [jnp.max((code == q).astype(F32)) for q in range(SEQS)]
    count = has[0] * has[1] + has[2] * has[3]

    low_half, high_half = frozen[:, :, :COLS], frozen[:, :, SKIP:]
    mine = jnp.where(t == 0, low_half, high_half).reshape(2 * SLICE, COLS)
    other = jnp.where(t == 0, high_half, low_half).reshape(2 * SLICE, COLS)
    count_rows = jnp.broadcast_to(count.astype(BF16), (16, COLS))
    y1 = fetch(other, YH, 4, 1)
    y3 = fetch(other, YH, 4, 3)
    y2 = fetch(jnp.concatenate([mine, count_rows], axis=0), YH, 4, 2)
    own1 = fetch(mine, "x", 4, 1)
    own3 = fetch(mine, "x", 4, 3)
    y1, y2, y3, own1, own3 = lax.optimization_barrier((y1, y2, y3, own1, own3))
    rest = jnp.concatenate([y1, y3, y2[: 2 * SLICE], y2[2 * SLICE :] + count_rows], axis=0)
    rest1 = fetch(rest, "x", 4, 1)
    rest3 = fetch(rest, "x", 4, 3)
    own2g = fetch(own3[:SLICE], "x", 4, 3)
    own2u = fetch(own1[SLICE:], "x", 4, 1)
    rest2a = fetch(rest3[: 3 * SLICE], "x", 4, 3)
    rest2b = fetch(rest1[3 * SLICE :], "x", 4, 1)
    count = sum(p[-1, 0].astype(F32) for p in (rest, rest1, rest3, rest2b))
    count_lanes = jnp.where(jnp.arange(LANES) == 64, count, 0.0).reshape(1, LANES)

    place = jnp.stack([2 * s + t, x, core]).astype(jnp.int32)
    down_wide = jnp.pad(down, ((0, 0), (0, LANES - 2 * RANK)))
    (acc,) = kernel(
        early_products,
        [((2 * GROUP, WIDE), F32)],
        [((13 * SLICE, WIDE), BF16), ((2 * GROUP, 13 * SLICE), BF16)],
        (place, tok, mine, own1, own3, own2g, own2u, rest, rest1, rest3, down_wide),
        4 * GROUP * 13 * SLICE * WIDE,
    )
    late = [((3 * SLICE, WIDE), BF16), ((GROUP, 3 * SLICE), BF16)]
    late_in = (place, tok, acc, rest2a, rest2b, down_wide)
    late_flops = 2 * GROUP * 3 * SLICE * WIDE
    (far,) = kernel(functools.partial(late_products, True), [((GROUP, WIDE), F32)], late, late_in, late_flops)
    partner = lax.ppermute(far, "c", SWAP)
    (near,) = kernel(functools.partial(late_products, False), [((GROUP, WIDE), F32)], late, late_in, late_flops)

    units = jnp.where(t == 0, up[:, :COLS], up[:, SKIP:])
    b_gate = jnp.pad(units[:RANK], ((0, LANES - RANK), (0, 0)))
    b_up = jnp.pad(units[RANK:], ((RANK, LANES - 2 * RANK), (0, 0)))
    shared = (jnp.arange(COLS) >= 2 * COLS - readout.shape[0]).astype(BF16)
    read = jnp.where(t == 0, readout[:COLS], readout[SKIP:] * shared).reshape(1, COLS)

    codes = tok[:, HALF].astype(jnp.int32).reshape(2, GROUP)
    pair_of = jnp.arange(LANES, dtype=jnp.int32)
    block_of = jnp.arange(GROUP, dtype=jnp.int32) // ROWS
    inside = (pair_of[:, None] // 2 == block_of[None, :])[None]
    chosen = inside & (codes[:, None, :] == 2 * (pair_of % 2)[None, :, None])
    rejected = inside & (codes[:, None, :] == 2 * (pair_of % 2)[None, :, None] + 1)
    signs = chosen.astype(BF16) - rejected.astype(BF16)
    valid = (jnp.any(chosen, axis=2) & jnp.any(rejected, axis=2)).astype(F32).reshape(2, 1, LANES)

    message, gate_high, gate_low, up_high, up_low, low_t = kernel(
        score,
        [((2 * RANK, GROUP + LANES), F32)] + [((GROUP, COLS), BF16)] * 4 + [((2 * RANK, GROUP), F32)],
        [],
        (place, near, partner, b_gate, b_up, read, signs, count_lanes),
        8 * GROUP * COLS * LANES,
    )
    arrived = lax.all_to_all(
        jnp.broadcast_to(message[None], (2, 2 * RANK, GROUP + LANES)).reshape(4 * RANK, -1),
        ("c", "t", "z", "yl"), split_axis=0, concat_axis=0, tiled=True,
    ).reshape(2, 2 * RANK, -1)
    outgoing, pair_total = kernel(
        close,
        [((2 * RANK, COLS + SLICE + LANES), F32), ((8, LANES), F32)],
        [],
        (place, arrived, signs, valid, low_t, gate_high, gate_low, up_high, up_low, tok),
        16 * GROUP * HALF * 2,
    )

    arrived = lax.all_to_all(outgoing, DP, split_axis=0, concat_axis=0, tiled=True)
    summed = jnp.sum(arrived.reshape(2, 2, 8, -1), axis=(0, 2))
    spare = readout.shape[0] - COLS
    grad_b = jnp.pad(summed[0, :COLS], (0, spare)) + jnp.pad(summed[1, :COLS], (spare, 0))
    columns = summed[:, COLS : COLS + SLICE]
    log_total = summed[0, COLS + SLICE]
    grad_a = lax.all_to_all(
        jnp.broadcast_to(columns[None], (16, 2, SLICE)), BLK, split_axis=0, concat_axis=0
    )
    grad_a = grad_a.transpose(2, 1, 0).reshape(SLICE, 2 * RANK)
    return -log_total / pair_total[0, 0], grad_a, grad_b[None]


def solution(mesh):
    fine = Mesh(mesh.devices.reshape(SIZES), AXES)
    in_specs = (
        P(AXES, None),
        P(AXES, None),
        P(AXES, None),
        P(None, DP, BLK),
        P(),
        P(None, BLK),
        P(BLK),
    )
    out_specs = (P(), P(DP, None), P(DP, BLK))
    return jax.shard_map(
        on_device, mesh=fine, in_specs=in_specs, out_specs=out_specs, check_vma=False
    )
```

time: 220 us -> 225 us (1.023)
  blocking collectives: 39.6 us -> 0 us
  waiting for transfers between devices: 51.4 us -> 70.1 us
  Pallas kernels: 6.79 us -> 22.3 us
  starting transfers between devices: 60.3 us -> 73.7 us
  matrix products: 10.7 us -> 0 us
  local copies, waits for them, and re-layouts: 23.8 us -> 30.1 us
    all_to_all x2 -> x0, blocking collectives: 39.6 us -> none  [the longest x1 25 us: on_device(): lax.all_to_all(message.reshape(8, ROWS, HALF + LANES), ('c', 't', 'yl'),...]
    pallas_call x1 -> x5, Pallas kernels: 6.79 us -> 22.3 us  [kernel(): pl.pallas_call(function, out_shape=tuple((jax.ShapeDtypeStruct(*s) for s...]
    ppermute x2 -> x4, waiting for transfers between devices: 3.24 us -> 17.2 us  [the longest x2 16.4 us: swapped(): far = lax.ppermute(value, axis, SWAP)]
    dot_general x8 -> x0, matrix products: 10.7 us -> none  [the longest x1 5.56 us: on_device(): both = jnp.dot(near_x, w, preferred_element_type=F32) + from_partner]
    all_to_all x1 -> x2, waiting for transfers between devices: 9.1 us -> 18.9 us  [the longest x1 9.73 us: on_device(): lax.all_to_all(outgoing, DP, split_axis=0, concat_axis=0, tiled=True)]
    ppermute x2 -> x4, starting transfers between devices: 8.01 us -> 16.9 us  [the longest x1 8.79 us: on_device(): take = lax.ppermute(give, 'c', SWAP)]
    all_to_all x1 -> x2, starting transfers between devices: 12.4 us -> 20.8 us  [the longest x1 13.6 us: on_device(): lax.all_to_all(jnp.broadcast_to(message[None], (2, 2 * RANK, GROUP + LANE...]
    unnamed x27 -> x59, local copies, waits for them, and re-layouts: 6.75 us -> 14.7 us
  transfers between devices with their start and end apart: 16 -> 19, of which waited for: 7 -> 10; matrix products, arithmetic and copies ran while one was open for 6% -> 6% of each run, Pallas kernels for 0% -> 5%
where the time goes in v3:
time: 225 us; the launch traced here: 224 us
  starting transfers between devices  73.7 us (33%)
  waiting for transfers between devices  70.1 us (31%)
  local copies, waits for them, and re-layouts  30.1 us (13%)
  Pallas kernels  22.3 us (10%)
  between operations  22.3 us (10%)
  other arithmetic  5.23 us (2%)
    ppermute x11, starting transfers between devices, fetch(): return lax.ppermute(value, axes, [((i + k) % size, i) for i in range(size)])  32.5 us
    ppermute x11, waiting for transfers between devices, fetch(): return lax.ppermute(value, axes, [((i + k) % size, i) for i in range(size)])  29 us
    pallas_call x5, Pallas kernels, kernel(): pl.pallas_call(function, out_shape=tuple((jax.ShapeDtypeStruct(*s) for s...  22.3 us
    ppermute x2, waiting for transfers between devices, swapped(): far = lax.ppermute(value, axis, SWAP)  16.4 us
    unnamed x59, local copies, waits for them, and re-layouts  14.7 us
    all_to_all x1, starting transfers between devices, on_device(): lax.all_to_all(jnp.broadcast_to(message[None], (2, 2 * RANK, GROUP + LANE...  13.6 us
    all_to_all x1, waiting for transfers between devices, on_device(): lax.all_to_all(outgoing, DP, split_axis=0, concat_axis=0, tiled=True)  9.73 us
    all_to_all x1, waiting for transfers between devices, on_device(): lax.all_to_all(jnp.broadcast_to(message[None], (2, 2 * RANK, GROUP + LANE...  9.14 us
  transfers between devices with their start and end apart: 19, of which 10 were waited for; matrix products, arithmetic and copies ran while one was open for 6% of the time, Pallas kernels for 5%

profile of v3, /device:TPU:1, one launch (start us, length us, event | category | flops | bytes accessed | tf_op | source)
XLA Modules:
  0.0 223.8 jit_solution(668049411530559108)
XLA Ops:
  9.9 8.8 %collective-permute-start = (bf16[12,2176]{1,0:T(8,128)(2,1)S(1)}, bf16[12,2176]{1,0:T(8,128)(2,1)S(1)}, u32[]{:S(2)}, u32[]{:S(2)}) collective-permute-start(bf16[12,2176]{1,0:T(8,128)(2,1)S(1)} %get-tuple-element.45), channel_id=1, source_target_pairs={{0,16},{16,0},{1,17},{17,1},{2,18},{18,2},{3,19},{19,3},{4,20},{20... | collective-permute-start | bytes 156680 | tf_op jit(solution)/shard_map/ppermute | solution.py:196
  19.6 1.9 collective-permute-start.1
  21.6 4.1 %collective-permute-done.1 = bf16[24,2176]{1,0:T(8,128)(2,1)S(1)} collective-permute-done((bf16[24,2176]{1,0:T(8,128)(2,1)S(1)}, bf16[24,2176]{1,0:T(8,128)(2,1)S(1)}, u32[]{:S(2)}, u32[]{:S(2)}) %collective-permute-start.1) | collective-permute-done | bytes 104480 | tf_op jit(solution)/shard_map/ppermute | solution.py:42
  25.7 1.9 collective-permute-start.2
  27.7 12.3 %collective-permute-done.2 = bf16[2,24,2176]{2,1,0:T(8,128)(2,1)S(1)} collective-permute-done((bf16[2,24,2176]{2,1,0:T(8,128)(2,1)S(1)}, bf16[2,24,2176]{2,1,0:T(8,128)(2,1)S(1)}, u32[]{:S(2)}, u32[]{:S(2)}) %collective-permute-start.2) | collective-permute-done | bytes 208928 | tf_op jit(solution)/shard_map/ppermute | solution.py:42
  43.6 2.0 collective-permute-start.4
  45.7 4.4 %collective-permute-start.6 = (bf16[256,512]{1,0:T(8,128)(2,1)S(1)}, bf16[256,512]{1,0:T(8,128)(2,1)S(1)}, u32[]{:S(2)}, u32[]{:S(2)}) collective-permute-start(bf16[256,512]{1,0:T(8,128)(2,1)S(1)} %bitcast.40), channel_id=1, source_target_pairs={{32,0},{64,32},{96,64},{0,96},{33,1},{65,33},{97,65},{1,97},{34,2}... | collective-permute-start | bytes 786440 | tf_op jit(solution)/shard_map/ppermute | solution.py:38
  50.1 1.9 collective-permute-start.7
  52.0 3.3 %collective-permute-start.3 = (bf16[256,512]{1,0:T(8,128)(2,1)S(1)}, bf16[256,512]{1,0:T(8,128)(2,1)S(1)}, u32[]{:S(2)}, u32[]{:S(2)}) collective-permute-start(bf16[256,512]{1,0:T(8,128)(2,1)S(1)} %bitcast.58), channel_id=1, source_target_pairs={{128,0},{256,128},{384,256},{0,384},{129,1},{257,129},{385,257},{1... | collective-permute-start | bytes 786440 | tf_op jit(solution)/shard_map/ppermute | solution.py:38
  55.3 2.8 %collective-permute-start.5 = (bf16[256,512]{1,0:T(8,128)(2,1)S(1)}, bf16[256,512]{1,0:T(8,128)(2,1)S(1)}, u32[]{:S(2)}, u32[]{:S(2)}) collective-permute-start(bf16[256,512]{1,0:T(8,128)(2,1)S(1)} %bitcast.59), channel_id=1, source_target_pairs={{384,0},{0,128},{128,256},{256,384},{385,1},{1,129},{129,257},{257... | collective-permute-start | bytes 786440 | tf_op jit(solution)/shard_map/ppermute | solution.py:38
  58.2 1.7 collective-permute-done.7.own3
  59.9 10.1 %collective-permute-done.3 = bf16[256,512]{1,0:T(8,128)(2,1)S(1)} collective-permute-done((bf16[256,512]{1,0:T(8,128)(2,1)S(1)}, bf16[256,512]{1,0:T(8,128)(2,1)S(1)}, u32[]{:S(2)}, u32[]{:S(2)}) %collective-permute-start.3) | collective-permute-done | bytes 262176 | tf_op jit(solution)/shard_map/ppermute | solution.py:38
  70.0 2.1 collective-permute-done.5
  72.2 2.9 %collective-permute-start.10 = (bf16[784,512]{1,0:T(8,128)(2,1)S(1)}, bf16[784,512]{1,0:T(8,128)(2,1)S(1)}, u32[]{:S(2)}, u32[]{:S(2)}) collective-permute-start(bf16[784,512]{1,0:T(8,128)(2,1)S(1)} %pad_maximum_fusion.rest), channel_id=1, source_target_pairs={{32,0},{64,32},{96,64},{0,96},{33,1},{65,33},{97,65},{1,97},{34,2}... | collective-permute-start | bytes 2408456 | tf_op jit(solution)/shard_map/ppermute | solution.py:38
  75.1 2.4 %collective-permute-start.11 = (bf16[784,512]{1,0:T(8,128)(2,1)S(1)}, bf16[784,512]{1,0:T(8,128)(2,1)S(1)}, u32[]{:S(2)}, u32[]{:S(2)}) collective-permute-start(bf16[784,512]{1,0:T(8,128)(2,1)S(1)} %pad_maximum_fusion.rest), channel_id=1, source_target_pairs={{96,0},{0,32},{32,64},{64,96},{97,1},{1,33},{33,65},{65,97},{98,2}... | collective-permute-start | bytes 2408456 | tf_op jit(solution)/shard_map/ppermute | solution.py:38
  77.5 15.1 %collective-permute-done.10.rest1 = bf16[784,512]{1,0:T(8,128)(2,1)S(1)} collective-permute-done((bf16[784,512]{1,0:T(8,128)(2,1)S(1)}, bf16[784,512]{1,0:T(8,128)(2,1)S(1)}, u32[]{:S(2)}, u32[]{:S(2)}) %collective-permute-start.10) | collective-permute-done | bytes 802848 | tf_op jit(solution)/shard_map/ppermute | solution.py:38
  93.4 4.3 %collective-permute-start.13 = (bf16[400,512]{1,0:T(8,128)(2,1)}, bf16[400,512]{1,0:T(8,128)(2,1)S(1)}, u32[]{:S(2)}, u32[]{:S(2)}) collective-permute-start(bf16[400,512]{1,0:T(8,128)(2,1)} %slice.111), channel_id=1, source_target_pairs={{32,0},{64,32},{96,64},{0,96},{33,1},{65,33},{97,65},{1,97},{34,2}... | collective-permute-start | bytes 1228808 | tf_op jit(solution)/shard_map/ppermute | solution.py:38
  98.4 1.9 collective-permute-start.8
  101.0 4.6 %collective-permute-start.9 = (bf16[128,512]{1,0:T(8,128)(2,1)}, bf16[128,512]{1,0:T(8,128)(2,1)}, u32[]{:S(2)}, u32[]{:S(2)}) collective-permute-start(bf16[128,512]{1,0:T(8,128)(2,1)} %slice.87), channel_id=1, source_target_pairs={{32,0},{64,32},{96,64},{0,96},{33,1},{65,33},{97,65},{1,97},{34,2}... | collective-permute-start | bytes 393224 | tf_op jit(solution)/shard_map/ppermute | solution.py:38
  107.2 1.9 collective-permute-start.12
  115.1 8.1 %shard_map.94.acc = f32[768,1152]{1,0:T(8,128)} custom-call(s32[3]{0:T(128)S(1)} %pad_add_fusion.1.place, bf16[768,2176]{1,0:T(8,128)(2,1)} %all-gather.2.cloned.1.call-done.tok, bf16[256,512]{1,0:T(8,128)(2,1)S(1)} %bitcast.42, bf16[256,512]{1,0:T(8,128)(2,1)S(1)} %copy-done.4, bf16[256,512]{1,0:T(8,128)(2,1)S(1)} %copy-done.6, ...), custom_call_target="tpu_custom_call" | custom-call | flops 2944401408 | bytes 10000000 | tf_op jit(solution)/shard_map/pallas_call | solution.py:177
  123.2 5.0 %shard_map.96 = f32[384,1152]{1,0:T(8,128)} custom-call(s32[3]{0:T(128)S(1)} %pad_add_fusion.1.place, bf16[768,2176]{1,0:T(8,128)(2,1)} %all-gather.2.cloned.1.call-done.tok, f32[768,1152]{1,0:T(8,128)} %shard_map.94.acc, bf16[384,512]{1,0:T(8,128)(2,1)} %collective-permute-done.12.rest2a, bf16[400,512]{1,0:T(8,128)(2,1)S(1)} %collective-permute-done.13.rest2b, ...), custom_call_target="tpu_custom_call" | custom-call | flops 339738624 | bytes 10000000 | tf_op jit(solution)/shard_map/pallas_call | solution.py:177
  128.2 4.2 %collective-permute-start.14 = (f32[384,1152]{1,0:T(8,128)}, f32[384,1152]{1,0:T(8,128)}, u32[]{:S(2)}, u32[]{:S(2)}) collective-permute-start(f32[384,1152]{1,0:T(8,128)} %shard_map.96), channel_id=1, source_target_pairs={{0,16},{16,0},{1,17},{17,1},{2,18},{18,2},{3,19},{19,3},{4,20},{20... | collective-permute-start | bytes 5308424 | tf_op jit(solution)/shard_map/ppermute | solution.py:239
  140.5 3.8 %shard_map.95.near = f32[384,1152]{1,0:T(8,128)S(1)} custom-call(s32[3]{0:T(128)S(1)} %pad_add_fusion.1.place, bf16[768,2176]{1,0:T(8,128)(2,1)} %all-gather.2.cloned.1.call-done.tok, f32[768,1152]{1,0:T(8,128)} %shard_map.94.acc, bf16[384,512]{1,0:T(8,128)(2,1)} %collective-permute-done.12.rest2a, bf16[400,512]{1,0:T(8,128)(2,1)S(1)} %collective-permute-done.13.rest2b, ...), custom_call_target="tpu_custom_call" | custom-call | flops 339738624 | bytes 10000000 | tf_op jit(solution)/shard_map/pallas_call | solution.py:177
  144.6 3.8 %shard_map.97 = (f32[32,512]{1,0:T(8,128)S(1)}, bf16[384,512]{1,0:T(8,128)(2,1)S(1)}, bf16[384,512]{1,0:T(8,128)(2,1)S(1)}, bf16[384,512]{1,0:T(8,128)(2,1)S(1)}...) custom-call(s32[3]{0:T(128)S(1)} %pad_add_fusion.1.place, f32[384,1152]{1,0:T(8,128)S(1)} %shard_map.95.near, ...), custom_call_target="tpu_custom_call" | custom-call | flops 201326592 | bytes 10000000 | tf_op jit(solution)/shard_map/pallas_call | solution.py:177
  152.7 1.7 all_to_all.15
  154.4 13.6 %all-to-all-start = ((f32[64,1,512]{2,1,0:T(1,128)}), f32[64,1,512]{2,1,0:T(1,128)}, u32[]{:S(2)}, u32[]{:S(2)}) async-start(f32[64,1,512]{2,1,0:T(1,128)} %all_to_all.15), calls=%async_computation | async-start | bytes 262144 | tf_op jit(solution)/shard_map/all_to_all | solution.py:264
  169.0 9.1 %all-to-all-done = f32[64,1,512]{2,1,0:T(1,128)} async-done(((f32[64,1,512]{2,1,0:T(1,128)}), f32[64,1,512]{2,1,0:T(1,128)}, u32[]{:S(2)}, u32[]{:S(2)}) %all-to-all-start) | async-done | bytes 131104 | tf_op jit(solution)/shard_map/all_to_all | solution.py:264
  186.2 7.2 %all-to-all-start.1 = ((f32[32,1,768]{2,1,0:T(1,128)}), f32[32,1,768]{2,1,0:T(1,128)S(1)}, u32[]{:S(2)}, u32[]{:S(2)}) async-start(f32[32,1,768]{2,1,0:T(1,128)} %copy.23), calls=%async_computation.1 | async-start | bytes 196608 | tf_op jit(solution)/shard_map/all_to_all | solution.py:276
  194.0 9.7 %all-to-all-done.1 = f32[32,1,768]{2,1,0:T(1,128)S(1)} async-done(((f32[32,1,768]{2,1,0:T(1,128)}), f32[32,1,768]{2,1,0:T(1,128)S(1)}, u32[]{:S(2)}, u32[]{:S(2)}) %all-to-all-start.1) | async-done | bytes 98336 | tf_op jit(solution)/shard_map/all_to_all | solution.py:276
  204.4 3.5 %all-to-all-start.2 = ((f32[16,2,128]{2,1,0:T(2,128)}), f32[16,2,128]{2,1,0:T(2,128)S(1)}, u32[]{:S(2)}, u32[]{:S(2)}) async-start(f32[16,2,128]{2,1,0:T(2,128)} %broadcast_in_dim.40), calls=%async_computation.2 | async-start | bytes 32768 | tf_op jit(solution)/shard_map/all_to_all | solution.py:282
  210.3 5.0 %all-to-all-done.2 = f32[16,2,128]{2,1,0:T(2,128)S(1)} async-done(((f32[16,2,128]{2,1,0:T(2,128)}), f32[16,2,128]{2,1,0:T(2,128)S(1)}, u32[]{:S(2)}, u32[]{:S(2)}) %all-to-all-start.2) | async-done | bytes 16416 | tf_op jit(solution)/shard_map/all_to_all | solution.py:282
  (127 shorter events, 36.2 us)
Async XLA Ops:
  7.2 104.9 %all-gather.2.cloned.1.call-start = ((), (), s32[]{:S(2)}) async-start(), calls=%async_computation.3 | async-start | bytes 3760128 | tf_op jit(solution)/shard_map/all_gather | solution.py:201
  8.3 35.3 %copy-start.19 = (bf16[2,128,896]{2,1,0:T(8,128)(2,1)S(1)}, bf16[2,128,896]{2,1,0:T(8,128)(2,1)}, u32[]{:S(2)}) copy-start(bf16[2,128,896]{2,1,0:T(8,128)(2,1)} %param.10) | copy-start | bytes 1376260
  9.9 9.7 %collective-permute-start = (bf16[12,2176]{1,0:T(8,128)(2,1)S(1)}, bf16[12,2176]{1,0:T(8,128)(2,1)S(1)}, u32[]{:S(2)}, u32[]{:S(2)}) collective-permute-start(bf16[12,2176]{1,0:T(8,128)(2,1)S(1)} %get-tuple-element.45), channel_id=1, source_target_pairs={{0,16},{16,0},{1,17},{17,1},{2,18},{18,2},{3,19},{19,3},{4,20},{20... | collective-permute-start | bytes 156680 | tf_op jit(solution)/shard_map/ppermute | solution.py:196
  19.6 6.1 %collective-permute-start.1 = (bf16[24,2176]{1,0:T(8,128)(2,1)S(1)}, bf16[24,2176]{1,0:T(8,128)(2,1)S(1)}, u32[]{:S(2)}, u32[]{:S(2)}) collective-permute-start(bf16[24,2176]{1,0:T(8,128)(2,1)S(1)} %maximum_select_fusion.4), channel_id=1, source_target_pairs={{0,1},{1,0},{2,3},{3,2},{4,5},{5,4},{6,7},{7,6},{8,9},{9,8},{10,11... | collective-permute-start | bytes 313352 | tf_op jit(solution)/shard_map/ppermute | solution.py:42
  25.7 14.3 %collective-permute-start.2 = (bf16[2,24,2176]{2,1,0:T(8,128)(2,1)S(1)}, bf16[2,24,2176]{2,1,0:T(8,128)(2,1)S(1)}, u32[]{:S(2)}, u32[]{:S(2)}) collective-permute-start(bf16[2,24,2176]{2,1,0:T(8,128)(2,1)S(1)} %maximum_select_fusion.2), channel_id=1, source_target_pairs={{0,128},{128,0},{1,129},{129,1},{2,130},{130,2},{3,131},{131,3},{4... | collective-permute-start | bytes 626696 | tf_op jit(solution)/shard_map/ppermute | solution.py:42
  43.6 28.4 %collective-permute-start.4 = (bf16[272,512]{1,0:T(8,128)(2,1)S(1)}, bf16[272,512]{1,0:T(8,128)(2,1)S(1)}, u32[]{:S(2)}, u32[]{:S(2)}) collective-permute-start(bf16[272,512]{1,0:T(8,128)(2,1)S(1)} %concatenate.80), channel_id=1, source_target_pairs={{256,0},{384,128},{0,256},{128,384},{257,1},{385,129},{1,257},{129... | collective-permute-start | bytes 835592 | tf_op jit(solution)/shard_map/ppermute | solution.py:38
  45.7 12.5 %collective-permute-start.6 = (bf16[256,512]{1,0:T(8,128)(2,1)S(1)}, bf16[256,512]{1,0:T(8,128)(2,1)S(1)}, u32[]{:S(2)}, u32[]{:S(2)}) collective-permute-start(bf16[256,512]{1,0:T(8,128)(2,1)S(1)} %bitcast.40), channel_id=1, source_target_pairs={{32,0},{64,32},{96,64},{0,96},{33,1},{65,33},{97,65},{1,97},{34,2}... | collective-permute-start | bytes 786440 | tf_op jit(solution)/shard_map/ppermute | solution.py:38
  50.1 9.8 %collective-permute-start.7 = (bf16[256,512]{1,0:T(8,128)(2,1)S(1)}, bf16[256,512]{1,0:T(8,128)(2,1)S(1)}, u32[]{:S(2)}, u32[]{:S(2)}) collective-permute-start(bf16[256,512]{1,0:T(8,128)(2,1)S(1)} %bitcast.41), channel_id=1, source_target_pairs={{96,0},{0,32},{32,64},{64,96},{97,1},{1,33},{33,65},{65,97},{98,2}... | collective-permute-start | bytes 786440 | tf_op jit(solution)/shard_map/ppermute | solution.py:38
  52.0 18.0 %collective-permute-start.3 = (bf16[256,512]{1,0:T(8,128)(2,1)S(1)}, bf16[256,512]{1,0:T(8,128)(2,1)S(1)}, u32[]{:S(2)}, u32[]{:S(2)}) collective-permute-start(bf16[256,512]{1,0:T(8,128)(2,1)S(1)} %bitcast.58), channel_id=1, source_target_pairs={{128,0},{256,128},{384,256},{0,384},{129,1},{257,129},{385,257},{1... | collective-permute-start | bytes 786440 | tf_op jit(solution)/shard_map/ppermute | solution.py:38
  55.3 16.7 %collective-permute-start.5 = (bf16[256,512]{1,0:T(8,128)(2,1)S(1)}, bf16[256,512]{1,0:T(8,128)(2,1)S(1)}, u32[]{:S(2)}, u32[]{:S(2)}) collective-permute-start(bf16[256,512]{1,0:T(8,128)(2,1)S(1)} %bitcast.59), channel_id=1, source_target_pairs={{384,0},{0,128},{128,256},{256,384},{385,1},{1,129},{129,257},{257... | collective-permute-start | bytes 786440 | tf_op jit(solution)/shard_map/ppermute | solution.py:38
  58.2 42.1 %copy-start.3 = (bf16[256,512]{1,0:T(8,128)(2,1)}, bf16[256,512]{1,0:T(8,128)(2,1)S(1)}, u32[]{:S(2)}) copy-start(bf16[256,512]{1,0:T(8,128)(2,1)S(1)} %collective-permute-done.6.own1) | copy-start | bytes 786436
  59.9 38.5 %copy-start.5 = (bf16[256,512]{1,0:T(8,128)(2,1)}, bf16[256,512]{1,0:T(8,128)(2,1)S(1)}, u32[]{:S(2)}) copy-start(bf16[256,512]{1,0:T(8,128)(2,1)S(1)} %collective-permute-done.7.own3) | copy-start | bytes 786436
  72.1 37.0 %copy-start.21 = (bf16[4096,32]{0,1:T(8,128)(2,1)S(1)}, bf16[4096,32]{0,1:T(8,128)(2,1)}, u32[]{:S(2)}) copy-start(bf16[4096,32]{0,1:T(8,128)(2,1)} %param.11) | copy-start | bytes 786436
  72.2 20.4 %collective-permute-start.10 = (bf16[784,512]{1,0:T(8,128)(2,1)S(1)}, bf16[784,512]{1,0:T(8,128)(2,1)S(1)}, u32[]{:S(2)}, u32[]{:S(2)}) collective-permute-start(bf16[784,512]{1,0:T(8,128)(2,1)S(1)} %pad_maximum_fusion.rest), channel_id=1, source_target_pairs={{32,0},{64,32},{96,64},{0,96},{33,1},{65,33},{97,65},{1,97},{34,2}... | collective-permute-start | bytes 2408456 | tf_op jit(solution)/shard_map/ppermute | solution.py:38
  75.1 30.5 %collective-permute-start.11 = (bf16[784,512]{1,0:T(8,128)(2,1)S(1)}, bf16[784,512]{1,0:T(8,128)(2,1)S(1)}, u32[]{:S(2)}, u32[]{:S(2)}) collective-permute-start(bf16[784,512]{1,0:T(8,128)(2,1)S(1)} %pad_maximum_fusion.rest), channel_id=1, source_target_pairs={{96,0},{0,32},{32,64},{64,96},{97,1},{1,33},{33,65},{65,97},{98,2}... | collective-permute-start | bytes 2408456 | tf_op jit(solution)/shard_map/ppermute | solution.py:38
  93.4 29.8 %collective-permute-start.13 = (bf16[400,512]{1,0:T(8,128)(2,1)}, bf16[400,512]{1,0:T(8,128)(2,1)S(1)}, u32[]{:S(2)}, u32[]{:S(2)}) collective-permute-start(bf16[400,512]{1,0:T(8,128)(2,1)} %slice.111), channel_id=1, source_target_pairs={{32,0},{64,32},{96,64},{0,96},{33,1},{65,33},{97,65},{1,97},{34,2}... | collective-permute-start | bytes 1228808 | tf_op jit(solution)/shard_map/ppermute | solution.py:38
  98.4 13.6 %collective-permute-start.8 = (bf16[128,512]{1,0:T(8,128)(2,1)}, bf16[128,512]{1,0:T(8,128)(2,1)S(1)}, u32[]{:S(2)}, u32[]{:S(2)}) collective-permute-start(bf16[128,512]{1,0:T(8,128)(2,1)} %slice.86), channel_id=1, source_target_pairs={{96,0},{0,32},{32,64},{64,96},{97,1},{1,33},{33,65},{65,97},{98,2}... | collective-permute-start | bytes 393224 | tf_op jit(solution)/shard_map/ppermute | solution.py:38
  101.0 11.0 %collective-permute-start.9 = (bf16[128,512]{1,0:T(8,128)(2,1)}, bf16[128,512]{1,0:T(8,128)(2,1)}, u32[]{:S(2)}, u32[]{:S(2)}) collective-permute-start(bf16[128,512]{1,0:T(8,128)(2,1)} %slice.87), channel_id=1, source_target_pairs={{32,0},{64,32},{96,64},{0,96},{33,1},{65,33},{97,65},{1,97},{34,2}... | collective-permute-start | bytes 393224 | tf_op jit(solution)/shard_map/ppermute | solution.py:38
  107.2 16.0 %collective-permute-start.12 = (bf16[384,512]{1,0:T(8,128)(2,1)}, bf16[384,512]{1,0:T(8,128)(2,1)}, u32[]{:S(2)}, u32[]{:S(2)}) collective-permute-start(bf16[384,512]{1,0:T(8,128)(2,1)} %slice.110), channel_id=1, source_target_pairs={{96,0},{0,32},{32,64},{64,96},{97,1},{1,33},{33,65},{65,97},{98,2}... | collective-permute-start | bytes 1179656 | tf_op jit(solution)/shard_map/ppermute | solution.py:38
  112.0 1.1 copy-start.2
  123.2 9.3 %copy-start.22 = (bf16[32,896]{1,0:T(8,128)(2,1)S(1)}, bf16[32,896]{1,0:T(8,128)(2,1)}, u32[]{:S(2)}) copy-start(bf16[32,896]{1,0:T(8,128)(2,1)} %param.12) | copy-start | bytes 172036
  123.2 10.6 %copy-start.25 = (bf16[896]{0:T(1024)(128)(2,1)S(1)}, bf16[896]{0:T(1024)(128)(2,1)}, u32[]{:S(2)}) copy-start(bf16[896]{0:T(1024)(128)(2,1)} %param.13) | copy-start | bytes 5380
  128.2 16.3 %collective-permute-start.14 = (f32[384,1152]{1,0:T(8,128)}, f32[384,1152]{1,0:T(8,128)}, u32[]{:S(2)}, u32[]{:S(2)}) collective-permute-start(f32[384,1152]{1,0:T(8,128)} %shard_map.96), channel_id=1, source_target_pairs={{0,16},{16,0},{1,17},{17,1},{2,18},{18,2},{3,19},{19,3},{4,20},{20... | collective-permute-start | bytes 5308424 | tf_op jit(solution)/shard_map/ppermute | solution.py:239
  133.9 10.4 %copy-start.23 = (s32[128]{0:T(128)}, s32[128]{0:T(128)S(1)}, u32[]{:S(2)}) copy-start(s32[128]{0:T(128)S(1)} %get-tuple-element.46) | copy-start | bytes 1540
  133.9 10.4 %copy-start.24 = (s32[128]{0:T(128)}, s32[128]{0:T(128)S(1)}, u32[]{:S(2)}) copy-start(s32[128]{0:T(128)S(1)} %get-tuple-element.47) | copy-start | bytes 1540
  134.0 10.3 %copy-start.20 = (pred[128,384]{1,0:T(8,128)(4,1)}, pred[128,384]{1,0:T(8,128)(4,1)S(1)}, u32[]{:S(2)}) copy-start(pred[128,384]{1,0:T(8,128)(4,1)S(1)} %broadcast_compare_fusion) | copy-start | bytes 147460
  140.5 4.1 %copy-start.7 = (bf16[128,512]{1,0:T(8,128)(2,1)S(1)}, bf16[128,512]{1,0:T(8,128)(2,1)}, u32[]{:S(2)}) copy-start(bf16[128,512]{1,0:T(8,128)(2,1)} %pad.27.b_gate) | copy-start | bytes 393220
  140.5 4.1 %copy-start.8 = (bf16[128,512]{1,0:T(8,128)(2,1)S(1)}, bf16[128,512]{1,0:T(8,128)(2,1)}, u32[]{:S(2)}) copy-start(bf16[128,512]{1,0:T(8,128)(2,1)} %pad.28.b_up) | copy-start | bytes 393220
  144.6 34.5 %copy-start = (bf16[768,2176]{1,0:T(8,128)(2,1)S(1)}, bf16[768,2176]{1,0:T(8,128)(2,1)}, u32[]{:S(2)}) copy-start(bf16[768,2176]{1,0:T(8,128)(2,1)} %all-gather.2.cloned.1.call-done.tok) | copy-start | bytes 10027012
  154.4 23.8 %all-to-all-start = ((f32[64,1,512]{2,1,0:T(1,128)}), f32[64,1,512]{2,1,0:T(1,128)}, u32[]{:S(2)}, u32[]{:S(2)}) async-start(f32[64,1,512]{2,1,0:T(1,128)} %all_to_all.15), calls=%async_computation | async-start | bytes 262144 | tf_op jit(solution)/shard_map/all_to_all | solution.py:264
  186.2 17.5 %all-to-all-start.1 = ((f32[32,1,768]{2,1,0:T(1,128)}), f32[32,1,768]{2,1,0:T(1,128)S(1)}, u32[]{:S(2)}, u32[]{:S(2)}) async-start(f32[32,1,768]{2,1,0:T(1,128)} %copy.23), calls=%async_computation.1 | async-start | bytes 196608 | tf_op jit(solution)/shard_map/all_to_all | solution.py:276
  204.4 10.8 %all-to-all-start.2 = ((f32[16,2,128]{2,1,0:T(2,128)}), f32[16,2,128]{2,1,0:T(2,128)S(1)}, u32[]{:S(2)}, u32[]{:S(2)}) async-start(f32[16,2,128]{2,1,0:T(2,128)} %broadcast_in_dim.40), calls=%async_computation.2 | async-start | bytes 32768 | tf_op jit(solution)/shard_map/all_to_all | solution.py:282
  (13 other events, 11.2 us)
Sparse Core Ops, SparseCore 0:
  41.0 49.4 all-gather.1

commit v4 on v3

v4 whole, which is shorter than its diff:
```python
import functools

import jax
import jax.numpy as jnp
from jax import lax
from jax.experimental import pallas as pl
from jax.experimental.pallas import tpu as pltpu
from jax.sharding import Mesh, PartitionSpec as P

SEQS = 4
ROWS = 12
RANK = 16
WIDTH = 4096
DPO_BETA = 0.1
LOSS_SCALE = 1024.0
F32 = jnp.float32
BF16 = jnp.bfloat16

AXES = ("s", "t", "x", "c", "z", "yl")
SIZES = (2, 2, 4, 2, 8, 2)
DP = ("s", "t", "x", "c")
BLK = ("z", "yl")
YH = ("s", "t")
SWAP = [(0, 1), (1, 0)]

SLICE = 128
HALF = WIDTH // 2
LANES = 128
COLS = 512
SKIP = 384
GROUP = 384
BLOCKS = GROUP // ROWS
WIDE = 2 * COLS + LANES
CONTRACT_LAST = (((1,), (1,)), ((), ()))


def fetch(value, axes, size, k):
    return lax.ppermute(value, axes, [((i + k) % size, i) for i in range(size)])


def swapped(value, axis, index):
    far = lax.ppermute(value, axis, SWAP)
    return jnp.where(index == 0, jnp.stack([value, far]), jnp.stack([far, value]))


def split(value, terms):
    parts = []
    for _ in range(terms):
        parts.append(value.astype(BF16))
        value = value - parts[-1].astype(F32)
    return parts


def dot(a, b, dims=(((1,), (0,)), ((), ()))):
    return lax.dot_general(a, b, dims, preferred_element_type=F32)


def assemble(place, own, own1, own3, own2g, own2u, rest, rest1, rest3, rest2a, rest2b, w):
    pieces = []
    for j, ref in ((0, own), (1, own1), (3, own3)):
        pieces.append((0, j, ref[0:SLICE, :], ref[SLICE : 2 * SLICE, :]))
    pieces.append((0, 2, own2g[...], own2u[...]))
    for j, ref in ((0, rest), (1, rest1), (3, rest3)):
        for at, k in enumerate((1, 3, 2)):
            begin = 2 * at * SLICE
            pieces.append((k, j, ref[begin : begin + SLICE, :], ref[begin + SLICE : begin + 2 * SLICE, :]))
    pieces.append((1, 2, rest2a[0:SLICE, :], rest2a[SLICE : 2 * SLICE, :]))
    pieces.append((3, 2, rest2a[2 * SLICE : 3 * SLICE, :], rest2b[0:SLICE, :]))
    pieces.append((2, 2, rest2b[SLICE : 2 * SLICE, :], rest2b[2 * SLICE : 3 * SLICE, :]))
    for k, j, gate, up in pieces:
        source = lax.rem(place[0] + k, 4) * 4 + lax.rem(place[1] + j, 4)
        rows = pl.ds(pl.multiple_of(source * SLICE, SLICE), SLICE)
        w[rows, 0:COLS] = gate
        w[rows, COLS : 2 * COLS] = up


def products(far, place, tok, w, down, out):
    half = 1 - place[2] if far else place[2]
    rows = pl.ds(pl.multiple_of(half * GROUP, GROUP), GROUP)
    for n in range(4):
        part = slice(n * COLS // 2, (n + 1) * COLS // 2)
        out[:, part] = dot(tok[rows, 0:HALF], w[:, part])
    out[:, 2 * COLS : WIDE] = dot(tok[rows, 0:HALF], down[...])


def score(place, near, partner, b_gate, b_up, readout, signs, count, message, gate_high, gate_low, up_high,
          up_low, low_t):
    low = near[:, 2 * COLS : WIDE] + partner[:, 2 * COLS : WIDE]
    low_b = low.astype(BF16)
    gate_ref = near[:, 0:COLS] + partner[:, 0:COLS]
    up_ref = near[:, COLS : 2 * COLS] + partner[:, COLS : 2 * COLS]
    gate_pol = gate_ref + dot(low_b, b_gate[...])
    up_pol = up_ref + dot(low_b, b_up[...])
    sig_ref = jax.nn.sigmoid(gate_ref)
    sig_pol = jax.nn.sigmoid(gate_pol)
    act_pol = gate_pol * sig_pol
    read = readout[...].astype(F32)
    change = act_pol * up_pol - gate_ref * sig_ref * up_ref
    k_gate = read * sig_pol * (1.0 + gate_pol * (1.0 - sig_pol)) * up_pol
    k_up = read * act_pol
    read_b = jnp.broadcast_to(readout[...], (8, COLS))
    change_row = sum(dot(read_b, part, CONTRACT_LAST) for part in split(change, 3))
    sign = signs[place[2]]
    gaps = sum(dot(part, sign, CONTRACT_LAST) for part in split(change_row, 3))
    tail = jnp.broadcast_to(gaps[0:1, :] + count[...], (2 * RANK, LANES))
    high, rest = split(k_gate, 2)
    gate_high[...], gate_low[...] = high, rest
    mixed = dot(b_gate[0 : 2 * RANK, :], high, CONTRACT_LAST) + dot(b_gate[0 : 2 * RANK, :], rest, CONTRACT_LAST)
    high, rest = split(k_up, 2)
    up_high[...], up_low[...] = high, rest
    mixed_up = dot(b_up[0 : 2 * RANK, :], high, CONTRACT_LAST) + dot(b_up[0 : 2 * RANK, :], rest, CONTRACT_LAST)
    mixed = mixed + mixed_up
    for core in range(2):
        lines = slice(2 * RANK * core, 2 * RANK * (core + 1))
        for i in range(3):
            message[lines, i, :] = mixed[:, i * LANES : (i + 1) * LANES]
        message[lines, 3, :] = tail
    low_t[...] = low_b.astype(F32).T[0 : 2 * RANK, :]


def close(place, arrived, signs, valid, low_t, gate_high, gate_low, up_high, up_low, tok, out, total_out):
    core = place[2]
    sums = [jnp.sum(arrived[2 * RANK * h : 2 * RANK * (h + 1)], axis=0) for h in range(2)]
    totals = [jnp.concatenate([total[i : i + 1, :] for i in range(3)], axis=1) for total in sums]
    tails = [total[3:4, :] for total in sums]
    pair_total = jnp.maximum(tails[0][:, 64:65] + tails[1][:, 64:65], 1.0)
    logs, cotangents, terms = 0.0, [], []
    for h in range(2):
        logit = DPO_BETA * tails[h]
        logs = logs + jnp.sum(
            valid[h] * (jnp.minimum(logit, 0.0) - jnp.log1p(jnp.exp(-jnp.abs(logit)))), axis=1, keepdims=True
        )
        scaled = -LOSS_SCALE * DPO_BETA * valid[h] * jax.nn.sigmoid(-logit) / pair_total
        scaled = jnp.broadcast_to(scaled, (8, LANES))
        cotangent = sum(dot(part, signs[h]) for part in split(scaled, 3))
        cotangents.append(cotangent[0:1, :])
        projected = jnp.broadcast_to(totals[h], (8, GROUP)) * cotangent
        terms.append(dot(projected.astype(BF16), tok[h * GROUP : (h + 1) * GROUP, 0:HALF]))
    grad_a = (terms[0] + terms[1])[0:1, :]
    own = jnp.where(core == 0, cotangents[0], cotangents[1])
    high, rest = split(low_t[...] * own, 2)
    gate = dot(high[0:RANK], gate_high[...]) + dot(high[0:RANK], gate_low[...]) + dot(rest[0:RANK], gate_high[...])
    up = dot(high[RANK:], up_high[...]) + dot(high[RANK:], up_low[...]) + dot(rest[RANK:], up_high[...])
    for i in range(4):
        out[0:RANK, i, :] = gate[:, i * LANES : (i + 1) * LANES]
        out[RANK : 2 * RANK, i, :] = up[:, i * LANES : (i + 1) * LANES]
    line = lax.broadcasted_iota(jnp.int32, (2 * RANK, SLICE), 0)
    slices = jnp.zeros((2 * RANK, SLICE), F32)
    for i in range(RANK):
        here = jnp.broadcast_to(grad_a[:, i * SLICE : (i + 1) * SLICE], (2 * RANK, SLICE))
        slices = jnp.where(line == 2 * i + core, here, slices)
    out[:, 4, :] = slices
    out[:, 5, :] = jnp.broadcast_to(0.5 * logs, (2 * RANK, LANES))
    total_out[...] = jnp.broadcast_to(pair_total, (8, LANES))


def kernel(function, shapes, arguments, flops, grant):
    vmem = pl.BlockSpec(memory_space=pltpu.VMEM)
    smem = pl.BlockSpec(memory_space=pltpu.SMEM)
    return pl.pallas_call(
        function,
        out_shape=tuple(jax.ShapeDtypeStruct(*s) for s in shapes),
        in_specs=[smem] + [vmem] * (len(arguments) - 1),
        out_specs=(vmem,) * len(shapes),
        compiler_params=pltpu.CompilerParams(vmem_limit_bytes=grant * 1024 * 1024),
        cost_estimate=pl.CostEstimate(flops=flops, bytes_accessed=10_000_000, transcendentals=0),
    )(*arguments)


def on_device(tokens, sequence_labels, response_mask, frozen, down, up, readout):
    s, t, x, core, yl = (lax.axis_index(a) for a in ("s", "t", "x", "c", "yl"))
    code = jnp.where(response_mask > 0, sequence_labels, SEQS)

    by_core = tokens.reshape(ROWS, WIDTH // (2 * SLICE), 2, SLICE).transpose(2, 0, 1, 3).reshape(2, ROWS, HALF)
    code_lanes = jnp.pad(code.reshape(ROWS, 1).astype(BF16), ((0, 0), (0, LANES - 1)))
    keep = jnp.concatenate([jnp.where(core == 0, by_core[0], by_core[1]), code_lanes], axis=1)
    give = jnp.concatenate([jnp.where(core == 0, by_core[1], by_core[0]), code_lanes], axis=1)
    take = lax.ppermute(give, "c", SWAP)
    pair = jnp.where(
        core == 0, jnp.concatenate([keep, take], axis=0), jnp.concatenate([take, keep], axis=0)
    )
    eight = swapped(swapped(pair, "yl", yl), "t", t)
    has = [jnp.max((code == q).astype(F32)) for q in range(SEQS)]
    count = has[0] * has[1] + has[2] * has[3]

    low_half, high_half = frozen[:, :, :COLS], frozen[:, :, SKIP:]
    mine = jnp.where(t == 0, low_half, high_half).reshape(2 * SLICE, COLS)
    other = jnp.where(t == 0, high_half, low_half).reshape(2 * SLICE, COLS)
    count_rows = jnp.broadcast_to(count.astype(BF16), (16, COLS))
    y1 = fetch(other, YH, 4, 1)
    y3 = fetch(other, YH, 4, 3)
    y2 = fetch(jnp.concatenate([mine, count_rows], axis=0), YH, 4, 2)
    own1 = fetch(mine, "x", 4, 1)
    own3 = fetch(mine, "x", 4, 3)
    eight, y1, y2, y3, own1, own3 = lax.optimization_barrier((eight, y1, y2, y3, own1, own3))
    tok = lax.all_gather(eight.reshape(8 * ROWS, HALF + LANES), "z", axis=0, tiled=True)
    rest = jnp.concatenate([y1, y3, y2[: 2 * SLICE], y2[2 * SLICE :] + count_rows], axis=0)
    rest1 = fetch(rest, "x", 4, 1)
    rest3 = fetch(rest, "x", 4, 3)
    own2g = fetch(own3[:SLICE], "x", 4, 3)
    own2u = fetch(own1[SLICE:], "x", 4, 1)
    rest2a = fetch(rest3[: 3 * SLICE], "x", 4, 3)
    rest2b = fetch(rest1[3 * SLICE :], "x", 4, 1)
    count = sum(p[-1, 0].astype(F32) for p in (rest, rest1, rest3, rest2b))
    count_lanes = jnp.where(jnp.arange(LANES) == 64, count, 0.0).reshape(1, LANES)

    place = jnp.stack([2 * s + t, x, core]).astype(jnp.int32)
    down_half = down.reshape(16, 2, SLICE, 2 * RANK)
    down_half = jnp.where(core == 0, down_half[:, 0], down_half[:, 1]).reshape(HALF, 2 * RANK)
    down_half = jnp.pad(down_half, ((0, 0), (0, LANES - 2 * RANK)))
    (w,) = kernel(
        assemble,
        [((HALF, 2 * COLS), BF16)],
        (place, mine, own1, own3, own2g, own2u, rest, rest1, rest3, rest2a, rest2b),
        0, 8,
    )
    flops = 2 * GROUP * HALF * WIDE
    (far,) = kernel(functools.partial(products, True), [((GROUP, WIDE), F32)], (place, tok, w, down_half), flops, 12)
    partner = lax.ppermute(far, "c", SWAP)
    (near,) = kernel(functools.partial(products, False), [((GROUP, WIDE), F32)], (place, tok, w, down_half), flops, 12)

    units = jnp.where(t == 0, up[:, :COLS], up[:, SKIP:])
    b_gate = jnp.pad(units[:RANK], ((0, LANES - RANK), (0, 0)))
    b_up = jnp.pad(units[RANK:], ((RANK, LANES - 2 * RANK), (0, 0)))
    shared = (jnp.arange(COLS) >= 2 * COLS - readout.shape[0]).astype(BF16)
    read = jnp.where(t == 0, readout[:COLS], readout[SKIP:] * shared).reshape(1, COLS)

    codes = tok[:, HALF].astype(jnp.int32).reshape(2, GROUP)
    pair_of = jnp.arange(LANES, dtype=jnp.int32)
    block_of = jnp.arange(GROUP, dtype=jnp.int32) // ROWS
    inside = (pair_of[:, None] // 2 == block_of[None, :])[None]
    chosen = inside & (codes[:, None, :] == 2 * (pair_of % 2)[None, :, None])
    rejected = inside & (codes[:, None, :] == 2 * (pair_of % 2)[None, :, None] + 1)
    signs = chosen.astype(BF16) - rejected.astype(BF16)
    valid = (jnp.any(chosen, axis=2) & jnp.any(rejected, axis=2)).astype(F32).reshape(2, 1, LANES)

    message, gate_high, gate_low, up_high, up_low, low_t = kernel(
        score,
        [((4 * RANK, 4, LANES), F32)] + [((GROUP, COLS), BF16)] * 4 + [((2 * RANK, GROUP), F32)],
        (place, near, partner, b_gate, b_up, read, signs, count_lanes),
        8 * GROUP * COLS * LANES, 16,
    )
    arrived = lax.all_to_all(message, ("c", "t", "z", "yl"), split_axis=0, concat_axis=0)
    outgoing, pair_total = kernel(
        close,
        [((2 * RANK, 6, LANES), F32), ((8, LANES), F32)],
        (place, arrived, signs, valid, low_t, gate_high, gate_low, up_high, up_low, tok),
        16 * GROUP * HALF * 2, 12,
    )

    arrived = lax.all_to_all(outgoing, DP, split_axis=0, concat_axis=0)
    summed = jnp.sum(arrived.reshape(2, 2, 8, 6, LANES), axis=(0, 2))
    grad_b = jnp.pad(summed[0, :4], ((0, 3), (0, 0))) + jnp.pad(summed[1, :4], ((3, 0), (0, 0)))
    columns = summed[:, 4]
    log_total = summed[0, 5, 0]
    grad_a = lax.all_to_all(
        jnp.broadcast_to(columns[None], (16, 2, SLICE)), BLK, split_axis=0, concat_axis=0
    )
    grad_a = grad_a.transpose(2, 1, 0).reshape(SLICE, 2 * RANK)
    return -log_total / pair_total[0, 0], grad_a, grad_b.reshape(1, 7 * LANES)


def solution(mesh):
    fine = Mesh(mesh.devices.reshape(SIZES), AXES)
    in_specs = (
        P(AXES, None),
        P(AXES, None),
        P(AXES, None),
        P(None, DP, BLK),
        P(),
        P(None, BLK),
        P(BLK),
    )
    out_specs = (P(), P(DP, None), P(DP, BLK))
    return jax.shard_map(
        on_device, mesh=fine, in_specs=in_specs, out_specs=out_specs, check_vma=False
    )
```

time: 225 us -> 233 us (1.036)
  local copies, waits for them, and re-layouts: 30.1 us -> 40.9 us
  Pallas kernels: 22.3 us -> 13.8 us
  waiting for transfers between devices: 70.1 us -> 73.1 us
    unnamed x59 -> x65, local copies, waits for them, and re-layouts: 14.7 us -> 24.9 us
    pallas_call x5, Pallas kernels: 22.3 us -> 13.8 us  [kernel(): pl.pallas_call(function, out_shape=tuple((jax.ShapeDtypeStruct(*s) for s...]
    ppermute x2, waiting for transfers between devices: 16.4 us -> 20.3 us  [swapped(): far = lax.ppermute(value, axis, SWAP)]
    ppermute x11, waiting for transfers between devices: 29 us -> 26.4 us  [fetch(): return lax.ppermute(value, axes, [((i + k) % size, i) for i in range(size)])]
    all_to_all x2 -> x0, local copies, waits for them, and re-layouts: 2.45 us -> none  [the longest x1 1.7 us: on_device(): lax.all_to_all(jnp.broadcast_to(message[None], (2, 2 * RANK, GROUP + LANE...]
  transfers between devices with their start and end apart: 19 -> 19, of which waited for: 10 -> 8; matrix products, arithmetic and copies ran while one was open for 6% -> 10% of each run, Pallas kernels for 5% -> 2%
where the time goes in v4:
time: 233 us; the launch traced here: 232 us
  starting transfers between devices  74.4 us (32%)
  waiting for transfers between devices  73.1 us (31%)
  local copies, waits for them, and re-layouts  40.9 us (18%)
  between operations  22.2 us (10%)
  Pallas kernels  13.8 us (6%)
  other arithmetic  7.32 us (3%)
    ppermute x11, starting transfers between devices, fetch(): return lax.ppermute(value, axes, [((i + k) % size, i) for i in range(size)])  34.8 us
    ppermute x11, waiting for transfers between devices, fetch(): return lax.ppermute(value, axes, [((i + k) % size, i) for i in range(size)])  26.4 us
    unnamed x65, local copies, waits for them, and re-layouts  24.9 us
    ppermute x2, waiting for transfers between devices, swapped(): far = lax.ppermute(value, axis, SWAP)  20.3 us
    pallas_call x5, Pallas kernels, kernel(): pl.pallas_call(function, out_shape=tuple((jax.ShapeDtypeStruct(*s) for s...  13.8 us
    all_to_all x1, starting transfers between devices, on_device(): lax.all_to_all(message, ('c', 't', 'z', 'yl'), split_axis=0, concat_axis=0)  13.2 us
    all_to_all x1, waiting for transfers between devices, on_device(): arrived = lax.all_to_all(outgoing, DP, split_axis=0, concat_axis=0)  10.3 us
    all_to_all x1, waiting for transfers between devices, on_device(): lax.all_to_all(message, ('c', 't', 'z', 'yl'), split_axis=0, concat_axis=0)  9.14 us
  transfers between devices with their start and end apart: 19, of which 8 were waited for; matrix products, arithmetic and copies ran while one was open for 10% of the time, Pallas kernels for 2%

profile of v4, /device:TPU:1, one launch (start us, length us, event | category | flops | bytes accessed | tf_op | source)
XLA Modules:
  0.0 231.7 jit_solution(7883574716995302318)
XLA Ops:
  9.9 8.8 %collective-permute-start = (bf16[12,2176]{1,0:T(8,128)(2,1)S(1)}, bf16[12,2176]{1,0:T(8,128)(2,1)S(1)}, u32[]{:S(2)}, u32[]{:S(2)}) collective-permute-start(bf16[12,2176]{1,0:T(8,128)(2,1)S(1)} %get-tuple-element.49), channel_id=1, source_target_pairs={{0,16},{16,0},{1,17},{17,1},{2,18},{18,2},{3,19},{19,3},{4,20},{20... | collective-permute-start | bytes 156680 | tf_op jit(solution)/shard_map/ppermute | solution.py:178
  18.7 1.9 collective-permute-start.6
  20.7 3.4 %collective-permute-start.7 = (bf16[256,512]{1,0:T(8,128)(2,1)S(1)}, bf16[256,512]{1,0:T(8,128)(2,1)S(1)}, u32[]{:S(2)}, u32[]{:S(2)}) collective-permute-start(bf16[256,512]{1,0:T(8,128)(2,1)S(1)} %bitcast.51), channel_id=1, source_target_pairs={{96,0},{0,32},{32,64},{64,96},{97,1},{1,33},{33,65},{65,97},{98,2}... | collective-permute-start | bytes 786440 | tf_op jit(solution)/shard_map/ppermute | solution.py:38
  24.0 1.9 collective-permute-start.3
  26.0 4.3 %collective-permute-start.5 = (bf16[256,512]{1,0:T(8,128)(2,1)S(1)}, bf16[256,512]{1,0:T(8,128)(2,1)S(1)}, u32[]{:S(2)}, u32[]{:S(2)}) collective-permute-start(bf16[256,512]{1,0:T(8,128)(2,1)S(1)} %bitcast.69), channel_id=1, source_target_pairs={{384,0},{0,128},{128,256},{256,384},{385,1},{1,129},{129,257},{257... | collective-permute-start | bytes 786440 | tf_op jit(solution)/shard_map/ppermute | solution.py:38
  34.9 8.9 %collective-permute-done.1 = bf16[24,2176]{1,0:T(8,128)(2,1)S(1)} collective-permute-done((bf16[24,2176]{1,0:T(8,128)(2,1)S(1)}, bf16[24,2176]{1,0:T(8,128)(2,1)S(1)}, u32[]{:S(2)}, u32[]{:S(2)}) %collective-permute-start.1) | collective-permute-done | bytes 104480 | tf_op jit(solution)/shard_map/ppermute | solution.py:42
  45.9 11.4 %collective-permute-done.2 = bf16[2,24,2176]{2,1,0:T(8,128)(2,1)S(1)} collective-permute-done((bf16[2,24,2176]{2,1,0:T(8,128)(2,1)S(1)}, bf16[2,24,2176]{2,1,0:T(8,128)(2,1)S(1)}, u32[]{:S(2)}, u32[]{:S(2)}) %collective-permute-start.2) | collective-permute-done | bytes 208928 | tf_op jit(solution)/shard_map/ppermute | solution.py:42
  60.1 12.7 %collective-permute-done.4 = bf16[272,512]{1,0:T(8,128)(2,1)S(1)} collective-permute-done((bf16[272,512]{1,0:T(8,128)(2,1)S(1)}, bf16[272,512]{1,0:T(8,128)(2,1)S(1)}, u32[]{:S(2)}, u32[]{:S(2)}) %collective-permute-start.4) | collective-permute-done | bytes 278560 | tf_op jit(solution)/shard_map/ppermute | solution.py:38
  72.9 5.7 %collective-permute-start.10 = (bf16[784,512]{1,0:T(8,128)(2,1)S(1)}, bf16[784,512]{1,0:T(8,128)(2,1)S(1)}, u32[]{:S(2)}, u32[]{:S(2)}) collective-permute-start(bf16[784,512]{1,0:T(8,128)(2,1)S(1)} %pad_maximum_fusion.rest), channel_id=1, source_target_pairs={{32,0},{64,32},{96,64},{0,96},{33,1},{65,33},{97,65},{1,97},{34,2}... | collective-permute-start | bytes 2408456 | tf_op jit(solution)/shard_map/ppermute | solution.py:38
  78.6 1.9 collective-permute-start.11
  81.6 13.7 %collective-permute-done.10.rest1 = bf16[784,512]{1,0:T(8,128)(2,1)S(1)} collective-permute-done((bf16[784,512]{1,0:T(8,128)(2,1)S(1)}, bf16[784,512]{1,0:T(8,128)(2,1)S(1)}, u32[]{:S(2)}, u32[]{:S(2)}) %collective-permute-start.10) | collective-permute-done | bytes 802848 | tf_op jit(solution)/shard_map/ppermute | solution.py:38
  96.2 5.4 %collective-permute-start.13 = (bf16[400,512]{1,0:T(8,128)(2,1)}, bf16[400,512]{1,0:T(8,128)(2,1)}, u32[]{:S(2)}, u32[]{:S(2)}) collective-permute-start(bf16[400,512]{1,0:T(8,128)(2,1)} %slice.119), channel_id=1, source_target_pairs={{32,0},{64,32},{96,64},{0,96},{33,1},{65,33},{97,65},{1,97},{34,2}... | collective-permute-start | bytes 1228808 | tf_op jit(solution)/shard_map/ppermute | solution.py:38
  105.6 2.0 copy.34
  107.6 2.1 copy.35
  112.9 4.6 %collective-permute-start.9 = (bf16[128,512]{1,0:T(8,128)(2,1)}, bf16[128,512]{1,0:T(8,128)(2,1)S(1)}, u32[]{:S(2)}, u32[]{:S(2)}) collective-permute-start(bf16[128,512]{1,0:T(8,128)(2,1)} %slice.93), channel_id=1, source_target_pairs={{32,0},{64,32},{96,64},{0,96},{33,1},{65,33},{97,65},{1,97},{34,2}... | collective-permute-start | bytes 393224 | tf_op jit(solution)/shard_map/ppermute | solution.py:38
  117.5 1.9 broadcast_select_fusion
  119.4 2.0 pad.26.down
  123.0 2.0 copy-done
  126.8 2.2 copy-done.1
  129.0 1.9 copy-done.3
  132.0 4.0 %shard_map.96 = f32[384,1152]{1,0:T(8,128)} custom-call(s32[3]{0:T(128)S(1)} %pad_add_fusion.place, bf16[768,2176]{1,0:T(8,128)(2,1)S(1)} %copy-done.3, bf16[2048,1024]{1,0:T(8,128)(2,1)S(1)} %copy-done.1, bf16[2048,128]{1,0:T(8,128)(2,1)S(1)} %copy-done.5), custom_call_target="tpu_custom_call" | custom-call | flops 1811939328 | bytes 10000000 | tf_op jit(solution)/shard_map/pallas_call | solution.py:160
  135.9 2.6 %collective-permute-start.14 = (f32[384,1152]{1,0:T(8,128)}, f32[384,1152]{1,0:T(8,128)}, u32[]{:S(2)}, u32[]{:S(2)}) collective-permute-start(f32[384,1152]{1,0:T(8,128)} %shard_map.96), channel_id=1, source_target_pairs={{0,16},{16,0},{1,17},{17,1},{2,18},{18,2},{3,19},{19,3},{4,20},{20... | collective-permute-start | bytes 5308424 | tf_op jit(solution)/shard_map/ppermute | solution.py:219
  148.0 2.2 copy-done.2
  151.2 2.7 %shard_map.95.near = f32[384,1152]{1,0:T(8,128)S(1)} custom-call(s32[3]{0:T(128)S(1)} %pad_add_fusion.place, bf16[768,2176]{1,0:T(8,128)(2,1)S(1)} %copy-done.4, bf16[2048,1024]{1,0:T(8,128)(2,1)S(1)} %copy-done.2, bf16[2048,128]{1,0:T(8,128)(2,1)S(1)} %copy-done.6), custom_call_target="tpu_custom_call" | custom-call | flops 1811939328 | bytes 10000000 | tf_op jit(solution)/shard_map/pallas_call | solution.py:160
  154.2 3.7 %shard_map.97 = (f32[64,4,128]{2,1,0:T(4,128)S(1)}, bf16[384,512]{1,0:T(8,128)(2,1)S(1)}, bf16[384,512]{1,0:T(8,128)(2,1)S(1)}, bf16[384,512]{1,0:T(8,128)(2,1)S...) custom-call(s32[3]{0:T(128)S(1)} %pad_add_fusion.place, f32[384,1152]{1,0:T(8,128)S(1)} %shard_map.95.near, ...), custom_call_target="tpu_custom_call" | custom-call | flops 201326592 | bytes 10000000 | tf_op jit(solution)/shard_map/pallas_call | solution.py:160
  162.2 13.2 %all-to-all-start = ((f32[64,4,128]{2,1,0:T(4,128)}), f32[64,4,128]{2,1,0:T(4,128)}, u32[]{:S(2)}, u32[]{:S(2)}) async-start(f32[64,4,128]{2,1,0:T(4,128)} %copy-done.19), calls=%async_computation | async-start | bytes 262144 | tf_op jit(solution)/shard_map/all_to_all | solution.py:243
  176.5 9.1 %all-to-all-done.arrived = f32[64,4,128]{2,1,0:T(4,128)} async-done(((f32[64,4,128]{2,1,0:T(4,128)}), f32[64,4,128]{2,1,0:T(4,128)}, u32[]{:S(2)}, u32[]{:S(2)}) %all-to-all-start) | async-done | bytes 131104 | tf_op jit(solution)/shard_map/all_to_all | solution.py:243
  190.4 2.0 shard_map.98
  193.1 7.6 %all-to-all-start.1 = ((f32[32,6,128]{2,1,0:T(8,128)}), f32[32,6,128]{2,1,0:T(8,128)S(1)}, u32[]{:S(2)}, u32[]{:S(2)}) async-start(f32[32,6,128]{2,1,0:T(8,128)} %copy-done.20), calls=%async_computation.1 | async-start | bytes 262144 | tf_op jit(solution)/shard_map/all_to_all | solution.py:251
  201.3 10.3 %all-to-all-done.1 = f32[32,6,128]{2,1,0:T(8,128)S(1)} async-done(((f32[32,6,128]{2,1,0:T(8,128)}), f32[32,6,128]{2,1,0:T(8,128)S(1)}, u32[]{:S(2)}, u32[]{:S(2)}) %all-to-all-start.1) | async-done | bytes 98336 | tf_op jit(solution)/shard_map/all_to_all | solution.py:251
  212.3 3.5 %all-to-all-start.2 = ((f32[16,2,128]{2,1,0:T(2,128)}), f32[16,2,128]{2,1,0:T(2,128)S(1)}, u32[]{:S(2)}, u32[]{:S(2)}) async-start(f32[16,2,128]{2,1,0:T(2,128)} %broadcast_in_dim.32), calls=%async_computation.2 | async-start | bytes 32768 | tf_op jit(solution)/shard_map/all_to_all | solution.py:256
  218.1 5.0 %all-to-all-done.2 = f32[16,2,128]{2,1,0:T(2,128)S(1)} async-done(((f32[16,2,128]{2,1,0:T(2,128)}), f32[16,2,128]{2,1,0:T(2,128)S(1)}, u32[]{:S(2)}, u32[]{:S(2)}) %all-to-all-start.2) | async-done | bytes 16416 | tf_op jit(solution)/shard_map/all_to_all | solution.py:256
  (132 shorter events, 44.8 us)
Async XLA Ops:
  7.2 11.5 %copy-start.23 = (bf16[2,128,896]{2,1,0:T(8,128)(2,1)S(1)}, bf16[2,128,896]{2,1,0:T(8,128)(2,1)}, u32[]{:S(2)}) copy-start(bf16[2,128,896]{2,1,0:T(8,128)(2,1)} %param.10) | copy-start | bytes 1376260
  7.2 119.6 %all-gather.2.cloned.1.call-start = ((), (), s32[]{:S(2)}) async-start(), calls=%async_computation.3 | async-start | bytes 3760128 | tf_op jit(solution)/shard_map/all_gather | solution.py:196
  9.9 22.9 %collective-permute-start = (bf16[12,2176]{1,0:T(8,128)(2,1)S(1)}, bf16[12,2176]{1,0:T(8,128)(2,1)S(1)}, u32[]{:S(2)}, u32[]{:S(2)}) collective-permute-start(bf16[12,2176]{1,0:T(8,128)(2,1)S(1)} %get-tuple-element.49), channel_id=1, source_target_pairs={{0,16},{16,0},{1,17},{17,1},{2,18},{18,2},{3,19},{19,3},{4,20},{20... | collective-permute-start | bytes 156680 | tf_op jit(solution)/shard_map/ppermute | solution.py:178
  18.7 41.3 %collective-permute-start.6 = (bf16[256,512]{1,0:T(8,128)(2,1)S(1)}, bf16[256,512]{1,0:T(8,128)(2,1)S(1)}, u32[]{:S(2)}, u32[]{:S(2)}) collective-permute-start(bf16[256,512]{1,0:T(8,128)(2,1)S(1)} %bitcast.50), channel_id=1, source_target_pairs={{32,0},{64,32},{96,64},{0,96},{33,1},{65,33},{97,65},{1,97},{34,2}... | collective-permute-start | bytes 786440 | tf_op jit(solution)/shard_map/ppermute | solution.py:38
  20.7 39.4 %collective-permute-start.7 = (bf16[256,512]{1,0:T(8,128)(2,1)S(1)}, bf16[256,512]{1,0:T(8,128)(2,1)S(1)}, u32[]{:S(2)}, u32[]{:S(2)}) collective-permute-start(bf16[256,512]{1,0:T(8,128)(2,1)S(1)} %bitcast.51), channel_id=1, source_target_pairs={{96,0},{0,32},{32,64},{64,96},{97,1},{1,33},{33,65},{65,97},{98,2}... | collective-permute-start | bytes 786440 | tf_op jit(solution)/shard_map/ppermute | solution.py:38
  24.0 36.0 %collective-permute-start.3 = (bf16[256,512]{1,0:T(8,128)(2,1)S(1)}, bf16[256,512]{1,0:T(8,128)(2,1)S(1)}, u32[]{:S(2)}, u32[]{:S(2)}) collective-permute-start(bf16[256,512]{1,0:T(8,128)(2,1)S(1)} %bitcast.68), channel_id=1, source_target_pairs={{128,0},{256,128},{384,256},{0,384},{129,1},{257,129},{385,257},{1... | collective-permute-start | bytes 786440 | tf_op jit(solution)/shard_map/ppermute | solution.py:38
  26.0 34.1 %collective-permute-start.5 = (bf16[256,512]{1,0:T(8,128)(2,1)S(1)}, bf16[256,512]{1,0:T(8,128)(2,1)S(1)}, u32[]{:S(2)}, u32[]{:S(2)}) collective-permute-start(bf16[256,512]{1,0:T(8,128)(2,1)S(1)} %bitcast.69), channel_id=1, source_target_pairs={{384,0},{0,128},{128,256},{256,384},{385,1},{1,129},{129,257},{257... | collective-permute-start | bytes 786440 | tf_op jit(solution)/shard_map/ppermute | solution.py:38
  32.9 10.9 %collective-permute-start.1 = (bf16[24,2176]{1,0:T(8,128)(2,1)S(1)}, bf16[24,2176]{1,0:T(8,128)(2,1)S(1)}, u32[]{:S(2)}, u32[]{:S(2)}) collective-permute-start(bf16[24,2176]{1,0:T(8,128)(2,1)S(1)} %maximum_select_fusion.4), channel_id=1, source_target_pairs={{0,1},{1,0},{2,3},{3,2},{4,5},{5,4},{6,7},{7,6},{8,9},{9,8},{10,11... | collective-permute-start | bytes 313352 | tf_op jit(solution)/shard_map/ppermute | solution.py:42
  43.9 13.4 %collective-permute-start.2 = (bf16[2,24,2176]{2,1,0:T(8,128)(2,1)S(1)}, bf16[2,24,2176]{2,1,0:T(8,128)(2,1)S(1)}, u32[]{:S(2)}, u32[]{:S(2)}) collective-permute-start(bf16[2,24,2176]{2,1,0:T(8,128)(2,1)S(1)} %maximum_select_fusion.2), channel_id=1, source_target_pairs={{0,128},{128,0},{1,129},{129,1},{2,130},{130,2},{3,131},{131,3},{4... | collective-permute-start | bytes 626696 | tf_op jit(solution)/shard_map/ppermute | solution.py:42
  57.3 15.5 %collective-permute-start.4 = (bf16[272,512]{1,0:T(8,128)(2,1)S(1)}, bf16[272,512]{1,0:T(8,128)(2,1)S(1)}, u32[]{:S(2)}, u32[]{:S(2)}) collective-permute-start(bf16[272,512]{1,0:T(8,128)(2,1)S(1)} %concatenate.80), channel_id=1, source_target_pairs={{256,0},{384,128},{0,256},{128,384},{257,1},{385,129},{1,257},{129... | collective-permute-start | bytes 835592 | tf_op jit(solution)/shard_map/ppermute | solution.py:38
  72.9 22.5 %collective-permute-start.10 = (bf16[784,512]{1,0:T(8,128)(2,1)S(1)}, bf16[784,512]{1,0:T(8,128)(2,1)S(1)}, u32[]{:S(2)}, u32[]{:S(2)}) collective-permute-start(bf16[784,512]{1,0:T(8,128)(2,1)S(1)} %pad_maximum_fusion.rest), channel_id=1, source_target_pairs={{32,0},{64,32},{96,64},{0,96},{33,1},{65,33},{97,65},{1,97},{34,2}... | collective-permute-start | bytes 2408456 | tf_op jit(solution)/shard_map/ppermute | solution.py:38
  78.6 23.0 %collective-permute-start.11 = (bf16[784,512]{1,0:T(8,128)(2,1)S(1)}, bf16[784,512]{1,0:T(8,128)(2,1)S(1)}, u32[]{:S(2)}, u32[]{:S(2)}) collective-permute-start(bf16[784,512]{1,0:T(8,128)(2,1)S(1)} %pad_maximum_fusion.rest), channel_id=1, source_target_pairs={{96,0},{0,32},{32,64},{64,96},{97,1},{1,33},{33,65},{65,97},{98,2}... | collective-permute-start | bytes 2408456 | tf_op jit(solution)/shard_map/ppermute | solution.py:38
  95.3 26.2 %copy-start.7 = (bf16[784,512]{1,0:T(8,128)(2,1)}, bf16[784,512]{1,0:T(8,128)(2,1)S(1)}, u32[]{:S(2)}) copy-start(bf16[784,512]{1,0:T(8,128)(2,1)S(1)} %collective-permute-done.10.rest1) | copy-start | bytes 2408452
  96.2 25.3 %collective-permute-start.13 = (bf16[400,512]{1,0:T(8,128)(2,1)}, bf16[400,512]{1,0:T(8,128)(2,1)}, u32[]{:S(2)}, u32[]{:S(2)}) collective-permute-start(bf16[400,512]{1,0:T(8,128)(2,1)} %slice.119), channel_id=1, source_target_pairs={{32,0},{64,32},{96,64},{0,96},{33,1},{65,33},{97,65},{1,97},{34,2}... | collective-permute-start | bytes 1228808 | tf_op jit(solution)/shard_map/ppermute | solution.py:38
  101.6 19.9 %copy-start.8 = (bf16[784,512]{1,0:T(8,128)(2,1)}, bf16[784,512]{1,0:T(8,128)(2,1)S(1)}, u32[]{:S(2)}) copy-start(bf16[784,512]{1,0:T(8,128)(2,1)S(1)} %collective-permute-done.11.rest3) | copy-start | bytes 2408452
  102.5 19.0 %collective-permute-start.12 = (bf16[384,512]{1,0:T(8,128)(2,1)}, bf16[384,512]{1,0:T(8,128)(2,1)}, u32[]{:S(2)}, u32[]{:S(2)}) collective-permute-start(bf16[384,512]{1,0:T(8,128)(2,1)} %slice.118), channel_id=1, source_target_pairs={{96,0},{0,32},{32,64},{64,96},{97,1},{1,33},{33,65},{65,97},{98,2}... | collective-permute-start | bytes 1179656 | tf_op jit(solution)/shard_map/ppermute | solution.py:38
  110.3 11.1 %collective-permute-start.8 = (bf16[128,512]{1,0:T(8,128)(2,1)}, bf16[128,512]{1,0:T(8,128)(2,1)S(1)}, u32[]{:S(2)}, u32[]{:S(2)}) collective-permute-start(bf16[128,512]{1,0:T(8,128)(2,1)} %slice.92), channel_id=1, source_target_pairs={{96,0},{0,32},{32,64},{64,96},{97,1},{1,33},{33,65},{65,97},{98,2}... | collective-permute-start | bytes 393224 | tf_op jit(solution)/shard_map/ppermute | solution.py:38
  112.9 8.6 %collective-permute-start.9 = (bf16[128,512]{1,0:T(8,128)(2,1)}, bf16[128,512]{1,0:T(8,128)(2,1)S(1)}, u32[]{:S(2)}, u32[]{:S(2)}) collective-permute-start(bf16[128,512]{1,0:T(8,128)(2,1)} %slice.93), channel_id=1, source_target_pairs={{32,0},{64,32},{96,64},{0,96},{33,1},{65,33},{97,65},{1,97},{34,2}... | collective-permute-start | bytes 393224 | tf_op jit(solution)/shard_map/ppermute | solution.py:38
  126.8 2.2 copy-start.1
  132.0 6.5 %copy-start.25 = (bf16[32,896]{1,0:T(8,128)(2,1)S(1)}, bf16[32,896]{1,0:T(8,128)(2,1)}, u32[]{:S(2)}) copy-start(bf16[32,896]{1,0:T(8,128)(2,1)} %param.12) | copy-start | bytes 172036
  132.0 7.9 %copy-start.28 = (bf16[896]{0:T(1024)(128)(2,1)S(1)}, bf16[896]{0:T(1024)(128)(2,1)}, u32[]{:S(2)}) copy-start(bf16[896]{0:T(1024)(128)(2,1)} %param.13) | copy-start | bytes 5380
  132.0 16.0 %copy-start.4 = (bf16[768,2176]{1,0:T(8,128)(2,1)S(1)}, bf16[768,2176]{1,0:T(8,128)(2,1)}, u32[]{:S(2)}) copy-start(bf16[768,2176]{1,0:T(8,128)(2,1)} %all-gather.2.cloned.1.call-done.tok) | copy-start | bytes 10027012
  135.9 18.3 %collective-permute-start.14 = (f32[384,1152]{1,0:T(8,128)}, f32[384,1152]{1,0:T(8,128)}, u32[]{:S(2)}, u32[]{:S(2)}) collective-permute-start(f32[384,1152]{1,0:T(8,128)} %shard_map.96), channel_id=1, source_target_pairs={{0,16},{16,0},{1,17},{17,1},{2,18},{18,2},{3,19},{19,3},{4,20},{20... | collective-permute-start | bytes 5308424 | tf_op jit(solution)/shard_map/ppermute | solution.py:219
  148.0 2.2 copy-start.2
  151.2 2.8 %copy-start.24 = (pred[128,384]{1,0:T(8,128)(4,1)S(1)}, pred[128,384]{1,0:T(8,128)(4,1)}, u32[]{:S(2)}) copy-start(pred[128,384]{1,0:T(8,128)(4,1)} %broadcast_compare_fusion) | copy-start | bytes 147460
  151.2 2.8 %copy-start.26 = (s32[128]{0:T(128)S(1)}, s32[128]{0:T(128)}, u32[]{:S(2)}) copy-start(s32[128]{0:T(128)} %get-tuple-element.50) | copy-start | bytes 1540
  151.2 2.8 %copy-start.27 = (s32[128]{0:T(128)S(1)}, s32[128]{0:T(128)}, u32[]{:S(2)}) copy-start(s32[128]{0:T(128)} %get-tuple-element.51) | copy-start | bytes 1540
  151.2 3.0 %copy-start.9 = (bf16[128,512]{1,0:T(8,128)(2,1)S(1)}, bf16[128,512]{1,0:T(8,128)(2,1)}, u32[]{:S(2)}) copy-start(bf16[128,512]{1,0:T(8,128)(2,1)} %pad.27.b_gate) | copy-start | bytes 393220
  151.2 3.0 %copy-start.10 = (bf16[128,512]{1,0:T(8,128)(2,1)S(1)}, bf16[128,512]{1,0:T(8,128)(2,1)}, u32[]{:S(2)}) copy-start(bf16[128,512]{1,0:T(8,128)(2,1)} %pad.28.b_up) | copy-start | bytes 393220
  162.2 23.5 %all-to-all-start = ((f32[64,4,128]{2,1,0:T(4,128)}), f32[64,4,128]{2,1,0:T(4,128)}, u32[]{:S(2)}, u32[]{:S(2)}) async-start(f32[64,4,128]{2,1,0:T(4,128)} %copy-done.19), calls=%async_computation | async-start | bytes 262144 | tf_op jit(solution)/shard_map/all_to_all | solution.py:243
  193.1 18.5 %all-to-all-start.1 = ((f32[32,6,128]{2,1,0:T(8,128)}), f32[32,6,128]{2,1,0:T(8,128)S(1)}, u32[]{:S(2)}, u32[]{:S(2)}) async-start(f32[32,6,128]{2,1,0:T(8,128)} %copy-done.20), calls=%async_computation.1 | async-start | bytes 262144 | tf_op jit(solution)/shard_map/all_to_all | solution.py:251
  212.3 10.8 %all-to-all-start.2 = ((f32[16,2,128]{2,1,0:T(2,128)}), f32[16,2,128]{2,1,0:T(2,128)S(1)}, u32[]{:S(2)}, u32[]{:S(2)}) async-start(f32[16,2,128]{2,1,0:T(2,128)} %broadcast_in_dim.32), calls=%async_computation.2 | async-start | bytes 32768 | tf_op jit(solution)/shard_map/all_to_all | solution.py:256
  (16 other events, 15.7 us)
Sparse Core Ops, SparseCore 0:
  72.9 53.8 all-gather.1

commit v5 on v4

v5 whole, which is shorter than its diff:
```python
import functools

import jax
import jax.numpy as jnp
from jax import lax
from jax.experimental import pallas as pl
from jax.experimental.pallas import tpu as pltpu
from jax.sharding import Mesh, PartitionSpec as P

SEQS = 4
ROWS = 12
RANK = 16
WIDTH = 4096
DPO_BETA = 0.1
LOSS_SCALE = 1024.0
F32 = jnp.float32
BF16 = jnp.bfloat16

AXES = ("s", "t", "x", "c", "z", "yl")
SIZES = (2, 2, 4, 2, 8, 2)
DP = ("s", "t", "x", "c")
BLK = ("z", "yl")
SWAP = [(0, 1), (1, 0)]

SLICE = 128
HALF = WIDTH // 2
LANES = 128
COLS = 512
SKIP = 384
GROUP = 384
BLOCKS = GROUP // ROWS
CONTRACT_LAST = (((1,), (1,)), ((), ()))


def swapped(value, axis, index):
    far = lax.ppermute(value, axis, SWAP)
    return jnp.where(index == 0, jnp.stack([value, far]), jnp.stack([far, value]))


def split(value, terms):
    parts = []
    for _ in range(terms):
        parts.append(value.astype(BF16))
        value = value - parts[-1].astype(F32)
    return parts


def dot(a, b, dims=(((1,), (0,)), ((), ()))):
    return lax.dot_general(a, b, dims, preferred_element_type=F32)


def early_products(place, w, down, p0, r1, l1, r2, l2, r3, l3, r4, l4, tok, acc, low):
    z = place[1]

    def put(k, begin, value):
        start = lax.rem(z + 8 + k, 8) * 8 * ROWS + begin
        tok[pl.ds(pl.multiple_of(start, 48), value.shape[0]), :] = value

    put(0, 0, p0[...])
    for k, (right, left) in enumerate(((r1, l1), (r2, l2), (r3, l3)), 1):
        put(-k, 0, right[...])
        put(k, 0, left[...])
    put(4, 0, r4[...])
    put(4, 4 * ROWS, l4[...])
    for n in range(4):
        part = slice(n * COLS // 2, (n + 1) * COLS // 2)
        acc[:, part] = dot(tok[:, 0 : HALF // 2], w[:, part])
    low[...] = dot(tok[:, 0:HALF], down[...])


def late_products(place, rows, w, acc, out):
    out[...] = acc[...] + dot(rows[...], w[...])


def products(far, place, tok, w, acc):
    half = (lambda place: 1 - place[0]) if far else (lambda place: place[0])
    part = COLS // 2
    return pl.pallas_call(
        late_products,
        grid_spec=pltpu.PrefetchScalarGridSpec(
            num_scalar_prefetch=1,
            grid=(4,),
            in_specs=[
                pl.BlockSpec((GROUP, HALF // 2), lambda n, place: (half(place), 1)),
                pl.BlockSpec((HALF // 2, part), lambda n, place: (0, n)),
                pl.BlockSpec((GROUP, part), lambda n, place: (half(place), n)),
            ],
            out_specs=pl.BlockSpec((GROUP, part), lambda n, place: (0, n)),
        ),
        out_shape=jax.ShapeDtypeStruct((GROUP, 2 * COLS), F32),
        compiler_params=pltpu.CompilerParams(vmem_limit_bytes=12 * 1024 * 1024),
        cost_estimate=pl.CostEstimate(flops=GROUP * HALF * 2 * COLS, bytes_accessed=6_000_000, transcendentals=0),
    )(place, tok, w, acc)


def score(place, near, partner, low_ref, b_gate, b_up, readout, signs, count, message, low_t, k_out, k, sems):
    low_b = low_ref[...]
    gate_ref = near[:, 0:COLS] + partner[:, 0:COLS]
    up_ref = near[:, COLS : 2 * COLS] + partner[:, COLS : 2 * COLS]
    gate_pol = gate_ref + dot(low_b, b_gate[...])
    up_pol = up_ref + dot(low_b, b_up[...])
    sig_ref = jax.nn.sigmoid(gate_ref)
    sig_pol = jax.nn.sigmoid(gate_pol)
    act_pol = gate_pol * sig_pol
    read = readout[...].astype(F32)
    change = act_pol * up_pol - gate_ref * sig_ref * up_ref
    k_gate = read * sig_pol * (1.0 + gate_pol * (1.0 - sig_pol)) * up_pol
    k_up = read * act_pol
    read_b = jnp.broadcast_to(readout[...], (8, COLS))
    change_row = sum(dot(read_b, part, CONTRACT_LAST) for part in split(change, 3))
    sign = signs[place[0]]
    gaps = sum(dot(part, sign, CONTRACT_LAST) for part in split(change_row, 3))
    tail = jnp.broadcast_to(gaps[0:1, :] + count[...], (2 * RANK, LANES))
    high, rest = split(k_gate, 2)
    k[0], k[1] = high, rest
    copies = [pltpu.make_async_copy(k.at[i], k_out.at[i], sems.at[i]) for i in range(4)]
    copies[0].start()
    copies[1].start()
    mixed = dot(b_gate[0 : 2 * RANK, :], high, CONTRACT_LAST) + dot(b_gate[0 : 2 * RANK, :], rest, CONTRACT_LAST)
    high, rest = split(k_up, 2)
    k[2], k[3] = high, rest
    copies[2].start()
    copies[3].start()
    mixed_up = dot(b_up[0 : 2 * RANK, :], high, CONTRACT_LAST) + dot(b_up[0 : 2 * RANK, :], rest, CONTRACT_LAST)
    mixed = mixed + mixed_up
    for core in range(2):
        lines = slice(2 * RANK * core, 2 * RANK * (core + 1))
        for i in range(3):
            message[lines, i, :] = mixed[:, i * LANES : (i + 1) * LANES]
        message[lines, 3, :] = tail
    low_t[...] = low_b.astype(F32).T[0 : 2 * RANK, :]
    for copy in copies:
        copy.wait()


def close(place, arrived, signs, valid, low_t, k_in, tok_in, out, total_out, k, tok, sems):
    tok_copy = pltpu.make_async_copy(tok_in, tok, sems.at[0])
    k_copy = pltpu.make_async_copy(k_in, k, sems.at[1])
    tok_copy.start()
    k_copy.start()
    core = place[0]
    sums = [jnp.sum(arrived[2 * RANK * h : 2 * RANK * (h + 1)], axis=0) for h in range(2)]
    totals = [jnp.concatenate([total[i : i + 1, :] for i in range(3)], axis=1) for total in sums]
    tails = [total[3:4, :] for total in sums]
    pair_total = jnp.maximum(tails[0][:, 64:65] + tails[1][:, 64:65], 1.0)
    logs, cotangents, terms = 0.0, [], []
    for h in range(2):
        logit = DPO_BETA * tails[h]
        logs = logs + jnp.sum(
            valid[h] * (jnp.minimum(logit, 0.0) - jnp.log1p(jnp.exp(-jnp.abs(logit)))), axis=1, keepdims=True
        )
        scaled = -LOSS_SCALE * DPO_BETA * valid[h] * jax.nn.sigmoid(-logit) / pair_total
        scaled = jnp.broadcast_to(scaled, (8, LANES))
        cotangent = sum(dot(part, signs[h]) for part in split(scaled, 3))
        cotangents.append(cotangent[0:1, :])
        projected = jnp.broadcast_to(totals[h], (8, GROUP)) * cotangent
        if h == 0:
            tok_copy.wait()
        terms.append(dot(projected.astype(BF16), tok[h * GROUP : (h + 1) * GROUP, 0:HALF]))
    grad_a = (terms[0] + terms[1])[0:1, :]
    own = jnp.where(core == 0, cotangents[0], cotangents[1])
    high, rest = split(low_t[...] * own, 2)
    k_copy.wait()
    gate = dot(high[0:RANK], k[0]) + dot(high[0:RANK], k[1]) + dot(rest[0:RANK], k[0])
    up = dot(high[RANK:], k[2]) + dot(high[RANK:], k[3]) + dot(rest[RANK:], k[2])
    for i in range(4):
        out[0:RANK, i, :] = gate[:, i * LANES : (i + 1) * LANES]
        out[RANK : 2 * RANK, i, :] = up[:, i * LANES : (i + 1) * LANES]
    line = lax.broadcasted_iota(jnp.int32, (2 * RANK, SLICE), 0)
    slices = jnp.zeros((2 * RANK, SLICE), F32)
    for i in range(RANK):
        here = jnp.broadcast_to(grad_a[:, i * SLICE : (i + 1) * SLICE], (2 * RANK, SLICE))
        other_s, at_x, at_t = i // 8, i // 2 % 4, i % 2
        yh = 2 * (1 - place[2] if other_s else place[2]) + at_t
        slices = jnp.where(line == (yh * 4 + at_x) * 2 + core, here, slices)
    out[:, 4, :] = slices
    out[:, 5, :] = jnp.broadcast_to(0.5 * logs, (2 * RANK, LANES))
    total_out[...] = jnp.broadcast_to(pair_total, (8, LANES))


def kernel(function, shapes, arguments, flops, grant, scratch=(), in_hbm=0, out_hbm=0):
    vmem = pl.BlockSpec(memory_space=pltpu.VMEM)
    smem = pl.BlockSpec(memory_space=pltpu.SMEM)
    hbm = pl.BlockSpec(memory_space=pltpu.HBM)
    return pl.pallas_call(
        function,
        out_shape=tuple(jax.ShapeDtypeStruct(*s) for s in shapes),
        in_specs=[smem] + [vmem] * (len(arguments) - 1 - in_hbm) + [hbm] * in_hbm,
        out_specs=(vmem,) * (len(shapes) - out_hbm) + (hbm,) * out_hbm,
        scratch_shapes=list(scratch),
        compiler_params=pltpu.CompilerParams(vmem_limit_bytes=grant * 1024 * 1024),
        cost_estimate=pl.CostEstimate(flops=flops, bytes_accessed=10_000_000, transcendentals=0),
    )(*arguments)


def along(value, axis, k):
    n = lax.axis_size(axis)
    return lax.ppermute(value, axis, [(i, (i + k) % n) for i in range(n)])


def on_device(tokens, sequence_labels, response_mask, frozen, down, up, readout):
    s, t, core, z, yl = (lax.axis_index(a) for a in ("s", "t", "c", "z", "yl"))
    place = jnp.stack([core, z, s]).astype(jnp.int32)
    code = jnp.where(response_mask > 0, sequence_labels, SEQS)

    low_half = jnp.concatenate([frozen[0, :, :COLS], frozen[1, :, :COLS]], axis=1)
    high_half = jnp.concatenate([frozen[0, :, SKIP:], frozen[1, :, SKIP:]], axis=1)
    mine = jnp.where(t == 0, low_half, high_half)
    other = lax.ppermute(jnp.where(t == 0, high_half, low_half), "t", SWAP)
    pair_w = jnp.where(
        t == 0, jnp.concatenate([mine, other], axis=0), jnp.concatenate([other, mine], axis=0)
    )
    w_own = lax.all_gather(pair_w, "x", axis=0, tiled=True)

    by_core = tokens.reshape(ROWS, 2, 2, 4, 2, SLICE).transpose(4, 1, 0, 3, 2, 5)
    by_core = jnp.where(s == 0, by_core, by_core[:, ::-1]).transpose(0, 2, 1, 3, 4, 5)
    by_core = by_core.reshape(2, ROWS, HALF)
    code_lanes = jnp.pad(code.reshape(ROWS, 1).astype(BF16), ((0, 0), (0, LANES - 1)))
    keep = jnp.concatenate([jnp.where(core == 0, by_core[0], by_core[1]), code_lanes], axis=1)
    give = jnp.concatenate([jnp.where(core == 0, by_core[1], by_core[0]), code_lanes], axis=1)
    take = lax.ppermute(give, "c", SWAP)
    pair = jnp.where(
        core == 0, jnp.concatenate([keep, take], axis=0), jnp.concatenate([take, keep], axis=0)
    )
    eight = swapped(swapped(pair, "yl", yl), "t", t).reshape(8 * ROWS, HALF + LANES)

    eight, pair_w = lax.optimization_barrier((eight, pair_w))
    other_s = lax.ppermute(pair_w, "s", SWAP)
    right, left, ring = eight, eight, [eight]
    for step in range(3):
        right, left = along(right, "z", 1), along(left, "z", -1)
        ring += [right, left]
        if step == 1:
            right, left, other_s = lax.optimization_barrier((right, left, other_s))
    ring += [along(right[: 4 * ROWS], "z", 1), along(left[4 * ROWS :], "z", -1)]
    w_other = lax.all_gather(other_s, "x", axis=0, tiled=True)

    has = [jnp.max((code == q).astype(F32)) for q in range(SEQS)]
    count = jnp.where(jnp.arange(LANES) == 64, has[0] * has[1] + has[2] * has[3], 0.0).reshape(1, LANES)
    count = count + lax.ppermute(count, "s", SWAP)
    count = count + lax.ppermute(count, "x", [(0, 1), (1, 0), (2, 3), (3, 2)])
    count_lanes = count + lax.ppermute(count, "x", [(0, 2), (2, 0), (1, 3), (3, 1)])

    down_half = down.reshape(2, 2, 4, 2, SLICE, 2 * RANK).transpose(3, 0, 2, 1, 4, 5)
    down_half = jnp.where(core == 0, down_half[0], down_half[1])
    down_half = jnp.where(s == 0, down_half, down_half[::-1]).reshape(HALF, 2 * RANK)
    down_half = jnp.pad(down_half, ((0, 0), (0, LANES - 2 * RANK)))
    tok, acc, low_acc = kernel(
        early_products,
        [((2 * GROUP, HALF + LANES), BF16), ((2 * GROUP, 2 * COLS), F32), ((2 * GROUP, LANES), F32)],
        (place, w_own, down_half, *ring),
        2 * GROUP * HALF * 2 * COLS, 16,
    )
    low_acc = low_acc.reshape(2, GROUP, LANES)
    low_near = jnp.where(core == 0, low_acc[0], low_acc[1])
    low_far = jnp.where(core == 0, low_acc[1], low_acc[0])
    low = (low_near + lax.ppermute(low_far, "c", SWAP)).astype(BF16)

    units = jnp.where(t == 0, up[:, :COLS], up[:, SKIP:])
    b_gate = jnp.pad(units[:RANK], ((0, LANES - RANK), (0, 0)))
    b_up = jnp.pad(units[RANK:], ((RANK, LANES - 2 * RANK), (0, 0)))
    shared = (jnp.arange(COLS) >= 2 * COLS - readout.shape[0]).astype(BF16)
    read = jnp.where(t == 0, readout[:COLS], readout[SKIP:] * shared).reshape(1, COLS)

    codes = tok[:, HALF].astype(jnp.int32).reshape(2, GROUP)
    pair_of = jnp.arange(LANES, dtype=jnp.int32)
    block_of = jnp.arange(GROUP, dtype=jnp.int32) // ROWS
    inside = (pair_of[:, None] // 2 == block_of[None, :])[None]
    chosen = inside & (codes[:, None, :] == 2 * (pair_of % 2)[None, :, None])
    rejected = inside & (codes[:, None, :] == 2 * (pair_of % 2)[None, :, None] + 1)
    signs = chosen.astype(BF16) - rejected.astype(BF16)
    valid = (jnp.any(chosen, axis=2) & jnp.any(rejected, axis=2)).astype(F32).reshape(2, 1, LANES)

    w_other, low, b_gate, b_up, read, signs, valid, count_lanes = lax.optimization_barrier(
        (w_other, low, b_gate, b_up, read, signs, valid, count_lanes)
    )
    far = products(True, place, tok, w_other, acc)
    partner = lax.ppermute(far, "c", SWAP)
    near = products(False, place, tok, w_other, acc)
    message, low_t, k = kernel(
        score,
        [((4 * RANK, 4, LANES), F32), ((2 * RANK, GROUP), F32), ((4, GROUP, COLS), BF16)],
        (place, near, partner, low, b_gate, b_up, read, signs, count_lanes),
        8 * GROUP * COLS * LANES, 16,
        scratch=[pltpu.VMEM((4, GROUP, COLS), BF16), pltpu.SemaphoreType.DMA((4,))],
        out_hbm=1,
    )
    arrived = lax.all_to_all(message, ("c", "t", "z", "yl"), split_axis=0, concat_axis=0)
    outgoing, pair_total = kernel(
        close,
        [((2 * RANK, 6, LANES), F32), ((8, LANES), F32)],
        (place, arrived, signs, valid, low_t, k, tok),
        16 * GROUP * HALF * 2, 16,
        scratch=[
            pltpu.VMEM((4, GROUP, COLS), BF16),
            pltpu.VMEM((2 * GROUP, HALF + LANES), BF16),
            pltpu.SemaphoreType.DMA((2,)),
        ],
        in_hbm=2,
    )

    arrived = lax.all_to_all(outgoing, DP, split_axis=0, concat_axis=0)
    summed = jnp.sum(arrived.reshape(2, 2, 8, 6, LANES), axis=(0, 2))
    grad_b = jnp.pad(summed[0, :4], ((0, 3), (0, 0))) + jnp.pad(summed[1, :4], ((3, 0), (0, 0)))
    columns = summed[:, 4]
    log_total = summed[0, 5, 0]
    grad_a = lax.all_to_all(
        jnp.broadcast_to(columns[None], (16, 2, SLICE)), BLK, split_axis=0, concat_axis=0
    )
    grad_a = grad_a.transpose(2, 1, 0).reshape(SLICE, 2 * RANK)
    return -log_total / pair_total[0, 0], grad_a, grad_b.reshape(1, 7 * LANES)


def solution(mesh):
    fine = Mesh(mesh.devices.reshape(SIZES), AXES)
    in_specs = (
        P(AXES, None),
        P(AXES, None),
        P(AXES, None),
        P(None, DP, BLK),
        P(),
        P(None, BLK),
        P(BLK),
    )
    out_specs = (P(), P(DP, None), P(DP, BLK))
    return jax.shard_map(
        on_device, mesh=fine, in_specs=in_specs, out_specs=out_specs, check_vma=False
    )
```

time: 233 us -> 229 us (0.983)
  blocking collectives: 0 us -> 18.3 us
  waiting for transfers between devices: 73.1 us -> 55.9 us
  local copies, waits for them, and re-layouts: 40.9 us -> 25.9 us
  starting transfers between devices: 74.4 us -> 82.5 us
  other arithmetic: 7.32 us -> 10.3 us
    ppermute x11 -> x14, starting transfers between devices: 34.8 us -> 59.9 us  [the longest x8 32.2 us: along(): return lax.ppermute(value, axis, [(i, (i + k) % n) for i in range(n)])]
    all_to_all x0 -> x1, blocking collectives: none -> 18.3 us  [on_device(): lax.all_to_all(message, ('c', 't', 'z', 'yl'), split_axis=0, concat_axis=0)]
    all_to_all x1 -> x0, starting transfers between devices: 13.2 us -> none  [on_device(): lax.all_to_all(message, ('c', 't', 'z', 'yl'), split_axis=0, concat_axis=0)]
    all_to_all x1 -> x0, waiting for transfers between devices: 9.14 us -> none  [on_device(): lax.all_to_all(message, ('c', 't', 'z', 'yl'), split_axis=0, concat_axis=0)]
    slice x10 -> x2, local copies, waits for them, and re-layouts: 8.24 us -> 0.03 us  [on_device(): ring += [along(right[:4 * ROWS], 'z', 1), along(left[4 * ROWS:], 'z', -1)]]
    ppermute x2, waiting for transfers between devices: 20.3 us -> 12.7 us  [swapped(): far = lax.ppermute(value, axis, SWAP)]
    unnamed x65 -> x72, local copies, waits for them, and re-layouts: 24.9 us -> 18.5 us
    pallas_call x0 -> x2, Pallas kernels: none -> 5.36 us  [products(): pl.pallas_call(late_products, grid_spec=pltpu.PrefetchScalarGridSpec(num_...]
  transfers between devices with their start and end apart: 19 -> 22, of which waited for: 8 -> 9; matrix products, arithmetic and copies ran while one was open for 10% -> 7% of each run, Pallas kernels for 2% -> 3%
where the time goes in v5:
time: 229 us; the launch traced here: 228 us
  starting transfers between devices  82.5 us (36%)
  waiting for transfers between devices  55.9 us (24%)
  local copies, waits for them, and re-layouts  25.9 us (11%)
  between operations  19.9 us (9%)
  blocking collectives  18.3 us (8%)
  Pallas kernels  15 us (7%)
  other arithmetic  10.3 us (4%)
    ppermute x8, starting transfers between devices, along(): return lax.ppermute(value, axis, [(i, (i + k) % n) for i in range(n)])  32.2 us
    unnamed x72, local copies, waits for them, and re-layouts  18.5 us
    all_to_all x1, blocking collectives, on_device(): lax.all_to_all(message, ('c', 't', 'z', 'yl'), split_axis=0, concat_axis=0)  18.3 us
    ppermute x1, waiting for transfers between devices, on_device(): other_s = lax.ppermute(pair_w, 's', SWAP)  13.7 us
    ppermute x2, waiting for transfers between devices, swapped(): far = lax.ppermute(value, axis, SWAP)  12.7 us
    all_to_all x1, waiting for transfers between devices, on_device(): arrived = lax.all_to_all(outgoing, DP, split_axis=0, concat_axis=0)  10.2 us
    ppermute x1, waiting for transfers between devices, on_device(): other = lax.ppermute(jnp.where(t == 0, high_half, low_half), 't', SWAP)  9.92 us
    pallas_call x3, Pallas kernels, kernel(): pl.pallas_call(function, out_shape=tuple((jax.ShapeDtypeStruct(*s) for s...  9.61 us
  transfers between devices with their start and end apart: 22, of which 9 were waited for; matrix products, arithmetic and copies ran while one was open for 7% of the time, Pallas kernels for 3%

profile of v5, /device:TPU:1, one launch (start us, length us, event | category | flops | bytes accessed | tf_op | source)
XLA Modules:
  0.0 227.7 jit_solution(5841946060635853507)
XLA Ops:
  8.5 5.0 %collective-permute-start = (bf16[128,1024]{1,0:T(8,128)(2,1)S(1)}, bf16[128,1024]{1,0:T(8,128)(2,1)S(1)}, u32[]{:S(2)}, u32[]{:S(2)}) collective-permute-start(bf16[128,1024]{1,0:T(8,128)(2,1)S(1)} %get-tuple-element.53), channel_id=1, source_target_pairs={{0,128},{128,0},{1,129},{129,1},{2,130},{130,2},{3,131},{131,3},{4... | collective-permute-start | bytes 786440 | tf_op jit(solution)/shard_map/ppermute | solution.py:209
  14.9 9.9 %collective-permute-done = bf16[128,1024]{1,0:T(8,128)(2,1)S(1)} collective-permute-done((bf16[128,1024]{1,0:T(8,128)(2,1)S(1)}, bf16[128,1024]{1,0:T(8,128)(2,1)S(1)}, u32[]{:S(2)}, u32[]{:S(2)}) %collective-permute-start) | collective-permute-done | bytes 262176 | tf_op jit(solution)/shard_map/ppermute | solution.py:209
  26.0 3.5 %collective-permute-start.1 = (bf16[12,2176]{1,0:T(8,128)(2,1)S(1)}, bf16[12,2176]{1,0:T(8,128)(2,1)S(1)}, u32[]{:S(2)}, u32[]{:S(2)}) collective-permute-start(bf16[12,2176]{1,0:T(8,128)(2,1)S(1)} %get-tuple-element.65), channel_id=1, source_target_pairs={{0,16},{16,0},{1,17},{17,1},{2,18},{18,2},{3,19},{19,3},{4,20},{20... | collective-permute-start | bytes 156680 | tf_op jit(solution)/shard_map/ppermute | solution.py:221
  30.5 2.3 %collective-permute-start.2 = (bf16[24,2176]{1,0:T(8,128)(2,1)S(1)}, bf16[24,2176]{1,0:T(8,128)(2,1)S(1)}, u32[]{:S(2)}, u32[]{:S(2)}) collective-permute-start(bf16[24,2176]{1,0:T(8,128)(2,1)S(1)} %maximum_select_fusion.5), channel_id=1, source_target_pairs={{0,1},{1,0},{2,3},{3,2},{4,5},{5,4},{6,7},{7,6},{8,9},{9,8},{10,11... | collective-permute-start | bytes 313352 | tf_op jit(solution)/shard_map/ppermute | solution.py:36
  32.9 3.6 %collective-permute-done.2 = bf16[24,2176]{1,0:T(8,128)(2,1)S(1)} collective-permute-done((bf16[24,2176]{1,0:T(8,128)(2,1)S(1)}, bf16[24,2176]{1,0:T(8,128)(2,1)S(1)}, u32[]{:S(2)}, u32[]{:S(2)}) %collective-permute-start.2) | collective-permute-done | bytes 104480 | tf_op jit(solution)/shard_map/ppermute | solution.py:36
  36.6 4.3 %collective-permute-start.3 = (bf16[2,24,2176]{2,1,0:T(8,128)(2,1)S(1)}, bf16[2,24,2176]{2,1,0:T(8,128)(2,1)S(1)}, u32[]{:S(2)}, u32[]{:S(2)}) collective-permute-start(bf16[2,24,2176]{2,1,0:T(8,128)(2,1)S(1)} %maximum_select_fusion.3), channel_id=1, source_target_pairs={{0,128},{128,0},{1,129},{129,1},{2,130},{130,2},{3,131},{131,3},{4... | collective-permute-start | bytes 626696 | tf_op jit(solution)/shard_map/ppermute | solution.py:36
  41.0 9.1 %collective-permute-done.3 = bf16[2,24,2176]{2,1,0:T(8,128)(2,1)S(1)} collective-permute-done((bf16[2,24,2176]{2,1,0:T(8,128)(2,1)S(1)}, bf16[2,24,2176]{2,1,0:T(8,128)(2,1)S(1)}, u32[]{:S(2)}, u32[]{:S(2)}) %collective-permute-start.3) | collective-permute-done | bytes 208928 | tf_op jit(solution)/shard_map/ppermute | solution.py:36
  50.1 4.0 %collective-permute-start.4 = (bf16[96,2176]{1,0:T(8,128)(2,1)S(1)}, bf16[96,2176]{1,0:T(8,128)(2,1)S(1)}, u32[]{:S(2)}, u32[]{:S(2)}) collective-permute-start(bf16[96,2176]{1,0:T(8,128)(2,1)S(1)} %bitcast.48), channel_id=1, source_target_pairs={{0,2},{2,4},{4,6},{6,8},{8,10},{10,12},{12,14},{14,0},{1,3},{3,5},... | collective-permute-start | bytes 1253384 | tf_op jit(solution)/shard_map/ppermute | solution.py:198
  54.2 8.7 %collective-permute-start.5 = (bf16[96,2176]{1,0:T(8,128)(2,1)S(1)}, bf16[96,2176]{1,0:T(8,128)(2,1)S(1)}, u32[]{:S(2)}, u32[]{:S(2)}) collective-permute-start(bf16[96,2176]{1,0:T(8,128)(2,1)S(1)} %bitcast.49), channel_id=1, source_target_pairs={{0,14},{2,0},{4,2},{6,4},{8,6},{10,8},{12,10},{14,12},{1,15},{3,1}... | collective-permute-start | bytes 1253384 | tf_op jit(solution)/shard_map/ppermute | solution.py:198
  65.4 8.3 %collective-permute-start.8 = (bf16[256,1024]{1,0:T(8,128)(2,1)}, bf16[256,1024]{1,0:T(8,128)(2,1)}, u32[]{:S(2)}, u32[]{:S(2)}) collective-permute-start(bf16[256,1024]{1,0:T(8,128)(2,1)} %maximum_select_fusion), channel_id=1, source_target_pairs={{0,256},{256,0},{1,257},{257,1},{2,258},{258,2},{3,259},{259,3},{4... | collective-permute-start | bytes 1572872 | tf_op jit(solution)/shard_map/ppermute | solution.py:228
  73.7 1.9 collective-permute-start.14
  76.5 1.9 collective-permute-start.6
  78.5 4.6 %collective-permute-start.7 = (bf16[96,2176]{1,0:T(8,128)(2,1)S(1)}, bf16[96,2176]{1,0:T(8,128)(2,1)S(1)}, u32[]{:S(2)}, u32[]{:S(2)}) collective-permute-start(bf16[96,2176]{1,0:T(8,128)(2,1)S(1)} %collective-permute-done.5.l1), channel_id=1, source_target_pairs={{0,14},{2,0},{4,2},{6,4},{8,6},{10,8},{12,10},{14,12},{1,15},{3,1}... | collective-permute-start | bytes 1253384 | tf_op jit(solution)/shard_map/ppermute | solution.py:198
  83.1 13.7 %collective-permute-done.8 = bf16[256,1024]{1,0:T(8,128)(2,1)} collective-permute-done((bf16[256,1024]{1,0:T(8,128)(2,1)}, bf16[256,1024]{1,0:T(8,128)(2,1)}, u32[]{:S(2)}, u32[]{:S(2)}) %collective-permute-start.8) | collective-permute-done | bytes 524320 | tf_op jit(solution)/shard_map/ppermute | solution.py:228
  98.1 1.9 collective-permute-start.9
  100.0 4.6 %collective-permute-start.10 = (bf16[96,2176]{1,0:T(8,128)(2,1)S(1)}, bf16[96,2176]{1,0:T(8,128)(2,1)S(1)}, u32[]{:S(2)}, u32[]{:S(2)}) collective-permute-start(bf16[96,2176]{1,0:T(8,128)(2,1)S(1)} %collective-permute-done.7.l2), channel_id=1, source_target_pairs={{0,14},{2,0},{4,2},{6,4},{8,6},{10,8},{12,10},{14,12},{1,15},{3,1}... | collective-permute-start | bytes 1253384 | tf_op jit(solution)/shard_map/ppermute | solution.py:198
  104.7 2.9 %collective-permute-start.15 = (f32[1,128]{1,0:T(1,128)S(1)}, f32[1,128]{1,0:T(1,128)S(1)}, u32[]{:S(2)}, u32[]{:S(2)}) collective-permute-start(f32[1,128]{1,0:T(1,128)S(1)} %fusion.18), channel_id=1, source_target_pairs={{0,32},{32,0},{64,96},{96,64},{1,33},{33,1},{65,97},{97,65},{2,34}... | collective-permute-start | bytes 1544 | tf_op jit(solution)/shard_map/ppermute | solution.py:241
  108.1 2.8 %collective-permute-done.9.r3 = bf16[96,2176]{1,0:T(8,128)(2,1)S(1)} collective-permute-done((bf16[96,2176]{1,0:T(8,128)(2,1)S(1)}, bf16[96,2176]{1,0:T(8,128)(2,1)S(1)}, u32[]{:S(2)}, u32[]{:S(2)}) %collective-permute-start.9) | collective-permute-done | bytes 417824 | tf_op jit(solution)/shard_map/ppermute | solution.py:198
  112.9 4.6 %collective-permute-start.12 = (bf16[48,2176]{1,0:T(8,128)(2,1)S(1)}, bf16[48,2176]{1,0:T(8,128)(2,1)S(1)}, u32[]{:S(2)}, u32[]{:S(2)}) collective-permute-start(bf16[48,2176]{1,0:T(8,128)(2,1)S(1)} %slice.109), channel_id=1, source_target_pairs={{0,14},{2,0},{4,2},{6,4},{8,6},{10,8},{12,10},{14,12},{1,15},{3,1}... | collective-permute-start | bytes 626696 | tf_op jit(solution)/shard_map/ppermute | solution.py:198
  118.1 4.3 %collective-permute-start.16 = (f32[1,128]{1,0:T(1,128)S(1)}, f32[1,128]{1,0:T(1,128)S(1)}, u32[]{:S(2)}, u32[]{:S(2)}) collective-permute-start(f32[1,128]{1,0:T(1,128)S(1)} %fusion.20), channel_id=1, source_target_pairs={{0,64},{64,0},{32,96},{96,32},{1,65},{65,1},{33,97},{97,33},{2,66}... | collective-permute-start | bytes 1544 | tf_op jit(solution)/shard_map/ppermute | solution.py:242
  137.1 3.4 %shard_map.94 = (bf16[768,2176]{1,0:T(8,128)(2,1)S(1)}, f32[768,1024]{1,0:T(8,128)S(1)}, f32[768,128]{1,0:T(8,128)S(1)}) custom-call(s32[3]{0:T(128)S(1)} %pad_add_fusion.place, bf16[1024,1024]{1,0:T(8,128)(2,1)S(1)} %copy-done.3, bf16[2048,128]{1,0:T(8,128)(2,1)S(1)} %copy-done.4, bf16[96,2176]{1,0:T(8,128)(2,1)S(1)} %bitcast.50, ...), custom_call_target="tpu_custom_call" | custom-call | flops 1610612736 | bytes 10000000 | tf_op jit(solution)/shard_map/pallas_call | solution.py:185
  144.1 5.2 %collective-permute-start.13 = (f32[384,128]{1,0:T(8,128)S(1)}, f32[384,128]{1,0:T(8,128)S(1)}, u32[]{:S(2)}, u32[]{:S(2)}) collective-permute-start(f32[384,128]{1,0:T(8,128)S(1)} %slice_select_fusion.1), channel_id=1, source_target_pairs={{0,16},{16,0},{1,17},{17,1},{2,18},{18,2},{3,19},{19,3},{4,20},{20... | collective-permute-start | bytes 589832 | tf_op jit(solution)/shard_map/ppermute | solution.py:257
  156.6 2.7 %shard_map.96 = f32[384,1024]{1,0:T(8,128)S(1)} custom-call(s32[3]{0:T(128)S(1)} %pad_add_fusion.place, bf16[768,2176]{1,0:T(8,128)(2,1)S(1)} %get-tuple-element.28.rows.tok_in, bf16[1024,1024]{1,0:T(8,128)(2,1)S(1)} %copy-done.2, f32[768,1024]{1,0:T(8,128)S(1)} %copy-done.1), custom_call_target="tpu_custom_call" | custom-call | flops 805306368 | bytes 6000000 | tf_op jit(solution)/shard_map/pallas_call | solution.py:78
  159.4 2.1 collective-permute-start.17
  161.4 2.7 %shard_map.95.near = f32[384,1024]{1,0:T(8,128)S(1)} custom-call(s32[3]{0:T(128)S(1)} %pad_add_fusion.place, bf16[768,2176]{1,0:T(8,128)(2,1)S(1)} %get-tuple-element.28.rows.tok_in, bf16[1024,1024]{1,0:T(8,128)(2,1)S(1)} %copy-done.2, f32[768,1024]{1,0:T(8,128)S(1)} %copy-done.1), custom_call_target="tpu_custom_call" | custom-call | flops 805306368 | bytes 6000000 | tf_op jit(solution)/shard_map/pallas_call | solution.py:78
  164.8 3.7 %shard_map.97 = (f32[64,4,128]{2,1,0:T(4,128)S(1)}, f32[32,384]{1,0:T(8,128)S(1)}, bf16[4,384,512]{2,1,0:T(8,128)(2,1)S(1)}) custom-call(s32[3]{0:T(128)S(1)} %pad_add_fusion.place, f32[384,1024]{1,0:T(8,128)S(1)} %shard_map.95.near, f32[384,1024]{1,0:T(8,128)S(1)} %collective-permute-done.17.partner, bf16[384,128]{1,0:T(8,128)(2,1)S(1)} %copy-done.22, ...), custom_call_target="tpu_custom_call" | custom-call | flops 201326592 | bytes 10000000 | tf_op jit(solution)/shard_map/pallas_call | solution.py:185
  168.6 18.3 %all_to_all.15.arrived = f32[64,4,128]{2,1,0:T(4,128)S(1)} all-to-all(f32[64,4,128]{2,1,0:T(4,128)S(1)} %get-tuple-element.39), channel_id=1, replica_groups=mesh['s'=2,'t'=2,'x'=4,'c'=2,'z'=8,'yl'=2] {'c','t','z','yl'}, dimensions={0} | all-to-all | bytes 262144 | tf_op jit(solution)/shard_map/all_to_all | solution.py:288
  186.9 2.5 %shard_map.98 = (f32[32,6,128]{2,1,0:T(8,128)S(1)}, f32[8,128]{1,0:T(8,128)S(1)}) custom-call(s32[3]{0:T(128)S(1)} %pad_add_fusion.place, f32[64,4,128]{2,1,0:T(4,128)S(1)} %all_to_all.15.arrived, bf16[2,128,384]{2,1,0:T(8,128)(2,1)S(1)} %fusion.5.signs, f32[2,1,128]{2,1,0:T(1,128)S(1)} %bitcast.51, f32[32,384]{1,0:T(8,128)S(1)} %get-tuple-element.41.low_t, ...), custom_call_target="tpu_custom_call" | custom-call | flops 25165824 | bytes 10000000 | tf_op jit(solution)/shard_map/pallas_call | solution.py:185
  190.0 6.8 %all-to-all-start.1 = ((f32[32,6,128]{2,1,0:T(8,128)}), f32[32,6,128]{2,1,0:T(8,128)S(1)}, u32[]{:S(2)}, u32[]{:S(2)}) async-start(f32[32,6,128]{2,1,0:T(8,128)} %copy-done.25), calls=%async_computation.1 | async-start | bytes 262144 | tf_op jit(solution)/shard_map/all_to_all | solution.py:302
  197.4 10.2 %all-to-all-done.1 = f32[32,6,128]{2,1,0:T(8,128)S(1)} async-done(((f32[32,6,128]{2,1,0:T(8,128)}), f32[32,6,128]{2,1,0:T(8,128)S(1)}, u32[]{:S(2)}, u32[]{:S(2)}) %all-to-all-start.1) | async-done | bytes 98336 | tf_op jit(solution)/shard_map/all_to_all | solution.py:302
  208.3 3.5 %all-to-all-start.2 = ((f32[16,2,128]{2,1,0:T(2,128)}), f32[16,2,128]{2,1,0:T(2,128)S(1)}, u32[]{:S(2)}, u32[]{:S(2)}) async-start(f32[16,2,128]{2,1,0:T(2,128)} %broadcast_in_dim.28), calls=%async_computation.2 | async-start | bytes 32768 | tf_op jit(solution)/shard_map/all_to_all | solution.py:307
  214.2 4.9 %all-to-all-done.2 = f32[16,2,128]{2,1,0:T(2,128)S(1)} async-done(((f32[16,2,128]{2,1,0:T(2,128)}), f32[16,2,128]{2,1,0:T(2,128)S(1)}, u32[]{:S(2)}, u32[]{:S(2)}) %all-to-all-start.2) | async-done | bytes 16416 | tf_op jit(solution)/shard_map/all_to_all | solution.py:307
  (148 shorter events, 39.9 us)
Async XLA Ops:
  7.2 119.3 %all-gather.3.cloned.1.call-start = ((), (), s32[]{:S(2)}) async-start(), calls=%async_computation.3 | async-start | bytes 2621440 | tf_op jit(solution)/shard_map/all_gather | solution.py:213
  8.5 16.3 %collective-permute-start = (bf16[128,1024]{1,0:T(8,128)(2,1)S(1)}, bf16[128,1024]{1,0:T(8,128)(2,1)S(1)}, u32[]{:S(2)}, u32[]{:S(2)}) collective-permute-start(bf16[128,1024]{1,0:T(8,128)(2,1)S(1)} %get-tuple-element.53), channel_id=1, source_target_pairs={{0,128},{128,0},{1,129},{129,1},{2,130},{130,2},{3,131},{131,3},{4... | collective-permute-start | bytes 786440 | tf_op jit(solution)/shard_map/ppermute | solution.py:209
  14.1 61.5 %copy-start.28 = (bf16[4096,32]{0,1:T(8,128)(2,1)S(1)}, bf16[4096,32]{0,1:T(8,128)(2,1)}, u32[]{:S(2)}) copy-start(bf16[4096,32]{0,1:T(8,128)(2,1)} %param.11) | copy-start | bytes 786436
  25.8 127.4 %all-gather.5.cloned.1.call-start = ((), (), s32[]{:S(2)}) async-start(), calls=%async_computation.4 | async-start | bytes 2621440 | tf_op jit(solution)/shard_map/all_gather | solution.py:236
  25.9 57.2 %copy-start.30 = (bf16[32,896]{1,0:T(8,128)(2,1)S(1)}, bf16[32,896]{1,0:T(8,128)(2,1)}, u32[]{:S(2)}) copy-start(bf16[32,896]{1,0:T(8,128)(2,1)} %param.12) | copy-start | bytes 172036
  26.0 4.4 %collective-permute-start.1 = (bf16[12,2176]{1,0:T(8,128)(2,1)S(1)}, bf16[12,2176]{1,0:T(8,128)(2,1)S(1)}, u32[]{:S(2)}, u32[]{:S(2)}) collective-permute-start(bf16[12,2176]{1,0:T(8,128)(2,1)S(1)} %get-tuple-element.65), channel_id=1, source_target_pairs={{0,16},{16,0},{1,17},{17,1},{2,18},{18,2},{3,19},{19,3},{4,20},{20... | collective-permute-start | bytes 156680 | tf_op jit(solution)/shard_map/ppermute | solution.py:221
  30.5 6.1 %collective-permute-start.2 = (bf16[24,2176]{1,0:T(8,128)(2,1)S(1)}, bf16[24,2176]{1,0:T(8,128)(2,1)S(1)}, u32[]{:S(2)}, u32[]{:S(2)}) collective-permute-start(bf16[24,2176]{1,0:T(8,128)(2,1)S(1)} %maximum_select_fusion.5), channel_id=1, source_target_pairs={{0,1},{1,0},{2,3},{3,2},{4,5},{5,4},{6,7},{7,6},{8,9},{9,8},{10,11... | collective-permute-start | bytes 313352 | tf_op jit(solution)/shard_map/ppermute | solution.py:36
  36.6 13.5 %collective-permute-start.3 = (bf16[2,24,2176]{2,1,0:T(8,128)(2,1)S(1)}, bf16[2,24,2176]{2,1,0:T(8,128)(2,1)S(1)}, u32[]{:S(2)}, u32[]{:S(2)}) collective-permute-start(bf16[2,24,2176]{2,1,0:T(8,128)(2,1)S(1)} %maximum_select_fusion.3), channel_id=1, source_target_pairs={{0,128},{128,0},{1,129},{129,1},{2,130},{130,2},{3,131},{131,3},{4... | collective-permute-start | bytes 626696 | tf_op jit(solution)/shard_map/ppermute | solution.py:36
  50.1 48.0 %copy-start.5 = (bf16[2,2,24,2176]{3,2,1,0:T(8,128)(2,1)}, bf16[2,2,24,2176]{3,2,1,0:T(8,128)(2,1)S(1)}, u32[]{:S(2)}) copy-start(bf16[2,2,24,2176]{3,2,1,0:T(8,128)(2,1)S(1)} %maximum_select_fusion.1) | copy-start | bytes 1253380
  50.1 26.4 %collective-permute-start.4 = (bf16[96,2176]{1,0:T(8,128)(2,1)S(1)}, bf16[96,2176]{1,0:T(8,128)(2,1)S(1)}, u32[]{:S(2)}, u32[]{:S(2)}) collective-permute-start(bf16[96,2176]{1,0:T(8,128)(2,1)S(1)} %bitcast.48), channel_id=1, source_target_pairs={{0,2},{2,4},{4,6},{6,8},{8,10},{10,12},{12,14},{14,0},{1,3},{3,5},... | collective-permute-start | bytes 1253384 | tf_op jit(solution)/shard_map/ppermute | solution.py:198
  54.2 24.3 %collective-permute-start.5 = (bf16[96,2176]{1,0:T(8,128)(2,1)S(1)}, bf16[96,2176]{1,0:T(8,128)(2,1)S(1)}, u32[]{:S(2)}, u32[]{:S(2)}) collective-permute-start(bf16[96,2176]{1,0:T(8,128)(2,1)S(1)} %bitcast.49), channel_id=1, source_target_pairs={{0,14},{2,0},{4,2},{6,4},{8,6},{10,8},{12,10},{14,12},{1,15},{3,1}... | collective-permute-start | bytes 1253384 | tf_op jit(solution)/shard_map/ppermute | solution.py:198
  65.4 31.5 %collective-permute-start.8 = (bf16[256,1024]{1,0:T(8,128)(2,1)}, bf16[256,1024]{1,0:T(8,128)(2,1)}, u32[]{:S(2)}, u32[]{:S(2)}) collective-permute-start(bf16[256,1024]{1,0:T(8,128)(2,1)} %maximum_select_fusion), channel_id=1, source_target_pairs={{0,256},{256,0},{1,257},{257,1},{2,258},{258,2},{3,259},{259,3},{4... | collective-permute-start | bytes 1572872 | tf_op jit(solution)/shard_map/ppermute | solution.py:228
  73.7 30.9 %collective-permute-start.14 = (f32[1,128]{1,0:T(1,128)S(1)}, f32[1,128]{1,0:T(1,128)S(1)}, u32[]{:S(2)}, u32[]{:S(2)}) collective-permute-start(f32[1,128]{1,0:T(1,128)S(1)} %compare_select_fusion), channel_id=1, source_target_pairs={{0,256},{256,0},{1,257},{257,1},{2,258},{258,2},{3,259},{259,3},{4... | collective-permute-start | bytes 1544 | tf_op jit(solution)/shard_map/ppermute | solution.py:240
  75.8 28.8 %copy-start.31 = (bf16[896]{0:T(1024)(128)(2,1)S(1)}, bf16[896]{0:T(1024)(128)(2,1)}, u32[]{:S(2)}) copy-start(bf16[896]{0:T(1024)(128)(2,1)} %param.13) | copy-start | bytes 5380
  76.5 21.4 %copy-start.14 = (bf16[96,2176]{1,0:T(8,128)(2,1)}, bf16[96,2176]{1,0:T(8,128)(2,1)S(1)}, u32[]{:S(2)}) copy-start(bf16[96,2176]{1,0:T(8,128)(2,1)S(1)} %collective-permute-done.4.r1) | copy-start | bytes 1253380
  76.5 20.3 %collective-permute-start.6 = (bf16[96,2176]{1,0:T(8,128)(2,1)S(1)}, bf16[96,2176]{1,0:T(8,128)(2,1)S(1)}, u32[]{:S(2)}, u32[]{:S(2)}) collective-permute-start(bf16[96,2176]{1,0:T(8,128)(2,1)S(1)} %collective-permute-done.4.r1), channel_id=1, source_target_pairs={{0,2},{2,4},{4,6},{6,8},{8,10},{10,12},{12,14},{14,0},{1,3},{3,5},... | collective-permute-start | bytes 1253384 | tf_op jit(solution)/shard_map/ppermute | solution.py:198
  78.5 34.4 %copy-start.16 = (bf16[96,2176]{1,0:T(8,128)(2,1)}, bf16[96,2176]{1,0:T(8,128)(2,1)S(1)}, u32[]{:S(2)}) copy-start(bf16[96,2176]{1,0:T(8,128)(2,1)S(1)} %collective-permute-done.5.l1) | copy-start | bytes 1253380
  78.5 18.4 %collective-permute-start.7 = (bf16[96,2176]{1,0:T(8,128)(2,1)S(1)}, bf16[96,2176]{1,0:T(8,128)(2,1)S(1)}, u32[]{:S(2)}, u32[]{:S(2)}) collective-permute-start(bf16[96,2176]{1,0:T(8,128)(2,1)S(1)} %collective-permute-done.5.l1), channel_id=1, source_target_pairs={{0,14},{2,0},{4,2},{6,4},{8,6},{10,8},{12,10},{14,12},{1,15},{3,1}... | collective-permute-start | bytes 1253384 | tf_op jit(solution)/shard_map/ppermute | solution.py:198
  96.9 26.5 %copy-start.18 = (bf16[96,2176]{1,0:T(8,128)(2,1)}, bf16[96,2176]{1,0:T(8,128)(2,1)S(1)}, u32[]{:S(2)}) copy-start(bf16[96,2176]{1,0:T(8,128)(2,1)S(1)} %collective-permute-done.6.r2) | copy-start | bytes 1253380
  96.9 26.5 %copy-start.20 = (bf16[96,2176]{1,0:T(8,128)(2,1)}, bf16[96,2176]{1,0:T(8,128)(2,1)S(1)}, u32[]{:S(2)}) copy-start(bf16[96,2176]{1,0:T(8,128)(2,1)S(1)} %collective-permute-done.7.l2) | copy-start | bytes 1253380
  98.1 12.8 %collective-permute-start.9 = (bf16[96,2176]{1,0:T(8,128)(2,1)S(1)}, bf16[96,2176]{1,0:T(8,128)(2,1)S(1)}, u32[]{:S(2)}, u32[]{:S(2)}) collective-permute-start(bf16[96,2176]{1,0:T(8,128)(2,1)S(1)} %collective-permute-done.6.r2), channel_id=1, source_target_pairs={{0,2},{2,4},{4,6},{6,8},{8,10},{10,12},{12,14},{14,0},{1,3},{3,5},... | collective-permute-start | bytes 1253384 | tf_op jit(solution)/shard_map/ppermute | solution.py:198
  100.0 12.8 %collective-permute-start.10 = (bf16[96,2176]{1,0:T(8,128)(2,1)S(1)}, bf16[96,2176]{1,0:T(8,128)(2,1)S(1)}, u32[]{:S(2)}, u32[]{:S(2)}) collective-permute-start(bf16[96,2176]{1,0:T(8,128)(2,1)S(1)} %collective-permute-done.7.l2), channel_id=1, source_target_pairs={{0,14},{2,0},{4,2},{6,4},{8,6},{10,8},{12,10},{14,12},{1,15},{3,1}... | collective-permute-start | bytes 1253384 | tf_op jit(solution)/shard_map/ppermute | solution.py:198
  104.7 12.8 %collective-permute-start.15 = (f32[1,128]{1,0:T(1,128)S(1)}, f32[1,128]{1,0:T(1,128)S(1)}, u32[]{:S(2)}, u32[]{:S(2)}) collective-permute-start(f32[1,128]{1,0:T(1,128)S(1)} %fusion.18), channel_id=1, source_target_pairs={{0,32},{32,0},{64,96},{96,64},{1,33},{33,1},{65,97},{97,65},{2,34}... | collective-permute-start | bytes 1544 | tf_op jit(solution)/shard_map/ppermute | solution.py:241
  110.9 15.0 %copy-start.8 = (bf16[96,2176]{1,0:T(8,128)(2,1)}, bf16[96,2176]{1,0:T(8,128)(2,1)S(1)}, u32[]{:S(2)}) copy-start(bf16[96,2176]{1,0:T(8,128)(2,1)S(1)} %collective-permute-done.9.r3) | copy-start | bytes 1253380
  110.9 14.9 %collective-permute-start.11 = (bf16[48,2176]{1,0:T(8,128)(2,1)S(1)}, bf16[48,2176]{1,0:T(8,128)(2,1)S(1)}, u32[]{:S(2)}, u32[]{:S(2)}) collective-permute-start(bf16[48,2176]{1,0:T(8,128)(2,1)S(1)} %slice.108), channel_id=1, source_target_pairs={{0,2},{2,4},{4,6},{6,8},{8,10},{10,12},{12,14},{14,0},{1,3},{3,5},... | collective-permute-start | bytes 626696 | tf_op jit(solution)/shard_map/ppermute | solution.py:198
  112.8 13.0 %copy-start.10 = (bf16[96,2176]{1,0:T(8,128)(2,1)}, bf16[96,2176]{1,0:T(8,128)(2,1)S(1)}, u32[]{:S(2)}) copy-start(bf16[96,2176]{1,0:T(8,128)(2,1)S(1)} %collective-permute-done.10.l3) | copy-start | bytes 1253380
  112.9 12.9 %collective-permute-start.12 = (bf16[48,2176]{1,0:T(8,128)(2,1)S(1)}, bf16[48,2176]{1,0:T(8,128)(2,1)S(1)}, u32[]{:S(2)}, u32[]{:S(2)}) collective-permute-start(bf16[48,2176]{1,0:T(8,128)(2,1)S(1)} %slice.109), channel_id=1, source_target_pairs={{0,14},{2,0},{4,2},{6,4},{8,6},{10,8},{12,10},{14,12},{1,15},{3,1}... | collective-permute-start | bytes 626696 | tf_op jit(solution)/shard_map/ppermute | solution.py:198
  118.1 7.2 %collective-permute-start.16 = (f32[1,128]{1,0:T(1,128)S(1)}, f32[1,128]{1,0:T(1,128)S(1)}, u32[]{:S(2)}, u32[]{:S(2)}) collective-permute-start(f32[1,128]{1,0:T(1,128)S(1)} %fusion.20), channel_id=1, source_target_pairs={{0,64},{64,0},{32,96},{96,32},{1,65},{65,1},{33,97},{97,33},{2,66}... | collective-permute-start | bytes 1544 | tf_op jit(solution)/shard_map/ppermute | solution.py:242
  144.1 7.3 %collective-permute-start.13 = (f32[384,128]{1,0:T(8,128)S(1)}, f32[384,128]{1,0:T(8,128)S(1)}, u32[]{:S(2)}, u32[]{:S(2)}) collective-permute-start(f32[384,128]{1,0:T(8,128)S(1)} %slice_select_fusion.1), channel_id=1, source_target_pairs={{0,16},{16,0},{1,17},{17,1},{2,18},{18,2},{3,19},{19,3},{4,20},{20... | collective-permute-start | bytes 589832 | tf_op jit(solution)/shard_map/ppermute | solution.py:257
  159.4 5.4 %collective-permute-start.17 = (f32[384,1024]{1,0:T(8,128)S(1)}, f32[384,1024]{1,0:T(8,128)S(1)}, u32[]{:S(2)}, u32[]{:S(2)}) collective-permute-start(f32[384,1024]{1,0:T(8,128)S(1)} %shard_map.96), channel_id=1, source_target_pairs={{0,16},{16,0},{1,17},{17,1},{2,18},{18,2},{3,19},{19,3},{4,20},{20... | collective-permute-start | bytes 4718600 | tf_op jit(solution)/shard_map/ppermute | solution.py:278
  190.0 17.6 %all-to-all-start.1 = ((f32[32,6,128]{2,1,0:T(8,128)}), f32[32,6,128]{2,1,0:T(8,128)S(1)}, u32[]{:S(2)}, u32[]{:S(2)}) async-start(f32[32,6,128]{2,1,0:T(8,128)} %copy-done.25), calls=%async_computation.1 | async-start | bytes 262144 | tf_op jit(solution)/shard_map/all_to_all | solution.py:302
  208.3 10.8 %all-to-all-start.2 = ((f32[16,2,128]{2,1,0:T(2,128)}), f32[16,2,128]{2,1,0:T(2,128)S(1)}, u32[]{:S(2)}, u32[]{:S(2)}) async-start(f32[16,2,128]{2,1,0:T(2,128)} %broadcast_in_dim.28), calls=%async_computation.2 | async-start | bytes 32768 | tf_op jit(solution)/shard_map/all_to_all | solution.py:307
  (25 other events, 71.8 us)
Sparse Core Ops, SparseCore 0:
  25.9 41.7 all-gather.2
  97.0 32.3 all-gather.4

commit v6 on v5

--- a/solution.py
+++ b/solution.py
@@ -49,27 +49,34 @@
     return lax.dot_general(a, b, dims, preferred_element_type=F32)
 
 
-def early_products(place, w, down, p0, r1, l1, r2, l2, r3, l3, r4, l4, tok, acc, low):
+def early_products(place, down, w_in, p0, r1, l1, r2, l2, r3, l3, r4, l4, low, tok_out, acc_out, tok, w, acc, sems):
     z = place[1]
-
-    def put(k, begin, value):
-        start = lax.rem(z + 8 + k, 8) * 8 * ROWS + begin
-        tok[pl.ds(pl.multiple_of(start, 48), value.shape[0]), :] = value
-
-    put(0, 0, p0[...])
-    for k, (right, left) in enumerate(((r1, l1), (r2, l2), (r3, l3)), 1):
-        put(-k, 0, right[...])
-        put(k, 0, left[...])
-    put(4, 0, r4[...])
-    put(4, 4 * ROWS, l4[...])
+    block = 8 * ROWS
+    w_copy = pltpu.make_async_copy(w_in, w, sems.at[9])
+    w_copy.start()
+    moves = [(0, 0, p0), (-1, 0, r1), (1, 0, l1), (-2, 0, r2), (2, 0, l2), (-3, 0, r3), (3, 0, l3), (4, 0, r4), (4, 4 * ROWS, l4)]
+    copies = []
+    for n, (k, begin, ref) in enumerate(moves):
+        start = pl.multiple_of(lax.rem(z + 8 + k, 8) * block + begin, 4 * ROWS)
+        copies.append(pltpu.make_async_copy(ref, tok.at[pl.ds(start, ref.shape[0]), :], sems.at[n]))
+        copies[-1].start()
+    for copy in copies:
+        copy.wait()
+    tok_copy = pltpu.make_async_copy(tok, tok_out, sems.at[10])
+    tok_copy.start()
+    low[...] = dot(tok[:, 0:HALF], down[...])
+    w_copy.wait()
     for n in range(4):
         part = slice(n * COLS // 2, (n + 1) * COLS // 2)
         acc[:, part] = dot(tok[:, 0 : HALF // 2], w[:, part])
-    low[...] = dot(tok[:, 0:HALF], down[...])
+    acc_copy = pltpu.make_async_copy(acc, acc_out, sems.at[11])
+    acc_copy.start()
+    acc_copy.wait()
+    tok_copy.wait()
 
 
 def late_products(place, rows, w, acc, out):
-    out[...] = acc[...] + dot(rows[...], w[...])
+    out[...] = acc[...] + dot(rows[...], w[...].reshape(HALF // 2, COLS // 2))
 
 
 def products(far, place, tok, w, acc):
@@ -82,7 +89,7 @@
             grid=(4,),
             in_specs=[
                 pl.BlockSpec((GROUP, HALF // 2), lambda n, place: (half(place), 1)),
-                pl.BlockSpec((HALF // 2, part), lambda n, place: (0, n)),
+                pl.BlockSpec((4, 2 * SLICE, part), lambda n, place: (0, 0, n)),
                 pl.BlockSpec((GROUP, part), lambda n, place: (half(place), n)),
             ],
             out_specs=pl.BlockSpec((GROUP, part), lambda n, place: (0, n)),
@@ -178,14 +185,14 @@
     total_out[...] = jnp.broadcast_to(pair_total, (8, LANES))
 
 
-def kernel(function, shapes, arguments, flops, grant, scratch=(), in_hbm=0, out_hbm=0):
+def kernel(function, shapes, arguments, flops, grant, scratch=(), in_any=0, out_hbm=0):
     vmem = pl.BlockSpec(memory_space=pltpu.VMEM)
     smem = pl.BlockSpec(memory_space=pltpu.SMEM)
     hbm = pl.BlockSpec(memory_space=pltpu.HBM)
     return pl.pallas_call(
         function,
         out_shape=tuple(jax.ShapeDtypeStruct(*s) for s in shapes),
-        in_specs=[smem] + [vmem] * (len(arguments) - 1 - in_hbm) + [hbm] * in_hbm,
+        in_specs=[smem] + [vmem] * (len(arguments) - 1 - in_any) + [pl.BlockSpec(memory_space=pl.ANY)] * in_any,
         out_specs=(vmem,) * (len(shapes) - out_hbm) + (hbm,) * out_hbm,
         scratch_shapes=list(scratch),
         compiler_params=pltpu.CompilerParams(vmem_limit_bytes=grant * 1024 * 1024),
@@ -202,15 +209,6 @@
     s, t, core, z, yl = (lax.axis_index(a) for a in ("s", "t", "c", "z", "yl"))
     place = jnp.stack([core, z, s]).astype(jnp.int32)
     code = jnp.where(response_mask > 0, sequence_labels, SEQS)
-
-    low_half = jnp.concatenate([frozen[0, :, :COLS], frozen[1, :, :COLS]], axis=1)
-    high_half = jnp.concatenate([frozen[0, :, SKIP:], frozen[1, :, SKIP:]], axis=1)
-    mine = jnp.where(t == 0, low_half, high_half)
-    other = lax.ppermute(jnp.where(t == 0, high_half, low_half), "t", SWAP)
-    pair_w = jnp.where(
-        t == 0, jnp.concatenate([mine, other], axis=0), jnp.concatenate([other, mine], axis=0)
-    )
-    w_own = lax.all_gather(pair_w, "x", axis=0, tiled=True)
 
     by_core = tokens.reshape(ROWS, 2, 2, 4, 2, SLICE).transpose(4, 1, 0, 3, 2, 5)
     by_core = jnp.where(s == 0, by_core, by_core[:, ::-1]).transpose(0, 2, 1, 3, 4, 5)
@@ -222,10 +220,24 @@
     pair = jnp.where(
         core == 0, jnp.concatenate([keep, take], axis=0), jnp.concatenate([take, keep], axis=0)
     )
-    eight = swapped(swapped(pair, "yl", yl), "t", t).reshape(8 * ROWS, HALF + LANES)
-
+    four = swapped(pair, "yl", yl)
+
+    low_half = jnp.concatenate([frozen[0, :, :COLS], frozen[1, :, :COLS]], axis=1)
+    high_half = jnp.concatenate([frozen[0, :, SKIP:], frozen[1, :, SKIP:]], axis=1)
+    mine = jnp.where(t == 0, low_half, high_half)
+    other = lax.ppermute(jnp.where(t == 0, high_half, low_half), "t", SWAP)
+    four, other = lax.optimization_barrier((four, other))
+    pair_w = jnp.where(
+        t == 0, jnp.concatenate([mine, other], axis=0), jnp.concatenate([other, mine], axis=0)
+    )
+    w_own = lax.all_gather(pair_w, "x", axis=0, tiled=True)
+
+    eight = swapped(four, "t", t).reshape(8 * ROWS, HALF + LANES)
+
+    has = [jnp.max((code == q).astype(F32)) for q in range(SEQS)]
+    count_rows = jnp.broadcast_to((has[0] * has[1] + has[2] * has[3]).astype(BF16), (16, 2 * COLS))
     eight, pair_w = lax.optimization_barrier((eight, pair_w))
-    other_s = lax.ppermute(pair_w, "s", SWAP)
+    other_s = lax.ppermute(jnp.concatenate([pair_w, count_rows], axis=0), "s", SWAP)
     right, left, ring = eight, eight, [eight]
     for step in range(3):
         right, left = along(right, "z", 1), along(left, "z", -1)
@@ -233,23 +245,25 @@
         if step == 1:
             right, left, other_s = lax.optimization_barrier((right, left, other_s))
     ring += [along(right[: 4 * ROWS], "z", 1), along(left[4 * ROWS :], "z", -1)]
-    w_other = lax.all_gather(other_s, "x", axis=0, tiled=True)
-
-    has = [jnp.max((code == q).astype(F32)) for q in range(SEQS)]
-    count = jnp.where(jnp.arange(LANES) == 64, has[0] * has[1] + has[2] * has[3], 0.0).reshape(1, LANES)
-    count = count + lax.ppermute(count, "s", SWAP)
-    count = count + lax.ppermute(count, "x", [(0, 1), (1, 0), (2, 3), (3, 2)])
-    count_lanes = count + lax.ppermute(count, "x", [(0, 2), (2, 0), (1, 3), (3, 1)])
+    other_s = jnp.concatenate([other_s[: 2 * SLICE], other_s[2 * SLICE :] + count_rows], axis=0)
+    w_other = lax.all_gather(other_s, "x", axis=0, tiled=True).reshape(4, 2 * SLICE + 16, 2 * COLS)
 
     down_half = down.reshape(2, 2, 4, 2, SLICE, 2 * RANK).transpose(3, 0, 2, 1, 4, 5)
     down_half = jnp.where(core == 0, down_half[0], down_half[1])
     down_half = jnp.where(s == 0, down_half, down_half[::-1]).reshape(HALF, 2 * RANK)
     down_half = jnp.pad(down_half, ((0, 0), (0, LANES - 2 * RANK)))
-    tok, acc, low_acc = kernel(
+    low_acc, tok, acc = kernel(
         early_products,
-        [((2 * GROUP, HALF + LANES), BF16), ((2 * GROUP, 2 * COLS), F32), ((2 * GROUP, LANES), F32)],
-        (place, w_own, down_half, *ring),
-        2 * GROUP * HALF * 2 * COLS, 16,
+        [((2 * GROUP, LANES), F32), ((2 * GROUP, HALF + LANES), BF16), ((2 * GROUP, 2 * COLS), F32)],
+        (place, down_half, w_own, *ring),
+        2 * GROUP * HALF * 2 * COLS, 20,
+        scratch=[
+            pltpu.VMEM((2 * GROUP, HALF + LANES), BF16),
+            pltpu.VMEM((HALF // 2, 2 * COLS), BF16),
+            pltpu.VMEM((2 * GROUP, 2 * COLS), F32),
+            pltpu.SemaphoreType.DMA((12,)),
+        ],
+        in_any=10, out_hbm=2,
     )
     low_acc = low_acc.reshape(2, GROUP, LANES)
     low_near = jnp.where(core == 0, low_acc[0], low_acc[1])
@@ -271,9 +285,11 @@
     signs = chosen.astype(BF16) - rejected.astype(BF16)
     valid = (jnp.any(chosen, axis=2) & jnp.any(rejected, axis=2)).astype(F32).reshape(2, 1, LANES)
 
-    w_other, low, b_gate, b_up, read, signs, valid, count_lanes = lax.optimization_barrier(
-        (w_other, low, b_gate, b_up, read, signs, valid, count_lanes)
-    )
+    w_other, low, b_gate, b_up, read, signs, valid = lax.optimization_barrier(
+        (w_other, low, b_gate, b_up, read, signs, valid)
+    )
+    count = jnp.sum(w_other[:, 2 * SLICE, 0].astype(F32))
+    count_lanes = jnp.where(jnp.arange(LANES) == 64, count, 0.0).reshape(1, LANES)
     far = products(True, place, tok, w_other, acc)
     partner = lax.ppermute(far, "c", SWAP)
     near = products(False, place, tok, w_other, acc)
@@ -296,7 +312,7 @@
             pltpu.VMEM((2 * GROUP, HALF + LANES), BF16),
             pltpu.SemaphoreType.DMA((2,)),
         ],
-        in_hbm=2,
+        in_any=2,
     )
 
     arrived = lax.all_to_all(outgoing, DP, split_axis=0, concat_axis=0)

time: 229 us -> 229 us (level)
  starting transfers between devices: 82.5 us -> 69.6 us
  Pallas kernels: 15 us -> 19.6 us
  waiting for transfers between devices: 55.9 us -> 60.2 us
    ppermute x4 -> x1, starting transfers between devices: 17.4 us -> 7.04 us  [on_device(): lax.ppermute(jnp.concatenate([pair_w, count_rows], axis=0), 's', SWAP)]
    ppermute x1, waiting for transfers between devices: 9.92 us -> 0.01 us  [on_device(): other = lax.ppermute(jnp.where(t == 0, high_half, low_half), 't', SWAP)]
    ppermute x2, waiting for transfers between devices: 12.7 us -> 21.4 us  [swapped(): far = lax.ppermute(value, axis, SWAP)]
    ppermute x1, starting transfers between devices: 3.53 us -> 8.79 us  [on_device(): take = lax.ppermute(give, 'c', SWAP)]
    pallas_call x3, Pallas kernels: 9.61 us -> 14.2 us  [kernel(): pl.pallas_call(function, out_shape=tuple((jax.ShapeDtypeStruct(*s) for s...]
    ppermute x8, waiting for transfers between devices: 2.78 us -> 6.61 us  [along(): return lax.ppermute(value, axis, [(i, (i + k) % n) for i in range(n)])]
    ppermute x8, starting transfers between devices: 32.2 us -> 28.7 us  [along(): return lax.ppermute(value, axis, [(i, (i + k) % n) for i in range(n)])]
    ppermute x4 -> x1, waiting for transfers between devices: 13.7 us -> 17 us  [on_device(): lax.ppermute(jnp.concatenate([pair_w, count_rows], axis=0), 's', SWAP)]
  transfers between devices with their start and end apart: 22 -> 19, of which waited for: 9 -> 8; matrix products, arithmetic and copies ran while one was open for 7% -> 6% of each run, Pallas kernels for 3% -> 5%
where the time goes in v6:
time: 229 us; the launch traced here: 227 us
  starting transfers between devices  69.6 us (30%)
  waiting for transfers between devices  60.2 us (26%)
  local copies, waits for them, and re-layouts  27.6 us (12%)
  between operations  19.7 us (9%)
  Pallas kernels  19.6 us (9%)
  blocking collectives  18.8 us (8%)
  other arithmetic  11.8 us (5%)
    ppermute x8, starting transfers between devices, along(): return lax.ppermute(value, axis, [(i, (i + k) % n) for i in range(n)])  28.7 us
    ppermute x2, waiting for transfers between devices, swapped(): far = lax.ppermute(value, axis, SWAP)  21.4 us
    unnamed x66, local copies, waits for them, and re-layouts  20.2 us
    all_to_all x1, blocking collectives, on_device(): lax.all_to_all(message, ('c', 't', 'z', 'yl'), split_axis=0, concat_axis=0)  18.8 us
    ppermute x1, waiting for transfers between devices, on_device(): lax.ppermute(jnp.concatenate([pair_w, count_rows], axis=0), 's', SWAP)  17 us
    pallas_call x3, Pallas kernels, kernel(): pl.pallas_call(function, out_shape=tuple((jax.ShapeDtypeStruct(*s) for s...  14.2 us
    all_to_all x1, waiting for transfers between devices, on_device(): arrived = lax.all_to_all(outgoing, DP, split_axis=0, concat_axis=0)  10.2 us
    ppermute x1, starting transfers between devices, on_device(): take = lax.ppermute(give, 'c', SWAP)  8.79 us
  transfers between devices with their start and end apart: 19, of which 8 were waited for; matrix products, arithmetic and copies ran while one was open for 6% of the time, Pallas kernels for 5%

profile of v6, /device:TPU:1, one launch (start us, length us, event | category | flops | bytes accessed | tf_op | source)
XLA Modules:
  0.0 227.2 jit_solution(7149795425671380307)
XLA Ops:
  10.2 8.8 %collective-permute-start = (bf16[12,2176]{1,0:T(8,128)(2,1)S(1)}, bf16[12,2176]{1,0:T(8,128)(2,1)S(1)}, u32[]{:S(2)}, u32[]{:S(2)}) collective-permute-start(bf16[12,2176]{1,0:T(8,128)(2,1)S(1)} %get-tuple-element.67), channel_id=1, source_target_pairs={{0,16},{16,0},{1,17},{17,1},{2,18},{18,2},{3,19},{19,3},{4,20},{20... | collective-permute-start | bytes 156680 | tf_op jit(solution)/shard_map/ppermute | solution.py:219
  19.2 1.9 collective-permute-start.2
  21.2 1.9 collective-permute-start.1
  23.2 10.0 %collective-permute-done.1 = bf16[24,2176]{1,0:T(8,128)(2,1)S(1)} collective-permute-done((bf16[24,2176]{1,0:T(8,128)(2,1)S(1)}, bf16[24,2176]{1,0:T(8,128)(2,1)S(1)}, u32[]{:S(2)}, u32[]{:S(2)}) %collective-permute-start.1) | collective-permute-done | bytes 104480 | tf_op jit(solution)/shard_map/ppermute | solution.py:36
  34.3 2.1 collective-permute-start.3
  36.4 11.4 %collective-permute-done.3 = bf16[2,24,2176]{2,1,0:T(8,128)(2,1)S(1)} collective-permute-done((bf16[2,24,2176]{2,1,0:T(8,128)(2,1)S(1)}, bf16[2,24,2176]{2,1,0:T(8,128)(2,1)S(1)}, u32[]{:S(2)}, u32[]{:S(2)}) %collective-permute-start.3) | collective-permute-done | bytes 208928 | tf_op jit(solution)/shard_map/ppermute | solution.py:36
  47.9 1.9 collective-permute-start.4
  49.8 7.4 %collective-permute-start.5 = (bf16[96,2176]{1,0:T(8,128)(2,1)S(1)}, bf16[96,2176]{1,0:T(8,128)(2,1)S(1)}, u32[]{:S(2)}, u32[]{:S(2)}) collective-permute-start(bf16[96,2176]{1,0:T(8,128)(2,1)S(1)} %bitcast.52), channel_id=1, source_target_pairs={{0,14},{2,0},{4,2},{6,4},{8,6},{10,8},{12,10},{14,12},{1,15},{3,1}... | collective-permute-start | bytes 1253384 | tf_op jit(solution)/shard_map/ppermute | solution.py:205
  59.7 7.0 %collective-permute-start.8 = (bf16[272,1024]{1,0:T(8,128)(2,1)S(1)}, bf16[272,1024]{1,0:T(8,128)(2,1)S(1)}, u32[]{:S(2)}, u32[]{:S(2)}) collective-permute-start(bf16[272,1024]{1,0:T(8,128)(2,1)S(1)} %concatenate.64), channel_id=1, source_target_pairs={{0,256},{256,0},{1,257},{257,1},{2,258},{258,2},{3,259},{259,3},{4... | collective-permute-start | bytes 1671176 | tf_op jit(solution)/shard_map/ppermute | solution.py:240
  66.8 1.9 collective-permute-start.6
  68.7 4.6 %collective-permute-start.7 = (bf16[96,2176]{1,0:T(8,128)(2,1)S(1)}, bf16[96,2176]{1,0:T(8,128)(2,1)S(1)}, u32[]{:S(2)}, u32[]{:S(2)}) collective-permute-start(bf16[96,2176]{1,0:T(8,128)(2,1)S(1)} %collective-permute-done.5.l1), channel_id=1, source_target_pairs={{0,14},{2,0},{4,2},{6,4},{8,6},{10,8},{12,10},{14,12},{1,15},{3,1}... | collective-permute-start | bytes 1253384 | tf_op jit(solution)/shard_map/ppermute | solution.py:205
  73.3 17.0 %collective-permute-done.8 = bf16[272,1024]{1,0:T(8,128)(2,1)S(1)} collective-permute-done((bf16[272,1024]{1,0:T(8,128)(2,1)S(1)}, bf16[272,1024]{1,0:T(8,128)(2,1)S(1)}, u32[]{:S(2)}, u32[]{:S(2)}) %collective-permute-start.8) | collective-permute-done | bytes 557088 | tf_op jit(solution)/shard_map/ppermute | solution.py:240
  95.4 1.9 collective-permute-start.9
  97.3 4.6 %collective-permute-start.10 = (bf16[96,2176]{1,0:T(8,128)(2,1)S(1)}, bf16[96,2176]{1,0:T(8,128)(2,1)S(1)}, u32[]{:S(2)}, u32[]{:S(2)}) collective-permute-start(bf16[96,2176]{1,0:T(8,128)(2,1)S(1)} %collective-permute-done.7.l2), channel_id=1, source_target_pairs={{0,14},{2,0},{4,2},{6,4},{8,6},{10,8},{12,10},{14,12},{1,15},{3,1}... | collective-permute-start | bytes 1253384 | tf_op jit(solution)/shard_map/ppermute | solution.py:205
  102.5 4.6 %collective-permute-done.9.r3 = bf16[96,2176]{1,0:T(8,128)(2,1)S(1)} collective-permute-done((bf16[96,2176]{1,0:T(8,128)(2,1)S(1)}, bf16[96,2176]{1,0:T(8,128)(2,1)S(1)}, u32[]{:S(2)}, u32[]{:S(2)}) %collective-permute-start.9) | collective-permute-done | bytes 417824 | tf_op jit(solution)/shard_map/ppermute | solution.py:205
  107.9 1.9 collective-permute-start.11
  110.6 4.6 %collective-permute-start.12 = (bf16[48,2176]{1,0:T(8,128)(2,1)S(1)}, bf16[48,2176]{1,0:T(8,128)(2,1)S(1)}, u32[]{:S(2)}, u32[]{:S(2)}) collective-permute-start(bf16[48,2176]{1,0:T(8,128)(2,1)S(1)} %slice.121), channel_id=1, source_target_pairs={{0,14},{2,0},{4,2},{6,4},{8,6},{10,8},{12,10},{14,12},{1,15},{3,1}... | collective-permute-start | bytes 626696 | tf_op jit(solution)/shard_map/ppermute | solution.py:205
  116.1 1.9 collective-permute-done.12.l4
  129.3 8.0 %shard_map.94 = (f32[768,128]{1,0:T(8,128)S(1)}, bf16[768,2176]{1,0:T(8,128)(2,1)S(1)}, f32[768,1024]{1,0:T(8,128)S(1)}) custom-call(s32[3]{0:T(128)S(1)} %pad_add_fusion.place, bf16[2048,128]{1,0:T(8,128)(2,1)S(1)} %copy-done.4, bf16[1024,1024]{1,0:T(8,128)(2,1)S(1)} %copy-done.3, bf16[96,2176]{1,0:T(8,128)(2,1)S(1)} %bitcast.53, ...), custom_call_target="tpu_custom_call" | custom-call | flops 1610612736 | bytes 10000000 | tf_op jit(solution)/shard_map/pallas_call | solution.py:192
  141.0 6.4 %collective-permute-start.13 = (f32[384,128]{1,0:T(8,128)S(1)}, f32[384,128]{1,0:T(8,128)S(1)}, u32[]{:S(2)}, u32[]{:S(2)}) collective-permute-start(f32[384,128]{1,0:T(8,128)S(1)} %slice_select_fusion.1), channel_id=1, source_target_pairs={{0,16},{16,0},{1,17},{17,1},{2,18},{18,2},{3,19},{19,3},{4,20},{20... | collective-permute-start | bytes 589832 | tf_op jit(solution)/shard_map/ppermute | solution.py:271
  149.5 1.7 add_convert_fusion.low_ref
  151.2 1.9 copy-done.1
  154.7 2.7 %shard_map.96 = f32[384,1024]{1,0:T(8,128)S(1)} custom-call(s32[3]{0:T(128)S(1)} %pad_add_fusion.place, bf16[768,2176]{1,0:T(8,128)(2,1)S(1)} %get-tuple-element.31.rows.tok_in, bf16[4,272,1024]{2,1,0:T(8,128)(2,1)S(1)} %bitcast.48, f32[768,1024]{1,0:T(8,128)S(1)} %copy-done.1), custom_call_target="tpu_custom_call" | custom-call | flops 805306368 | bytes 6000000 | tf_op jit(solution)/shard_map/pallas_call | solution.py:85
  157.5 2.1 collective-permute-start.14
  159.5 2.7 %shard_map.95.near = f32[384,1024]{1,0:T(8,128)S(1)} custom-call(s32[3]{0:T(128)S(1)} %pad_add_fusion.place, bf16[768,2176]{1,0:T(8,128)(2,1)S(1)} %get-tuple-element.31.rows.tok_in, bf16[4,272,1024]{2,1,0:T(8,128)(2,1)S(1)} %bitcast.49, f32[768,1024]{1,0:T(8,128)S(1)} %copy-done.1), custom_call_target="tpu_custom_call" | custom-call | flops 805306368 | bytes 6000000 | tf_op jit(solution)/shard_map/pallas_call | solution.py:85
  163.5 3.7 %shard_map.97 = (f32[64,4,128]{2,1,0:T(4,128)S(1)}, f32[32,384]{1,0:T(8,128)S(1)}, bf16[4,384,512]{2,1,0:T(8,128)(2,1)S(1)}) custom-call(s32[3]{0:T(128)S(1)} %pad_add_fusion.place, f32[384,1024]{1,0:T(8,128)S(1)} %shard_map.95.near, f32[384,1024]{1,0:T(8,128)S(1)} %collective-permute-done.14.partner, bf16[384,128]{1,0:T(8,128)(2,1)S(1)} %copy-done.22, ...), custom_call_target="tpu_custom_call" | custom-call | flops 201326592 | bytes 10000000 | tf_op jit(solution)/shard_map/pallas_call | solution.py:192
  167.3 18.8 %all_to_all.15.arrived = f32[64,4,128]{2,1,0:T(4,128)S(1)} all-to-all(f32[64,4,128]{2,1,0:T(4,128)S(1)} %get-tuple-element.41), channel_id=1, replica_groups=mesh['s'=2,'t'=2,'x'=4,'c'=2,'z'=8,'yl'=2] {'c','t','z','yl'}, dimensions={0} | all-to-all | bytes 262144 | tf_op jit(solution)/shard_map/all_to_all | solution.py:304
  186.1 2.5 %shard_map.98 = (f32[32,6,128]{2,1,0:T(8,128)S(1)}, f32[8,128]{1,0:T(8,128)S(1)}) custom-call(s32[3]{0:T(128)S(1)} %pad_add_fusion.place, f32[64,4,128]{2,1,0:T(4,128)S(1)} %all_to_all.15.arrived, bf16[2,128,384]{2,1,0:T(8,128)(2,1)S(1)} %fusion.5.signs, f32[2,1,128]{2,1,0:T(1,128)S(1)} %bitcast.54, f32[32,384]{1,0:T(8,128)S(1)} %get-tuple-element.43.low_t, ...), custom_call_target="tpu_custom_call" | custom-call | flops 25165824 | bytes 10000000 | tf_op jit(solution)/shard_map/pallas_call | solution.py:192
  189.2 7.1 %all-to-all-start.1 = ((f32[32,6,128]{2,1,0:T(8,128)}), f32[32,6,128]{2,1,0:T(8,128)S(1)}, u32[]{:S(2)}, u32[]{:S(2)}) async-start(f32[32,6,128]{2,1,0:T(8,128)} %copy-done.25), calls=%async_computation.1 | async-start | bytes 262144 | tf_op jit(solution)/shard_map/all_to_all | solution.py:318
  196.9 10.2 %all-to-all-done.1 = f32[32,6,128]{2,1,0:T(8,128)S(1)} async-done(((f32[32,6,128]{2,1,0:T(8,128)}), f32[32,6,128]{2,1,0:T(8,128)S(1)}, u32[]{:S(2)}, u32[]{:S(2)}) %all-to-all-start.1) | async-done | bytes 98336 | tf_op jit(solution)/shard_map/all_to_all | solution.py:318
  207.8 3.5 %all-to-all-start.2 = ((f32[16,2,128]{2,1,0:T(2,128)}), f32[16,2,128]{2,1,0:T(2,128)S(1)}, u32[]{:S(2)}, u32[]{:S(2)}) async-start(f32[16,2,128]{2,1,0:T(2,128)} %broadcast_in_dim.32), calls=%async_computation.2 | async-start | bytes 32768 | tf_op jit(solution)/shard_map/all_to_all | solution.py:323
  213.7 4.9 %all-to-all-done.2 = f32[16,2,128]{2,1,0:T(2,128)S(1)} async-done(((f32[16,2,128]{2,1,0:T(2,128)}), f32[16,2,128]{2,1,0:T(2,128)S(1)}, u32[]{:S(2)}, u32[]{:S(2)}) %all-to-all-start.2) | async-done | bytes 16416 | tf_op jit(solution)/shard_map/all_to_all | solution.py:323
  (137 shorter events, 36.0 us)
Async XLA Ops:
  7.2 11.8 %copy-start.28 = (bf16[2,128,896]{2,1,0:T(8,128)(2,1)S(1)}, bf16[2,128,896]{2,1,0:T(8,128)(2,1)}, u32[]{:S(2)}) copy-start(bf16[2,128,896]{2,1,0:T(8,128)(2,1)} %param.10) | copy-start | bytes 1376260
  7.2 111.5 %all-gather.3.cloned.1.call-start = ((), (), s32[]{:S(2)}) async-start(), calls=%async_computation.3 | async-start | bytes 2621440 | tf_op jit(solution)/shard_map/all_gather | solution.py:233
  10.2 10.9 %collective-permute-start = (bf16[12,2176]{1,0:T(8,128)(2,1)S(1)}, bf16[12,2176]{1,0:T(8,128)(2,1)S(1)}, u32[]{:S(2)}, u32[]{:S(2)}) collective-permute-start(bf16[12,2176]{1,0:T(8,128)(2,1)S(1)} %get-tuple-element.67), channel_id=1, source_target_pairs={{0,16},{16,0},{1,17},{17,1},{2,18},{18,2},{3,19},{19,3},{4,20},{20... | collective-permute-start | bytes 156680 | tf_op jit(solution)/shard_map/ppermute | solution.py:219
  19.2 14.1 %collective-permute-start.2 = (bf16[128,1024]{1,0:T(8,128)(2,1)S(1)}, bf16[128,1024]{1,0:T(8,128)(2,1)S(1)}, u32[]{:S(2)}, u32[]{:S(2)}) collective-permute-start(bf16[128,1024]{1,0:T(8,128)(2,1)S(1)} %get-tuple-element.55), channel_id=1, source_target_pairs={{0,128},{128,0},{1,129},{129,1},{2,130},{130,2},{3,131},{131,3},{4... | collective-permute-start | bytes 786440 | tf_op jit(solution)/shard_map/ppermute | solution.py:228
  21.2 12.0 %collective-permute-start.1 = (bf16[24,2176]{1,0:T(8,128)(2,1)S(1)}, bf16[24,2176]{1,0:T(8,128)(2,1)S(1)}, u32[]{:S(2)}, u32[]{:S(2)}) collective-permute-start(bf16[24,2176]{1,0:T(8,128)(2,1)S(1)} %maximum_select_fusion.4), channel_id=1, source_target_pairs={{0,1},{1,0},{2,3},{3,2},{4,5},{5,4},{6,7},{7,6},{8,9},{9,8},{10,11... | collective-permute-start | bytes 313352 | tf_op jit(solution)/shard_map/ppermute | solution.py:36
  34.3 25.4 %copy-start.27 = (bf16[256,1024]{1,0:T(8,128)(2,1)S(1)}, bf16[256,1024]{1,0:T(8,128)(2,1)}, u32[]{:S(2)}) copy-start(bf16[256,1024]{1,0:T(8,128)(2,1)} %maximum_select_fusion) | copy-start | bytes 1572868
  34.3 116.9 %all-gather.5.cloned.1.call-start = ((), (), s32[]{:S(2)}) async-start(), calls=%async_computation.4 | async-start | bytes 2785280 | tf_op jit(solution)/shard_map/all_gather | solution.py:249
  34.3 13.5 %collective-permute-start.3 = (bf16[2,24,2176]{2,1,0:T(8,128)(2,1)S(1)}, bf16[2,24,2176]{2,1,0:T(8,128)(2,1)S(1)}, u32[]{:S(2)}, u32[]{:S(2)}) collective-permute-start(bf16[2,24,2176]{2,1,0:T(8,128)(2,1)S(1)} %maximum_select_fusion.2), channel_id=1, source_target_pairs={{0,128},{128,0},{1,129},{129,1},{2,130},{130,2},{3,131},{131,3},{4... | collective-permute-start | bytes 626696 | tf_op jit(solution)/shard_map/ppermute | solution.py:36
  47.9 43.5 %copy-start.5 = (bf16[2,2,24,2176]{3,2,1,0:T(8,128)(2,1)}, bf16[2,2,24,2176]{3,2,1,0:T(8,128)(2,1)S(1)}, u32[]{:S(2)}) copy-start(bf16[2,2,24,2176]{3,2,1,0:T(8,128)(2,1)S(1)} %maximum_select_fusion.1) | copy-start | bytes 1253380
  47.9 18.9 %collective-permute-start.4 = (bf16[96,2176]{1,0:T(8,128)(2,1)S(1)}, bf16[96,2176]{1,0:T(8,128)(2,1)S(1)}, u32[]{:S(2)}, u32[]{:S(2)}) collective-permute-start(bf16[96,2176]{1,0:T(8,128)(2,1)S(1)} %bitcast.51), channel_id=1, source_target_pairs={{0,2},{2,4},{4,6},{6,8},{8,10},{10,12},{12,14},{14,0},{1,3},{3,5},... | collective-permute-start | bytes 1253384 | tf_op jit(solution)/shard_map/ppermute | solution.py:205
  49.8 18.9 %collective-permute-start.5 = (bf16[96,2176]{1,0:T(8,128)(2,1)S(1)}, bf16[96,2176]{1,0:T(8,128)(2,1)S(1)}, u32[]{:S(2)}, u32[]{:S(2)}) collective-permute-start(bf16[96,2176]{1,0:T(8,128)(2,1)S(1)} %bitcast.52), channel_id=1, source_target_pairs={{0,14},{2,0},{4,2},{6,4},{8,6},{10,8},{12,10},{14,12},{1,15},{3,1}... | collective-permute-start | bytes 1253384 | tf_op jit(solution)/shard_map/ppermute | solution.py:205
  59.7 31.7 %copy-start.29 = (bf16[4096,32]{0,1:T(8,128)(2,1)S(1)}, bf16[4096,32]{0,1:T(8,128)(2,1)}, u32[]{:S(2)}) copy-start(bf16[4096,32]{0,1:T(8,128)(2,1)} %param.11) | copy-start | bytes 786436
  59.7 30.6 %collective-permute-start.8 = (bf16[272,1024]{1,0:T(8,128)(2,1)S(1)}, bf16[272,1024]{1,0:T(8,128)(2,1)S(1)}, u32[]{:S(2)}, u32[]{:S(2)}) collective-permute-start(bf16[272,1024]{1,0:T(8,128)(2,1)S(1)} %concatenate.64), channel_id=1, source_target_pairs={{0,256},{256,0},{1,257},{257,1},{2,258},{258,2},{3,259},{259,3},{4... | collective-permute-start | bytes 1671176 | tf_op jit(solution)/shard_map/ppermute | solution.py:240
  66.8 24.8 %copy-start.14 = (bf16[96,2176]{1,0:T(8,128)(2,1)}, bf16[96,2176]{1,0:T(8,128)(2,1)S(1)}, u32[]{:S(2)}) copy-start(bf16[96,2176]{1,0:T(8,128)(2,1)S(1)} %collective-permute-done.4.r1) | copy-start | bytes 1253380
  66.8 23.5 %collective-permute-start.6 = (bf16[96,2176]{1,0:T(8,128)(2,1)S(1)}, bf16[96,2176]{1,0:T(8,128)(2,1)S(1)}, u32[]{:S(2)}, u32[]{:S(2)}) collective-permute-start(bf16[96,2176]{1,0:T(8,128)(2,1)S(1)} %collective-permute-done.4.r1), channel_id=1, source_target_pairs={{0,2},{2,4},{4,6},{6,8},{8,10},{10,12},{12,14},{14,0},{1,3},{3,5},... | collective-permute-start | bytes 1253384 | tf_op jit(solution)/shard_map/ppermute | solution.py:205
  68.7 22.9 %copy-start.16 = (bf16[96,2176]{1,0:T(8,128)(2,1)}, bf16[96,2176]{1,0:T(8,128)(2,1)S(1)}, u32[]{:S(2)}) copy-start(bf16[96,2176]{1,0:T(8,128)(2,1)S(1)} %collective-permute-done.5.l1) | copy-start | bytes 1253380
  68.7 21.6 %collective-permute-start.7 = (bf16[96,2176]{1,0:T(8,128)(2,1)S(1)}, bf16[96,2176]{1,0:T(8,128)(2,1)S(1)}, u32[]{:S(2)}, u32[]{:S(2)}) collective-permute-start(bf16[96,2176]{1,0:T(8,128)(2,1)S(1)} %collective-permute-done.5.l1), channel_id=1, source_target_pairs={{0,14},{2,0},{4,2},{6,4},{8,6},{10,8},{12,10},{14,12},{1,15},{3,1}... | collective-permute-start | bytes 1253384 | tf_op jit(solution)/shard_map/ppermute | solution.py:205
  90.3 5.1 %copy-start.18 = (bf16[96,2176]{1,0:T(8,128)(2,1)}, bf16[96,2176]{1,0:T(8,128)(2,1)S(1)}, u32[]{:S(2)}) copy-start(bf16[96,2176]{1,0:T(8,128)(2,1)S(1)} %collective-permute-done.6.r2) | copy-start | bytes 1253380
  90.3 7.0 %copy-start.20 = (bf16[96,2176]{1,0:T(8,128)(2,1)}, bf16[96,2176]{1,0:T(8,128)(2,1)S(1)}, u32[]{:S(2)}) copy-start(bf16[96,2176]{1,0:T(8,128)(2,1)S(1)} %collective-permute-done.7.l2) | copy-start | bytes 1253380
  92.4 2.5 %copy-start.31 = (bf16[896]{0:T(1024)(128)(2,1)S(1)}, bf16[896]{0:T(1024)(128)(2,1)}, u32[]{:S(2)}) copy-start(bf16[896]{0:T(1024)(128)(2,1)} %param.13) | copy-start | bytes 5380
  95.4 11.7 %collective-permute-start.9 = (bf16[96,2176]{1,0:T(8,128)(2,1)S(1)}, bf16[96,2176]{1,0:T(8,128)(2,1)S(1)}, u32[]{:S(2)}, u32[]{:S(2)}) collective-permute-start(bf16[96,2176]{1,0:T(8,128)(2,1)S(1)} %collective-permute-done.6.r2), channel_id=1, source_target_pairs={{0,2},{2,4},{4,6},{6,8},{8,10},{10,12},{12,14},{14,0},{1,3},{3,5},... | collective-permute-start | bytes 1253384 | tf_op jit(solution)/shard_map/ppermute | solution.py:205
  97.3 12.5 %collective-permute-start.10 = (bf16[96,2176]{1,0:T(8,128)(2,1)S(1)}, bf16[96,2176]{1,0:T(8,128)(2,1)S(1)}, u32[]{:S(2)}, u32[]{:S(2)}) collective-permute-start(bf16[96,2176]{1,0:T(8,128)(2,1)S(1)} %collective-permute-done.7.l2), channel_id=1, source_target_pairs={{0,14},{2,0},{4,2},{6,4},{8,6},{10,8},{12,10},{14,12},{1,15},{3,1}... | collective-permute-start | bytes 1253384 | tf_op jit(solution)/shard_map/ppermute | solution.py:205
  107.9 8.1 %collective-permute-start.11 = (bf16[48,2176]{1,0:T(8,128)(2,1)S(1)}, bf16[48,2176]{1,0:T(8,128)(2,1)S(1)}, u32[]{:S(2)}, u32[]{:S(2)}) collective-permute-start(bf16[48,2176]{1,0:T(8,128)(2,1)S(1)} %slice.120), channel_id=1, source_target_pairs={{0,2},{2,4},{4,6},{6,8},{8,10},{10,12},{12,14},{14,0},{1,3},{3,5},... | collective-permute-start | bytes 626696 | tf_op jit(solution)/shard_map/ppermute | solution.py:205
  110.6 7.3 %collective-permute-start.12 = (bf16[48,2176]{1,0:T(8,128)(2,1)S(1)}, bf16[48,2176]{1,0:T(8,128)(2,1)S(1)}, u32[]{:S(2)}, u32[]{:S(2)}) collective-permute-start(bf16[48,2176]{1,0:T(8,128)(2,1)S(1)} %slice.121), channel_id=1, source_target_pairs={{0,14},{2,0},{4,2},{6,4},{8,6},{10,8},{12,10},{14,12},{1,15},{3,1}... | collective-permute-start | bytes 626696 | tf_op jit(solution)/shard_map/ppermute | solution.py:205
  141.0 8.5 %collective-permute-start.13 = (f32[384,128]{1,0:T(8,128)S(1)}, f32[384,128]{1,0:T(8,128)S(1)}, u32[]{:S(2)}, u32[]{:S(2)}) collective-permute-start(f32[384,128]{1,0:T(8,128)S(1)} %slice_select_fusion.1), channel_id=1, source_target_pairs={{0,16},{16,0},{1,17},{17,1},{2,18},{18,2},{3,19},{19,3},{4,20},{20... | collective-permute-start | bytes 589832 | tf_op jit(solution)/shard_map/ppermute | solution.py:271
  157.4 6.1 %copy-start.12 = (bf16[128,512]{1,0:T(8,128)(2,1)S(1)}, bf16[128,512]{1,0:T(8,128)(2,1)}, u32[]{:S(2)}) copy-start(bf16[128,512]{1,0:T(8,128)(2,1)} %pad.27.b_gate) | copy-start | bytes 393220
  157.4 6.1 %copy-start.13 = (bf16[128,512]{1,0:T(8,128)(2,1)S(1)}, bf16[128,512]{1,0:T(8,128)(2,1)}, u32[]{:S(2)}) copy-start(bf16[128,512]{1,0:T(8,128)(2,1)} %pad.28.b_up) | copy-start | bytes 393220
  157.4 6.1 %copy-start.22 = (bf16[384,128]{1,0:T(8,128)(2,1)S(1)}, bf16[384,128]{1,0:T(8,128)(2,1)}, u32[]{:S(2)}) copy-start(bf16[384,128]{1,0:T(8,128)(2,1)} %add_convert_fusion.low_ref) | copy-start | bytes 294916
  157.4 6.1 %copy-start.26 = (bf16[1,512]{1,0:T(2,128)(2,1)S(1)}, bf16[1,512]{1,0:T(2,128)(2,1)}, u32[]{:S(2)}) copy-start(bf16[1,512]{1,0:T(2,128)(2,1)} %reshape.255.readout) | copy-start | bytes 3076
  157.5 6.0 %collective-permute-start.14 = (f32[384,1024]{1,0:T(8,128)S(1)}, f32[384,1024]{1,0:T(8,128)S(1)}, u32[]{:S(2)}, u32[]{:S(2)}) collective-permute-start(f32[384,1024]{1,0:T(8,128)S(1)} %shard_map.96), channel_id=1, source_target_pairs={{0,16},{16,0},{1,17},{17,1},{2,18},{18,2},{3,19},{19,3},{4,20},{20... | collective-permute-start | bytes 4718600 | tf_op jit(solution)/shard_map/ppermute | solution.py:294
  189.2 17.9 %all-to-all-start.1 = ((f32[32,6,128]{2,1,0:T(8,128)}), f32[32,6,128]{2,1,0:T(8,128)S(1)}, u32[]{:S(2)}, u32[]{:S(2)}) async-start(f32[32,6,128]{2,1,0:T(8,128)} %copy-done.25), calls=%async_computation.1 | async-start | bytes 262144 | tf_op jit(solution)/shard_map/all_to_all | solution.py:318
  207.8 10.8 %all-to-all-start.2 = ((f32[16,2,128]{2,1,0:T(2,128)}), f32[16,2,128]{2,1,0:T(2,128)S(1)}, u32[]{:S(2)}, u32[]{:S(2)}) async-start(f32[16,2,128]{2,1,0:T(2,128)} %broadcast_in_dim.32), calls=%async_computation.2 | async-start | bytes 32768 | tf_op jit(solution)/shard_map/all_to_all | solution.py:323
  (19 other events, 20.7 us)
Sparse Core Ops, SparseCore 0:
  34.4 37.7 all-gather.2
  91.5 34.4 all-gather.4

commit v7 on v6

--- a/solution.py
+++ b/solution.py
@@ -52,7 +52,7 @@
 def early_products(place, down, w_in, p0, r1, l1, r2, l2, r3, l3, r4, l4, low, tok_out, acc_out, tok, w, acc, sems):
     z = place[1]
     block = 8 * ROWS
-    w_copy = pltpu.make_async_copy(w_in, w, sems.at[9])
+    w_copy = pltpu.make_async_copy(w_in.at[:, pl.ds(0, 2 * SLICE), :], w, sems.at[9])
     w_copy.start()
     moves = [(0, 0, p0), (-1, 0, r1), (1, 0, l1), (-2, 0, r2), (2, 0, l2), (-3, 0, r3), (3, 0, l3), (4, 0, r4), (4, 4 * ROWS, l4)]
     copies = []
@@ -66,38 +66,53 @@
     tok_copy.start()
     low[...] = dot(tok[:, 0:HALF], down[...])
     w_copy.wait()
+    copies = [tok_copy]
     for n in range(4):
-        part = slice(n * COLS // 2, (n + 1) * COLS // 2)
-        acc[:, part] = dot(tok[:, 0 : HALF // 2], w[:, part])
-    acc_copy = pltpu.make_async_copy(acc, acc_out, sems.at[11])
-    acc_copy.start()
-    acc_copy.wait()
-    tok_copy.wait()
-
-
-def late_products(place, rows, w, acc, out):
-    out[...] = acc[...] + dot(rows[...], w[...].reshape(HALF // 2, COLS // 2))
+        part = pl.ds(n * COLS // 2, COLS // 2)
+        acc[:, part] = dot(tok[:, 0 : HALF // 2], w[:, :, part].reshape(HALF // 2, COLS // 2))
+        copies.append(pltpu.make_async_copy(acc.at[:, part], acc_out.at[:, part], sems.at[11 + n]))
+        copies[-1].start()
+    for copy in copies:
+        copy.wait()
+
+
+def late_products(far, place, tok, w_in, acc_in, out, rows, w, acc, sems):
+    half = 1 - place[0] if far else place[0]
+    mine = pl.ds(pl.multiple_of(half * GROUP, GROUP), GROUP)
+    parts = [pl.ds(n * COLS // 2, COLS // 2) for n in range(4)]
+    rows_copy = pltpu.make_async_copy(tok.at[mine, pl.ds(HALF // 2, HALF // 2)], rows, sems.at[0])
+    rows_copy.start()
+    copies = []
+    for n, part in enumerate(parts):
+        copies.append(
+            (
+                pltpu.make_async_copy(w_in.at[:, pl.ds(0, 2 * SLICE), part], w.at[:, :, part], sems.at[1 + n]),
+                pltpu.make_async_copy(acc_in.at[mine, part], acc.at[:, part], sems.at[5 + n]),
+            )
+        )
+        copies[-1][0].start()
+        copies[-1][1].start()
+    rows_copy.wait()
+    for part, pair in zip(parts, copies):
+        pair[0].wait()
+        pair[1].wait()
+        out[:, part] = acc[:, part] + dot(rows[...], w[:, :, part].reshape(HALF // 2, COLS // 2))
 
 
 def products(far, place, tok, w, acc):
-    half = (lambda place: 1 - place[0]) if far else (lambda place: place[0])
-    part = COLS // 2
-    return pl.pallas_call(
-        late_products,
-        grid_spec=pltpu.PrefetchScalarGridSpec(
-            num_scalar_prefetch=1,
-            grid=(4,),
-            in_specs=[
-                pl.BlockSpec((GROUP, HALF // 2), lambda n, place: (half(place), 1)),
-                pl.BlockSpec((4, 2 * SLICE, part), lambda n, place: (0, 0, n)),
-                pl.BlockSpec((GROUP, part), lambda n, place: (half(place), n)),
-            ],
-            out_specs=pl.BlockSpec((GROUP, part), lambda n, place: (0, n)),
-        ),
-        out_shape=jax.ShapeDtypeStruct((GROUP, 2 * COLS), F32),
-        compiler_params=pltpu.CompilerParams(vmem_limit_bytes=12 * 1024 * 1024),
-        cost_estimate=pl.CostEstimate(flops=GROUP * HALF * 2 * COLS, bytes_accessed=6_000_000, transcendentals=0),
-    )(place, tok, w, acc)
+    return kernel(
+        functools.partial(late_products, far),
+        [((GROUP, 2 * COLS), F32)],
+        (place, tok, w, acc),
+        GROUP * HALF * 2 * COLS, 56,
+        scratch=[
+            pltpu.VMEM((GROUP, HALF // 2), BF16),
+            pltpu.VMEM((4, 2 * SLICE, 2 * COLS), BF16),
+            pltpu.VMEM((GROUP, 2 * COLS), F32),
+            pltpu.SemaphoreType.DMA((9,)),
+        ],
+        in_hbm=3,
+    )[0]
 
 
 def score(place, near, partner, low_ref, b_gate, b_up, readout, signs, count, message, low_t, k_out, k, sems):
@@ -185,14 +200,14 @@
     total_out[...] = jnp.broadcast_to(pair_total, (8, LANES))
 
 
-def kernel(function, shapes, arguments, flops, grant, scratch=(), in_any=0, out_hbm=0):
+def kernel(function, shapes, arguments, flops, grant, scratch=(), in_hbm=0, out_hbm=0):
     vmem = pl.BlockSpec(memory_space=pltpu.VMEM)
     smem = pl.BlockSpec(memory_space=pltpu.SMEM)
     hbm = pl.BlockSpec(memory_space=pltpu.HBM)
     return pl.pallas_call(
         function,
         out_shape=tuple(jax.ShapeDtypeStruct(*s) for s in shapes),
-        in_specs=[smem] + [vmem] * (len(arguments) - 1 - in_any) + [pl.BlockSpec(memory_space=pl.ANY)] * in_any,
+        in_specs=[smem] + [vmem] * (len(arguments) - 1 - in_hbm) + [hbm] * in_hbm,
         out_specs=(vmem,) * (len(shapes) - out_hbm) + (hbm,) * out_hbm,
         scratch_shapes=list(scratch),
         compiler_params=pltpu.CompilerParams(vmem_limit_bytes=grant * 1024 * 1024),
@@ -227,17 +242,20 @@
     mine = jnp.where(t == 0, low_half, high_half)
     other = lax.ppermute(jnp.where(t == 0, high_half, low_half), "t", SWAP)
     four, other = lax.optimization_barrier((four, other))
-    pair_w = jnp.where(
-        t == 0, jnp.concatenate([mine, other], axis=0), jnp.concatenate([other, mine], axis=0)
-    )
-    w_own = lax.all_gather(pair_w, "x", axis=0, tiled=True)
-
-    eight = swapped(four, "t", t).reshape(8 * ROWS, HALF + LANES)
-
     has = [jnp.max((code == q).astype(F32)) for q in range(SEQS)]
     count_rows = jnp.broadcast_to((has[0] * has[1] + has[2] * has[3]).astype(BF16), (16, 2 * COLS))
-    eight, pair_w = lax.optimization_barrier((eight, pair_w))
-    other_s = lax.ppermute(jnp.concatenate([pair_w, count_rows], axis=0), "s", SWAP)
+
+    def both_t(mine, other):
+        return jnp.concatenate(
+            [jnp.where(t == 0, mine, other), jnp.where(t == 0, other, mine), count_rows], axis=0
+        )
+
+    pair_w = both_t(mine, other)
+    w_own = lax.all_gather(pair_w, "x", axis=0, tiled=True).reshape(4, 2 * SLICE + 16, 2 * COLS)
+
+    eight = swapped(four, "t", t).reshape(8 * ROWS, HALF + LANES)
+
+    other_s = lax.ppermute(both_t(*lax.optimization_barrier((mine, other))), "s", SWAP)
     right, left, ring = eight, eight, [eight]
     for step in range(3):
         right, left = along(right, "z", 1), along(left, "z", -1)
@@ -245,7 +263,6 @@
         if step == 1:
             right, left, other_s = lax.optimization_barrier((right, left, other_s))
     ring += [along(right[: 4 * ROWS], "z", 1), along(left[4 * ROWS :], "z", -1)]
-    other_s = jnp.concatenate([other_s[: 2 * SLICE], other_s[2 * SLICE :] + count_rows], axis=0)
     w_other = lax.all_gather(other_s, "x", axis=0, tiled=True).reshape(4, 2 * SLICE + 16, 2 * COLS)
 
     down_half = down.reshape(2, 2, 4, 2, SLICE, 2 * RANK).transpose(3, 0, 2, 1, 4, 5)
@@ -256,14 +273,14 @@
         early_products,
         [((2 * GROUP, LANES), F32), ((2 * GROUP, HALF + LANES), BF16), ((2 * GROUP, 2 * COLS), F32)],
         (place, down_half, w_own, *ring),
-        2 * GROUP * HALF * 2 * COLS, 20,
+        2 * GROUP * HALF * 2 * COLS, 56,
         scratch=[
             pltpu.VMEM((2 * GROUP, HALF + LANES), BF16),
-            pltpu.VMEM((HALF // 2, 2 * COLS), BF16),
+            pltpu.VMEM((4, 2 * SLICE, 2 * COLS), BF16),
             pltpu.VMEM((2 * GROUP, 2 * COLS), F32),
-            pltpu.SemaphoreType.DMA((12,)),
+            pltpu.SemaphoreType.DMA((15,)),
         ],
-        in_any=10, out_hbm=2,
+        in_hbm=10, out_hbm=2,
     )
     low_acc = low_acc.reshape(2, GROUP, LANES)
     low_near = jnp.where(core == 0, low_acc[0], low_acc[1])
@@ -288,7 +305,7 @@
     w_other, low, b_gate, b_up, read, signs, valid = lax.optimization_barrier(
         (w_other, low, b_gate, b_up, read, signs, valid)
     )
-    count = jnp.sum(w_other[:, 2 * SLICE, 0].astype(F32))
+    count = jnp.sum((w_own[:, 2 * SLICE, 0] + w_other[:, 2 * SLICE, 0]).astype(F32))
     count_lanes = jnp.where(jnp.arange(LANES) == 64, count, 0.0).reshape(1, LANES)
     far = products(True, place, tok, w_other, acc)
     partner = lax.ppermute(far, "c", SWAP)
@@ -312,7 +329,7 @@
             pltpu.VMEM((2 * GROUP, HALF + LANES), BF16),
             pltpu.SemaphoreType.DMA((2,)),
         ],
-        in_any=2,
+        in_hbm=2,
     )
 
     arrived = lax.all_to_all(outgoing, DP, split_axis=0, concat_axis=0)

time: 229 us -> 218 us (0.952)
  local copies, waits for them, and re-layouts: 27.6 us -> 10.2 us
  Pallas kernels: 19.6 us -> 27.8 us
  waiting for transfers between devices: 60.2 us -> 63.4 us
    unnamed x66 -> x36, local copies, waits for them, and re-layouts: 20.2 us -> 3.87 us
    pallas_call x3 -> x5, Pallas kernels: 14.2 us -> 27.8 us  [kernel(): pl.pallas_call(function, out_shape=tuple((jax.ShapeDtypeStruct(*s) for s...]
    pallas_call x2 -> x0, Pallas kernels: 5.36 us -> none  [products(): pl.pallas_call(late_products, grid_spec=pltpu.PrefetchScalarGridSpec(num_...]
    ppermute x8, waiting for transfers between devices: 6.61 us -> 10.8 us  [along(): return lax.ppermute(value, axis, [(i, (i + k) % n) for i in range(n)])]
  transfers between devices with their start and end apart: 19 -> 19, of which waited for: 8 -> 10; matrix products, arithmetic and copies ran while one was open for 6% -> 5% of each run, Pallas kernels for 5% -> 7%
where the time goes in v7:
time: 218 us; the launch traced here: 217 us
  starting transfers between devices  69.5 us (32%)
  waiting for transfers between devices  63.4 us (29%)
  Pallas kernels  27.8 us (13%)
  between operations  19.8 us (9%)
  blocking collectives  16.6 us (8%)
  local copies, waits for them, and re-layouts  10.2 us (5%)
  other arithmetic  9.88 us (5%)
    ppermute x8, starting transfers between devices, along(): return lax.ppermute(value, axis, [(i, (i + k) % n) for i in range(n)])  30.6 us
    pallas_call x5, Pallas kernels, kernel(): pl.pallas_call(function, out_shape=tuple((jax.ShapeDtypeStruct(*s) for s...  27.8 us
    ppermute x2, waiting for transfers between devices, swapped(): far = lax.ppermute(value, axis, SWAP)  19.4 us
    ppermute x1, waiting for transfers between devices, on_device(): lax.ppermute(both_t(*lax.optimization_barrier((mine, other))), 's', SWAP)  17.4 us
    all_to_all x1, blocking collectives, on_device(): lax.all_to_all(message, ('c', 't', 'z', 'yl'), split_axis=0, concat_axis=0)  16.6 us
    ppermute x8, waiting for transfers between devices, along(): return lax.ppermute(value, axis, [(i, (i + k) % n) for i in range(n)])  10.8 us
    all_to_all x1, waiting for transfers between devices, on_device(): arrived = lax.all_to_all(outgoing, DP, split_axis=0, concat_axis=0)  10.2 us
    ppermute x1, starting transfers between devices, on_device(): take = lax.ppermute(give, 'c', SWAP)  8.79 us
  transfers between devices with their start and end apart: 19, of which 10 were waited for; matrix products, arithmetic and copies ran while one was open for 5% of the time, Pallas kernels for 7%

profile of v7, /device:TPU:1, one launch (start us, length us, event | category | flops | bytes accessed | tf_op | source)
XLA Modules:
  0.0 217.2 jit_solution(6083370598863064318)
XLA Ops:
  10.3 8.8 %collective-permute-start = (bf16[12,2176]{1,0:T(8,128)(2,1)S(1)}, bf16[12,2176]{1,0:T(8,128)(2,1)S(1)}, u32[]{:S(2)}, u32[]{:S(2)}) collective-permute-start(bf16[12,2176]{1,0:T(8,128)(2,1)S(1)} %get-tuple-element.69), channel_id=1, source_target_pairs={{0,16},{16,0},{1,17},{17,1},{2,18},{18,2},{3,19},{19,3},{4,20},{20... | collective-permute-start | bytes 156680 | tf_op jit(solution)/shard_map/ppermute | solution.py:234
  19.2 1.9 collective-permute-start.2
  23.8 1.9 collective-permute-start.1
  25.8 8.0 %collective-permute-done.1 = bf16[24,2176]{1,0:T(8,128)(2,1)S(1)} collective-permute-done((bf16[24,2176]{1,0:T(8,128)(2,1)S(1)}, bf16[24,2176]{1,0:T(8,128)(2,1)S(1)}, u32[]{:S(2)}, u32[]{:S(2)}) %collective-permute-start.1) | collective-permute-done | bytes 104480 | tf_op jit(solution)/shard_map/ppermute | solution.py:36
  35.2 1.9 collective-permute-start.3
  37.1 11.4 %collective-permute-done.3 = bf16[2,24,2176]{2,1,0:T(8,128)(2,1)S(1)} collective-permute-done((bf16[2,24,2176]{2,1,0:T(8,128)(2,1)S(1)}, bf16[2,24,2176]{2,1,0:T(8,128)(2,1)S(1)}, u32[]{:S(2)}, u32[]{:S(2)}) %collective-permute-start.3) | collective-permute-done | bytes 208928 | tf_op jit(solution)/shard_map/ppermute | solution.py:36
  48.6 2.6 %collective-permute-start.4 = (bf16[96,2176]{1,0:T(8,128)(2,1)S(1)}, bf16[96,2176]{1,0:T(8,128)(2,1)S(1)}, u32[]{:S(2)}, u32[]{:S(2)}) collective-permute-start(bf16[96,2176]{1,0:T(8,128)(2,1)S(1)} %bitcast.57), channel_id=1, source_target_pairs={{0,2},{2,4},{4,6},{6,8},{8,10},{10,12},{12,14},{14,0},{1,3},{3,5},... | collective-permute-start | bytes 1253384 | tf_op jit(solution)/shard_map/ppermute | solution.py:220
  51.2 8.6 %collective-permute-start.5 = (bf16[96,2176]{1,0:T(8,128)(2,1)S(1)}, bf16[96,2176]{1,0:T(8,128)(2,1)S(1)}, u32[]{:S(2)}, u32[]{:S(2)}) collective-permute-start(bf16[96,2176]{1,0:T(8,128)(2,1)S(1)} %bitcast.58), channel_id=1, source_target_pairs={{0,14},{2,0},{4,2},{6,4},{8,6},{10,8},{12,10},{14,12},{1,15},{3,1}... | collective-permute-start | bytes 1253384 | tf_op jit(solution)/shard_map/ppermute | solution.py:220
  59.8 5.6 %collective-permute-start.8 = (bf16[272,1024]{1,0:T(8,128)(2,1)S(1)}, bf16[272,1024]{1,0:T(8,128)(2,1)S(1)}, u32[]{:S(2)}, u32[]{:S(2)}) collective-permute-start(bf16[272,1024]{1,0:T(8,128)(2,1)S(1)} %get-tuple-element.70), channel_id=1, source_target_pairs={{0,256},{256,0},{1,257},{257,1},{2,258},{258,2},{3,259},{259,3},{4... | collective-permute-start | bytes 1671176 | tf_op jit(solution)/shard_map/ppermute | solution.py:258
  65.4 2.1 collective-permute-done.4.r1
  67.6 1.9 collective-permute-start.6
  69.5 4.6 %collective-permute-start.7 = (bf16[96,2176]{1,0:T(8,128)(2,1)S(1)}, bf16[96,2176]{1,0:T(8,128)(2,1)S(1)}, u32[]{:S(2)}, u32[]{:S(2)}) collective-permute-start(bf16[96,2176]{1,0:T(8,128)(2,1)S(1)} %collective-permute-done.5.l1), channel_id=1, source_target_pairs={{0,14},{2,0},{4,2},{6,4},{8,6},{10,8},{12,10},{14,12},{1,15},{3,1}... | collective-permute-start | bytes 1253384 | tf_op jit(solution)/shard_map/ppermute | solution.py:220
  74.1 17.4 %collective-permute-done.8 = bf16[272,1024]{1,0:T(8,128)(2,1)S(1)} collective-permute-done((bf16[272,1024]{1,0:T(8,128)(2,1)S(1)}, bf16[272,1024]{1,0:T(8,128)(2,1)S(1)}, u32[]{:S(2)}, u32[]{:S(2)}) %collective-permute-start.8) | collective-permute-done | bytes 557088 | tf_op jit(solution)/shard_map/ppermute | solution.py:258
  95.6 1.9 collective-permute-start.9
  97.5 4.6 %collective-permute-start.10 = (bf16[96,2176]{1,0:T(8,128)(2,1)S(1)}, bf16[96,2176]{1,0:T(8,128)(2,1)S(1)}, u32[]{:S(2)}, u32[]{:S(2)}) collective-permute-start(bf16[96,2176]{1,0:T(8,128)(2,1)S(1)} %copy-done.12), channel_id=1, source_target_pairs={{0,14},{2,0},{4,2},{6,4},{8,6},{10,8},{12,10},{14,12},{1,15},{3,1}... | collective-permute-start | bytes 1253384 | tf_op jit(solution)/shard_map/ppermute | solution.py:220
  102.8 6.1 %collective-permute-done.9.r3 = bf16[96,2176]{1,0:T(8,128)(2,1)S(1)} collective-permute-done((bf16[96,2176]{1,0:T(8,128)(2,1)S(1)}, bf16[96,2176]{1,0:T(8,128)(2,1)S(1)}, u32[]{:S(2)}, u32[]{:S(2)}) %collective-permute-start.9) | collective-permute-done | bytes 417824 | tf_op jit(solution)/shard_map/ppermute | solution.py:220
  108.9 1.9 collective-permute-start.11
  110.8 4.6 %collective-permute-start.12 = (bf16[48,2176]{1,0:T(8,128)(2,1)S(1)}, bf16[48,2176]{1,0:T(8,128)(2,1)S(1)}, u32[]{:S(2)}, u32[]{:S(2)}) collective-permute-start(bf16[48,2176]{1,0:T(8,128)(2,1)S(1)} %slice.117), channel_id=1, source_target_pairs={{0,14},{2,0},{4,2},{6,4},{8,6},{10,8},{12,10},{14,12},{1,15},{3,1}... | collective-permute-start | bytes 626696 | tf_op jit(solution)/shard_map/ppermute | solution.py:220
  115.5 1.5 collective-permute-done.11.r4
  118.8 9.8 %shard_map.94 = (f32[768,128]{1,0:T(8,128)}, bf16[768,2176]{1,0:T(8,128)(2,1)}, f32[768,1024]{1,0:T(8,128)}) custom-call(s32[3]{0:T(128)} %pad_add_fusion.place, bf16[2048,128]{1,0:T(8,128)(2,1)} %pad.24.down, bf16[4,272,1024]{2,1,0:T(8,128)(2,1)} %bitcast.54, bf16[96,2176]{1,0:T(8,128)(2,1)} %bitcast.59, bf16[96,2176]{1,0:T(8,128)(2,1)} %copy-done.8, ...), custom_call_target="tpu_custom_call" | custom-call | flops 1610612736 | bytes 10000000 | tf_op jit(solution)/shard_map/pallas_call | solution.py:207
  130.8 4.9 %collective-permute-start.13 = (f32[384,128]{1,0:T(8,128)S(1)}, f32[384,128]{1,0:T(8,128)S(1)}, u32[]{:S(2)}, u32[]{:S(2)}) collective-permute-start(f32[384,128]{1,0:T(8,128)S(1)} %slice_select_fusion.1), channel_id=1, source_target_pairs={{0,16},{16,0},{1,17},{17,1},{2,18},{18,2},{3,19},{19,3},{4,20},{20... | collective-permute-start | bytes 589832 | tf_op jit(solution)/shard_map/ppermute | solution.py:288
  137.9 5.5 %shard_map.96 = f32[384,1024]{1,0:T(8,128)} custom-call(s32[3]{0:T(128)} %pad_add_fusion.place, bf16[768,2176]{1,0:T(8,128)(2,1)} %get-tuple-element.31.tok.tok_in, bf16[4,272,1024]{2,1,0:T(8,128)(2,1)} %bitcast.50, f32[768,1024]{1,0:T(8,128)} %get-tuple-element.35.acc_in), custom_call_target="tpu_custom_call" | custom-call | flops 805306368 | bytes 10000000 | tf_op jit(solution)/shard_map/pallas_call | solution.py:207
  143.4 2.3 %collective-permute-start.14 = (f32[384,1024]{1,0:T(8,128)}, f32[384,1024]{1,0:T(8,128)S(1)}, u32[]{:S(2)}, u32[]{:S(2)}) collective-permute-start(f32[384,1024]{1,0:T(8,128)} %shard_map.96), channel_id=1, source_target_pairs={{0,16},{16,0},{1,17},{17,1},{2,18},{18,2},{3,19},{19,3},{4,20},{20... | collective-permute-start | bytes 4718600 | tf_op jit(solution)/shard_map/ppermute | solution.py:311
  145.7 5.6 %shard_map.95.near = f32[384,1024]{1,0:T(8,128)} custom-call(s32[3]{0:T(128)} %pad_add_fusion.place, bf16[768,2176]{1,0:T(8,128)(2,1)} %get-tuple-element.31.tok.tok_in, bf16[4,272,1024]{2,1,0:T(8,128)(2,1)} %bitcast.51, f32[768,1024]{1,0:T(8,128)} %get-tuple-element.35.acc_in), custom_call_target="tpu_custom_call" | custom-call | flops 805306368 | bytes 10000000 | tf_op jit(solution)/shard_map/pallas_call | solution.py:207
  153.3 1.5 copy-done.1
  154.8 3.7 %shard_map.97 = (f32[64,4,128]{2,1,0:T(4,128)S(1)}, f32[32,384]{1,0:T(8,128)S(1)}, bf16[4,384,512]{2,1,0:T(8,128)(2,1)S(1)}) custom-call(s32[3]{0:T(128)S(1)} %copy-done.2, f32[384,1024]{1,0:T(8,128)S(1)} %copy-done.1, f32[384,1024]{1,0:T(8,128)S(1)} %collective-permute-done.14.partner, bf16[384,128]{1,0:T(8,128)(2,1)S(1)} %add_convert_fusion.low_ref, ...), custom_call_target="tpu_custom_call" | custom-call | flops 201326592 | bytes 10000000 | tf_op jit(solution)/shard_map/pallas_call | solution.py:207
  158.6 16.6 %all_to_all.15.arrived = f32[64,4,128]{2,1,0:T(4,128)S(1)} all-to-all(f32[64,4,128]{2,1,0:T(4,128)S(1)} %get-tuple-element.41), channel_id=1, replica_groups=mesh['s'=2,'t'=2,'x'=4,'c'=2,'z'=8,'yl'=2] {'c','t','z','yl'}, dimensions={0} | all-to-all | bytes 262144 | tf_op jit(solution)/shard_map/all_to_all | solution.py:321
  175.2 3.2 %shard_map.98 = (f32[32,6,128]{2,1,0:T(8,128)}, f32[8,128]{1,0:T(8,128)S(1)}) custom-call(s32[3]{0:T(128)S(1)} %copy-done.2, f32[64,4,128]{2,1,0:T(4,128)S(1)} %all_to_all.15.arrived, bf16[2,128,384]{2,1,0:T(8,128)(2,1)S(1)} %fusion.5.signs, f32[2,1,128]{2,1,0:T(1,128)S(1)} %bitcast.49, f32[32,384]{1,0:T(8,128)S(1)} %get-tuple-element.43.low_t, ...), custom_call_target="tpu_custom_call" | custom-call | flops 25165824 | bytes 10000000 | tf_op jit(solution)/shard_map/pallas_call | solution.py:207
  178.3 8.0 %all-to-all-start.1 = ((f32[32,6,128]{2,1,0:T(8,128)}), f32[32,6,128]{2,1,0:T(8,128)S(1)}, u32[]{:S(2)}, u32[]{:S(2)}) async-start(f32[32,6,128]{2,1,0:T(8,128)} %get-tuple-element.45), calls=%async_computation.1 | async-start | bytes 262144 | tf_op jit(solution)/shard_map/all_to_all | solution.py:335
  186.9 10.2 %all-to-all-done.1 = f32[32,6,128]{2,1,0:T(8,128)S(1)} async-done(((f32[32,6,128]{2,1,0:T(8,128)}), f32[32,6,128]{2,1,0:T(8,128)S(1)}, u32[]{:S(2)}, u32[]{:S(2)}) %all-to-all-start.1) | async-done | bytes 98336 | tf_op jit(solution)/shard_map/all_to_all | solution.py:335
  197.8 3.5 %all-to-all-start.2 = ((f32[16,2,128]{2,1,0:T(2,128)}), f32[16,2,128]{2,1,0:T(2,128)S(1)}, u32[]{:S(2)}, u32[]{:S(2)}) async-start(f32[16,2,128]{2,1,0:T(2,128)} %broadcast_in_dim.32), calls=%async_computation.2 | async-start | bytes 32768 | tf_op jit(solution)/shard_map/all_to_all | solution.py:340
  203.7 4.9 %all-to-all-done.2 = f32[16,2,128]{2,1,0:T(2,128)S(1)} async-done(((f32[16,2,128]{2,1,0:T(2,128)}), f32[16,2,128]{2,1,0:T(2,128)S(1)}, u32[]{:S(2)}, u32[]{:S(2)}) %all-to-all-start.2) | async-done | bytes 16416 | tf_op jit(solution)/shard_map/all_to_all | solution.py:340
  (108 shorter events, 20.4 us)
Async XLA Ops:
  7.2 11.9 %copy-start.6 = (bf16[2,128,896]{2,1,0:T(8,128)(2,1)S(1)}, bf16[2,128,896]{2,1,0:T(8,128)(2,1)}, u32[]{:S(2)}) copy-start(bf16[2,128,896]{2,1,0:T(8,128)(2,1)} %param.10) | copy-start | bytes 1376260
  7.2 111.0 %all-gather.3.cloned.1.call-start = ((), (), s32[]{:S(2)}) async-start(), calls=%async_computation.3 | async-start | bytes 2785280 | tf_op jit(solution)/shard_map/all_gather | solution.py:254
  10.3 13.5 %collective-permute-start = (bf16[12,2176]{1,0:T(8,128)(2,1)S(1)}, bf16[12,2176]{1,0:T(8,128)(2,1)S(1)}, u32[]{:S(2)}, u32[]{:S(2)}) collective-permute-start(bf16[12,2176]{1,0:T(8,128)(2,1)S(1)} %get-tuple-element.69), channel_id=1, source_target_pairs={{0,16},{16,0},{1,17},{17,1},{2,18},{18,2},{3,19},{19,3},{4,20},{20... | collective-permute-start | bytes 156680 | tf_op jit(solution)/shard_map/ppermute | solution.py:234
  19.2 14.6 %collective-permute-start.2 = (bf16[128,1024]{1,0:T(8,128)(2,1)S(1)}, bf16[128,1024]{1,0:T(8,128)(2,1)S(1)}, u32[]{:S(2)}, u32[]{:S(2)}) collective-permute-start(bf16[128,1024]{1,0:T(8,128)(2,1)S(1)} %broadcast_select_fusion.4), channel_id=1, source_target_pairs={{0,128},{128,0},{1,129},{129,1},{2,130},{130,2},{3,131},{131,3},{4... | collective-permute-start | bytes 786440 | tf_op jit(solution)/shard_map/ppermute | solution.py:243
  23.8 10.0 %collective-permute-start.1 = (bf16[24,2176]{1,0:T(8,128)(2,1)S(1)}, bf16[24,2176]{1,0:T(8,128)(2,1)S(1)}, u32[]{:S(2)}, u32[]{:S(2)}) collective-permute-start(bf16[24,2176]{1,0:T(8,128)(2,1)S(1)} %maximum_select_fusion.3), channel_id=1, source_target_pairs={{0,1},{1,0},{2,3},{3,2},{4,5},{5,4},{6,7},{7,6},{8,9},{9,8},{10,11... | collective-permute-start | bytes 313352 | tf_op jit(solution)/shard_map/ppermute | solution.py:36
  35.2 102.7 %all-gather.5.cloned.1.call-start = ((), (), s32[]{:S(2)}) async-start(), calls=%async_computation.4 | async-start | bytes 2785280 | tf_op jit(solution)/shard_map/all_gather | solution.py:266
  35.2 13.3 %collective-permute-start.3 = (bf16[2,24,2176]{2,1,0:T(8,128)(2,1)S(1)}, bf16[2,24,2176]{2,1,0:T(8,128)(2,1)S(1)}, u32[]{:S(2)}, u32[]{:S(2)}) collective-permute-start(bf16[2,24,2176]{2,1,0:T(8,128)(2,1)S(1)} %maximum_select_fusion.1), channel_id=1, source_target_pairs={{0,128},{128,0},{1,129},{129,1},{2,130},{130,2},{3,131},{131,3},{4... | collective-permute-start | bytes 626696 | tf_op jit(solution)/shard_map/ppermute | solution.py:36
  48.6 45.8 %copy-start.3 = (bf16[2,2,24,2176]{3,2,1,0:T(8,128)(2,1)}, bf16[2,2,24,2176]{3,2,1,0:T(8,128)(2,1)S(1)}, u32[]{:S(2)}) copy-start(bf16[2,2,24,2176]{3,2,1,0:T(8,128)(2,1)S(1)} %maximum_select_fusion) | copy-start | bytes 1253380
  48.6 18.9 %collective-permute-start.4 = (bf16[96,2176]{1,0:T(8,128)(2,1)S(1)}, bf16[96,2176]{1,0:T(8,128)(2,1)S(1)}, u32[]{:S(2)}, u32[]{:S(2)}) collective-permute-start(bf16[96,2176]{1,0:T(8,128)(2,1)S(1)} %bitcast.57), channel_id=1, source_target_pairs={{0,2},{2,4},{4,6},{6,8},{8,10},{10,12},{12,14},{14,0},{1,3},{3,5},... | collective-permute-start | bytes 1253384 | tf_op jit(solution)/shard_map/ppermute | solution.py:220
  51.2 18.3 %collective-permute-start.5 = (bf16[96,2176]{1,0:T(8,128)(2,1)S(1)}, bf16[96,2176]{1,0:T(8,128)(2,1)S(1)}, u32[]{:S(2)}, u32[]{:S(2)}) collective-permute-start(bf16[96,2176]{1,0:T(8,128)(2,1)S(1)} %bitcast.58), channel_id=1, source_target_pairs={{0,14},{2,0},{4,2},{6,4},{8,6},{10,8},{12,10},{14,12},{1,15},{3,1}... | collective-permute-start | bytes 1253384 | tf_op jit(solution)/shard_map/ppermute | solution.py:220
  59.8 31.7 %collective-permute-start.8 = (bf16[272,1024]{1,0:T(8,128)(2,1)S(1)}, bf16[272,1024]{1,0:T(8,128)(2,1)S(1)}, u32[]{:S(2)}, u32[]{:S(2)}) collective-permute-start(bf16[272,1024]{1,0:T(8,128)(2,1)S(1)} %get-tuple-element.70), channel_id=1, source_target_pairs={{0,256},{256,0},{1,257},{257,1},{2,258},{258,2},{3,259},{259,3},{4... | collective-permute-start | bytes 1671176 | tf_op jit(solution)/shard_map/ppermute | solution.py:258
  67.6 50.6 %copy-start.8 = (bf16[96,2176]{1,0:T(8,128)(2,1)}, bf16[96,2176]{1,0:T(8,128)(2,1)S(1)}, u32[]{:S(2)}) copy-start(bf16[96,2176]{1,0:T(8,128)(2,1)S(1)} %collective-permute-done.4.r1) | copy-start | bytes 1253380
  67.6 23.9 %collective-permute-start.6 = (bf16[96,2176]{1,0:T(8,128)(2,1)S(1)}, bf16[96,2176]{1,0:T(8,128)(2,1)S(1)}, u32[]{:S(2)}, u32[]{:S(2)}) collective-permute-start(bf16[96,2176]{1,0:T(8,128)(2,1)S(1)} %collective-permute-done.4.r1), channel_id=1, source_target_pairs={{0,2},{2,4},{4,6},{6,8},{8,10},{10,12},{12,14},{14,0},{1,3},{3,5},... | collective-permute-start | bytes 1253384 | tf_op jit(solution)/shard_map/ppermute | solution.py:220
  69.5 48.7 %copy-start.9 = (bf16[96,2176]{1,0:T(8,128)(2,1)}, bf16[96,2176]{1,0:T(8,128)(2,1)S(1)}, u32[]{:S(2)}) copy-start(bf16[96,2176]{1,0:T(8,128)(2,1)S(1)} %collective-permute-done.5.l1) | copy-start | bytes 1253380
  69.5 22.0 %collective-permute-start.7 = (bf16[96,2176]{1,0:T(8,128)(2,1)S(1)}, bf16[96,2176]{1,0:T(8,128)(2,1)S(1)}, u32[]{:S(2)}, u32[]{:S(2)}) collective-permute-start(bf16[96,2176]{1,0:T(8,128)(2,1)S(1)} %collective-permute-done.5.l1), channel_id=1, source_target_pairs={{0,14},{2,0},{4,2},{6,4},{8,6},{10,8},{12,10},{14,12},{1,15},{3,1}... | collective-permute-start | bytes 1253384 | tf_op jit(solution)/shard_map/ppermute | solution.py:220
  91.5 4.1 %copy-start.10 = (bf16[96,2176]{1,0:T(8,128)(2,1)}, bf16[96,2176]{1,0:T(8,128)(2,1)S(1)}, u32[]{:S(2)}) copy-start(bf16[96,2176]{1,0:T(8,128)(2,1)S(1)} %collective-permute-done.6.r2) | copy-start | bytes 1253380
  94.4 1.1 copy-start.15
  94.5 3.1 %copy-start.12 = (bf16[96,2176]{1,0:T(8,128)(2,1)S(1)}, bf16[96,2176]{1,0:T(8,128)(2,1)}, u32[]{:S(2)}) copy-start(bf16[96,2176]{1,0:T(8,128)(2,1)} %copy-done.11) | copy-start | bytes 1253380
  95.6 13.2 %collective-permute-start.9 = (bf16[96,2176]{1,0:T(8,128)(2,1)S(1)}, bf16[96,2176]{1,0:T(8,128)(2,1)S(1)}, u32[]{:S(2)}, u32[]{:S(2)}) collective-permute-start(bf16[96,2176]{1,0:T(8,128)(2,1)S(1)} %collective-permute-done.6.r2), channel_id=1, source_target_pairs={{0,2},{2,4},{4,6},{6,8},{8,10},{10,12},{12,14},{14,0},{1,3},{3,5},... | collective-permute-start | bytes 1253384 | tf_op jit(solution)/shard_map/ppermute | solution.py:220
  97.5 13.2 %collective-permute-start.10 = (bf16[96,2176]{1,0:T(8,128)(2,1)S(1)}, bf16[96,2176]{1,0:T(8,128)(2,1)S(1)}, u32[]{:S(2)}, u32[]{:S(2)}) collective-permute-start(bf16[96,2176]{1,0:T(8,128)(2,1)S(1)} %copy-done.12), channel_id=1, source_target_pairs={{0,14},{2,0},{4,2},{6,4},{8,6},{10,8},{12,10},{14,12},{1,15},{3,1}... | collective-permute-start | bytes 1253384 | tf_op jit(solution)/shard_map/ppermute | solution.py:220
  108.8 9.3 %copy-start.4 = (bf16[96,2176]{1,0:T(8,128)(2,1)}, bf16[96,2176]{1,0:T(8,128)(2,1)S(1)}, u32[]{:S(2)}) copy-start(bf16[96,2176]{1,0:T(8,128)(2,1)S(1)} %collective-permute-done.9.r3) | copy-start | bytes 1253380
  108.9 8.2 %collective-permute-start.11 = (bf16[48,2176]{1,0:T(8,128)(2,1)S(1)}, bf16[48,2176]{1,0:T(8,128)(2,1)S(1)}, u32[]{:S(2)}, u32[]{:S(2)}) collective-permute-start(bf16[48,2176]{1,0:T(8,128)(2,1)S(1)} %slice.116), channel_id=1, source_target_pairs={{0,2},{2,4},{4,6},{6,8},{8,10},{10,12},{12,14},{14,0},{1,3},{3,5},... | collective-permute-start | bytes 626696 | tf_op jit(solution)/shard_map/ppermute | solution.py:220
  110.8 7.4 %copy-start.5 = (bf16[96,2176]{1,0:T(8,128)(2,1)}, bf16[96,2176]{1,0:T(8,128)(2,1)S(1)}, u32[]{:S(2)}) copy-start(bf16[96,2176]{1,0:T(8,128)(2,1)S(1)} %collective-permute-done.10.l3) | copy-start | bytes 1253380
  110.8 7.3 %collective-permute-start.12 = (bf16[48,2176]{1,0:T(8,128)(2,1)S(1)}, bf16[48,2176]{1,0:T(8,128)(2,1)S(1)}, u32[]{:S(2)}, u32[]{:S(2)}) collective-permute-start(bf16[48,2176]{1,0:T(8,128)(2,1)S(1)} %slice.117), channel_id=1, source_target_pairs={{0,14},{2,0},{4,2},{6,4},{8,6},{10,8},{12,10},{14,12},{1,15},{3,1}... | collective-permute-start | bytes 626696 | tf_op jit(solution)/shard_map/ppermute | solution.py:220
  117.0 1.2 copy-start.13
  130.8 6.0 %collective-permute-start.13 = (f32[384,128]{1,0:T(8,128)S(1)}, f32[384,128]{1,0:T(8,128)S(1)}, u32[]{:S(2)}, u32[]{:S(2)}) collective-permute-start(f32[384,128]{1,0:T(8,128)S(1)} %slice_select_fusion.1), channel_id=1, source_target_pairs={{0,16},{16,0},{1,17},{17,1},{2,18},{18,2},{3,19},{19,3},{4,20},{20... | collective-permute-start | bytes 589832 | tf_op jit(solution)/shard_map/ppermute | solution.py:288
  143.4 9.9 %copy-start.2 = (s32[3]{0:T(128)S(1)}, s32[3]{0:T(128)}, u32[]{:S(2)}) copy-start(s32[3]{0:T(128)} %pad_add_fusion.place) | copy-start | bytes 40
  143.4 9.9 %collective-permute-start.14 = (f32[384,1024]{1,0:T(8,128)}, f32[384,1024]{1,0:T(8,128)S(1)}, u32[]{:S(2)}, u32[]{:S(2)}) collective-permute-start(f32[384,1024]{1,0:T(8,128)} %shard_map.96), channel_id=1, source_target_pairs={{0,16},{16,0},{1,17},{17,1},{2,18},{18,2},{3,19},{19,3},{4,20},{20... | collective-permute-start | bytes 4718600 | tf_op jit(solution)/shard_map/ppermute | solution.py:311
  153.3 21.9 %copy-start = (bf16[768,2176]{1,0:T(8,128)(2,1)S(1)}, bf16[768,2176]{1,0:T(8,128)(2,1)}, u32[]{:S(2)}) copy-start(bf16[768,2176]{1,0:T(8,128)(2,1)} %get-tuple-element.31.tok.tok_in) | copy-start | bytes 10027012
  153.3 1.6 copy-start.1
  178.3 18.8 %all-to-all-start.1 = ((f32[32,6,128]{2,1,0:T(8,128)}), f32[32,6,128]{2,1,0:T(8,128)S(1)}, u32[]{:S(2)}, u32[]{:S(2)}) async-start(f32[32,6,128]{2,1,0:T(8,128)} %get-tuple-element.45), calls=%async_computation.1 | async-start | bytes 262144 | tf_op jit(solution)/shard_map/all_to_all | solution.py:335
  197.8 10.8 %all-to-all-start.2 = ((f32[16,2,128]{2,1,0:T(2,128)}), f32[16,2,128]{2,1,0:T(2,128)S(1)}, u32[]{:S(2)}, u32[]{:S(2)}) async-start(f32[16,2,128]{2,1,0:T(2,128)} %broadcast_in_dim.32), calls=%async_computation.2 | async-start | bytes 32768 | tf_op jit(solution)/shard_map/all_to_all | solution.py:340
  (4 other events, 3.7 us)
Sparse Core Ops, SparseCore 0:
  35.3 39.0 all-gather.2
  92.6 32.9 all-gather.4

commit v8 on v5

v8 whole, which is shorter than its diff:
```python
import functools

import jax
import jax.numpy as jnp
from jax import lax
from jax.experimental import pallas as pl
from jax.experimental.pallas import tpu as pltpu
from jax.sharding import Mesh, PartitionSpec as P

SEQS = 4
ROWS = 12
RANK = 16
WIDTH = 4096
DPO_BETA = 0.1
LOSS_SCALE = 1024.0
F32 = jnp.float32
BF16 = jnp.bfloat16

AXES = ("yh", "x", "c", "z", "yl")
SIZES = (4, 4, 2, 8, 2)
DP = ("yh", "x", "c")
BLK = ("z", "yl")
SWAP = [(0, 1), (1, 0)]

SLICE = 128
HALF = WIDTH // 2
LANES = 128
UNITS = 896
MAIN = 640
SIDE = UNITS - MAIN
PIECE = SLICE + 16
GROUP = 192
BLOCKS = GROUP // ROWS
CONTRACT_LAST = (((1,), (1,)), ((), ()))


def swapped(value, axis, index):
    far = lax.ppermute(value, axis, SWAP)
    return jnp.where(index == 0, jnp.stack([value, far]), jnp.stack([far, value]))


def split(value, terms):
    parts = []
    for _ in range(terms):
        parts.append(value.astype(BF16))
        value = value - parts[-1].astype(F32)
    return parts


def dot(a, b, dims=(((1,), (0,)), ((), ()))):
    return lax.dot_general(a, b, dims, preferred_element_type=F32)


def early_products(place, down, p0, r1, l1, r2, l2, r3, l3, far_z, s0, s1, s2, s3, out, tok_out, tok, w, sems):
    z, yh, x = place[1], place[2], place[3]
    block = 4 * ROWS
    moves = ((0, p0), (-1, r1), (1, l1), (-2, r2), (2, l2), (-3, r3), (3, l3), (4, far_z))
    copies = []
    for n, (k, ref) in enumerate(moves):
        rows = pl.ds(pl.multiple_of(lax.rem(z + 8 + k, 8) * block, block), block)
        copies.append(pltpu.make_async_copy(ref, tok.at[rows, :], sems.at[n]))
    for j, ref in enumerate((s0, s1, s2, s3)):
        for k in range(4):
            source = lax.rem(yh + k, 4) * 4 + lax.rem(x + j, 4)
            rows = pl.ds(pl.multiple_of(source * SLICE, SLICE), SLICE)
            copies.append(
                pltpu.make_async_copy(ref.at[pl.ds(k * PIECE, SLICE), :], w.at[rows, :], sems.at[8 + 4 * j + k])
            )
    for copy in copies:
        copy.start()
    for copy in copies:
        copy.wait()
    tok_copy = pltpu.make_async_copy(tok, tok_out, sems.at[24])
    tok_copy.start()
    for n in range(2):
        part = slice(n * SIDE, (n + 1) * SIDE)
        out[:, part] = dot(tok[:, 0:HALF], w[:, part])
    out[:, 2 * SIDE :] = dot(tok[:, 0:HALF], down[...])
    tok_copy.wait()


def main_products(far, place, tok, w_in, out, rows, w, sems):
    half = 1 - place[0] if far else place[0]
    mine = pl.ds(pl.multiple_of(half * GROUP, GROUP), GROUP)
    parts = [pl.ds(n * 256, 256) for n in range(2 * MAIN // 256)]
    rows_copy = pltpu.make_async_copy(tok.at[mine, pl.ds(0, HALF)], rows, sems.at[0])
    rows_copy.start()
    copies = [
        pltpu.make_async_copy(w_in.at[:, part], w.at[:, part], sems.at[1 + n]) for n, part in enumerate(parts)
    ]
    for copy in copies:
        copy.start()
    rows_copy.wait()
    for part, copy in zip(parts, copies):
        copy.wait()
        out[:, part] = dot(rows[...], w[:, part])


def products(far, place, tok, w):
    return kernel(
        functools.partial(main_products, far),
        [((GROUP, 2 * MAIN), F32)],
        (place, tok, w),
        2 * GROUP * HALF * 2 * MAIN, 56,
        scratch=[
            pltpu.VMEM((GROUP, HALF), BF16),
            pltpu.VMEM((HALF, 2 * MAIN), BF16),
            pltpu.SemaphoreType.DMA((6,)),
        ],
        in_hbm=2,
    )[0]


def score(place, near, partner, side, b_gate, b_up, readout, signs, count, message, low_t, k_out, k, sems):
    low_b = side[:, 2 * SIDE :].astype(BF16)
    main = near[...] + partner[...]
    gate_ref = jnp.concatenate([main[:, 0:MAIN], side[:, 0:SIDE]], axis=1)
    up_ref = jnp.concatenate([main[:, MAIN:], side[:, SIDE : 2 * SIDE]], axis=1)
    gate_pol = gate_ref + dot(low_b, b_gate[...])
    up_pol = up_ref + dot(low_b, b_up[...])
    sig_ref = jax.nn.sigmoid(gate_ref)
    sig_pol = jax.nn.sigmoid(gate_pol)
    act_pol = gate_pol * sig_pol
    read = readout[...].astype(F32)
    change = act_pol * up_pol - gate_ref * sig_ref * up_ref
    k_gate = read * sig_pol * (1.0 + gate_pol * (1.0 - sig_pol)) * up_pol
    k_up = read * act_pol
    read_b = jnp.broadcast_to(readout[...], (8, UNITS))
    change_row = sum(dot(read_b, part, CONTRACT_LAST) for part in split(change, 3))
    sign = signs[place[0]]
    gaps = sum(dot(part, sign, CONTRACT_LAST) for part in split(change_row, 3))
    tail = jnp.broadcast_to(gaps[0:1, :] + count[...], (RANK, LANES))
    high, rest = split(k_gate, 2)
    k[0], k[1] = high, rest
    copies = [pltpu.make_async_copy(k.at[i], k_out.at[i], sems.at[i]) for i in range(4)]
    copies[0].start()
    copies[1].start()
    mixed = dot(b_gate[0:RANK, :], high, CONTRACT_LAST) + dot(b_gate[0:RANK, :], rest, CONTRACT_LAST)
    high, rest = split(k_up, 2)
    k[2], k[3] = high, rest
    copies[2].start()
    copies[3].start()
    mixed_up = dot(b_up[RANK : 2 * RANK, :], high, CONTRACT_LAST) + dot(b_up[RANK : 2 * RANK, :], rest, CONTRACT_LAST)
    for core in range(2):
        lines = slice(RANK * core, RANK * (core + 1))
        for i, value in enumerate((mixed, mixed_up)):
            message[lines, 2 * i, :] = value[:, 0:LANES]
            message[lines, 2 * i + 1, :] = jnp.concatenate(
                [value[:, LANES:], jnp.zeros((RANK, 2 * LANES - GROUP), F32)], axis=1
            )
        message[lines, 4, :] = tail
    low_t[...] = low_b.astype(F32).T[0 : 2 * RANK, :]
    for copy in copies:
        copy.wait()


def close(place, arrived, signs, valid, low_t, k_in, tok_in, out, total_out, k, tok, sems):
    tok_copy = pltpu.make_async_copy(tok_in, tok, sems.at[0])
    k_copy = pltpu.make_async_copy(k_in, k, sems.at[1])
    tok_copy.start()
    k_copy.start()
    core = place[0]
    sums = [jnp.sum(arrived[RANK * h : RANK * (h + 1)], axis=0) for h in range(2)]
    tails = [total[4:5, :] for total in sums]
    line = lax.broadcasted_iota(jnp.int32, (8, GROUP), 0)
    pair_total = jnp.maximum(tails[0][:, 64:65] + tails[1][:, 64:65], 1.0)
    logs, cotangents, terms = 0.0, [], []
    for h in range(2):
        logit = DPO_BETA * tails[h]
        logs = logs + jnp.sum(
            valid[h] * (jnp.minimum(logit, 0.0) - jnp.log1p(jnp.exp(-jnp.abs(logit)))), axis=1, keepdims=True
        )
        scaled = -LOSS_SCALE * DPO_BETA * valid[h] * jax.nn.sigmoid(-logit) / pair_total
        scaled = jnp.broadcast_to(scaled, (8, LANES))
        cotangent = sum(dot(part, signs[h]) for part in split(scaled, 3))
        cotangents.append(cotangent[0:1, :])
        gate, up = (
            jnp.concatenate([sums[h][i : i + 1, :], sums[h][i + 1 : i + 2, 0 : GROUP - LANES]], axis=1) for i in (0, 2)
        )
        projected = jnp.where(line == 0, gate, jnp.where(line == 1, up, 0.0)) * cotangent
        if h == 0:
            tok_copy.wait()
        terms.append(dot(projected.astype(BF16), tok[h * GROUP : (h + 1) * GROUP, 0:HALF]))
    grad_a = terms[0] + terms[1]
    own = jnp.where(core == 0, cotangents[0], cotangents[1])
    high, rest = split(low_t[...] * own, 2)
    k_copy.wait()
    gate = dot(high[0:RANK], k[0]) + dot(high[0:RANK], k[1]) + dot(rest[0:RANK], k[0])
    up = dot(high[RANK:], k[2]) + dot(high[RANK:], k[3]) + dot(rest[RANK:], k[2])
    for i in range(UNITS // LANES):
        out[0:RANK, i, :] = gate[:, i * LANES : (i + 1) * LANES]
        out[RANK : 2 * RANK, i, :] = up[:, i * LANES : (i + 1) * LANES]
    line = lax.broadcasted_iota(jnp.int32, (2 * RANK, SLICE), 0)
    for column in range(2):
        slices = jnp.zeros((2 * RANK, SLICE), F32)
        for i in range(RANK):
            here = jnp.broadcast_to(
                grad_a[column : column + 1, i * SLICE : (i + 1) * SLICE], (2 * RANK, SLICE)
            )
            slices = jnp.where(line == 2 * i + core, here, slices)
        out[:, 7 + column, :] = slices
    out[:, 9, :] = jnp.broadcast_to(0.5 * logs, (2 * RANK, LANES))
    total_out[...] = jnp.broadcast_to(pair_total, (8, LANES))


def kernel(function, shapes, arguments, flops, grant, scratch=(), in_hbm=0, out_hbm=0):
    vmem = pl.BlockSpec(memory_space=pltpu.VMEM)
    smem = pl.BlockSpec(memory_space=pltpu.SMEM)
    hbm = pl.BlockSpec(memory_space=pltpu.HBM)
    return pl.pallas_call(
        function,
        out_shape=tuple(jax.ShapeDtypeStruct(*s) for s in shapes),
        in_specs=[smem] + [vmem] * (len(arguments) - 1 - in_hbm) + [hbm] * in_hbm,
        out_specs=(vmem,) * (len(shapes) - out_hbm) + (hbm,) * out_hbm,
        scratch_shapes=list(scratch),
        compiler_params=pltpu.CompilerParams(vmem_limit_bytes=grant * 1024 * 1024),
        cost_estimate=pl.CostEstimate(flops=flops, bytes_accessed=10_000_000, transcendentals=0),
    )(*arguments)


def along(value, axis, k):
    n = lax.axis_size(axis)
    return lax.ppermute(value, axis, [(i, (i + k) % n) for i in range(n)])


def fetch(value, axis, k):
    n = lax.axis_size(axis)
    return lax.ppermute(value, axis, [((i + k) % n, i) for i in range(n)])


def on_device(tokens, sequence_labels, response_mask, frozen, down, up, readout):
    yh, x, core, z, yl = (lax.axis_index(a) for a in AXES)
    place = jnp.stack([core, z, yh, x]).astype(jnp.int32)
    code = jnp.where(response_mask > 0, sequence_labels, SEQS)

    main = jnp.concatenate([frozen[0, :, :MAIN], frozen[1, :, :MAIN]], axis=1)
    w_main = lax.all_gather(main, ("yh", "x"), axis=0, tiled=True)

    by_core = tokens.reshape(ROWS, 16, 2, SLICE).transpose(2, 0, 1, 3).reshape(2, ROWS, HALF)
    code_lanes = jnp.pad(code.reshape(ROWS, 1).astype(BF16), ((0, 0), (0, LANES - 1)))
    keep = jnp.concatenate([jnp.where(core == 0, by_core[0], by_core[1]), code_lanes], axis=1)
    give = jnp.concatenate([jnp.where(core == 0, by_core[1], by_core[0]), code_lanes], axis=1)
    take = lax.ppermute(give, "c", SWAP)
    pair = jnp.where(
        core == 0, jnp.concatenate([keep, take], axis=0), jnp.concatenate([take, keep], axis=0)
    )
    four = swapped(pair, "yl", yl).reshape(4 * ROWS, HALF + LANES)
    ring = [four, along(four, "z", 1), along(four, "z", -1)]

    has = [jnp.max((code == q).astype(F32)) for q in range(SEQS)]
    count_rows = jnp.broadcast_to((has[0] * has[1] + has[2] * has[3]).astype(BF16), (16, 2 * SIDE))
    piece = jnp.concatenate(
        [jnp.concatenate([frozen[0, :, MAIN:], frozen[1, :, MAIN:]], axis=1), count_rows], axis=0
    )
    pieces = [piece] + [fetch(piece, "yh", k) for k in (1, 2, 3)]
    ring[1], ring[2], *pieces = lax.optimization_barrier((ring[1], ring[2], *pieces))
    stack = jnp.concatenate(pieces, axis=0)
    stacks = [stack] + [fetch(stack, "x", j) for j in (1, 2, 3)]
    for step in range(2):
        ring += [along(ring[-2], "z", 1), along(ring[-1], "z", -1)]
    ring.append(along(ring[-2], "z", 1))
    count = sum(jnp.sum(p.reshape(4, PIECE, 2 * SIDE)[:, SLICE, 0].astype(F32)) for p in stacks)
    count_lanes = jnp.where(jnp.arange(LANES) == 64, count, 0.0).reshape(1, LANES)

    down_half = down.reshape(16, 2, SLICE, 2 * RANK)
    down_half = jnp.where(core == 0, down_half[:, 0], down_half[:, 1]).reshape(HALF, 2 * RANK)
    down_half = jnp.pad(down_half, ((0, 0), (0, LANES - 2 * RANK)))
    side, tok = kernel(
        early_products,
        [((2 * GROUP, 2 * SIDE + LANES), F32), ((2 * GROUP, HALF + LANES), BF16)],
        (place, down_half, *ring, *stacks),
        4 * GROUP * HALF * (2 * SIDE + LANES), 56,
        scratch=[
            pltpu.VMEM((2 * GROUP, HALF + LANES), BF16),
            pltpu.VMEM((HALF, 2 * SIDE), BF16),
            pltpu.SemaphoreType.DMA((25,)),
        ],
        in_hbm=12, out_hbm=1,
    )
    side = side.reshape(2, GROUP, 2 * SIDE + LANES)
    side_far = jnp.where(core == 0, side[1], side[0])
    side = jnp.where(core == 0, side[0], side[1]) + lax.ppermute(side_far, "c", SWAP)

    b_gate = jnp.pad(up[:RANK], ((0, LANES - RANK), (0, 0)))
    b_up = jnp.pad(up[RANK:], ((RANK, LANES - 2 * RANK), (0, 0)))
    read = readout.reshape(1, UNITS)

    codes = tok[:, HALF].astype(jnp.int32).reshape(2, GROUP)
    pair_of = jnp.arange(LANES, dtype=jnp.int32)
    block_of = jnp.arange(GROUP, dtype=jnp.int32) // ROWS
    inside = (pair_of[:, None] // 2 == block_of[None, :])[None]
    chosen = inside & (codes[:, None, :] == 2 * (pair_of % 2)[None, :, None])
    rejected = inside & (codes[:, None, :] == 2 * (pair_of % 2)[None, :, None] + 1)
    signs = chosen.astype(BF16) - rejected.astype(BF16)
    valid = (jnp.any(chosen, axis=2) & jnp.any(rejected, axis=2)).astype(F32).reshape(2, 1, LANES)

    w_main, side, b_gate, b_up, read, signs, valid, count_lanes = lax.optimization_barrier(
        (w_main, side, b_gate, b_up, read, signs, valid, count_lanes)
    )
    far = products(True, place, tok, w_main)
    partner = lax.ppermute(far, "c", SWAP)
    near = products(False, place, tok, w_main)
    message, low_t, k = kernel(
        score,
        [((2 * RANK, 5, LANES), F32), ((2 * RANK, GROUP), F32), ((4, GROUP, UNITS), BF16)],
        (place, near, partner, side, b_gate, b_up, read, signs, count_lanes),
        8 * GROUP * UNITS * LANES, 16,
        scratch=[pltpu.VMEM((4, GROUP, UNITS), BF16), pltpu.SemaphoreType.DMA((4,))],
        out_hbm=1,
    )
    arrived = lax.all_to_all(message, ("c", "z", "yl"), split_axis=0, concat_axis=0)
    outgoing, pair_total = kernel(
        close,
        [((2 * RANK, 10, LANES), F32), ((8, LANES), F32)],
        (place, arrived, signs, valid, low_t, k, tok),
        16 * GROUP * HALF * 2, 16,
        scratch=[
            pltpu.VMEM((4, GROUP, UNITS), BF16),
            pltpu.VMEM((2 * GROUP, HALF + LANES), BF16),
            pltpu.SemaphoreType.DMA((2,)),
        ],
        in_hbm=2,
    )

    summed = jnp.sum(lax.all_to_all(outgoing, DP, split_axis=0, concat_axis=0), axis=0)
    grad_a = lax.all_to_all(
        jnp.broadcast_to(summed[None, 7:9], (16, 2, SLICE)), BLK, split_axis=0, concat_axis=0
    )
    grad_a = grad_a.transpose(2, 1, 0).reshape(SLICE, 2 * RANK)
    return -summed[9, 0] / pair_total[0, 0], grad_a, summed[:7].reshape(1, UNITS)


def solution(mesh):
    fine = Mesh(mesh.devices.reshape(SIZES), AXES)
    in_specs = (
        P(AXES, None),
        P(AXES, None),
        P(AXES, None),
        P(None, DP, BLK),
        P(),
        P(None, BLK),
        P(BLK),
    )
    out_specs = (P(), P(DP, None), P(DP, BLK))
    return jax.shard_map(
        on_device, mesh=fine, in_specs=in_specs, out_specs=out_specs, check_vma=False
    )
```

time: 229 us -> 211 us (0.921)
  local copies, waits for them, and re-layouts: 25.9 us -> 10.9 us
  waiting for transfers between devices: 55.9 us -> 45.4 us
  Pallas kernels: 15 us -> 23.8 us
  between operations: 19.9 us -> 22.3 us
    unnamed x72 -> x41, local copies, waits for them, and re-layouts: 18.5 us -> 2.68 us
    pallas_call x3 -> x5, Pallas kernels: 9.61 us -> 23.8 us  [kernel(): pl.pallas_call(function, out_shape=tuple((jax.ShapeDtypeStruct(*s) for s...]
    ppermute x2 -> x1, waiting for transfers between devices: 12.7 us -> 5.52 us  [swapped(): far = lax.ppermute(value, axis, SWAP)]
    pallas_call x2 -> x0, Pallas kernels: 5.36 us -> none  [products(): pl.pallas_call(late_products, grid_spec=pltpu.PrefetchScalarGridSpec(num_...]
    ppermute x6 -> x7, waiting for transfers between devices: 23.6 us -> 19 us  [the longest x6 17.9 us: fetch(): return lax.ppermute(value, axis, [((i + k) % n, i) for i in range(n)])]
    ppermute x2 -> x1, starting transfers between devices: 6.65 us -> 2.31 us  [swapped(): far = lax.ppermute(value, axis, SWAP)]
    all_to_all x2, waiting for transfers between devices: 15.1 us -> 18 us  [the longest x1 13.1 us: on_device(): lax.all_to_all(outgoing, DP, split_axis=0, concat_axis=0)]
    reduce_sum x1 -> x5, other arithmetic: 0.02 us -> 2.74 us  [the longest x4 2.7 us: on_device(): jnp.sum(p.reshape(4, PIECE, 2 * SIDE)[:, SLICE, 0].astype(F32))]
  transfers between devices with their start and end apart: 22 -> 20, of which waited for: 9 -> 9; matrix products, arithmetic and copies ran while one was open for 7% -> 7% of each run, Pallas kernels for 3% -> 5%
where the time goes in v8:
time: 211 us; the launch traced here: 210 us
  starting transfers between devices  81.5 us (39%)
  waiting for transfers between devices  45.4 us (22%)
  Pallas kernels  23.8 us (11%)
  between operations  22.3 us (11%)
  blocking collectives  17.4 us (8%)
  local copies, waits for them, and re-layouts  10.9 us (5%)
  other arithmetic  8.6 us (4%)
    ppermute x7, starting transfers between devices, along(): return lax.ppermute(value, axis, [(i, (i + k) % n) for i in range(n)])  33.2 us
    pallas_call x5, Pallas kernels, kernel(): pl.pallas_call(function, out_shape=tuple((jax.ShapeDtypeStruct(*s) for s...  23.8 us
    ppermute x6, starting transfers between devices, fetch(): return lax.ppermute(value, axis, [((i + k) % n, i) for i in range(n)])  23.8 us
    ppermute x6, waiting for transfers between devices, fetch(): return lax.ppermute(value, axis, [((i + k) % n, i) for i in range(n)])  17.9 us
    all_to_all x1, blocking collectives, on_device(): lax.all_to_all(message, ('c', 'z', 'yl'), split_axis=0, concat_axis=0)  17.4 us
    all_to_all x1, waiting for transfers between devices, on_device(): lax.all_to_all(outgoing, DP, split_axis=0, concat_axis=0)  13.1 us
    all_to_all x1, starting transfers between devices, on_device(): lax.all_to_all(outgoing, DP, split_axis=0, concat_axis=0)  7.79 us
    ppermute x1, waiting for transfers between devices, swapped(): far = lax.ppermute(value, axis, SWAP)  5.52 us
  transfers between devices with their start and end apart: 20, of which 9 were waited for; matrix products, arithmetic and copies ran while one was open for 7% of the time, Pallas kernels for 5%

profile of v8, /device:TPU:1, one launch (start us, length us, event | category | flops | bytes accessed | tf_op | source)
XLA Modules:
  0.0 210.0 jit_solution(2669776071518950585)
XLA Ops:
  13.8 6.7 %collective-permute-start.4 = (bf16[144,512]{1,0:T(8,128)(2,1)S(1)}, bf16[144,512]{1,0:T(8,128)(2,1)S(1)}, u32[]{:S(2)}, u32[]{:S(2)}) collective-permute-start(bf16[144,512]{1,0:T(8,128)(2,1)S(1)} %fusion.6), channel_id=1, source_target_pairs={{128,0},{256,128},{384,256},{0,384},{129,1},{257,129},{385,257},{1... | collective-permute-start | bytes 442376 | tf_op jit(solution)/shard_map/ppermute | solution.py:228
  20.5 3.5 %collective-permute-start.5 = (bf16[144,512]{1,0:T(8,128)(2,1)S(1)}, bf16[144,512]{1,0:T(8,128)(2,1)S(1)}, u32[]{:S(2)}, u32[]{:S(2)}) collective-permute-start(bf16[144,512]{1,0:T(8,128)(2,1)S(1)} %fusion.6), channel_id=1, source_target_pairs={{256,0},{384,128},{0,256},{128,384},{257,1},{385,129},{1,257},{129... | collective-permute-start | bytes 442376 | tf_op jit(solution)/shard_map/ppermute | solution.py:228
  24.1 4.2 %collective-permute-start.6 = (bf16[144,512]{1,0:T(8,128)(2,1)S(1)}, bf16[144,512]{1,0:T(8,128)(2,1)S(1)}, u32[]{:S(2)}, u32[]{:S(2)}) collective-permute-start(bf16[144,512]{1,0:T(8,128)(2,1)S(1)} %fusion.6), channel_id=1, source_target_pairs={{384,0},{0,128},{128,256},{256,384},{385,1},{1,129},{129,257},{257... | collective-permute-start | bytes 442376 | tf_op jit(solution)/shard_map/ppermute | solution.py:228
  28.7 3.4 %collective-permute-start = (bf16[12,2176]{1,0:T(8,128)(2,1)S(1)}, bf16[12,2176]{1,0:T(8,128)(2,1)S(1)}, u32[]{:S(2)}, u32[]{:S(2)}) collective-permute-start(bf16[12,2176]{1,0:T(8,128)(2,1)S(1)} %get-tuple-element.63), channel_id=1, source_target_pairs={{0,16},{16,0},{1,17},{17,1},{2,18},{18,2},{3,19},{19,3},{4,20},{20... | collective-permute-start | bytes 156680 | tf_op jit(solution)/shard_map/ppermute | solution.py:243
  33.5 2.3 %collective-permute-start.1 = (bf16[24,2176]{1,0:T(8,128)(2,1)S(1)}, bf16[24,2176]{1,0:T(8,128)(2,1)S(1)}, u32[]{:S(2)}, u32[]{:S(2)}) collective-permute-start(bf16[24,2176]{1,0:T(8,128)(2,1)S(1)} %maximum_select_fusion.2), channel_id=1, source_target_pairs={{0,1},{1,0},{2,3},{3,2},{4,5},{5,4},{6,7},{7,6},{8,9},{9,8},{10,11... | collective-permute-start | bytes 313352 | tf_op jit(solution)/shard_map/ppermute | solution.py:38
  35.8 5.5 %collective-permute-done.1 = bf16[24,2176]{1,0:T(8,128)(2,1)S(1)} collective-permute-done((bf16[24,2176]{1,0:T(8,128)(2,1)S(1)}, bf16[24,2176]{1,0:T(8,128)(2,1)S(1)}, u32[]{:S(2)}, u32[]{:S(2)}) %collective-permute-start.1) | collective-permute-done | bytes 104480 | tf_op jit(solution)/shard_map/ppermute | solution.py:38
  41.4 8.2 %collective-permute-start.2 = (bf16[48,2176]{1,0:T(8,128)(2,1)S(1)}, bf16[48,2176]{1,0:T(8,128)(2,1)S(1)}, u32[]{:S(2)}, u32[]{:S(2)}) collective-permute-start(bf16[48,2176]{1,0:T(8,128)(2,1)S(1)} %bitcast.53), channel_id=1, source_target_pairs={{0,2},{2,4},{4,6},{6,8},{8,10},{10,12},{12,14},{14,0},{1,3},{3,5},... | collective-permute-start | bytes 626696 | tf_op jit(solution)/shard_map/ppermute | solution.py:223
  49.6 8.9 %collective-permute-start.3 = (bf16[48,2176]{1,0:T(8,128)(2,1)S(1)}, bf16[48,2176]{1,0:T(8,128)(2,1)S(1)}, u32[]{:S(2)}, u32[]{:S(2)}) collective-permute-start(bf16[48,2176]{1,0:T(8,128)(2,1)S(1)} %bitcast.54), channel_id=1, source_target_pairs={{0,14},{2,0},{4,2},{6,4},{8,6},{10,8},{12,10},{14,12},{1,15},{3,1}... | collective-permute-start | bytes 626696 | tf_op jit(solution)/shard_map/ppermute | solution.py:223
  59.2 1.7 collective-permute-done.2.r1
  61.9 4.4 %collective-permute-start.12 = (bf16[576,512]{1,0:T(8,128)(2,1)S(1)}, bf16[576,512]{1,0:T(8,128)(2,1)S(1)}, u32[]{:S(2)}, u32[]{:S(2)}) collective-permute-start(bf16[576,512]{1,0:T(8,128)(2,1)S(1)} %constant_dynamic-update-slice_fusion.s0), channel_id=1, source_target_pairs={{32,0},{64,32},{96,64},{0,96},{33,1},{65,33},{97,65},{1,97},{34,2}... | collective-permute-start | bytes 1769480 | tf_op jit(solution)/shard_map/ppermute | solution.py:228
  66.3 2.4 %collective-permute-start.13 = (bf16[576,512]{1,0:T(8,128)(2,1)S(1)}, bf16[576,512]{1,0:T(8,128)(2,1)S(1)}, u32[]{:S(2)}, u32[]{:S(2)}) collective-permute-start(bf16[576,512]{1,0:T(8,128)(2,1)S(1)} %constant_dynamic-update-slice_fusion.s0), channel_id=1, source_target_pairs={{64,0},{96,32},{0,64},{32,96},{65,1},{97,33},{1,65},{33,97},{66,2}... | collective-permute-start | bytes 1769480 | tf_op jit(solution)/shard_map/ppermute | solution.py:228
  68.8 2.5 %collective-permute-start.14 = (bf16[576,512]{1,0:T(8,128)(2,1)S(1)}, bf16[576,512]{1,0:T(8,128)(2,1)S(1)}, u32[]{:S(2)}, u32[]{:S(2)}) collective-permute-start(bf16[576,512]{1,0:T(8,128)(2,1)S(1)} %constant_dynamic-update-slice_fusion.s0), channel_id=1, source_target_pairs={{96,0},{0,32},{32,64},{64,96},{97,1},{1,33},{33,65},{65,97},{98,2}... | collective-permute-start | bytes 1769480 | tf_op jit(solution)/shard_map/ppermute | solution.py:228
  71.3 1.9 collective-permute-start.7
  75.8 5.3 %collective-permute-start.8 = (bf16[48,2176]{1,0:T(8,128)(2,1)S(1)}, bf16[48,2176]{1,0:T(8,128)(2,1)}, u32[]{:S(2)}, u32[]{:S(2)}) collective-permute-start(bf16[48,2176]{1,0:T(8,128)(2,1)S(1)} %collective-permute-done.3.l1), channel_id=1, source_target_pairs={{0,14},{2,0},{4,2},{6,4},{8,6},{10,8},{12,10},{14,12},{1,15},{3,1}... | collective-permute-start | bytes 626696 | tf_op jit(solution)/shard_map/ppermute | solution.py:223
  81.2 1.9 collective-permute-start.9
  84.3 5.0 %collective-permute-start.10 = (bf16[48,2176]{1,0:T(8,128)(2,1)}, bf16[48,2176]{1,0:T(8,128)(2,1)}, u32[]{:S(2)}, u32[]{:S(2)}) collective-permute-start(bf16[48,2176]{1,0:T(8,128)(2,1)} %collective-permute-done.8.l2), channel_id=1, source_target_pairs={{0,14},{2,0},{4,2},{6,4},{8,6},{10,8},{12,10},{14,12},{1,15},{3,1}... | collective-permute-start | bytes 626696 | tf_op jit(solution)/shard_map/ppermute | solution.py:223
  89.5 1.9 collective-permute-start.11
  93.5 2.4 %collective-permute-done.13.s2 = bf16[576,512]{1,0:T(8,128)(2,1)S(1)} collective-permute-done((bf16[576,512]{1,0:T(8,128)(2,1)S(1)}, bf16[576,512]{1,0:T(8,128)(2,1)S(1)}, u32[]{:S(2)}, u32[]{:S(2)}) %collective-permute-start.13) | collective-permute-done | bytes 589856 | tf_op jit(solution)/shard_map/ppermute | solution.py:228
  97.3 15.4 %collective-permute-done.14.s3 = bf16[576,512]{1,0:T(8,128)(2,1)S(1)} collective-permute-done((bf16[576,512]{1,0:T(8,128)(2,1)S(1)}, bf16[576,512]{1,0:T(8,128)(2,1)S(1)}, u32[]{:S(2)}, u32[]{:S(2)}) %collective-permute-start.14) | collective-permute-done | bytes 589856 | tf_op jit(solution)/shard_map/ppermute | solution.py:228
  114.2 5.8 %shard_map.94 = (f32[384,640]{1,0:T(8,128)}, bf16[384,2176]{1,0:T(8,128)(2,1)}) custom-call(s32[4]{0:T(128)} %pad_add_fusion.place, bf16[2048,128]{1,0:T(8,128)(2,1)} %pad.17.down, bf16[48,2176]{1,0:T(8,128)(2,1)} %bitcast.55, bf16[48,2176]{1,0:T(8,128)(2,1)} %copy-done.10, bf16[48,2176]{1,0:T(8,128)(2,1)} %copy-done.11, ...), custom_call_target="tpu_custom_call" | custom-call | flops 1006632960 | bytes 10000000 | tf_op jit(solution)/shard_map/pallas_call | solution.py:210
  122.4 5.1 %collective-permute-start.15 = (f32[192,640]{1,0:T(8,128)S(1)}, f32[192,640]{1,0:T(8,128)S(1)}, u32[]{:S(2)}, u32[]{:S(2)}) collective-permute-start(f32[192,640]{1,0:T(8,128)S(1)} %slice_select_fusion), channel_id=1, source_target_pairs={{0,16},{16,0},{1,17},{17,1},{2,18},{18,2},{3,19},{19,3},{4,20},{20... | collective-permute-start | bytes 1474568 | tf_op jit(solution)/shard_map/ppermute | solution.py:282
  129.1 5.8 %shard_map.96 = f32[192,1280]{1,0:T(8,128)} custom-call(s32[4]{0:T(128)} %pad_add_fusion.place, bf16[384,2176]{1,0:T(8,128)(2,1)} %get-tuple-element.30.tok.tok_in, bf16[2048,1280]{1,0:T(8,128)(2,1)} %all-gather.2.cloned.1.call-done.w_in), custom_call_target="tpu_custom_call" | custom-call | flops 1006632960 | bytes 10000000 | tf_op jit(solution)/shard_map/pallas_call | solution.py:210
  134.9 2.3 %collective-permute-start.16 = (f32[192,1280]{1,0:T(8,128)}, f32[192,1280]{1,0:T(8,128)S(1)}, u32[]{:S(2)}, u32[]{:S(2)}) collective-permute-start(f32[192,1280]{1,0:T(8,128)} %shard_map.96), channel_id=1, source_target_pairs={{0,16},{16,0},{1,17},{17,1},{2,18},{18,2},{3,19},{19,3},{4,20},{20... | collective-permute-start | bytes 2949128 | tf_op jit(solution)/shard_map/ppermute | solution.py:301
  137.2 5.7 %shard_map.95.near = f32[192,1280]{1,0:T(8,128)} custom-call(s32[4]{0:T(128)} %pad_add_fusion.place, bf16[384,2176]{1,0:T(8,128)(2,1)} %get-tuple-element.30.tok.tok_in, bf16[2048,1280]{1,0:T(8,128)(2,1)} %all-gather.2.cloned.1.call-done.w_in), custom_call_target="tpu_custom_call" | custom-call | flops 1006632960 | bytes 10000000 | tf_op jit(solution)/shard_map/pallas_call | solution.py:210
  143.0 1.3 copy-done.1
  144.3 3.7 %shard_map.97 = (f32[32,5,128]{2,1,0:T(8,128)S(1)}, f32[32,192]{1,0:T(8,128)S(1)}, bf16[4,192,896]{2,1,0:T(8,128)(2,1)S(1)}) custom-call(s32[4]{0:T(128)S(1)} %copy-done.2, f32[192,1280]{1,0:T(8,128)S(1)} %copy-done.1, f32[192,1280]{1,0:T(8,128)S(1)} %collective-permute-done.16.partner, f32[192,640]{1,0:T(8,128)S(1)} %select_add_fusion.side, ...), custom_call_target="tpu_custom_call" | custom-call | flops 176160768 | bytes 10000000 | tf_op jit(solution)/shard_map/pallas_call | solution.py:210
  148.0 17.4 %all_to_all.15.arrived = f32[32,5,128]{2,1,0:T(8,128)S(1)} all-to-all(f32[32,5,128]{2,1,0:T(8,128)S(1)} %get-tuple-element.39), channel_id=1, replica_groups=mesh['yh'=4,'x'=4,'c'=2,'z'=8,'yl'=2] {'c','z','yl'}, dimensions={0} | all-to-all | bytes 163840 | tf_op jit(solution)/shard_map/all_to_all | solution.py:311
  165.4 2.8 %shard_map.98 = (f32[32,10,128]{2,1,0:T(8,128)}, f32[8,128]{1,0:T(8,128)S(1)}) custom-call(s32[4]{0:T(128)S(1)} %copy-done.2, f32[32,5,128]{2,1,0:T(8,128)S(1)} %all_to_all.15.arrived, bf16[2,128,192]{2,1,0:T(8,128)(2,1)S(1)} %fusion.7.signs, f32[2,1,128]{2,1,0:T(1,128)S(1)} %bitcast.50, f32[32,192]{1,0:T(8,128)S(1)} %get-tuple-element.41.low_t, ...), custom_call_target="tpu_custom_call" | custom-call | flops 12582912 | bytes 10000000 | tf_op jit(solution)/shard_map/pallas_call | solution.py:210
  168.3 7.8 %all-to-all-start.1 = ((f32[32,10,128]{2,1,0:T(8,128)}), f32[32,10,128]{2,1,0:T(8,128)S(1)}, u32[]{:S(2)}, u32[]{:S(2)}) async-start(f32[32,10,128]{2,1,0:T(8,128)} %get-tuple-element.43), calls=%async_computation.1 | async-start | bytes 524288 | tf_op jit(solution)/shard_map/all_to_all | solution.py:325
  176.7 13.1 %all-to-all-done.1 = f32[32,10,128]{2,1,0:T(8,128)S(1)} async-done(((f32[32,10,128]{2,1,0:T(8,128)}), f32[32,10,128]{2,1,0:T(8,128)S(1)}, u32[]{:S(2)}, u32[]{:S(2)}) %all-to-all-start.1) | async-done | bytes 163872 | tf_op jit(solution)/shard_map/all_to_all | solution.py:325
  190.4 3.5 %all-to-all-start.2 = ((f32[16,2,128]{2,1,0:T(2,128)}), f32[16,2,128]{2,1,0:T(2,128)S(1)}, u32[]{:S(2)}, u32[]{:S(2)}) async-start(f32[16,2,128]{2,1,0:T(2,128)} %broadcast_in_dim.27), calls=%async_computation.2 | async-start | bytes 32768 | tf_op jit(solution)/shard_map/all_to_all | solution.py:326
  196.4 4.9 %all-to-all-done.2 = f32[16,2,128]{2,1,0:T(2,128)S(1)} async-done(((f32[16,2,128]{2,1,0:T(2,128)}), f32[16,2,128]{2,1,0:T(2,128)S(1)}, u32[]{:S(2)}, u32[]{:S(2)}) %all-to-all-start.2) | async-done | bytes 16416 | tf_op jit(solution)/shard_map/all_to_all | solution.py:326
  (103 shorter events, 20.5 us)
Async XLA Ops:
  7.2 21.1 %copy-start.12 = (bf16[12,4096]{1,0:T(8,128)(2,1)S(1)}, bf16[12,4096]{1,0:T(8,128)(2,1)}, u32[]{:S(2)}) copy-start(bf16[12,4096]{1,0:T(8,128)(2,1)} %param.7) | copy-start | bytes 294916
  7.2 24.9 %copy-start.9 = (bf16[4096,32]{0,1:T(8,128)(2,1)S(1)}, bf16[4096,32]{0,1:T(8,128)(2,1)}, u32[]{:S(2)}) copy-start(bf16[4096,32]{0,1:T(8,128)(2,1)} %param.11) | copy-start | bytes 786436
  7.2 121.9 %all-gather.2.cloned.1.call-start = ((), (), s32[]{:S(2)}) async-start(), calls=%async_computation.3 | async-start | bytes 5570560 | tf_op jit(solution)/shard_map/all_gather | solution.py:237
  13.8 45.4 %collective-permute-start.4 = (bf16[144,512]{1,0:T(8,128)(2,1)S(1)}, bf16[144,512]{1,0:T(8,128)(2,1)S(1)}, u32[]{:S(2)}, u32[]{:S(2)}) collective-permute-start(bf16[144,512]{1,0:T(8,128)(2,1)S(1)} %fusion.6), channel_id=1, source_target_pairs={{128,0},{256,128},{384,256},{0,384},{129,1},{257,129},{385,257},{1... | collective-permute-start | bytes 442376 | tf_op jit(solution)/shard_map/ppermute | solution.py:228
  20.5 38.7 %collective-permute-start.5 = (bf16[144,512]{1,0:T(8,128)(2,1)S(1)}, bf16[144,512]{1,0:T(8,128)(2,1)S(1)}, u32[]{:S(2)}, u32[]{:S(2)}) collective-permute-start(bf16[144,512]{1,0:T(8,128)(2,1)S(1)} %fusion.6), channel_id=1, source_target_pairs={{256,0},{384,128},{0,256},{128,384},{257,1},{385,129},{1,257},{129... | collective-permute-start | bytes 442376 | tf_op jit(solution)/shard_map/ppermute | solution.py:228
  24.1 35.2 %collective-permute-start.6 = (bf16[144,512]{1,0:T(8,128)(2,1)S(1)}, bf16[144,512]{1,0:T(8,128)(2,1)S(1)}, u32[]{:S(2)}, u32[]{:S(2)}) collective-permute-start(bf16[144,512]{1,0:T(8,128)(2,1)S(1)} %fusion.6), channel_id=1, source_target_pairs={{384,0},{0,128},{128,256},{256,384},{385,1},{1,129},{129,257},{257... | collective-permute-start | bytes 442376 | tf_op jit(solution)/shard_map/ppermute | solution.py:228
  28.7 4.7 %collective-permute-start = (bf16[12,2176]{1,0:T(8,128)(2,1)S(1)}, bf16[12,2176]{1,0:T(8,128)(2,1)S(1)}, u32[]{:S(2)}, u32[]{:S(2)}) collective-permute-start(bf16[12,2176]{1,0:T(8,128)(2,1)S(1)} %get-tuple-element.63), channel_id=1, source_target_pairs={{0,16},{16,0},{1,17},{17,1},{2,18},{18,2},{3,19},{19,3},{4,20},{20... | collective-permute-start | bytes 156680 | tf_op jit(solution)/shard_map/ppermute | solution.py:243
  33.0 25.6 %copy-start.13 = (bf16[32,896]{1,0:T(8,128)(2,1)S(1)}, bf16[32,896]{1,0:T(8,128)(2,1)}, u32[]{:S(2)}) copy-start(bf16[32,896]{1,0:T(8,128)(2,1)} %param.12) | copy-start | bytes 172036
  33.5 7.9 %collective-permute-start.1 = (bf16[24,2176]{1,0:T(8,128)(2,1)S(1)}, bf16[24,2176]{1,0:T(8,128)(2,1)S(1)}, u32[]{:S(2)}, u32[]{:S(2)}) collective-permute-start(bf16[24,2176]{1,0:T(8,128)(2,1)S(1)} %maximum_select_fusion.2), channel_id=1, source_target_pairs={{0,1},{1,0},{2,3},{3,2},{4,5},{5,4},{6,7},{7,6},{8,9},{9,8},{10,11... | collective-permute-start | bytes 313352 | tf_op jit(solution)/shard_map/ppermute | solution.py:38
  41.4 34.4 %copy-start.14 = (bf16[896]{0:T(1024)(128)(2,1)S(1)}, bf16[896]{0:T(1024)(128)(2,1)}, u32[]{:S(2)}) copy-start(bf16[896]{0:T(1024)(128)(2,1)} %param.13) | copy-start | bytes 5380
  41.4 72.7 %copy-start.5 = (bf16[2,24,2176]{2,1,0:T(8,128)(2,1)}, bf16[2,24,2176]{2,1,0:T(8,128)(2,1)S(1)}, u32[]{:S(2)}) copy-start(bf16[2,24,2176]{2,1,0:T(8,128)(2,1)S(1)} %maximum_select_fusion) | copy-start | bytes 626692
  41.4 19.5 %collective-permute-start.2 = (bf16[48,2176]{1,0:T(8,128)(2,1)S(1)}, bf16[48,2176]{1,0:T(8,128)(2,1)S(1)}, u32[]{:S(2)}, u32[]{:S(2)}) collective-permute-start(bf16[48,2176]{1,0:T(8,128)(2,1)S(1)} %bitcast.53), channel_id=1, source_target_pairs={{0,2},{2,4},{4,6},{6,8},{8,10},{10,12},{12,14},{14,0},{1,3},{3,5},... | collective-permute-start | bytes 626696 | tf_op jit(solution)/shard_map/ppermute | solution.py:223
  49.6 12.2 %collective-permute-start.3 = (bf16[48,2176]{1,0:T(8,128)(2,1)S(1)}, bf16[48,2176]{1,0:T(8,128)(2,1)S(1)}, u32[]{:S(2)}, u32[]{:S(2)}) collective-permute-start(bf16[48,2176]{1,0:T(8,128)(2,1)S(1)} %bitcast.54), channel_id=1, source_target_pairs={{0,14},{2,0},{4,2},{6,4},{8,6},{10,8},{12,10},{14,12},{1,15},{3,1}... | collective-permute-start | bytes 626696 | tf_op jit(solution)/shard_map/ppermute | solution.py:223
  61.0 53.1 %copy-start.10 = (bf16[48,2176]{1,0:T(8,128)(2,1)}, bf16[48,2176]{1,0:T(8,128)(2,1)S(1)}, u32[]{:S(2)}) copy-start(bf16[48,2176]{1,0:T(8,128)(2,1)S(1)} %collective-permute-done.2.r1) | copy-start | bytes 626692
  61.8 52.3 %copy-start.11 = (bf16[48,2176]{1,0:T(8,128)(2,1)}, bf16[48,2176]{1,0:T(8,128)(2,1)S(1)}, u32[]{:S(2)}) copy-start(bf16[48,2176]{1,0:T(8,128)(2,1)S(1)} %collective-permute-done.3.l1) | copy-start | bytes 626692
  61.9 52.2 %copy-start.4 = (bf16[576,512]{1,0:T(8,128)(2,1)}, bf16[576,512]{1,0:T(8,128)(2,1)S(1)}, u32[]{:S(2)}) copy-start(bf16[576,512]{1,0:T(8,128)(2,1)S(1)} %constant_dynamic-update-slice_fusion.s0) | copy-start | bytes 1769476
  61.9 29.5 %collective-permute-start.12 = (bf16[576,512]{1,0:T(8,128)(2,1)S(1)}, bf16[576,512]{1,0:T(8,128)(2,1)S(1)}, u32[]{:S(2)}, u32[]{:S(2)}) collective-permute-start(bf16[576,512]{1,0:T(8,128)(2,1)S(1)} %constant_dynamic-update-slice_fusion.s0), channel_id=1, source_target_pairs={{32,0},{64,32},{96,64},{0,96},{33,1},{65,33},{97,65},{1,97},{34,2}... | collective-permute-start | bytes 1769480 | tf_op jit(solution)/shard_map/ppermute | solution.py:228
  66.3 29.6 %collective-permute-start.13 = (bf16[576,512]{1,0:T(8,128)(2,1)S(1)}, bf16[576,512]{1,0:T(8,128)(2,1)S(1)}, u32[]{:S(2)}, u32[]{:S(2)}) collective-permute-start(bf16[576,512]{1,0:T(8,128)(2,1)S(1)} %constant_dynamic-update-slice_fusion.s0), channel_id=1, source_target_pairs={{64,0},{96,32},{0,64},{32,96},{65,1},{97,33},{1,65},{33,97},{66,2}... | collective-permute-start | bytes 1769480 | tf_op jit(solution)/shard_map/ppermute | solution.py:228
  68.8 43.9 %collective-permute-start.14 = (bf16[576,512]{1,0:T(8,128)(2,1)S(1)}, bf16[576,512]{1,0:T(8,128)(2,1)S(1)}, u32[]{:S(2)}, u32[]{:S(2)}) collective-permute-start(bf16[576,512]{1,0:T(8,128)(2,1)S(1)} %constant_dynamic-update-slice_fusion.s0), channel_id=1, source_target_pairs={{96,0},{0,32},{32,64},{64,96},{97,1},{1,33},{33,65},{65,97},{98,2}... | collective-permute-start | bytes 1769480 | tf_op jit(solution)/shard_map/ppermute | solution.py:228
  71.3 9.9 %collective-permute-start.7 = (bf16[48,2176]{1,0:T(8,128)(2,1)S(1)}, bf16[48,2176]{1,0:T(8,128)(2,1)}, u32[]{:S(2)}, u32[]{:S(2)}) collective-permute-start(bf16[48,2176]{1,0:T(8,128)(2,1)S(1)} %collective-permute-done.2.r1), channel_id=1, source_target_pairs={{0,2},{2,4},{4,6},{6,8},{8,10},{10,12},{12,14},{14,0},{1,3},{3,5},... | collective-permute-start | bytes 626696 | tf_op jit(solution)/shard_map/ppermute | solution.py:223
  75.8 8.5 %collective-permute-start.8 = (bf16[48,2176]{1,0:T(8,128)(2,1)S(1)}, bf16[48,2176]{1,0:T(8,128)(2,1)}, u32[]{:S(2)}, u32[]{:S(2)}) collective-permute-start(bf16[48,2176]{1,0:T(8,128)(2,1)S(1)} %collective-permute-done.3.l1), channel_id=1, source_target_pairs={{0,14},{2,0},{4,2},{6,4},{8,6},{10,8},{12,10},{14,12},{1,15},{3,1}... | collective-permute-start | bytes 626696 | tf_op jit(solution)/shard_map/ppermute | solution.py:223
  81.2 8.4 %collective-permute-start.9 = (bf16[48,2176]{1,0:T(8,128)(2,1)}, bf16[48,2176]{1,0:T(8,128)(2,1)}, u32[]{:S(2)}, u32[]{:S(2)}) collective-permute-start(bf16[48,2176]{1,0:T(8,128)(2,1)} %collective-permute-done.7.r2), channel_id=1, source_target_pairs={{0,2},{2,4},{4,6},{6,8},{8,10},{10,12},{12,14},{14,0},{1,3},{3,5},... | collective-permute-start | bytes 626696 | tf_op jit(solution)/shard_map/ppermute | solution.py:223
  84.3 29.8 %collective-permute-start.10 = (bf16[48,2176]{1,0:T(8,128)(2,1)}, bf16[48,2176]{1,0:T(8,128)(2,1)}, u32[]{:S(2)}, u32[]{:S(2)}) collective-permute-start(bf16[48,2176]{1,0:T(8,128)(2,1)} %collective-permute-done.8.l2), channel_id=1, source_target_pairs={{0,14},{2,0},{4,2},{6,4},{8,6},{10,8},{12,10},{14,12},{1,15},{3,1}... | collective-permute-start | bytes 626696 | tf_op jit(solution)/shard_map/ppermute | solution.py:223
  89.5 24.5 %collective-permute-start.11 = (bf16[48,2176]{1,0:T(8,128)(2,1)}, bf16[48,2176]{1,0:T(8,128)(2,1)}, u32[]{:S(2)}, u32[]{:S(2)}) collective-permute-start(bf16[48,2176]{1,0:T(8,128)(2,1)} %collective-permute-done.9.r3), channel_id=1, source_target_pairs={{0,2},{2,4},{4,6},{6,8},{8,10},{10,12},{12,14},{14,0},{1,3},{3,5},... | collective-permute-start | bytes 626696 | tf_op jit(solution)/shard_map/ppermute | solution.py:223
  91.5 22.7 %copy-start.6 = (bf16[576,512]{1,0:T(8,128)(2,1)}, bf16[576,512]{1,0:T(8,128)(2,1)S(1)}, u32[]{:S(2)}) copy-start(bf16[576,512]{1,0:T(8,128)(2,1)S(1)} %collective-permute-done.12.s1) | copy-start | bytes 1769476
  95.9 18.2 %copy-start.7 = (bf16[576,512]{1,0:T(8,128)(2,1)}, bf16[576,512]{1,0:T(8,128)(2,1)S(1)}, u32[]{:S(2)}) copy-start(bf16[576,512]{1,0:T(8,128)(2,1)S(1)} %collective-permute-done.13.s2) | copy-start | bytes 1769476
  119.9 9.1 %copy-start.3 = (f32[384,640]{1,0:T(8,128)S(1)}, f32[384,640]{1,0:T(8,128)}, u32[]{:S(2)}) copy-start(f32[384,640]{1,0:T(8,128)} %get-tuple-element.31) | copy-start | bytes 2949124
  122.4 6.6 %collective-permute-start.15 = (f32[192,640]{1,0:T(8,128)S(1)}, f32[192,640]{1,0:T(8,128)S(1)}, u32[]{:S(2)}, u32[]{:S(2)}) collective-permute-start(f32[192,640]{1,0:T(8,128)S(1)} %slice_select_fusion), channel_id=1, source_target_pairs={{0,16},{16,0},{1,17},{17,1},{2,18},{18,2},{3,19},{19,3},{4,20},{20... | collective-permute-start | bytes 1474568 | tf_op jit(solution)/shard_map/ppermute | solution.py:282
  134.9 8.0 %collective-permute-start.16 = (f32[192,1280]{1,0:T(8,128)}, f32[192,1280]{1,0:T(8,128)S(1)}, u32[]{:S(2)}, u32[]{:S(2)}) collective-permute-start(f32[192,1280]{1,0:T(8,128)} %shard_map.96), channel_id=1, source_target_pairs={{0,16},{16,0},{1,17},{17,1},{2,18},{18,2},{3,19},{19,3},{4,20},{20... | collective-permute-start | bytes 2949128 | tf_op jit(solution)/shard_map/ppermute | solution.py:301
  142.9 22.5 %copy-start = (bf16[384,2176]{1,0:T(8,128)(2,1)S(1)}, bf16[384,2176]{1,0:T(8,128)(2,1)}, u32[]{:S(2)}) copy-start(bf16[384,2176]{1,0:T(8,128)(2,1)} %get-tuple-element.30.tok.tok_in) | copy-start | bytes 5013508
  168.3 21.5 %all-to-all-start.1 = ((f32[32,10,128]{2,1,0:T(8,128)}), f32[32,10,128]{2,1,0:T(8,128)S(1)}, u32[]{:S(2)}, u32[]{:S(2)}) async-start(f32[32,10,128]{2,1,0:T(8,128)} %get-tuple-element.43), calls=%async_computation.1 | async-start | bytes 524288 | tf_op jit(solution)/shard_map/all_to_all | solution.py:325
  190.4 10.9 %all-to-all-start.2 = ((f32[16,2,128]{2,1,0:T(2,128)}), f32[16,2,128]{2,1,0:T(2,128)S(1)}, u32[]{:S(2)}, u32[]{:S(2)}) async-start(f32[16,2,128]{2,1,0:T(2,128)} %broadcast_in_dim.27), calls=%async_computation.2 | async-start | bytes 32768 | tf_op jit(solution)/shard_map/all_to_all | solution.py:326
  (3 other events, 10.8 us)
Sparse Core Ops, SparseCore 0:
  11.0 108.1 all-gather.1

commit v9 on v8

--- a/solution.py
+++ b/solution.py
@@ -29,6 +29,7 @@
 MAIN = 640
 SIDE = UNITS - MAIN
 PIECE = SLICE + 16
+COLUMNS = 512
 GROUP = 192
 BLOCKS = GROUP // ROWS
 CONTRACT_LAST = (((1,), (1,)), ((), ()))
@@ -79,36 +80,44 @@
     tok_copy.wait()
 
 
-def main_products(far, place, tok, w_in, out, rows, w, sems):
-    half = 1 - place[0] if far else place[0]
-    mine = pl.ds(pl.multiple_of(half * GROUP, GROUP), GROUP)
-    parts = [pl.ds(n * 256, 256) for n in range(2 * MAIN // 256)]
-    rows_copy = pltpu.make_async_copy(tok.at[mine, pl.ds(0, HALF)], rows, sems.at[0])
-    rows_copy.start()
+def main_products(place, tok, w_in, far, near, rows, w, sems):
+    halves = [
+        pl.ds(pl.multiple_of(half * GROUP, GROUP), GROUP) for half in (1 - place[0], place[0])
+    ]
+    chunks = [pl.ds(n * COLUMNS, COLUMNS) for n in range(HALF // COLUMNS)]
+    row_copies = [
+        pltpu.make_async_copy(tok.at[half, pl.ds(0, HALF)], rows.at[n], sems.at[n]) for n, half in enumerate(halves)
+    ]
     copies = [
-        pltpu.make_async_copy(w_in.at[:, part], w.at[:, part], sems.at[1 + n]) for n, part in enumerate(parts)
+        pltpu.make_async_copy(w_in.at[chunk, :], w.at[chunk, :], sems.at[2 + n]) for n, chunk in enumerate(chunks)
     ]
-    for copy in copies:
+    row_copies[0].start()
+    copies[0].start()
+    row_copies[1].start()
+    for copy in copies[1:]:
         copy.start()
-    rows_copy.wait()
-    for part, copy in zip(parts, copies):
+    for copy in row_copies:
         copy.wait()
-        out[:, part] = dot(rows[...], w[:, part])
-
-
-def products(far, place, tok, w):
+    for n, (chunk, copy) in enumerate(zip(chunks, copies)):
+        copy.wait()
+        for at, out in enumerate((far, near)):
+            term = dot(rows[at, :, chunk], w[chunk, :])
+            out[...] = term if n == 0 else out[...] + term
+
+
+def products(place, tok, w):
     return kernel(
-        functools.partial(main_products, far),
-        [((GROUP, 2 * MAIN), F32)],
+        main_products,
+        [((GROUP, 2 * MAIN), F32)] * 2,
         (place, tok, w),
-        2 * GROUP * HALF * 2 * MAIN, 56,
+        4 * GROUP * HALF * 2 * MAIN, 56,
         scratch=[
-            pltpu.VMEM((GROUP, HALF), BF16),
+            pltpu.VMEM((2, GROUP, HALF), BF16),
             pltpu.VMEM((HALF, 2 * MAIN), BF16),
-            pltpu.SemaphoreType.DMA((6,)),
+            pltpu.SemaphoreType.DMA((2 + HALF // COLUMNS,)),
         ],
         in_hbm=2,
-    )[0]
+    )
 
 
 def score(place, near, partner, side, b_gate, b_up, readout, signs, count, message, low_t, k_out, k, sems):
@@ -141,14 +150,12 @@
     copies[2].start()
     copies[3].start()
     mixed_up = dot(b_up[RANK : 2 * RANK, :], high, CONTRACT_LAST) + dot(b_up[RANK : 2 * RANK, :], rest, CONTRACT_LAST)
+    message[...] = jnp.zeros_like(message)
     for core in range(2):
         lines = slice(RANK * core, RANK * (core + 1))
         for i, value in enumerate((mixed, mixed_up)):
-            message[lines, 2 * i, :] = value[:, 0:LANES]
-            message[lines, 2 * i + 1, :] = jnp.concatenate(
-                [value[:, LANES:], jnp.zeros((RANK, 2 * LANES - GROUP), F32)], axis=1
-            )
-        message[lines, 4, :] = tail
+            message[lines, 0, 2 * i * LANES : 2 * i * LANES + GROUP] = value
+        message[lines, 0, 4 * LANES :] = tail
     low_t[...] = low_b.astype(F32).T[0 : 2 * RANK, :]
     for copy in copies:
         copy.wait()
@@ -161,7 +168,7 @@
     k_copy.start()
     core = place[0]
     sums = [jnp.sum(arrived[RANK * h : RANK * (h + 1)], axis=0) for h in range(2)]
-    tails = [total[4:5, :] for total in sums]
+    tails = [total[:, 4 * LANES :] for total in sums]
     line = lax.broadcasted_iota(jnp.int32, (8, GROUP), 0)
     pair_total = jnp.maximum(tails[0][:, 64:65] + tails[1][:, 64:65], 1.0)
     logs, cotangents, terms = 0.0, [], []
@@ -174,9 +181,7 @@
         scaled = jnp.broadcast_to(scaled, (8, LANES))
         cotangent = sum(dot(part, signs[h]) for part in split(scaled, 3))
         cotangents.append(cotangent[0:1, :])
-        gate, up = (
-            jnp.concatenate([sums[h][i : i + 1, :], sums[h][i + 1 : i + 2, 0 : GROUP - LANES]], axis=1) for i in (0, 2)
-        )
+        gate, up = (sums[h][:, i * LANES : i * LANES + GROUP] for i in (0, 2))
         projected = jnp.where(line == 0, gate, jnp.where(line == 1, up, 0.0)) * cotangent
         if h == 0:
             tok_copy.wait()
@@ -187,9 +192,8 @@
     k_copy.wait()
     gate = dot(high[0:RANK], k[0]) + dot(high[0:RANK], k[1]) + dot(rest[0:RANK], k[0])
     up = dot(high[RANK:], k[2]) + dot(high[RANK:], k[3]) + dot(rest[RANK:], k[2])
-    for i in range(UNITS // LANES):
-        out[0:RANK, i, :] = gate[:, i * LANES : (i + 1) * LANES]
-        out[RANK : 2 * RANK, i, :] = up[:, i * LANES : (i + 1) * LANES]
+    out[0:RANK, 0, 0:UNITS] = gate
+    out[RANK : 2 * RANK, 0, 0:UNITS] = up
     line = lax.broadcasted_iota(jnp.int32, (2 * RANK, SLICE), 0)
     for column in range(2):
         slices = jnp.zeros((2 * RANK, SLICE), F32)
@@ -198,8 +202,8 @@
                 grad_a[column : column + 1, i * SLICE : (i + 1) * SLICE], (2 * RANK, SLICE)
             )
             slices = jnp.where(line == 2 * i + core, here, slices)
-        out[:, 7 + column, :] = slices
-    out[:, 9, :] = jnp.broadcast_to(0.5 * logs, (2 * RANK, LANES))
+        out[:, 0, UNITS + column * SLICE : UNITS + (column + 1) * SLICE] = slices
+    out[:, 0, UNITS + 2 * SLICE :] = jnp.broadcast_to(0.5 * logs, (2 * RANK, LANES))
     total_out[...] = jnp.broadcast_to(pair_total, (8, LANES))
 
 
@@ -245,20 +249,19 @@
         core == 0, jnp.concatenate([keep, take], axis=0), jnp.concatenate([take, keep], axis=0)
     )
     four = swapped(pair, "yl", yl).reshape(4 * ROWS, HALF + LANES)
-    ring = [four, along(four, "z", 1), along(four, "z", -1)]
-
     has = [jnp.max((code == q).astype(F32)) for q in range(SEQS)]
     count_rows = jnp.broadcast_to((has[0] * has[1] + has[2] * has[3]).astype(BF16), (16, 2 * SIDE))
     piece = jnp.concatenate(
         [jnp.concatenate([frozen[0, :, MAIN:], frozen[1, :, MAIN:]], axis=1), count_rows], axis=0
     )
     pieces = [piece] + [fetch(piece, "yh", k) for k in (1, 2, 3)]
-    ring[1], ring[2], *pieces = lax.optimization_barrier((ring[1], ring[2], *pieces))
+    four, *pieces = lax.optimization_barrier((four, *pieces))
+    ring = [four, along(four, "z", 1), along(four, "z", -1)]
     stack = jnp.concatenate(pieces, axis=0)
     stacks = [stack] + [fetch(stack, "x", j) for j in (1, 2, 3)]
     for step in range(2):
         ring += [along(ring[-2], "z", 1), along(ring[-1], "z", -1)]
-    ring.append(along(ring[-2], "z", 1))
+    ring.append(along(four, "z", 4))
     count = sum(jnp.sum(p.reshape(4, PIECE, 2 * SIDE)[:, SLICE, 0].astype(F32)) for p in stacks)
     count_lanes = jnp.where(jnp.arange(LANES) == 64, count, 0.0).reshape(1, LANES)
 
@@ -297,12 +300,11 @@
     w_main, side, b_gate, b_up, read, signs, valid, count_lanes = lax.optimization_barrier(
         (w_main, side, b_gate, b_up, read, signs, valid, count_lanes)
     )
-    far = products(True, place, tok, w_main)
+    far, near = products(place, tok, w_main)
     partner = lax.ppermute(far, "c", SWAP)
-    near = products(False, place, tok, w_main)
     message, low_t, k = kernel(
         score,
-        [((2 * RANK, 5, LANES), F32), ((2 * RANK, GROUP), F32), ((4, GROUP, UNITS), BF16)],
+        [((2 * RANK, 1, 5 * LANES), F32), ((2 * RANK, GROUP), F32), ((4, GROUP, UNITS), BF16)],
         (place, near, partner, side, b_gate, b_up, read, signs, count_lanes),
         8 * GROUP * UNITS * LANES, 16,
         scratch=[pltpu.VMEM((4, GROUP, UNITS), BF16), pltpu.SemaphoreType.DMA((4,))],
@@ -311,7 +313,7 @@
     arrived = lax.all_to_all(message, ("c", "z", "yl"), split_axis=0, concat_axis=0)
     outgoing, pair_total = kernel(
         close,
-        [((2 * RANK, 10, LANES), F32), ((8, LANES), F32)],
+        [((2 * RANK, 1, UNITS + 2 * SLICE + LANES), F32), ((8, LANES), F32)],
         (place, arrived, signs, valid, low_t, k, tok),
         16 * GROUP * HALF * 2, 16,
         scratch=[
@@ -323,11 +325,12 @@
     )
 
     summed = jnp.sum(lax.all_to_all(outgoing, DP, split_axis=0, concat_axis=0), axis=0)
+    columns = summed[:, UNITS : UNITS + 2 * SLICE].reshape(1, 2, SLICE)
     grad_a = lax.all_to_all(
-        jnp.broadcast_to(summed[None, 7:9], (16, 2, SLICE)), BLK, split_axis=0, concat_axis=0
+        jnp.broadcast_to(columns, (16, 2, SLICE)), BLK, split_axis=0, concat_axis=0
     )
     grad_a = grad_a.transpose(2, 1, 0).reshape(SLICE, 2 * RANK)
-    return -summed[9, 0] / pair_total[0, 0], grad_a, summed[:7].reshape(1, UNITS)
+    return -summed[0, UNITS + 2 * SLICE] / pair_total[0, 0], grad_a, summed[:, :UNITS]
 
 
 def solution(mesh):

time: 211 us -> 195 us (0.924)
  waiting for transfers between devices: 45.4 us -> 19.6 us
  blocking collectives: 17.4 us -> 35.9 us
  Pallas kernels: 23.8 us -> 17.8 us
    all_to_all x0 -> x1, blocking collectives: none -> 22.5 us  [on_device(): lax.all_to_all(outgoing, DP, split_axis=0, concat_axis=0)]
    ppermute x6, waiting for transfers between devices: 17.9 us -> 0.02 us  [fetch(): return lax.ppermute(value, axis, [((i + k) % n, i) for i in range(n)])]
    all_to_all x2 -> x1, waiting for transfers between devices: 18 us -> 4.38 us  [on_device(): lax.all_to_all(jnp.broadcast_to(columns, (16, 2, SLICE)), BLK, split_axis...]
    all_to_all x2 -> x1, starting transfers between devices: 11.3 us -> 3.49 us  [on_device(): lax.all_to_all(jnp.broadcast_to(columns, (16, 2, SLICE)), BLK, split_axis...]
    ppermute x1, starting transfers between devices: 5.14 us -> 12.3 us  [on_device(): lax.ppermute(side_far, 'c', SWAP)]
    pallas_call x5 -> x4, Pallas kernels: 23.8 us -> 17.8 us  [kernel(): pl.pallas_call(function, out_shape=tuple((jax.ShapeDtypeStruct(*s) for s...]
    ppermute x7, starting transfers between devices: 33.2 us -> 28.3 us  [along(): return lax.ppermute(value, axis, [(i, (i + k) % n) for i in range(n)])]
    all_to_all x1, blocking collectives: 17.4 us -> 13.4 us  [on_device(): lax.all_to_all(message, ('c', 'z', 'yl'), split_axis=0, concat_axis=0)]
  transfers between devices with their start and end apart: 20 -> 19, of which waited for: 9 -> 8; matrix products, arithmetic and copies ran while one was open for 7% -> 7% of each run, Pallas kernels for 5% -> 3%
where the time goes in v9:
time: 195 us; the launch traced here: 194 us
  starting transfers between devices  79.5 us (41%)
  blocking collectives  35.9 us (18%)
  between operations  22.4 us (11%)
  waiting for transfers between devices  19.6 us (10%)
  Pallas kernels  17.8 us (9%)
  other arithmetic  9.31 us (5%)
  local copies, waits for them, and re-layouts  9.22 us (5%)
    ppermute x7, starting transfers between devices, along(): return lax.ppermute(value, axis, [(i, (i + k) % n) for i in range(n)])  28.3 us
    ppermute x6, starting transfers between devices, fetch(): return lax.ppermute(value, axis, [((i + k) % n, i) for i in range(n)])  27.3 us
    all_to_all x1, blocking collectives, on_device(): lax.all_to_all(outgoing, DP, split_axis=0, concat_axis=0)  22.5 us
    pallas_call x4, Pallas kernels, kernel(): pl.pallas_call(function, out_shape=tuple((jax.ShapeDtypeStruct(*s) for s...  17.8 us
    all_to_all x1, blocking collectives, on_device(): lax.all_to_all(message, ('c', 'z', 'yl'), split_axis=0, concat_axis=0)  13.4 us
    ppermute x1, starting transfers between devices, on_device(): lax.ppermute(side_far, 'c', SWAP)  12.3 us
    ppermute x1, waiting for transfers between devices, swapped(): far = lax.ppermute(value, axis, SWAP)  6.07 us
    ppermute x7, waiting for transfers between devices, along(): return lax.ppermute(value, axis, [(i, (i + k) % n) for i in range(n)])  5.68 us
  transfers between devices with their start and end apart: 19, of which 8 were waited for; matrix products, arithmetic and copies ran while one was open for 7% of the time, Pallas kernels for 3%

profile of v9, /device:TPU:1, one launch (start us, length us, event | category | flops | bytes accessed | tf_op | source)
XLA Modules:
  0.0 193.8 jit_solution(1672337004181113031)
XLA Ops:
  9.1 1.4 fusion.17
  14.0 6.7 %collective-permute-start.2 = (bf16[144,512]{1,0:T(8,128)(2,1)S(1)}, bf16[144,512]{1,0:T(8,128)(2,1)S(1)}, u32[]{:S(2)}, u32[]{:S(2)}) collective-permute-start(bf16[144,512]{1,0:T(8,128)(2,1)S(1)} %fusion.6), channel_id=1, source_target_pairs={{128,0},{256,128},{384,256},{0,384},{129,1},{257,129},{385,257},{1... | collective-permute-start | bytes 442376 | tf_op jit(solution)/shard_map/ppermute | solution.py:232
  20.7 3.5 %collective-permute-start.3 = (bf16[144,512]{1,0:T(8,128)(2,1)S(1)}, bf16[144,512]{1,0:T(8,128)(2,1)S(1)}, u32[]{:S(2)}, u32[]{:S(2)}) collective-permute-start(bf16[144,512]{1,0:T(8,128)(2,1)S(1)} %fusion.6), channel_id=1, source_target_pairs={{256,0},{384,128},{0,256},{128,384},{257,1},{385,129},{1,257},{129... | collective-permute-start | bytes 442376 | tf_op jit(solution)/shard_map/ppermute | solution.py:232
  24.3 4.2 %collective-permute-start.4 = (bf16[144,512]{1,0:T(8,128)(2,1)S(1)}, bf16[144,512]{1,0:T(8,128)(2,1)S(1)}, u32[]{:S(2)}, u32[]{:S(2)}) collective-permute-start(bf16[144,512]{1,0:T(8,128)(2,1)S(1)} %fusion.6), channel_id=1, source_target_pairs={{384,0},{0,128},{128,256},{256,384},{385,1},{1,129},{129,257},{257... | collective-permute-start | bytes 442376 | tf_op jit(solution)/shard_map/ppermute | solution.py:232
  28.9 3.4 %collective-permute-start = (bf16[12,2176]{1,0:T(8,128)(2,1)S(1)}, bf16[12,2176]{1,0:T(8,128)(2,1)S(1)}, u32[]{:S(2)}, u32[]{:S(2)}) collective-permute-start(bf16[12,2176]{1,0:T(8,128)(2,1)S(1)} %get-tuple-element.65), channel_id=1, source_target_pairs={{0,16},{16,0},{1,17},{17,1},{2,18},{18,2},{3,19},{19,3},{4,20},{20... | collective-permute-start | bytes 156680 | tf_op jit(solution)/shard_map/ppermute | solution.py:247
  34.3 2.3 %collective-permute-start.1 = (bf16[24,2176]{1,0:T(8,128)(2,1)S(1)}, bf16[24,2176]{1,0:T(8,128)(2,1)S(1)}, u32[]{:S(2)}, u32[]{:S(2)}) collective-permute-start(bf16[24,2176]{1,0:T(8,128)(2,1)S(1)} %maximum_select_fusion.2), channel_id=1, source_target_pairs={{0,1},{1,0},{2,3},{3,2},{4,5},{5,4},{6,7},{7,6},{8,9},{9,8},{10,11... | collective-permute-start | bytes 313352 | tf_op jit(solution)/shard_map/ppermute | solution.py:39
  36.7 6.1 %collective-permute-done.1 = bf16[24,2176]{1,0:T(8,128)(2,1)S(1)} collective-permute-done((bf16[24,2176]{1,0:T(8,128)(2,1)S(1)}, bf16[24,2176]{1,0:T(8,128)(2,1)S(1)}, u32[]{:S(2)}, u32[]{:S(2)}) %collective-permute-start.1) | collective-permute-done | bytes 104480 | tf_op jit(solution)/shard_map/ppermute | solution.py:39
  42.9 7.8 %collective-permute-start.12 = (bf16[576,512]{1,0:T(8,128)(2,1)S(1)}, bf16[576,512]{1,0:T(8,128)(2,1)S(1)}, u32[]{:S(2)}, u32[]{:S(2)}) collective-permute-start(bf16[576,512]{1,0:T(8,128)(2,1)S(1)} %constant_dynamic-update-slice_fusion.s0), channel_id=1, source_target_pairs={{32,0},{64,32},{96,64},{0,96},{33,1},{65,33},{97,65},{1,97},{34,2}... | collective-permute-start | bytes 1769480 | tf_op jit(solution)/shard_map/ppermute | solution.py:232
  50.8 2.5 %collective-permute-start.13 = (bf16[576,512]{1,0:T(8,128)(2,1)S(1)}, bf16[576,512]{1,0:T(8,128)(2,1)S(1)}, u32[]{:S(2)}, u32[]{:S(2)}) collective-permute-start(bf16[576,512]{1,0:T(8,128)(2,1)S(1)} %constant_dynamic-update-slice_fusion.s0), channel_id=1, source_target_pairs={{64,0},{96,32},{0,64},{32,96},{65,1},{97,33},{1,65},{33,97},{66,2}... | collective-permute-start | bytes 1769480 | tf_op jit(solution)/shard_map/ppermute | solution.py:232
  53.3 2.5 %collective-permute-start.14 = (bf16[576,512]{1,0:T(8,128)(2,1)S(1)}, bf16[576,512]{1,0:T(8,128)(2,1)}, u32[]{:S(2)}, u32[]{:S(2)}) collective-permute-start(bf16[576,512]{1,0:T(8,128)(2,1)S(1)} %constant_dynamic-update-slice_fusion.s0), channel_id=1, source_target_pairs={{96,0},{0,32},{32,64},{64,96},{97,1},{1,33},{33,65},{65,97},{98,2}... | collective-permute-start | bytes 1769480 | tf_op jit(solution)/shard_map/ppermute | solution.py:232
  55.8 10.7 %collective-permute-start.6 = (bf16[48,2176]{1,0:T(8,128)(2,1)S(1)}, bf16[48,2176]{1,0:T(8,128)(2,1)S(1)}, u32[]{:S(2)}, u32[]{:S(2)}) collective-permute-start(bf16[48,2176]{1,0:T(8,128)(2,1)S(1)} %bitcast.48), channel_id=1, source_target_pairs={{0,14},{2,0},{4,2},{6,4},{8,6},{10,8},{12,10},{14,12},{1,15},{3,1}... | collective-permute-start | bytes 626696 | tf_op jit(solution)/shard_map/ppermute | solution.py:227
  66.5 1.9 collective-permute-start.5
  69.6 5.0 %collective-permute-start.8 = (bf16[48,2176]{1,0:T(8,128)(2,1)S(1)}, bf16[48,2176]{1,0:T(8,128)(2,1)S(1)}, u32[]{:S(2)}, u32[]{:S(2)}) collective-permute-start(bf16[48,2176]{1,0:T(8,128)(2,1)S(1)} %collective-permute-done.6.l1), channel_id=1, source_target_pairs={{0,14},{2,0},{4,2},{6,4},{8,6},{10,8},{12,10},{14,12},{1,15},{3,1}... | collective-permute-start | bytes 626696 | tf_op jit(solution)/shard_map/ppermute | solution.py:227
  74.7 1.9 collective-permute-start.7
  77.8 3.5 %collective-permute-start.11 = (bf16[48,2176]{1,0:T(8,128)(2,1)S(1)}, bf16[48,2176]{1,0:T(8,128)(2,1)}, u32[]{:S(2)}, u32[]{:S(2)}) collective-permute-start(bf16[48,2176]{1,0:T(8,128)(2,1)S(1)} %bitcast.50), channel_id=1, source_target_pairs={{0,8},{2,10},{4,12},{6,14},{8,0},{10,2},{12,4},{14,6},{1,9},{3,11}... | collective-permute-start | bytes 626696 | tf_op jit(solution)/shard_map/ppermute | solution.py:227
  81.3 1.5 collective-permute-done.7.r2
  82.8 3.1 %collective-permute-start.10 = (bf16[48,2176]{1,0:T(8,128)(2,1)S(1)}, bf16[48,2176]{1,0:T(8,128)(2,1)}, u32[]{:S(2)}, u32[]{:S(2)}) collective-permute-start(bf16[48,2176]{1,0:T(8,128)(2,1)S(1)} %collective-permute-done.8.l2), channel_id=1, source_target_pairs={{0,14},{2,0},{4,2},{6,4},{8,6},{10,8},{12,10},{14,12},{1,15},{3,1}... | collective-permute-start | bytes 626696 | tf_op jit(solution)/shard_map/ppermute | solution.py:227
  86.0 2.1 %collective-permute-start.9 = (bf16[48,2176]{1,0:T(8,128)(2,1)S(1)}, bf16[48,2176]{1,0:T(8,128)(2,1)}, u32[]{:S(2)}, u32[]{:S(2)}) collective-permute-start(bf16[48,2176]{1,0:T(8,128)(2,1)S(1)} %collective-permute-done.7.r2), channel_id=1, source_target_pairs={{0,2},{2,4},{4,6},{6,8},{8,10},{10,12},{12,14},{14,0},{1,3},{3,5},... | collective-permute-start | bytes 626696 | tf_op jit(solution)/shard_map/ppermute | solution.py:227
  91.4 1.3 fusion.9
  93.4 2.4 %collective-permute-done.10.l3 = bf16[48,2176]{1,0:T(8,128)(2,1)} collective-permute-done((bf16[48,2176]{1,0:T(8,128)(2,1)S(1)}, bf16[48,2176]{1,0:T(8,128)(2,1)}, u32[]{:S(2)}, u32[]{:S(2)}) %collective-permute-start.10) | collective-permute-done | bytes 208928 | tf_op jit(solution)/shard_map/ppermute | solution.py:227
  95.9 1.6 collective-permute-done.9.r3
  97.5 5.9 %shard_map.94 = (f32[384,640]{1,0:T(8,128)}, bf16[384,2176]{1,0:T(8,128)(2,1)}) custom-call(s32[4]{0:T(128)} %pad_add_fusion.place, bf16[2048,128]{1,0:T(8,128)(2,1)} %pad.17.down, bf16[48,2176]{1,0:T(8,128)(2,1)} %bitcast.51, bf16[48,2176]{1,0:T(8,128)(2,1)} %copy-done.10, bf16[48,2176]{1,0:T(8,128)(2,1)} %copy-done.9, bf16[48,2176]{1,0:T(8,128)(2,1)} %copy-done.12, ...), custom_call_target="tpu_custom_call" | custom-call | flops 1006632960 | bytes 10000000 | tf_op jit(solution)/shard_map/pallas_call | solution.py:214
  105.9 12.3 %collective-permute-start.15 = (f32[192,640]{1,0:T(8,128)S(1)}, f32[192,640]{1,0:T(8,128)S(1)}, u32[]{:S(2)}, u32[]{:S(2)}) collective-permute-start(f32[192,640]{1,0:T(8,128)S(1)} %slice_select_fusion), channel_id=1, source_target_pairs={{0,16},{16,0},{1,17},{17,1},{2,18},{18,2},{3,19},{19,3},{4,20},{20... | collective-permute-start | bytes 1474568 | tf_op jit(solution)/shard_map/ppermute | solution.py:285
  119.8 6.0 %shard_map.95 = (f32[192,1280]{1,0:T(8,128)}, f32[192,1280]{1,0:T(8,128)}) custom-call(s32[4]{0:T(128)} %pad_add_fusion.place, bf16[384,2176]{1,0:T(8,128)(2,1)} %get-tuple-element.30.tok.tok_in, bf16[2048,1280]{1,0:T(8,128)(2,1)} %all-gather.2.cloned.1.call-done.w_in), custom_call_target="tpu_custom_call" | custom-call | flops 2013265920 | bytes 10000000 | tf_op jit(solution)/shard_map/pallas_call | solution.py:214
  125.8 2.4 %collective-permute-start.16 = (f32[192,1280]{1,0:T(8,128)}, f32[192,1280]{1,0:T(8,128)S(1)}, u32[]{:S(2)}, u32[]{:S(2)}) collective-permute-start(f32[192,1280]{1,0:T(8,128)} %get-tuple-element.34), channel_id=1, source_target_pairs={{0,16},{16,0},{1,17},{17,1},{2,18},{18,2},{3,19},{19,3},{4,20},{20... | collective-permute-start | bytes 2949128 | tf_op jit(solution)/shard_map/ppermute | solution.py:304
  128.3 2.4 %collective-permute-done.16.partner = f32[192,1280]{1,0:T(8,128)S(1)} collective-permute-done((f32[192,1280]{1,0:T(8,128)}, f32[192,1280]{1,0:T(8,128)S(1)}, u32[]{:S(2)}, u32[]{:S(2)}) %collective-permute-start.16) | collective-permute-done | bytes 983072 | tf_op jit(solution)/shard_map/ppermute | solution.py:304
  131.8 3.7 %shard_map.96 = (f32[32,1,640]{2,1,0:T(1,128)S(1)}, f32[32,192]{1,0:T(8,128)S(1)}, bf16[4,192,896]{2,1,0:T(8,128)(2,1)S(1)}) custom-call(s32[4]{0:T(128)S(1)} %copy-done.2, f32[192,1280]{1,0:T(8,128)S(1)} %copy-done.1, f32[192,1280]{1,0:T(8,128)S(1)} %collective-permute-done.16.partner, f32[192,640]{1,0:T(8,128)S(1)} %select_add_fusion.side, ...), custom_call_target="tpu_custom_call" | custom-call | flops 176160768 | bytes 10000000 | tf_op jit(solution)/shard_map/pallas_call | solution.py:214
  135.6 13.4 %all_to_all.15.arrived = f32[32,1,640]{2,1,0:T(1,128)S(1)} all-to-all(f32[32,1,640]{2,1,0:T(1,128)S(1)} %get-tuple-element.41), channel_id=1, replica_groups=mesh['yh'=4,'x'=4,'c'=2,'z'=8,'yl'=2] {'c','z','yl'}, dimensions={0} | all-to-all | bytes 163840 | tf_op jit(solution)/shard_map/all_to_all | solution.py:313
  149.0 2.1 %shard_map.97 = (f32[32,1,1280]{2,1,0:T(1,128)S(1)}, f32[8,128]{1,0:T(8,128)S(1)}) custom-call(s32[4]{0:T(128)S(1)} %copy-done.2, f32[32,1,640]{2,1,0:T(1,128)S(1)} %all_to_all.15.arrived, bf16[2,128,192]{2,1,0:T(8,128)(2,1)S(1)} %fusion.7.signs, f32[2,1,128]{2,1,0:T(1,128)S(1)} %bitcast.45, f32[32,192]{1,0:T(8,128)S(1)} %get-tuple-element.43.low_t, ...), custom_call_target="tpu_custom_call" | custom-call | flops 12582912 | bytes 10000000 | tf_op jit(solution)/shard_map/pallas_call | solution.py:214
  151.2 22.5 %all_to_all.16 = f32[32,1,1280]{2,1,0:T(1,128)S(1)} all-to-all(f32[32,1,1280]{2,1,0:T(1,128)S(1)} %get-tuple-element.45), channel_id=1, replica_groups=mesh['yh'=4,'x'=4,'c'=2,'z'=8,'yl'=2] {'yh','x','c'}, dimensions={0} | all-to-all | bytes 327680 | tf_op jit(solution)/shard_map/all_to_all | solution.py:327
  174.4 3.5 %all-to-all-start.2 = ((f32[16,2,128]{2,1,0:T(2,128)}), f32[16,2,128]{2,1,0:T(2,128)S(1)}, u32[]{:S(2)}, u32[]{:S(2)}) async-start(f32[16,2,128]{2,1,0:T(2,128)} %broadcast_in_dim.29), calls=%async_computation.2 | async-start | bytes 32768 | tf_op jit(solution)/shard_map/all_to_all | solution.py:329
  180.9 4.4 %all-to-all-done.2 = f32[16,2,128]{2,1,0:T(2,128)S(1)} async-done(((f32[16,2,128]{2,1,0:T(2,128)}), f32[16,2,128]{2,1,0:T(2,128)S(1)}, u32[]{:S(2)}, u32[]{:S(2)}) %all-to-all-start.2) | async-done | bytes 16416 | tf_op jit(solution)/shard_map/all_to_all | solution.py:329
  (105 shorter events, 17.1 us)
Async XLA Ops:
  7.2 21.3 %copy-start.13 = (bf16[12,4096]{1,0:T(8,128)(2,1)S(1)}, bf16[12,4096]{1,0:T(8,128)(2,1)}, u32[]{:S(2)}) copy-start(bf16[12,4096]{1,0:T(8,128)(2,1)} %param.7) | copy-start | bytes 294916
  7.2 25.1 %copy-start.8 = (bf16[4096,32]{0,1:T(8,128)(2,1)S(1)}, bf16[4096,32]{0,1:T(8,128)(2,1)}, u32[]{:S(2)}) copy-start(bf16[4096,32]{0,1:T(8,128)(2,1)} %param.11) | copy-start | bytes 786436
  7.2 112.6 %all-gather.2.cloned.1.call-start = ((), (), s32[]{:S(2)}) async-start(), calls=%async_computation.3 | async-start | bytes 5570560 | tf_op jit(solution)/shard_map/all_gather | solution.py:241
  14.0 28.8 %collective-permute-start.2 = (bf16[144,512]{1,0:T(8,128)(2,1)S(1)}, bf16[144,512]{1,0:T(8,128)(2,1)S(1)}, u32[]{:S(2)}, u32[]{:S(2)}) collective-permute-start(bf16[144,512]{1,0:T(8,128)(2,1)S(1)} %fusion.6), channel_id=1, source_target_pairs={{128,0},{256,128},{384,256},{0,384},{129,1},{257,129},{385,257},{1... | collective-permute-start | bytes 442376 | tf_op jit(solution)/shard_map/ppermute | solution.py:232
  20.7 22.1 %collective-permute-start.3 = (bf16[144,512]{1,0:T(8,128)(2,1)S(1)}, bf16[144,512]{1,0:T(8,128)(2,1)S(1)}, u32[]{:S(2)}, u32[]{:S(2)}) collective-permute-start(bf16[144,512]{1,0:T(8,128)(2,1)S(1)} %fusion.6), channel_id=1, source_target_pairs={{256,0},{384,128},{0,256},{128,384},{257,1},{385,129},{1,257},{129... | collective-permute-start | bytes 442376 | tf_op jit(solution)/shard_map/ppermute | solution.py:232
  24.3 18.6 %collective-permute-start.4 = (bf16[144,512]{1,0:T(8,128)(2,1)S(1)}, bf16[144,512]{1,0:T(8,128)(2,1)S(1)}, u32[]{:S(2)}, u32[]{:S(2)}) collective-permute-start(bf16[144,512]{1,0:T(8,128)(2,1)S(1)} %fusion.6), channel_id=1, source_target_pairs={{384,0},{0,128},{128,256},{256,384},{385,1},{1,129},{129,257},{257... | collective-permute-start | bytes 442376 | tf_op jit(solution)/shard_map/ppermute | solution.py:232
  28.9 5.3 %collective-permute-start = (bf16[12,2176]{1,0:T(8,128)(2,1)S(1)}, bf16[12,2176]{1,0:T(8,128)(2,1)S(1)}, u32[]{:S(2)}, u32[]{:S(2)}) collective-permute-start(bf16[12,2176]{1,0:T(8,128)(2,1)S(1)} %get-tuple-element.65), channel_id=1, source_target_pairs={{0,16},{16,0},{1,17},{17,1},{2,18},{18,2},{3,19},{19,3},{4,20},{20... | collective-permute-start | bytes 156680 | tf_op jit(solution)/shard_map/ppermute | solution.py:247
  34.2 35.3 %copy-start.14 = (bf16[16,896]{1,0:T(8,128)(2,1)S(1)}, bf16[16,896]{1,0:T(8,128)(2,1)}, u32[]{:S(2)}) copy-start(bf16[16,896]{1,0:T(8,128)(2,1)} %get-tuple-element.63) | copy-start | bytes 86020
  34.3 8.5 %collective-permute-start.1 = (bf16[24,2176]{1,0:T(8,128)(2,1)S(1)}, bf16[24,2176]{1,0:T(8,128)(2,1)S(1)}, u32[]{:S(2)}, u32[]{:S(2)}) collective-permute-start(bf16[24,2176]{1,0:T(8,128)(2,1)S(1)} %maximum_select_fusion.2), channel_id=1, source_target_pairs={{0,1},{1,0},{2,3},{3,2},{4,5},{5,4},{6,7},{7,6},{8,9},{9,8},{10,11... | collective-permute-start | bytes 313352 | tf_op jit(solution)/shard_map/ppermute | solution.py:39
  36.7 32.9 %copy-start.16 = (bf16[896]{0:T(1024)(128)(2,1)S(1)}, bf16[896]{0:T(1024)(128)(2,1)}, u32[]{:S(2)}) copy-start(bf16[896]{0:T(1024)(128)(2,1)} %param.13) | copy-start | bytes 5380
  42.8 54.6 %copy-start.5 = (bf16[2,24,2176]{2,1,0:T(8,128)(2,1)}, bf16[2,24,2176]{2,1,0:T(8,128)(2,1)S(1)}, u32[]{:S(2)}) copy-start(bf16[2,24,2176]{2,1,0:T(8,128)(2,1)S(1)} %maximum_select_fusion) | copy-start | bytes 626692
  42.9 54.5 %copy-start.4 = (bf16[576,512]{1,0:T(8,128)(2,1)}, bf16[576,512]{1,0:T(8,128)(2,1)S(1)}, u32[]{:S(2)}) copy-start(bf16[576,512]{1,0:T(8,128)(2,1)S(1)} %constant_dynamic-update-slice_fusion.s0) | copy-start | bytes 1769476
  42.9 43.0 %collective-permute-start.12 = (bf16[576,512]{1,0:T(8,128)(2,1)S(1)}, bf16[576,512]{1,0:T(8,128)(2,1)S(1)}, u32[]{:S(2)}, u32[]{:S(2)}) collective-permute-start(bf16[576,512]{1,0:T(8,128)(2,1)S(1)} %constant_dynamic-update-slice_fusion.s0), channel_id=1, source_target_pairs={{32,0},{64,32},{96,64},{0,96},{33,1},{65,33},{97,65},{1,97},{34,2}... | collective-permute-start | bytes 1769480 | tf_op jit(solution)/shard_map/ppermute | solution.py:232
  50.8 39.3 %collective-permute-start.13 = (bf16[576,512]{1,0:T(8,128)(2,1)S(1)}, bf16[576,512]{1,0:T(8,128)(2,1)S(1)}, u32[]{:S(2)}, u32[]{:S(2)}) collective-permute-start(bf16[576,512]{1,0:T(8,128)(2,1)S(1)} %constant_dynamic-update-slice_fusion.s0), channel_id=1, source_target_pairs={{64,0},{96,32},{0,64},{32,96},{65,1},{97,33},{1,65},{33,97},{66,2}... | collective-permute-start | bytes 1769480 | tf_op jit(solution)/shard_map/ppermute | solution.py:232
  53.3 38.1 %collective-permute-start.14 = (bf16[576,512]{1,0:T(8,128)(2,1)S(1)}, bf16[576,512]{1,0:T(8,128)(2,1)}, u32[]{:S(2)}, u32[]{:S(2)}) collective-permute-start(bf16[576,512]{1,0:T(8,128)(2,1)S(1)} %constant_dynamic-update-slice_fusion.s0), channel_id=1, source_target_pairs={{96,0},{0,32},{32,64},{64,96},{97,1},{1,33},{33,65},{65,97},{98,2}... | collective-permute-start | bytes 1769480 | tf_op jit(solution)/shard_map/ppermute | solution.py:232
  55.8 13.8 %collective-permute-start.6 = (bf16[48,2176]{1,0:T(8,128)(2,1)S(1)}, bf16[48,2176]{1,0:T(8,128)(2,1)S(1)}, u32[]{:S(2)}, u32[]{:S(2)}) collective-permute-start(bf16[48,2176]{1,0:T(8,128)(2,1)S(1)} %bitcast.48), channel_id=1, source_target_pairs={{0,14},{2,0},{4,2},{6,4},{8,6},{10,8},{12,10},{14,12},{1,15},{3,1}... | collective-permute-start | bytes 626696 | tf_op jit(solution)/shard_map/ppermute | solution.py:227
  66.5 8.2 %collective-permute-start.5 = (bf16[48,2176]{1,0:T(8,128)(2,1)S(1)}, bf16[48,2176]{1,0:T(8,128)(2,1)S(1)}, u32[]{:S(2)}, u32[]{:S(2)}) collective-permute-start(bf16[48,2176]{1,0:T(8,128)(2,1)S(1)} %bitcast.49), channel_id=1, source_target_pairs={{0,2},{2,4},{4,6},{6,8},{8,10},{10,12},{12,14},{14,0},{1,3},{3,5},... | collective-permute-start | bytes 626696 | tf_op jit(solution)/shard_map/ppermute | solution.py:227
  69.6 27.9 %copy-start.9 = (bf16[48,2176]{1,0:T(8,128)(2,1)}, bf16[48,2176]{1,0:T(8,128)(2,1)S(1)}, u32[]{:S(2)}) copy-start(bf16[48,2176]{1,0:T(8,128)(2,1)S(1)} %collective-permute-done.6.l1) | copy-start | bytes 626692
  69.6 8.3 %collective-permute-start.8 = (bf16[48,2176]{1,0:T(8,128)(2,1)S(1)}, bf16[48,2176]{1,0:T(8,128)(2,1)S(1)}, u32[]{:S(2)}, u32[]{:S(2)}) collective-permute-start(bf16[48,2176]{1,0:T(8,128)(2,1)S(1)} %collective-permute-done.6.l1), channel_id=1, source_target_pairs={{0,14},{2,0},{4,2},{6,4},{8,6},{10,8},{12,10},{14,12},{1,15},{3,1}... | collective-permute-start | bytes 626696 | tf_op jit(solution)/shard_map/ppermute | solution.py:227
  74.7 22.8 %copy-start.10 = (bf16[48,2176]{1,0:T(8,128)(2,1)}, bf16[48,2176]{1,0:T(8,128)(2,1)S(1)}, u32[]{:S(2)}) copy-start(bf16[48,2176]{1,0:T(8,128)(2,1)S(1)} %collective-permute-done.5.r1) | copy-start | bytes 626692
  74.7 8.1 %collective-permute-start.7 = (bf16[48,2176]{1,0:T(8,128)(2,1)S(1)}, bf16[48,2176]{1,0:T(8,128)(2,1)S(1)}, u32[]{:S(2)}, u32[]{:S(2)}) collective-permute-start(bf16[48,2176]{1,0:T(8,128)(2,1)S(1)} %collective-permute-done.5.r1), channel_id=1, source_target_pairs={{0,2},{2,4},{4,6},{6,8},{8,10},{10,12},{12,14},{14,0},{1,3},{3,5},... | collective-permute-start | bytes 626696 | tf_op jit(solution)/shard_map/ppermute | solution.py:227
  77.8 19.6 %copy-start.11 = (bf16[48,2176]{1,0:T(8,128)(2,1)}, bf16[48,2176]{1,0:T(8,128)(2,1)S(1)}, u32[]{:S(2)}) copy-start(bf16[48,2176]{1,0:T(8,128)(2,1)S(1)} %collective-permute-done.8.l2) | copy-start | bytes 626692
  77.8 15.5 %collective-permute-start.11 = (bf16[48,2176]{1,0:T(8,128)(2,1)S(1)}, bf16[48,2176]{1,0:T(8,128)(2,1)}, u32[]{:S(2)}, u32[]{:S(2)}) collective-permute-start(bf16[48,2176]{1,0:T(8,128)(2,1)S(1)} %bitcast.50), channel_id=1, source_target_pairs={{0,8},{2,10},{4,12},{6,14},{8,0},{10,2},{12,4},{14,6},{1,9},{3,11}... | collective-permute-start | bytes 626696 | tf_op jit(solution)/shard_map/ppermute | solution.py:227
  82.8 14.7 %copy-start.12 = (bf16[48,2176]{1,0:T(8,128)(2,1)}, bf16[48,2176]{1,0:T(8,128)(2,1)S(1)}, u32[]{:S(2)}) copy-start(bf16[48,2176]{1,0:T(8,128)(2,1)S(1)} %collective-permute-done.7.r2) | copy-start | bytes 626692
  82.8 13.0 %collective-permute-start.10 = (bf16[48,2176]{1,0:T(8,128)(2,1)S(1)}, bf16[48,2176]{1,0:T(8,128)(2,1)}, u32[]{:S(2)}, u32[]{:S(2)}) collective-permute-start(bf16[48,2176]{1,0:T(8,128)(2,1)S(1)} %collective-permute-done.8.l2), channel_id=1, source_target_pairs={{0,14},{2,0},{4,2},{6,4},{8,6},{10,8},{12,10},{14,12},{1,15},{3,1}... | collective-permute-start | bytes 626696 | tf_op jit(solution)/shard_map/ppermute | solution.py:227
  86.0 11.5 %copy-start.6 = (bf16[576,512]{1,0:T(8,128)(2,1)}, bf16[576,512]{1,0:T(8,128)(2,1)S(1)}, u32[]{:S(2)}) copy-start(bf16[576,512]{1,0:T(8,128)(2,1)S(1)} %collective-permute-done.12.s1) | copy-start | bytes 1769476
  86.0 11.5 %collective-permute-start.9 = (bf16[48,2176]{1,0:T(8,128)(2,1)S(1)}, bf16[48,2176]{1,0:T(8,128)(2,1)}, u32[]{:S(2)}, u32[]{:S(2)}) collective-permute-start(bf16[48,2176]{1,0:T(8,128)(2,1)S(1)} %collective-permute-done.7.r2), channel_id=1, source_target_pairs={{0,2},{2,4},{4,6},{6,8},{8,10},{10,12},{12,14},{14,0},{1,3},{3,5},... | collective-permute-start | bytes 626696 | tf_op jit(solution)/shard_map/ppermute | solution.py:227
  103.4 16.2 %copy-start.3 = (f32[384,640]{1,0:T(8,128)S(1)}, f32[384,640]{1,0:T(8,128)}, u32[]{:S(2)}) copy-start(f32[384,640]{1,0:T(8,128)} %get-tuple-element.31) | copy-start | bytes 2949124
  105.9 13.8 %collective-permute-start.15 = (f32[192,640]{1,0:T(8,128)S(1)}, f32[192,640]{1,0:T(8,128)S(1)}, u32[]{:S(2)}, u32[]{:S(2)}) collective-permute-start(f32[192,640]{1,0:T(8,128)S(1)} %slice_select_fusion), channel_id=1, source_target_pairs={{0,16},{16,0},{1,17},{17,1},{2,18},{18,2},{3,19},{19,3},{4,20},{20... | collective-permute-start | bytes 1474568 | tf_op jit(solution)/shard_map/ppermute | solution.py:285
  125.8 23.2 %copy-start = (bf16[384,2176]{1,0:T(8,128)(2,1)S(1)}, bf16[384,2176]{1,0:T(8,128)(2,1)}, u32[]{:S(2)}) copy-start(bf16[384,2176]{1,0:T(8,128)(2,1)} %get-tuple-element.30.tok.tok_in) | copy-start | bytes 5013508
  125.8 4.8 %collective-permute-start.16 = (f32[192,1280]{1,0:T(8,128)}, f32[192,1280]{1,0:T(8,128)S(1)}, u32[]{:S(2)}, u32[]{:S(2)}) collective-permute-start(f32[192,1280]{1,0:T(8,128)} %get-tuple-element.34), channel_id=1, source_target_pairs={{0,16},{16,0},{1,17},{17,1},{2,18},{18,2},{3,19},{19,3},{4,20},{20... | collective-permute-start | bytes 2949128 | tf_op jit(solution)/shard_map/ppermute | solution.py:304
  174.4 10.8 %all-to-all-start.2 = ((f32[16,2,128]{2,1,0:T(2,128)}), f32[16,2,128]{2,1,0:T(2,128)S(1)}, u32[]{:S(2)}, u32[]{:S(2)}) async-start(f32[16,2,128]{2,1,0:T(2,128)} %broadcast_in_dim.29), calls=%async_computation.2 | async-start | bytes 32768 | tf_op jit(solution)/shard_map/all_to_all | solution.py:329
  (4 other events, 24.2 us)
Sparse Core Ops, SparseCore 0:
  11.0 99.5 all-gather.1

commit v10 on v9

--- a/solution.py
+++ b/solution.py
@@ -52,7 +52,7 @@
     return lax.dot_general(a, b, dims, preferred_element_type=F32)
 
 
-def early_products(place, down, p0, r1, l1, r2, l2, r3, l3, far_z, s0, s1, s2, s3, out, tok_out, tok, w, sems):
+def early_products(place, down, p0, r1, l1, r2, l2, r3, l3, far_z, s0, s1, s2, s3, far, near, tok_out, tok, w, sems):
     z, yh, x = place[1], place[2], place[3]
     block = 4 * ROWS
     moves = ((0, p0), (-1, r1), (1, l1), (-2, r2), (2, l2), (-3, r3), (3, l3), (4, far_z))
@@ -73,10 +73,12 @@
         copy.wait()
     tok_copy = pltpu.make_async_copy(tok, tok_out, sems.at[24])
     tok_copy.start()
-    for n in range(2):
-        part = slice(n * SIDE, (n + 1) * SIDE)
-        out[:, part] = dot(tok[:, 0:HALF], w[:, part])
-    out[:, 2 * SIDE :] = dot(tok[:, 0:HALF], down[...])
+    for half, out in ((1 - place[0], far), (place[0], near)):
+        rows = pl.ds(pl.multiple_of(half * GROUP, GROUP), GROUP)
+        for n in range(2):
+            part = slice(n * SIDE, (n + 1) * SIDE)
+            out[:, part] = dot(tok[rows, 0:HALF], w[:, part])
+        out[:, 2 * SIDE :] = dot(tok[rows, 0:HALF], down[...])
     tok_copy.wait()
 
 
@@ -120,8 +122,13 @@
     )
 
 
-def score(place, near, partner, side, b_gate, b_up, readout, signs, count, message, low_t, k_out, k, sems):
+def score(place, partner, side_near, side_partner, b_gate, b_up, readout, signs, count, near_in, message, low_t, k_out, k,
+          near, sems):
+    near_copy = pltpu.make_async_copy(near_in, near, sems.at[4])
+    near_copy.start()
+    side = side_near[...] + side_partner[...]
     low_b = side[:, 2 * SIDE :].astype(BF16)
+    near_copy.wait()
     main = near[...] + partner[...]
     gate_ref = jnp.concatenate([main[:, 0:MAIN], side[:, 0:SIDE]], axis=1)
     up_ref = jnp.concatenate([main[:, MAIN:], side[:, SIDE : 2 * SIDE]], axis=1)
@@ -238,6 +245,7 @@
     code = jnp.where(response_mask > 0, sequence_labels, SEQS)
 
     main = jnp.concatenate([frozen[0, :, :MAIN], frozen[1, :, :MAIN]], axis=1)
+    main, tokens, frozen = lax.optimization_barrier((main, tokens, frozen))
     w_main = lax.all_gather(main, ("yh", "x"), axis=0, tiled=True)
 
     by_core = tokens.reshape(ROWS, 16, 2, SLICE).transpose(2, 0, 1, 3).reshape(2, ROWS, HALF)
@@ -255,22 +263,22 @@
         [jnp.concatenate([frozen[0, :, MAIN:], frozen[1, :, MAIN:]], axis=1), count_rows], axis=0
     )
     pieces = [piece] + [fetch(piece, "yh", k) for k in (1, 2, 3)]
-    four, *pieces = lax.optimization_barrier((four, *pieces))
     ring = [four, along(four, "z", 1), along(four, "z", -1)]
     stack = jnp.concatenate(pieces, axis=0)
     stacks = [stack] + [fetch(stack, "x", j) for j in (1, 2, 3)]
     for step in range(2):
         ring += [along(ring[-2], "z", 1), along(ring[-1], "z", -1)]
     ring.append(along(four, "z", 4))
+    ring[5], ring[6], stacks[1] = lax.optimization_barrier((ring[5], ring[6], stacks[1]))
     count = sum(jnp.sum(p.reshape(4, PIECE, 2 * SIDE)[:, SLICE, 0].astype(F32)) for p in stacks)
     count_lanes = jnp.where(jnp.arange(LANES) == 64, count, 0.0).reshape(1, LANES)
 
     down_half = down.reshape(16, 2, SLICE, 2 * RANK)
     down_half = jnp.where(core == 0, down_half[:, 0], down_half[:, 1]).reshape(HALF, 2 * RANK)
     down_half = jnp.pad(down_half, ((0, 0), (0, LANES - 2 * RANK)))
-    side, tok = kernel(
+    side_far, side, tok = kernel(
         early_products,
-        [((2 * GROUP, 2 * SIDE + LANES), F32), ((2 * GROUP, HALF + LANES), BF16)],
+        [((GROUP, 2 * SIDE + LANES), F32)] * 2 + [((2 * GROUP, HALF + LANES), BF16)],
         (place, down_half, *ring, *stacks),
         4 * GROUP * HALF * (2 * SIDE + LANES), 56,
         scratch=[
@@ -280,9 +288,7 @@
         ],
         in_hbm=12, out_hbm=1,
     )
-    side = side.reshape(2, GROUP, 2 * SIDE + LANES)
-    side_far = jnp.where(core == 0, side[1], side[0])
-    side = jnp.where(core == 0, side[0], side[1]) + lax.ppermute(side_far, "c", SWAP)
+    side_partner = lax.ppermute(side_far, "c", SWAP)
 
     b_gate = jnp.pad(up[:RANK], ((0, LANES - RANK), (0, 0)))
     b_up = jnp.pad(up[RANK:], ((RANK, LANES - 2 * RANK), (0, 0)))
@@ -297,18 +303,22 @@
     signs = chosen.astype(BF16) - rejected.astype(BF16)
     valid = (jnp.any(chosen, axis=2) & jnp.any(rejected, axis=2)).astype(F32).reshape(2, 1, LANES)
 
-    w_main, side, b_gate, b_up, read, signs, valid, count_lanes = lax.optimization_barrier(
-        (w_main, side, b_gate, b_up, read, signs, valid, count_lanes)
+    w_main, b_gate, b_up, read, count_lanes = lax.optimization_barrier(
+        (w_main, b_gate, b_up, read, count_lanes)
     )
     far, near = products(place, tok, w_main)
     partner = lax.ppermute(far, "c", SWAP)
     message, low_t, k = kernel(
         score,
         [((2 * RANK, 1, 5 * LANES), F32), ((2 * RANK, GROUP), F32), ((4, GROUP, UNITS), BF16)],
-        (place, near, partner, side, b_gate, b_up, read, signs, count_lanes),
+        (place, partner, side, side_partner, b_gate, b_up, read, signs, count_lanes, near),
         8 * GROUP * UNITS * LANES, 16,
-        scratch=[pltpu.VMEM((4, GROUP, UNITS), BF16), pltpu.SemaphoreType.DMA((4,))],
-        out_hbm=1,
+        scratch=[
+            pltpu.VMEM((4, GROUP, UNITS), BF16),
+            pltpu.VMEM((GROUP, 2 * MAIN), F32),
+            pltpu.SemaphoreType.DMA((5,)),
+        ],
+        in_hbm=1, out_hbm=1,
     )
     arrived = lax.all_to_all(message, ("c", "z", "yl"), split_axis=0, concat_axis=0)
     outgoing, pair_total = kernel(

time: 195 us -> 202 us (1.036)
  blocking collectives: 35.9 us -> 18.4 us
  waiting for transfers between devices: 19.6 us -> 36.5 us
  local copies, waits for them, and re-layouts: 9.22 us -> 14.8 us
  starting transfers between devices: 79.5 us -> 83 us
  other arithmetic: 9.31 us -> 6.38 us
    all_gather x1, waiting for transfers between devices: 0.02 us -> 17.4 us  [on_device(): w_main = lax.all_gather(main, ('yh', 'x'), axis=0, tiled=True)]
    all_to_all x0 -> x1, starting transfers between devices: none -> 13.6 us  [on_device(): lax.all_to_all(message, ('c', 'z', 'yl'), split_axis=0, concat_axis=0)]
    all_to_all x1 -> x0, blocking collectives: 13.4 us -> none  [on_device(): lax.all_to_all(message, ('c', 'z', 'yl'), split_axis=0, concat_axis=0)]
    ppermute x1, starting transfers between devices: 12.3 us -> 1.92 us  [on_device(): side_partner = lax.ppermute(side_far, 'c', SWAP)]
    all_to_all x0 -> x1, waiting for transfers between devices: none -> 8.02 us  [on_device(): lax.all_to_all(message, ('c', 'z', 'yl'), split_axis=0, concat_axis=0)]
    ppermute x1, waiting for transfers between devices: 6.07 us -> 0.01 us  [swapped(): far = lax.ppermute(value, axis, SWAP)]
    unnamed x43 -> x53, local copies, waits for them, and re-layouts: 2 us -> 7.52 us
    all_to_all x1, blocking collectives: 22.5 us -> 18.4 us  [on_device(): lax.all_to_all(outgoing, DP, split_axis=0, concat_axis=0)]
  transfers between devices with their start and end apart: 19 -> 20, of which waited for: 8 -> 7; matrix products, arithmetic and copies ran while one was open for 7% -> 6% of each run, Pallas kernels for 3% -> 3%
where the time goes in v10:
time: 202 us; the launch traced here: 201 us
  starting transfers between devices  83 us (41%)
  waiting for transfers between devices  36.5 us (18%)
  between operations  22.3 us (11%)
  Pallas kernels  19.3 us (10%)
  blocking collectives  18.4 us (9%)
  local copies, waits for them, and re-layouts  14.8 us (7%)
  other arithmetic  6.38 us (3%)
    ppermute x7, starting transfers between devices, along(): return lax.ppermute(value, axis, [(i, (i + k) % n) for i in range(n)])  30.8 us
    ppermute x6, starting transfers between devices, fetch(): return lax.ppermute(value, axis, [((i + k) % n, i) for i in range(n)])  23.8 us
    pallas_call x4, Pallas kernels, kernel(): pl.pallas_call(function, out_shape=tuple((jax.ShapeDtypeStruct(*s) for s...  19.3 us
    all_to_all x1, blocking collectives, on_device(): lax.all_to_all(outgoing, DP, split_axis=0, concat_axis=0)  18.4 us
    all_gather x1, waiting for transfers between devices, on_device(): w_main = lax.all_gather(main, ('yh', 'x'), axis=0, tiled=True)  17.4 us
    all_to_all x1, starting transfers between devices, on_device(): lax.all_to_all(message, ('c', 'z', 'yl'), split_axis=0, concat_axis=0)  13.6 us
    all_to_all x1, waiting for transfers between devices, on_device(): lax.all_to_all(message, ('c', 'z', 'yl'), split_axis=0, concat_axis=0)  8.02 us
    unnamed x53, local copies, waits for them, and re-layouts  7.52 us
  transfers between devices with their start and end apart: 20, of which 7 were waited for; matrix products, arithmetic and copies ran while one was open for 6% of the time, Pallas kernels for 3%

profile of v10, /device:TPU:1, one launch (start us, length us, event | category | flops | bytes accessed | tf_op | source)
XLA Modules:
  0.0 200.7 jit_solution(17122751559245447403)
XLA Ops:
  9.1 1.3 fusion.14
  13.8 6.7 %collective-permute-start.8 = (bf16[144,512]{1,0:T(8,128)(2,1)S(1)}, bf16[144,512]{1,0:T(8,128)(2,1)S(1)}, u32[]{:S(2)}, u32[]{:S(2)}) collective-permute-start(bf16[144,512]{1,0:T(8,128)(2,1)S(1)} %concatenate.57), channel_id=1, source_target_pairs={{128,0},{256,128},{384,256},{0,384},{129,1},{257,129},{385,257},{1... | collective-permute-start | bytes 442376 | tf_op jit(solution)/shard_map/ppermute | solution.py:239
  20.5 3.5 %collective-permute-start.9 = (bf16[144,512]{1,0:T(8,128)(2,1)S(1)}, bf16[144,512]{1,0:T(8,128)(2,1)S(1)}, u32[]{:S(2)}, u32[]{:S(2)}) collective-permute-start(bf16[144,512]{1,0:T(8,128)(2,1)S(1)} %concatenate.57), channel_id=1, source_target_pairs={{256,0},{384,128},{0,256},{128,384},{257,1},{385,129},{1,257},{129... | collective-permute-start | bytes 442376 | tf_op jit(solution)/shard_map/ppermute | solution.py:239
  24.1 4.2 %collective-permute-start.10 = (bf16[144,512]{1,0:T(8,128)(2,1)S(1)}, bf16[144,512]{1,0:T(8,128)(2,1)S(1)}, u32[]{:S(2)}, u32[]{:S(2)}) collective-permute-start(bf16[144,512]{1,0:T(8,128)(2,1)S(1)} %concatenate.57), channel_id=1, source_target_pairs={{384,0},{0,128},{128,256},{256,384},{385,1},{1,129},{129,257},{257... | collective-permute-start | bytes 442376 | tf_op jit(solution)/shard_map/ppermute | solution.py:239
  28.7 3.4 %collective-permute-start = (bf16[12,2176]{1,0:T(8,128)(2,1)S(1)}, bf16[12,2176]{1,0:T(8,128)(2,1)S(1)}, u32[]{:S(2)}, u32[]{:S(2)}) collective-permute-start(bf16[12,2176]{1,0:T(8,128)(2,1)S(1)} %get-tuple-element.65), channel_id=1, source_target_pairs={{0,16},{16,0},{1,17},{17,1},{2,18},{18,2},{3,19},{19,3},{4,20},{20... | collective-permute-start | bytes 156680 | tf_op jit(solution)/shard_map/ppermute | solution.py:255
  34.4 2.3 %collective-permute-start.1 = (bf16[24,2176]{1,0:T(8,128)(2,1)S(1)}, bf16[24,2176]{1,0:T(8,128)(2,1)S(1)}, u32[]{:S(2)}, u32[]{:S(2)}) collective-permute-start(bf16[24,2176]{1,0:T(8,128)(2,1)S(1)} %maximum_select_fusion.2), channel_id=1, source_target_pairs={{0,1},{1,0},{2,3},{3,2},{4,5},{5,4},{6,7},{7,6},{8,9},{9,8},{10,11... | collective-permute-start | bytes 313352 | tf_op jit(solution)/shard_map/ppermute | solution.py:39
  36.9 4.4 %collective-permute-start.11 = (bf16[576,512]{1,0:T(8,128)(2,1)S(1)}, bf16[576,512]{1,0:T(8,128)(2,1)S(1)}, u32[]{:S(2)}, u32[]{:S(2)}) collective-permute-start(bf16[576,512]{1,0:T(8,128)(2,1)S(1)} %constant_dynamic-update-slice_fusion.s0), channel_id=1, source_target_pairs={{32,0},{64,32},{96,64},{0,96},{33,1},{65,33},{97,65},{1,97},{34,2}... | collective-permute-start | bytes 1769480 | tf_op jit(solution)/shard_map/ppermute | solution.py:239
  41.3 2.4 %collective-permute-start.13 = (bf16[576,512]{1,0:T(8,128)(2,1)S(1)}, bf16[576,512]{1,0:T(8,128)(2,1)S(1)}, u32[]{:S(2)}, u32[]{:S(2)}) collective-permute-start(bf16[576,512]{1,0:T(8,128)(2,1)S(1)} %constant_dynamic-update-slice_fusion.s0), channel_id=1, source_target_pairs={{64,0},{96,32},{0,64},{32,96},{65,1},{97,33},{1,65},{33,97},{66,2}... | collective-permute-start | bytes 1769480 | tf_op jit(solution)/shard_map/ppermute | solution.py:239
  43.7 2.5 %collective-permute-start.14 = (bf16[576,512]{1,0:T(8,128)(2,1)S(1)}, bf16[576,512]{1,0:T(8,128)(2,1)S(1)}, u32[]{:S(2)}, u32[]{:S(2)}) collective-permute-start(bf16[576,512]{1,0:T(8,128)(2,1)S(1)} %constant_dynamic-update-slice_fusion.s0), channel_id=1, source_target_pairs={{96,0},{0,32},{32,64},{64,96},{97,1},{1,33},{33,65},{65,97},{98,2}... | collective-permute-start | bytes 1769480 | tf_op jit(solution)/shard_map/ppermute | solution.py:239
  46.3 4.0 %collective-permute-start.2 = (bf16[48,2176]{1,0:T(8,128)(2,1)S(1)}, bf16[48,2176]{1,0:T(8,128)(2,1)S(1)}, u32[]{:S(2)}, u32[]{:S(2)}) collective-permute-start(bf16[48,2176]{1,0:T(8,128)(2,1)S(1)} %bitcast.48), channel_id=1, source_target_pairs={{0,2},{2,4},{4,6},{6,8},{8,10},{10,12},{12,14},{14,0},{1,3},{3,5},... | collective-permute-start | bytes 626696 | tf_op jit(solution)/shard_map/ppermute | solution.py:234
  50.3 8.6 %collective-permute-start.3 = (bf16[48,2176]{1,0:T(8,128)(2,1)S(1)}, bf16[48,2176]{1,0:T(8,128)(2,1)S(1)}, u32[]{:S(2)}, u32[]{:S(2)}) collective-permute-start(bf16[48,2176]{1,0:T(8,128)(2,1)S(1)} %bitcast.49), channel_id=1, source_target_pairs={{0,14},{2,0},{4,2},{6,4},{8,6},{10,8},{12,10},{14,12},{1,15},{3,1}... | collective-permute-start | bytes 626696 | tf_op jit(solution)/shard_map/ppermute | solution.py:234
  60.6 1.9 collective-permute-start.4
  62.5 4.6 %collective-permute-start.5 = (bf16[48,2176]{1,0:T(8,128)(2,1)S(1)}, bf16[48,2176]{1,0:T(8,128)(2,1)S(1)}, u32[]{:S(2)}, u32[]{:S(2)}) collective-permute-start(bf16[48,2176]{1,0:T(8,128)(2,1)S(1)} %collective-permute-done.3.l1), channel_id=1, source_target_pairs={{0,14},{2,0},{4,2},{6,4},{8,6},{10,8},{12,10},{14,12},{1,15},{3,1}... | collective-permute-start | bytes 626696 | tf_op jit(solution)/shard_map/ppermute | solution.py:234
  68.6 5.2 %collective-permute-start.12 = (bf16[48,2176]{1,0:T(8,128)(2,1)S(1)}, bf16[48,2176]{1,0:T(8,128)(2,1)}, u32[]{:S(2)}, u32[]{:S(2)}) collective-permute-start(bf16[48,2176]{1,0:T(8,128)(2,1)S(1)} %bitcast.50), channel_id=1, source_target_pairs={{0,8},{2,10},{4,12},{6,14},{8,0},{10,2},{12,4},{14,6},{1,9},{3,11}... | collective-permute-start | bytes 626696 | tf_op jit(solution)/shard_map/ppermute | solution.py:234
  73.9 1.9 collective-permute-start.6
  75.8 4.6 %collective-permute-start.7 = (bf16[48,2176]{1,0:T(8,128)(2,1)S(1)}, bf16[48,2176]{1,0:T(8,128)(2,1)S(1)}, u32[]{:S(2)}, u32[]{:S(2)}) collective-permute-start(bf16[48,2176]{1,0:T(8,128)(2,1)S(1)} %collective-permute-done.5.l2), channel_id=1, source_target_pairs={{0,14},{2,0},{4,2},{6,4},{8,6},{10,8},{12,10},{14,12},{1,15},{3,1}... | collective-permute-start | bytes 626696 | tf_op jit(solution)/shard_map/ppermute | solution.py:234
  81.8 3.9 %collective-permute-done.6.r3 = bf16[48,2176]{1,0:T(8,128)(2,1)S(1)} collective-permute-done((bf16[48,2176]{1,0:T(8,128)(2,1)S(1)}, bf16[48,2176]{1,0:T(8,128)(2,1)S(1)}, u32[]{:S(2)}, u32[]{:S(2)}) %collective-permute-start.6) | collective-permute-done | bytes 208928 | tf_op jit(solution)/shard_map/ppermute | solution.py:234
  90.4 5.8 %shard_map.94 = (f32[192,640]{1,0:T(8,128)}, f32[192,640]{1,0:T(8,128)}, bf16[384,2176]{1,0:T(8,128)(2,1)}) custom-call(s32[4]{0:T(128)} %pad_add_fusion.place, bf16[2048,128]{1,0:T(8,128)(2,1)} %pad.17.down, bf16[48,2176]{1,0:T(8,128)(2,1)} %bitcast.51, bf16[48,2176]{1,0:T(8,128)(2,1)} %copy-done.13, bf16[48,2176]{1,0:T(8,128)(2,1)} %copy-done.14, ...), custom_call_target="tpu_custom_call" | custom-call | flops 1006632960 | bytes 10000000 | tf_op jit(solution)/shard_map/pallas_call | solution.py:221
  96.2 17.4 %all-gather.2.cloned.1.call-done.w_in = bf16[2048,1280]{1,0:T(8,128)(2,1)} async-done(((bf16[128,1280]{1,0:T(8,128)(2,1)}), bf16[2048,1280]{1,0:T(8,128)(2,1)}) %all-gather.2.cloned.1.call-update) | async-done | bytes 5242896 | tf_op jit(solution)/shard_map/all_gather | solution.py:249
  113.7 6.1 %shard_map.95 = (f32[192,1280]{1,0:T(8,128)}, f32[192,1280]{1,0:T(8,128)}) custom-call(s32[4]{0:T(128)} %pad_add_fusion.place, bf16[384,2176]{1,0:T(8,128)(2,1)} %get-tuple-element.29.tok.tok_in, bf16[2048,1280]{1,0:T(8,128)(2,1)} %all-gather.2.cloned.1.call-done.w_in), custom_call_target="tpu_custom_call" | custom-call | flops 2013265920 | bytes 10000000 | tf_op jit(solution)/shard_map/pallas_call | solution.py:221
  119.8 3.7 %collective-permute-start.15 = (f32[192,1280]{1,0:T(8,128)}, f32[192,1280]{1,0:T(8,128)S(1)}, u32[]{:S(2)}, u32[]{:S(2)}) collective-permute-start(f32[192,1280]{1,0:T(8,128)} %get-tuple-element.32), channel_id=1, source_target_pairs={{0,16},{16,0},{1,17},{17,1},{2,18},{18,2},{3,19},{19,3},{4,20},{20... | collective-permute-start | bytes 2949128 | tf_op jit(solution)/shard_map/ppermute | solution.py:310
  123.6 1.9 collective-permute-start.16
  126.2 1.5 collective-permute-done.16.side_partner
  128.7 1.2 copy-done.1
  129.9 1.2 copy-done.3
  133.1 5.2 %shard_map.96 = (f32[32,1,640]{2,1,0:T(1,128)}, f32[32,192]{1,0:T(8,128)S(1)}, bf16[4,192,896]{2,1,0:T(8,128)(2,1)S(1)}) custom-call(s32[4]{0:T(128)S(1)} %copy-done.6, f32[192,1280]{1,0:T(8,128)S(1)} %copy-done.3, f32[192,640]{1,0:T(8,128)S(1)} %copy-done.5, f32[192,640]{1,0:T(8,128)} %collective-permute-done.16.side_partner, ...), custom_call_target="tpu_custom_call" | custom-call | flops 176160768 | bytes 10000000 | tf_op jit(solution)/shard_map/pallas_call | solution.py:221
  138.3 13.6 %all-to-all-start = ((f32[32,1,640]{2,1,0:T(1,128)}), f32[32,1,640]{2,1,0:T(1,128)S(1)}, u32[]{:S(2)}, u32[]{:S(2)}) async-start(f32[32,1,640]{2,1,0:T(1,128)} %get-tuple-element.40), calls=%async_computation | async-start | bytes 163840 | tf_op jit(solution)/shard_map/all_to_all | solution.py:323
  151.9 8.0 %all-to-all-done.arrived = f32[32,1,640]{2,1,0:T(1,128)S(1)} async-done(((f32[32,1,640]{2,1,0:T(1,128)}), f32[32,1,640]{2,1,0:T(1,128)S(1)}, u32[]{:S(2)}, u32[]{:S(2)}) %all-to-all-start) | async-done | bytes 81952 | tf_op jit(solution)/shard_map/all_to_all | solution.py:323
  160.0 2.1 %shard_map.97 = (f32[32,1,1280]{2,1,0:T(1,128)S(1)}, f32[8,128]{1,0:T(8,128)S(1)}) custom-call(s32[4]{0:T(128)S(1)} %copy-done.6, f32[32,1,640]{2,1,0:T(1,128)S(1)} %all-to-all-done.arrived, bf16[2,128,192]{2,1,0:T(8,128)(2,1)S(1)} %fusion.4.signs, f32[2,1,128]{2,1,0:T(1,128)S(1)} %bitcast.45, f32[32,192]{1,0:T(8,128)S(1)} %get-tuple-element.41.low_t, ...), custom_call_target="tpu_custom_call" | custom-call | flops 12582912 | bytes 10000000 | tf_op jit(solution)/shard_map/pallas_call | solution.py:221
  162.1 18.4 %all_to_all.15 = f32[32,1,1280]{2,1,0:T(1,128)S(1)} all-to-all(f32[32,1,1280]{2,1,0:T(1,128)S(1)} %get-tuple-element.43), channel_id=1, replica_groups=mesh['yh'=4,'x'=4,'c'=2,'z'=8,'yl'=2] {'yh','x','c'}, dimensions={0} | all-to-all | bytes 327680 | tf_op jit(solution)/shard_map/all_to_all | solution.py:337
  181.3 3.5 %all-to-all-start.2 = ((f32[16,2,128]{2,1,0:T(2,128)}), f32[16,2,128]{2,1,0:T(2,128)S(1)}, u32[]{:S(2)}, u32[]{:S(2)}) async-start(f32[16,2,128]{2,1,0:T(2,128)} %broadcast_in_dim.32), calls=%async_computation.2 | async-start | bytes 32768 | tf_op jit(solution)/shard_map/all_to_all | solution.py:339
  187.7 4.4 %all-to-all-done.2 = f32[16,2,128]{2,1,0:T(2,128)S(1)} async-done(((f32[16,2,128]{2,1,0:T(2,128)}), f32[16,2,128]{2,1,0:T(2,128)S(1)}, u32[]{:S(2)}, u32[]{:S(2)}) %all-to-all-start.2) | async-done | bytes 16416 | tf_op jit(solution)/shard_map/all_to_all | solution.py:339
  (115 shorter events, 18.7 us)
Async XLA Ops:
  7.2 21.2 %copy-start.19 = (bf16[12,4096]{1,0:T(8,128)(2,1)S(1)}, bf16[12,4096]{1,0:T(8,128)(2,1)}, u32[]{:S(2)}) copy-start(bf16[12,4096]{1,0:T(8,128)(2,1)} %param.7) | copy-start | bytes 294916
  7.2 106.5 %all-gather.2.cloned.1.call-start = ((), (), s32[]{:S(2)}) async-start(), calls=%async_computation.3 | async-start | bytes 5570560 | tf_op jit(solution)/shard_map/all_gather | solution.py:249
  8.3 23.8 %copy-start.12 = (bf16[4096,32]{0,1:T(8,128)(2,1)S(1)}, bf16[4096,32]{0,1:T(8,128)(2,1)}, u32[]{:S(2)}) copy-start(bf16[4096,32]{0,1:T(8,128)(2,1)} %param.11) | copy-start | bytes 786436
  13.8 23.0 %collective-permute-start.8 = (bf16[144,512]{1,0:T(8,128)(2,1)S(1)}, bf16[144,512]{1,0:T(8,128)(2,1)S(1)}, u32[]{:S(2)}, u32[]{:S(2)}) collective-permute-start(bf16[144,512]{1,0:T(8,128)(2,1)S(1)} %concatenate.57), channel_id=1, source_target_pairs={{128,0},{256,128},{384,256},{0,384},{129,1},{257,129},{385,257},{1... | collective-permute-start | bytes 442376 | tf_op jit(solution)/shard_map/ppermute | solution.py:239
  20.5 16.3 %collective-permute-start.9 = (bf16[144,512]{1,0:T(8,128)(2,1)S(1)}, bf16[144,512]{1,0:T(8,128)(2,1)S(1)}, u32[]{:S(2)}, u32[]{:S(2)}) collective-permute-start(bf16[144,512]{1,0:T(8,128)(2,1)S(1)} %concatenate.57), channel_id=1, source_target_pairs={{256,0},{384,128},{0,256},{128,384},{257,1},{385,129},{1,257},{129... | collective-permute-start | bytes 442376 | tf_op jit(solution)/shard_map/ppermute | solution.py:239
  24.1 12.8 %collective-permute-start.10 = (bf16[144,512]{1,0:T(8,128)(2,1)S(1)}, bf16[144,512]{1,0:T(8,128)(2,1)S(1)}, u32[]{:S(2)}, u32[]{:S(2)}) collective-permute-start(bf16[144,512]{1,0:T(8,128)(2,1)S(1)} %concatenate.57), channel_id=1, source_target_pairs={{384,0},{0,128},{128,256},{256,384},{385,1},{1,129},{129,257},{257... | collective-permute-start | bytes 442376 | tf_op jit(solution)/shard_map/ppermute | solution.py:239
  28.7 5.7 %collective-permute-start = (bf16[12,2176]{1,0:T(8,128)(2,1)S(1)}, bf16[12,2176]{1,0:T(8,128)(2,1)S(1)}, u32[]{:S(2)}, u32[]{:S(2)}) collective-permute-start(bf16[12,2176]{1,0:T(8,128)(2,1)S(1)} %get-tuple-element.65), channel_id=1, source_target_pairs={{0,16},{16,0},{1,17},{17,1},{2,18},{18,2},{3,19},{19,3},{4,20},{20... | collective-permute-start | bytes 156680 | tf_op jit(solution)/shard_map/ppermute | solution.py:255
  33.4 25.6 %copy-start.20 = (bf16[32,896]{1,0:T(8,128)(2,1)S(1)}, bf16[32,896]{1,0:T(8,128)(2,1)}, u32[]{:S(2)}) copy-start(bf16[32,896]{1,0:T(8,128)(2,1)} %param.12) | copy-start | bytes 172036
  33.4 26.3 %copy-start.21 = (bf16[896]{0:T(1024)(128)(2,1)S(1)}, bf16[896]{0:T(1024)(128)(2,1)}, u32[]{:S(2)}) copy-start(bf16[896]{0:T(1024)(128)(2,1)} %param.13) | copy-start | bytes 5380
  34.4 11.8 %collective-permute-start.1 = (bf16[24,2176]{1,0:T(8,128)(2,1)S(1)}, bf16[24,2176]{1,0:T(8,128)(2,1)S(1)}, u32[]{:S(2)}, u32[]{:S(2)}) collective-permute-start(bf16[24,2176]{1,0:T(8,128)(2,1)S(1)} %maximum_select_fusion.2), channel_id=1, source_target_pairs={{0,1},{1,0},{2,3},{3,2},{4,5},{5,4},{6,7},{7,6},{8,9},{9,8},{10,11... | collective-permute-start | bytes 313352 | tf_op jit(solution)/shard_map/ppermute | solution.py:39
  36.9 53.5 %copy-start.7 = (bf16[576,512]{1,0:T(8,128)(2,1)}, bf16[576,512]{1,0:T(8,128)(2,1)S(1)}, u32[]{:S(2)}) copy-start(bf16[576,512]{1,0:T(8,128)(2,1)S(1)} %constant_dynamic-update-slice_fusion.s0) | copy-start | bytes 1769476
  36.9 44.9 %collective-permute-start.11 = (bf16[576,512]{1,0:T(8,128)(2,1)S(1)}, bf16[576,512]{1,0:T(8,128)(2,1)S(1)}, u32[]{:S(2)}, u32[]{:S(2)}) collective-permute-start(bf16[576,512]{1,0:T(8,128)(2,1)S(1)} %constant_dynamic-update-slice_fusion.s0), channel_id=1, source_target_pairs={{32,0},{64,32},{96,64},{0,96},{33,1},{65,33},{97,65},{1,97},{34,2}... | collective-permute-start | bytes 1769480 | tf_op jit(solution)/shard_map/ppermute | solution.py:239
  41.3 34.5 %collective-permute-start.13 = (bf16[576,512]{1,0:T(8,128)(2,1)S(1)}, bf16[576,512]{1,0:T(8,128)(2,1)S(1)}, u32[]{:S(2)}, u32[]{:S(2)}) collective-permute-start(bf16[576,512]{1,0:T(8,128)(2,1)S(1)} %constant_dynamic-update-slice_fusion.s0), channel_id=1, source_target_pairs={{64,0},{96,32},{0,64},{32,96},{65,1},{97,33},{1,65},{33,97},{66,2}... | collective-permute-start | bytes 1769480 | tf_op jit(solution)/shard_map/ppermute | solution.py:239
  43.7 37.3 %collective-permute-start.14 = (bf16[576,512]{1,0:T(8,128)(2,1)S(1)}, bf16[576,512]{1,0:T(8,128)(2,1)S(1)}, u32[]{:S(2)}, u32[]{:S(2)}) collective-permute-start(bf16[576,512]{1,0:T(8,128)(2,1)S(1)} %constant_dynamic-update-slice_fusion.s0), channel_id=1, source_target_pairs={{96,0},{0,32},{32,64},{64,96},{97,1},{1,33},{33,65},{65,97},{98,2}... | collective-permute-start | bytes 1769480 | tf_op jit(solution)/shard_map/ppermute | solution.py:239
  46.3 44.0 %copy-start.8 = (bf16[2,24,2176]{2,1,0:T(8,128)(2,1)}, bf16[2,24,2176]{2,1,0:T(8,128)(2,1)S(1)}, u32[]{:S(2)}) copy-start(bf16[2,24,2176]{2,1,0:T(8,128)(2,1)S(1)} %maximum_select_fusion) | copy-start | bytes 626692
  46.3 14.3 %collective-permute-start.2 = (bf16[48,2176]{1,0:T(8,128)(2,1)S(1)}, bf16[48,2176]{1,0:T(8,128)(2,1)S(1)}, u32[]{:S(2)}, u32[]{:S(2)}) collective-permute-start(bf16[48,2176]{1,0:T(8,128)(2,1)S(1)} %bitcast.48), channel_id=1, source_target_pairs={{0,2},{2,4},{4,6},{6,8},{8,10},{10,12},{12,14},{14,0},{1,3},{3,5},... | collective-permute-start | bytes 626696 | tf_op jit(solution)/shard_map/ppermute | solution.py:234
  50.3 12.2 %collective-permute-start.3 = (bf16[48,2176]{1,0:T(8,128)(2,1)S(1)}, bf16[48,2176]{1,0:T(8,128)(2,1)S(1)}, u32[]{:S(2)}, u32[]{:S(2)}) collective-permute-start(bf16[48,2176]{1,0:T(8,128)(2,1)S(1)} %bitcast.49), channel_id=1, source_target_pairs={{0,14},{2,0},{4,2},{6,4},{8,6},{10,8},{12,10},{14,12},{1,15},{3,1}... | collective-permute-start | bytes 626696 | tf_op jit(solution)/shard_map/ppermute | solution.py:234
  60.6 29.8 %copy-start.13 = (bf16[48,2176]{1,0:T(8,128)(2,1)}, bf16[48,2176]{1,0:T(8,128)(2,1)S(1)}, u32[]{:S(2)}) copy-start(bf16[48,2176]{1,0:T(8,128)(2,1)S(1)} %collective-permute-done.2.r1) | copy-start | bytes 626692
  60.6 8.0 %collective-permute-start.4 = (bf16[48,2176]{1,0:T(8,128)(2,1)S(1)}, bf16[48,2176]{1,0:T(8,128)(2,1)S(1)}, u32[]{:S(2)}, u32[]{:S(2)}) collective-permute-start(bf16[48,2176]{1,0:T(8,128)(2,1)S(1)} %collective-permute-done.2.r1), channel_id=1, source_target_pairs={{0,2},{2,4},{4,6},{6,8},{8,10},{10,12},{12,14},{14,0},{1,3},{3,5},... | collective-permute-start | bytes 626696 | tf_op jit(solution)/shard_map/ppermute | solution.py:234
  62.5 27.9 %copy-start.14 = (bf16[48,2176]{1,0:T(8,128)(2,1)}, bf16[48,2176]{1,0:T(8,128)(2,1)S(1)}, u32[]{:S(2)}) copy-start(bf16[48,2176]{1,0:T(8,128)(2,1)S(1)} %collective-permute-done.3.l1) | copy-start | bytes 626692
  62.5 11.3 %collective-permute-start.5 = (bf16[48,2176]{1,0:T(8,128)(2,1)S(1)}, bf16[48,2176]{1,0:T(8,128)(2,1)S(1)}, u32[]{:S(2)}, u32[]{:S(2)}) collective-permute-start(bf16[48,2176]{1,0:T(8,128)(2,1)S(1)} %collective-permute-done.3.l1), channel_id=1, source_target_pairs={{0,14},{2,0},{4,2},{6,4},{8,6},{10,8},{12,10},{14,12},{1,15},{3,1}... | collective-permute-start | bytes 626696 | tf_op jit(solution)/shard_map/ppermute | solution.py:234
  68.6 13.2 %copy-start.15 = (bf16[48,2176]{1,0:T(8,128)(2,1)}, bf16[48,2176]{1,0:T(8,128)(2,1)S(1)}, u32[]{:S(2)}) copy-start(bf16[48,2176]{1,0:T(8,128)(2,1)S(1)} %collective-permute-done.4.r2) | copy-start | bytes 626692
  68.6 21.7 %collective-permute-start.12 = (bf16[48,2176]{1,0:T(8,128)(2,1)S(1)}, bf16[48,2176]{1,0:T(8,128)(2,1)}, u32[]{:S(2)}, u32[]{:S(2)}) collective-permute-start(bf16[48,2176]{1,0:T(8,128)(2,1)S(1)} %bitcast.50), channel_id=1, source_target_pairs={{0,8},{2,10},{4,12},{6,14},{8,0},{10,2},{12,4},{14,6},{1,9},{3,11}... | collective-permute-start | bytes 626696 | tf_op jit(solution)/shard_map/ppermute | solution.py:234
  73.9 11.8 %collective-permute-start.6 = (bf16[48,2176]{1,0:T(8,128)(2,1)S(1)}, bf16[48,2176]{1,0:T(8,128)(2,1)S(1)}, u32[]{:S(2)}, u32[]{:S(2)}) collective-permute-start(bf16[48,2176]{1,0:T(8,128)(2,1)S(1)} %collective-permute-done.4.r2), channel_id=1, source_target_pairs={{0,2},{2,4},{4,6},{6,8},{8,10},{10,12},{12,14},{14,0},{1,3},{3,5},... | collective-permute-start | bytes 626696 | tf_op jit(solution)/shard_map/ppermute | solution.py:234
  75.8 14.6 %copy-start.10 = (bf16[576,512]{1,0:T(8,128)(2,1)}, bf16[576,512]{1,0:T(8,128)(2,1)S(1)}, u32[]{:S(2)}) copy-start(bf16[576,512]{1,0:T(8,128)(2,1)S(1)} %collective-permute-done.13.s2) | copy-start | bytes 1769476
  75.8 9.9 %collective-permute-start.7 = (bf16[48,2176]{1,0:T(8,128)(2,1)S(1)}, bf16[48,2176]{1,0:T(8,128)(2,1)S(1)}, u32[]{:S(2)}, u32[]{:S(2)}) collective-permute-start(bf16[48,2176]{1,0:T(8,128)(2,1)S(1)} %collective-permute-done.5.l2), channel_id=1, source_target_pairs={{0,14},{2,0},{4,2},{6,4},{8,6},{10,8},{12,10},{14,12},{1,15},{3,1}... | collective-permute-start | bytes 626696 | tf_op jit(solution)/shard_map/ppermute | solution.py:234
  113.7 11.9 %copy-start = (bf16[384,2176]{1,0:T(8,128)(2,1)S(1)}, bf16[384,2176]{1,0:T(8,128)(2,1)}, u32[]{:S(2)}) copy-start(bf16[384,2176]{1,0:T(8,128)(2,1)} %get-tuple-element.29.tok.tok_in) | copy-start | bytes 5013508
  113.7 15.0 %copy-start.6 = (s32[4]{0:T(128)S(1)}, s32[4]{0:T(128)}, u32[]{:S(2)}) copy-start(s32[4]{0:T(128)} %pad_add_fusion.place) | copy-start | bytes 52
  119.8 7.9 %collective-permute-start.15 = (f32[192,1280]{1,0:T(8,128)}, f32[192,1280]{1,0:T(8,128)S(1)}, u32[]{:S(2)}, u32[]{:S(2)}) collective-permute-start(f32[192,1280]{1,0:T(8,128)} %get-tuple-element.32), channel_id=1, source_target_pairs={{0,16},{16,0},{1,17},{17,1},{2,18},{18,2},{3,19},{19,3},{4,20},{20... | collective-permute-start | bytes 2949128 | tf_op jit(solution)/shard_map/ppermute | solution.py:310
  123.6 4.1 %collective-permute-start.16 = (f32[192,640]{1,0:T(8,128)}, f32[192,640]{1,0:T(8,128)}, u32[]{:S(2)}, u32[]{:S(2)}) collective-permute-start(f32[192,640]{1,0:T(8,128)} %get-tuple-element.34), channel_id=1, source_target_pairs={{0,16},{16,0},{1,17},{17,1},{2,18},{18,2},{3,19},{19,3},{4,20},{20... | collective-permute-start | bytes 1474568 | tf_op jit(solution)/shard_map/ppermute | solution.py:291
  138.3 21.7 %all-to-all-start = ((f32[32,1,640]{2,1,0:T(1,128)}), f32[32,1,640]{2,1,0:T(1,128)S(1)}, u32[]{:S(2)}, u32[]{:S(2)}) async-start(f32[32,1,640]{2,1,0:T(1,128)} %get-tuple-element.40), calls=%async_computation | async-start | bytes 163840 | tf_op jit(solution)/shard_map/all_to_all | solution.py:323
  181.3 10.8 %all-to-all-start.2 = ((f32[16,2,128]{2,1,0:T(2,128)}), f32[16,2,128]{2,1,0:T(2,128)S(1)}, u32[]{:S(2)}, u32[]{:S(2)}) async-start(f32[16,2,128]{2,1,0:T(2,128)} %broadcast_in_dim.32), calls=%async_computation.2 | async-start | bytes 32768 | tf_op jit(solution)/shard_map/all_to_all | solution.py:339
  (10 other events, 36.6 us)
Sparse Core Ops, SparseCore 0:
  11.0 102.6 all-gather.1

commit v11 on v10

--- a/solution.py
+++ b/solution.py
@@ -122,13 +122,23 @@
     )
 
 
-def score(place, partner, side_near, side_partner, b_gate, b_up, readout, signs, count, near_in, message, low_t, k_out, k,
-          near, sems):
-    near_copy = pltpu.make_async_copy(near_in, near, sems.at[4])
-    near_copy.start()
+def score(place, partner, readout, count, near_in, side_in, side_partner_in, gate_in, up_in, signs_in, message, low_t,
+          k_out, k, near, side_near, side_partner, b_gate, b_up, signs, sems):
+    fetches = [
+        pltpu.make_async_copy(source, target, sems.at[4 + n])
+        for n, (source, target) in enumerate(
+            (
+                (side_in, side_near), (side_partner_in, side_partner), (near_in, near),
+                (gate_in, b_gate), (up_in, b_up), (signs_in, signs),
+            )
+        )
+    ]
+    for copy in fetches:
+        copy.start()
+    for copy in fetches:
+        copy.wait()
     side = side_near[...] + side_partner[...]
     low_b = side[:, 2 * SIDE :].astype(BF16)
-    near_copy.wait()
     main = near[...] + partner[...]
     gate_ref = jnp.concatenate([main[:, 0:MAIN], side[:, 0:SIDE]], axis=1)
     up_ref = jnp.concatenate([main[:, MAIN:], side[:, SIDE : 2 * SIDE]], axis=1)
@@ -268,8 +278,8 @@
     stacks = [stack] + [fetch(stack, "x", j) for j in (1, 2, 3)]
     for step in range(2):
         ring += [along(ring[-2], "z", 1), along(ring[-1], "z", -1)]
-    ring.append(along(four, "z", 4))
-    ring[5], ring[6], stacks[1] = lax.optimization_barrier((ring[5], ring[6], stacks[1]))
+    ring.append(along(ring[-2], "z", 1))
+    ring[7], *stacks[1:] = lax.optimization_barrier((ring[7], *stacks[1:]))
     count = sum(jnp.sum(p.reshape(4, PIECE, 2 * SIDE)[:, SLICE, 0].astype(F32)) for p in stacks)
     count_lanes = jnp.where(jnp.arange(LANES) == 64, count, 0.0).reshape(1, LANES)
 
@@ -303,22 +313,27 @@
     signs = chosen.astype(BF16) - rejected.astype(BF16)
     valid = (jnp.any(chosen, axis=2) & jnp.any(rejected, axis=2)).astype(F32).reshape(2, 1, LANES)
 
-    w_main, b_gate, b_up, read, count_lanes = lax.optimization_barrier(
-        (w_main, b_gate, b_up, read, count_lanes)
+    w_main, side, side_partner, b_gate, b_up, read, signs, valid, count_lanes = lax.optimization_barrier(
+        (w_main, side, side_partner, b_gate, b_up, read, signs, valid, count_lanes)
     )
     far, near = products(place, tok, w_main)
     partner = lax.ppermute(far, "c", SWAP)
     message, low_t, k = kernel(
         score,
         [((2 * RANK, 1, 5 * LANES), F32), ((2 * RANK, GROUP), F32), ((4, GROUP, UNITS), BF16)],
-        (place, partner, side, side_partner, b_gate, b_up, read, signs, count_lanes, near),
-        8 * GROUP * UNITS * LANES, 16,
+        (place, partner, read, count_lanes, near, side, side_partner, b_gate, b_up, signs),
+        8 * GROUP * UNITS * LANES, 56,
         scratch=[
             pltpu.VMEM((4, GROUP, UNITS), BF16),
             pltpu.VMEM((GROUP, 2 * MAIN), F32),
-            pltpu.SemaphoreType.DMA((5,)),
+            pltpu.VMEM((GROUP, 2 * SIDE + LANES), F32),
+            pltpu.VMEM((GROUP, 2 * SIDE + LANES), F32),
+            pltpu.VMEM((LANES, UNITS), BF16),
+            pltpu.VMEM((LANES, UNITS), BF16),
+            pltpu.VMEM((2, LANES, GROUP), BF16),
+            pltpu.SemaphoreType.DMA((10,)),
         ],
-        in_hbm=1, out_hbm=1,
+        in_hbm=6, out_hbm=1,
     )
     arrived = lax.all_to_all(message, ("c", "z", "yl"), split_axis=0, concat_axis=0)
     outgoing, pair_total = kernel(

time: 202 us -> 209 us (1.035)
  blocking collectives: 18.4 us -> 47.4 us
  waiting for transfers between devices: 36.5 us -> 20.1 us
  starting transfers between devices: 83 us -> 71.8 us
  other arithmetic: 6.38 us -> 10.3 us
    all_to_all x0 -> x1, blocking collectives: none -> 25 us  [on_device(): lax.all_to_all(message, ('c', 'z', 'yl'), split_axis=0, concat_axis=0)]
    all_gather x1, waiting for transfers between devices: 17.4 us -> 0.01 us  [on_device(): w_main = lax.all_gather(main, ('yh', 'x'), axis=0, tiled=True)]
    all_to_all x1 -> x0, starting transfers between devices: 13.6 us -> none  [on_device(): lax.all_to_all(message, ('c', 'z', 'yl'), split_axis=0, concat_axis=0)]
    all_to_all x1 -> x0, waiting for transfers between devices: 8.02 us -> none  [on_device(): lax.all_to_all(message, ('c', 'z', 'yl'), split_axis=0, concat_axis=0)]
    ppermute x1, waiting for transfers between devices: 0.01 us -> 7 us  [swapped(): far = lax.ppermute(value, axis, SWAP)]
    ppermute x6, waiting for transfers between devices: 0.02 us -> 5.03 us  [fetch(): return lax.ppermute(value, axis, [((i + k) % n, i) for i in range(n)])]
    ppermute x1, starting transfers between devices: 1.92 us -> 6.03 us  [on_device(): side_partner = lax.ppermute(side_far, 'c', SWAP)]
    ppermute x7, waiting for transfers between devices: 5.03 us -> 0.96 us  [along(): return lax.ppermute(value, axis, [(i, (i + k) % n) for i in range(n)])]
  transfers between devices with their start and end apart: 20 -> 19, of which waited for: 7 -> 6; matrix products, arithmetic and copies ran while one was open for 6% -> 9% of each run, Pallas kernels for 3% -> 3%
where the time goes in v11:
time: 209 us; the launch traced here: 207 us
  starting transfers between devices  71.8 us (34%)
  blocking collectives  47.4 us (23%)
  between operations  22.3 us (11%)
  waiting for transfers between devices  20.1 us (10%)
  Pallas kernels  20.1 us (10%)
  local copies, waits for them, and re-layouts  15.2 us (7%)
  other arithmetic  10.3 us (5%)
    ppermute x7, starting transfers between devices, along(): return lax.ppermute(value, axis, [(i, (i + k) % n) for i in range(n)])  31.1 us
    all_to_all x1, blocking collectives, on_device(): lax.all_to_all(message, ('c', 'z', 'yl'), split_axis=0, concat_axis=0)  25 us
    ppermute x6, starting transfers between devices, fetch(): return lax.ppermute(value, axis, [((i + k) % n, i) for i in range(n)])  23.6 us
    all_to_all x1, blocking collectives, on_device(): lax.all_to_all(outgoing, DP, split_axis=0, concat_axis=0)  22.4 us
    pallas_call x4, Pallas kernels, kernel(): pl.pallas_call(function, out_shape=tuple((jax.ShapeDtypeStruct(*s) for s...  20.1 us
    ppermute x1, waiting for transfers between devices, swapped(): far = lax.ppermute(value, axis, SWAP)  7 us
    ppermute x1, starting transfers between devices, on_device(): side_partner = lax.ppermute(side_far, 'c', SWAP)  6.03 us
    unnamed x53, local copies, waits for them, and re-layouts  5.32 us
  transfers between devices with their start and end apart: 19, of which 6 were waited for; matrix products, arithmetic and copies ran while one was open for 9% of the time, Pallas kernels for 3%

profile of v11, /device:TPU:1, one launch (start us, length us, event | category | flops | bytes accessed | tf_op | source)
XLA Modules:
  0.0 207.3 jit_solution(5678056806163019989)
XLA Ops:
  13.9 6.7 %collective-permute-start.9 = (bf16[144,512]{1,0:T(8,128)(2,1)S(1)}, bf16[144,512]{1,0:T(8,128)(2,1)S(1)}, u32[]{:S(2)}, u32[]{:S(2)}) collective-permute-start(bf16[144,512]{1,0:T(8,128)(2,1)S(1)} %concatenate.57), channel_id=1, source_target_pairs={{128,0},{256,128},{384,256},{0,384},{129,1},{257,129},{385,257},{1... | collective-permute-start | bytes 442376 | tf_op jit(solution)/shard_map/ppermute | solution.py:249
  20.6 3.5 %collective-permute-start.10 = (bf16[144,512]{1,0:T(8,128)(2,1)S(1)}, bf16[144,512]{1,0:T(8,128)(2,1)S(1)}, u32[]{:S(2)}, u32[]{:S(2)}) collective-permute-start(bf16[144,512]{1,0:T(8,128)(2,1)S(1)} %concatenate.57), channel_id=1, source_target_pairs={{256,0},{384,128},{0,256},{128,384},{257,1},{385,129},{1,257},{129... | collective-permute-start | bytes 442376 | tf_op jit(solution)/shard_map/ppermute | solution.py:249
  24.2 4.2 %collective-permute-start.11 = (bf16[144,512]{1,0:T(8,128)(2,1)S(1)}, bf16[144,512]{1,0:T(8,128)(2,1)S(1)}, u32[]{:S(2)}, u32[]{:S(2)}) collective-permute-start(bf16[144,512]{1,0:T(8,128)(2,1)S(1)} %concatenate.57), channel_id=1, source_target_pairs={{384,0},{0,128},{128,256},{256,384},{385,1},{1,129},{129,257},{257... | collective-permute-start | bytes 442376 | tf_op jit(solution)/shard_map/ppermute | solution.py:249
  28.8 3.4 %collective-permute-start = (bf16[12,2176]{1,0:T(8,128)(2,1)S(1)}, bf16[12,2176]{1,0:T(8,128)(2,1)S(1)}, u32[]{:S(2)}, u32[]{:S(2)}) collective-permute-start(bf16[12,2176]{1,0:T(8,128)(2,1)S(1)} %get-tuple-element.75), channel_id=1, source_target_pairs={{0,16},{16,0},{1,17},{17,1},{2,18},{18,2},{3,19},{19,3},{4,20},{20... | collective-permute-start | bytes 156680 | tf_op jit(solution)/shard_map/ppermute | solution.py:265
  34.2 2.3 %collective-permute-start.1 = (bf16[24,2176]{1,0:T(8,128)(2,1)S(1)}, bf16[24,2176]{1,0:T(8,128)(2,1)S(1)}, u32[]{:S(2)}, u32[]{:S(2)}) collective-permute-start(bf16[24,2176]{1,0:T(8,128)(2,1)S(1)} %maximum_select_fusion.2), channel_id=1, source_target_pairs={{0,1},{1,0},{2,3},{3,2},{4,5},{5,4},{6,7},{7,6},{8,9},{9,8},{10,11... | collective-permute-start | bytes 313352 | tf_op jit(solution)/shard_map/ppermute | solution.py:39
  36.6 7.0 %collective-permute-done.1 = bf16[24,2176]{1,0:T(8,128)(2,1)S(1)} collective-permute-done((bf16[24,2176]{1,0:T(8,128)(2,1)S(1)}, bf16[24,2176]{1,0:T(8,128)(2,1)S(1)}, u32[]{:S(2)}, u32[]{:S(2)}) %collective-permute-start.1) | collective-permute-done | bytes 104480 | tf_op jit(solution)/shard_map/ppermute | solution.py:39
  43.7 5.4 %collective-permute-start.2 = (bf16[48,2176]{1,0:T(8,128)(2,1)S(1)}, bf16[48,2176]{1,0:T(8,128)(2,1)S(1)}, u32[]{:S(2)}, u32[]{:S(2)}) collective-permute-start(bf16[48,2176]{1,0:T(8,128)(2,1)S(1)} %bitcast.48), channel_id=1, source_target_pairs={{0,2},{2,4},{4,6},{6,8},{8,10},{10,12},{12,14},{14,0},{1,3},{3,5},... | collective-permute-start | bytes 626696 | tf_op jit(solution)/shard_map/ppermute | solution.py:244
  49.2 4.1 %collective-permute-start.12 = (bf16[576,512]{1,0:T(8,128)(2,1)S(1)}, bf16[576,512]{1,0:T(8,128)(2,1)S(1)}, u32[]{:S(2)}, u32[]{:S(2)}) collective-permute-start(bf16[576,512]{1,0:T(8,128)(2,1)S(1)} %constant_dynamic-update-slice_fusion.s0), channel_id=1, source_target_pairs={{32,0},{64,32},{96,64},{0,96},{33,1},{65,33},{97,65},{1,97},{34,2}... | collective-permute-start | bytes 1769480 | tf_op jit(solution)/shard_map/ppermute | solution.py:249
  53.3 2.4 %collective-permute-start.13 = (bf16[576,512]{1,0:T(8,128)(2,1)S(1)}, bf16[576,512]{1,0:T(8,128)(2,1)S(1)}, u32[]{:S(2)}, u32[]{:S(2)}) collective-permute-start(bf16[576,512]{1,0:T(8,128)(2,1)S(1)} %constant_dynamic-update-slice_fusion.s0), channel_id=1, source_target_pairs={{64,0},{96,32},{0,64},{32,96},{65,1},{97,33},{1,65},{33,97},{66,2}... | collective-permute-start | bytes 1769480 | tf_op jit(solution)/shard_map/ppermute | solution.py:249
  55.8 2.5 %collective-permute-start.14 = (bf16[576,512]{1,0:T(8,128)(2,1)S(1)}, bf16[576,512]{1,0:T(8,128)(2,1)S(1)}, u32[]{:S(2)}, u32[]{:S(2)}) collective-permute-start(bf16[576,512]{1,0:T(8,128)(2,1)S(1)} %constant_dynamic-update-slice_fusion.s0), channel_id=1, source_target_pairs={{96,0},{0,32},{32,64},{64,96},{97,1},{1,33},{33,65},{65,97},{98,2}... | collective-permute-start | bytes 1769480 | tf_op jit(solution)/shard_map/ppermute | solution.py:249
  58.3 9.9 %collective-permute-start.3 = (bf16[48,2176]{1,0:T(8,128)(2,1)S(1)}, bf16[48,2176]{1,0:T(8,128)(2,1)S(1)}, u32[]{:S(2)}, u32[]{:S(2)}) collective-permute-start(bf16[48,2176]{1,0:T(8,128)(2,1)S(1)} %bitcast.49), channel_id=1, source_target_pairs={{0,14},{2,0},{4,2},{6,4},{8,6},{10,8},{12,10},{14,12},{1,15},{3,1}... | collective-permute-start | bytes 626696 | tf_op jit(solution)/shard_map/ppermute | solution.py:244
  68.3 1.9 collective-permute-start.4
  71.1 1.5 pad.19.gate_in
  73.9 4.6 %collective-permute-start.5 = (bf16[48,2176]{1,0:T(8,128)(2,1)S(1)}, bf16[48,2176]{1,0:T(8,128)(2,1)S(1)}, u32[]{:S(2)}, u32[]{:S(2)}) collective-permute-start(bf16[48,2176]{1,0:T(8,128)(2,1)S(1)} %collective-permute-done.3.l1), channel_id=1, source_target_pairs={{0,14},{2,0},{4,2},{6,4},{8,6},{10,8},{12,10},{14,12},{1,15},{3,1}... | collective-permute-start | bytes 626696 | tf_op jit(solution)/shard_map/ppermute | solution.py:244
  78.5 1.9 collective-permute-start.6
  81.2 5.4 %collective-permute-start.7 = (bf16[48,2176]{1,0:T(8,128)(2,1)S(1)}, bf16[48,2176]{1,0:T(8,128)(2,1)S(1)}, u32[]{:S(2)}, u32[]{:S(2)}) collective-permute-start(bf16[48,2176]{1,0:T(8,128)(2,1)S(1)} %collective-permute-done.5.l2), channel_id=1, source_target_pairs={{0,14},{2,0},{4,2},{6,4},{8,6},{10,8},{12,10},{14,12},{1,15},{3,1}... | collective-permute-start | bytes 626696 | tf_op jit(solution)/shard_map/ppermute | solution.py:244
  86.8 1.9 collective-permute-start.8
  89.9 5.0 %collective-permute-done.14.s3 = bf16[576,512]{1,0:T(8,128)(2,1)S(1)} collective-permute-done((bf16[576,512]{1,0:T(8,128)(2,1)S(1)}, bf16[576,512]{1,0:T(8,128)(2,1)S(1)}, u32[]{:S(2)}, u32[]{:S(2)}) %collective-permute-start.14) | collective-permute-done | bytes 589856 | tf_op jit(solution)/shard_map/ppermute | solution.py:249
  96.5 5.8 %shard_map.94 = (f32[192,640]{1,0:T(8,128)}, f32[192,640]{1,0:T(8,128)}, bf16[384,2176]{1,0:T(8,128)(2,1)}) custom-call(s32[4]{0:T(128)} %pad_add_fusion.place, bf16[2048,128]{1,0:T(8,128)(2,1)} %pad.17.down, bf16[48,2176]{1,0:T(8,128)(2,1)} %bitcast.50, bf16[48,2176]{1,0:T(8,128)(2,1)} %copy-done.13, bf16[48,2176]{1,0:T(8,128)(2,1)} %copy-done.14, ...), custom_call_target="tpu_custom_call" | custom-call | flops 1006632960 | bytes 10000000 | tf_op jit(solution)/shard_map/pallas_call | solution.py:231
  103.5 6.0 %collective-permute-start.15 = (f32[192,640]{1,0:T(8,128)}, f32[192,640]{1,0:T(8,128)S(1)}, u32[]{:S(2)}, u32[]{:S(2)}) collective-permute-start(f32[192,640]{1,0:T(8,128)} %get-tuple-element.38), channel_id=1, source_target_pairs={{0,16},{16,0},{1,17},{17,1},{2,18},{18,2},{3,19},{19,3},{4,20},{20... | collective-permute-start | bytes 1474568 | tf_op jit(solution)/shard_map/ppermute | solution.py:301
  109.6 1.3 fusion.8
  112.2 1.3 fusion.7
  117.7 6.0 %shard_map.95 = (f32[192,1280]{1,0:T(8,128)}, f32[192,1280]{1,0:T(8,128)}) custom-call(s32[4]{0:T(128)} %pad_add_fusion.place, bf16[384,2176]{1,0:T(8,128)(2,1)} %get-tuple-element.35.tok.tok_in, bf16[2048,1280]{1,0:T(8,128)(2,1)} %all-gather.2.cloned.1.call-done.w_in), custom_call_target="tpu_custom_call" | custom-call | flops 2013265920 | bytes 10000000 | tf_op jit(solution)/shard_map/pallas_call | solution.py:231
  123.7 1.9 collective-permute-start.16
  125.6 2.7 %collective-permute-done.16.partner = f32[192,1280]{1,0:T(8,128)S(1)} collective-permute-done((f32[192,1280]{1,0:T(8,128)}, f32[192,1280]{1,0:T(8,128)S(1)}, u32[]{:S(2)}, u32[]{:S(2)}) %collective-permute-start.16) | collective-permute-done | bytes 983072 | tf_op jit(solution)/shard_map/ppermute | solution.py:320
  129.3 6.2 %shard_map.96 = (f32[32,1,640]{2,1,0:T(1,128)}, f32[32,192]{1,0:T(8,128)}, bf16[4,192,896]{2,1,0:T(8,128)(2,1)}) custom-call(s32[4]{0:T(128)} %pad_add_fusion.place, f32[192,1280]{1,0:T(8,128)} %copy-done.5, bf16[1,896]{1,0:T(2,128)(2,1)} %reshape.257.readout, f32[1,128]{1,0:T(1,128)} %compare_select_fusion.count, f32[192,1280]{1,0:T(8,128)} %get-tuple-element.43.near_in, ...), custom_call_target="tpu_custom_call" | custom-call | flops 176160768 | bytes 10000000 | tf_op jit(solution)/shard_map/pallas_call | solution.py:231
  135.5 25.0 %all_to_all.15.arrived = f32[32,1,640]{2,1,0:T(1,128)S(1)} all-to-all(f32[32,1,640]{2,1,0:T(1,128)} %get-tuple-element.49), channel_id=1, replica_groups=mesh['yh'=4,'x'=4,'c'=2,'z'=8,'yl'=2] {'c','z','yl'}, dimensions={0} | all-to-all | bytes 163840 | tf_op jit(solution)/shard_map/all_to_all | solution.py:338
  160.5 1.3 copy-done.1
  162.6 2.1 %shard_map.97 = (f32[32,1,1280]{2,1,0:T(1,128)S(1)}, f32[8,128]{1,0:T(8,128)S(1)}) custom-call(s32[4]{0:T(128)S(1)} %copy-done.4, f32[32,1,640]{2,1,0:T(1,128)S(1)} %all_to_all.15.arrived, bf16[2,128,192]{2,1,0:T(8,128)(2,1)S(1)} %copy-done.2, f32[2,1,128]{2,1,0:T(1,128)S(1)} %bitcast.45, f32[32,192]{1,0:T(8,128)S(1)} %copy-done.3, ...), custom_call_target="tpu_custom_call" | custom-call | flops 12582912 | bytes 10000000 | tf_op jit(solution)/shard_map/pallas_call | solution.py:231
  164.8 22.4 %all_to_all.16 = f32[32,1,1280]{2,1,0:T(1,128)S(1)} all-to-all(f32[32,1,1280]{2,1,0:T(1,128)S(1)} %get-tuple-element.53), channel_id=1, replica_groups=mesh['yh'=4,'x'=4,'c'=2,'z'=8,'yl'=2] {'yh','x','c'}, dimensions={0} | all-to-all | bytes 327680 | tf_op jit(solution)/shard_map/all_to_all | solution.py:352
  187.9 3.5 %all-to-all-start.2 = ((f32[16,2,128]{2,1,0:T(2,128)}), f32[16,2,128]{2,1,0:T(2,128)S(1)}, u32[]{:S(2)}, u32[]{:S(2)}) async-start(f32[16,2,128]{2,1,0:T(2,128)} %broadcast_in_dim.32), calls=%async_computation.2 | async-start | bytes 32768 | tf_op jit(solution)/shard_map/all_to_all | solution.py:354
  194.4 4.4 %all-to-all-done.2 = f32[16,2,128]{2,1,0:T(2,128)S(1)} async-done(((f32[16,2,128]{2,1,0:T(2,128)}), f32[16,2,128]{2,1,0:T(2,128)S(1)}, u32[]{:S(2)}, u32[]{:S(2)}) %all-to-all-start.2) | async-done | bytes 16416 | tf_op jit(solution)/shard_map/all_to_all | solution.py:354
  (114 shorter events, 21.1 us)
Async XLA Ops:
  7.2 21.2 %copy-start.19 = (bf16[12,4096]{1,0:T(8,128)(2,1)S(1)}, bf16[12,4096]{1,0:T(8,128)(2,1)}, u32[]{:S(2)}) copy-start(bf16[12,4096]{1,0:T(8,128)(2,1)} %param.7) | copy-start | bytes 294916
  7.2 110.5 %all-gather.2.cloned.1.call-start = ((), (), s32[]{:S(2)}) async-start(), calls=%async_computation.3 | async-start | bytes 5570560 | tf_op jit(solution)/shard_map/all_gather | solution.py:259
  8.3 23.9 %copy-start.12 = (bf16[4096,32]{0,1:T(8,128)(2,1)S(1)}, bf16[4096,32]{0,1:T(8,128)(2,1)}, u32[]{:S(2)}) copy-start(bf16[4096,32]{0,1:T(8,128)(2,1)} %param.11) | copy-start | bytes 786436
  13.9 22.7 %collective-permute-start.9 = (bf16[144,512]{1,0:T(8,128)(2,1)S(1)}, bf16[144,512]{1,0:T(8,128)(2,1)S(1)}, u32[]{:S(2)}, u32[]{:S(2)}) collective-permute-start(bf16[144,512]{1,0:T(8,128)(2,1)S(1)} %concatenate.57), channel_id=1, source_target_pairs={{128,0},{256,128},{384,256},{0,384},{129,1},{257,129},{385,257},{1... | collective-permute-start | bytes 442376 | tf_op jit(solution)/shard_map/ppermute | solution.py:249
  20.6 28.5 %collective-permute-start.10 = (bf16[144,512]{1,0:T(8,128)(2,1)S(1)}, bf16[144,512]{1,0:T(8,128)(2,1)S(1)}, u32[]{:S(2)}, u32[]{:S(2)}) collective-permute-start(bf16[144,512]{1,0:T(8,128)(2,1)S(1)} %concatenate.57), channel_id=1, source_target_pairs={{256,0},{384,128},{0,256},{128,384},{257,1},{385,129},{1,257},{129... | collective-permute-start | bytes 442376 | tf_op jit(solution)/shard_map/ppermute | solution.py:249
  24.2 25.0 %collective-permute-start.11 = (bf16[144,512]{1,0:T(8,128)(2,1)S(1)}, bf16[144,512]{1,0:T(8,128)(2,1)S(1)}, u32[]{:S(2)}, u32[]{:S(2)}) collective-permute-start(bf16[144,512]{1,0:T(8,128)(2,1)S(1)} %concatenate.57), channel_id=1, source_target_pairs={{384,0},{0,128},{128,256},{256,384},{385,1},{1,129},{129,257},{257... | collective-permute-start | bytes 442376 | tf_op jit(solution)/shard_map/ppermute | solution.py:249
  28.8 5.4 %collective-permute-start = (bf16[12,2176]{1,0:T(8,128)(2,1)S(1)}, bf16[12,2176]{1,0:T(8,128)(2,1)S(1)}, u32[]{:S(2)}, u32[]{:S(2)}) collective-permute-start(bf16[12,2176]{1,0:T(8,128)(2,1)S(1)} %get-tuple-element.75), channel_id=1, source_target_pairs={{0,16},{16,0},{1,17},{17,1},{2,18},{18,2},{3,19},{19,3},{4,20},{20... | collective-permute-start | bytes 156680 | tf_op jit(solution)/shard_map/ppermute | solution.py:265
  34.1 39.2 %copy-start.21 = (bf16[896]{0:T(1024)(128)(2,1)S(1)}, bf16[896]{0:T(1024)(128)(2,1)}, u32[]{:S(2)}) copy-start(bf16[896]{0:T(1024)(128)(2,1)} %param.13) | copy-start | bytes 5380
  34.2 9.4 %collective-permute-start.1 = (bf16[24,2176]{1,0:T(8,128)(2,1)S(1)}, bf16[24,2176]{1,0:T(8,128)(2,1)S(1)}, u32[]{:S(2)}, u32[]{:S(2)}) collective-permute-start(bf16[24,2176]{1,0:T(8,128)(2,1)S(1)} %maximum_select_fusion.2), channel_id=1, source_target_pairs={{0,1},{1,0},{2,3},{3,2},{4,5},{5,4},{6,7},{7,6},{8,9},{9,8},{10,11... | collective-permute-start | bytes 313352 | tf_op jit(solution)/shard_map/ppermute | solution.py:39
  43.7 51.3 %copy-start.7 = (bf16[2,24,2176]{2,1,0:T(8,128)(2,1)}, bf16[2,24,2176]{2,1,0:T(8,128)(2,1)S(1)}, u32[]{:S(2)}) copy-start(bf16[2,24,2176]{2,1,0:T(8,128)(2,1)S(1)} %maximum_select_fusion) | copy-start | bytes 626692
  43.7 24.5 %collective-permute-start.2 = (bf16[48,2176]{1,0:T(8,128)(2,1)S(1)}, bf16[48,2176]{1,0:T(8,128)(2,1)S(1)}, u32[]{:S(2)}, u32[]{:S(2)}) collective-permute-start(bf16[48,2176]{1,0:T(8,128)(2,1)S(1)} %bitcast.48), channel_id=1, source_target_pairs={{0,2},{2,4},{4,6},{6,8},{8,10},{10,12},{12,14},{14,0},{1,3},{3,5},... | collective-permute-start | bytes 626696 | tf_op jit(solution)/shard_map/ppermute | solution.py:244
  49.2 45.8 %copy-start.6 = (bf16[576,512]{1,0:T(8,128)(2,1)}, bf16[576,512]{1,0:T(8,128)(2,1)S(1)}, u32[]{:S(2)}) copy-start(bf16[576,512]{1,0:T(8,128)(2,1)S(1)} %constant_dynamic-update-slice_fusion.s0) | copy-start | bytes 1769476
  49.2 40.7 %collective-permute-start.12 = (bf16[576,512]{1,0:T(8,128)(2,1)S(1)}, bf16[576,512]{1,0:T(8,128)(2,1)S(1)}, u32[]{:S(2)}, u32[]{:S(2)}) collective-permute-start(bf16[576,512]{1,0:T(8,128)(2,1)S(1)} %constant_dynamic-update-slice_fusion.s0), channel_id=1, source_target_pairs={{32,0},{64,32},{96,64},{0,96},{33,1},{65,33},{97,65},{1,97},{34,2}... | collective-permute-start | bytes 1769480 | tf_op jit(solution)/shard_map/ppermute | solution.py:249
  53.3 36.6 %collective-permute-start.13 = (bf16[576,512]{1,0:T(8,128)(2,1)S(1)}, bf16[576,512]{1,0:T(8,128)(2,1)S(1)}, u32[]{:S(2)}, u32[]{:S(2)}) collective-permute-start(bf16[576,512]{1,0:T(8,128)(2,1)S(1)} %constant_dynamic-update-slice_fusion.s0), channel_id=1, source_target_pairs={{64,0},{96,32},{0,64},{32,96},{65,1},{97,33},{1,65},{33,97},{66,2}... | collective-permute-start | bytes 1769480 | tf_op jit(solution)/shard_map/ppermute | solution.py:249
  55.8 39.2 %collective-permute-start.14 = (bf16[576,512]{1,0:T(8,128)(2,1)S(1)}, bf16[576,512]{1,0:T(8,128)(2,1)S(1)}, u32[]{:S(2)}, u32[]{:S(2)}) collective-permute-start(bf16[576,512]{1,0:T(8,128)(2,1)S(1)} %constant_dynamic-update-slice_fusion.s0), channel_id=1, source_target_pairs={{96,0},{0,32},{32,64},{64,96},{97,1},{1,33},{33,65},{65,97},{98,2}... | collective-permute-start | bytes 1769480 | tf_op jit(solution)/shard_map/ppermute | solution.py:249
  58.3 15.6 %collective-permute-start.3 = (bf16[48,2176]{1,0:T(8,128)(2,1)S(1)}, bf16[48,2176]{1,0:T(8,128)(2,1)S(1)}, u32[]{:S(2)}, u32[]{:S(2)}) collective-permute-start(bf16[48,2176]{1,0:T(8,128)(2,1)S(1)} %bitcast.49), channel_id=1, source_target_pairs={{0,14},{2,0},{4,2},{6,4},{8,6},{10,8},{12,10},{14,12},{1,15},{3,1}... | collective-permute-start | bytes 626696 | tf_op jit(solution)/shard_map/ppermute | solution.py:244
  68.2 26.8 %copy-start.13 = (bf16[48,2176]{1,0:T(8,128)(2,1)}, bf16[48,2176]{1,0:T(8,128)(2,1)S(1)}, u32[]{:S(2)}) copy-start(bf16[48,2176]{1,0:T(8,128)(2,1)S(1)} %collective-permute-done.2.r1) | copy-start | bytes 626692
  68.3 10.2 %collective-permute-start.4 = (bf16[48,2176]{1,0:T(8,128)(2,1)S(1)}, bf16[48,2176]{1,0:T(8,128)(2,1)}, u32[]{:S(2)}, u32[]{:S(2)}) collective-permute-start(bf16[48,2176]{1,0:T(8,128)(2,1)S(1)} %collective-permute-done.2.r1), channel_id=1, source_target_pairs={{0,2},{2,4},{4,6},{6,8},{8,10},{10,12},{12,14},{14,0},{1,3},{3,5},... | collective-permute-start | bytes 626696 | tf_op jit(solution)/shard_map/ppermute | solution.py:244
  73.9 21.1 %copy-start.14 = (bf16[48,2176]{1,0:T(8,128)(2,1)}, bf16[48,2176]{1,0:T(8,128)(2,1)S(1)}, u32[]{:S(2)}) copy-start(bf16[48,2176]{1,0:T(8,128)(2,1)S(1)} %collective-permute-done.3.l1) | copy-start | bytes 626692
  73.9 7.3 %collective-permute-start.5 = (bf16[48,2176]{1,0:T(8,128)(2,1)S(1)}, bf16[48,2176]{1,0:T(8,128)(2,1)S(1)}, u32[]{:S(2)}, u32[]{:S(2)}) collective-permute-start(bf16[48,2176]{1,0:T(8,128)(2,1)S(1)} %collective-permute-done.3.l1), channel_id=1, source_target_pairs={{0,14},{2,0},{4,2},{6,4},{8,6},{10,8},{12,10},{14,12},{1,15},{3,1}... | collective-permute-start | bytes 626696 | tf_op jit(solution)/shard_map/ppermute | solution.py:244
  78.5 8.4 %collective-permute-start.6 = (bf16[48,2176]{1,0:T(8,128)(2,1)}, bf16[48,2176]{1,0:T(8,128)(2,1)S(1)}, u32[]{:S(2)}, u32[]{:S(2)}) collective-permute-start(bf16[48,2176]{1,0:T(8,128)(2,1)} %collective-permute-done.4.r2), channel_id=1, source_target_pairs={{0,2},{2,4},{4,6},{6,8},{8,10},{10,12},{12,14},{14,0},{1,3},{3,5},... | collective-permute-start | bytes 626696 | tf_op jit(solution)/shard_map/ppermute | solution.py:244
  81.2 13.8 %copy-start.15 = (bf16[48,2176]{1,0:T(8,128)(2,1)}, bf16[48,2176]{1,0:T(8,128)(2,1)S(1)}, u32[]{:S(2)}) copy-start(bf16[48,2176]{1,0:T(8,128)(2,1)S(1)} %collective-permute-done.5.l2) | copy-start | bytes 626692
  81.2 13.8 %collective-permute-start.7 = (bf16[48,2176]{1,0:T(8,128)(2,1)S(1)}, bf16[48,2176]{1,0:T(8,128)(2,1)S(1)}, u32[]{:S(2)}, u32[]{:S(2)}) collective-permute-start(bf16[48,2176]{1,0:T(8,128)(2,1)S(1)} %collective-permute-done.5.l2), channel_id=1, source_target_pairs={{0,14},{2,0},{4,2},{6,4},{8,6},{10,8},{12,10},{14,12},{1,15},{3,1}... | collective-permute-start | bytes 626696 | tf_op jit(solution)/shard_map/ppermute | solution.py:244
  86.8 8.2 %copy-start.16 = (bf16[48,2176]{1,0:T(8,128)(2,1)}, bf16[48,2176]{1,0:T(8,128)(2,1)S(1)}, u32[]{:S(2)}) copy-start(bf16[48,2176]{1,0:T(8,128)(2,1)S(1)} %collective-permute-done.6.r3) | copy-start | bytes 626692
  86.8 8.1 %collective-permute-start.8 = (bf16[48,2176]{1,0:T(8,128)(2,1)S(1)}, bf16[48,2176]{1,0:T(8,128)(2,1)S(1)}, u32[]{:S(2)}, u32[]{:S(2)}) collective-permute-start(bf16[48,2176]{1,0:T(8,128)(2,1)S(1)} %collective-permute-done.6.r3), channel_id=1, source_target_pairs={{0,2},{2,4},{4,6},{6,8},{8,10},{10,12},{12,14},{14,0},{1,3},{3,5},... | collective-permute-start | bytes 626696 | tf_op jit(solution)/shard_map/ppermute | solution.py:244
  103.5 14.1 %collective-permute-start.15 = (f32[192,640]{1,0:T(8,128)}, f32[192,640]{1,0:T(8,128)S(1)}, u32[]{:S(2)}, u32[]{:S(2)}) collective-permute-start(f32[192,640]{1,0:T(8,128)} %get-tuple-element.38), channel_id=1, source_target_pairs={{0,16},{16,0},{1,17},{17,1},{2,18},{18,2},{3,19},{19,3},{4,20},{20... | collective-permute-start | bytes 1474568 | tf_op jit(solution)/shard_map/ppermute | solution.py:301
  117.7 6.0 %copy-start.11 = (f32[192,640]{1,0:T(8,128)}, f32[192,640]{1,0:T(8,128)S(1)}, u32[]{:S(2)}) copy-start(f32[192,640]{1,0:T(8,128)S(1)} %collective-permute-done.15.side_partner_in) | copy-start | bytes 1474564
  123.7 4.7 %collective-permute-start.16 = (f32[192,1280]{1,0:T(8,128)}, f32[192,1280]{1,0:T(8,128)S(1)}, u32[]{:S(2)}, u32[]{:S(2)}) collective-permute-start(f32[192,1280]{1,0:T(8,128)} %get-tuple-element.40), channel_id=1, source_target_pairs={{0,16},{16,0},{1,17},{17,1},{2,18},{18,2},{3,19},{19,3},{4,20},{20... | collective-permute-start | bytes 2949128 | tf_op jit(solution)/shard_map/ppermute | solution.py:320
  129.3 31.2 %copy-start = (bf16[384,2176]{1,0:T(8,128)(2,1)S(1)}, bf16[384,2176]{1,0:T(8,128)(2,1)}, u32[]{:S(2)}) copy-start(bf16[384,2176]{1,0:T(8,128)(2,1)} %get-tuple-element.35.tok.tok_in) | copy-start | bytes 5013508
  129.3 31.2 %copy-start.2 = (bf16[2,128,192]{2,1,0:T(8,128)(2,1)S(1)}, bf16[2,128,192]{2,1,0:T(8,128)(2,1)}, u32[]{:S(2)}) copy-start(bf16[2,128,192]{2,1,0:T(8,128)(2,1)} %fusion.4.signs_in.signs) | copy-start | bytes 294916
  129.3 31.2 %copy-start.4 = (s32[4]{0:T(128)S(1)}, s32[4]{0:T(128)}, u32[]{:S(2)}) copy-start(s32[4]{0:T(128)} %pad_add_fusion.place) | copy-start | bytes 52
  187.9 10.8 %all-to-all-start.2 = ((f32[16,2,128]{2,1,0:T(2,128)}), f32[16,2,128]{2,1,0:T(2,128)S(1)}, u32[]{:S(2)}, u32[]{:S(2)}) async-start(f32[16,2,128]{2,1,0:T(2,128)} %broadcast_in_dim.32), calls=%async_computation.2 | async-start | bytes 32768 | tf_op jit(solution)/shard_map/all_to_all | solution.py:354
  (9 other events, 20.4 us)
Sparse Core Ops, SparseCore 0:
  11.0 99.4 all-gather.1

commit v12 on v9

--- a/solution.py
+++ b/solution.py
@@ -52,7 +52,8 @@
     return lax.dot_general(a, b, dims, preferred_element_type=F32)
 
 
-def early_products(place, down, p0, r1, l1, r2, l2, r3, l3, far_z, s0, s1, s2, s3, out, tok_out, tok, w, sems):
+def early_products(place, down, p0, r1, l1, r2, l2, r3, l3, far_z, s0, s1, s2, s3, far, near, count,
+                   tok_out, tok, w, counts, sems):
     z, yh, x = place[1], place[2], place[3]
     block = 4 * ROWS
     moves = ((0, p0), (-1, r1), (1, l1), (-2, r2), (2, l2), (-3, r3), (3, l3), (4, far_z))
@@ -64,19 +65,24 @@
         for k in range(4):
             source = lax.rem(yh + k, 4) * 4 + lax.rem(x + j, 4)
             rows = pl.ds(pl.multiple_of(source * SLICE, SLICE), SLICE)
-            copies.append(
-                pltpu.make_async_copy(ref.at[pl.ds(k * PIECE, SLICE), :], w.at[rows, :], sems.at[8 + 4 * j + k])
-            )
+            at = 4 * j + k
+            copies.append(pltpu.make_async_copy(ref.at[pl.ds(k * PIECE, SLICE), :], w.at[rows, :], sems.at[8 + at]))
+            spare = ref.at[pl.ds(k * PIECE + SLICE, PIECE - SLICE), pl.ds(0, LANES)]
+            copies.append(pltpu.make_async_copy(spare, counts.at[at], sems.at[25 + at]))
     for copy in copies:
         copy.start()
     for copy in copies:
         copy.wait()
     tok_copy = pltpu.make_async_copy(tok, tok_out, sems.at[24])
     tok_copy.start()
-    for n in range(2):
-        part = slice(n * SIDE, (n + 1) * SIDE)
-        out[:, part] = dot(tok[:, 0:HALF], w[:, part])
-    out[:, 2 * SIDE :] = dot(tok[:, 0:HALF], down[...])
+    total = jnp.sum(counts[...].astype(F32), axis=0)[0:1, :]
+    count[...] = jnp.where(lax.broadcasted_iota(jnp.int32, (1, LANES), 1) == 64, total, 0.0)
+    for half, out in ((1 - place[0], far), (place[0], near)):
+        rows = pl.ds(pl.multiple_of(half * GROUP, GROUP), GROUP)
+        for n in range(2):
+            part = slice(n * SIDE, (n + 1) * SIDE)
+            out[:, part] = dot(tok[rows, 0:HALF], w[:, part])
+        out[:, 2 * SIDE :] = dot(tok[rows, 0:HALF], down[...])
     tok_copy.wait()
 
 
@@ -261,28 +267,25 @@
     stacks = [stack] + [fetch(stack, "x", j) for j in (1, 2, 3)]
     for step in range(2):
         ring += [along(ring[-2], "z", 1), along(ring[-1], "z", -1)]
-    ring.append(along(four, "z", 4))
-    count = sum(jnp.sum(p.reshape(4, PIECE, 2 * SIDE)[:, SLICE, 0].astype(F32)) for p in stacks)
-    count_lanes = jnp.where(jnp.arange(LANES) == 64, count, 0.0).reshape(1, LANES)
+    ring.append(along(ring[-2], "z", 1))
 
     down_half = down.reshape(16, 2, SLICE, 2 * RANK)
     down_half = jnp.where(core == 0, down_half[:, 0], down_half[:, 1]).reshape(HALF, 2 * RANK)
     down_half = jnp.pad(down_half, ((0, 0), (0, LANES - 2 * RANK)))
-    side, tok = kernel(
+    side_far, side, count_lanes, tok = kernel(
         early_products,
-        [((2 * GROUP, 2 * SIDE + LANES), F32), ((2 * GROUP, HALF + LANES), BF16)],
+        [((GROUP, 2 * SIDE + LANES), F32)] * 2 + [((1, LANES), F32), ((2 * GROUP, HALF + LANES), BF16)],
         (place, down_half, *ring, *stacks),
         4 * GROUP * HALF * (2 * SIDE + LANES), 56,
         scratch=[
             pltpu.VMEM((2 * GROUP, HALF + LANES), BF16),
             pltpu.VMEM((HALF, 2 * SIDE), BF16),
-            pltpu.SemaphoreType.DMA((25,)),
+            pltpu.VMEM((16, PIECE - SLICE, LANES), BF16),
+            pltpu.SemaphoreType.DMA((41,)),
         ],
         in_hbm=12, out_hbm=1,
     )
-    side = side.reshape(2, GROUP, 2 * SIDE + LANES)
-    side_far = jnp.where(core == 0, side[1], side[0])
-    side = jnp.where(core == 0, side[0], side[1]) + lax.ppermute(side_far, "c", SWAP)
+    side = side + lax.ppermute(side_far, "c", SWAP)
 
     b_gate = jnp.pad(up[:RANK], ((0, LANES - RANK), (0, 0)))
     b_up = jnp.pad(up[RANK:], ((RANK, LANES - 2 * RANK), (0, 0)))

time: 195 us -> 199 us (1.021)
  blocking collectives: 35.9 us -> 48.6 us
  starting transfers between devices: 79.5 us -> 71.7 us
  waiting for transfers between devices: 19.6 us -> 24.4 us
  other arithmetic: 9.31 us -> 5.7 us
  between operations: 22.4 us -> 19.7 us
    all_to_all x1, blocking collectives: 13.4 us -> 25.8 us  [on_device(): lax.all_to_all(message, ('c', 'z', 'yl'), split_axis=0, concat_axis=0)]
    ppermute x6, waiting for transfers between devices: 0.02 us -> 10.1 us  [fetch(): return lax.ppermute(value, axis, [((i + k) % n, i) for i in range(n)])]
    ppermute x1, starting transfers between devices: 12.3 us -> 3.16 us  [on_device(): side = side + lax.ppermute(side_far, 'c', SWAP)]
    ppermute x7, waiting for transfers between devices: 5.68 us -> 0.54 us  [along(): return lax.ppermute(value, axis, [(i, (i + k) % n) for i in range(n)])]
    ppermute x7, starting transfers between devices: 28.3 us -> 33.1 us  [along(): return lax.ppermute(value, axis, [(i, (i + k) % n) for i in range(n)])]
    ppermute x6, starting transfers between devices: 27.3 us -> 23.8 us  [fetch(): return lax.ppermute(value, axis, [((i + k) % n, i) for i in range(n)])]
    reduce_sum x4 -> x0, other arithmetic: 3.21 us -> none  [on_device(): jnp.sum(p.reshape(4, PIECE, 2 * SIDE)[:, SLICE, 0].astype(F32))]
  transfers between devices with their start and end apart: 19 -> 19, of which waited for: 8 -> 7; matrix products, arithmetic and copies ran while one was open for 7% -> 5% of each run, Pallas kernels for 3% -> 3%
where the time goes in v12:
time: 199 us; the launch traced here: 198 us
  starting transfers between devices  71.7 us (36%)
  blocking collectives  48.6 us (24%)
  waiting for transfers between devices  24.4 us (12%)
  between operations  19.7 us (10%)
  Pallas kernels  18.1 us (9%)
  local copies, waits for them, and re-layouts  9.99 us (5%)
  other arithmetic  5.7 us (3%)
    ppermute x7, starting transfers between devices, along(): return lax.ppermute(value, axis, [(i, (i + k) % n) for i in range(n)])  33.1 us
    all_to_all x1, blocking collectives, on_device(): lax.all_to_all(message, ('c', 'z', 'yl'), split_axis=0, concat_axis=0)  25.8 us
    ppermute x6, starting transfers between devices, fetch(): return lax.ppermute(value, axis, [((i + k) % n, i) for i in range(n)])  23.8 us
    all_to_all x1, blocking collectives, on_device(): lax.all_to_all(outgoing, DP, split_axis=0, concat_axis=0)  22.8 us
    pallas_call x4, Pallas kernels, kernel(): pl.pallas_call(function, out_shape=tuple((jax.ShapeDtypeStruct(*s) for s...  18.1 us
    ppermute x6, waiting for transfers between devices, fetch(): return lax.ppermute(value, axis, [((i + k) % n, i) for i in range(n)])  10.1 us
    ppermute x1, waiting for transfers between devices, swapped(): far = lax.ppermute(value, axis, SWAP)  5.62 us
    all_to_all x1, waiting for transfers between devices, on_device(): lax.all_to_all(jnp.broadcast_to(columns, (16, 2, SLICE)), BLK, split_axis...  4.39 us
  transfers between devices with their start and end apart: 19, of which 7 were waited for; matrix products, arithmetic and copies ran while one was open for 5% of the time, Pallas kernels for 3%

profile of v12, /device:TPU:1, one launch (start us, length us, event | category | flops | bytes accessed | tf_op | source)
XLA Modules:
  0.0 198.2 jit_solution(12018611824020998345)
XLA Ops:
  9.1 1.3 fusion.13
  13.9 6.7 %collective-permute-start.2 = (bf16[144,512]{1,0:T(8,128)(2,1)S(1)}, bf16[144,512]{1,0:T(8,128)(2,1)S(1)}, u32[]{:S(2)}, u32[]{:S(2)}) collective-permute-start(bf16[144,512]{1,0:T(8,128)(2,1)S(1)} %fusion.6), channel_id=1, source_target_pairs={{128,0},{256,128},{384,256},{0,384},{129,1},{257,129},{385,257},{1... | collective-permute-start | bytes 442376 | tf_op jit(solution)/shard_map/ppermute | solution.py:238
  20.6 3.5 %collective-permute-start.3 = (bf16[144,512]{1,0:T(8,128)(2,1)S(1)}, bf16[144,512]{1,0:T(8,128)(2,1)S(1)}, u32[]{:S(2)}, u32[]{:S(2)}) collective-permute-start(bf16[144,512]{1,0:T(8,128)(2,1)S(1)} %fusion.6), channel_id=1, source_target_pairs={{256,0},{384,128},{0,256},{128,384},{257,1},{385,129},{1,257},{129... | collective-permute-start | bytes 442376 | tf_op jit(solution)/shard_map/ppermute | solution.py:238
  24.1 4.2 %collective-permute-start.4 = (bf16[144,512]{1,0:T(8,128)(2,1)S(1)}, bf16[144,512]{1,0:T(8,128)(2,1)S(1)}, u32[]{:S(2)}, u32[]{:S(2)}) collective-permute-start(bf16[144,512]{1,0:T(8,128)(2,1)S(1)} %fusion.6), channel_id=1, source_target_pairs={{384,0},{0,128},{128,256},{256,384},{385,1},{1,129},{129,257},{257... | collective-permute-start | bytes 442376 | tf_op jit(solution)/shard_map/ppermute | solution.py:238
  28.7 3.4 %collective-permute-start = (bf16[12,2176]{1,0:T(8,128)(2,1)S(1)}, bf16[12,2176]{1,0:T(8,128)(2,1)S(1)}, u32[]{:S(2)}, u32[]{:S(2)}) collective-permute-start(bf16[12,2176]{1,0:T(8,128)(2,1)S(1)} %get-tuple-element.69), channel_id=1, source_target_pairs={{0,16},{16,0},{1,17},{17,1},{2,18},{18,2},{3,19},{19,3},{4,20},{20... | collective-permute-start | bytes 156680 | tf_op jit(solution)/shard_map/ppermute | solution.py:253
  33.6 2.3 %collective-permute-start.1 = (bf16[24,2176]{1,0:T(8,128)(2,1)S(1)}, bf16[24,2176]{1,0:T(8,128)(2,1)S(1)}, u32[]{:S(2)}, u32[]{:S(2)}) collective-permute-start(bf16[24,2176]{1,0:T(8,128)(2,1)S(1)} %maximum_select_fusion.2), channel_id=1, source_target_pairs={{0,1},{1,0},{2,3},{3,2},{4,5},{5,4},{6,7},{7,6},{8,9},{9,8},{10,11... | collective-permute-start | bytes 313352 | tf_op jit(solution)/shard_map/ppermute | solution.py:39
  36.0 5.6 %collective-permute-done.1 = bf16[24,2176]{1,0:T(8,128)(2,1)S(1)} collective-permute-done((bf16[24,2176]{1,0:T(8,128)(2,1)S(1)}, bf16[24,2176]{1,0:T(8,128)(2,1)S(1)}, u32[]{:S(2)}, u32[]{:S(2)}) %collective-permute-start.1) | collective-permute-done | bytes 104480 | tf_op jit(solution)/shard_map/ppermute | solution.py:39
  41.8 7.9 %collective-permute-start.5 = (bf16[48,2176]{1,0:T(8,128)(2,1)S(1)}, bf16[48,2176]{1,0:T(8,128)(2,1)S(1)}, u32[]{:S(2)}, u32[]{:S(2)}) collective-permute-start(bf16[48,2176]{1,0:T(8,128)(2,1)S(1)} %bitcast.43), channel_id=1, source_target_pairs={{0,2},{2,4},{4,6},{6,8},{8,10},{10,12},{12,14},{14,0},{1,3},{3,5},... | collective-permute-start | bytes 626696 | tf_op jit(solution)/shard_map/ppermute | solution.py:233
  49.8 4.4 %collective-permute-start.12 = (bf16[576,512]{1,0:T(8,128)(2,1)S(1)}, bf16[576,512]{1,0:T(8,128)(2,1)S(1)}, u32[]{:S(2)}, u32[]{:S(2)}) collective-permute-start(bf16[576,512]{1,0:T(8,128)(2,1)S(1)} %constant_dynamic-update-slice_fusion.s0), channel_id=1, source_target_pairs={{32,0},{64,32},{96,64},{0,96},{33,1},{65,33},{97,65},{1,97},{34,2}... | collective-permute-start | bytes 1769480 | tf_op jit(solution)/shard_map/ppermute | solution.py:238
  54.2 2.4 %collective-permute-start.13 = (bf16[576,512]{1,0:T(8,128)(2,1)S(1)}, bf16[576,512]{1,0:T(8,128)(2,1)S(1)}, u32[]{:S(2)}, u32[]{:S(2)}) collective-permute-start(bf16[576,512]{1,0:T(8,128)(2,1)S(1)} %constant_dynamic-update-slice_fusion.s0), channel_id=1, source_target_pairs={{64,0},{96,32},{0,64},{32,96},{65,1},{97,33},{1,65},{33,97},{66,2}... | collective-permute-start | bytes 1769480 | tf_op jit(solution)/shard_map/ppermute | solution.py:238
  56.6 2.5 %collective-permute-start.14 = (bf16[576,512]{1,0:T(8,128)(2,1)S(1)}, bf16[576,512]{1,0:T(8,128)(2,1)}, u32[]{:S(2)}, u32[]{:S(2)}) collective-permute-start(bf16[576,512]{1,0:T(8,128)(2,1)S(1)} %constant_dynamic-update-slice_fusion.s0), channel_id=1, source_target_pairs={{96,0},{0,32},{32,64},{64,96},{97,1},{1,33},{33,65},{65,97},{98,2}... | collective-permute-start | bytes 1769480 | tf_op jit(solution)/shard_map/ppermute | solution.py:238
  59.1 9.0 %collective-permute-start.6 = (bf16[48,2176]{1,0:T(8,128)(2,1)S(1)}, bf16[48,2176]{1,0:T(8,128)(2,1)S(1)}, u32[]{:S(2)}, u32[]{:S(2)}) collective-permute-start(bf16[48,2176]{1,0:T(8,128)(2,1)S(1)} %bitcast.44), channel_id=1, source_target_pairs={{0,14},{2,0},{4,2},{6,4},{8,6},{10,8},{12,10},{14,12},{1,15},{3,1}... | collective-permute-start | bytes 626696 | tf_op jit(solution)/shard_map/ppermute | solution.py:233
  68.1 1.9 collective-permute-start.7
  71.1 5.1 %collective-permute-start.8 = (bf16[48,2176]{1,0:T(8,128)(2,1)S(1)}, bf16[48,2176]{1,0:T(8,128)(2,1)S(1)}, u32[]{:S(2)}, u32[]{:S(2)}) collective-permute-start(bf16[48,2176]{1,0:T(8,128)(2,1)S(1)} %collective-permute-done.6.l1), channel_id=1, source_target_pairs={{0,14},{2,0},{4,2},{6,4},{8,6},{10,8},{12,10},{14,12},{1,15},{3,1}... | collective-permute-start | bytes 626696 | tf_op jit(solution)/shard_map/ppermute | solution.py:233
  76.3 1.9 collective-permute-start.9
  78.9 5.4 %collective-permute-start.10 = (bf16[48,2176]{1,0:T(8,128)(2,1)S(1)}, bf16[48,2176]{1,0:T(8,128)(2,1)S(1)}, u32[]{:S(2)}, u32[]{:S(2)}) collective-permute-start(bf16[48,2176]{1,0:T(8,128)(2,1)S(1)} %collective-permute-done.8.l2), channel_id=1, source_target_pairs={{0,14},{2,0},{4,2},{6,4},{8,6},{10,8},{12,10},{14,12},{1,15},{3,1}... | collective-permute-start | bytes 626696 | tf_op jit(solution)/shard_map/ppermute | solution.py:233
  84.6 1.9 collective-permute-start.11
  86.7 10.1 %collective-permute-done.14.s3 = bf16[576,512]{1,0:T(8,128)(2,1)} collective-permute-done((bf16[576,512]{1,0:T(8,128)(2,1)S(1)}, bf16[576,512]{1,0:T(8,128)(2,1)}, u32[]{:S(2)}, u32[]{:S(2)}) %collective-permute-start.14) | collective-permute-done | bytes 589856 | tf_op jit(solution)/shard_map/ppermute | solution.py:238
  98.2 6.1 %shard_map.94 = (f32[192,640]{1,0:T(8,128)}, f32[192,640]{1,0:T(8,128)}, f32[1,128]{1,0:T(1,128)}, bf16[384,2176]{1,0:T(8,128)(2,1)}) custom-call(s32[4]{0:T(128)} %pad_add_fusion.place, bf16[2048,128]{1,0:T(8,128)(2,1)} %pad.17.down, bf16[48,2176]{1,0:T(8,128)(2,1)} %bitcast.45, bf16[48,2176]{1,0:T(8,128)(2,1)} %copy-done.9, bf16[48,2176]{1,0:T(8,128)(2,1)} %copy-done.10, ...), custom_call_target="tpu_custom_call" | custom-call | flops 1006632960 | bytes 10000000 | tf_op jit(solution)/shard_map/pallas_call | solution.py:220
  105.4 3.2 %collective-permute-start.15 = (f32[192,640]{1,0:T(8,128)}, f32[192,640]{1,0:T(8,128)S(1)}, u32[]{:S(2)}, u32[]{:S(2)}) collective-permute-start(f32[192,640]{1,0:T(8,128)} %get-tuple-element.34), channel_id=1, source_target_pairs={{0,16},{16,0},{1,17},{17,1},{2,18},{18,2},{3,19},{19,3},{4,20},{20... | collective-permute-start | bytes 1474568 | tf_op jit(solution)/shard_map/ppermute | solution.py:288
  109.0 1.3 collective-permute-done.15
  110.2 1.1 add.54.side
  111.4 6.1 %shard_map.95 = (f32[192,1280]{1,0:T(8,128)}, f32[192,1280]{1,0:T(8,128)}) custom-call(s32[4]{0:T(128)} %pad_add_fusion.place, bf16[384,2176]{1,0:T(8,128)(2,1)} %get-tuple-element.32.tok.tok_in, bf16[2048,1280]{1,0:T(8,128)(2,1)} %all-gather.2.cloned.1.call-done.w_in), custom_call_target="tpu_custom_call" | custom-call | flops 2013265920 | bytes 10000000 | tf_op jit(solution)/shard_map/pallas_call | solution.py:220
  117.5 2.4 %collective-permute-start.16 = (f32[192,1280]{1,0:T(8,128)}, f32[192,1280]{1,0:T(8,128)S(1)}, u32[]{:S(2)}, u32[]{:S(2)}) collective-permute-start(f32[192,1280]{1,0:T(8,128)} %get-tuple-element.38), channel_id=1, source_target_pairs={{0,16},{16,0},{1,17},{17,1},{2,18},{18,2},{3,19},{19,3},{4,20},{20... | collective-permute-start | bytes 2949128 | tf_op jit(solution)/shard_map/ppermute | solution.py:307
  119.9 2.4 %collective-permute-done.16.partner = f32[192,1280]{1,0:T(8,128)S(1)} collective-permute-done((f32[192,1280]{1,0:T(8,128)}, f32[192,1280]{1,0:T(8,128)S(1)}, u32[]{:S(2)}, u32[]{:S(2)}) %collective-permute-start.16) | collective-permute-done | bytes 983072 | tf_op jit(solution)/shard_map/ppermute | solution.py:307
  122.3 1.2 copy-done.1
  123.5 3.8 %shard_map.96 = (f32[32,1,640]{2,1,0:T(1,128)S(1)}, f32[32,192]{1,0:T(8,128)S(1)}, bf16[4,192,896]{2,1,0:T(8,128)(2,1)S(1)}) custom-call(s32[4]{0:T(128)S(1)} %copy-done.2, f32[192,1280]{1,0:T(8,128)S(1)} %copy-done.1, f32[192,1280]{1,0:T(8,128)S(1)} %collective-permute-done.16.partner, f32[192,640]{1,0:T(8,128)S(1)} %add.54.side, ...), custom_call_target="tpu_custom_call" | custom-call | flops 176160768 | bytes 10000000 | tf_op jit(solution)/shard_map/pallas_call | solution.py:220
  127.3 25.8 %all_to_all.15.arrived = f32[32,1,640]{2,1,0:T(1,128)S(1)} all-to-all(f32[32,1,640]{2,1,0:T(1,128)S(1)} %get-tuple-element.45), channel_id=1, replica_groups=mesh['yh'=4,'x'=4,'c'=2,'z'=8,'yl'=2] {'c','z','yl'}, dimensions={0} | all-to-all | bytes 163840 | tf_op jit(solution)/shard_map/all_to_all | solution.py:316
  153.1 2.1 %shard_map.97 = (f32[32,1,1280]{2,1,0:T(1,128)S(1)}, f32[8,128]{1,0:T(8,128)S(1)}) custom-call(s32[4]{0:T(128)S(1)} %copy-done.2, f32[32,1,640]{2,1,0:T(1,128)S(1)} %all_to_all.15.arrived, bf16[2,128,192]{2,1,0:T(8,128)(2,1)S(1)} %fusion.7.signs, f32[2,1,128]{2,1,0:T(1,128)S(1)} %bitcast.41, f32[32,192]{1,0:T(8,128)S(1)} %get-tuple-element.47.low_t, ...), custom_call_target="tpu_custom_call" | custom-call | flops 12582912 | bytes 10000000 | tf_op jit(solution)/shard_map/pallas_call | solution.py:220
  155.2 22.8 %all_to_all.16 = f32[32,1,1280]{2,1,0:T(1,128)S(1)} all-to-all(f32[32,1,1280]{2,1,0:T(1,128)S(1)} %get-tuple-element.49), channel_id=1, replica_groups=mesh['yh'=4,'x'=4,'c'=2,'z'=8,'yl'=2] {'yh','x','c'}, dimensions={0} | all-to-all | bytes 327680 | tf_op jit(solution)/shard_map/all_to_all | solution.py:330
  178.8 3.5 %all-to-all-start.2 = ((f32[16,2,128]{2,1,0:T(2,128)}), f32[16,2,128]{2,1,0:T(2,128)S(1)}, u32[]{:S(2)}, u32[]{:S(2)}) async-start(f32[16,2,128]{2,1,0:T(2,128)} %broadcast_in_dim.10), calls=%async_computation.2 | async-start | bytes 32768 | tf_op jit(solution)/shard_map/all_to_all | solution.py:332
  185.2 4.4 %all-to-all-done.2 = f32[16,2,128]{2,1,0:T(2,128)S(1)} async-done(((f32[16,2,128]{2,1,0:T(2,128)}), f32[16,2,128]{2,1,0:T(2,128)S(1)}, u32[]{:S(2)}, u32[]{:S(2)}) %all-to-all-start.2) | async-done | bytes 16416 | tf_op jit(solution)/shard_map/all_to_all | solution.py:332
  (101 shorter events, 12.7 us)
Async XLA Ops:
  7.2 21.2 %copy-start.15 = (bf16[12,4096]{1,0:T(8,128)(2,1)S(1)}, bf16[12,4096]{1,0:T(8,128)(2,1)}, u32[]{:S(2)}) copy-start(bf16[12,4096]{1,0:T(8,128)(2,1)} %param.7) | copy-start | bytes 294916
  7.2 25.0 %copy-start.8 = (bf16[4096,32]{0,1:T(8,128)(2,1)S(1)}, bf16[4096,32]{0,1:T(8,128)(2,1)}, u32[]{:S(2)}) copy-start(bf16[4096,32]{0,1:T(8,128)(2,1)} %param.11) | copy-start | bytes 786436
  7.2 104.2 %all-gather.2.cloned.1.call-start = ((), (), s32[]{:S(2)}) async-start(), calls=%async_computation.3 | async-start | bytes 5570560 | tf_op jit(solution)/shard_map/all_gather | solution.py:247
  13.9 27.8 %collective-permute-start.2 = (bf16[144,512]{1,0:T(8,128)(2,1)S(1)}, bf16[144,512]{1,0:T(8,128)(2,1)S(1)}, u32[]{:S(2)}, u32[]{:S(2)}) collective-permute-start(bf16[144,512]{1,0:T(8,128)(2,1)S(1)} %fusion.6), channel_id=1, source_target_pairs={{128,0},{256,128},{384,256},{0,384},{129,1},{257,129},{385,257},{1... | collective-permute-start | bytes 442376 | tf_op jit(solution)/shard_map/ppermute | solution.py:238
  20.6 21.1 %collective-permute-start.3 = (bf16[144,512]{1,0:T(8,128)(2,1)S(1)}, bf16[144,512]{1,0:T(8,128)(2,1)S(1)}, u32[]{:S(2)}, u32[]{:S(2)}) collective-permute-start(bf16[144,512]{1,0:T(8,128)(2,1)S(1)} %fusion.6), channel_id=1, source_target_pairs={{256,0},{384,128},{0,256},{128,384},{257,1},{385,129},{1,257},{129... | collective-permute-start | bytes 442376 | tf_op jit(solution)/shard_map/ppermute | solution.py:238
  24.1 17.6 %collective-permute-start.4 = (bf16[144,512]{1,0:T(8,128)(2,1)S(1)}, bf16[144,512]{1,0:T(8,128)(2,1)S(1)}, u32[]{:S(2)}, u32[]{:S(2)}) collective-permute-start(bf16[144,512]{1,0:T(8,128)(2,1)S(1)} %fusion.6), channel_id=1, source_target_pairs={{384,0},{0,128},{128,256},{256,384},{385,1},{1,129},{129,257},{257... | collective-permute-start | bytes 442376 | tf_op jit(solution)/shard_map/ppermute | solution.py:238
  28.7 4.8 %collective-permute-start = (bf16[12,2176]{1,0:T(8,128)(2,1)S(1)}, bf16[12,2176]{1,0:T(8,128)(2,1)S(1)}, u32[]{:S(2)}, u32[]{:S(2)}) collective-permute-start(bf16[12,2176]{1,0:T(8,128)(2,1)S(1)} %get-tuple-element.69), channel_id=1, source_target_pairs={{0,16},{16,0},{1,17},{17,1},{2,18},{18,2},{3,19},{19,3},{4,20},{20... | collective-permute-start | bytes 156680 | tf_op jit(solution)/shard_map/ppermute | solution.py:253
  33.6 8.0 %collective-permute-start.1 = (bf16[24,2176]{1,0:T(8,128)(2,1)S(1)}, bf16[24,2176]{1,0:T(8,128)(2,1)S(1)}, u32[]{:S(2)}, u32[]{:S(2)}) collective-permute-start(bf16[24,2176]{1,0:T(8,128)(2,1)S(1)} %maximum_select_fusion.2), channel_id=1, source_target_pairs={{0,1},{1,0},{2,3},{3,2},{4,5},{5,4},{6,7},{7,6},{8,9},{9,8},{10,11... | collective-permute-start | bytes 313352 | tf_op jit(solution)/shard_map/ppermute | solution.py:39
  36.0 35.1 %copy-start.17 = (bf16[896]{0:T(1024)(128)(2,1)S(1)}, bf16[896]{0:T(1024)(128)(2,1)}, u32[]{:S(2)}) copy-start(bf16[896]{0:T(1024)(128)(2,1)} %param.13) | copy-start | bytes 5380
  41.7 55.1 %copy-start.5 = (bf16[2,24,2176]{2,1,0:T(8,128)(2,1)}, bf16[2,24,2176]{2,1,0:T(8,128)(2,1)S(1)}, u32[]{:S(2)}) copy-start(bf16[2,24,2176]{2,1,0:T(8,128)(2,1)S(1)} %maximum_select_fusion) | copy-start | bytes 626692
  41.8 26.4 %collective-permute-start.5 = (bf16[48,2176]{1,0:T(8,128)(2,1)S(1)}, bf16[48,2176]{1,0:T(8,128)(2,1)S(1)}, u32[]{:S(2)}, u32[]{:S(2)}) collective-permute-start(bf16[48,2176]{1,0:T(8,128)(2,1)S(1)} %bitcast.43), channel_id=1, source_target_pairs={{0,2},{2,4},{4,6},{6,8},{8,10},{10,12},{12,14},{14,0},{1,3},{3,5},... | collective-permute-start | bytes 626696 | tf_op jit(solution)/shard_map/ppermute | solution.py:233
  49.8 47.0 %copy-start.4 = (bf16[576,512]{1,0:T(8,128)(2,1)}, bf16[576,512]{1,0:T(8,128)(2,1)S(1)}, u32[]{:S(2)}) copy-start(bf16[576,512]{1,0:T(8,128)(2,1)S(1)} %constant_dynamic-update-slice_fusion.s0) | copy-start | bytes 1769476
  49.8 36.9 %collective-permute-start.12 = (bf16[576,512]{1,0:T(8,128)(2,1)S(1)}, bf16[576,512]{1,0:T(8,128)(2,1)S(1)}, u32[]{:S(2)}, u32[]{:S(2)}) collective-permute-start(bf16[576,512]{1,0:T(8,128)(2,1)S(1)} %constant_dynamic-update-slice_fusion.s0), channel_id=1, source_target_pairs={{32,0},{64,32},{96,64},{0,96},{33,1},{65,33},{97,65},{1,97},{34,2}... | collective-permute-start | bytes 1769480 | tf_op jit(solution)/shard_map/ppermute | solution.py:238
  54.2 32.5 %collective-permute-start.13 = (bf16[576,512]{1,0:T(8,128)(2,1)S(1)}, bf16[576,512]{1,0:T(8,128)(2,1)S(1)}, u32[]{:S(2)}, u32[]{:S(2)}) collective-permute-start(bf16[576,512]{1,0:T(8,128)(2,1)S(1)} %constant_dynamic-update-slice_fusion.s0), channel_id=1, source_target_pairs={{64,0},{96,32},{0,64},{32,96},{65,1},{97,33},{1,65},{33,97},{66,2}... | collective-permute-start | bytes 1769480 | tf_op jit(solution)/shard_map/ppermute | solution.py:238
  56.6 40.2 %collective-permute-start.14 = (bf16[576,512]{1,0:T(8,128)(2,1)S(1)}, bf16[576,512]{1,0:T(8,128)(2,1)}, u32[]{:S(2)}, u32[]{:S(2)}) collective-permute-start(bf16[576,512]{1,0:T(8,128)(2,1)S(1)} %constant_dynamic-update-slice_fusion.s0), channel_id=1, source_target_pairs={{96,0},{0,32},{32,64},{64,96},{97,1},{1,33},{33,65},{65,97},{98,2}... | collective-permute-start | bytes 1769480 | tf_op jit(solution)/shard_map/ppermute | solution.py:238
  59.1 11.9 %collective-permute-start.6 = (bf16[48,2176]{1,0:T(8,128)(2,1)S(1)}, bf16[48,2176]{1,0:T(8,128)(2,1)S(1)}, u32[]{:S(2)}, u32[]{:S(2)}) collective-permute-start(bf16[48,2176]{1,0:T(8,128)(2,1)S(1)} %bitcast.44), channel_id=1, source_target_pairs={{0,14},{2,0},{4,2},{6,4},{8,6},{10,8},{12,10},{14,12},{1,15},{3,1}... | collective-permute-start | bytes 626696 | tf_op jit(solution)/shard_map/ppermute | solution.py:233
  68.1 28.7 %copy-start.9 = (bf16[48,2176]{1,0:T(8,128)(2,1)}, bf16[48,2176]{1,0:T(8,128)(2,1)S(1)}, u32[]{:S(2)}) copy-start(bf16[48,2176]{1,0:T(8,128)(2,1)S(1)} %collective-permute-done.5.r1) | copy-start | bytes 626692
  68.1 8.2 %collective-permute-start.7 = (bf16[48,2176]{1,0:T(8,128)(2,1)S(1)}, bf16[48,2176]{1,0:T(8,128)(2,1)}, u32[]{:S(2)}, u32[]{:S(2)}) collective-permute-start(bf16[48,2176]{1,0:T(8,128)(2,1)S(1)} %collective-permute-done.5.r1), channel_id=1, source_target_pairs={{0,2},{2,4},{4,6},{6,8},{8,10},{10,12},{12,14},{14,0},{1,3},{3,5},... | collective-permute-start | bytes 626696 | tf_op jit(solution)/shard_map/ppermute | solution.py:233
  71.1 25.8 %copy-start.10 = (bf16[48,2176]{1,0:T(8,128)(2,1)}, bf16[48,2176]{1,0:T(8,128)(2,1)S(1)}, u32[]{:S(2)}) copy-start(bf16[48,2176]{1,0:T(8,128)(2,1)S(1)} %collective-permute-done.6.l1) | copy-start | bytes 626692
  71.1 7.8 %collective-permute-start.8 = (bf16[48,2176]{1,0:T(8,128)(2,1)S(1)}, bf16[48,2176]{1,0:T(8,128)(2,1)S(1)}, u32[]{:S(2)}, u32[]{:S(2)}) collective-permute-start(bf16[48,2176]{1,0:T(8,128)(2,1)S(1)} %collective-permute-done.6.l1), channel_id=1, source_target_pairs={{0,14},{2,0},{4,2},{6,4},{8,6},{10,8},{12,10},{14,12},{1,15},{3,1}... | collective-permute-start | bytes 626696 | tf_op jit(solution)/shard_map/ppermute | solution.py:233
  76.3 8.4 %collective-permute-start.9 = (bf16[48,2176]{1,0:T(8,128)(2,1)}, bf16[48,2176]{1,0:T(8,128)(2,1)S(1)}, u32[]{:S(2)}, u32[]{:S(2)}) collective-permute-start(bf16[48,2176]{1,0:T(8,128)(2,1)} %collective-permute-done.7.r2), channel_id=1, source_target_pairs={{0,2},{2,4},{4,6},{6,8},{8,10},{10,12},{12,14},{14,0},{1,3},{3,5},... | collective-permute-start | bytes 626696 | tf_op jit(solution)/shard_map/ppermute | solution.py:233
  78.9 18.0 %copy-start.11 = (bf16[48,2176]{1,0:T(8,128)(2,1)}, bf16[48,2176]{1,0:T(8,128)(2,1)S(1)}, u32[]{:S(2)}) copy-start(bf16[48,2176]{1,0:T(8,128)(2,1)S(1)} %collective-permute-done.8.l2) | copy-start | bytes 626692
  78.9 17.9 %collective-permute-start.10 = (bf16[48,2176]{1,0:T(8,128)(2,1)S(1)}, bf16[48,2176]{1,0:T(8,128)(2,1)S(1)}, u32[]{:S(2)}, u32[]{:S(2)}) collective-permute-start(bf16[48,2176]{1,0:T(8,128)(2,1)S(1)} %collective-permute-done.8.l2), channel_id=1, source_target_pairs={{0,14},{2,0},{4,2},{6,4},{8,6},{10,8},{12,10},{14,12},{1,15},{3,1}... | collective-permute-start | bytes 626696 | tf_op jit(solution)/shard_map/ppermute | solution.py:233
  84.6 12.2 %copy-start.12 = (bf16[48,2176]{1,0:T(8,128)(2,1)}, bf16[48,2176]{1,0:T(8,128)(2,1)S(1)}, u32[]{:S(2)}) copy-start(bf16[48,2176]{1,0:T(8,128)(2,1)S(1)} %collective-permute-done.9.r3) | copy-start | bytes 626692
  84.6 12.2 %collective-permute-start.11 = (bf16[48,2176]{1,0:T(8,128)(2,1)S(1)}, bf16[48,2176]{1,0:T(8,128)(2,1)S(1)}, u32[]{:S(2)}, u32[]{:S(2)}) collective-permute-start(bf16[48,2176]{1,0:T(8,128)(2,1)S(1)} %collective-permute-done.9.r3), channel_id=1, source_target_pairs={{0,2},{2,4},{4,6},{6,8},{8,10},{10,12},{12,14},{14,0},{1,3},{3,5},... | collective-permute-start | bytes 626696 | tf_op jit(solution)/shard_map/ppermute | solution.py:233
  86.7 10.2 %copy-start.6 = (bf16[576,512]{1,0:T(8,128)(2,1)}, bf16[576,512]{1,0:T(8,128)(2,1)S(1)}, u32[]{:S(2)}) copy-start(bf16[576,512]{1,0:T(8,128)(2,1)S(1)} %collective-permute-done.12.s1) | copy-start | bytes 1769476
  105.4 4.8 %collective-permute-start.15 = (f32[192,640]{1,0:T(8,128)}, f32[192,640]{1,0:T(8,128)S(1)}, u32[]{:S(2)}, u32[]{:S(2)}) collective-permute-start(f32[192,640]{1,0:T(8,128)} %get-tuple-element.34), channel_id=1, source_target_pairs={{0,16},{16,0},{1,17},{17,1},{2,18},{18,2},{3,19},{19,3},{4,20},{20... | collective-permute-start | bytes 1474568 | tf_op jit(solution)/shard_map/ppermute | solution.py:288
  111.4 10.9 %copy-start.2 = (s32[4]{0:T(128)S(1)}, s32[4]{0:T(128)}, u32[]{:S(2)}) copy-start(s32[4]{0:T(128)} %pad_add_fusion.place) | copy-start | bytes 52
  111.4 10.9 %copy-start.3 = (f32[1,128]{1,0:T(1,128)S(1)}, f32[1,128]{1,0:T(1,128)}, u32[]{:S(2)}) copy-start(f32[1,128]{1,0:T(1,128)} %get-tuple-element.44.count) | copy-start | bytes 1540
  117.5 35.6 %copy-start = (bf16[384,2176]{1,0:T(8,128)(2,1)S(1)}, bf16[384,2176]{1,0:T(8,128)(2,1)}, u32[]{:S(2)}) copy-start(bf16[384,2176]{1,0:T(8,128)(2,1)} %get-tuple-element.32.tok.tok_in) | copy-start | bytes 5013508
  117.5 4.8 %collective-permute-start.16 = (f32[192,1280]{1,0:T(8,128)}, f32[192,1280]{1,0:T(8,128)S(1)}, u32[]{:S(2)}, u32[]{:S(2)}) collective-permute-start(f32[192,1280]{1,0:T(8,128)} %get-tuple-element.38), channel_id=1, source_target_pairs={{0,16},{16,0},{1,17},{17,1},{2,18},{18,2},{3,19},{19,3},{4,20},{20... | collective-permute-start | bytes 2949128 | tf_op jit(solution)/shard_map/ppermute | solution.py:307
  178.8 10.8 %all-to-all-start.2 = ((f32[16,2,128]{2,1,0:T(2,128)}), f32[16,2,128]{2,1,0:T(2,128)S(1)}, u32[]{:S(2)}, u32[]{:S(2)}) async-start(f32[16,2,128]{2,1,0:T(2,128)} %broadcast_in_dim.10), calls=%async_computation.2 | async-start | bytes 32768 | tf_op jit(solution)/shard_map/all_to_all | solution.py:332
  (5 other events, 13.6 us)
Sparse Core Ops, SparseCore 0:
  11.0 99.4 all-gather.1

commit v13 on v12

--- a/solution.py
+++ b/solution.py
@@ -28,6 +28,7 @@
 UNITS = 896
 MAIN = 640
 SIDE = UNITS - MAIN
+EXTRA = 2 * SIDE + LANES
 PIECE = SLICE + 16
 COLUMNS = 512
 GROUP = 192
@@ -52,8 +53,8 @@
     return lax.dot_general(a, b, dims, preferred_element_type=F32)
 
 
-def early_products(place, down, p0, r1, l1, r2, l2, r3, l3, far_z, s0, s1, s2, s3, far, near, count,
-                   tok_out, tok, w, counts, sems):
+def early_products(place, down, p0, r1, l1, r2, l2, r3, l3, far_z, s0, s1, s2, s3, count, side_out,
+                   tok_out, tok, w, counts, side, sems):
     z, yh, x = place[1], place[2], place[3]
     block = 4 * ROWS
     moves = ((0, p0), (-1, r1), (1, l1), (-2, r2), (2, l2), (-3, r3), (3, l3), (4, far_z))
@@ -77,60 +78,64 @@
     tok_copy.start()
     total = jnp.sum(counts[...].astype(F32), axis=0)[0:1, :]
     count[...] = jnp.where(lax.broadcasted_iota(jnp.int32, (1, LANES), 1) == 64, total, 0.0)
-    for half, out in ((1 - place[0], far), (place[0], near)):
-        rows = pl.ds(pl.multiple_of(half * GROUP, GROUP), GROUP)
-        for n in range(2):
-            part = slice(n * SIDE, (n + 1) * SIDE)
-            out[:, part] = dot(tok[rows, 0:HALF], w[:, part])
-        out[:, 2 * SIDE :] = dot(tok[rows, 0:HALF], down[...])
+    for n in range(2):
+        part = slice(n * SIDE, (n + 1) * SIDE)
+        side[:, part] = dot(tok[:, 0:HALF], w[:, part])
+    side[:, 2 * SIDE :] = dot(tok[:, 0:HALF], down[...])
+    side_copy = pltpu.make_async_copy(side, side_out, sems.at[41])
+    side_copy.start()
     tok_copy.wait()
-
-
-def main_products(place, tok, w_in, far, near, rows, w, sems):
-    halves = [
-        pl.ds(pl.multiple_of(half * GROUP, GROUP), GROUP) for half in (1 - place[0], place[0])
+    side_copy.wait()
+
+
+def main_products(place, tok, side, w_in, far, near, rows, w, sems):
+    chunks = [pl.ds(n * COLUMNS, COLUMNS) for n in range(HALF // COLUMNS)]
+    last = len(chunks)
+    starts, copies = [], []
+    for n, (half, out) in enumerate(((1 - place[0], far), (place[0], near))):
+        mine = pl.ds(pl.multiple_of(half * GROUP, GROUP), GROUP)
+        starts.append(
+            pltpu.make_async_copy(tok.at[mine, pl.ds(0, HALF)], rows.at[pl.ds(n * GROUP, GROUP), :], sems.at[n])
+        )
+        copies.append(pltpu.make_async_copy(side.at[mine, :], out.at[:, pl.ds(2 * MAIN, EXTRA)], sems.at[2 + n]))
+    weights = [
+        pltpu.make_async_copy(w_in.at[chunk, :], w.at[chunk, :], sems.at[4 + n]) for n, chunk in enumerate(chunks)
     ]
-    chunks = [pl.ds(n * COLUMNS, COLUMNS) for n in range(HALF // COLUMNS)]
-    row_copies = [
-        pltpu.make_async_copy(tok.at[half, pl.ds(0, HALF)], rows.at[n], sems.at[n]) for n, half in enumerate(halves)
-    ]
-    copies = [
-        pltpu.make_async_copy(w_in.at[chunk, :], w.at[chunk, :], sems.at[2 + n]) for n, chunk in enumerate(chunks)
-    ]
-    row_copies[0].start()
-    copies[0].start()
-    row_copies[1].start()
-    for copy in copies[1:]:
+    for copy in starts + weights + copies:
         copy.start()
-    for copy in row_copies:
+    for copy in starts:
         copy.wait()
-    for n, (chunk, copy) in enumerate(zip(chunks, copies)):
+    for n in range(last):
+        weights[n].wait()
+        term = dot(rows[:, chunks[n]], w[chunks[n], :])
+        for out, part in ((far, term[0:GROUP]), (near, term[GROUP:])):
+            out[:, 0 : 2 * MAIN] = part if n == 0 else out[:, 0 : 2 * MAIN] + part
+    for copy in copies:
         copy.wait()
-        for at, out in enumerate((far, near)):
-            term = dot(rows[at, :, chunk], w[chunk, :])
-            out[...] = term if n == 0 else out[...] + term
-
-
-def products(place, tok, w):
+
+
+def products(place, tok, side, w):
     return kernel(
         main_products,
-        [((GROUP, 2 * MAIN), F32)] * 2,
-        (place, tok, w),
+        [((GROUP, 2 * MAIN + EXTRA), F32)] * 2,
+        (place, tok, side, w),
         4 * GROUP * HALF * 2 * MAIN, 56,
         scratch=[
-            pltpu.VMEM((2, GROUP, HALF), BF16),
+            pltpu.VMEM((2 * GROUP, HALF), BF16),
             pltpu.VMEM((HALF, 2 * MAIN), BF16),
-            pltpu.SemaphoreType.DMA((2 + HALF // COLUMNS,)),
+            pltpu.SemaphoreType.DMA((4 + HALF // COLUMNS,)),
         ],
-        in_hbm=2,
-    )
-
-
-def score(place, near, partner, side, b_gate, b_up, readout, signs, count, message, low_t, k_out, k, sems):
-    low_b = side[:, 2 * SIDE :].astype(BF16)
-    main = near[...] + partner[...]
-    gate_ref = jnp.concatenate([main[:, 0:MAIN], side[:, 0:SIDE]], axis=1)
-    up_ref = jnp.concatenate([main[:, MAIN:], side[:, SIDE : 2 * SIDE]], axis=1)
+        in_hbm=3,
+    )
+
+
+def score(place, near, partner, b_gate, b_up, readout, signs, count, message, low_t, k_out, k, sems):
+    both = near[...] + partner[...]
+    low_b = both[:, 2 * MAIN + 2 * SIDE :].astype(BF16)
+    gate_ref = jnp.concatenate([both[:, 0:MAIN], both[:, 2 * MAIN : 2 * MAIN + SIDE]], axis=1)
+    up_ref = jnp.concatenate(
+        [both[:, MAIN : 2 * MAIN], both[:, 2 * MAIN + SIDE : 2 * MAIN + 2 * SIDE]], axis=1
+    )
     gate_pol = gate_ref + dot(low_b, b_gate[...])
     up_pol = up_ref + dot(low_b, b_up[...])
     sig_ref = jax.nn.sigmoid(gate_ref)
@@ -267,26 +272,25 @@
     stacks = [stack] + [fetch(stack, "x", j) for j in (1, 2, 3)]
     for step in range(2):
         ring += [along(ring[-2], "z", 1), along(ring[-1], "z", -1)]
-    ring.append(along(ring[-2], "z", 1))
+    ring.append(along(four, "z", 4))
 
     down_half = down.reshape(16, 2, SLICE, 2 * RANK)
     down_half = jnp.where(core == 0, down_half[:, 0], down_half[:, 1]).reshape(HALF, 2 * RANK)
     down_half = jnp.pad(down_half, ((0, 0), (0, LANES - 2 * RANK)))
-    side_far, side, count_lanes, tok = kernel(
+    count_lanes, side, tok = kernel(
         early_products,
-        [((GROUP, 2 * SIDE + LANES), F32)] * 2 + [((1, LANES), F32), ((2 * GROUP, HALF + LANES), BF16)],
+        [((1, LANES), F32), ((2 * GROUP, EXTRA), F32), ((2 * GROUP, HALF + LANES), BF16)],
         (place, down_half, *ring, *stacks),
         4 * GROUP * HALF * (2 * SIDE + LANES), 56,
         scratch=[
             pltpu.VMEM((2 * GROUP, HALF + LANES), BF16),
             pltpu.VMEM((HALF, 2 * SIDE), BF16),
             pltpu.VMEM((16, PIECE - SLICE, LANES), BF16),
-            pltpu.SemaphoreType.DMA((41,)),
+            pltpu.VMEM((2 * GROUP, EXTRA), F32),
+            pltpu.SemaphoreType.DMA((42,)),
         ],
-        in_hbm=12, out_hbm=1,
-    )
-    side = side + lax.ppermute(side_far, "c", SWAP)
-
+        in_hbm=12, out_hbm=2,
+    )
     b_gate = jnp.pad(up[:RANK], ((0, LANES - RANK), (0, 0)))
     b_up = jnp.pad(up[RANK:], ((RANK, LANES - 2 * RANK), (0, 0)))
     read = readout.reshape(1, UNITS)
@@ -300,15 +304,13 @@
     signs = chosen.astype(BF16) - rejected.astype(BF16)
     valid = (jnp.any(chosen, axis=2) & jnp.any(rejected, axis=2)).astype(F32).reshape(2, 1, LANES)
 
-    w_main, side, b_gate, b_up, read, signs, valid, count_lanes = lax.optimization_barrier(
-        (w_main, side, b_gate, b_up, read, signs, valid, count_lanes)
-    )
-    far, near = products(place, tok, w_main)
+    w_main, b_gate, b_up, read = lax.optimization_barrier((w_main, b_gate, b_up, read))
+    far, near = products(place, tok, side, w_main)
     partner = lax.ppermute(far, "c", SWAP)
     message, low_t, k = kernel(
         score,
         [((2 * RANK, 1, 5 * LANES), F32), ((2 * RANK, GROUP), F32), ((4, GROUP, UNITS), BF16)],
-        (place, near, partner, side, b_gate, b_up, read, signs, count_lanes),
+        (place, near, partner, b_gate, b_up, read, signs, count_lanes),
         8 * GROUP * UNITS * LANES, 16,
         scratch=[pltpu.VMEM((4, GROUP, UNITS), BF16), pltpu.SemaphoreType.DMA((4,))],
         out_hbm=1,

time: 199 us -> 205 us (1.030)
  blocking collectives: 48.6 us -> 19.7 us
  waiting for transfers between devices: 24.4 us -> 42.9 us
  starting transfers between devices: 71.7 us -> 81.3 us
  local copies, waits for them, and re-layouts: 9.99 us -> 15.7 us
    all_to_all x1 -> x0, blocking collectives: 25.8 us -> none  [on_device(): lax.all_to_all(message, ('c', 'z', 'yl'), split_axis=0, concat_axis=0)]
    ppermute x6, waiting for transfers between devices: 10.1 us -> 23 us  [fetch(): return lax.ppermute(value, axis, [((i + k) % n, i) for i in range(n)])]
    all_to_all x0 -> x1, starting transfers between devices: none -> 9.08 us  [on_device(): lax.all_to_all(message, ('c', 'z', 'yl'), split_axis=0, concat_axis=0)]
    all_to_all x0 -> x1, waiting for transfers between devices: none -> 7.36 us  [on_device(): lax.all_to_all(message, ('c', 'z', 'yl'), split_axis=0, concat_axis=0)]
    unnamed x45 -> x59, local copies, waits for them, and re-layouts: 3.39 us -> 8.37 us
    ppermute x1 -> x0, starting transfers between devices: 3.16 us -> none  [on_device(): side = side + lax.ppermute(side_far, 'c', SWAP)]
    all_to_all x1, blocking collectives: 22.8 us -> 19.7 us  [on_device(): lax.all_to_all(outgoing, DP, split_axis=0, concat_axis=0)]
    ppermute x1, starting transfers between devices: 2.41 us -> 5.33 us  [on_device(): partner = lax.ppermute(far, 'c', SWAP)]
  transfers between devices with their start and end apart: 19 -> 19, of which waited for: 7 -> 8; matrix products, arithmetic and copies ran while one was open for 5% -> 5% of each run, Pallas kernels for 3% -> 3%
where the time goes in v13:
time: 205 us; the launch traced here: 204 us
  starting transfers between devices  81.3 us (40%)
  waiting for transfers between devices  42.9 us (21%)
  Pallas kernels  19.7 us (10%)
  blocking collectives  19.7 us (10%)
  between operations  19.7 us (10%)
  local copies, waits for them, and re-layouts  15.7 us (8%)
  other arithmetic  4.77 us (2%)
    ppermute x7, starting transfers between devices, along(): return lax.ppermute(value, axis, [(i, (i + k) % n) for i in range(n)])  33.7 us
    ppermute x6, starting transfers between devices, fetch(): return lax.ppermute(value, axis, [((i + k) % n, i) for i in range(n)])  23.9 us
    ppermute x6, waiting for transfers between devices, fetch(): return lax.ppermute(value, axis, [((i + k) % n, i) for i in range(n)])  23 us
    all_to_all x1, blocking collectives, on_device(): lax.all_to_all(outgoing, DP, split_axis=0, concat_axis=0)  19.7 us
    pallas_call x4, Pallas kernels, kernel(): pl.pallas_call(function, out_shape=tuple((jax.ShapeDtypeStruct(*s) for s...  19.7 us
    all_to_all x1, starting transfers between devices, on_device(): lax.all_to_all(message, ('c', 'z', 'yl'), split_axis=0, concat_axis=0)  9.08 us
    unnamed x59, local copies, waits for them, and re-layouts  8.37 us
    all_to_all x1, waiting for transfers between devices, on_device(): lax.all_to_all(message, ('c', 'z', 'yl'), split_axis=0, concat_axis=0)  7.36 us
  transfers between devices with their start and end apart: 19, of which 8 were waited for; matrix products, arithmetic and copies ran while one was open for 5% of the time, Pallas kernels for 3%

profile of v13, /device:TPU:1, one launch (start us, length us, event | category | flops | bytes accessed | tf_op | source)
XLA Modules:
  0.0 203.8 jit_solution(7992627809640517584)
XLA Ops:
  7.2 1.1 slice_bitcast_fusion.1
  13.1 6.7 %collective-permute-start.2 = (bf16[144,512]{1,0:T(8,128)(2,1)S(1)}, bf16[144,512]{1,0:T(8,128)(2,1)S(1)}, u32[]{:S(2)}, u32[]{:S(2)}) collective-permute-start(bf16[144,512]{1,0:T(8,128)(2,1)S(1)} %fusion.6), channel_id=1, source_target_pairs={{128,0},{256,128},{384,256},{0,384},{129,1},{257,129},{385,257},{1... | collective-permute-start | bytes 442376 | tf_op jit(solution)/shard_map/ppermute | solution.py:243
  19.8 3.5 %collective-permute-start.3 = (bf16[144,512]{1,0:T(8,128)(2,1)S(1)}, bf16[144,512]{1,0:T(8,128)(2,1)S(1)}, u32[]{:S(2)}, u32[]{:S(2)}) collective-permute-start(bf16[144,512]{1,0:T(8,128)(2,1)S(1)} %fusion.6), channel_id=1, source_target_pairs={{256,0},{384,128},{0,256},{128,384},{257,1},{385,129},{1,257},{129... | collective-permute-start | bytes 442376 | tf_op jit(solution)/shard_map/ppermute | solution.py:243
  23.4 4.2 %collective-permute-start.4 = (bf16[144,512]{1,0:T(8,128)(2,1)S(1)}, bf16[144,512]{1,0:T(8,128)(2,1)S(1)}, u32[]{:S(2)}, u32[]{:S(2)}) collective-permute-start(bf16[144,512]{1,0:T(8,128)(2,1)S(1)} %fusion.6), channel_id=1, source_target_pairs={{384,0},{0,128},{128,256},{256,384},{385,1},{1,129},{129,257},{257... | collective-permute-start | bytes 442376 | tf_op jit(solution)/shard_map/ppermute | solution.py:243
  28.0 3.4 %collective-permute-start = (bf16[12,2176]{1,0:T(8,128)(2,1)S(1)}, bf16[12,2176]{1,0:T(8,128)(2,1)S(1)}, u32[]{:S(2)}, u32[]{:S(2)}) collective-permute-start(bf16[12,2176]{1,0:T(8,128)(2,1)S(1)} %get-tuple-element.59), channel_id=1, source_target_pairs={{0,16},{16,0},{1,17},{17,1},{2,18},{18,2},{3,19},{19,3},{4,20},{20... | collective-permute-start | bytes 156680 | tf_op jit(solution)/shard_map/ppermute | solution.py:258
  32.7 2.3 %collective-permute-start.1 = (bf16[24,2176]{1,0:T(8,128)(2,1)S(1)}, bf16[24,2176]{1,0:T(8,128)(2,1)S(1)}, u32[]{:S(2)}, u32[]{:S(2)}) collective-permute-start(bf16[24,2176]{1,0:T(8,128)(2,1)S(1)} %maximum_select_fusion.2), channel_id=1, source_target_pairs={{0,1},{1,0},{2,3},{3,2},{4,5},{5,4},{6,7},{7,6},{8,9},{9,8},{10,11... | collective-permute-start | bytes 313352 | tf_op jit(solution)/shard_map/ppermute | solution.py:40
  35.1 5.7 %collective-permute-done.1 = bf16[24,2176]{1,0:T(8,128)(2,1)S(1)} collective-permute-done((bf16[24,2176]{1,0:T(8,128)(2,1)S(1)}, bf16[24,2176]{1,0:T(8,128)(2,1)S(1)}, u32[]{:S(2)}, u32[]{:S(2)}) %collective-permute-start.1) | collective-permute-done | bytes 104480 | tf_op jit(solution)/shard_map/ppermute | solution.py:40
  40.9 8.4 %collective-permute-start.5 = (bf16[48,2176]{1,0:T(8,128)(2,1)S(1)}, bf16[48,2176]{1,0:T(8,128)(2,1)S(1)}, u32[]{:S(2)}, u32[]{:S(2)}) collective-permute-start(bf16[48,2176]{1,0:T(8,128)(2,1)S(1)} %bitcast.43), channel_id=1, source_target_pairs={{0,2},{2,4},{4,6},{6,8},{8,10},{10,12},{12,14},{14,0},{1,3},{3,5},... | collective-permute-start | bytes 626696 | tf_op jit(solution)/shard_map/ppermute | solution.py:238
  49.3 8.8 %collective-permute-start.6 = (bf16[48,2176]{1,0:T(8,128)(2,1)S(1)}, bf16[48,2176]{1,0:T(8,128)(2,1)S(1)}, u32[]{:S(2)}, u32[]{:S(2)}) collective-permute-start(bf16[48,2176]{1,0:T(8,128)(2,1)S(1)} %bitcast.44), channel_id=1, source_target_pairs={{0,14},{2,0},{4,2},{6,4},{8,6},{10,8},{12,10},{14,12},{1,15},{3,1}... | collective-permute-start | bytes 626696 | tf_op jit(solution)/shard_map/ppermute | solution.py:238
  58.1 3.6 %collective-permute-start.11 = (bf16[48,2176]{1,0:T(8,128)(2,1)S(1)}, bf16[48,2176]{1,0:T(8,128)(2,1)S(1)}, u32[]{:S(2)}, u32[]{:S(2)}) collective-permute-start(bf16[48,2176]{1,0:T(8,128)(2,1)S(1)} %bitcast.45), channel_id=1, source_target_pairs={{0,8},{2,10},{4,12},{6,14},{8,0},{10,2},{12,4},{14,6},{1,9},{3,11}... | collective-permute-start | bytes 626696 | tf_op jit(solution)/shard_map/ppermute | solution.py:238
  61.8 4.5 %collective-permute-start.12 = (bf16[576,512]{1,0:T(8,128)(2,1)S(1)}, bf16[576,512]{1,0:T(8,128)(2,1)S(1)}, u32[]{:S(2)}, u32[]{:S(2)}) collective-permute-start(bf16[576,512]{1,0:T(8,128)(2,1)S(1)} %constant_dynamic-update-slice_fusion.s0), channel_id=1, source_target_pairs={{32,0},{64,32},{96,64},{0,96},{33,1},{65,33},{97,65},{1,97},{34,2}... | collective-permute-start | bytes 1769480 | tf_op jit(solution)/shard_map/ppermute | solution.py:243
  66.3 2.2 %collective-permute-start.13 = (bf16[576,512]{1,0:T(8,128)(2,1)S(1)}, bf16[576,512]{1,0:T(8,128)(2,1)}, u32[]{:S(2)}, u32[]{:S(2)}) collective-permute-start(bf16[576,512]{1,0:T(8,128)(2,1)S(1)} %constant_dynamic-update-slice_fusion.s0), channel_id=1, source_target_pairs={{64,0},{96,32},{0,64},{32,96},{65,1},{97,33},{1,65},{33,97},{66,2}... | collective-permute-start | bytes 1769480 | tf_op jit(solution)/shard_map/ppermute | solution.py:243
  68.6 2.7 %collective-permute-start.14 = (bf16[576,512]{1,0:T(8,128)(2,1)S(1)}, bf16[576,512]{1,0:T(8,128)(2,1)}, u32[]{:S(2)}, u32[]{:S(2)}) collective-permute-start(bf16[576,512]{1,0:T(8,128)(2,1)S(1)} %constant_dynamic-update-slice_fusion.s0), channel_id=1, source_target_pairs={{96,0},{0,32},{32,64},{64,96},{97,1},{1,33},{33,65},{65,97},{98,2}... | collective-permute-start | bytes 1769480 | tf_op jit(solution)/shard_map/ppermute | solution.py:243
  71.3 3.3 %collective-permute-start.7 = (bf16[48,2176]{1,0:T(8,128)(2,1)S(1)}, bf16[48,2176]{1,0:T(8,128)(2,1)}, u32[]{:S(2)}, u32[]{:S(2)}) collective-permute-start(bf16[48,2176]{1,0:T(8,128)(2,1)S(1)} %collective-permute-done.5.r1), channel_id=1, source_target_pairs={{0,2},{2,4},{4,6},{6,8},{8,10},{10,12},{12,14},{14,0},{1,3},{3,5},... | collective-permute-start | bytes 626696 | tf_op jit(solution)/shard_map/ppermute | solution.py:238
  75.2 3.2 %collective-permute-start.8 = (bf16[48,2176]{1,0:T(8,128)(2,1)S(1)}, bf16[48,2176]{1,0:T(8,128)(2,1)}, u32[]{:S(2)}, u32[]{:S(2)}) collective-permute-start(bf16[48,2176]{1,0:T(8,128)(2,1)S(1)} %collective-permute-done.6.l1), channel_id=1, source_target_pairs={{0,14},{2,0},{4,2},{6,4},{8,6},{10,8},{12,10},{14,12},{1,15},{3,1}... | collective-permute-start | bytes 626696 | tf_op jit(solution)/shard_map/ppermute | solution.py:238
  79.4 2.0 collective-permute-start.9
  82.2 4.4 %collective-permute-start.10 = (bf16[48,2176]{1,0:T(8,128)(2,1)}, bf16[48,2176]{1,0:T(8,128)(2,1)S(1)}, u32[]{:S(2)}, u32[]{:S(2)}) collective-permute-start(bf16[48,2176]{1,0:T(8,128)(2,1)} %collective-permute-done.8.l2), channel_id=1, source_target_pairs={{0,14},{2,0},{4,2},{6,4},{8,6},{10,8},{12,10},{14,12},{1,15},{3,1}... | collective-permute-start | bytes 626696 | tf_op jit(solution)/shard_map/ppermute | solution.py:238
  88.9 7.2 %collective-permute-done.13.s2 = bf16[576,512]{1,0:T(8,128)(2,1)} collective-permute-done((bf16[576,512]{1,0:T(8,128)(2,1)S(1)}, bf16[576,512]{1,0:T(8,128)(2,1)}, u32[]{:S(2)}, u32[]{:S(2)}) %collective-permute-start.13) | collective-permute-done | bytes 589856 | tf_op jit(solution)/shard_map/ppermute | solution.py:243
  96.1 15.8 %collective-permute-done.14.s3 = bf16[576,512]{1,0:T(8,128)(2,1)} collective-permute-done((bf16[576,512]{1,0:T(8,128)(2,1)S(1)}, bf16[576,512]{1,0:T(8,128)(2,1)}, u32[]{:S(2)}, u32[]{:S(2)}) %collective-permute-start.14) | collective-permute-done | bytes 589856 | tf_op jit(solution)/shard_map/ppermute | solution.py:243
  113.2 6.6 %shard_map.94 = (f32[1,128]{1,0:T(1,128)}, f32[384,640]{1,0:T(8,128)}, bf16[384,2176]{1,0:T(8,128)(2,1)}) custom-call(s32[4]{0:T(128)} %pad_add_fusion.place, bf16[2048,128]{1,0:T(8,128)(2,1)} %pad.17.down, bf16[48,2176]{1,0:T(8,128)(2,1)} %bitcast.46, bf16[48,2176]{1,0:T(8,128)(2,1)} %copy-done.12, bf16[48,2176]{1,0:T(8,128)(2,1)} %copy-done.13, ...), custom_call_target="tpu_custom_call" | custom-call | flops 1006632960 | bytes 10000000 | tf_op jit(solution)/shard_map/pallas_call | solution.py:225
  119.9 7.3 %shard_map.95 = (f32[192,1920]{1,0:T(8,128)}, f32[192,1920]{1,0:T(8,128)}) custom-call(s32[4]{0:T(128)} %pad_add_fusion.place, bf16[384,2176]{1,0:T(8,128)(2,1)} %get-tuple-element.27.tok.tok_in, f32[384,640]{1,0:T(8,128)} %get-tuple-element.28.side, bf16[2048,1280]{1,0:T(8,128)(2,1)} %all-gather.2.cloned.1.call-done.w_in), custom_call_target="tpu_custom_call" | custom-call | flops 2013265920 | bytes 10000000 | tf_op jit(solution)/shard_map/pallas_call | solution.py:225
  127.1 5.3 %collective-permute-start.15 = (f32[192,1920]{1,0:T(8,128)}, f32[192,1920]{1,0:T(8,128)S(1)}, u32[]{:S(2)}, u32[]{:S(2)}) collective-permute-start(f32[192,1920]{1,0:T(8,128)} %get-tuple-element.31), channel_id=1, source_target_pairs={{0,16},{16,0},{1,17},{17,1},{2,18},{18,2},{3,19},{19,3},{4,20},{20... | collective-permute-start | bytes 4423688 | tf_op jit(solution)/shard_map/ppermute | solution.py:309
  135.6 1.4 copy-done.1
  137.9 3.7 %shard_map.96 = (f32[32,1,640]{2,1,0:T(1,128)S(1)}, f32[32,192]{1,0:T(8,128)S(1)}, bf16[4,192,896]{2,1,0:T(8,128)(2,1)S(1)}) custom-call(s32[4]{0:T(128)S(1)} %copy-done.6, f32[192,1920]{1,0:T(8,128)S(1)} %copy-done.1, f32[192,1920]{1,0:T(8,128)S(1)} %collective-permute-done.15.partner, bf16[128,896]{1,0:T(8,128)(2,1)S(1)} %pad.19.b_gate, ...), custom_call_target="tpu_custom_call" | custom-call | flops 176160768 | bytes 10000000 | tf_op jit(solution)/shard_map/pallas_call | solution.py:225
  141.6 1.1 copy-done.2
  143.4 9.1 %all-to-all-start = ((f32[32,1,640]{2,1,0:T(1,128)}), f32[32,1,640]{2,1,0:T(1,128)S(1)}, u32[]{:S(2)}, u32[]{:S(2)}) async-start(f32[32,1,640]{2,1,0:T(1,128)} %copy-done.5), calls=%async_computation | async-start | bytes 163840 | tf_op jit(solution)/shard_map/all_to_all | solution.py:318
  153.1 7.4 %all-to-all-done.arrived = f32[32,1,640]{2,1,0:T(1,128)S(1)} async-done(((f32[32,1,640]{2,1,0:T(1,128)}), f32[32,1,640]{2,1,0:T(1,128)S(1)}, u32[]{:S(2)}, u32[]{:S(2)}) %all-to-all-start) | async-done | bytes 81952 | tf_op jit(solution)/shard_map/all_to_all | solution.py:318
  160.4 1.3 copy-done.3
  161.8 2.1 %shard_map.97 = (f32[32,1,1280]{2,1,0:T(1,128)S(1)}, f32[8,128]{1,0:T(8,128)S(1)}) custom-call(s32[4]{0:T(128)S(1)} %copy-done.6, f32[32,1,640]{2,1,0:T(1,128)S(1)} %all-to-all-done.arrived, bf16[2,128,192]{2,1,0:T(8,128)(2,1)S(1)} %fusion.7.signs, f32[2,1,128]{2,1,0:T(1,128)S(1)} %bitcast.41, f32[32,192]{1,0:T(8,128)S(1)} %get-tuple-element.37.low_t, ...), custom_call_target="tpu_custom_call" | custom-call | flops 12582912 | bytes 10000000 | tf_op jit(solution)/shard_map/pallas_call | solution.py:225
  163.9 19.7 %all_to_all.15 = f32[32,1,1280]{2,1,0:T(1,128)S(1)} all-to-all(f32[32,1,1280]{2,1,0:T(1,128)S(1)} %get-tuple-element.39), channel_id=1, replica_groups=mesh['yh'=4,'x'=4,'c'=2,'z'=8,'yl'=2] {'yh','x','c'}, dimensions={0} | all-to-all | bytes 327680 | tf_op jit(solution)/shard_map/all_to_all | solution.py:332
  184.4 3.5 %all-to-all-start.2 = ((f32[16,2,128]{2,1,0:T(2,128)}), f32[16,2,128]{2,1,0:T(2,128)S(1)}, u32[]{:S(2)}, u32[]{:S(2)}) async-start(f32[16,2,128]{2,1,0:T(2,128)} %broadcast_in_dim.10), calls=%async_computation.2 | async-start | bytes 32768 | tf_op jit(solution)/shard_map/all_to_all | solution.py:334
  190.9 4.3 %all-to-all-done.2 = f32[16,2,128]{2,1,0:T(2,128)S(1)} async-done(((f32[16,2,128]{2,1,0:T(2,128)}), f32[16,2,128]{2,1,0:T(2,128)S(1)}, u32[]{:S(2)}, u32[]{:S(2)}) %all-to-all-start.2) | async-done | bytes 16416 | tf_op jit(solution)/shard_map/all_to_all | solution.py:334
  (113 shorter events, 18.2 us)
Async XLA Ops:
  7.2 20.5 %copy-start.17 = (bf16[12,4096]{1,0:T(8,128)(2,1)S(1)}, bf16[12,4096]{1,0:T(8,128)(2,1)}, u32[]{:S(2)}) copy-start(bf16[12,4096]{1,0:T(8,128)(2,1)} %param.7) | copy-start | bytes 294916
  7.2 112.6 %all-gather.2.cloned.1.call-start = ((), (), s32[]{:S(2)}) async-start(), calls=%async_computation.3 | async-start | bytes 5570560 | tf_op jit(solution)/shard_map/all_gather | solution.py:252
  8.3 23.1 %copy-start.11 = (bf16[4096,32]{0,1:T(8,128)(2,1)S(1)}, bf16[4096,32]{0,1:T(8,128)(2,1)}, u32[]{:S(2)}) copy-start(bf16[4096,32]{0,1:T(8,128)(2,1)} %param.11) | copy-start | bytes 786436
  13.1 27.7 %collective-permute-start.2 = (bf16[144,512]{1,0:T(8,128)(2,1)S(1)}, bf16[144,512]{1,0:T(8,128)(2,1)S(1)}, u32[]{:S(2)}, u32[]{:S(2)}) collective-permute-start(bf16[144,512]{1,0:T(8,128)(2,1)S(1)} %fusion.6), channel_id=1, source_target_pairs={{128,0},{256,128},{384,256},{0,384},{129,1},{257,129},{385,257},{1... | collective-permute-start | bytes 442376 | tf_op jit(solution)/shard_map/ppermute | solution.py:243
  19.8 21.0 %collective-permute-start.3 = (bf16[144,512]{1,0:T(8,128)(2,1)S(1)}, bf16[144,512]{1,0:T(8,128)(2,1)S(1)}, u32[]{:S(2)}, u32[]{:S(2)}) collective-permute-start(bf16[144,512]{1,0:T(8,128)(2,1)S(1)} %fusion.6), channel_id=1, source_target_pairs={{256,0},{384,128},{0,256},{128,384},{257,1},{385,129},{1,257},{129... | collective-permute-start | bytes 442376 | tf_op jit(solution)/shard_map/ppermute | solution.py:243
  23.4 17.5 %collective-permute-start.4 = (bf16[144,512]{1,0:T(8,128)(2,1)S(1)}, bf16[144,512]{1,0:T(8,128)(2,1)S(1)}, u32[]{:S(2)}, u32[]{:S(2)}) collective-permute-start(bf16[144,512]{1,0:T(8,128)(2,1)S(1)} %fusion.6), channel_id=1, source_target_pairs={{384,0},{0,128},{128,256},{256,384},{385,1},{1,129},{129,257},{257... | collective-permute-start | bytes 442376 | tf_op jit(solution)/shard_map/ppermute | solution.py:243
  28.0 4.6 %collective-permute-start = (bf16[12,2176]{1,0:T(8,128)(2,1)S(1)}, bf16[12,2176]{1,0:T(8,128)(2,1)S(1)}, u32[]{:S(2)}, u32[]{:S(2)}) collective-permute-start(bf16[12,2176]{1,0:T(8,128)(2,1)S(1)} %get-tuple-element.59), channel_id=1, source_target_pairs={{0,16},{16,0},{1,17},{17,1},{2,18},{18,2},{3,19},{19,3},{4,20},{20... | collective-permute-start | bytes 156680 | tf_op jit(solution)/shard_map/ppermute | solution.py:258
  32.7 8.1 %collective-permute-start.1 = (bf16[24,2176]{1,0:T(8,128)(2,1)S(1)}, bf16[24,2176]{1,0:T(8,128)(2,1)S(1)}, u32[]{:S(2)}, u32[]{:S(2)}) collective-permute-start(bf16[24,2176]{1,0:T(8,128)(2,1)S(1)} %maximum_select_fusion.2), channel_id=1, source_target_pairs={{0,1},{1,0},{2,3},{3,2},{4,5},{5,4},{6,7},{7,6},{8,9},{9,8},{10,11... | collective-permute-start | bytes 313352 | tf_op jit(solution)/shard_map/ppermute | solution.py:40
  40.8 46.7 %copy-start.9 = (bf16[2,24,2176]{2,1,0:T(8,128)(2,1)}, bf16[2,24,2176]{2,1,0:T(8,128)(2,1)S(1)}, u32[]{:S(2)}) copy-start(bf16[2,24,2176]{2,1,0:T(8,128)(2,1)S(1)} %maximum_select_fusion) | copy-start | bytes 626692
  40.8 45.8 %copy-start.18 = (bf16[32,896]{1,0:T(8,128)(2,1)S(1)}, bf16[32,896]{1,0:T(8,128)(2,1)}, u32[]{:S(2)}) copy-start(bf16[32,896]{1,0:T(8,128)(2,1)} %param.12) | copy-start | bytes 172036
  40.9 27.6 %collective-permute-start.5 = (bf16[48,2176]{1,0:T(8,128)(2,1)S(1)}, bf16[48,2176]{1,0:T(8,128)(2,1)S(1)}, u32[]{:S(2)}, u32[]{:S(2)}) collective-permute-start(bf16[48,2176]{1,0:T(8,128)(2,1)S(1)} %bitcast.43), channel_id=1, source_target_pairs={{0,2},{2,4},{4,6},{6,8},{8,10},{10,12},{12,14},{14,0},{1,3},{3,5},... | collective-permute-start | bytes 626696 | tf_op jit(solution)/shard_map/ppermute | solution.py:238
  49.3 21.9 %collective-permute-start.6 = (bf16[48,2176]{1,0:T(8,128)(2,1)S(1)}, bf16[48,2176]{1,0:T(8,128)(2,1)S(1)}, u32[]{:S(2)}, u32[]{:S(2)}) collective-permute-start(bf16[48,2176]{1,0:T(8,128)(2,1)S(1)} %bitcast.44), channel_id=1, source_target_pairs={{0,14},{2,0},{4,2},{6,4},{8,6},{10,8},{12,10},{14,12},{1,15},{3,1}... | collective-permute-start | bytes 626696 | tf_op jit(solution)/shard_map/ppermute | solution.py:238
  58.1 16.4 %collective-permute-start.11 = (bf16[48,2176]{1,0:T(8,128)(2,1)S(1)}, bf16[48,2176]{1,0:T(8,128)(2,1)S(1)}, u32[]{:S(2)}, u32[]{:S(2)}) collective-permute-start(bf16[48,2176]{1,0:T(8,128)(2,1)S(1)} %bitcast.45), channel_id=1, source_target_pairs={{0,8},{2,10},{4,12},{6,14},{8,0},{10,2},{12,4},{14,6},{1,9},{3,11}... | collective-permute-start | bytes 626696 | tf_op jit(solution)/shard_map/ppermute | solution.py:238
  61.8 25.8 %copy-start.8 = (bf16[576,512]{1,0:T(8,128)(2,1)}, bf16[576,512]{1,0:T(8,128)(2,1)S(1)}, u32[]{:S(2)}) copy-start(bf16[576,512]{1,0:T(8,128)(2,1)S(1)} %constant_dynamic-update-slice_fusion.s0) | copy-start | bytes 1769476
  61.8 26.5 %copy-start.22 = (bf16[896]{0:T(1024)(128)(2,1)S(1)}, bf16[896]{0:T(1024)(128)(2,1)}, u32[]{:S(2)}) copy-start(bf16[896]{0:T(1024)(128)(2,1)} %param.13) | copy-start | bytes 5380
  61.8 27.1 %collective-permute-start.12 = (bf16[576,512]{1,0:T(8,128)(2,1)S(1)}, bf16[576,512]{1,0:T(8,128)(2,1)S(1)}, u32[]{:S(2)}, u32[]{:S(2)}) collective-permute-start(bf16[576,512]{1,0:T(8,128)(2,1)S(1)} %constant_dynamic-update-slice_fusion.s0), channel_id=1, source_target_pairs={{32,0},{64,32},{96,64},{0,96},{33,1},{65,33},{97,65},{1,97},{34,2}... | collective-permute-start | bytes 1769480 | tf_op jit(solution)/shard_map/ppermute | solution.py:243
  66.3 29.8 %collective-permute-start.13 = (bf16[576,512]{1,0:T(8,128)(2,1)S(1)}, bf16[576,512]{1,0:T(8,128)(2,1)}, u32[]{:S(2)}, u32[]{:S(2)}) collective-permute-start(bf16[576,512]{1,0:T(8,128)(2,1)S(1)} %constant_dynamic-update-slice_fusion.s0), channel_id=1, source_target_pairs={{64,0},{96,32},{0,64},{32,96},{65,1},{97,33},{1,65},{33,97},{66,2}... | collective-permute-start | bytes 1769480 | tf_op jit(solution)/shard_map/ppermute | solution.py:243
  68.5 19.0 %copy-start.12 = (bf16[48,2176]{1,0:T(8,128)(2,1)}, bf16[48,2176]{1,0:T(8,128)(2,1)S(1)}, u32[]{:S(2)}) copy-start(bf16[48,2176]{1,0:T(8,128)(2,1)S(1)} %collective-permute-done.5.r1) | copy-start | bytes 626692
  68.6 43.3 %collective-permute-start.14 = (bf16[576,512]{1,0:T(8,128)(2,1)S(1)}, bf16[576,512]{1,0:T(8,128)(2,1)}, u32[]{:S(2)}, u32[]{:S(2)}) collective-permute-start(bf16[576,512]{1,0:T(8,128)(2,1)S(1)} %constant_dynamic-update-slice_fusion.s0), channel_id=1, source_target_pairs={{96,0},{0,32},{32,64},{64,96},{97,1},{1,33},{33,65},{65,97},{98,2}... | collective-permute-start | bytes 1769480 | tf_op jit(solution)/shard_map/ppermute | solution.py:243
  71.3 16.3 %copy-start.13 = (bf16[48,2176]{1,0:T(8,128)(2,1)}, bf16[48,2176]{1,0:T(8,128)(2,1)S(1)}, u32[]{:S(2)}) copy-start(bf16[48,2176]{1,0:T(8,128)(2,1)S(1)} %collective-permute-done.6.l1) | copy-start | bytes 626692
  71.3 8.2 %collective-permute-start.7 = (bf16[48,2176]{1,0:T(8,128)(2,1)S(1)}, bf16[48,2176]{1,0:T(8,128)(2,1)}, u32[]{:S(2)}, u32[]{:S(2)}) collective-permute-start(bf16[48,2176]{1,0:T(8,128)(2,1)S(1)} %collective-permute-done.5.r1), channel_id=1, source_target_pairs={{0,2},{2,4},{4,6},{6,8},{8,10},{10,12},{12,14},{14,0},{1,3},{3,5},... | collective-permute-start | bytes 626696 | tf_op jit(solution)/shard_map/ppermute | solution.py:238
  75.2 6.9 %collective-permute-start.8 = (bf16[48,2176]{1,0:T(8,128)(2,1)S(1)}, bf16[48,2176]{1,0:T(8,128)(2,1)}, u32[]{:S(2)}, u32[]{:S(2)}) collective-permute-start(bf16[48,2176]{1,0:T(8,128)(2,1)S(1)} %collective-permute-done.6.l1), channel_id=1, source_target_pairs={{0,14},{2,0},{4,2},{6,4},{8,6},{10,8},{12,10},{14,12},{1,15},{3,1}... | collective-permute-start | bytes 626696 | tf_op jit(solution)/shard_map/ppermute | solution.py:238
  79.4 32.4 %collective-permute-start.9 = (bf16[48,2176]{1,0:T(8,128)(2,1)}, bf16[48,2176]{1,0:T(8,128)(2,1)S(1)}, u32[]{:S(2)}, u32[]{:S(2)}) collective-permute-start(bf16[48,2176]{1,0:T(8,128)(2,1)} %collective-permute-done.7.r2), channel_id=1, source_target_pairs={{0,2},{2,4},{4,6},{6,8},{8,10},{10,12},{12,14},{14,0},{1,3},{3,5},... | collective-permute-start | bytes 626696 | tf_op jit(solution)/shard_map/ppermute | solution.py:238
  82.2 29.7 %collective-permute-start.10 = (bf16[48,2176]{1,0:T(8,128)(2,1)}, bf16[48,2176]{1,0:T(8,128)(2,1)S(1)}, u32[]{:S(2)}, u32[]{:S(2)}) collective-permute-start(bf16[48,2176]{1,0:T(8,128)(2,1)} %collective-permute-done.8.l2), channel_id=1, source_target_pairs={{0,14},{2,0},{4,2},{6,4},{8,6},{10,8},{12,10},{14,12},{1,15},{3,1}... | collective-permute-start | bytes 626696 | tf_op jit(solution)/shard_map/ppermute | solution.py:238
  88.9 23.0 %copy-start.10 = (bf16[576,512]{1,0:T(8,128)(2,1)}, bf16[576,512]{1,0:T(8,128)(2,1)S(1)}, u32[]{:S(2)}) copy-start(bf16[576,512]{1,0:T(8,128)(2,1)S(1)} %collective-permute-done.12.s1) | copy-start | bytes 1769476
  119.8 12.8 %copy-start = (bf16[384,2176]{1,0:T(8,128)(2,1)S(1)}, bf16[384,2176]{1,0:T(8,128)(2,1)}, u32[]{:S(2)}) copy-start(bf16[384,2176]{1,0:T(8,128)(2,1)} %get-tuple-element.27.tok.tok_in) | copy-start | bytes 5013508
  119.8 15.7 %copy-start.6 = (s32[4]{0:T(128)S(1)}, s32[4]{0:T(128)}, u32[]{:S(2)}) copy-start(s32[4]{0:T(128)} %pad_add_fusion.place) | copy-start | bytes 52
  119.8 15.7 %copy-start.7 = (f32[1,128]{1,0:T(1,128)S(1)}, f32[1,128]{1,0:T(1,128)}, u32[]{:S(2)}) copy-start(f32[1,128]{1,0:T(1,128)} %get-tuple-element.35.count) | copy-start | bytes 1540
  127.1 8.4 %collective-permute-start.15 = (f32[192,1920]{1,0:T(8,128)}, f32[192,1920]{1,0:T(8,128)S(1)}, u32[]{:S(2)}, u32[]{:S(2)}) collective-permute-start(f32[192,1920]{1,0:T(8,128)} %get-tuple-element.31), channel_id=1, source_target_pairs={{0,16},{16,0},{1,17},{17,1},{2,18},{18,2},{3,19},{19,3},{4,20},{20... | collective-permute-start | bytes 4423688 | tf_op jit(solution)/shard_map/ppermute | solution.py:309
  137.9 14.6 %copy-start.21 = (pred[2,128]{1,0:T(4,128)(4,1)S(1)}, pred[2,128]{1,0:T(4,128)(4,1)}, u32[]{:S(2)}) copy-start(pred[2,128]{1,0:T(4,128)(4,1)} %get-tuple-element.41) | copy-start | bytes 772
  143.4 17.1 %all-to-all-start = ((f32[32,1,640]{2,1,0:T(1,128)}), f32[32,1,640]{2,1,0:T(1,128)S(1)}, u32[]{:S(2)}, u32[]{:S(2)}) async-start(f32[32,1,640]{2,1,0:T(1,128)} %copy-done.5), calls=%async_computation | async-start | bytes 163840 | tf_op jit(solution)/shard_map/all_to_all | solution.py:318
  184.4 10.8 %all-to-all-start.2 = ((f32[16,2,128]{2,1,0:T(2,128)}), f32[16,2,128]{2,1,0:T(2,128)S(1)}, u32[]{:S(2)}, u32[]{:S(2)}) async-start(f32[16,2,128]{2,1,0:T(2,128)} %broadcast_in_dim.10), calls=%async_computation.2 | async-start | bytes 32768 | tf_op jit(solution)/shard_map/all_to_all | solution.py:334
  (12 other events, 12.3 us)
Sparse Core Ops, SparseCore 0:
  11.0 107.4 all-gather.1

commit v14 on v12

--- a/solution.py
+++ b/solution.py
@@ -52,7 +52,7 @@
     return lax.dot_general(a, b, dims, preferred_element_type=F32)
 
 
-def early_products(place, down, p0, r1, l1, r2, l2, r3, l3, far_z, s0, s1, s2, s3, far, near, count,
+def early_products(place, down, p0, r1, l1, r2, l2, r3, l3, far_z, s0, s1, s3, s2_low, s2_high, far, near, count,
                    tok_out, tok, w, counts, sems):
     z, yh, x = place[1], place[2], place[3]
     block = 4 * ROWS
@@ -61,13 +61,14 @@
     for n, (k, ref) in enumerate(moves):
         rows = pl.ds(pl.multiple_of(lax.rem(z + 8 + k, 8) * block, block), block)
         copies.append(pltpu.make_async_copy(ref, tok.at[rows, :], sems.at[n]))
-    for j, ref in enumerate((s0, s1, s2, s3)):
-        for k in range(4):
+    parts = [(0, s0, range(4)), (1, s1, range(4)), (3, s3, range(4)), (2, s2_low, (0, 1)), (2, s2_high, (2, 3))]
+    for j, ref, ks in parts:
+        for k in ks:
             source = lax.rem(yh + k, 4) * 4 + lax.rem(x + j, 4)
             rows = pl.ds(pl.multiple_of(source * SLICE, SLICE), SLICE)
             at = 4 * j + k
-            copies.append(pltpu.make_async_copy(ref.at[pl.ds(k * PIECE, SLICE), :], w.at[rows, :], sems.at[8 + at]))
-            spare = ref.at[pl.ds(k * PIECE + SLICE, PIECE - SLICE), pl.ds(0, LANES)]
+            copies.append(pltpu.make_async_copy(ref.at[pl.ds((k - ks[0]) * PIECE, SLICE), :], w.at[rows, :], sems.at[8 + at]))
+            spare = ref.at[pl.ds((k - ks[0]) * PIECE + SLICE, PIECE - SLICE), pl.ds(0, LANES)]
             copies.append(pltpu.make_async_copy(spare, counts.at[at], sems.at[25 + at]))
     for copy in copies:
         copy.start()
@@ -254,17 +255,18 @@
     pair = jnp.where(
         core == 0, jnp.concatenate([keep, take], axis=0), jnp.concatenate([take, keep], axis=0)
     )
-    four = swapped(pair, "yl", yl).reshape(4 * ROWS, HALF + LANES)
     has = [jnp.max((code == q).astype(F32)) for q in range(SEQS)]
     count_rows = jnp.broadcast_to((has[0] * has[1] + has[2] * has[3]).astype(BF16), (16, 2 * SIDE))
     piece = jnp.concatenate(
         [jnp.concatenate([frozen[0, :, MAIN:], frozen[1, :, MAIN:]], axis=1), count_rows], axis=0
     )
     pieces = [piece] + [fetch(piece, "yh", k) for k in (1, 2, 3)]
-    four, *pieces = lax.optimization_barrier((four, *pieces))
+    pair, *pieces = lax.optimization_barrier((pair, *pieces))
+    four = swapped(pair, "yl", yl).reshape(4 * ROWS, HALF + LANES)
     ring = [four, along(four, "z", 1), along(four, "z", -1)]
     stack = jnp.concatenate(pieces, axis=0)
-    stacks = [stack] + [fetch(stack, "x", j) for j in (1, 2, 3)]
+    next_x, last_x = fetch(stack, "x", 1), fetch(stack, "x", 3)
+    stacks = [stack, next_x, last_x, fetch(last_x[: 2 * PIECE], "x", 3), fetch(next_x[2 * PIECE :], "x", 1)]
     for step in range(2):
         ring += [along(ring[-2], "z", 1), along(ring[-1], "z", -1)]
     ring.append(along(ring[-2], "z", 1))
@@ -283,7 +285,7 @@
             pltpu.VMEM((16, PIECE - SLICE, LANES), BF16),
             pltpu.SemaphoreType.DMA((41,)),
         ],
-        in_hbm=12, out_hbm=1,
+        in_hbm=13, out_hbm=1,
     )
     side = side + lax.ppermute(side_far, "c", SWAP)
 

time: 199 us -> 190 us (0.955)
  blocking collectives: 48.6 us -> 35.4 us
  starting transfers between devices: 71.7 us -> 83.9 us
  waiting for transfers between devices: 24.4 us -> 16.7 us
    ppermute x1, starting transfers between devices: 2.31 us -> 12.5 us  [swapped(): far = lax.ppermute(value, axis, SWAP)]
    ppermute x6 -> x7, waiting for transfers between devices: 10.1 us -> 0.02 us  [fetch(): return lax.ppermute(value, axis, [((i + k) % n, i) for i in range(n)])]
    all_to_all x1, blocking collectives: 25.8 us -> 17 us  [on_device(): lax.all_to_all(message, ('c', 'z', 'yl'), split_axis=0, concat_axis=0)]
    ppermute x7, waiting for transfers between devices: 0.54 us -> 8.51 us  [along(): return lax.ppermute(value, axis, [(i, (i + k) % n) for i in range(n)])]
    ppermute x7, starting transfers between devices: 33.1 us -> 27 us  [along(): return lax.ppermute(value, axis, [(i, (i + k) % n) for i in range(n)])]
    ppermute x1, waiting for transfers between devices: 5.62 us -> 0.01 us  [swapped(): far = lax.ppermute(value, axis, SWAP)]
    ppermute x1, starting transfers between devices: 3.16 us -> 7.59 us  [on_device(): side = side + lax.ppermute(side_far, 'c', SWAP)]
    all_to_all x1, blocking collectives: 22.8 us -> 18.4 us  [on_device(): lax.all_to_all(outgoing, DP, split_axis=0, concat_axis=0)]
  transfers between devices with their start and end apart: 19 -> 20, of which waited for: 7 -> 7; matrix products, arithmetic and copies ran while one was open for 5% -> 5% of each run, Pallas kernels for 3% -> 3%
where the time goes in v14:
time: 190 us; the launch traced here: 189 us
  starting transfers between devices  83.9 us (44%)
  blocking collectives  35.4 us (19%)
  between operations  19.7 us (10%)
  Pallas kernels  18 us (9%)
  waiting for transfers between devices  16.7 us (9%)
  local copies, waits for them, and re-layouts  9.32 us (5%)
  other arithmetic  5.71 us (3%)
    ppermute x7, starting transfers between devices, fetch(): return lax.ppermute(value, axis, [((i + k) % n, i) for i in range(n)])  27.5 us
    ppermute x7, starting transfers between devices, along(): return lax.ppermute(value, axis, [(i, (i + k) % n) for i in range(n)])  27 us
    all_to_all x1, blocking collectives, on_device(): lax.all_to_all(outgoing, DP, split_axis=0, concat_axis=0)  18.4 us
    pallas_call x4, Pallas kernels, kernel(): pl.pallas_call(function, out_shape=tuple((jax.ShapeDtypeStruct(*s) for s...  18 us
    all_to_all x1, blocking collectives, on_device(): lax.all_to_all(message, ('c', 'z', 'yl'), split_axis=0, concat_axis=0)  17 us
    ppermute x1, starting transfers between devices, swapped(): far = lax.ppermute(value, axis, SWAP)  12.5 us
    ppermute x7, waiting for transfers between devices, along(): return lax.ppermute(value, axis, [(i, (i + k) % n) for i in range(n)])  8.51 us
    ppermute x1, starting transfers between devices, on_device(): side = side + lax.ppermute(side_far, 'c', SWAP)  7.59 us
  transfers between devices with their start and end apart: 20, of which 7 were waited for; matrix products, arithmetic and copies ran while one was open for 5% of the time, Pallas kernels for 3%

profile of v14, /device:TPU:1, one launch (start us, length us, event | category | flops | bytes accessed | tf_op | source)
XLA Modules:
  0.0 188.8 jit_solution(3207964581712466191)
XLA Ops:
  9.1 1.3 fusion.12
  13.8 6.7 %collective-permute-start.1 = (bf16[144,512]{1,0:T(8,128)(2,1)S(1)}, bf16[144,512]{1,0:T(8,128)(2,1)S(1)}, u32[]{:S(2)}, u32[]{:S(2)}) collective-permute-start(bf16[144,512]{1,0:T(8,128)(2,1)S(1)} %fusion.6), channel_id=1, source_target_pairs={{128,0},{256,128},{384,256},{0,384},{129,1},{257,129},{385,257},{1... | collective-permute-start | bytes 442376 | tf_op jit(solution)/shard_map/ppermute | solution.py:239
  20.6 3.5 %collective-permute-start.2 = (bf16[144,512]{1,0:T(8,128)(2,1)S(1)}, bf16[144,512]{1,0:T(8,128)(2,1)S(1)}, u32[]{:S(2)}, u32[]{:S(2)}) collective-permute-start(bf16[144,512]{1,0:T(8,128)(2,1)S(1)} %fusion.6), channel_id=1, source_target_pairs={{256,0},{384,128},{0,256},{128,384},{257,1},{385,129},{1,257},{129... | collective-permute-start | bytes 442376 | tf_op jit(solution)/shard_map/ppermute | solution.py:239
  24.1 4.2 %collective-permute-start.3 = (bf16[144,512]{1,0:T(8,128)(2,1)S(1)}, bf16[144,512]{1,0:T(8,128)(2,1)S(1)}, u32[]{:S(2)}, u32[]{:S(2)}) collective-permute-start(bf16[144,512]{1,0:T(8,128)(2,1)S(1)} %fusion.6), channel_id=1, source_target_pairs={{384,0},{0,128},{128,256},{256,384},{385,1},{1,129},{129,257},{257... | collective-permute-start | bytes 442376 | tf_op jit(solution)/shard_map/ppermute | solution.py:239
  28.6 3.4 %collective-permute-start = (bf16[12,2176]{1,0:T(8,128)(2,1)S(1)}, bf16[12,2176]{1,0:T(8,128)(2,1)S(1)}, u32[]{:S(2)}, u32[]{:S(2)}) collective-permute-start(bf16[12,2176]{1,0:T(8,128)(2,1)S(1)} %pad_maximum_fusion.1), channel_id=1, source_target_pairs={{0,16},{16,0},{1,17},{17,1},{2,18},{18,2},{3,19},{19,3},{4,20},{20... | collective-permute-start | bytes 156680 | tf_op jit(solution)/shard_map/ppermute | solution.py:254
  34.4 12.5 %collective-permute-start.4 = (bf16[24,2176]{1,0:T(8,128)(2,1)S(1)}, bf16[24,2176]{1,0:T(8,128)(2,1)S(1)}, u32[]{:S(2)}, u32[]{:S(2)}) collective-permute-start(bf16[24,2176]{1,0:T(8,128)(2,1)S(1)} %maximum_select_fusion.1), channel_id=1, source_target_pairs={{0,1},{1,0},{2,3},{3,2},{4,5},{5,4},{6,7},{7,6},{8,9},{9,8},{10,11... | collective-permute-start | bytes 313352 | tf_op jit(solution)/shard_map/ppermute | solution.py:39
  47.1 2.0 %collective-permute-start.13 = (bf16[576,512]{1,0:T(8,128)(2,1)S(1)}, bf16[576,512]{1,0:T(8,128)(2,1)S(1)}, u32[]{:S(2)}, u32[]{:S(2)}) collective-permute-start(bf16[576,512]{1,0:T(8,128)(2,1)S(1)} %constant_dynamic-update-slice_fusion.s0), channel_id=1, source_target_pairs={{96,0},{0,32},{32,64},{64,96},{97,1},{1,33},{33,65},{65,97},{98,2}... | collective-permute-start | bytes 1769480 | tf_op jit(solution)/shard_map/ppermute | solution.py:239
  49.1 4.5 %collective-permute-start.12 = (bf16[576,512]{1,0:T(8,128)(2,1)S(1)}, bf16[576,512]{1,0:T(8,128)(2,1)S(1)}, u32[]{:S(2)}, u32[]{:S(2)}) collective-permute-start(bf16[576,512]{1,0:T(8,128)(2,1)S(1)} %constant_dynamic-update-slice_fusion.s0), channel_id=1, source_target_pairs={{32,0},{64,32},{96,64},{0,96},{33,1},{65,33},{97,65},{1,97},{34,2}... | collective-permute-start | bytes 1769480 | tf_op jit(solution)/shard_map/ppermute | solution.py:239
  53.7 2.6 %collective-permute-start.5 = (bf16[48,2176]{1,0:T(8,128)(2,1)S(1)}, bf16[48,2176]{1,0:T(8,128)(2,1)S(1)}, u32[]{:S(2)}, u32[]{:S(2)}) collective-permute-start(bf16[48,2176]{1,0:T(8,128)(2,1)S(1)} %bitcast.41), channel_id=1, source_target_pairs={{0,2},{2,4},{4,6},{6,8},{8,10},{10,12},{12,14},{14,0},{1,3},{3,5},... | collective-permute-start | bytes 626696 | tf_op jit(solution)/shard_map/ppermute | solution.py:234
  56.4 9.1 %collective-permute-start.6 = (bf16[48,2176]{1,0:T(8,128)(2,1)S(1)}, bf16[48,2176]{1,0:T(8,128)(2,1)S(1)}, u32[]{:S(2)}, u32[]{:S(2)}) collective-permute-start(bf16[48,2176]{1,0:T(8,128)(2,1)S(1)} %bitcast.42), channel_id=1, source_target_pairs={{0,14},{2,0},{4,2},{6,4},{8,6},{10,8},{12,10},{14,12},{1,15},{3,1}... | collective-permute-start | bytes 626696 | tf_op jit(solution)/shard_map/ppermute | solution.py:234
  66.7 1.9 %collective-permute-start.7 = (bf16[48,2176]{1,0:T(8,128)(2,1)S(1)}, bf16[48,2176]{1,0:T(8,128)(2,1)S(1)}, u32[]{:S(2)}, u32[]{:S(2)}) collective-permute-start(bf16[48,2176]{1,0:T(8,128)(2,1)S(1)} %collective-permute-done.5.r1), channel_id=1, source_target_pairs={{0,2},{2,4},{4,6},{6,8},{8,10},{10,12},{12,14},{14,0},{1,3},{3,5},... | collective-permute-start | bytes 626696 | tf_op jit(solution)/shard_map/ppermute | solution.py:234
  68.7 4.9 %collective-permute-start.8 = (bf16[48,2176]{1,0:T(8,128)(2,1)S(1)}, bf16[48,2176]{1,0:T(8,128)(2,1)S(1)}, u32[]{:S(2)}, u32[]{:S(2)}) collective-permute-start(bf16[48,2176]{1,0:T(8,128)(2,1)S(1)} %collective-permute-done.6.l1), channel_id=1, source_target_pairs={{0,14},{2,0},{4,2},{6,4},{8,6},{10,8},{12,10},{14,12},{1,15},{3,1}... | collective-permute-start | bytes 626696 | tf_op jit(solution)/shard_map/ppermute | solution.py:234
  73.6 1.2 collective-permute-done.7.r2
  74.9 1.9 %collective-permute-start.9 = (bf16[48,2176]{1,0:T(8,128)(2,1)S(1)}, bf16[48,2176]{1,0:T(8,128)(2,1)S(1)}, u32[]{:S(2)}, u32[]{:S(2)}) collective-permute-start(bf16[48,2176]{1,0:T(8,128)(2,1)S(1)} %collective-permute-done.7.r2), channel_id=1, source_target_pairs={{0,2},{2,4},{4,6},{6,8},{8,10},{10,12},{12,14},{14,0},{1,3},{3,5},... | collective-permute-start | bytes 626696 | tf_op jit(solution)/shard_map/ppermute | solution.py:234
  76.8 2.5 %collective-permute-start.14 = (bf16[288,512]{1,0:T(8,128)(2,1)S(1)}, bf16[288,512]{1,0:T(8,128)(2,1)S(1)}, u32[]{:S(2)}, u32[]{:S(2)}) collective-permute-start(bf16[288,512]{1,0:T(8,128)(2,1)S(1)} %slice.76), channel_id=1, source_target_pairs={{96,0},{0,32},{32,64},{64,96},{97,1},{1,33},{33,65},{65,97},{98,2}... | collective-permute-start | bytes 884744 | tf_op jit(solution)/shard_map/ppermute | solution.py:239
  79.4 3.9 %collective-permute-start.15 = (bf16[288,512]{1,0:T(8,128)(2,1)S(1)}, bf16[288,512]{1,0:T(8,128)(2,1)S(1)}, u32[]{:S(2)}, u32[]{:S(2)}) collective-permute-start(bf16[288,512]{1,0:T(8,128)(2,1)S(1)} %slice.77), channel_id=1, source_target_pairs={{32,0},{64,32},{96,64},{0,96},{33,1},{65,33},{97,65},{1,97},{34,2}... | collective-permute-start | bytes 884744 | tf_op jit(solution)/shard_map/ppermute | solution.py:239
  84.1 4.6 %collective-permute-start.10 = (bf16[48,2176]{1,0:T(8,128)(2,1)S(1)}, bf16[48,2176]{1,0:T(8,128)(2,1)S(1)}, u32[]{:S(2)}, u32[]{:S(2)}) collective-permute-start(bf16[48,2176]{1,0:T(8,128)(2,1)S(1)} %collective-permute-done.8.l2), channel_id=1, source_target_pairs={{0,14},{2,0},{4,2},{6,4},{8,6},{10,8},{12,10},{14,12},{1,15},{3,1}... | collective-permute-start | bytes 626696 | tf_op jit(solution)/shard_map/ppermute | solution.py:234
  88.7 1.9 %collective-permute-start.11 = (bf16[48,2176]{1,0:T(8,128)(2,1)S(1)}, bf16[48,2176]{1,0:T(8,128)(2,1)S(1)}, u32[]{:S(2)}, u32[]{:S(2)}) collective-permute-start(bf16[48,2176]{1,0:T(8,128)(2,1)S(1)} %collective-permute-done.9.r3), channel_id=1, source_target_pairs={{0,2},{2,4},{4,6},{6,8},{8,10},{10,12},{12,14},{14,0},{1,3},{3,5},... | collective-permute-start | bytes 626696 | tf_op jit(solution)/shard_map/ppermute | solution.py:234
  91.4 5.4 %collective-permute-done.11.far_z = bf16[48,2176]{1,0:T(8,128)(2,1)S(1)} collective-permute-done((bf16[48,2176]{1,0:T(8,128)(2,1)S(1)}, bf16[48,2176]{1,0:T(8,128)(2,1)S(1)}, u32[]{:S(2)}, u32[]{:S(2)}) %collective-permute-start.11) | collective-permute-done | bytes 208928 | tf_op jit(solution)/shard_map/ppermute | solution.py:234
  97.6 6.0 %shard_map.94 = (f32[192,640]{1,0:T(8,128)}, f32[192,640]{1,0:T(8,128)}, f32[1,128]{1,0:T(1,128)}, bf16[384,2176]{1,0:T(8,128)(2,1)}) custom-call(s32[4]{0:T(128)} %pad_add_fusion.place, bf16[2048,128]{1,0:T(8,128)(2,1)} %pad.17.down, bf16[48,2176]{1,0:T(8,128)(2,1)} %bitcast.43, bf16[48,2176]{1,0:T(8,128)(2,1)} %copy-done.11, bf16[48,2176]{1,0:T(8,128)(2,1)} %copy-done.12, ...), custom_call_target="tpu_custom_call" | custom-call | flops 1006632960 | bytes 10000000 | tf_op jit(solution)/shard_map/pallas_call | solution.py:221
  104.8 7.6 %collective-permute-start.16 = (f32[192,640]{1,0:T(8,128)}, f32[192,640]{1,0:T(8,128)S(1)}, u32[]{:S(2)}, u32[]{:S(2)}) collective-permute-start(f32[192,640]{1,0:T(8,128)} %get-tuple-element.34), channel_id=1, source_target_pairs={{0,16},{16,0},{1,17},{17,1},{2,18},{18,2},{3,19},{19,3},{4,20},{20... | collective-permute-start | bytes 1474568 | tf_op jit(solution)/shard_map/ppermute | solution.py:290
  112.8 1.3 collective-permute-done.16
  115.2 6.1 %shard_map.95 = (f32[192,1280]{1,0:T(8,128)}, f32[192,1280]{1,0:T(8,128)}) custom-call(s32[4]{0:T(128)} %pad_add_fusion.place, bf16[384,2176]{1,0:T(8,128)(2,1)} %get-tuple-element.32.tok.tok_in, bf16[2048,1280]{1,0:T(8,128)(2,1)} %all-gather.2.cloned.1.call-done.w_in), custom_call_target="tpu_custom_call" | custom-call | flops 2013265920 | bytes 10000000 | tf_op jit(solution)/shard_map/pallas_call | solution.py:221
  121.3 2.4 %collective-permute-start.17 = (f32[192,1280]{1,0:T(8,128)}, f32[192,1280]{1,0:T(8,128)S(1)}, u32[]{:S(2)}, u32[]{:S(2)}) collective-permute-start(f32[192,1280]{1,0:T(8,128)} %get-tuple-element.38), channel_id=1, source_target_pairs={{0,16},{16,0},{1,17},{17,1},{2,18},{18,2},{3,19},{19,3},{4,20},{20... | collective-permute-start | bytes 2949128 | tf_op jit(solution)/shard_map/ppermute | solution.py:309
  123.7 2.4 %collective-permute-done.17.partner = f32[192,1280]{1,0:T(8,128)S(1)} collective-permute-done((f32[192,1280]{1,0:T(8,128)}, f32[192,1280]{1,0:T(8,128)S(1)}, u32[]{:S(2)}, u32[]{:S(2)}) %collective-permute-start.17) | collective-permute-done | bytes 983072 | tf_op jit(solution)/shard_map/ppermute | solution.py:309
  126.1 1.2 copy-done.1
  127.3 3.8 %shard_map.96 = (f32[32,1,640]{2,1,0:T(1,128)S(1)}, f32[32,192]{1,0:T(8,128)S(1)}, bf16[4,192,896]{2,1,0:T(8,128)(2,1)S(1)}) custom-call(s32[4]{0:T(128)S(1)} %copy-done.2, f32[192,1280]{1,0:T(8,128)S(1)} %copy-done.1, f32[192,1280]{1,0:T(8,128)S(1)} %collective-permute-done.17.partner, f32[192,640]{1,0:T(8,128)S(1)} %add.54.side, ...), custom_call_target="tpu_custom_call" | custom-call | flops 176160768 | bytes 10000000 | tf_op jit(solution)/shard_map/pallas_call | solution.py:221
  131.1 17.0 %all_to_all.15.arrived = f32[32,1,640]{2,1,0:T(1,128)S(1)} all-to-all(f32[32,1,640]{2,1,0:T(1,128)S(1)} %get-tuple-element.45), channel_id=1, replica_groups=mesh['yh'=4,'x'=4,'c'=2,'z'=8,'yl'=2] {'c','z','yl'}, dimensions={0} | all-to-all | bytes 163840 | tf_op jit(solution)/shard_map/all_to_all | solution.py:318
  148.1 2.1 %shard_map.97 = (f32[32,1,1280]{2,1,0:T(1,128)S(1)}, f32[8,128]{1,0:T(8,128)S(1)}) custom-call(s32[4]{0:T(128)S(1)} %copy-done.2, f32[32,1,640]{2,1,0:T(1,128)S(1)} %all_to_all.15.arrived, bf16[2,128,192]{2,1,0:T(8,128)(2,1)S(1)} %fusion.7.signs, f32[2,1,128]{2,1,0:T(1,128)S(1)} %bitcast.39, f32[32,192]{1,0:T(8,128)S(1)} %get-tuple-element.47.low_t, ...), custom_call_target="tpu_custom_call" | custom-call | flops 12582912 | bytes 10000000 | tf_op jit(solution)/shard_map/pallas_call | solution.py:221
  150.2 18.4 %all_to_all.16 = f32[32,1,1280]{2,1,0:T(1,128)S(1)} all-to-all(f32[32,1,1280]{2,1,0:T(1,128)S(1)} %get-tuple-element.49), channel_id=1, replica_groups=mesh['yh'=4,'x'=4,'c'=2,'z'=8,'yl'=2] {'yh','x','c'}, dimensions={0} | all-to-all | bytes 327680 | tf_op jit(solution)/shard_map/all_to_all | solution.py:332
  169.4 3.5 %all-to-all-start.2 = ((f32[16,2,128]{2,1,0:T(2,128)}), f32[16,2,128]{2,1,0:T(2,128)S(1)}, u32[]{:S(2)}, u32[]{:S(2)}) async-start(f32[16,2,128]{2,1,0:T(2,128)} %broadcast_in_dim.10), calls=%async_computation.2 | async-start | bytes 32768 | tf_op jit(solution)/shard_map/all_to_all | solution.py:334
  175.7 4.5 %all-to-all-done.2 = f32[16,2,128]{2,1,0:T(2,128)S(1)} async-done(((f32[16,2,128]{2,1,0:T(2,128)}), f32[16,2,128]{2,1,0:T(2,128)S(1)}, u32[]{:S(2)}, u32[]{:S(2)}) %all-to-all-start.2) | async-done | bytes 16416 | tf_op jit(solution)/shard_map/all_to_all | solution.py:334
  (110 shorter events, 14.5 us)
Async XLA Ops:
  7.2 21.2 %copy-start.18 = (bf16[12,4096]{1,0:T(8,128)(2,1)S(1)}, bf16[12,4096]{1,0:T(8,128)(2,1)}, u32[]{:S(2)}) copy-start(bf16[12,4096]{1,0:T(8,128)(2,1)} %param.7) | copy-start | bytes 294916
  7.2 24.9 %copy-start.10 = (bf16[4096,32]{0,1:T(8,128)(2,1)S(1)}, bf16[4096,32]{0,1:T(8,128)(2,1)}, u32[]{:S(2)}) copy-start(bf16[4096,32]{0,1:T(8,128)(2,1)} %param.11) | copy-start | bytes 786436
  7.2 108.0 %all-gather.2.cloned.1.call-start = ((), (), s32[]{:S(2)}) async-start(), calls=%async_computation.3 | async-start | bytes 5570560 | tf_op jit(solution)/shard_map/all_gather | solution.py:248
  13.8 20.6 %collective-permute-start.1 = (bf16[144,512]{1,0:T(8,128)(2,1)S(1)}, bf16[144,512]{1,0:T(8,128)(2,1)S(1)}, u32[]{:S(2)}, u32[]{:S(2)}) collective-permute-start(bf16[144,512]{1,0:T(8,128)(2,1)S(1)} %fusion.6), channel_id=1, source_target_pairs={{128,0},{256,128},{384,256},{0,384},{129,1},{257,129},{385,257},{1... | collective-permute-start | bytes 442376 | tf_op jit(solution)/shard_map/ppermute | solution.py:239
  20.6 13.9 %collective-permute-start.2 = (bf16[144,512]{1,0:T(8,128)(2,1)S(1)}, bf16[144,512]{1,0:T(8,128)(2,1)S(1)}, u32[]{:S(2)}, u32[]{:S(2)}) collective-permute-start(bf16[144,512]{1,0:T(8,128)(2,1)S(1)} %fusion.6), channel_id=1, source_target_pairs={{256,0},{384,128},{0,256},{128,384},{257,1},{385,129},{1,257},{129... | collective-permute-start | bytes 442376 | tf_op jit(solution)/shard_map/ppermute | solution.py:239
  24.1 10.3 %collective-permute-start.3 = (bf16[144,512]{1,0:T(8,128)(2,1)S(1)}, bf16[144,512]{1,0:T(8,128)(2,1)S(1)}, u32[]{:S(2)}, u32[]{:S(2)}) collective-permute-start(bf16[144,512]{1,0:T(8,128)(2,1)S(1)} %fusion.6), channel_id=1, source_target_pairs={{384,0},{0,128},{128,256},{256,384},{385,1},{1,129},{129,257},{257... | collective-permute-start | bytes 442376 | tf_op jit(solution)/shard_map/ppermute | solution.py:239
  28.6 5.7 %collective-permute-start = (bf16[12,2176]{1,0:T(8,128)(2,1)S(1)}, bf16[12,2176]{1,0:T(8,128)(2,1)S(1)}, u32[]{:S(2)}, u32[]{:S(2)}) collective-permute-start(bf16[12,2176]{1,0:T(8,128)(2,1)S(1)} %pad_maximum_fusion.1), channel_id=1, source_target_pairs={{0,16},{16,0},{1,17},{17,1},{2,18},{18,2},{3,19},{19,3},{4,20},{20... | collective-permute-start | bytes 156680 | tf_op jit(solution)/shard_map/ppermute | solution.py:254
  33.4 23.0 %copy-start.19 = (bf16[32,896]{1,0:T(8,128)(2,1)S(1)}, bf16[32,896]{1,0:T(8,128)(2,1)}, u32[]{:S(2)}) copy-start(bf16[32,896]{1,0:T(8,128)(2,1)} %param.12) | copy-start | bytes 172036
  33.4 23.0 %copy-start.20 = (bf16[896]{0:T(1024)(128)(2,1)S(1)}, bf16[896]{0:T(1024)(128)(2,1)}, u32[]{:S(2)}) copy-start(bf16[896]{0:T(1024)(128)(2,1)} %param.13) | copy-start | bytes 5380
  34.4 19.1 %collective-permute-start.4 = (bf16[24,2176]{1,0:T(8,128)(2,1)S(1)}, bf16[24,2176]{1,0:T(8,128)(2,1)S(1)}, u32[]{:S(2)}, u32[]{:S(2)}) collective-permute-start(bf16[24,2176]{1,0:T(8,128)(2,1)S(1)} %maximum_select_fusion.1), channel_id=1, source_target_pairs={{0,1},{1,0},{2,3},{3,2},{4,5},{5,4},{6,7},{7,6},{8,9},{9,8},{10,11... | collective-permute-start | bytes 313352 | tf_op jit(solution)/shard_map/ppermute | solution.py:39
  47.1 49.8 %copy-start.6 = (bf16[576,512]{1,0:T(8,128)(2,1)}, bf16[576,512]{1,0:T(8,128)(2,1)S(1)}, u32[]{:S(2)}) copy-start(bf16[576,512]{1,0:T(8,128)(2,1)S(1)} %constant_dynamic-update-slice_fusion.s0) | copy-start | bytes 1769476
  47.1 29.7 %collective-permute-start.13 = (bf16[576,512]{1,0:T(8,128)(2,1)S(1)}, bf16[576,512]{1,0:T(8,128)(2,1)S(1)}, u32[]{:S(2)}, u32[]{:S(2)}) collective-permute-start(bf16[576,512]{1,0:T(8,128)(2,1)S(1)} %constant_dynamic-update-slice_fusion.s0), channel_id=1, source_target_pairs={{96,0},{0,32},{32,64},{64,96},{97,1},{1,33},{33,65},{65,97},{98,2}... | collective-permute-start | bytes 1769480 | tf_op jit(solution)/shard_map/ppermute | solution.py:239
  49.1 30.3 %collective-permute-start.12 = (bf16[576,512]{1,0:T(8,128)(2,1)S(1)}, bf16[576,512]{1,0:T(8,128)(2,1)S(1)}, u32[]{:S(2)}, u32[]{:S(2)}) collective-permute-start(bf16[576,512]{1,0:T(8,128)(2,1)S(1)} %constant_dynamic-update-slice_fusion.s0), channel_id=1, source_target_pairs={{32,0},{64,32},{96,64},{0,96},{33,1},{65,33},{97,65},{1,97},{34,2}... | collective-permute-start | bytes 1769480 | tf_op jit(solution)/shard_map/ppermute | solution.py:239
  53.7 43.2 %copy-start.7 = (bf16[2,24,2176]{2,1,0:T(8,128)(2,1)}, bf16[2,24,2176]{2,1,0:T(8,128)(2,1)S(1)}, u32[]{:S(2)}) copy-start(bf16[2,24,2176]{2,1,0:T(8,128)(2,1)S(1)} %maximum_select_fusion) | copy-start | bytes 626692
  53.7 13.1 %collective-permute-start.5 = (bf16[48,2176]{1,0:T(8,128)(2,1)S(1)}, bf16[48,2176]{1,0:T(8,128)(2,1)S(1)}, u32[]{:S(2)}, u32[]{:S(2)}) collective-permute-start(bf16[48,2176]{1,0:T(8,128)(2,1)S(1)} %bitcast.41), channel_id=1, source_target_pairs={{0,2},{2,4},{4,6},{6,8},{8,10},{10,12},{12,14},{14,0},{1,3},{3,5},... | collective-permute-start | bytes 626696 | tf_op jit(solution)/shard_map/ppermute | solution.py:234
  56.4 12.2 %collective-permute-start.6 = (bf16[48,2176]{1,0:T(8,128)(2,1)S(1)}, bf16[48,2176]{1,0:T(8,128)(2,1)S(1)}, u32[]{:S(2)}, u32[]{:S(2)}) collective-permute-start(bf16[48,2176]{1,0:T(8,128)(2,1)S(1)} %bitcast.42), channel_id=1, source_target_pairs={{0,14},{2,0},{4,2},{6,4},{8,6},{10,8},{12,10},{14,12},{1,15},{3,1}... | collective-permute-start | bytes 626696 | tf_op jit(solution)/shard_map/ppermute | solution.py:234
  66.7 30.1 %copy-start.11 = (bf16[48,2176]{1,0:T(8,128)(2,1)}, bf16[48,2176]{1,0:T(8,128)(2,1)S(1)}, u32[]{:S(2)}) copy-start(bf16[48,2176]{1,0:T(8,128)(2,1)S(1)} %collective-permute-done.5.r1) | copy-start | bytes 626692
  66.7 8.1 %collective-permute-start.7 = (bf16[48,2176]{1,0:T(8,128)(2,1)S(1)}, bf16[48,2176]{1,0:T(8,128)(2,1)S(1)}, u32[]{:S(2)}, u32[]{:S(2)}) collective-permute-start(bf16[48,2176]{1,0:T(8,128)(2,1)S(1)} %collective-permute-done.5.r1), channel_id=1, source_target_pairs={{0,2},{2,4},{4,6},{6,8},{8,10},{10,12},{12,14},{14,0},{1,3},{3,5},... | collective-permute-start | bytes 626696 | tf_op jit(solution)/shard_map/ppermute | solution.py:234
  68.7 28.2 %copy-start.12 = (bf16[48,2176]{1,0:T(8,128)(2,1)}, bf16[48,2176]{1,0:T(8,128)(2,1)S(1)}, u32[]{:S(2)}) copy-start(bf16[48,2176]{1,0:T(8,128)(2,1)S(1)} %collective-permute-done.6.l1) | copy-start | bytes 626692
  68.7 15.4 %collective-permute-start.8 = (bf16[48,2176]{1,0:T(8,128)(2,1)S(1)}, bf16[48,2176]{1,0:T(8,128)(2,1)S(1)}, u32[]{:S(2)}, u32[]{:S(2)}) collective-permute-start(bf16[48,2176]{1,0:T(8,128)(2,1)S(1)} %collective-permute-done.6.l1), channel_id=1, source_target_pairs={{0,14},{2,0},{4,2},{6,4},{8,6},{10,8},{12,10},{14,12},{1,15},{3,1}... | collective-permute-start | bytes 626696 | tf_op jit(solution)/shard_map/ppermute | solution.py:234
  74.9 22.0 %copy-start.13 = (bf16[48,2176]{1,0:T(8,128)(2,1)}, bf16[48,2176]{1,0:T(8,128)(2,1)S(1)}, u32[]{:S(2)}) copy-start(bf16[48,2176]{1,0:T(8,128)(2,1)S(1)} %collective-permute-done.7.r2) | copy-start | bytes 626692
  74.9 13.8 %collective-permute-start.9 = (bf16[48,2176]{1,0:T(8,128)(2,1)S(1)}, bf16[48,2176]{1,0:T(8,128)(2,1)S(1)}, u32[]{:S(2)}, u32[]{:S(2)}) collective-permute-start(bf16[48,2176]{1,0:T(8,128)(2,1)S(1)} %collective-permute-done.7.r2), channel_id=1, source_target_pairs={{0,2},{2,4},{4,6},{6,8},{8,10},{10,12},{12,14},{14,0},{1,3},{3,5},... | collective-permute-start | bytes 626696 | tf_op jit(solution)/shard_map/ppermute | solution.py:234
  76.8 20.1 %copy-start.4 = (bf16[576,512]{1,0:T(8,128)(2,1)}, bf16[576,512]{1,0:T(8,128)(2,1)S(1)}, u32[]{:S(2)}) copy-start(bf16[576,512]{1,0:T(8,128)(2,1)S(1)} %collective-permute-done.13.s3) | copy-start | bytes 1769476
  76.8 14.5 %collective-permute-start.14 = (bf16[288,512]{1,0:T(8,128)(2,1)S(1)}, bf16[288,512]{1,0:T(8,128)(2,1)S(1)}, u32[]{:S(2)}, u32[]{:S(2)}) collective-permute-start(bf16[288,512]{1,0:T(8,128)(2,1)S(1)} %slice.76), channel_id=1, source_target_pairs={{96,0},{0,32},{32,64},{64,96},{97,1},{1,33},{33,65},{65,97},{98,2}... | collective-permute-start | bytes 884744 | tf_op jit(solution)/shard_map/ppermute | solution.py:239
  79.4 17.5 %copy-start.5 = (bf16[576,512]{1,0:T(8,128)(2,1)}, bf16[576,512]{1,0:T(8,128)(2,1)S(1)}, u32[]{:S(2)}) copy-start(bf16[576,512]{1,0:T(8,128)(2,1)S(1)} %collective-permute-done.12.s1) | copy-start | bytes 1769476
  79.4 11.9 %collective-permute-start.15 = (bf16[288,512]{1,0:T(8,128)(2,1)S(1)}, bf16[288,512]{1,0:T(8,128)(2,1)S(1)}, u32[]{:S(2)}, u32[]{:S(2)}) collective-permute-start(bf16[288,512]{1,0:T(8,128)(2,1)S(1)} %slice.77), channel_id=1, source_target_pairs={{32,0},{64,32},{96,64},{0,96},{33,1},{65,33},{97,65},{1,97},{34,2}... | collective-permute-start | bytes 884744 | tf_op jit(solution)/shard_map/ppermute | solution.py:239
  84.1 7.3 %collective-permute-start.10 = (bf16[48,2176]{1,0:T(8,128)(2,1)S(1)}, bf16[48,2176]{1,0:T(8,128)(2,1)S(1)}, u32[]{:S(2)}, u32[]{:S(2)}) collective-permute-start(bf16[48,2176]{1,0:T(8,128)(2,1)S(1)} %collective-permute-done.8.l2), channel_id=1, source_target_pairs={{0,14},{2,0},{4,2},{6,4},{8,6},{10,8},{12,10},{14,12},{1,15},{3,1}... | collective-permute-start | bytes 626696 | tf_op jit(solution)/shard_map/ppermute | solution.py:234
  88.7 8.2 %collective-permute-start.11 = (bf16[48,2176]{1,0:T(8,128)(2,1)S(1)}, bf16[48,2176]{1,0:T(8,128)(2,1)S(1)}, u32[]{:S(2)}, u32[]{:S(2)}) collective-permute-start(bf16[48,2176]{1,0:T(8,128)(2,1)S(1)} %collective-permute-done.9.r3), channel_id=1, source_target_pairs={{0,2},{2,4},{4,6},{6,8},{8,10},{10,12},{12,14},{14,0},{1,3},{3,5},... | collective-permute-start | bytes 626696 | tf_op jit(solution)/shard_map/ppermute | solution.py:234
  104.8 9.3 %collective-permute-start.16 = (f32[192,640]{1,0:T(8,128)}, f32[192,640]{1,0:T(8,128)S(1)}, u32[]{:S(2)}, u32[]{:S(2)}) collective-permute-start(f32[192,640]{1,0:T(8,128)} %get-tuple-element.34), channel_id=1, source_target_pairs={{0,16},{16,0},{1,17},{17,1},{2,18},{18,2},{3,19},{19,3},{4,20},{20... | collective-permute-start | bytes 1474568 | tf_op jit(solution)/shard_map/ppermute | solution.py:290
  121.3 26.8 %copy-start = (bf16[384,2176]{1,0:T(8,128)(2,1)S(1)}, bf16[384,2176]{1,0:T(8,128)(2,1)}, u32[]{:S(2)}) copy-start(bf16[384,2176]{1,0:T(8,128)(2,1)} %get-tuple-element.32.tok.tok_in) | copy-start | bytes 5013508
  121.3 4.8 %collective-permute-start.17 = (f32[192,1280]{1,0:T(8,128)}, f32[192,1280]{1,0:T(8,128)S(1)}, u32[]{:S(2)}, u32[]{:S(2)}) collective-permute-start(f32[192,1280]{1,0:T(8,128)} %get-tuple-element.38), channel_id=1, source_target_pairs={{0,16},{16,0},{1,17},{17,1},{2,18},{18,2},{3,19},{19,3},{4,20},{20... | collective-permute-start | bytes 2949128 | tf_op jit(solution)/shard_map/ppermute | solution.py:309
  169.4 10.8 %all-to-all-start.2 = ((f32[16,2,128]{2,1,0:T(2,128)}), f32[16,2,128]{2,1,0:T(2,128)S(1)}, u32[]{:S(2)}, u32[]{:S(2)}) async-start(f32[16,2,128]{2,1,0:T(2,128)} %broadcast_in_dim.10), calls=%async_computation.2 | async-start | bytes 32768 | tf_op jit(solution)/shard_map/all_to_all | solution.py:334
  (9 other events, 61.4 us)
Sparse Core Ops, SparseCore 0:
  11.0 98.5 all-gather.1

commit v15 on v14

--- a/solution.py
+++ b/solution.py
@@ -26,8 +26,9 @@
 HALF = WIDTH // 2
 LANES = 128
 UNITS = 896
-MAIN = 640
-SIDE = UNITS - MAIN
+GATE, UP = 640, 512
+MAIN = GATE + UP
+SIDE = 2 * UNITS - MAIN
 PIECE = SLICE + 16
 COLUMNS = 512
 GROUP = 192
@@ -72,18 +73,22 @@
             copies.append(pltpu.make_async_copy(spare, counts.at[at], sems.at[25 + at]))
     for copy in copies:
         copy.start()
-    for copy in copies:
+    for copy in copies[: len(moves)]:
         copy.wait()
     tok_copy = pltpu.make_async_copy(tok, tok_out, sems.at[24])
     tok_copy.start()
+    halves = [
+        (pl.ds(pl.multiple_of(half * GROUP, GROUP), GROUP), out) for half, out in ((1 - place[0], far), (place[0], near))
+    ]
+    for rows, out in halves:
+        out[:, SIDE:] = dot(tok[rows, 0:HALF], down[...])
+    for copy in copies[len(moves) :]:
+        copy.wait()
     total = jnp.sum(counts[...].astype(F32), axis=0)[0:1, :]
     count[...] = jnp.where(lax.broadcasted_iota(jnp.int32, (1, LANES), 1) == 64, total, 0.0)
-    for half, out in ((1 - place[0], far), (place[0], near)):
-        rows = pl.ds(pl.multiple_of(half * GROUP, GROUP), GROUP)
-        for n in range(2):
-            part = slice(n * SIDE, (n + 1) * SIDE)
+    for rows, out in halves:
+        for part in (slice(0, UNITS - GATE), slice(UNITS - GATE, SIDE)):
             out[:, part] = dot(tok[rows, 0:HALF], w[:, part])
-        out[:, 2 * SIDE :] = dot(tok[rows, 0:HALF], down[...])
     tok_copy.wait()
 
 
@@ -115,12 +120,12 @@
 def products(place, tok, w):
     return kernel(
         main_products,
-        [((GROUP, 2 * MAIN), F32)] * 2,
+        [((GROUP, MAIN), F32)] * 2,
         (place, tok, w),
-        4 * GROUP * HALF * 2 * MAIN, 56,
+        4 * GROUP * HALF * MAIN, 56,
         scratch=[
             pltpu.VMEM((2, GROUP, HALF), BF16),
-            pltpu.VMEM((HALF, 2 * MAIN), BF16),
+            pltpu.VMEM((HALF, MAIN), BF16),
             pltpu.SemaphoreType.DMA((2 + HALF // COLUMNS,)),
         ],
         in_hbm=2,
@@ -128,10 +133,10 @@
 
 
 def score(place, near, partner, side, b_gate, b_up, readout, signs, count, message, low_t, k_out, k, sems):
-    low_b = side[:, 2 * SIDE :].astype(BF16)
+    low_b = side[:, SIDE:].astype(BF16)
     main = near[...] + partner[...]
-    gate_ref = jnp.concatenate([main[:, 0:MAIN], side[:, 0:SIDE]], axis=1)
-    up_ref = jnp.concatenate([main[:, MAIN:], side[:, SIDE : 2 * SIDE]], axis=1)
+    gate_ref = jnp.concatenate([main[:, 0:GATE], side[:, 0 : UNITS - GATE]], axis=1)
+    up_ref = jnp.concatenate([main[:, GATE:], side[:, UNITS - GATE : SIDE]], axis=1)
     gate_pol = gate_ref + dot(low_b, b_gate[...])
     up_pol = up_ref + dot(low_b, b_up[...])
     sig_ref = jax.nn.sigmoid(gate_ref)
@@ -244,7 +249,7 @@
     place = jnp.stack([core, z, yh, x]).astype(jnp.int32)
     code = jnp.where(response_mask > 0, sequence_labels, SEQS)
 
-    main = jnp.concatenate([frozen[0, :, :MAIN], frozen[1, :, :MAIN]], axis=1)
+    main = jnp.concatenate([frozen[0, :, :GATE], frozen[1, :, :UP]], axis=1)
     w_main = lax.all_gather(main, ("yh", "x"), axis=0, tiled=True)
 
     by_core = tokens.reshape(ROWS, 16, 2, SLICE).transpose(2, 0, 1, 3).reshape(2, ROWS, HALF)
@@ -256,9 +261,9 @@
         core == 0, jnp.concatenate([keep, take], axis=0), jnp.concatenate([take, keep], axis=0)
     )
     has = [jnp.max((code == q).astype(F32)) for q in range(SEQS)]
-    count_rows = jnp.broadcast_to((has[0] * has[1] + has[2] * has[3]).astype(BF16), (16, 2 * SIDE))
+    count_rows = jnp.broadcast_to((has[0] * has[1] + has[2] * has[3]).astype(BF16), (16, SIDE))
     piece = jnp.concatenate(
-        [jnp.concatenate([frozen[0, :, MAIN:], frozen[1, :, MAIN:]], axis=1), count_rows], axis=0
+        [jnp.concatenate([frozen[0, :, GATE:], frozen[1, :, UP:]], axis=1), count_rows], axis=0
     )
     pieces = [piece] + [fetch(piece, "yh", k) for k in (1, 2, 3)]
     pair, *pieces = lax.optimization_barrier((pair, *pieces))
@@ -276,12 +281,12 @@
     down_half = jnp.pad(down_half, ((0, 0), (0, LANES - 2 * RANK)))
     side_far, side, count_lanes, tok = kernel(
         early_products,
-        [((GROUP, 2 * SIDE + LANES), F32)] * 2 + [((1, LANES), F32), ((2 * GROUP, HALF + LANES), BF16)],
+        [((GROUP, SIDE + LANES), F32)] * 2 + [((1, LANES), F32), ((2 * GROUP, HALF + LANES), BF16)],
         (place, down_half, *ring, *stacks),
-        4 * GROUP * HALF * (2 * SIDE + LANES), 56,
+        4 * GROUP * HALF * (SIDE + LANES), 56,
         scratch=[
             pltpu.VMEM((2 * GROUP, HALF + LANES), BF16),
-            pltpu.VMEM((HALF, 2 * SIDE), BF16),
+            pltpu.VMEM((HALF, SIDE), BF16),
             pltpu.VMEM((16, PIECE - SLICE, LANES), BF16),
             pltpu.SemaphoreType.DMA((41,)),
         ],

time: 190 us -> 200 us (1.053)
  waiting for transfers between devices: 16.7 us -> 21.1 us
  starting transfers between devices: 83.9 us -> 87.7 us
  local copies, waits for them, and re-layouts: 9.32 us -> 11.9 us
    all_to_all x1, blocking collectives: 17 us -> 11.1 us  [on_device(): lax.all_to_all(message, ('c', 'z', 'yl'), split_axis=0, concat_axis=0)]
    all_to_all x1, blocking collectives: 18.4 us -> 23 us  [on_device(): lax.all_to_all(outgoing, DP, split_axis=0, concat_axis=0)]
    ppermute x7, waiting for transfers between devices: 0.02 us -> 4.26 us  [fetch(): return lax.ppermute(value, axis, [((i + k) % n, i) for i in range(n)])]
    ppermute x7, starting transfers between devices: 27 us -> 30.2 us  [along(): return lax.ppermute(value, axis, [(i, (i + k) % n) for i in range(n)])]
  transfers between devices with their start and end apart: 20 -> 20, of which waited for: 7 -> 8; matrix products, arithmetic and copies ran while one was open for 5% -> 5% of each run, Pallas kernels for 3% -> 3%
where the time goes in v15:
time: 200 us; the launch traced here: 199 us
  starting transfers between devices  87.7 us (44%)
  blocking collectives  34.1 us (17%)
  waiting for transfers between devices  21.1 us (11%)
  between operations  19.8 us (10%)
  Pallas kernels  18.4 us (9%)
  local copies, waits for them, and re-layouts  11.9 us (6%)
  other arithmetic  5.64 us (3%)
    ppermute x7, starting transfers between devices, along(): return lax.ppermute(value, axis, [(i, (i + k) % n) for i in range(n)])  30.2 us
    ppermute x7, starting transfers between devices, fetch(): return lax.ppermute(value, axis, [((i + k) % n, i) for i in range(n)])  27.5 us
    all_to_all x1, blocking collectives, on_device(): lax.all_to_all(outgoing, DP, split_axis=0, concat_axis=0)  23 us
    pallas_call x4, Pallas kernels, kernel(): pl.pallas_call(function, out_shape=tuple((jax.ShapeDtypeStruct(*s) for s...  18.4 us
    ppermute x1, starting transfers between devices, swapped(): far = lax.ppermute(value, axis, SWAP)  12.6 us
    all_to_all x1, blocking collectives, on_device(): lax.all_to_all(message, ('c', 'z', 'yl'), split_axis=0, concat_axis=0)  11.1 us
    ppermute x7, waiting for transfers between devices, along(): return lax.ppermute(value, axis, [(i, (i + k) % n) for i in range(n)])  9.89 us
    ppermute x1, starting transfers between devices, on_device(): side = side + lax.ppermute(side_far, 'c', SWAP)  8.16 us
  transfers between devices with their start and end apart: 20, of which 8 were waited for; matrix products, arithmetic and copies ran while one was open for 5% of the time, Pallas kernels for 3%

profile of v15, /device:TPU:1, one launch (start us, length us, event | category | flops | bytes accessed | tf_op | source)
XLA Modules:
  0.0 198.7 jit_solution(4135218393118195036)
XLA Ops:
  9.9 1.3 fusion.12
  15.6 6.7 %collective-permute-start.1 = (bf16[144,640]{1,0:T(8,128)(2,1)S(1)}, bf16[144,640]{1,0:T(8,128)(2,1)S(1)}, u32[]{:S(2)}, u32[]{:S(2)}) collective-permute-start(bf16[144,640]{1,0:T(8,128)(2,1)S(1)} %fusion.6), channel_id=1, source_target_pairs={{128,0},{256,128},{384,256},{0,384},{129,1},{257,129},{385,257},{1... | collective-permute-start | bytes 552968 | tf_op jit(solution)/shard_map/ppermute | solution.py:244
  22.3 3.5 %collective-permute-start.2 = (bf16[144,640]{1,0:T(8,128)(2,1)S(1)}, bf16[144,640]{1,0:T(8,128)(2,1)S(1)}, u32[]{:S(2)}, u32[]{:S(2)}) collective-permute-start(bf16[144,640]{1,0:T(8,128)(2,1)S(1)} %fusion.6), channel_id=1, source_target_pairs={{256,0},{384,128},{0,256},{128,384},{257,1},{385,129},{1,257},{129... | collective-permute-start | bytes 552968 | tf_op jit(solution)/shard_map/ppermute | solution.py:244
  25.8 4.2 %collective-permute-start.3 = (bf16[144,640]{1,0:T(8,128)(2,1)S(1)}, bf16[144,640]{1,0:T(8,128)(2,1)S(1)}, u32[]{:S(2)}, u32[]{:S(2)}) collective-permute-start(bf16[144,640]{1,0:T(8,128)(2,1)S(1)} %fusion.6), channel_id=1, source_target_pairs={{384,0},{0,128},{128,256},{256,384},{385,1},{1,129},{129,257},{257... | collective-permute-start | bytes 552968 | tf_op jit(solution)/shard_map/ppermute | solution.py:244
  30.4 3.4 %collective-permute-start = (bf16[12,2176]{1,0:T(8,128)(2,1)S(1)}, bf16[12,2176]{1,0:T(8,128)(2,1)S(1)}, u32[]{:S(2)}, u32[]{:S(2)}) collective-permute-start(bf16[12,2176]{1,0:T(8,128)(2,1)S(1)} %pad_maximum_fusion.1), channel_id=1, source_target_pairs={{0,16},{16,0},{1,17},{17,1},{2,18},{18,2},{3,19},{19,3},{4,20},{20... | collective-permute-start | bytes 156680 | tf_op jit(solution)/shard_map/ppermute | solution.py:259
  35.2 4.2 %collective-permute-done.3 = bf16[144,640]{1,0:T(8,128)(2,1)S(1)} collective-permute-done((bf16[144,640]{1,0:T(8,128)(2,1)S(1)}, bf16[144,640]{1,0:T(8,128)(2,1)S(1)}, u32[]{:S(2)}, u32[]{:S(2)}) %collective-permute-start.3) | collective-permute-done | bytes 184352 | tf_op jit(solution)/shard_map/ppermute | solution.py:244
  39.5 12.6 %collective-permute-start.4 = (bf16[24,2176]{1,0:T(8,128)(2,1)S(1)}, bf16[24,2176]{1,0:T(8,128)(2,1)S(1)}, u32[]{:S(2)}, u32[]{:S(2)}) collective-permute-start(bf16[24,2176]{1,0:T(8,128)(2,1)S(1)} %maximum_select_fusion.1), channel_id=1, source_target_pairs={{0,1},{1,0},{2,3},{3,2},{4,5},{5,4},{6,7},{7,6},{8,9},{9,8},{10,11... | collective-permute-start | bytes 313352 | tf_op jit(solution)/shard_map/ppermute | solution.py:40
  52.2 2.8 %collective-permute-start.13 = (bf16[576,640]{1,0:T(8,128)(2,1)S(1)}, bf16[576,640]{1,0:T(8,128)(2,1)S(1)}, u32[]{:S(2)}, u32[]{:S(2)}) collective-permute-start(bf16[576,640]{1,0:T(8,128)(2,1)S(1)} %constant_dynamic-update-slice_fusion.s0), channel_id=1, source_target_pairs={{96,0},{0,32},{32,64},{64,96},{97,1},{1,33},{33,65},{65,97},{98,2}... | collective-permute-start | bytes 2211848 | tf_op jit(solution)/shard_map/ppermute | solution.py:244
  55.0 3.7 %collective-permute-start.12 = (bf16[576,640]{1,0:T(8,128)(2,1)S(1)}, bf16[576,640]{1,0:T(8,128)(2,1)S(1)}, u32[]{:S(2)}, u32[]{:S(2)}) collective-permute-start(bf16[576,640]{1,0:T(8,128)(2,1)S(1)} %constant_dynamic-update-slice_fusion.s0), channel_id=1, source_target_pairs={{32,0},{64,32},{96,64},{0,96},{33,1},{65,33},{97,65},{1,97},{34,2}... | collective-permute-start | bytes 2211848 | tf_op jit(solution)/shard_map/ppermute | solution.py:244
  58.8 4.2 %collective-permute-start.5 = (bf16[48,2176]{1,0:T(8,128)(2,1)S(1)}, bf16[48,2176]{1,0:T(8,128)(2,1)S(1)}, u32[]{:S(2)}, u32[]{:S(2)}) collective-permute-start(bf16[48,2176]{1,0:T(8,128)(2,1)S(1)} %bitcast.41), channel_id=1, source_target_pairs={{0,2},{2,4},{4,6},{6,8},{8,10},{10,12},{12,14},{14,0},{1,3},{3,5},... | collective-permute-start | bytes 626696 | tf_op jit(solution)/shard_map/ppermute | solution.py:239
  63.0 9.4 %collective-permute-start.6 = (bf16[48,2176]{1,0:T(8,128)(2,1)S(1)}, bf16[48,2176]{1,0:T(8,128)(2,1)S(1)}, u32[]{:S(2)}, u32[]{:S(2)}) collective-permute-start(bf16[48,2176]{1,0:T(8,128)(2,1)S(1)} %bitcast.42), channel_id=1, source_target_pairs={{0,14},{2,0},{4,2},{6,4},{8,6},{10,8},{12,10},{14,12},{1,15},{3,1}... | collective-permute-start | bytes 626696 | tf_op jit(solution)/shard_map/ppermute | solution.py:239
  72.5 2.2 %collective-permute-done.5.r1 = bf16[48,2176]{1,0:T(8,128)(2,1)S(1)} collective-permute-done((bf16[48,2176]{1,0:T(8,128)(2,1)S(1)}, bf16[48,2176]{1,0:T(8,128)(2,1)S(1)}, u32[]{:S(2)}, u32[]{:S(2)}) %collective-permute-start.5) | collective-permute-done | bytes 208928 | tf_op jit(solution)/shard_map/ppermute | solution.py:239
  74.6 1.9 collective-permute-start.7
  76.6 4.6 %collective-permute-start.8 = (bf16[48,2176]{1,0:T(8,128)(2,1)S(1)}, bf16[48,2176]{1,0:T(8,128)(2,1)S(1)}, u32[]{:S(2)}, u32[]{:S(2)}) collective-permute-start(bf16[48,2176]{1,0:T(8,128)(2,1)S(1)} %collective-permute-done.6.l1), channel_id=1, source_target_pairs={{0,14},{2,0},{4,2},{6,4},{8,6},{10,8},{12,10},{14,12},{1,15},{3,1}... | collective-permute-start | bytes 626696 | tf_op jit(solution)/shard_map/ppermute | solution.py:239
  81.1 1.6 collective-permute-done.7.r2
  82.8 1.9 collective-permute-start.9
  84.7 1.9 collective-permute-start.14
  86.7 4.6 %collective-permute-start.15 = (bf16[288,640]{1,0:T(8,128)(2,1)S(1)}, bf16[288,640]{1,0:T(8,128)(2,1)S(1)}, u32[]{:S(2)}, u32[]{:S(2)}) collective-permute-start(bf16[288,640]{1,0:T(8,128)(2,1)S(1)} %slice.77), channel_id=1, source_target_pairs={{32,0},{64,32},{96,64},{0,96},{33,1},{65,33},{97,65},{1,97},{34,2}... | collective-permute-start | bytes 1105928 | tf_op jit(solution)/shard_map/ppermute | solution.py:244
  92.9 6.3 %collective-permute-start.10 = (bf16[48,2176]{1,0:T(8,128)(2,1)S(1)}, bf16[48,2176]{1,0:T(8,128)(2,1)S(1)}, u32[]{:S(2)}, u32[]{:S(2)}) collective-permute-start(bf16[48,2176]{1,0:T(8,128)(2,1)S(1)} %collective-permute-done.8.l2), channel_id=1, source_target_pairs={{0,14},{2,0},{4,2},{6,4},{8,6},{10,8},{12,10},{14,12},{1,15},{3,1}... | collective-permute-start | bytes 626696 | tf_op jit(solution)/shard_map/ppermute | solution.py:239
  99.2 1.9 collective-permute-start.11
  101.9 5.5 %collective-permute-done.11.far_z = bf16[48,2176]{1,0:T(8,128)(2,1)S(1)} collective-permute-done((bf16[48,2176]{1,0:T(8,128)(2,1)S(1)}, bf16[48,2176]{1,0:T(8,128)(2,1)S(1)}, u32[]{:S(2)}, u32[]{:S(2)}) %collective-permute-start.11) | collective-permute-done | bytes 208928 | tf_op jit(solution)/shard_map/ppermute | solution.py:239
  109.0 6.3 %shard_map.94 = (f32[192,768]{1,0:T(8,128)}, f32[192,768]{1,0:T(8,128)}, f32[1,128]{1,0:T(1,128)}, bf16[384,2176]{1,0:T(8,128)(2,1)}) custom-call(s32[4]{0:T(128)} %pad_add_fusion.place, bf16[2048,128]{1,0:T(8,128)(2,1)} %pad.17.down, bf16[48,2176]{1,0:T(8,128)(2,1)} %bitcast.43, bf16[48,2176]{1,0:T(8,128)(2,1)} %copy-done.11, bf16[48,2176]{1,0:T(8,128)(2,1)} %copy-done.12, ...), custom_call_target="tpu_custom_call" | custom-call | flops 1207959552 | bytes 10000000 | tf_op jit(solution)/shard_map/pallas_call | solution.py:226
  115.2 8.2 %collective-permute-start.16 = (f32[192,768]{1,0:T(8,128)}, f32[192,768]{1,0:T(8,128)S(1)}, u32[]{:S(2)}, u32[]{:S(2)}) collective-permute-start(f32[192,768]{1,0:T(8,128)} %get-tuple-element.34), channel_id=1, source_target_pairs={{0,16},{16,0},{1,17},{17,1},{2,18},{18,2},{3,19},{19,3},{4,20},{20... | collective-permute-start | bytes 1769480 | tf_op jit(solution)/shard_map/ppermute | solution.py:295
  126.4 6.3 %shard_map.95 = (f32[192,1152]{1,0:T(8,128)}, f32[192,1152]{1,0:T(8,128)}) custom-call(s32[4]{0:T(128)} %pad_add_fusion.place, bf16[384,2176]{1,0:T(8,128)(2,1)} %get-tuple-element.32.tok.tok_in, bf16[2048,1152]{1,0:T(8,128)(2,1)} %all-gather.2.cloned.1.call-done.w_in), custom_call_target="tpu_custom_call" | custom-call | flops 1811939328 | bytes 10000000 | tf_op jit(solution)/shard_map/pallas_call | solution.py:226
  132.7 2.4 %collective-permute-start.17 = (f32[192,1152]{1,0:T(8,128)}, f32[192,1152]{1,0:T(8,128)S(1)}, u32[]{:S(2)}, u32[]{:S(2)}) collective-permute-start(f32[192,1152]{1,0:T(8,128)} %get-tuple-element.38), channel_id=1, source_target_pairs={{0,16},{16,0},{1,17},{17,1},{2,18},{18,2},{3,19},{19,3},{4,20},{20... | collective-permute-start | bytes 2654216 | tf_op jit(solution)/shard_map/ppermute | solution.py:314
  135.1 2.2 %collective-permute-done.17.partner = f32[192,1152]{1,0:T(8,128)S(1)} collective-permute-done((f32[192,1152]{1,0:T(8,128)}, f32[192,1152]{1,0:T(8,128)S(1)}, u32[]{:S(2)}, u32[]{:S(2)}) %collective-permute-start.17) | collective-permute-done | bytes 884768 | tf_op jit(solution)/shard_map/ppermute | solution.py:314
  138.6 3.7 %shard_map.96 = (f32[32,1,640]{2,1,0:T(1,128)S(1)}, f32[32,192]{1,0:T(8,128)S(1)}, bf16[4,192,896]{2,1,0:T(8,128)(2,1)S(1)}) custom-call(s32[4]{0:T(128)S(1)} %copy-done.2, f32[192,1152]{1,0:T(8,128)S(1)} %copy-done.1, f32[192,1152]{1,0:T(8,128)S(1)} %collective-permute-done.17.partner, f32[192,768]{1,0:T(8,128)S(1)} %add.54.side, ...), custom_call_target="tpu_custom_call" | custom-call | flops 176160768 | bytes 10000000 | tf_op jit(solution)/shard_map/pallas_call | solution.py:226
  142.3 11.1 %all_to_all.15.arrived = f32[32,1,640]{2,1,0:T(1,128)S(1)} all-to-all(f32[32,1,640]{2,1,0:T(1,128)S(1)} %get-tuple-element.45), channel_id=1, replica_groups=mesh['yh'=4,'x'=4,'c'=2,'z'=8,'yl'=2] {'c','z','yl'}, dimensions={0} | all-to-all | bytes 163840 | tf_op jit(solution)/shard_map/all_to_all | solution.py:323
  153.4 2.1 %shard_map.97 = (f32[32,1,1280]{2,1,0:T(1,128)S(1)}, f32[8,128]{1,0:T(8,128)S(1)}) custom-call(s32[4]{0:T(128)S(1)} %copy-done.2, f32[32,1,640]{2,1,0:T(1,128)S(1)} %all_to_all.15.arrived, bf16[2,128,192]{2,1,0:T(8,128)(2,1)S(1)} %fusion.7.signs, f32[2,1,128]{2,1,0:T(1,128)S(1)} %bitcast.39, f32[32,192]{1,0:T(8,128)S(1)} %get-tuple-element.47.low_t, ...), custom_call_target="tpu_custom_call" | custom-call | flops 12582912 | bytes 10000000 | tf_op jit(solution)/shard_map/pallas_call | solution.py:226
  155.5 23.0 %all_to_all.16 = f32[32,1,1280]{2,1,0:T(1,128)S(1)} all-to-all(f32[32,1,1280]{2,1,0:T(1,128)S(1)} %get-tuple-element.49), channel_id=1, replica_groups=mesh['yh'=4,'x'=4,'c'=2,'z'=8,'yl'=2] {'yh','x','c'}, dimensions={0} | all-to-all | bytes 327680 | tf_op jit(solution)/shard_map/all_to_all | solution.py:337
  179.3 3.5 %all-to-all-start.2 = ((f32[16,2,128]{2,1,0:T(2,128)}), f32[16,2,128]{2,1,0:T(2,128)S(1)}, u32[]{:S(2)}, u32[]{:S(2)}) async-start(f32[16,2,128]{2,1,0:T(2,128)} %broadcast_in_dim.10), calls=%async_computation.2 | async-start | bytes 32768 | tf_op jit(solution)/shard_map/all_to_all | solution.py:339
  185.7 4.4 %all-to-all-done.2 = f32[16,2,128]{2,1,0:T(2,128)S(1)} async-done(((f32[16,2,128]{2,1,0:T(2,128)}), f32[16,2,128]{2,1,0:T(2,128)S(1)}, u32[]{:S(2)}, u32[]{:S(2)}) %all-to-all-start.2) | async-done | bytes 16416 | tf_op jit(solution)/shard_map/all_to_all | solution.py:339
  (112 shorter events, 17.3 us)
Async XLA Ops:
  7.2 22.9 %copy-start.18 = (bf16[12,4096]{1,0:T(8,128)(2,1)S(1)}, bf16[12,4096]{1,0:T(8,128)(2,1)}, u32[]{:S(2)}) copy-start(bf16[12,4096]{1,0:T(8,128)(2,1)} %param.7) | copy-start | bytes 294916
  7.2 26.7 %copy-start.10 = (bf16[4096,32]{0,1:T(8,128)(2,1)S(1)}, bf16[4096,32]{0,1:T(8,128)(2,1)}, u32[]{:S(2)}) copy-start(bf16[4096,32]{0,1:T(8,128)(2,1)} %param.11) | copy-start | bytes 786436
  7.2 119.2 %all-gather.2.cloned.1.call-start = ((), (), s32[]{:S(2)}) async-start(), calls=%async_computation.3 | async-start | bytes 5013504 | tf_op jit(solution)/shard_map/all_gather | solution.py:253
  15.6 19.6 %collective-permute-start.1 = (bf16[144,640]{1,0:T(8,128)(2,1)S(1)}, bf16[144,640]{1,0:T(8,128)(2,1)S(1)}, u32[]{:S(2)}, u32[]{:S(2)}) collective-permute-start(bf16[144,640]{1,0:T(8,128)(2,1)S(1)} %fusion.6), channel_id=1, source_target_pairs={{128,0},{256,128},{384,256},{0,384},{129,1},{257,129},{385,257},{1... | collective-permute-start | bytes 552968 | tf_op jit(solution)/shard_map/ppermute | solution.py:244
  22.3 12.9 %collective-permute-start.2 = (bf16[144,640]{1,0:T(8,128)(2,1)S(1)}, bf16[144,640]{1,0:T(8,128)(2,1)S(1)}, u32[]{:S(2)}, u32[]{:S(2)}) collective-permute-start(bf16[144,640]{1,0:T(8,128)(2,1)S(1)} %fusion.6), channel_id=1, source_target_pairs={{256,0},{384,128},{0,256},{128,384},{257,1},{385,129},{1,257},{129... | collective-permute-start | bytes 552968 | tf_op jit(solution)/shard_map/ppermute | solution.py:244
  25.8 13.6 %collective-permute-start.3 = (bf16[144,640]{1,0:T(8,128)(2,1)S(1)}, bf16[144,640]{1,0:T(8,128)(2,1)S(1)}, u32[]{:S(2)}, u32[]{:S(2)}) collective-permute-start(bf16[144,640]{1,0:T(8,128)(2,1)S(1)} %fusion.6), channel_id=1, source_target_pairs={{384,0},{0,128},{128,256},{256,384},{385,1},{1,129},{129,257},{257... | collective-permute-start | bytes 552968 | tf_op jit(solution)/shard_map/ppermute | solution.py:244
  30.4 4.7 %collective-permute-start = (bf16[12,2176]{1,0:T(8,128)(2,1)S(1)}, bf16[12,2176]{1,0:T(8,128)(2,1)S(1)}, u32[]{:S(2)}, u32[]{:S(2)}) collective-permute-start(bf16[12,2176]{1,0:T(8,128)(2,1)S(1)} %pad_maximum_fusion.1), channel_id=1, source_target_pairs={{0,16},{16,0},{1,17},{17,1},{2,18},{18,2},{3,19},{19,3},{4,20},{20... | collective-permute-start | bytes 156680 | tf_op jit(solution)/shard_map/ppermute | solution.py:259
  35.2 41.3 %copy-start.19 = (bf16[32,896]{1,0:T(8,128)(2,1)S(1)}, bf16[32,896]{1,0:T(8,128)(2,1)}, u32[]{:S(2)}) copy-start(bf16[32,896]{1,0:T(8,128)(2,1)} %param.12) | copy-start | bytes 172036
  39.5 19.2 %collective-permute-start.4 = (bf16[24,2176]{1,0:T(8,128)(2,1)S(1)}, bf16[24,2176]{1,0:T(8,128)(2,1)S(1)}, u32[]{:S(2)}, u32[]{:S(2)}) collective-permute-start(bf16[24,2176]{1,0:T(8,128)(2,1)S(1)} %maximum_select_fusion.1), channel_id=1, source_target_pairs={{0,1},{1,0},{2,3},{3,2},{4,5},{5,4},{6,7},{7,6},{8,9},{9,8},{10,11... | collective-permute-start | bytes 313352 | tf_op jit(solution)/shard_map/ppermute | solution.py:40
  52.2 34.6 %copy-start.6 = (bf16[576,640]{1,0:T(8,128)(2,1)}, bf16[576,640]{1,0:T(8,128)(2,1)S(1)}, u32[]{:S(2)}) copy-start(bf16[576,640]{1,0:T(8,128)(2,1)S(1)} %constant_dynamic-update-slice_fusion.s0) | copy-start | bytes 2211844
  52.2 32.5 %collective-permute-start.13 = (bf16[576,640]{1,0:T(8,128)(2,1)S(1)}, bf16[576,640]{1,0:T(8,128)(2,1)S(1)}, u32[]{:S(2)}, u32[]{:S(2)}) collective-permute-start(bf16[576,640]{1,0:T(8,128)(2,1)S(1)} %constant_dynamic-update-slice_fusion.s0), channel_id=1, source_target_pairs={{96,0},{0,32},{32,64},{64,96},{97,1},{1,33},{33,65},{65,97},{98,2}... | collective-permute-start | bytes 2211848 | tf_op jit(solution)/shard_map/ppermute | solution.py:244
  55.0 31.7 %collective-permute-start.12 = (bf16[576,640]{1,0:T(8,128)(2,1)S(1)}, bf16[576,640]{1,0:T(8,128)(2,1)S(1)}, u32[]{:S(2)}, u32[]{:S(2)}) collective-permute-start(bf16[576,640]{1,0:T(8,128)(2,1)S(1)} %constant_dynamic-update-slice_fusion.s0), channel_id=1, source_target_pairs={{32,0},{64,32},{96,64},{0,96},{33,1},{65,33},{97,65},{1,97},{34,2}... | collective-permute-start | bytes 2211848 | tf_op jit(solution)/shard_map/ppermute | solution.py:244
  58.8 34.0 %copy-start.7 = (bf16[2,24,2176]{2,1,0:T(8,128)(2,1)}, bf16[2,24,2176]{2,1,0:T(8,128)(2,1)S(1)}, u32[]{:S(2)}) copy-start(bf16[2,24,2176]{2,1,0:T(8,128)(2,1)S(1)} %maximum_select_fusion) | copy-start | bytes 626692
  58.8 15.8 %collective-permute-start.5 = (bf16[48,2176]{1,0:T(8,128)(2,1)S(1)}, bf16[48,2176]{1,0:T(8,128)(2,1)S(1)}, u32[]{:S(2)}, u32[]{:S(2)}) collective-permute-start(bf16[48,2176]{1,0:T(8,128)(2,1)S(1)} %bitcast.41), channel_id=1, source_target_pairs={{0,2},{2,4},{4,6},{6,8},{8,10},{10,12},{12,14},{14,0},{1,3},{3,5},... | collective-permute-start | bytes 626696 | tf_op jit(solution)/shard_map/ppermute | solution.py:239
  63.0 29.8 %copy-start.20 = (bf16[896]{0:T(1024)(128)(2,1)S(1)}, bf16[896]{0:T(1024)(128)(2,1)}, u32[]{:S(2)}) copy-start(bf16[896]{0:T(1024)(128)(2,1)} %param.13) | copy-start | bytes 5380
  63.0 13.5 %collective-permute-start.6 = (bf16[48,2176]{1,0:T(8,128)(2,1)S(1)}, bf16[48,2176]{1,0:T(8,128)(2,1)S(1)}, u32[]{:S(2)}, u32[]{:S(2)}) collective-permute-start(bf16[48,2176]{1,0:T(8,128)(2,1)S(1)} %bitcast.42), channel_id=1, source_target_pairs={{0,14},{2,0},{4,2},{6,4},{8,6},{10,8},{12,10},{14,12},{1,15},{3,1}... | collective-permute-start | bytes 626696 | tf_op jit(solution)/shard_map/ppermute | solution.py:239
  74.6 32.8 %copy-start.11 = (bf16[48,2176]{1,0:T(8,128)(2,1)}, bf16[48,2176]{1,0:T(8,128)(2,1)S(1)}, u32[]{:S(2)}) copy-start(bf16[48,2176]{1,0:T(8,128)(2,1)S(1)} %collective-permute-done.5.r1) | copy-start | bytes 626692
  74.6 8.1 %collective-permute-start.7 = (bf16[48,2176]{1,0:T(8,128)(2,1)S(1)}, bf16[48,2176]{1,0:T(8,128)(2,1)S(1)}, u32[]{:S(2)}, u32[]{:S(2)}) collective-permute-start(bf16[48,2176]{1,0:T(8,128)(2,1)S(1)} %collective-permute-done.5.r1), channel_id=1, source_target_pairs={{0,2},{2,4},{4,6},{6,8},{8,10},{10,12},{12,14},{14,0},{1,3},{3,5},... | collective-permute-start | bytes 626696 | tf_op jit(solution)/shard_map/ppermute | solution.py:239
  76.6 30.9 %copy-start.12 = (bf16[48,2176]{1,0:T(8,128)(2,1)}, bf16[48,2176]{1,0:T(8,128)(2,1)S(1)}, u32[]{:S(2)}) copy-start(bf16[48,2176]{1,0:T(8,128)(2,1)S(1)} %collective-permute-done.6.l1) | copy-start | bytes 626692
  76.6 16.3 %collective-permute-start.8 = (bf16[48,2176]{1,0:T(8,128)(2,1)S(1)}, bf16[48,2176]{1,0:T(8,128)(2,1)S(1)}, u32[]{:S(2)}, u32[]{:S(2)}) collective-permute-start(bf16[48,2176]{1,0:T(8,128)(2,1)S(1)} %collective-permute-done.6.l1), channel_id=1, source_target_pairs={{0,14},{2,0},{4,2},{6,4},{8,6},{10,8},{12,10},{14,12},{1,15},{3,1}... | collective-permute-start | bytes 626696 | tf_op jit(solution)/shard_map/ppermute | solution.py:239
  82.8 24.7 %copy-start.13 = (bf16[48,2176]{1,0:T(8,128)(2,1)}, bf16[48,2176]{1,0:T(8,128)(2,1)S(1)}, u32[]{:S(2)}) copy-start(bf16[48,2176]{1,0:T(8,128)(2,1)S(1)} %collective-permute-done.7.r2) | copy-start | bytes 626692
  82.8 16.5 %collective-permute-start.9 = (bf16[48,2176]{1,0:T(8,128)(2,1)S(1)}, bf16[48,2176]{1,0:T(8,128)(2,1)S(1)}, u32[]{:S(2)}, u32[]{:S(2)}) collective-permute-start(bf16[48,2176]{1,0:T(8,128)(2,1)S(1)} %collective-permute-done.7.r2), channel_id=1, source_target_pairs={{0,2},{2,4},{4,6},{6,8},{8,10},{10,12},{12,14},{14,0},{1,3},{3,5},... | collective-permute-start | bytes 626696 | tf_op jit(solution)/shard_map/ppermute | solution.py:239
  84.7 22.7 %copy-start.4 = (bf16[576,640]{1,0:T(8,128)(2,1)}, bf16[576,640]{1,0:T(8,128)(2,1)S(1)}, u32[]{:S(2)}) copy-start(bf16[576,640]{1,0:T(8,128)(2,1)S(1)} %collective-permute-done.13.s3) | copy-start | bytes 2211844
  84.7 22.7 %collective-permute-start.14 = (bf16[288,640]{1,0:T(8,128)(2,1)S(1)}, bf16[288,640]{1,0:T(8,128)(2,1)S(1)}, u32[]{:S(2)}, u32[]{:S(2)}) collective-permute-start(bf16[288,640]{1,0:T(8,128)(2,1)S(1)} %slice.76), channel_id=1, source_target_pairs={{96,0},{0,32},{32,64},{64,96},{97,1},{1,33},{33,65},{65,97},{98,2}... | collective-permute-start | bytes 1105928 | tf_op jit(solution)/shard_map/ppermute | solution.py:244
  86.7 20.8 %copy-start.5 = (bf16[576,640]{1,0:T(8,128)(2,1)}, bf16[576,640]{1,0:T(8,128)(2,1)S(1)}, u32[]{:S(2)}) copy-start(bf16[576,640]{1,0:T(8,128)(2,1)S(1)} %collective-permute-done.12.s1) | copy-start | bytes 2211844
  86.7 20.7 %collective-permute-start.15 = (bf16[288,640]{1,0:T(8,128)(2,1)S(1)}, bf16[288,640]{1,0:T(8,128)(2,1)S(1)}, u32[]{:S(2)}, u32[]{:S(2)}) collective-permute-start(bf16[288,640]{1,0:T(8,128)(2,1)S(1)} %slice.77), channel_id=1, source_target_pairs={{32,0},{64,32},{96,64},{0,96},{33,1},{65,33},{97,65},{1,97},{34,2}... | collective-permute-start | bytes 1105928 | tf_op jit(solution)/shard_map/ppermute | solution.py:244
  92.9 9.0 %collective-permute-start.10 = (bf16[48,2176]{1,0:T(8,128)(2,1)S(1)}, bf16[48,2176]{1,0:T(8,128)(2,1)S(1)}, u32[]{:S(2)}, u32[]{:S(2)}) collective-permute-start(bf16[48,2176]{1,0:T(8,128)(2,1)S(1)} %collective-permute-done.8.l2), channel_id=1, source_target_pairs={{0,14},{2,0},{4,2},{6,4},{8,6},{10,8},{12,10},{14,12},{1,15},{3,1}... | collective-permute-start | bytes 626696 | tf_op jit(solution)/shard_map/ppermute | solution.py:239
  99.2 8.2 %collective-permute-start.11 = (bf16[48,2176]{1,0:T(8,128)(2,1)S(1)}, bf16[48,2176]{1,0:T(8,128)(2,1)S(1)}, u32[]{:S(2)}, u32[]{:S(2)}) collective-permute-start(bf16[48,2176]{1,0:T(8,128)(2,1)S(1)} %collective-permute-done.9.r3), channel_id=1, source_target_pairs={{0,2},{2,4},{4,6},{6,8},{8,10},{10,12},{12,14},{14,0},{1,3},{3,5},... | collective-permute-start | bytes 626696 | tf_op jit(solution)/shard_map/ppermute | solution.py:239
  115.2 10.0 %collective-permute-start.16 = (f32[192,768]{1,0:T(8,128)}, f32[192,768]{1,0:T(8,128)S(1)}, u32[]{:S(2)}, u32[]{:S(2)}) collective-permute-start(f32[192,768]{1,0:T(8,128)} %get-tuple-element.34), channel_id=1, source_target_pairs={{0,16},{16,0},{1,17},{17,1},{2,18},{18,2},{3,19},{19,3},{4,20},{20... | collective-permute-start | bytes 1769480 | tf_op jit(solution)/shard_map/ppermute | solution.py:295
  132.7 20.7 %copy-start = (bf16[384,2176]{1,0:T(8,128)(2,1)S(1)}, bf16[384,2176]{1,0:T(8,128)(2,1)}, u32[]{:S(2)}) copy-start(bf16[384,2176]{1,0:T(8,128)(2,1)} %get-tuple-element.32.tok.tok_in) | copy-start | bytes 5013508
  132.7 4.7 %collective-permute-start.17 = (f32[192,1152]{1,0:T(8,128)}, f32[192,1152]{1,0:T(8,128)S(1)}, u32[]{:S(2)}, u32[]{:S(2)}) collective-permute-start(f32[192,1152]{1,0:T(8,128)} %get-tuple-element.38), channel_id=1, source_target_pairs={{0,16},{16,0},{1,17},{17,1},{2,18},{18,2},{3,19},{19,3},{4,20},{20... | collective-permute-start | bytes 2654216 | tf_op jit(solution)/shard_map/ppermute | solution.py:314
  179.3 10.8 %all-to-all-start.2 = ((f32[16,2,128]{2,1,0:T(2,128)}), f32[16,2,128]{2,1,0:T(2,128)S(1)}, u32[]{:S(2)}, u32[]{:S(2)}) async-start(f32[16,2,128]{2,1,0:T(2,128)} %broadcast_in_dim.10), calls=%async_computation.2 | async-start | bytes 32768 | tf_op jit(solution)/shard_map/all_to_all | solution.py:339
  (9 other events, 53.8 us)
Sparse Core Ops, SparseCore 0:
  11.0 99.6 all-gather.1

commit v16 on v15

--- a/solution.py
+++ b/solution.py
@@ -26,7 +26,7 @@
 HALF = WIDTH // 2
 LANES = 128
 UNITS = 896
-GATE, UP = 640, 512
+GATE, UP = 768, 640
 MAIN = GATE + UP
 SIDE = 2 * UNITS - MAIN
 PIECE = SLICE + 16

time: 200 us -> 194 us (0.970)
  starting transfers between devices: 87.7 us -> 79.1 us
  blocking collectives: 34.1 us -> 36.6 us
    all_to_all x1, blocking collectives: 11.1 us -> 18.2 us  [on_device(): lax.all_to_all(message, ('c', 'z', 'yl'), split_axis=0, concat_axis=0)]
    ppermute x1, waiting for transfers between devices: 0.01 us -> 6.96 us  [swapped(): far = lax.ppermute(value, axis, SWAP)]
    all_to_all x1, blocking collectives: 23 us -> 18.3 us  [on_device(): lax.all_to_all(outgoing, DP, split_axis=0, concat_axis=0)]
    ppermute x7, waiting for transfers between devices: 4.26 us -> 0.02 us  [fetch(): return lax.ppermute(value, axis, [((i + k) % n, i) for i in range(n)])]
    ppermute x7, starting transfers between devices: 30.2 us -> 26.7 us  [along(): return lax.ppermute(value, axis, [(i, (i + k) % n) for i in range(n)])]
    ppermute x1, starting transfers between devices: 12.6 us -> 9.37 us  [swapped(): far = lax.ppermute(value, axis, SWAP)]
    ppermute x7, waiting for transfers between devices: 9.89 us -> 7.13 us  [along(): return lax.ppermute(value, axis, [(i, (i + k) % n) for i in range(n)])]
  transfers between devices with their start and end apart: 20 -> 20, of which waited for: 8 -> 7; matrix products, arithmetic and copies ran while one was open for 5% -> 5% of each run, Pallas kernels for 3% -> 3%
where the time goes in v16:
time: 194 us; the launch traced here: 193 us
  starting transfers between devices  79.1 us (41%)
  blocking collectives  36.6 us (19%)
  waiting for transfers between devices  22.3 us (11%)
  between operations  19.8 us (10%)
  Pallas kernels  18.7 us (10%)
  local copies, waits for them, and re-layouts  11.4 us (6%)
  other arithmetic  4.94 us (3%)
    ppermute x7, starting transfers between devices, fetch(): return lax.ppermute(value, axis, [((i + k) % n, i) for i in range(n)])  27.5 us
    ppermute x7, starting transfers between devices, along(): return lax.ppermute(value, axis, [(i, (i + k) % n) for i in range(n)])  26.7 us
    pallas_call x4, Pallas kernels, kernel(): pl.pallas_call(function, out_shape=tuple((jax.ShapeDtypeStruct(*s) for s...  18.7 us
    all_to_all x1, blocking collectives, on_device(): lax.all_to_all(outgoing, DP, split_axis=0, concat_axis=0)  18.3 us
    all_to_all x1, blocking collectives, on_device(): lax.all_to_all(message, ('c', 'z', 'yl'), split_axis=0, concat_axis=0)  18.2 us
    ppermute x1, starting transfers between devices, swapped(): far = lax.ppermute(value, axis, SWAP)  9.37 us
    ppermute x7, waiting for transfers between devices, along(): return lax.ppermute(value, axis, [(i, (i + k) % n) for i in range(n)])  7.13 us
    ppermute x1, waiting for transfers between devices, swapped(): far = lax.ppermute(value, axis, SWAP)  6.96 us
  transfers between devices with their start and end apart: 20, of which 7 were waited for; matrix products, arithmetic and copies ran while one was open for 5% of the time, Pallas kernels for 3%

profile of v16, /device:TPU:1, one launch (start us, length us, event | category | flops | bytes accessed | tf_op | source)
XLA Modules:
  0.0 192.9 jit_solution(7950647468257685103)
XLA Ops:
  14.9 6.7 %collective-permute-start.1 = (bf16[144,384]{1,0:T(8,128)(2,1)S(1)}, bf16[144,384]{1,0:T(8,128)(2,1)S(1)}, u32[]{:S(2)}, u32[]{:S(2)}) collective-permute-start(bf16[144,384]{1,0:T(8,128)(2,1)S(1)} %fusion.7), channel_id=1, source_target_pairs={{128,0},{256,128},{384,256},{0,384},{129,1},{257,129},{385,257},{1... | collective-permute-start | bytes 331784 | tf_op jit(solution)/shard_map/ppermute | solution.py:244
  21.6 3.5 %collective-permute-start.2 = (bf16[144,384]{1,0:T(8,128)(2,1)S(1)}, bf16[144,384]{1,0:T(8,128)(2,1)S(1)}, u32[]{:S(2)}, u32[]{:S(2)}) collective-permute-start(bf16[144,384]{1,0:T(8,128)(2,1)S(1)} %fusion.7), channel_id=1, source_target_pairs={{256,0},{384,128},{0,256},{128,384},{257,1},{385,129},{1,257},{129... | collective-permute-start | bytes 331784 | tf_op jit(solution)/shard_map/ppermute | solution.py:244
  25.1 4.2 %collective-permute-start.3 = (bf16[144,384]{1,0:T(8,128)(2,1)S(1)}, bf16[144,384]{1,0:T(8,128)(2,1)S(1)}, u32[]{:S(2)}, u32[]{:S(2)}) collective-permute-start(bf16[144,384]{1,0:T(8,128)(2,1)S(1)} %fusion.7), channel_id=1, source_target_pairs={{384,0},{0,128},{128,256},{256,384},{385,1},{1,129},{129,257},{257... | collective-permute-start | bytes 331784 | tf_op jit(solution)/shard_map/ppermute | solution.py:244
  29.7 3.4 %collective-permute-start = (bf16[12,2176]{1,0:T(8,128)(2,1)S(1)}, bf16[12,2176]{1,0:T(8,128)(2,1)S(1)}, u32[]{:S(2)}, u32[]{:S(2)}) collective-permute-start(bf16[12,2176]{1,0:T(8,128)(2,1)S(1)} %pad_maximum_fusion.1), channel_id=1, source_target_pairs={{0,16},{16,0},{1,17},{17,1},{2,18},{18,2},{3,19},{19,3},{4,20},{20... | collective-permute-start | bytes 156680 | tf_op jit(solution)/shard_map/ppermute | solution.py:259
  36.0 9.4 %collective-permute-start.4 = (bf16[24,2176]{1,0:T(8,128)(2,1)S(1)}, bf16[24,2176]{1,0:T(8,128)(2,1)S(1)}, u32[]{:S(2)}, u32[]{:S(2)}) collective-permute-start(bf16[24,2176]{1,0:T(8,128)(2,1)S(1)} %maximum_select_fusion.1), channel_id=1, source_target_pairs={{0,1},{1,0},{2,3},{3,2},{4,5},{5,4},{6,7},{7,6},{8,9},{9,8},{10,11... | collective-permute-start | bytes 313352 | tf_op jit(solution)/shard_map/ppermute | solution.py:40
  45.4 7.0 %collective-permute-done.4 = bf16[24,2176]{1,0:T(8,128)(2,1)S(1)} collective-permute-done((bf16[24,2176]{1,0:T(8,128)(2,1)S(1)}, bf16[24,2176]{1,0:T(8,128)(2,1)S(1)}, u32[]{:S(2)}, u32[]{:S(2)}) %collective-permute-start.4) | collective-permute-done | bytes 104480 | tf_op jit(solution)/shard_map/ppermute | solution.py:40
  52.5 2.3 %collective-permute-start.5 = (bf16[48,2176]{1,0:T(8,128)(2,1)S(1)}, bf16[48,2176]{1,0:T(8,128)(2,1)S(1)}, u32[]{:S(2)}, u32[]{:S(2)}) collective-permute-start(bf16[48,2176]{1,0:T(8,128)(2,1)S(1)} %bitcast.41), channel_id=1, source_target_pairs={{0,2},{2,4},{4,6},{6,8},{8,10},{10,12},{12,14},{14,0},{1,3},{3,5},... | collective-permute-start | bytes 626696 | tf_op jit(solution)/shard_map/ppermute | solution.py:239
  54.8 3.4 %collective-permute-start.13 = (bf16[576,384]{1,0:T(8,128)(2,1)S(1)}, bf16[576,384]{1,0:T(8,128)(2,1)S(1)}, u32[]{:S(2)}, u32[]{:S(2)}) collective-permute-start(bf16[576,384]{1,0:T(8,128)(2,1)S(1)} %constant_dynamic-update-slice_fusion.s0), channel_id=1, source_target_pairs={{96,0},{0,32},{32,64},{64,96},{97,1},{1,33},{33,65},{65,97},{98,2}... | collective-permute-start | bytes 1327112 | tf_op jit(solution)/shard_map/ppermute | solution.py:244
  58.3 3.2 %collective-permute-start.12 = (bf16[576,384]{1,0:T(8,128)(2,1)S(1)}, bf16[576,384]{1,0:T(8,128)(2,1)S(1)}, u32[]{:S(2)}, u32[]{:S(2)}) collective-permute-start(bf16[576,384]{1,0:T(8,128)(2,1)S(1)} %constant_dynamic-update-slice_fusion.s0), channel_id=1, source_target_pairs={{32,0},{64,32},{96,64},{0,96},{33,1},{65,33},{97,65},{1,97},{34,2}... | collective-permute-start | bytes 1327112 | tf_op jit(solution)/shard_map/ppermute | solution.py:244
  61.4 8.7 %collective-permute-start.6 = (bf16[48,2176]{1,0:T(8,128)(2,1)S(1)}, bf16[48,2176]{1,0:T(8,128)(2,1)S(1)}, u32[]{:S(2)}, u32[]{:S(2)}) collective-permute-start(bf16[48,2176]{1,0:T(8,128)(2,1)S(1)} %bitcast.42), channel_id=1, source_target_pairs={{0,14},{2,0},{4,2},{6,4},{8,6},{10,8},{12,10},{14,12},{1,15},{3,1}... | collective-permute-start | bytes 626696 | tf_op jit(solution)/shard_map/ppermute | solution.py:239
  70.2 1.9 collective-permute-start.7
  73.2 5.4 %collective-permute-start.8 = (bf16[48,2176]{1,0:T(8,128)(2,1)S(1)}, bf16[48,2176]{1,0:T(8,128)(2,1)S(1)}, u32[]{:S(2)}, u32[]{:S(2)}) collective-permute-start(bf16[48,2176]{1,0:T(8,128)(2,1)S(1)} %collective-permute-done.6.l1), channel_id=1, source_target_pairs={{0,14},{2,0},{4,2},{6,4},{8,6},{10,8},{12,10},{14,12},{1,15},{3,1}... | collective-permute-start | bytes 626696 | tf_op jit(solution)/shard_map/ppermute | solution.py:239
  78.6 1.9 collective-permute-start.9
  81.2 2.2 %collective-permute-start.14 = (bf16[288,384]{1,0:T(8,128)(2,1)S(1)}, bf16[288,384]{1,0:T(8,128)(2,1)S(1)}, u32[]{:S(2)}, u32[]{:S(2)}) collective-permute-start(bf16[288,384]{1,0:T(8,128)(2,1)S(1)} %slice.76), channel_id=1, source_target_pairs={{96,0},{0,32},{32,64},{64,96},{97,1},{1,33},{33,65},{65,97},{98,2}... | collective-permute-start | bytes 663560 | tf_op jit(solution)/shard_map/ppermute | solution.py:244
  83.4 4.3 %collective-permute-start.15 = (bf16[288,384]{1,0:T(8,128)(2,1)S(1)}, bf16[288,384]{1,0:T(8,128)(2,1)S(1)}, u32[]{:S(2)}, u32[]{:S(2)}) collective-permute-start(bf16[288,384]{1,0:T(8,128)(2,1)S(1)} %slice.77), channel_id=1, source_target_pairs={{32,0},{64,32},{96,64},{0,96},{33,1},{65,33},{97,65},{1,97},{34,2}... | collective-permute-start | bytes 663560 | tf_op jit(solution)/shard_map/ppermute | solution.py:244
  87.8 4.6 %collective-permute-start.10 = (bf16[48,2176]{1,0:T(8,128)(2,1)S(1)}, bf16[48,2176]{1,0:T(8,128)(2,1)S(1)}, u32[]{:S(2)}, u32[]{:S(2)}) collective-permute-start(bf16[48,2176]{1,0:T(8,128)(2,1)S(1)} %collective-permute-done.8.l2), channel_id=1, source_target_pairs={{0,14},{2,0},{4,2},{6,4},{8,6},{10,8},{12,10},{14,12},{1,15},{3,1}... | collective-permute-start | bytes 626696 | tf_op jit(solution)/shard_map/ppermute | solution.py:239
  92.4 1.9 collective-permute-start.11
  95.1 5.5 %collective-permute-done.11.far_z = bf16[48,2176]{1,0:T(8,128)(2,1)S(1)} collective-permute-done((bf16[48,2176]{1,0:T(8,128)(2,1)S(1)}, bf16[48,2176]{1,0:T(8,128)(2,1)S(1)}, u32[]{:S(2)}, u32[]{:S(2)}) %collective-permute-start.11) | collective-permute-done | bytes 208928 | tf_op jit(solution)/shard_map/ppermute | solution.py:239
  101.3 5.8 %shard_map.94 = (f32[192,512]{1,0:T(8,128)}, f32[192,512]{1,0:T(8,128)}, f32[1,128]{1,0:T(1,128)}, bf16[384,2176]{1,0:T(8,128)(2,1)}) custom-call(s32[4]{0:T(128)} %pad_add_fusion.place, bf16[2048,128]{1,0:T(8,128)(2,1)} %pad.17.down, bf16[48,2176]{1,0:T(8,128)(2,1)} %bitcast.43, bf16[48,2176]{1,0:T(8,128)(2,1)} %copy-done.11, bf16[48,2176]{1,0:T(8,128)(2,1)} %copy-done.12, ...), custom_call_target="tpu_custom_call" | custom-call | flops 805306368 | bytes 10000000 | tf_op jit(solution)/shard_map/pallas_call | solution.py:226
  108.3 6.3 %collective-permute-start.16 = (f32[192,512]{1,0:T(8,128)}, f32[192,512]{1,0:T(8,128)S(1)}, u32[]{:S(2)}, u32[]{:S(2)}) collective-permute-start(f32[192,512]{1,0:T(8,128)} %get-tuple-element.34), channel_id=1, source_target_pairs={{0,16},{16,0},{1,17},{17,1},{2,18},{18,2},{3,19},{19,3},{4,20},{20... | collective-permute-start | bytes 1179656 | tf_op jit(solution)/shard_map/ppermute | solution.py:295
  115.0 1.1 collective-permute-done.16
  116.1 1.1 add.54.side
  117.2 7.0 %shard_map.95 = (f32[192,1408]{1,0:T(8,128)}, f32[192,1408]{1,0:T(8,128)}) custom-call(s32[4]{0:T(128)} %pad_add_fusion.place, bf16[384,2176]{1,0:T(8,128)(2,1)} %get-tuple-element.32.tok.tok_in, bf16[2048,1408]{1,0:T(8,128)(2,1)} %all-gather.2.cloned.1.call-done.w_in), custom_call_target="tpu_custom_call" | custom-call | flops 2214592512 | bytes 10000000 | tf_op jit(solution)/shard_map/pallas_call | solution.py:226
  124.2 2.3 %collective-permute-start.17 = (f32[192,1408]{1,0:T(8,128)}, f32[192,1408]{1,0:T(8,128)S(1)}, u32[]{:S(2)}, u32[]{:S(2)}) collective-permute-start(f32[192,1408]{1,0:T(8,128)} %get-tuple-element.38), channel_id=1, source_target_pairs={{0,16},{16,0},{1,17},{17,1},{2,18},{18,2},{3,19},{19,3},{4,20},{20... | collective-permute-start | bytes 3244040 | tf_op jit(solution)/shard_map/ppermute | solution.py:314
  126.5 2.5 %collective-permute-done.17.partner = f32[192,1408]{1,0:T(8,128)S(1)} collective-permute-done((f32[192,1408]{1,0:T(8,128)}, f32[192,1408]{1,0:T(8,128)S(1)}, u32[]{:S(2)}, u32[]{:S(2)}) %collective-permute-start.17) | collective-permute-done | bytes 1081376 | tf_op jit(solution)/shard_map/ppermute | solution.py:314
  129.0 1.2 copy-done.1
  130.2 3.8 %shard_map.96 = (f32[32,1,640]{2,1,0:T(1,128)S(1)}, f32[32,192]{1,0:T(8,128)S(1)}, bf16[4,192,896]{2,1,0:T(8,128)(2,1)S(1)}) custom-call(s32[4]{0:T(128)S(1)} %copy-done.2, f32[192,1408]{1,0:T(8,128)S(1)} %copy-done.1, f32[192,1408]{1,0:T(8,128)S(1)} %collective-permute-done.17.partner, f32[192,512]{1,0:T(8,128)S(1)} %add.54.side, ...), custom_call_target="tpu_custom_call" | custom-call | flops 176160768 | bytes 10000000 | tf_op jit(solution)/shard_map/pallas_call | solution.py:226
  134.0 18.2 %all_to_all.15.arrived = f32[32,1,640]{2,1,0:T(1,128)S(1)} all-to-all(f32[32,1,640]{2,1,0:T(1,128)S(1)} %get-tuple-element.45), channel_id=1, replica_groups=mesh['yh'=4,'x'=4,'c'=2,'z'=8,'yl'=2] {'c','z','yl'}, dimensions={0} | all-to-all | bytes 163840 | tf_op jit(solution)/shard_map/all_to_all | solution.py:323
  152.3 2.1 %shard_map.97 = (f32[32,1,1280]{2,1,0:T(1,128)S(1)}, f32[8,128]{1,0:T(8,128)S(1)}) custom-call(s32[4]{0:T(128)S(1)} %copy-done.2, f32[32,1,640]{2,1,0:T(1,128)S(1)} %all_to_all.15.arrived, bf16[2,128,192]{2,1,0:T(8,128)(2,1)S(1)} %fusion.6.signs, f32[2,1,128]{2,1,0:T(1,128)S(1)} %bitcast.39, f32[32,192]{1,0:T(8,128)S(1)} %get-tuple-element.47.low_t, ...), custom_call_target="tpu_custom_call" | custom-call | flops 12582912 | bytes 10000000 | tf_op jit(solution)/shard_map/pallas_call | solution.py:226
  154.4 18.3 %all_to_all.16 = f32[32,1,1280]{2,1,0:T(1,128)S(1)} all-to-all(f32[32,1,1280]{2,1,0:T(1,128)S(1)} %get-tuple-element.49), channel_id=1, replica_groups=mesh['yh'=4,'x'=4,'c'=2,'z'=8,'yl'=2] {'yh','x','c'}, dimensions={0} | all-to-all | bytes 327680 | tf_op jit(solution)/shard_map/all_to_all | solution.py:337
  173.5 3.5 %all-to-all-start.2 = ((f32[16,2,128]{2,1,0:T(2,128)}), f32[16,2,128]{2,1,0:T(2,128)S(1)}, u32[]{:S(2)}, u32[]{:S(2)}) async-start(f32[16,2,128]{2,1,0:T(2,128)} %broadcast_in_dim.10), calls=%async_computation.2 | async-start | bytes 32768 | tf_op jit(solution)/shard_map/all_to_all | solution.py:339
  179.8 4.5 %all-to-all-done.2 = f32[16,2,128]{2,1,0:T(2,128)S(1)} async-done(((f32[16,2,128]{2,1,0:T(2,128)}), f32[16,2,128]{2,1,0:T(2,128)S(1)}, u32[]{:S(2)}, u32[]{:S(2)}) %all-to-all-start.2) | async-done | bytes 16416 | tf_op jit(solution)/shard_map/all_to_all | solution.py:339
  (116 shorter events, 15.9 us)
Async XLA Ops:
  7.2 22.2 %copy-start.18 = (bf16[12,4096]{1,0:T(8,128)(2,1)S(1)}, bf16[12,4096]{1,0:T(8,128)(2,1)}, u32[]{:S(2)}) copy-start(bf16[12,4096]{1,0:T(8,128)(2,1)} %param.7) | copy-start | bytes 294916
  7.2 110.0 %all-gather.2.cloned.1.call-start = ((), (), s32[]{:S(2)}) async-start(), calls=%async_computation.3 | async-start | bytes 6127616 | tf_op jit(solution)/shard_map/all_gather | solution.py:253
  8.2 24.9 %copy-start.8 = (bf16[4096,32]{0,1:T(8,128)(2,1)S(1)}, bf16[4096,32]{0,1:T(8,128)(2,1)}, u32[]{:S(2)}) copy-start(bf16[4096,32]{0,1:T(8,128)(2,1)} %param.11) | copy-start | bytes 786436
  14.9 21.1 %collective-permute-start.1 = (bf16[144,384]{1,0:T(8,128)(2,1)S(1)}, bf16[144,384]{1,0:T(8,128)(2,1)S(1)}, u32[]{:S(2)}, u32[]{:S(2)}) collective-permute-start(bf16[144,384]{1,0:T(8,128)(2,1)S(1)} %fusion.7), channel_id=1, source_target_pairs={{128,0},{256,128},{384,256},{0,384},{129,1},{257,129},{385,257},{1... | collective-permute-start | bytes 331784 | tf_op jit(solution)/shard_map/ppermute | solution.py:244
  21.6 14.4 %collective-permute-start.2 = (bf16[144,384]{1,0:T(8,128)(2,1)S(1)}, bf16[144,384]{1,0:T(8,128)(2,1)S(1)}, u32[]{:S(2)}, u32[]{:S(2)}) collective-permute-start(bf16[144,384]{1,0:T(8,128)(2,1)S(1)} %fusion.7), channel_id=1, source_target_pairs={{256,0},{384,128},{0,256},{128,384},{257,1},{385,129},{1,257},{129... | collective-permute-start | bytes 331784 | tf_op jit(solution)/shard_map/ppermute | solution.py:244
  25.1 10.9 %collective-permute-start.3 = (bf16[144,384]{1,0:T(8,128)(2,1)S(1)}, bf16[144,384]{1,0:T(8,128)(2,1)S(1)}, u32[]{:S(2)}, u32[]{:S(2)}) collective-permute-start(bf16[144,384]{1,0:T(8,128)(2,1)S(1)} %fusion.7), channel_id=1, source_target_pairs={{384,0},{0,128},{128,256},{256,384},{385,1},{1,129},{129,257},{257... | collective-permute-start | bytes 331784 | tf_op jit(solution)/shard_map/ppermute | solution.py:244
  29.7 6.2 %collective-permute-start = (bf16[12,2176]{1,0:T(8,128)(2,1)S(1)}, bf16[12,2176]{1,0:T(8,128)(2,1)S(1)}, u32[]{:S(2)}, u32[]{:S(2)}) collective-permute-start(bf16[12,2176]{1,0:T(8,128)(2,1)S(1)} %pad_maximum_fusion.1), channel_id=1, source_target_pairs={{0,16},{16,0},{1,17},{17,1},{2,18},{18,2},{3,19},{19,3},{4,20},{20... | collective-permute-start | bytes 156680 | tf_op jit(solution)/shard_map/ppermute | solution.py:259
  36.0 16.4 %collective-permute-start.4 = (bf16[24,2176]{1,0:T(8,128)(2,1)S(1)}, bf16[24,2176]{1,0:T(8,128)(2,1)S(1)}, u32[]{:S(2)}, u32[]{:S(2)}) collective-permute-start(bf16[24,2176]{1,0:T(8,128)(2,1)S(1)} %maximum_select_fusion.1), channel_id=1, source_target_pairs={{0,1},{1,0},{2,3},{3,2},{4,5},{5,4},{6,7},{7,6},{8,9},{9,8},{10,11... | collective-permute-start | bytes 313352 | tf_op jit(solution)/shard_map/ppermute | solution.py:40
  52.5 48.0 %copy-start.6 = (bf16[2,24,2176]{2,1,0:T(8,128)(2,1)}, bf16[2,24,2176]{2,1,0:T(8,128)(2,1)S(1)}, u32[]{:S(2)}) copy-start(bf16[2,24,2176]{2,1,0:T(8,128)(2,1)S(1)} %maximum_select_fusion) | copy-start | bytes 626692
  52.5 17.7 %collective-permute-start.5 = (bf16[48,2176]{1,0:T(8,128)(2,1)S(1)}, bf16[48,2176]{1,0:T(8,128)(2,1)S(1)}, u32[]{:S(2)}, u32[]{:S(2)}) collective-permute-start(bf16[48,2176]{1,0:T(8,128)(2,1)S(1)} %bitcast.41), channel_id=1, source_target_pairs={{0,2},{2,4},{4,6},{6,8},{8,10},{10,12},{12,14},{14,0},{1,3},{3,5},... | collective-permute-start | bytes 626696 | tf_op jit(solution)/shard_map/ppermute | solution.py:239
  54.8 45.7 %copy-start.7 = (bf16[576,384]{1,0:T(8,128)(2,1)}, bf16[576,384]{1,0:T(8,128)(2,1)S(1)}, u32[]{:S(2)}) copy-start(bf16[576,384]{1,0:T(8,128)(2,1)S(1)} %constant_dynamic-update-slice_fusion.s0) | copy-start | bytes 1327108
  54.8 26.3 %collective-permute-start.13 = (bf16[576,384]{1,0:T(8,128)(2,1)S(1)}, bf16[576,384]{1,0:T(8,128)(2,1)S(1)}, u32[]{:S(2)}, u32[]{:S(2)}) collective-permute-start(bf16[576,384]{1,0:T(8,128)(2,1)S(1)} %constant_dynamic-update-slice_fusion.s0), channel_id=1, source_target_pairs={{96,0},{0,32},{32,64},{64,96},{97,1},{1,33},{33,65},{65,97},{98,2}... | collective-permute-start | bytes 1327112 | tf_op jit(solution)/shard_map/ppermute | solution.py:244
  58.3 25.1 %collective-permute-start.12 = (bf16[576,384]{1,0:T(8,128)(2,1)S(1)}, bf16[576,384]{1,0:T(8,128)(2,1)S(1)}, u32[]{:S(2)}, u32[]{:S(2)}) collective-permute-start(bf16[576,384]{1,0:T(8,128)(2,1)S(1)} %constant_dynamic-update-slice_fusion.s0), channel_id=1, source_target_pairs={{32,0},{64,32},{96,64},{0,96},{33,1},{65,33},{97,65},{1,97},{34,2}... | collective-permute-start | bytes 1327112 | tf_op jit(solution)/shard_map/ppermute | solution.py:244
  61.4 11.7 %collective-permute-start.6 = (bf16[48,2176]{1,0:T(8,128)(2,1)S(1)}, bf16[48,2176]{1,0:T(8,128)(2,1)S(1)}, u32[]{:S(2)}, u32[]{:S(2)}) collective-permute-start(bf16[48,2176]{1,0:T(8,128)(2,1)S(1)} %bitcast.42), channel_id=1, source_target_pairs={{0,14},{2,0},{4,2},{6,4},{8,6},{10,8},{12,10},{14,12},{1,15},{3,1}... | collective-permute-start | bytes 626696 | tf_op jit(solution)/shard_map/ppermute | solution.py:239
  70.2 30.4 %copy-start.11 = (bf16[48,2176]{1,0:T(8,128)(2,1)}, bf16[48,2176]{1,0:T(8,128)(2,1)S(1)}, u32[]{:S(2)}) copy-start(bf16[48,2176]{1,0:T(8,128)(2,1)S(1)} %collective-permute-done.5.r1) | copy-start | bytes 626692
  70.2 8.4 %collective-permute-start.7 = (bf16[48,2176]{1,0:T(8,128)(2,1)S(1)}, bf16[48,2176]{1,0:T(8,128)(2,1)S(1)}, u32[]{:S(2)}, u32[]{:S(2)}) collective-permute-start(bf16[48,2176]{1,0:T(8,128)(2,1)S(1)} %collective-permute-done.5.r1), channel_id=1, source_target_pairs={{0,2},{2,4},{4,6},{6,8},{8,10},{10,12},{12,14},{14,0},{1,3},{3,5},... | collective-permute-start | bytes 626696 | tf_op jit(solution)/shard_map/ppermute | solution.py:239
  73.1 27.4 %copy-start.12 = (bf16[48,2176]{1,0:T(8,128)(2,1)}, bf16[48,2176]{1,0:T(8,128)(2,1)S(1)}, u32[]{:S(2)}) copy-start(bf16[48,2176]{1,0:T(8,128)(2,1)S(1)} %collective-permute-done.6.l1) | copy-start | bytes 626692
  73.2 14.6 %collective-permute-start.8 = (bf16[48,2176]{1,0:T(8,128)(2,1)S(1)}, bf16[48,2176]{1,0:T(8,128)(2,1)S(1)}, u32[]{:S(2)}, u32[]{:S(2)}) collective-permute-start(bf16[48,2176]{1,0:T(8,128)(2,1)S(1)} %collective-permute-done.6.l1), channel_id=1, source_target_pairs={{0,14},{2,0},{4,2},{6,4},{8,6},{10,8},{12,10},{14,12},{1,15},{3,1}... | collective-permute-start | bytes 626696 | tf_op jit(solution)/shard_map/ppermute | solution.py:239
  78.6 22.0 %copy-start.13 = (bf16[48,2176]{1,0:T(8,128)(2,1)}, bf16[48,2176]{1,0:T(8,128)(2,1)S(1)}, u32[]{:S(2)}) copy-start(bf16[48,2176]{1,0:T(8,128)(2,1)S(1)} %collective-permute-done.7.r2) | copy-start | bytes 626692
  78.6 13.7 %collective-permute-start.9 = (bf16[48,2176]{1,0:T(8,128)(2,1)S(1)}, bf16[48,2176]{1,0:T(8,128)(2,1)S(1)}, u32[]{:S(2)}, u32[]{:S(2)}) collective-permute-start(bf16[48,2176]{1,0:T(8,128)(2,1)S(1)} %collective-permute-done.7.r2), channel_id=1, source_target_pairs={{0,2},{2,4},{4,6},{6,8},{8,10},{10,12},{12,14},{14,0},{1,3},{3,5},... | collective-permute-start | bytes 626696 | tf_op jit(solution)/shard_map/ppermute | solution.py:239
  81.1 19.4 %copy-start.4 = (bf16[576,384]{1,0:T(8,128)(2,1)}, bf16[576,384]{1,0:T(8,128)(2,1)S(1)}, u32[]{:S(2)}) copy-start(bf16[576,384]{1,0:T(8,128)(2,1)S(1)} %collective-permute-done.13.s3) | copy-start | bytes 1327108
  81.2 13.2 %collective-permute-start.14 = (bf16[288,384]{1,0:T(8,128)(2,1)S(1)}, bf16[288,384]{1,0:T(8,128)(2,1)S(1)}, u32[]{:S(2)}, u32[]{:S(2)}) collective-permute-start(bf16[288,384]{1,0:T(8,128)(2,1)S(1)} %slice.76), channel_id=1, source_target_pairs={{96,0},{0,32},{32,64},{64,96},{97,1},{1,33},{33,65},{65,97},{98,2}... | collective-permute-start | bytes 663560 | tf_op jit(solution)/shard_map/ppermute | solution.py:244
  83.4 17.2 %copy-start.5 = (bf16[576,384]{1,0:T(8,128)(2,1)}, bf16[576,384]{1,0:T(8,128)(2,1)S(1)}, u32[]{:S(2)}) copy-start(bf16[576,384]{1,0:T(8,128)(2,1)S(1)} %collective-permute-done.12.s1) | copy-start | bytes 1327108
  83.4 11.0 %collective-permute-start.15 = (bf16[288,384]{1,0:T(8,128)(2,1)S(1)}, bf16[288,384]{1,0:T(8,128)(2,1)S(1)}, u32[]{:S(2)}, u32[]{:S(2)}) collective-permute-start(bf16[288,384]{1,0:T(8,128)(2,1)S(1)} %slice.77), channel_id=1, source_target_pairs={{32,0},{64,32},{96,64},{0,96},{33,1},{65,33},{97,65},{1,97},{34,2}... | collective-permute-start | bytes 663560 | tf_op jit(solution)/shard_map/ppermute | solution.py:244
  87.7 12.8 %copy-start.14 = (bf16[48,2176]{1,0:T(8,128)(2,1)}, bf16[48,2176]{1,0:T(8,128)(2,1)S(1)}, u32[]{:S(2)}) copy-start(bf16[48,2176]{1,0:T(8,128)(2,1)S(1)} %collective-permute-done.8.l2) | copy-start | bytes 626692
  87.8 7.3 %collective-permute-start.10 = (bf16[48,2176]{1,0:T(8,128)(2,1)S(1)}, bf16[48,2176]{1,0:T(8,128)(2,1)S(1)}, u32[]{:S(2)}, u32[]{:S(2)}) collective-permute-start(bf16[48,2176]{1,0:T(8,128)(2,1)S(1)} %collective-permute-done.8.l2), channel_id=1, source_target_pairs={{0,14},{2,0},{4,2},{6,4},{8,6},{10,8},{12,10},{14,12},{1,15},{3,1}... | collective-permute-start | bytes 626696 | tf_op jit(solution)/shard_map/ppermute | solution.py:239
  92.4 8.2 %collective-permute-start.11 = (bf16[48,2176]{1,0:T(8,128)(2,1)S(1)}, bf16[48,2176]{1,0:T(8,128)(2,1)S(1)}, u32[]{:S(2)}, u32[]{:S(2)}) collective-permute-start(bf16[48,2176]{1,0:T(8,128)(2,1)S(1)} %collective-permute-done.9.r3), channel_id=1, source_target_pairs={{0,2},{2,4},{4,6},{6,8},{8,10},{10,12},{12,14},{14,0},{1,3},{3,5},... | collective-permute-start | bytes 626696 | tf_op jit(solution)/shard_map/ppermute | solution.py:239
  108.3 7.8 %collective-permute-start.16 = (f32[192,512]{1,0:T(8,128)}, f32[192,512]{1,0:T(8,128)S(1)}, u32[]{:S(2)}, u32[]{:S(2)}) collective-permute-start(f32[192,512]{1,0:T(8,128)} %get-tuple-element.34), channel_id=1, source_target_pairs={{0,16},{16,0},{1,17},{17,1},{2,18},{18,2},{3,19},{19,3},{4,20},{20... | collective-permute-start | bytes 1179656 | tf_op jit(solution)/shard_map/ppermute | solution.py:295
  117.2 11.8 %copy-start.2 = (s32[4]{0:T(128)S(1)}, s32[4]{0:T(128)}, u32[]{:S(2)}) copy-start(s32[4]{0:T(128)} %pad_add_fusion.place) | copy-start | bytes 52
  124.2 4.8 %collective-permute-start.17 = (f32[192,1408]{1,0:T(8,128)}, f32[192,1408]{1,0:T(8,128)S(1)}, u32[]{:S(2)}, u32[]{:S(2)}) collective-permute-start(f32[192,1408]{1,0:T(8,128)} %get-tuple-element.38), channel_id=1, source_target_pairs={{0,16},{16,0},{1,17},{17,1},{2,18},{18,2},{3,19},{19,3},{4,20},{20... | collective-permute-start | bytes 3244040 | tf_op jit(solution)/shard_map/ppermute | solution.py:314
  130.2 22.0 %copy-start = (bf16[384,2176]{1,0:T(8,128)(2,1)S(1)}, bf16[384,2176]{1,0:T(8,128)(2,1)}, u32[]{:S(2)}) copy-start(bf16[384,2176]{1,0:T(8,128)(2,1)} %get-tuple-element.32.tok.tok_in) | copy-start | bytes 5013508
  173.5 10.8 %all-to-all-start.2 = ((f32[16,2,128]{2,1,0:T(2,128)}), f32[16,2,128]{2,1,0:T(2,128)S(1)}, u32[]{:S(2)}, u32[]{:S(2)}) async-start(f32[16,2,128]{2,1,0:T(2,128)} %broadcast_in_dim.10), calls=%async_computation.2 | async-start | bytes 32768 | tf_op jit(solution)/shard_map/all_to_all | solution.py:339
  (11 other events, 48.0 us)
Sparse Core Ops, SparseCore 0:
  11.0 103.0 all-gather.1

commit v17 on v16

--- a/solution.py
+++ b/solution.py
@@ -26,7 +26,7 @@
 HALF = WIDTH // 2
 LANES = 128
 UNITS = 896
-GATE, UP = 768, 640
+GATE, UP = 640, 640
 MAIN = GATE + UP
 SIDE = 2 * UNITS - MAIN
 PIECE = SLICE + 16
@@ -162,12 +162,11 @@
     copies[2].start()
     copies[3].start()
     mixed_up = dot(b_up[RANK : 2 * RANK, :], high, CONTRACT_LAST) + dot(b_up[RANK : 2 * RANK, :], rest, CONTRACT_LAST)
-    message[...] = jnp.zeros_like(message)
     for core in range(2):
         lines = slice(RANK * core, RANK * (core + 1))
         for i, value in enumerate((mixed, mixed_up)):
-            message[lines, 0, 2 * i * LANES : 2 * i * LANES + GROUP] = value
-        message[lines, 0, 4 * LANES :] = tail
+            message[lines, 0, i * GROUP : (i + 1) * GROUP] = value
+        message[lines, 0, 2 * GROUP :] = tail
     low_t[...] = low_b.astype(F32).T[0 : 2 * RANK, :]
     for copy in copies:
         copy.wait()
@@ -180,7 +179,7 @@
     k_copy.start()
     core = place[0]
     sums = [jnp.sum(arrived[RANK * h : RANK * (h + 1)], axis=0) for h in range(2)]
-    tails = [total[:, 4 * LANES :] for total in sums]
+    tails = [total[:, 2 * GROUP :] for total in sums]
     line = lax.broadcasted_iota(jnp.int32, (8, GROUP), 0)
     pair_total = jnp.maximum(tails[0][:, 64:65] + tails[1][:, 64:65], 1.0)
     logs, cotangents, terms = 0.0, [], []
@@ -193,7 +192,7 @@
         scaled = jnp.broadcast_to(scaled, (8, LANES))
         cotangent = sum(dot(part, signs[h]) for part in split(scaled, 3))
         cotangents.append(cotangent[0:1, :])
-        gate, up = (sums[h][:, i * LANES : i * LANES + GROUP] for i in (0, 2))
+        gate, up = (sums[h][:, i * GROUP : (i + 1) * GROUP] for i in range(2))
         projected = jnp.where(line == 0, gate, jnp.where(line == 1, up, 0.0)) * cotangent
         if h == 0:
             tok_copy.wait()
@@ -314,7 +313,7 @@
     partner = lax.ppermute(far, "c", SWAP)
     message, low_t, k = kernel(
         score,
-        [((2 * RANK, 1, 5 * LANES), F32), ((2 * RANK, GROUP), F32), ((4, GROUP, UNITS), BF16)],
+        [((2 * RANK, 1, 2 * GROUP + LANES), F32), ((2 * RANK, GROUP), F32), ((4, GROUP, UNITS), BF16)],
         (place, near, partner, side, b_gate, b_up, read, signs, count_lanes),
         8 * GROUP * UNITS * LANES, 16,
         scratch=[pltpu.VMEM((4, GROUP, UNITS), BF16), pltpu.SemaphoreType.DMA((4,))],

time: 194 us -> 190 us (0.979)
  waiting for transfers between devices: 22.3 us -> 16.7 us
  starting transfers between devices: 79.1 us -> 83.9 us
  local copies, waits for them, and re-layouts: 11.4 us -> 9.32 us
    ppermute x1, waiting for transfers between devices: 6.96 us -> 0.01 us  [swapped(): far = lax.ppermute(value, axis, SWAP)]
    ppermute x1, starting transfers between devices: 9.37 us -> 12.5 us  [swapped(): far = lax.ppermute(value, axis, SWAP)]
where the time goes in v17:
time: 190 us; the launch traced here: 189 us
  starting transfers between devices  83.9 us (44%)
  blocking collectives  35.5 us (19%)
  between operations  19.7 us (10%)
  Pallas kernels  17.7 us (9%)
  waiting for transfers between devices  16.7 us (9%)
  local copies, waits for them, and re-layouts  9.32 us (5%)
  other arithmetic  5.71 us (3%)
    ppermute x7, starting transfers between devices, fetch(): return lax.ppermute(value, axis, [((i + k) % n, i) for i in range(n)])  27.5 us
    ppermute x7, starting transfers between devices, along(): return lax.ppermute(value, axis, [(i, (i + k) % n) for i in range(n)])  27 us
    all_to_all x1, blocking collectives, on_device(): lax.all_to_all(outgoing, DP, split_axis=0, concat_axis=0)  18.1 us
    pallas_call x4, Pallas kernels, kernel(): pl.pallas_call(function, out_shape=tuple((jax.ShapeDtypeStruct(*s) for s...  17.7 us
    all_to_all x1, blocking collectives, on_device(): lax.all_to_all(message, ('c', 'z', 'yl'), split_axis=0, concat_axis=0)  17.3 us
    ppermute x1, starting transfers between devices, swapped(): far = lax.ppermute(value, axis, SWAP)  12.5 us
    ppermute x7, waiting for transfers between devices, along(): return lax.ppermute(value, axis, [(i, (i + k) % n) for i in range(n)])  8.51 us
    ppermute x1, starting transfers between devices, on_device(): side = side + lax.ppermute(side_far, 'c', SWAP)  7.59 us
  transfers between devices with their start and end apart: 20, of which 7 were waited for; matrix products, arithmetic and copies ran while one was open for 5% of the time, Pallas kernels for 3%

profile of v17, /device:TPU:1, one launch (start us, length us, event | category | flops | bytes accessed | tf_op | source)
XLA Modules:
  0.0 188.6 jit_solution(3018145955612070673)
XLA Ops:
  9.1 1.3 fusion.12
  13.8 6.7 %collective-permute-start.1 = (bf16[144,512]{1,0:T(8,128)(2,1)S(1)}, bf16[144,512]{1,0:T(8,128)(2,1)S(1)}, u32[]{:S(2)}, u32[]{:S(2)}) collective-permute-start(bf16[144,512]{1,0:T(8,128)(2,1)S(1)} %fusion.6), channel_id=1, source_target_pairs={{128,0},{256,128},{384,256},{0,384},{129,1},{257,129},{385,257},{1... | collective-permute-start | bytes 442376 | tf_op jit(solution)/shard_map/ppermute | solution.py:243
  20.6 3.5 %collective-permute-start.2 = (bf16[144,512]{1,0:T(8,128)(2,1)S(1)}, bf16[144,512]{1,0:T(8,128)(2,1)S(1)}, u32[]{:S(2)}, u32[]{:S(2)}) collective-permute-start(bf16[144,512]{1,0:T(8,128)(2,1)S(1)} %fusion.6), channel_id=1, source_target_pairs={{256,0},{384,128},{0,256},{128,384},{257,1},{385,129},{1,257},{129... | collective-permute-start | bytes 442376 | tf_op jit(solution)/shard_map/ppermute | solution.py:243
  24.1 4.2 %collective-permute-start.3 = (bf16[144,512]{1,0:T(8,128)(2,1)S(1)}, bf16[144,512]{1,0:T(8,128)(2,1)S(1)}, u32[]{:S(2)}, u32[]{:S(2)}) collective-permute-start(bf16[144,512]{1,0:T(8,128)(2,1)S(1)} %fusion.6), channel_id=1, source_target_pairs={{384,0},{0,128},{128,256},{256,384},{385,1},{1,129},{129,257},{257... | collective-permute-start | bytes 442376 | tf_op jit(solution)/shard_map/ppermute | solution.py:243
  28.6 3.4 %collective-permute-start = (bf16[12,2176]{1,0:T(8,128)(2,1)S(1)}, bf16[12,2176]{1,0:T(8,128)(2,1)S(1)}, u32[]{:S(2)}, u32[]{:S(2)}) collective-permute-start(bf16[12,2176]{1,0:T(8,128)(2,1)S(1)} %pad_maximum_fusion.1), channel_id=1, source_target_pairs={{0,16},{16,0},{1,17},{17,1},{2,18},{18,2},{3,19},{19,3},{4,20},{20... | collective-permute-start | bytes 156680 | tf_op jit(solution)/shard_map/ppermute | solution.py:258
  34.4 12.5 %collective-permute-start.4 = (bf16[24,2176]{1,0:T(8,128)(2,1)S(1)}, bf16[24,2176]{1,0:T(8,128)(2,1)S(1)}, u32[]{:S(2)}, u32[]{:S(2)}) collective-permute-start(bf16[24,2176]{1,0:T(8,128)(2,1)S(1)} %maximum_select_fusion.1), channel_id=1, source_target_pairs={{0,1},{1,0},{2,3},{3,2},{4,5},{5,4},{6,7},{7,6},{8,9},{9,8},{10,11... | collective-permute-start | bytes 313352 | tf_op jit(solution)/shard_map/ppermute | solution.py:40
  47.1 2.0 %collective-permute-start.13 = (bf16[576,512]{1,0:T(8,128)(2,1)S(1)}, bf16[576,512]{1,0:T(8,128)(2,1)S(1)}, u32[]{:S(2)}, u32[]{:S(2)}) collective-permute-start(bf16[576,512]{1,0:T(8,128)(2,1)S(1)} %constant_dynamic-update-slice_fusion.s0), channel_id=1, source_target_pairs={{96,0},{0,32},{32,64},{64,96},{97,1},{1,33},{33,65},{65,97},{98,2}... | collective-permute-start | bytes 1769480 | tf_op jit(solution)/shard_map/ppermute | solution.py:243
  49.1 4.5 %collective-permute-start.12 = (bf16[576,512]{1,0:T(8,128)(2,1)S(1)}, bf16[576,512]{1,0:T(8,128)(2,1)S(1)}, u32[]{:S(2)}, u32[]{:S(2)}) collective-permute-start(bf16[576,512]{1,0:T(8,128)(2,1)S(1)} %constant_dynamic-update-slice_fusion.s0), channel_id=1, source_target_pairs={{32,0},{64,32},{96,64},{0,96},{33,1},{65,33},{97,65},{1,97},{34,2}... | collective-permute-start | bytes 1769480 | tf_op jit(solution)/shard_map/ppermute | solution.py:243
  53.7 2.6 %collective-permute-start.5 = (bf16[48,2176]{1,0:T(8,128)(2,1)S(1)}, bf16[48,2176]{1,0:T(8,128)(2,1)S(1)}, u32[]{:S(2)}, u32[]{:S(2)}) collective-permute-start(bf16[48,2176]{1,0:T(8,128)(2,1)S(1)} %bitcast.41), channel_id=1, source_target_pairs={{0,2},{2,4},{4,6},{6,8},{8,10},{10,12},{12,14},{14,0},{1,3},{3,5},... | collective-permute-start | bytes 626696 | tf_op jit(solution)/shard_map/ppermute | solution.py:238
  56.4 9.1 %collective-permute-start.6 = (bf16[48,2176]{1,0:T(8,128)(2,1)S(1)}, bf16[48,2176]{1,0:T(8,128)(2,1)S(1)}, u32[]{:S(2)}, u32[]{:S(2)}) collective-permute-start(bf16[48,2176]{1,0:T(8,128)(2,1)S(1)} %bitcast.42), channel_id=1, source_target_pairs={{0,14},{2,0},{4,2},{6,4},{8,6},{10,8},{12,10},{14,12},{1,15},{3,1}... | collective-permute-start | bytes 626696 | tf_op jit(solution)/shard_map/ppermute | solution.py:238
  66.7 1.9 %collective-permute-start.7 = (bf16[48,2176]{1,0:T(8,128)(2,1)S(1)}, bf16[48,2176]{1,0:T(8,128)(2,1)S(1)}, u32[]{:S(2)}, u32[]{:S(2)}) collective-permute-start(bf16[48,2176]{1,0:T(8,128)(2,1)S(1)} %collective-permute-done.5.r1), channel_id=1, source_target_pairs={{0,2},{2,4},{4,6},{6,8},{8,10},{10,12},{12,14},{14,0},{1,3},{3,5},... | collective-permute-start | bytes 626696 | tf_op jit(solution)/shard_map/ppermute | solution.py:238
  68.7 4.9 %collective-permute-start.8 = (bf16[48,2176]{1,0:T(8,128)(2,1)S(1)}, bf16[48,2176]{1,0:T(8,128)(2,1)S(1)}, u32[]{:S(2)}, u32[]{:S(2)}) collective-permute-start(bf16[48,2176]{1,0:T(8,128)(2,1)S(1)} %collective-permute-done.6.l1), channel_id=1, source_target_pairs={{0,14},{2,0},{4,2},{6,4},{8,6},{10,8},{12,10},{14,12},{1,15},{3,1}... | collective-permute-start | bytes 626696 | tf_op jit(solution)/shard_map/ppermute | solution.py:238
  73.6 1.2 collective-permute-done.7.r2
  74.9 1.9 %collective-permute-start.9 = (bf16[48,2176]{1,0:T(8,128)(2,1)S(1)}, bf16[48,2176]{1,0:T(8,128)(2,1)S(1)}, u32[]{:S(2)}, u32[]{:S(2)}) collective-permute-start(bf16[48,2176]{1,0:T(8,128)(2,1)S(1)} %collective-permute-done.7.r2), channel_id=1, source_target_pairs={{0,2},{2,4},{4,6},{6,8},{8,10},{10,12},{12,14},{14,0},{1,3},{3,5},... | collective-permute-start | bytes 626696 | tf_op jit(solution)/shard_map/ppermute | solution.py:238
  76.8 2.5 %collective-permute-start.14 = (bf16[288,512]{1,0:T(8,128)(2,1)S(1)}, bf16[288,512]{1,0:T(8,128)(2,1)S(1)}, u32[]{:S(2)}, u32[]{:S(2)}) collective-permute-start(bf16[288,512]{1,0:T(8,128)(2,1)S(1)} %slice.76), channel_id=1, source_target_pairs={{96,0},{0,32},{32,64},{64,96},{97,1},{1,33},{33,65},{65,97},{98,2}... | collective-permute-start | bytes 884744 | tf_op jit(solution)/shard_map/ppermute | solution.py:243
  79.4 3.9 %collective-permute-start.15 = (bf16[288,512]{1,0:T(8,128)(2,1)S(1)}, bf16[288,512]{1,0:T(8,128)(2,1)S(1)}, u32[]{:S(2)}, u32[]{:S(2)}) collective-permute-start(bf16[288,512]{1,0:T(8,128)(2,1)S(1)} %slice.77), channel_id=1, source_target_pairs={{32,0},{64,32},{96,64},{0,96},{33,1},{65,33},{97,65},{1,97},{34,2}... | collective-permute-start | bytes 884744 | tf_op jit(solution)/shard_map/ppermute | solution.py:243
  84.1 4.6 %collective-permute-start.10 = (bf16[48,2176]{1,0:T(8,128)(2,1)S(1)}, bf16[48,2176]{1,0:T(8,128)(2,1)S(1)}, u32[]{:S(2)}, u32[]{:S(2)}) collective-permute-start(bf16[48,2176]{1,0:T(8,128)(2,1)S(1)} %collective-permute-done.8.l2), channel_id=1, source_target_pairs={{0,14},{2,0},{4,2},{6,4},{8,6},{10,8},{12,10},{14,12},{1,15},{3,1}... | collective-permute-start | bytes 626696 | tf_op jit(solution)/shard_map/ppermute | solution.py:238
  88.7 1.9 %collective-permute-start.11 = (bf16[48,2176]{1,0:T(8,128)(2,1)S(1)}, bf16[48,2176]{1,0:T(8,128)(2,1)S(1)}, u32[]{:S(2)}, u32[]{:S(2)}) collective-permute-start(bf16[48,2176]{1,0:T(8,128)(2,1)S(1)} %collective-permute-done.9.r3), channel_id=1, source_target_pairs={{0,2},{2,4},{4,6},{6,8},{8,10},{10,12},{12,14},{14,0},{1,3},{3,5},... | collective-permute-start | bytes 626696 | tf_op jit(solution)/shard_map/ppermute | solution.py:238
  91.4 5.4 %collective-permute-done.11.far_z = bf16[48,2176]{1,0:T(8,128)(2,1)S(1)} collective-permute-done((bf16[48,2176]{1,0:T(8,128)(2,1)S(1)}, bf16[48,2176]{1,0:T(8,128)(2,1)S(1)}, u32[]{:S(2)}, u32[]{:S(2)}) %collective-permute-start.11) | collective-permute-done | bytes 208928 | tf_op jit(solution)/shard_map/ppermute | solution.py:238
  97.6 5.6 %shard_map.94 = (f32[192,640]{1,0:T(8,128)}, f32[192,640]{1,0:T(8,128)}, f32[1,128]{1,0:T(1,128)}, bf16[384,2176]{1,0:T(8,128)(2,1)}) custom-call(s32[4]{0:T(128)} %pad_add_fusion.place, bf16[2048,128]{1,0:T(8,128)(2,1)} %pad.17.down, bf16[48,2176]{1,0:T(8,128)(2,1)} %bitcast.43, bf16[48,2176]{1,0:T(8,128)(2,1)} %copy-done.11, bf16[48,2176]{1,0:T(8,128)(2,1)} %copy-done.12, ...), custom_call_target="tpu_custom_call" | custom-call | flops 1006632960 | bytes 10000000 | tf_op jit(solution)/shard_map/pallas_call | solution.py:225
  104.4 7.6 %collective-permute-start.16 = (f32[192,640]{1,0:T(8,128)}, f32[192,640]{1,0:T(8,128)S(1)}, u32[]{:S(2)}, u32[]{:S(2)}) collective-permute-start(f32[192,640]{1,0:T(8,128)} %get-tuple-element.34), channel_id=1, source_target_pairs={{0,16},{16,0},{1,17},{17,1},{2,18},{18,2},{3,19},{19,3},{4,20},{20... | collective-permute-start | bytes 1474568 | tf_op jit(solution)/shard_map/ppermute | solution.py:294
  112.4 1.3 collective-permute-done.16
  114.8 6.1 %shard_map.95 = (f32[192,1280]{1,0:T(8,128)}, f32[192,1280]{1,0:T(8,128)}) custom-call(s32[4]{0:T(128)} %pad_add_fusion.place, bf16[384,2176]{1,0:T(8,128)(2,1)} %get-tuple-element.32.tok.tok_in, bf16[2048,1280]{1,0:T(8,128)(2,1)} %all-gather.2.cloned.1.call-done.w_in), custom_call_target="tpu_custom_call" | custom-call | flops 2013265920 | bytes 10000000 | tf_op jit(solution)/shard_map/pallas_call | solution.py:225
  120.9 2.4 %collective-permute-start.17 = (f32[192,1280]{1,0:T(8,128)}, f32[192,1280]{1,0:T(8,128)S(1)}, u32[]{:S(2)}, u32[]{:S(2)}) collective-permute-start(f32[192,1280]{1,0:T(8,128)} %get-tuple-element.38), channel_id=1, source_target_pairs={{0,16},{16,0},{1,17},{17,1},{2,18},{18,2},{3,19},{19,3},{4,20},{20... | collective-permute-start | bytes 2949128 | tf_op jit(solution)/shard_map/ppermute | solution.py:313
  123.3 2.4 %collective-permute-done.17.partner = f32[192,1280]{1,0:T(8,128)S(1)} collective-permute-done((f32[192,1280]{1,0:T(8,128)}, f32[192,1280]{1,0:T(8,128)S(1)}, u32[]{:S(2)}, u32[]{:S(2)}) %collective-permute-start.17) | collective-permute-done | bytes 983072 | tf_op jit(solution)/shard_map/ppermute | solution.py:313
  125.7 1.2 copy-done.1
  126.9 3.9 %shard_map.96 = (f32[32,1,512]{2,1,0:T(1,128)S(1)}, f32[32,192]{1,0:T(8,128)S(1)}, bf16[4,192,896]{2,1,0:T(8,128)(2,1)S(1)}) custom-call(s32[4]{0:T(128)S(1)} %copy-done.2, f32[192,1280]{1,0:T(8,128)S(1)} %copy-done.1, f32[192,1280]{1,0:T(8,128)S(1)} %collective-permute-done.17.partner, f32[192,640]{1,0:T(8,128)S(1)} %add.54.side, ...), custom_call_target="tpu_custom_call" | custom-call | flops 176160768 | bytes 10000000 | tf_op jit(solution)/shard_map/pallas_call | solution.py:225
  130.8 17.3 %all_to_all.15.arrived = f32[32,1,512]{2,1,0:T(1,128)S(1)} all-to-all(f32[32,1,512]{2,1,0:T(1,128)S(1)} %get-tuple-element.45), channel_id=1, replica_groups=mesh['yh'=4,'x'=4,'c'=2,'z'=8,'yl'=2] {'c','z','yl'}, dimensions={0} | all-to-all | bytes 131072 | tf_op jit(solution)/shard_map/all_to_all | solution.py:322
  148.1 2.1 %shard_map.97 = (f32[32,1,1280]{2,1,0:T(1,128)S(1)}, f32[8,128]{1,0:T(8,128)S(1)}) custom-call(s32[4]{0:T(128)S(1)} %copy-done.2, f32[32,1,512]{2,1,0:T(1,128)S(1)} %all_to_all.15.arrived, bf16[2,128,192]{2,1,0:T(8,128)(2,1)S(1)} %fusion.7.signs, f32[2,1,128]{2,1,0:T(1,128)S(1)} %bitcast.39, f32[32,192]{1,0:T(8,128)S(1)} %get-tuple-element.47.low_t, ...), custom_call_target="tpu_custom_call" | custom-call | flops 12582912 | bytes 10000000 | tf_op jit(solution)/shard_map/pallas_call | solution.py:225
  150.3 18.1 %all_to_all.16 = f32[32,1,1280]{2,1,0:T(1,128)S(1)} all-to-all(f32[32,1,1280]{2,1,0:T(1,128)S(1)} %get-tuple-element.49), channel_id=1, replica_groups=mesh['yh'=4,'x'=4,'c'=2,'z'=8,'yl'=2] {'yh','x','c'}, dimensions={0} | all-to-all | bytes 327680 | tf_op jit(solution)/shard_map/all_to_all | solution.py:336
  169.1 3.5 %all-to-all-start.2 = ((f32[16,2,128]{2,1,0:T(2,128)}), f32[16,2,128]{2,1,0:T(2,128)S(1)}, u32[]{:S(2)}, u32[]{:S(2)}) async-start(f32[16,2,128]{2,1,0:T(2,128)} %broadcast_in_dim.10), calls=%async_computation.2 | async-start | bytes 32768 | tf_op jit(solution)/shard_map/all_to_all | solution.py:338
  175.5 4.5 %all-to-all-done.2 = f32[16,2,128]{2,1,0:T(2,128)S(1)} async-done(((f32[16,2,128]{2,1,0:T(2,128)}), f32[16,2,128]{2,1,0:T(2,128)S(1)}, u32[]{:S(2)}, u32[]{:S(2)}) %all-to-all-start.2) | async-done | bytes 16416 | tf_op jit(solution)/shard_map/all_to_all | solution.py:338
  (110 shorter events, 14.5 us)
Async XLA Ops:
  7.2 21.2 %copy-start.18 = (bf16[12,4096]{1,0:T(8,128)(2,1)S(1)}, bf16[12,4096]{1,0:T(8,128)(2,1)}, u32[]{:S(2)}) copy-start(bf16[12,4096]{1,0:T(8,128)(2,1)} %param.7) | copy-start | bytes 294916
  7.2 24.9 %copy-start.10 = (bf16[4096,32]{0,1:T(8,128)(2,1)S(1)}, bf16[4096,32]{0,1:T(8,128)(2,1)}, u32[]{:S(2)}) copy-start(bf16[4096,32]{0,1:T(8,128)(2,1)} %param.11) | copy-start | bytes 786436
  7.2 107.6 %all-gather.2.cloned.1.call-start = ((), (), s32[]{:S(2)}) async-start(), calls=%async_computation.3 | async-start | bytes 5570560 | tf_op jit(solution)/shard_map/all_gather | solution.py:252
  13.8 20.6 %collective-permute-start.1 = (bf16[144,512]{1,0:T(8,128)(2,1)S(1)}, bf16[144,512]{1,0:T(8,128)(2,1)S(1)}, u32[]{:S(2)}, u32[]{:S(2)}) collective-permute-start(bf16[144,512]{1,0:T(8,128)(2,1)S(1)} %fusion.6), channel_id=1, source_target_pairs={{128,0},{256,128},{384,256},{0,384},{129,1},{257,129},{385,257},{1... | collective-permute-start | bytes 442376 | tf_op jit(solution)/shard_map/ppermute | solution.py:243
  20.6 13.9 %collective-permute-start.2 = (bf16[144,512]{1,0:T(8,128)(2,1)S(1)}, bf16[144,512]{1,0:T(8,128)(2,1)S(1)}, u32[]{:S(2)}, u32[]{:S(2)}) collective-permute-start(bf16[144,512]{1,0:T(8,128)(2,1)S(1)} %fusion.6), channel_id=1, source_target_pairs={{256,0},{384,128},{0,256},{128,384},{257,1},{385,129},{1,257},{129... | collective-permute-start | bytes 442376 | tf_op jit(solution)/shard_map/ppermute | solution.py:243
  24.1 10.3 %collective-permute-start.3 = (bf16[144,512]{1,0:T(8,128)(2,1)S(1)}, bf16[144,512]{1,0:T(8,128)(2,1)S(1)}, u32[]{:S(2)}, u32[]{:S(2)}) collective-permute-start(bf16[144,512]{1,0:T(8,128)(2,1)S(1)} %fusion.6), channel_id=1, source_target_pairs={{384,0},{0,128},{128,256},{256,384},{385,1},{1,129},{129,257},{257... | collective-permute-start | bytes 442376 | tf_op jit(solution)/shard_map/ppermute | solution.py:243
  28.6 5.7 %collective-permute-start = (bf16[12,2176]{1,0:T(8,128)(2,1)S(1)}, bf16[12,2176]{1,0:T(8,128)(2,1)S(1)}, u32[]{:S(2)}, u32[]{:S(2)}) collective-permute-start(bf16[12,2176]{1,0:T(8,128)(2,1)S(1)} %pad_maximum_fusion.1), channel_id=1, source_target_pairs={{0,16},{16,0},{1,17},{17,1},{2,18},{18,2},{3,19},{19,3},{4,20},{20... | collective-permute-start | bytes 156680 | tf_op jit(solution)/shard_map/ppermute | solution.py:258
  33.4 23.0 %copy-start.19 = (bf16[32,896]{1,0:T(8,128)(2,1)S(1)}, bf16[32,896]{1,0:T(8,128)(2,1)}, u32[]{:S(2)}) copy-start(bf16[32,896]{1,0:T(8,128)(2,1)} %param.12) | copy-start | bytes 172036
  33.4 23.0 %copy-start.20 = (bf16[896]{0:T(1024)(128)(2,1)S(1)}, bf16[896]{0:T(1024)(128)(2,1)}, u32[]{:S(2)}) copy-start(bf16[896]{0:T(1024)(128)(2,1)} %param.13) | copy-start | bytes 5380
  34.4 19.1 %collective-permute-start.4 = (bf16[24,2176]{1,0:T(8,128)(2,1)S(1)}, bf16[24,2176]{1,0:T(8,128)(2,1)S(1)}, u32[]{:S(2)}, u32[]{:S(2)}) collective-permute-start(bf16[24,2176]{1,0:T(8,128)(2,1)S(1)} %maximum_select_fusion.1), channel_id=1, source_target_pairs={{0,1},{1,0},{2,3},{3,2},{4,5},{5,4},{6,7},{7,6},{8,9},{9,8},{10,11... | collective-permute-start | bytes 313352 | tf_op jit(solution)/shard_map/ppermute | solution.py:40
  47.1 49.8 %copy-start.6 = (bf16[576,512]{1,0:T(8,128)(2,1)}, bf16[576,512]{1,0:T(8,128)(2,1)S(1)}, u32[]{:S(2)}) copy-start(bf16[576,512]{1,0:T(8,128)(2,1)S(1)} %constant_dynamic-update-slice_fusion.s0) | copy-start | bytes 1769476
  47.1 29.7 %collective-permute-start.13 = (bf16[576,512]{1,0:T(8,128)(2,1)S(1)}, bf16[576,512]{1,0:T(8,128)(2,1)S(1)}, u32[]{:S(2)}, u32[]{:S(2)}) collective-permute-start(bf16[576,512]{1,0:T(8,128)(2,1)S(1)} %constant_dynamic-update-slice_fusion.s0), channel_id=1, source_target_pairs={{96,0},{0,32},{32,64},{64,96},{97,1},{1,33},{33,65},{65,97},{98,2}... | collective-permute-start | bytes 1769480 | tf_op jit(solution)/shard_map/ppermute | solution.py:243
  49.1 30.3 %collective-permute-start.12 = (bf16[576,512]{1,0:T(8,128)(2,1)S(1)}, bf16[576,512]{1,0:T(8,128)(2,1)S(1)}, u32[]{:S(2)}, u32[]{:S(2)}) collective-permute-start(bf16[576,512]{1,0:T(8,128)(2,1)S(1)} %constant_dynamic-update-slice_fusion.s0), channel_id=1, source_target_pairs={{32,0},{64,32},{96,64},{0,96},{33,1},{65,33},{97,65},{1,97},{34,2}... | collective-permute-start | bytes 1769480 | tf_op jit(solution)/shard_map/ppermute | solution.py:243
  53.7 43.2 %copy-start.7 = (bf16[2,24,2176]{2,1,0:T(8,128)(2,1)}, bf16[2,24,2176]{2,1,0:T(8,128)(2,1)S(1)}, u32[]{:S(2)}) copy-start(bf16[2,24,2176]{2,1,0:T(8,128)(2,1)S(1)} %maximum_select_fusion) | copy-start | bytes 626692
  53.7 13.1 %collective-permute-start.5 = (bf16[48,2176]{1,0:T(8,128)(2,1)S(1)}, bf16[48,2176]{1,0:T(8,128)(2,1)S(1)}, u32[]{:S(2)}, u32[]{:S(2)}) collective-permute-start(bf16[48,2176]{1,0:T(8,128)(2,1)S(1)} %bitcast.41), channel_id=1, source_target_pairs={{0,2},{2,4},{4,6},{6,8},{8,10},{10,12},{12,14},{14,0},{1,3},{3,5},... | collective-permute-start | bytes 626696 | tf_op jit(solution)/shard_map/ppermute | solution.py:238
  56.4 12.2 %collective-permute-start.6 = (bf16[48,2176]{1,0:T(8,128)(2,1)S(1)}, bf16[48,2176]{1,0:T(8,128)(2,1)S(1)}, u32[]{:S(2)}, u32[]{:S(2)}) collective-permute-start(bf16[48,2176]{1,0:T(8,128)(2,1)S(1)} %bitcast.42), channel_id=1, source_target_pairs={{0,14},{2,0},{4,2},{6,4},{8,6},{10,8},{12,10},{14,12},{1,15},{3,1}... | collective-permute-start | bytes 626696 | tf_op jit(solution)/shard_map/ppermute | solution.py:238
  66.7 30.1 %copy-start.11 = (bf16[48,2176]{1,0:T(8,128)(2,1)}, bf16[48,2176]{1,0:T(8,128)(2,1)S(1)}, u32[]{:S(2)}) copy-start(bf16[48,2176]{1,0:T(8,128)(2,1)S(1)} %collective-permute-done.5.r1) | copy-start | bytes 626692
  66.7 8.1 %collective-permute-start.7 = (bf16[48,2176]{1,0:T(8,128)(2,1)S(1)}, bf16[48,2176]{1,0:T(8,128)(2,1)S(1)}, u32[]{:S(2)}, u32[]{:S(2)}) collective-permute-start(bf16[48,2176]{1,0:T(8,128)(2,1)S(1)} %collective-permute-done.5.r1), channel_id=1, source_target_pairs={{0,2},{2,4},{4,6},{6,8},{8,10},{10,12},{12,14},{14,0},{1,3},{3,5},... | collective-permute-start | bytes 626696 | tf_op jit(solution)/shard_map/ppermute | solution.py:238
  68.7 28.2 %copy-start.12 = (bf16[48,2176]{1,0:T(8,128)(2,1)}, bf16[48,2176]{1,0:T(8,128)(2,1)S(1)}, u32[]{:S(2)}) copy-start(bf16[48,2176]{1,0:T(8,128)(2,1)S(1)} %collective-permute-done.6.l1) | copy-start | bytes 626692
  68.7 15.4 %collective-permute-start.8 = (bf16[48,2176]{1,0:T(8,128)(2,1)S(1)}, bf16[48,2176]{1,0:T(8,128)(2,1)S(1)}, u32[]{:S(2)}, u32[]{:S(2)}) collective-permute-start(bf16[48,2176]{1,0:T(8,128)(2,1)S(1)} %collective-permute-done.6.l1), channel_id=1, source_target_pairs={{0,14},{2,0},{4,2},{6,4},{8,6},{10,8},{12,10},{14,12},{1,15},{3,1}... | collective-permute-start | bytes 626696 | tf_op jit(solution)/shard_map/ppermute | solution.py:238
  74.9 22.0 %copy-start.13 = (bf16[48,2176]{1,0:T(8,128)(2,1)}, bf16[48,2176]{1,0:T(8,128)(2,1)S(1)}, u32[]{:S(2)}) copy-start(bf16[48,2176]{1,0:T(8,128)(2,1)S(1)} %collective-permute-done.7.r2) | copy-start | bytes 626692
  74.9 13.8 %collective-permute-start.9 = (bf16[48,2176]{1,0:T(8,128)(2,1)S(1)}, bf16[48,2176]{1,0:T(8,128)(2,1)S(1)}, u32[]{:S(2)}, u32[]{:S(2)}) collective-permute-start(bf16[48,2176]{1,0:T(8,128)(2,1)S(1)} %collective-permute-done.7.r2), channel_id=1, source_target_pairs={{0,2},{2,4},{4,6},{6,8},{8,10},{10,12},{12,14},{14,0},{1,3},{3,5},... | collective-permute-start | bytes 626696 | tf_op jit(solution)/shard_map/ppermute | solution.py:238
  76.8 20.1 %copy-start.4 = (bf16[576,512]{1,0:T(8,128)(2,1)}, bf16[576,512]{1,0:T(8,128)(2,1)S(1)}, u32[]{:S(2)}) copy-start(bf16[576,512]{1,0:T(8,128)(2,1)S(1)} %collective-permute-done.13.s3) | copy-start | bytes 1769476
  76.8 14.5 %collective-permute-start.14 = (bf16[288,512]{1,0:T(8,128)(2,1)S(1)}, bf16[288,512]{1,0:T(8,128)(2,1)S(1)}, u32[]{:S(2)}, u32[]{:S(2)}) collective-permute-start(bf16[288,512]{1,0:T(8,128)(2,1)S(1)} %slice.76), channel_id=1, source_target_pairs={{96,0},{0,32},{32,64},{64,96},{97,1},{1,33},{33,65},{65,97},{98,2}... | collective-permute-start | bytes 884744 | tf_op jit(solution)/shard_map/ppermute | solution.py:243
  79.4 17.5 %copy-start.5 = (bf16[576,512]{1,0:T(8,128)(2,1)}, bf16[576,512]{1,0:T(8,128)(2,1)S(1)}, u32[]{:S(2)}) copy-start(bf16[576,512]{1,0:T(8,128)(2,1)S(1)} %collective-permute-done.12.s1) | copy-start | bytes 1769476
  79.4 11.9 %collective-permute-start.15 = (bf16[288,512]{1,0:T(8,128)(2,1)S(1)}, bf16[288,512]{1,0:T(8,128)(2,1)S(1)}, u32[]{:S(2)}, u32[]{:S(2)}) collective-permute-start(bf16[288,512]{1,0:T(8,128)(2,1)S(1)} %slice.77), channel_id=1, source_target_pairs={{32,0},{64,32},{96,64},{0,96},{33,1},{65,33},{97,65},{1,97},{34,2}... | collective-permute-start | bytes 884744 | tf_op jit(solution)/shard_map/ppermute | solution.py:243
  84.1 7.3 %collective-permute-start.10 = (bf16[48,2176]{1,0:T(8,128)(2,1)S(1)}, bf16[48,2176]{1,0:T(8,128)(2,1)S(1)}, u32[]{:S(2)}, u32[]{:S(2)}) collective-permute-start(bf16[48,2176]{1,0:T(8,128)(2,1)S(1)} %collective-permute-done.8.l2), channel_id=1, source_target_pairs={{0,14},{2,0},{4,2},{6,4},{8,6},{10,8},{12,10},{14,12},{1,15},{3,1}... | collective-permute-start | bytes 626696 | tf_op jit(solution)/shard_map/ppermute | solution.py:238
  88.7 8.2 %collective-permute-start.11 = (bf16[48,2176]{1,0:T(8,128)(2,1)S(1)}, bf16[48,2176]{1,0:T(8,128)(2,1)S(1)}, u32[]{:S(2)}, u32[]{:S(2)}) collective-permute-start(bf16[48,2176]{1,0:T(8,128)(2,1)S(1)} %collective-permute-done.9.r3), channel_id=1, source_target_pairs={{0,2},{2,4},{4,6},{6,8},{8,10},{10,12},{12,14},{14,0},{1,3},{3,5},... | collective-permute-start | bytes 626696 | tf_op jit(solution)/shard_map/ppermute | solution.py:238
  104.4 9.3 %collective-permute-start.16 = (f32[192,640]{1,0:T(8,128)}, f32[192,640]{1,0:T(8,128)S(1)}, u32[]{:S(2)}, u32[]{:S(2)}) collective-permute-start(f32[192,640]{1,0:T(8,128)} %get-tuple-element.34), channel_id=1, source_target_pairs={{0,16},{16,0},{1,17},{17,1},{2,18},{18,2},{3,19},{19,3},{4,20},{20... | collective-permute-start | bytes 1474568 | tf_op jit(solution)/shard_map/ppermute | solution.py:294
  120.9 27.2 %copy-start = (bf16[384,2176]{1,0:T(8,128)(2,1)S(1)}, bf16[384,2176]{1,0:T(8,128)(2,1)}, u32[]{:S(2)}) copy-start(bf16[384,2176]{1,0:T(8,128)(2,1)} %get-tuple-element.32.tok.tok_in) | copy-start | bytes 5013508
  120.9 4.8 %collective-permute-start.17 = (f32[192,1280]{1,0:T(8,128)}, f32[192,1280]{1,0:T(8,128)S(1)}, u32[]{:S(2)}, u32[]{:S(2)}) collective-permute-start(f32[192,1280]{1,0:T(8,128)} %get-tuple-element.38), channel_id=1, source_target_pairs={{0,16},{16,0},{1,17},{17,1},{2,18},{18,2},{3,19},{19,3},{4,20},{20... | collective-permute-start | bytes 2949128 | tf_op jit(solution)/shard_map/ppermute | solution.py:313
  169.1 10.8 %all-to-all-start.2 = ((f32[16,2,128]{2,1,0:T(2,128)}), f32[16,2,128]{2,1,0:T(2,128)S(1)}, u32[]{:S(2)}, u32[]{:S(2)}) async-start(f32[16,2,128]{2,1,0:T(2,128)} %broadcast_in_dim.10), calls=%async_computation.2 | async-start | bytes 32768 | tf_op jit(solution)/shard_map/all_to_all | solution.py:338
  (9 other events, 61.4 us)
Sparse Core Ops, SparseCore 0:
  11.0 98.5 all-gather.1

commit v18 on v17

--- a/solution.py
+++ b/solution.py
@@ -101,17 +101,26 @@
         pltpu.make_async_copy(tok.at[half, pl.ds(0, HALF)], rows.at[n], sems.at[n]) for n, half in enumerate(halves)
     ]
     copies = [
-        pltpu.make_async_copy(w_in.at[chunk, :], w.at[chunk, :], sems.at[2 + n]) for n, chunk in enumerate(chunks)
+        [
+            pltpu.make_async_copy(
+                w_in.at[pl.ds((4 * x + yh) * SLICE, SLICE), :], w.at[pl.ds((4 * yh + x) * SLICE, SLICE), :],
+                sems.at[2 + 4 * yh + x],
+            )
+            for x in range(4)
+        ]
+        for yh in range(4)
     ]
     row_copies[0].start()
-    copies[0].start()
+    for copy in copies[0]:
+        copy.start()
     row_copies[1].start()
-    for copy in copies[1:]:
+    for copy in copies[1] + copies[2] + copies[3]:
         copy.start()
     for copy in row_copies:
         copy.wait()
-    for n, (chunk, copy) in enumerate(zip(chunks, copies)):
-        copy.wait()
+    for n, (chunk, group) in enumerate(zip(chunks, copies)):
+        for copy in group:
+            copy.wait()
         for at, out in enumerate((far, near)):
             term = dot(rows[at, :, chunk], w[chunk, :])
             out[...] = term if n == 0 else out[...] + term
@@ -126,7 +135,7 @@
         scratch=[
             pltpu.VMEM((2, GROUP, HALF), BF16),
             pltpu.VMEM((HALF, MAIN), BF16),
-            pltpu.SemaphoreType.DMA((2 + HALF // COLUMNS,)),
+            pltpu.SemaphoreType.DMA((18,)),
         ],
         in_hbm=2,
     )
@@ -249,7 +258,7 @@
     code = jnp.where(response_mask > 0, sequence_labels, SEQS)
 
     main = jnp.concatenate([frozen[0, :, :GATE], frozen[1, :, :UP]], axis=1)
-    w_main = lax.all_gather(main, ("yh", "x"), axis=0, tiled=True)
+    w_main = lax.all_gather(main, ("x", "yh"), axis=0, tiled=True)
 
     by_core = tokens.reshape(ROWS, 16, 2, SLICE).transpose(2, 0, 1, 3).reshape(2, ROWS, HALF)
     code_lanes = jnp.pad(code.reshape(ROWS, 1).astype(BF16), ((0, 0), (0, LANES - 1)))

time: 190 us -> 190 us (level)
  no operation moved by 1% of the time
where the time goes in v18:
time: 190 us; the launch traced here: 189 us
  starting transfers between devices  83.9 us (44%)
  blocking collectives  35.5 us (19%)
  between operations  19.7 us (10%)
  Pallas kernels  17.8 us (9%)
  waiting for transfers between devices  16.7 us (9%)
  local copies, waits for them, and re-layouts  9.32 us (5%)
  other arithmetic  5.71 us (3%)
    ppermute x7, starting transfers between devices, fetch(): return lax.ppermute(value, axis, [((i + k) % n, i) for i in range(n)])  27.5 us
    ppermute x7, starting transfers between devices, along(): return lax.ppermute(value, axis, [(i, (i + k) % n) for i in range(n)])  27 us
    all_to_all x1, blocking collectives, on_device(): lax.all_to_all(outgoing, DP, split_axis=0, concat_axis=0)  18.1 us
    pallas_call x4, Pallas kernels, kernel(): pl.pallas_call(function, out_shape=tuple((jax.ShapeDtypeStruct(*s) for s...  17.8 us
    all_to_all x1, blocking collectives, on_device(): lax.all_to_all(message, ('c', 'z', 'yl'), split_axis=0, concat_axis=0)  17.3 us
    ppermute x1, starting transfers between devices, swapped(): far = lax.ppermute(value, axis, SWAP)  12.5 us
    ppermute x7, waiting for transfers between devices, along(): return lax.ppermute(value, axis, [(i, (i + k) % n) for i in range(n)])  8.51 us
    ppermute x1, starting transfers between devices, on_device(): side = side + lax.ppermute(side_far, 'c', SWAP)  7.59 us
  transfers between devices with their start and end apart: 20, of which 7 were waited for; matrix products, arithmetic and copies ran while one was open for 5% of the time, Pallas kernels for 3%

profile of v18, /device:TPU:1, one launch (start us, length us, event | category | flops | bytes accessed | tf_op | source)
XLA Modules:
  0.0 188.7 jit_solution(10389888180145717250)
XLA Ops:
  9.1 1.3 fusion.12
  13.8 6.7 %collective-permute-start.1 = (bf16[144,512]{1,0:T(8,128)(2,1)S(1)}, bf16[144,512]{1,0:T(8,128)(2,1)S(1)}, u32[]{:S(2)}, u32[]{:S(2)}) collective-permute-start(bf16[144,512]{1,0:T(8,128)(2,1)S(1)} %fusion.6), channel_id=1, source_target_pairs={{128,0},{256,128},{384,256},{0,384},{129,1},{257,129},{385,257},{1... | collective-permute-start | bytes 442376 | tf_op jit(solution)/shard_map/ppermute | solution.py:252
  20.6 3.5 %collective-permute-start.2 = (bf16[144,512]{1,0:T(8,128)(2,1)S(1)}, bf16[144,512]{1,0:T(8,128)(2,1)S(1)}, u32[]{:S(2)}, u32[]{:S(2)}) collective-permute-start(bf16[144,512]{1,0:T(8,128)(2,1)S(1)} %fusion.6), channel_id=1, source_target_pairs={{256,0},{384,128},{0,256},{128,384},{257,1},{385,129},{1,257},{129... | collective-permute-start | bytes 442376 | tf_op jit(solution)/shard_map/ppermute | solution.py:252
  24.1 4.2 %collective-permute-start.3 = (bf16[144,512]{1,0:T(8,128)(2,1)S(1)}, bf16[144,512]{1,0:T(8,128)(2,1)S(1)}, u32[]{:S(2)}, u32[]{:S(2)}) collective-permute-start(bf16[144,512]{1,0:T(8,128)(2,1)S(1)} %fusion.6), channel_id=1, source_target_pairs={{384,0},{0,128},{128,256},{256,384},{385,1},{1,129},{129,257},{257... | collective-permute-start | bytes 442376 | tf_op jit(solution)/shard_map/ppermute | solution.py:252
  28.6 3.4 %collective-permute-start = (bf16[12,2176]{1,0:T(8,128)(2,1)S(1)}, bf16[12,2176]{1,0:T(8,128)(2,1)S(1)}, u32[]{:S(2)}, u32[]{:S(2)}) collective-permute-start(bf16[12,2176]{1,0:T(8,128)(2,1)S(1)} %pad_maximum_fusion.1), channel_id=1, source_target_pairs={{0,16},{16,0},{1,17},{17,1},{2,18},{18,2},{3,19},{19,3},{4,20},{20... | collective-permute-start | bytes 156680 | tf_op jit(solution)/shard_map/ppermute | solution.py:267
  34.4 12.5 %collective-permute-start.4 = (bf16[24,2176]{1,0:T(8,128)(2,1)S(1)}, bf16[24,2176]{1,0:T(8,128)(2,1)S(1)}, u32[]{:S(2)}, u32[]{:S(2)}) collective-permute-start(bf16[24,2176]{1,0:T(8,128)(2,1)S(1)} %maximum_select_fusion.1), channel_id=1, source_target_pairs={{0,1},{1,0},{2,3},{3,2},{4,5},{5,4},{6,7},{7,6},{8,9},{9,8},{10,11... | collective-permute-start | bytes 313352 | tf_op jit(solution)/shard_map/ppermute | solution.py:40
  47.1 1.9 %collective-permute-start.13 = (bf16[576,512]{1,0:T(8,128)(2,1)S(1)}, bf16[576,512]{1,0:T(8,128)(2,1)S(1)}, u32[]{:S(2)}, u32[]{:S(2)}) collective-permute-start(bf16[576,512]{1,0:T(8,128)(2,1)S(1)} %constant_dynamic-update-slice_fusion.s0), channel_id=1, source_target_pairs={{96,0},{0,32},{32,64},{64,96},{97,1},{1,33},{33,65},{65,97},{98,2}... | collective-permute-start | bytes 1769480 | tf_op jit(solution)/shard_map/ppermute | solution.py:252
  49.0 4.6 %collective-permute-start.12 = (bf16[576,512]{1,0:T(8,128)(2,1)S(1)}, bf16[576,512]{1,0:T(8,128)(2,1)S(1)}, u32[]{:S(2)}, u32[]{:S(2)}) collective-permute-start(bf16[576,512]{1,0:T(8,128)(2,1)S(1)} %constant_dynamic-update-slice_fusion.s0), channel_id=1, source_target_pairs={{32,0},{64,32},{96,64},{0,96},{33,1},{65,33},{97,65},{1,97},{34,2}... | collective-permute-start | bytes 1769480 | tf_op jit(solution)/shard_map/ppermute | solution.py:252
  53.7 2.7 %collective-permute-start.5 = (bf16[48,2176]{1,0:T(8,128)(2,1)S(1)}, bf16[48,2176]{1,0:T(8,128)(2,1)S(1)}, u32[]{:S(2)}, u32[]{:S(2)}) collective-permute-start(bf16[48,2176]{1,0:T(8,128)(2,1)S(1)} %bitcast.41), channel_id=1, source_target_pairs={{0,2},{2,4},{4,6},{6,8},{8,10},{10,12},{12,14},{14,0},{1,3},{3,5},... | collective-permute-start | bytes 626696 | tf_op jit(solution)/shard_map/ppermute | solution.py:247
  56.5 9.1 %collective-permute-start.6 = (bf16[48,2176]{1,0:T(8,128)(2,1)S(1)}, bf16[48,2176]{1,0:T(8,128)(2,1)S(1)}, u32[]{:S(2)}, u32[]{:S(2)}) collective-permute-start(bf16[48,2176]{1,0:T(8,128)(2,1)S(1)} %bitcast.42), channel_id=1, source_target_pairs={{0,14},{2,0},{4,2},{6,4},{8,6},{10,8},{12,10},{14,12},{1,15},{3,1}... | collective-permute-start | bytes 626696 | tf_op jit(solution)/shard_map/ppermute | solution.py:247
  66.7 1.9 %collective-permute-start.7 = (bf16[48,2176]{1,0:T(8,128)(2,1)S(1)}, bf16[48,2176]{1,0:T(8,128)(2,1)S(1)}, u32[]{:S(2)}, u32[]{:S(2)}) collective-permute-start(bf16[48,2176]{1,0:T(8,128)(2,1)S(1)} %collective-permute-done.5.r1), channel_id=1, source_target_pairs={{0,2},{2,4},{4,6},{6,8},{8,10},{10,12},{12,14},{14,0},{1,3},{3,5},... | collective-permute-start | bytes 626696 | tf_op jit(solution)/shard_map/ppermute | solution.py:247
  68.7 4.9 %collective-permute-start.8 = (bf16[48,2176]{1,0:T(8,128)(2,1)S(1)}, bf16[48,2176]{1,0:T(8,128)(2,1)S(1)}, u32[]{:S(2)}, u32[]{:S(2)}) collective-permute-start(bf16[48,2176]{1,0:T(8,128)(2,1)S(1)} %collective-permute-done.6.l1), channel_id=1, source_target_pairs={{0,14},{2,0},{4,2},{6,4},{8,6},{10,8},{12,10},{14,12},{1,15},{3,1}... | collective-permute-start | bytes 626696 | tf_op jit(solution)/shard_map/ppermute | solution.py:247
  73.6 1.2 collective-permute-done.7.r2
  74.9 1.9 %collective-permute-start.9 = (bf16[48,2176]{1,0:T(8,128)(2,1)S(1)}, bf16[48,2176]{1,0:T(8,128)(2,1)S(1)}, u32[]{:S(2)}, u32[]{:S(2)}) collective-permute-start(bf16[48,2176]{1,0:T(8,128)(2,1)S(1)} %collective-permute-done.7.r2), channel_id=1, source_target_pairs={{0,2},{2,4},{4,6},{6,8},{8,10},{10,12},{12,14},{14,0},{1,3},{3,5},... | collective-permute-start | bytes 626696 | tf_op jit(solution)/shard_map/ppermute | solution.py:247
  76.8 2.5 %collective-permute-start.14 = (bf16[288,512]{1,0:T(8,128)(2,1)S(1)}, bf16[288,512]{1,0:T(8,128)(2,1)S(1)}, u32[]{:S(2)}, u32[]{:S(2)}) collective-permute-start(bf16[288,512]{1,0:T(8,128)(2,1)S(1)} %slice.76), channel_id=1, source_target_pairs={{96,0},{0,32},{32,64},{64,96},{97,1},{1,33},{33,65},{65,97},{98,2}... | collective-permute-start | bytes 884744 | tf_op jit(solution)/shard_map/ppermute | solution.py:252
  79.4 3.9 %collective-permute-start.15 = (bf16[288,512]{1,0:T(8,128)(2,1)S(1)}, bf16[288,512]{1,0:T(8,128)(2,1)S(1)}, u32[]{:S(2)}, u32[]{:S(2)}) collective-permute-start(bf16[288,512]{1,0:T(8,128)(2,1)S(1)} %slice.77), channel_id=1, source_target_pairs={{32,0},{64,32},{96,64},{0,96},{33,1},{65,33},{97,65},{1,97},{34,2}... | collective-permute-start | bytes 884744 | tf_op jit(solution)/shard_map/ppermute | solution.py:252
  84.1 4.6 %collective-permute-start.10 = (bf16[48,2176]{1,0:T(8,128)(2,1)S(1)}, bf16[48,2176]{1,0:T(8,128)(2,1)S(1)}, u32[]{:S(2)}, u32[]{:S(2)}) collective-permute-start(bf16[48,2176]{1,0:T(8,128)(2,1)S(1)} %collective-permute-done.8.l2), channel_id=1, source_target_pairs={{0,14},{2,0},{4,2},{6,4},{8,6},{10,8},{12,10},{14,12},{1,15},{3,1}... | collective-permute-start | bytes 626696 | tf_op jit(solution)/shard_map/ppermute | solution.py:247
  88.7 1.9 %collective-permute-start.11 = (bf16[48,2176]{1,0:T(8,128)(2,1)S(1)}, bf16[48,2176]{1,0:T(8,128)(2,1)S(1)}, u32[]{:S(2)}, u32[]{:S(2)}) collective-permute-start(bf16[48,2176]{1,0:T(8,128)(2,1)S(1)} %collective-permute-done.9.r3), channel_id=1, source_target_pairs={{0,2},{2,4},{4,6},{6,8},{8,10},{10,12},{12,14},{14,0},{1,3},{3,5},... | collective-permute-start | bytes 626696 | tf_op jit(solution)/shard_map/ppermute | solution.py:247
  91.4 5.4 %collective-permute-done.11.far_z = bf16[48,2176]{1,0:T(8,128)(2,1)S(1)} collective-permute-done((bf16[48,2176]{1,0:T(8,128)(2,1)S(1)}, bf16[48,2176]{1,0:T(8,128)(2,1)S(1)}, u32[]{:S(2)}, u32[]{:S(2)}) %collective-permute-start.11) | collective-permute-done | bytes 208928 | tf_op jit(solution)/shard_map/ppermute | solution.py:247
  97.6 5.6 %shard_map.94 = (f32[192,640]{1,0:T(8,128)}, f32[192,640]{1,0:T(8,128)}, f32[1,128]{1,0:T(1,128)}, bf16[384,2176]{1,0:T(8,128)(2,1)}) custom-call(s32[4]{0:T(128)} %pad_add_fusion.place, bf16[2048,128]{1,0:T(8,128)(2,1)} %pad.17.down, bf16[48,2176]{1,0:T(8,128)(2,1)} %bitcast.43, bf16[48,2176]{1,0:T(8,128)(2,1)} %copy-done.11, bf16[48,2176]{1,0:T(8,128)(2,1)} %copy-done.12, ...), custom_call_target="tpu_custom_call" | custom-call | flops 1006632960 | bytes 10000000 | tf_op jit(solution)/shard_map/pallas_call | solution.py:234
  104.4 7.6 %collective-permute-start.16 = (f32[192,640]{1,0:T(8,128)}, f32[192,640]{1,0:T(8,128)S(1)}, u32[]{:S(2)}, u32[]{:S(2)}) collective-permute-start(f32[192,640]{1,0:T(8,128)} %get-tuple-element.34), channel_id=1, source_target_pairs={{0,16},{16,0},{1,17},{17,1},{2,18},{18,2},{3,19},{19,3},{4,20},{20... | collective-permute-start | bytes 1474568 | tf_op jit(solution)/shard_map/ppermute | solution.py:303
  112.4 1.3 collective-permute-done.16
  114.8 6.2 %shard_map.95 = (f32[192,1280]{1,0:T(8,128)}, f32[192,1280]{1,0:T(8,128)}) custom-call(s32[4]{0:T(128)} %pad_add_fusion.place, bf16[384,2176]{1,0:T(8,128)(2,1)} %get-tuple-element.32.tok.tok_in, bf16[2048,1280]{1,0:T(8,128)(2,1)} %all-gather.2.cloned.1.call-done.w_in), custom_call_target="tpu_custom_call" | custom-call | flops 2013265920 | bytes 10000000 | tf_op jit(solution)/shard_map/pallas_call | solution.py:234
  121.0 2.4 %collective-permute-start.17 = (f32[192,1280]{1,0:T(8,128)}, f32[192,1280]{1,0:T(8,128)S(1)}, u32[]{:S(2)}, u32[]{:S(2)}) collective-permute-start(f32[192,1280]{1,0:T(8,128)} %get-tuple-element.38), channel_id=1, source_target_pairs={{0,16},{16,0},{1,17},{17,1},{2,18},{18,2},{3,19},{19,3},{4,20},{20... | collective-permute-start | bytes 2949128 | tf_op jit(solution)/shard_map/ppermute | solution.py:322
  123.4 2.4 %collective-permute-done.17.partner = f32[192,1280]{1,0:T(8,128)S(1)} collective-permute-done((f32[192,1280]{1,0:T(8,128)}, f32[192,1280]{1,0:T(8,128)S(1)}, u32[]{:S(2)}, u32[]{:S(2)}) %collective-permute-start.17) | collective-permute-done | bytes 983072 | tf_op jit(solution)/shard_map/ppermute | solution.py:322
  125.8 1.2 copy-done.1
  127.0 3.9 %shard_map.96 = (f32[32,1,512]{2,1,0:T(1,128)S(1)}, f32[32,192]{1,0:T(8,128)S(1)}, bf16[4,192,896]{2,1,0:T(8,128)(2,1)S(1)}) custom-call(s32[4]{0:T(128)S(1)} %copy-done.2, f32[192,1280]{1,0:T(8,128)S(1)} %copy-done.1, f32[192,1280]{1,0:T(8,128)S(1)} %collective-permute-done.17.partner, f32[192,640]{1,0:T(8,128)S(1)} %add.54.side, ...), custom_call_target="tpu_custom_call" | custom-call | flops 176160768 | bytes 10000000 | tf_op jit(solution)/shard_map/pallas_call | solution.py:234
  130.9 17.3 %all_to_all.15.arrived = f32[32,1,512]{2,1,0:T(1,128)S(1)} all-to-all(f32[32,1,512]{2,1,0:T(1,128)S(1)} %get-tuple-element.45), channel_id=1, replica_groups=mesh['yh'=4,'x'=4,'c'=2,'z'=8,'yl'=2] {'c','z','yl'}, dimensions={0} | all-to-all | bytes 131072 | tf_op jit(solution)/shard_map/all_to_all | solution.py:331
  148.2 2.1 %shard_map.97 = (f32[32,1,1280]{2,1,0:T(1,128)S(1)}, f32[8,128]{1,0:T(8,128)S(1)}) custom-call(s32[4]{0:T(128)S(1)} %copy-done.2, f32[32,1,512]{2,1,0:T(1,128)S(1)} %all_to_all.15.arrived, bf16[2,128,192]{2,1,0:T(8,128)(2,1)S(1)} %fusion.7.signs, f32[2,1,128]{2,1,0:T(1,128)S(1)} %bitcast.39, f32[32,192]{1,0:T(8,128)S(1)} %get-tuple-element.47.low_t, ...), custom_call_target="tpu_custom_call" | custom-call | flops 12582912 | bytes 10000000 | tf_op jit(solution)/shard_map/pallas_call | solution.py:234
  150.4 18.1 %all_to_all.16 = f32[32,1,1280]{2,1,0:T(1,128)S(1)} all-to-all(f32[32,1,1280]{2,1,0:T(1,128)S(1)} %get-tuple-element.49), channel_id=1, replica_groups=mesh['yh'=4,'x'=4,'c'=2,'z'=8,'yl'=2] {'yh','x','c'}, dimensions={0} | all-to-all | bytes 327680 | tf_op jit(solution)/shard_map/all_to_all | solution.py:345
  169.3 3.5 %all-to-all-start.2 = ((f32[16,2,128]{2,1,0:T(2,128)}), f32[16,2,128]{2,1,0:T(2,128)S(1)}, u32[]{:S(2)}, u32[]{:S(2)}) async-start(f32[16,2,128]{2,1,0:T(2,128)} %broadcast_in_dim.10), calls=%async_computation.2 | async-start | bytes 32768 | tf_op jit(solution)/shard_map/all_to_all | solution.py:347
  175.6 4.5 %all-to-all-done.2 = f32[16,2,128]{2,1,0:T(2,128)S(1)} async-done(((f32[16,2,128]{2,1,0:T(2,128)}), f32[16,2,128]{2,1,0:T(2,128)S(1)}, u32[]{:S(2)}, u32[]{:S(2)}) %all-to-all-start.2) | async-done | bytes 16416 | tf_op jit(solution)/shard_map/all_to_all | solution.py:347
  (110 shorter events, 14.5 us)
Async XLA Ops:
  7.2 21.2 %copy-start.18 = (bf16[12,4096]{1,0:T(8,128)(2,1)S(1)}, bf16[12,4096]{1,0:T(8,128)(2,1)}, u32[]{:S(2)}) copy-start(bf16[12,4096]{1,0:T(8,128)(2,1)} %param.7) | copy-start | bytes 294916
  7.2 24.9 %copy-start.10 = (bf16[4096,32]{0,1:T(8,128)(2,1)S(1)}, bf16[4096,32]{0,1:T(8,128)(2,1)}, u32[]{:S(2)}) copy-start(bf16[4096,32]{0,1:T(8,128)(2,1)} %param.11) | copy-start | bytes 786436
  7.2 107.6 %all-gather.2.cloned.1.call-start = ((), (), s32[]{:S(2)}) async-start(), calls=%async_computation.3 | async-start | bytes 5570560 | tf_op jit(solution)/shard_map/all_gather | solution.py:261
  13.8 20.6 %collective-permute-start.1 = (bf16[144,512]{1,0:T(8,128)(2,1)S(1)}, bf16[144,512]{1,0:T(8,128)(2,1)S(1)}, u32[]{:S(2)}, u32[]{:S(2)}) collective-permute-start(bf16[144,512]{1,0:T(8,128)(2,1)S(1)} %fusion.6), channel_id=1, source_target_pairs={{128,0},{256,128},{384,256},{0,384},{129,1},{257,129},{385,257},{1... | collective-permute-start | bytes 442376 | tf_op jit(solution)/shard_map/ppermute | solution.py:252
  20.6 13.9 %collective-permute-start.2 = (bf16[144,512]{1,0:T(8,128)(2,1)S(1)}, bf16[144,512]{1,0:T(8,128)(2,1)S(1)}, u32[]{:S(2)}, u32[]{:S(2)}) collective-permute-start(bf16[144,512]{1,0:T(8,128)(2,1)S(1)} %fusion.6), channel_id=1, source_target_pairs={{256,0},{384,128},{0,256},{128,384},{257,1},{385,129},{1,257},{129... | collective-permute-start | bytes 442376 | tf_op jit(solution)/shard_map/ppermute | solution.py:252
  24.1 10.3 %collective-permute-start.3 = (bf16[144,512]{1,0:T(8,128)(2,1)S(1)}, bf16[144,512]{1,0:T(8,128)(2,1)S(1)}, u32[]{:S(2)}, u32[]{:S(2)}) collective-permute-start(bf16[144,512]{1,0:T(8,128)(2,1)S(1)} %fusion.6), channel_id=1, source_target_pairs={{384,0},{0,128},{128,256},{256,384},{385,1},{1,129},{129,257},{257... | collective-permute-start | bytes 442376 | tf_op jit(solution)/shard_map/ppermute | solution.py:252
  28.6 5.7 %collective-permute-start = (bf16[12,2176]{1,0:T(8,128)(2,1)S(1)}, bf16[12,2176]{1,0:T(8,128)(2,1)S(1)}, u32[]{:S(2)}, u32[]{:S(2)}) collective-permute-start(bf16[12,2176]{1,0:T(8,128)(2,1)S(1)} %pad_maximum_fusion.1), channel_id=1, source_target_pairs={{0,16},{16,0},{1,17},{17,1},{2,18},{18,2},{3,19},{19,3},{4,20},{20... | collective-permute-start | bytes 156680 | tf_op jit(solution)/shard_map/ppermute | solution.py:267
  33.4 23.0 %copy-start.19 = (bf16[32,896]{1,0:T(8,128)(2,1)S(1)}, bf16[32,896]{1,0:T(8,128)(2,1)}, u32[]{:S(2)}) copy-start(bf16[32,896]{1,0:T(8,128)(2,1)} %param.12) | copy-start | bytes 172036
  33.4 23.0 %copy-start.20 = (bf16[896]{0:T(1024)(128)(2,1)S(1)}, bf16[896]{0:T(1024)(128)(2,1)}, u32[]{:S(2)}) copy-start(bf16[896]{0:T(1024)(128)(2,1)} %param.13) | copy-start | bytes 5380
  34.4 19.1 %collective-permute-start.4 = (bf16[24,2176]{1,0:T(8,128)(2,1)S(1)}, bf16[24,2176]{1,0:T(8,128)(2,1)S(1)}, u32[]{:S(2)}, u32[]{:S(2)}) collective-permute-start(bf16[24,2176]{1,0:T(8,128)(2,1)S(1)} %maximum_select_fusion.1), channel_id=1, source_target_pairs={{0,1},{1,0},{2,3},{3,2},{4,5},{5,4},{6,7},{7,6},{8,9},{9,8},{10,11... | collective-permute-start | bytes 313352 | tf_op jit(solution)/shard_map/ppermute | solution.py:40
  47.1 49.8 %copy-start.6 = (bf16[576,512]{1,0:T(8,128)(2,1)}, bf16[576,512]{1,0:T(8,128)(2,1)S(1)}, u32[]{:S(2)}) copy-start(bf16[576,512]{1,0:T(8,128)(2,1)S(1)} %constant_dynamic-update-slice_fusion.s0) | copy-start | bytes 1769476
  47.1 29.7 %collective-permute-start.13 = (bf16[576,512]{1,0:T(8,128)(2,1)S(1)}, bf16[576,512]{1,0:T(8,128)(2,1)S(1)}, u32[]{:S(2)}, u32[]{:S(2)}) collective-permute-start(bf16[576,512]{1,0:T(8,128)(2,1)S(1)} %constant_dynamic-update-slice_fusion.s0), channel_id=1, source_target_pairs={{96,0},{0,32},{32,64},{64,96},{97,1},{1,33},{33,65},{65,97},{98,2}... | collective-permute-start | bytes 1769480 | tf_op jit(solution)/shard_map/ppermute | solution.py:252
  49.0 30.4 %collective-permute-start.12 = (bf16[576,512]{1,0:T(8,128)(2,1)S(1)}, bf16[576,512]{1,0:T(8,128)(2,1)S(1)}, u32[]{:S(2)}, u32[]{:S(2)}) collective-permute-start(bf16[576,512]{1,0:T(8,128)(2,1)S(1)} %constant_dynamic-update-slice_fusion.s0), channel_id=1, source_target_pairs={{32,0},{64,32},{96,64},{0,96},{33,1},{65,33},{97,65},{1,97},{34,2}... | collective-permute-start | bytes 1769480 | tf_op jit(solution)/shard_map/ppermute | solution.py:252
  53.7 43.2 %copy-start.7 = (bf16[2,24,2176]{2,1,0:T(8,128)(2,1)}, bf16[2,24,2176]{2,1,0:T(8,128)(2,1)S(1)}, u32[]{:S(2)}) copy-start(bf16[2,24,2176]{2,1,0:T(8,128)(2,1)S(1)} %maximum_select_fusion) | copy-start | bytes 626692
  53.7 13.1 %collective-permute-start.5 = (bf16[48,2176]{1,0:T(8,128)(2,1)S(1)}, bf16[48,2176]{1,0:T(8,128)(2,1)S(1)}, u32[]{:S(2)}, u32[]{:S(2)}) collective-permute-start(bf16[48,2176]{1,0:T(8,128)(2,1)S(1)} %bitcast.41), channel_id=1, source_target_pairs={{0,2},{2,4},{4,6},{6,8},{8,10},{10,12},{12,14},{14,0},{1,3},{3,5},... | collective-permute-start | bytes 626696 | tf_op jit(solution)/shard_map/ppermute | solution.py:247
  56.5 12.2 %collective-permute-start.6 = (bf16[48,2176]{1,0:T(8,128)(2,1)S(1)}, bf16[48,2176]{1,0:T(8,128)(2,1)S(1)}, u32[]{:S(2)}, u32[]{:S(2)}) collective-permute-start(bf16[48,2176]{1,0:T(8,128)(2,1)S(1)} %bitcast.42), channel_id=1, source_target_pairs={{0,14},{2,0},{4,2},{6,4},{8,6},{10,8},{12,10},{14,12},{1,15},{3,1}... | collective-permute-start | bytes 626696 | tf_op jit(solution)/shard_map/ppermute | solution.py:247
  66.7 30.1 %copy-start.11 = (bf16[48,2176]{1,0:T(8,128)(2,1)}, bf16[48,2176]{1,0:T(8,128)(2,1)S(1)}, u32[]{:S(2)}) copy-start(bf16[48,2176]{1,0:T(8,128)(2,1)S(1)} %collective-permute-done.5.r1) | copy-start | bytes 626692
  66.7 8.1 %collective-permute-start.7 = (bf16[48,2176]{1,0:T(8,128)(2,1)S(1)}, bf16[48,2176]{1,0:T(8,128)(2,1)S(1)}, u32[]{:S(2)}, u32[]{:S(2)}) collective-permute-start(bf16[48,2176]{1,0:T(8,128)(2,1)S(1)} %collective-permute-done.5.r1), channel_id=1, source_target_pairs={{0,2},{2,4},{4,6},{6,8},{8,10},{10,12},{12,14},{14,0},{1,3},{3,5},... | collective-permute-start | bytes 626696 | tf_op jit(solution)/shard_map/ppermute | solution.py:247
  68.7 28.2 %copy-start.12 = (bf16[48,2176]{1,0:T(8,128)(2,1)}, bf16[48,2176]{1,0:T(8,128)(2,1)S(1)}, u32[]{:S(2)}) copy-start(bf16[48,2176]{1,0:T(8,128)(2,1)S(1)} %collective-permute-done.6.l1) | copy-start | bytes 626692
  68.7 15.4 %collective-permute-start.8 = (bf16[48,2176]{1,0:T(8,128)(2,1)S(1)}, bf16[48,2176]{1,0:T(8,128)(2,1)S(1)}, u32[]{:S(2)}, u32[]{:S(2)}) collective-permute-start(bf16[48,2176]{1,0:T(8,128)(2,1)S(1)} %collective-permute-done.6.l1), channel_id=1, source_target_pairs={{0,14},{2,0},{4,2},{6,4},{8,6},{10,8},{12,10},{14,12},{1,15},{3,1}... | collective-permute-start | bytes 626696 | tf_op jit(solution)/shard_map/ppermute | solution.py:247
  74.9 22.0 %copy-start.13 = (bf16[48,2176]{1,0:T(8,128)(2,1)}, bf16[48,2176]{1,0:T(8,128)(2,1)S(1)}, u32[]{:S(2)}) copy-start(bf16[48,2176]{1,0:T(8,128)(2,1)S(1)} %collective-permute-done.7.r2) | copy-start | bytes 626692
  74.9 13.8 %collective-permute-start.9 = (bf16[48,2176]{1,0:T(8,128)(2,1)S(1)}, bf16[48,2176]{1,0:T(8,128)(2,1)S(1)}, u32[]{:S(2)}, u32[]{:S(2)}) collective-permute-start(bf16[48,2176]{1,0:T(8,128)(2,1)S(1)} %collective-permute-done.7.r2), channel_id=1, source_target_pairs={{0,2},{2,4},{4,6},{6,8},{8,10},{10,12},{12,14},{14,0},{1,3},{3,5},... | collective-permute-start | bytes 626696 | tf_op jit(solution)/shard_map/ppermute | solution.py:247
  76.8 20.1 %copy-start.4 = (bf16[576,512]{1,0:T(8,128)(2,1)}, bf16[576,512]{1,0:T(8,128)(2,1)S(1)}, u32[]{:S(2)}) copy-start(bf16[576,512]{1,0:T(8,128)(2,1)S(1)} %collective-permute-done.13.s3) | copy-start | bytes 1769476
  76.8 14.5 %collective-permute-start.14 = (bf16[288,512]{1,0:T(8,128)(2,1)S(1)}, bf16[288,512]{1,0:T(8,128)(2,1)S(1)}, u32[]{:S(2)}, u32[]{:S(2)}) collective-permute-start(bf16[288,512]{1,0:T(8,128)(2,1)S(1)} %slice.76), channel_id=1, source_target_pairs={{96,0},{0,32},{32,64},{64,96},{97,1},{1,33},{33,65},{65,97},{98,2}... | collective-permute-start | bytes 884744 | tf_op jit(solution)/shard_map/ppermute | solution.py:252
  79.4 17.5 %copy-start.5 = (bf16[576,512]{1,0:T(8,128)(2,1)}, bf16[576,512]{1,0:T(8,128)(2,1)S(1)}, u32[]{:S(2)}) copy-start(bf16[576,512]{1,0:T(8,128)(2,1)S(1)} %collective-permute-done.12.s1) | copy-start | bytes 1769476
  79.4 11.9 %collective-permute-start.15 = (bf16[288,512]{1,0:T(8,128)(2,1)S(1)}, bf16[288,512]{1,0:T(8,128)(2,1)S(1)}, u32[]{:S(2)}, u32[]{:S(2)}) collective-permute-start(bf16[288,512]{1,0:T(8,128)(2,1)S(1)} %slice.77), channel_id=1, source_target_pairs={{32,0},{64,32},{96,64},{0,96},{33,1},{65,33},{97,65},{1,97},{34,2}... | collective-permute-start | bytes 884744 | tf_op jit(solution)/shard_map/ppermute | solution.py:252
  84.1 7.3 %collective-permute-start.10 = (bf16[48,2176]{1,0:T(8,128)(2,1)S(1)}, bf16[48,2176]{1,0:T(8,128)(2,1)S(1)}, u32[]{:S(2)}, u32[]{:S(2)}) collective-permute-start(bf16[48,2176]{1,0:T(8,128)(2,1)S(1)} %collective-permute-done.8.l2), channel_id=1, source_target_pairs={{0,14},{2,0},{4,2},{6,4},{8,6},{10,8},{12,10},{14,12},{1,15},{3,1}... | collective-permute-start | bytes 626696 | tf_op jit(solution)/shard_map/ppermute | solution.py:247
  88.7 8.2 %collective-permute-start.11 = (bf16[48,2176]{1,0:T(8,128)(2,1)S(1)}, bf16[48,2176]{1,0:T(8,128)(2,1)S(1)}, u32[]{:S(2)}, u32[]{:S(2)}) collective-permute-start(bf16[48,2176]{1,0:T(8,128)(2,1)S(1)} %collective-permute-done.9.r3), channel_id=1, source_target_pairs={{0,2},{2,4},{4,6},{6,8},{8,10},{10,12},{12,14},{14,0},{1,3},{3,5},... | collective-permute-start | bytes 626696 | tf_op jit(solution)/shard_map/ppermute | solution.py:247
  104.4 9.3 %collective-permute-start.16 = (f32[192,640]{1,0:T(8,128)}, f32[192,640]{1,0:T(8,128)S(1)}, u32[]{:S(2)}, u32[]{:S(2)}) collective-permute-start(f32[192,640]{1,0:T(8,128)} %get-tuple-element.34), channel_id=1, source_target_pairs={{0,16},{16,0},{1,17},{17,1},{2,18},{18,2},{3,19},{19,3},{4,20},{20... | collective-permute-start | bytes 1474568 | tf_op jit(solution)/shard_map/ppermute | solution.py:303
  121.0 27.2 %copy-start = (bf16[384,2176]{1,0:T(8,128)(2,1)S(1)}, bf16[384,2176]{1,0:T(8,128)(2,1)}, u32[]{:S(2)}) copy-start(bf16[384,2176]{1,0:T(8,128)(2,1)} %get-tuple-element.32.tok.tok_in) | copy-start | bytes 5013508
  121.0 4.8 %collective-permute-start.17 = (f32[192,1280]{1,0:T(8,128)}, f32[192,1280]{1,0:T(8,128)S(1)}, u32[]{:S(2)}, u32[]{:S(2)}) collective-permute-start(f32[192,1280]{1,0:T(8,128)} %get-tuple-element.38), channel_id=1, source_target_pairs={{0,16},{16,0},{1,17},{17,1},{2,18},{18,2},{3,19},{19,3},{4,20},{20... | collective-permute-start | bytes 2949128 | tf_op jit(solution)/shard_map/ppermute | solution.py:322
  169.3 10.8 %all-to-all-start.2 = ((f32[16,2,128]{2,1,0:T(2,128)}), f32[16,2,128]{2,1,0:T(2,128)S(1)}, u32[]{:S(2)}, u32[]{:S(2)}) async-start(f32[16,2,128]{2,1,0:T(2,128)} %broadcast_in_dim.10), calls=%async_computation.2 | async-start | bytes 32768 | tf_op jit(solution)/shard_map/all_to_all | solution.py:347
  (9 other events, 61.6 us)
Sparse Core Ops, SparseCore 0:
  11.1 98.5 all-gather.1

commit v19 on v17

--- a/solution.py
+++ b/solution.py
@@ -306,8 +306,8 @@
     signs = chosen.astype(BF16) - rejected.astype(BF16)
     valid = (jnp.any(chosen, axis=2) & jnp.any(rejected, axis=2)).astype(F32).reshape(2, 1, LANES)
 
-    w_main, side, b_gate, b_up, read, signs, valid, count_lanes = lax.optimization_barrier(
-        (w_main, side, b_gate, b_up, read, signs, valid, count_lanes)
+    w_main, side, b_gate, b_up, read, count_lanes = lax.optimization_barrier(
+        (w_main, side, b_gate, b_up, read, count_lanes)
     )
     far, near = products(place, tok, w_main)
     partner = lax.ppermute(far, "c", SWAP)

time: 190 us -> 205 us (1.079)
  waiting for transfers between devices: 16.7 us -> 44.2 us
  blocking collectives: 35.5 us -> 18.9 us
  local copies, waits for them, and re-layouts: 9.32 us -> 18.4 us
  starting transfers between devices: 83.9 us -> 79.2 us
    ppermute x7, waiting for transfers between devices: 0.02 us -> 26.9 us  [fetch(): return lax.ppermute(value, axis, [((i + k) % n, i) for i in range(n)])]
    all_to_all x1 -> x0, blocking collectives: 17.3 us -> none  [on_device(): lax.all_to_all(message, ('c', 'z', 'yl'), split_axis=0, concat_axis=0)]
    ppermute x1, starting transfers between devices: 12.5 us -> 4.45 us  [swapped(): far = lax.ppermute(value, axis, SWAP)]
    all_to_all x0 -> x1, starting transfers between devices: none -> 7.75 us  [on_device(): lax.all_to_all(message, ('c', 'z', 'yl'), split_axis=0, concat_axis=0)]
    all_to_all x0 -> x1, waiting for transfers between devices: none -> 7.32 us  [on_device(): lax.all_to_all(message, ('c', 'z', 'yl'), split_axis=0, concat_axis=0)]
    ppermute x7, waiting for transfers between devices: 8.51 us -> 1.59 us  [along(): return lax.ppermute(value, axis, [(i, (i + k) % n) for i in range(n)])]
    unnamed x51 -> x57, local copies, waits for them, and re-layouts: 2.7 us -> 9.59 us
    ppermute x7, starting transfers between devices: 27.5 us -> 21.2 us  [fetch(): return lax.ppermute(value, axis, [((i + k) % n, i) for i in range(n)])]
  transfers between devices with their start and end apart: 20 -> 21, of which waited for: 7 -> 12; matrix products, arithmetic and copies ran while one was open for 5% -> 6% of each run, Pallas kernels for 3% -> 3%
where the time goes in v19:
time: 205 us; the launch traced here: 204 us
  starting transfers between devices  79.2 us (39%)
  waiting for transfers between devices  44.2 us (22%)
  between operations  19.7 us (10%)
  blocking collectives  18.9 us (9%)
  local copies, waits for them, and re-layouts  18.4 us (9%)
  Pallas kernels  17.6 us (9%)
  other arithmetic  5.92 us (3%)
    ppermute x7, waiting for transfers between devices, fetch(): return lax.ppermute(value, axis, [((i + k) % n, i) for i in range(n)])  26.9 us
    ppermute x7, starting transfers between devices, along(): return lax.ppermute(value, axis, [(i, (i + k) % n) for i in range(n)])  26.3 us
    ppermute x7, starting transfers between devices, fetch(): return lax.ppermute(value, axis, [((i + k) % n, i) for i in range(n)])  21.2 us
    all_to_all x1, blocking collectives, on_device(): lax.all_to_all(outgoing, DP, split_axis=0, concat_axis=0)  18.9 us
    pallas_call x4, Pallas kernels, kernel(): pl.pallas_call(function, out_shape=tuple((jax.ShapeDtypeStruct(*s) for s...  17.6 us
    unnamed x57, local copies, waits for them, and re-layouts  9.59 us
    ppermute x1, starting transfers between devices, on_device(): take = lax.ppermute(give, 'c', SWAP)  8.79 us
    all_to_all x1, starting transfers between devices, on_device(): lax.all_to_all(message, ('c', 'z', 'yl'), split_axis=0, concat_axis=0)  7.75 us
  transfers between devices with their start and end apart: 21, of which 12 were waited for; matrix products, arithmetic and copies ran while one was open for 6% of the time, Pallas kernels for 3%

profile of v19, /device:TPU:1, one launch (start us, length us, event | category | flops | bytes accessed | tf_op | source)
XLA Modules:
  0.0 204.0 jit_solution(6810067029997660179)
XLA Ops:
  10.7 8.8 %collective-permute-start = (bf16[12,2176]{1,0:T(8,128)(2,1)S(1)}, bf16[12,2176]{1,0:T(8,128)(2,1)S(1)}, u32[]{:S(2)}, u32[]{:S(2)}) collective-permute-start(bf16[12,2176]{1,0:T(8,128)(2,1)S(1)} %pad_maximum_fusion.1), channel_id=1, source_target_pairs={{0,16},{16,0},{1,17},{17,1},{2,18},{18,2},{3,19},{19,3},{4,20},{20... | collective-permute-start | bytes 156680 | tf_op jit(solution)/shard_map/ppermute | solution.py:258
  23.0 1.9 collective-permute-start.1
  24.9 2.1 %collective-permute-start.2 = (bf16[144,512]{1,0:T(8,128)(2,1)S(1)}, bf16[144,512]{1,0:T(8,128)(2,1)S(1)}, u32[]{:S(2)}, u32[]{:S(2)}) collective-permute-start(bf16[144,512]{1,0:T(8,128)(2,1)S(1)} %fusion.6), channel_id=1, source_target_pairs={{256,0},{384,128},{0,256},{128,384},{257,1},{385,129},{1,257},{129... | collective-permute-start | bytes 442376 | tf_op jit(solution)/shard_map/ppermute | solution.py:243
  27.0 4.2 %collective-permute-start.3 = (bf16[144,512]{1,0:T(8,128)(2,1)S(1)}, bf16[144,512]{1,0:T(8,128)(2,1)S(1)}, u32[]{:S(2)}, u32[]{:S(2)}) collective-permute-start(bf16[144,512]{1,0:T(8,128)(2,1)S(1)} %fusion.6), channel_id=1, source_target_pairs={{384,0},{0,128},{128,256},{256,384},{385,1},{1,129},{129,257},{257... | collective-permute-start | bytes 442376 | tf_op jit(solution)/shard_map/ppermute | solution.py:243
  31.5 4.9 %collective-permute-done.2 = bf16[144,512]{1,0:T(8,128)(2,1)S(1)} collective-permute-done((bf16[144,512]{1,0:T(8,128)(2,1)S(1)}, bf16[144,512]{1,0:T(8,128)(2,1)S(1)}, u32[]{:S(2)}, u32[]{:S(2)}) %collective-permute-start.2) | collective-permute-done | bytes 147488 | tf_op jit(solution)/shard_map/ppermute | solution.py:243
  36.3 15.2 %collective-permute-done.3 = bf16[144,512]{1,0:T(8,128)(2,1)S(1)} collective-permute-done((bf16[144,512]{1,0:T(8,128)(2,1)S(1)}, bf16[144,512]{1,0:T(8,128)(2,1)S(1)}, u32[]{:S(2)}, u32[]{:S(2)}) %collective-permute-start.3) | collective-permute-done | bytes 147488 | tf_op jit(solution)/shard_map/ppermute | solution.py:243
  51.6 4.5 %collective-permute-start.4 = (bf16[24,2176]{1,0:T(8,128)(2,1)S(1)}, bf16[24,2176]{1,0:T(8,128)(2,1)S(1)}, u32[]{:S(2)}, u32[]{:S(2)}) collective-permute-start(bf16[24,2176]{1,0:T(8,128)(2,1)S(1)} %maximum_select_fusion.1), channel_id=1, source_target_pairs={{0,1},{1,0},{2,3},{3,2},{4,5},{5,4},{6,7},{7,6},{8,9},{9,8},{10,11... | collective-permute-start | bytes 313352 | tf_op jit(solution)/shard_map/ppermute | solution.py:40
  56.1 2.7 %collective-permute-done.4 = bf16[24,2176]{1,0:T(8,128)(2,1)S(1)} collective-permute-done((bf16[24,2176]{1,0:T(8,128)(2,1)S(1)}, bf16[24,2176]{1,0:T(8,128)(2,1)S(1)}, u32[]{:S(2)}, u32[]{:S(2)}) %collective-permute-start.4) | collective-permute-done | bytes 104480 | tf_op jit(solution)/shard_map/ppermute | solution.py:40
  58.9 1.9 collective-permute-start.5
  60.8 1.9 collective-permute-start.13
  62.7 4.6 %collective-permute-start.12 = (bf16[576,512]{1,0:T(8,128)(2,1)S(1)}, bf16[576,512]{1,0:T(8,128)(2,1)S(1)}, u32[]{:S(2)}, u32[]{:S(2)}) collective-permute-start(bf16[576,512]{1,0:T(8,128)(2,1)S(1)} %constant_dynamic-update-slice_fusion.s0), channel_id=1, source_target_pairs={{32,0},{64,32},{96,64},{0,96},{33,1},{65,33},{97,65},{1,97},{34,2}... | collective-permute-start | bytes 1769480 | tf_op jit(solution)/shard_map/ppermute | solution.py:243
  67.3 7.9 %collective-permute-start.6 = (bf16[48,2176]{1,0:T(8,128)(2,1)S(1)}, bf16[48,2176]{1,0:T(8,128)(2,1)}, u32[]{:S(2)}, u32[]{:S(2)}) collective-permute-start(bf16[48,2176]{1,0:T(8,128)(2,1)S(1)} %bitcast.42), channel_id=1, source_target_pairs={{0,14},{2,0},{4,2},{6,4},{8,6},{10,8},{12,10},{14,12},{1,15},{3,1}... | collective-permute-start | bytes 626696 | tf_op jit(solution)/shard_map/ppermute | solution.py:238
  75.2 1.9 collective-permute-start.7
  78.8 5.4 %collective-permute-start.8 = (bf16[48,2176]{1,0:T(8,128)(2,1)}, bf16[48,2176]{1,0:T(8,128)(2,1)}, u32[]{:S(2)}, u32[]{:S(2)}) collective-permute-start(bf16[48,2176]{1,0:T(8,128)(2,1)} %collective-permute-done.6.l1), channel_id=1, source_target_pairs={{0,14},{2,0},{4,2},{6,4},{8,6},{10,8},{12,10},{14,12},{1,15},{3,1}... | collective-permute-start | bytes 626696 | tf_op jit(solution)/shard_map/ppermute | solution.py:238
  84.3 1.9 collective-permute-start.9
  87.3 5.3 %collective-permute-start.10 = (bf16[48,2176]{1,0:T(8,128)(2,1)}, bf16[48,2176]{1,0:T(8,128)(2,1)S(1)}, u32[]{:S(2)}, u32[]{:S(2)}) collective-permute-start(bf16[48,2176]{1,0:T(8,128)(2,1)} %collective-permute-done.8.l2), channel_id=1, source_target_pairs={{0,14},{2,0},{4,2},{6,4},{8,6},{10,8},{12,10},{14,12},{1,15},{3,1}... | collective-permute-start | bytes 626696 | tf_op jit(solution)/shard_map/ppermute | solution.py:238
  93.5 1.9 collective-permute-start.14
  95.4 4.6 %collective-permute-start.15 = (bf16[288,512]{1,0:T(8,128)(2,1)S(1)}, bf16[288,512]{1,0:T(8,128)(2,1)S(1)}, u32[]{:S(2)}, u32[]{:S(2)}) collective-permute-start(bf16[288,512]{1,0:T(8,128)(2,1)S(1)} %slice.77), channel_id=1, source_target_pairs={{32,0},{64,32},{96,64},{0,96},{33,1},{65,33},{97,65},{1,97},{34,2}... | collective-permute-start | bytes 884744 | tf_op jit(solution)/shard_map/ppermute | solution.py:243
  100.0 1.9 collective-permute-start.11
  103.6 4.8 %collective-permute-done.14.s2_low = bf16[288,512]{1,0:T(8,128)(2,1)} collective-permute-done((bf16[288,512]{1,0:T(8,128)(2,1)}, bf16[288,512]{1,0:T(8,128)(2,1)}, u32[]{:S(2)}, u32[]{:S(2)}) %collective-permute-start.14) | collective-permute-done | bytes 294944 | tf_op jit(solution)/shard_map/ppermute | solution.py:243
  108.4 1.9 collective-permute-done.15.s2_high
  111.0 5.6 %shard_map.94 = (f32[192,640]{1,0:T(8,128)}, f32[192,640]{1,0:T(8,128)}, f32[1,128]{1,0:T(1,128)}, bf16[384,2176]{1,0:T(8,128)(2,1)}) custom-call(s32[4]{0:T(128)} %pad_add_fusion.place, bf16[2048,128]{1,0:T(8,128)(2,1)} %pad.17.down, bf16[48,2176]{1,0:T(8,128)(2,1)} %bitcast.43, bf16[48,2176]{1,0:T(8,128)(2,1)} %copy-done.19, ...), custom_call_target="tpu_custom_call" | custom-call | flops 1006632960 | bytes 10000000 | tf_op jit(solution)/shard_map/pallas_call | solution.py:225
  116.6 4.9 %collective-permute-start.16 = (f32[192,640]{1,0:T(8,128)}, f32[192,640]{1,0:T(8,128)S(1)}, u32[]{:S(2)}, u32[]{:S(2)}) collective-permute-start(f32[192,640]{1,0:T(8,128)} %get-tuple-element.32), channel_id=1, source_target_pairs={{0,16},{16,0},{1,17},{17,1},{2,18},{18,2},{3,19},{19,3},{4,20},{20... | collective-permute-start | bytes 1474568 | tf_op jit(solution)/shard_map/ppermute | solution.py:294
  124.3 6.1 %shard_map.95 = (f32[192,1280]{1,0:T(8,128)}, f32[192,1280]{1,0:T(8,128)}) custom-call(s32[4]{0:T(128)} %pad_add_fusion.place, bf16[384,2176]{1,0:T(8,128)(2,1)} %get-tuple-element.30.tok.tok_in, bf16[2048,1280]{1,0:T(8,128)(2,1)} %all-gather.2.cloned.1.call-done.w_in), custom_call_target="tpu_custom_call" | custom-call | flops 2013265920 | bytes 10000000 | tf_op jit(solution)/shard_map/pallas_call | solution.py:225
  130.4 2.3 %collective-permute-start.17 = (f32[192,1280]{1,0:T(8,128)}, f32[192,1280]{1,0:T(8,128)S(1)}, u32[]{:S(2)}, u32[]{:S(2)}) collective-permute-start(f32[192,1280]{1,0:T(8,128)} %get-tuple-element.36), channel_id=1, source_target_pairs={{0,16},{16,0},{1,17},{17,1},{2,18},{18,2},{3,19},{19,3},{4,20},{20... | collective-permute-start | bytes 2949128 | tf_op jit(solution)/shard_map/ppermute | solution.py:313
  140.3 3.8 %shard_map.96 = (f32[32,1,512]{2,1,0:T(1,128)S(1)}, f32[32,192]{1,0:T(8,128)S(1)}, bf16[4,192,896]{2,1,0:T(8,128)(2,1)S(1)}) custom-call(s32[4]{0:T(128)S(1)} %copy-done.11, f32[192,1280]{1,0:T(8,128)S(1)} %copy-done.3, f32[192,1280]{1,0:T(8,128)S(1)} %copy-done.5, f32[192,640]{1,0:T(8,128)S(1)} %add.54.side, bf16[128,896]{1,0:T(8,128)(2,1)S(1)} %copy-done.6, ...), custom_call_target="tpu_custom_call" | custom-call | flops 176160768 | bytes 10000000 | tf_op jit(solution)/shard_map/pallas_call | solution.py:225
  145.4 7.8 %all-to-all-start = ((f32[32,1,512]{2,1,0:T(1,128)}), f32[32,1,512]{2,1,0:T(1,128)S(1)}, u32[]{:S(2)}, u32[]{:S(2)}) async-start(f32[32,1,512]{2,1,0:T(1,128)} %copy-done.8), calls=%async_computation | async-start | bytes 131072 | tf_op jit(solution)/shard_map/all_to_all | solution.py:322
  153.8 7.3 %all-to-all-done.arrived = f32[32,1,512]{2,1,0:T(1,128)S(1)} async-done(((f32[32,1,512]{2,1,0:T(1,128)}), f32[32,1,512]{2,1,0:T(1,128)S(1)}, u32[]{:S(2)}, u32[]{:S(2)}) %all-to-all-start) | async-done | bytes 65568 | tf_op jit(solution)/shard_map/all_to_all | solution.py:322
  162.8 2.1 %shard_map.97 = (f32[32,1,1280]{2,1,0:T(1,128)S(1)}, f32[8,128]{1,0:T(8,128)S(1)}) custom-call(s32[4]{0:T(128)S(1)} %copy-done.11, f32[32,1,512]{2,1,0:T(1,128)S(1)} %all-to-all-done.arrived, bf16[2,128,192]{2,1,0:T(8,128)(2,1)S(1)} %copy-done.2, f32[2,1,128]{2,1,0:T(1,128)S(1)} %bitcast.39, f32[32,192]{1,0:T(8,128)S(1)} %copy-done.10, ...), custom_call_target="tpu_custom_call" | custom-call | flops 12582912 | bytes 10000000 | tf_op jit(solution)/shard_map/pallas_call | solution.py:225
  165.0 18.9 %all_to_all.15 = f32[32,1,1280]{2,1,0:T(1,128)S(1)} all-to-all(f32[32,1,1280]{2,1,0:T(1,128)S(1)} %get-tuple-element.45), channel_id=1, replica_groups=mesh['yh'=4,'x'=4,'c'=2,'z'=8,'yl'=2] {'yh','x','c'}, dimensions={0} | all-to-all | bytes 327680 | tf_op jit(solution)/shard_map/all_to_all | solution.py:336
  184.6 3.5 %all-to-all-start.2 = ((f32[16,2,128]{2,1,0:T(2,128)}), f32[16,2,128]{2,1,0:T(2,128)S(1)}, u32[]{:S(2)}, u32[]{:S(2)}) async-start(f32[16,2,128]{2,1,0:T(2,128)} %broadcast_in_dim.10), calls=%async_computation.2 | async-start | bytes 32768 | tf_op jit(solution)/shard_map/all_to_all | solution.py:338
  191.1 4.3 %all-to-all-done.2 = f32[16,2,128]{2,1,0:T(2,128)S(1)} async-done(((f32[16,2,128]{2,1,0:T(2,128)}), f32[16,2,128]{2,1,0:T(2,128)S(1)}, u32[]{:S(2)}, u32[]{:S(2)}) %all-to-all-start.2) | async-done | bytes 16416 | tf_op jit(solution)/shard_map/all_to_all | solution.py:338
  (117 shorter events, 27.4 us)
Async XLA Ops:
  7.2 117.1 %all-gather.2.cloned.1.call-start = ((), (), s32[]{:S(2)}) async-start(), calls=%async_computation.3 | async-start | bytes 5570560 | tf_op jit(solution)/shard_map/all_gather | solution.py:252
  10.6 66.5 %copy-start.18 = (bf16[4096,32]{0,1:T(8,128)(2,1)S(1)}, bf16[4096,32]{0,1:T(8,128)(2,1)}, u32[]{:S(2)}) copy-start(bf16[4096,32]{0,1:T(8,128)(2,1)} %param.11) | copy-start | bytes 786436
  10.7 20.6 %collective-permute-start = (bf16[12,2176]{1,0:T(8,128)(2,1)S(1)}, bf16[12,2176]{1,0:T(8,128)(2,1)S(1)}, u32[]{:S(2)}, u32[]{:S(2)}) collective-permute-start(bf16[12,2176]{1,0:T(8,128)(2,1)S(1)} %pad_maximum_fusion.1), channel_id=1, source_target_pairs={{0,16},{16,0},{1,17},{17,1},{2,18},{18,2},{3,19},{19,3},{4,20},{20... | collective-permute-start | bytes 156680 | tf_op jit(solution)/shard_map/ppermute | solution.py:258
  23.0 8.5 %collective-permute-start.1 = (bf16[144,512]{1,0:T(8,128)(2,1)S(1)}, bf16[144,512]{1,0:T(8,128)(2,1)S(1)}, u32[]{:S(2)}, u32[]{:S(2)}) collective-permute-start(bf16[144,512]{1,0:T(8,128)(2,1)S(1)} %fusion.6), channel_id=1, source_target_pairs={{128,0},{256,128},{384,256},{0,384},{129,1},{257,129},{385,257},{1... | collective-permute-start | bytes 442376 | tf_op jit(solution)/shard_map/ppermute | solution.py:243
  24.9 11.4 %collective-permute-start.2 = (bf16[144,512]{1,0:T(8,128)(2,1)S(1)}, bf16[144,512]{1,0:T(8,128)(2,1)S(1)}, u32[]{:S(2)}, u32[]{:S(2)}) collective-permute-start(bf16[144,512]{1,0:T(8,128)(2,1)S(1)} %fusion.6), channel_id=1, source_target_pairs={{256,0},{384,128},{0,256},{128,384},{257,1},{385,129},{1,257},{129... | collective-permute-start | bytes 442376 | tf_op jit(solution)/shard_map/ppermute | solution.py:243
  27.0 24.5 %collective-permute-start.3 = (bf16[144,512]{1,0:T(8,128)(2,1)S(1)}, bf16[144,512]{1,0:T(8,128)(2,1)S(1)}, u32[]{:S(2)}, u32[]{:S(2)}) collective-permute-start(bf16[144,512]{1,0:T(8,128)(2,1)S(1)} %fusion.6), channel_id=1, source_target_pairs={{384,0},{0,128},{128,256},{256,384},{385,1},{1,129},{129,257},{257... | collective-permute-start | bytes 442376 | tf_op jit(solution)/shard_map/ppermute | solution.py:243
  51.6 7.2 %collective-permute-start.4 = (bf16[24,2176]{1,0:T(8,128)(2,1)S(1)}, bf16[24,2176]{1,0:T(8,128)(2,1)S(1)}, u32[]{:S(2)}, u32[]{:S(2)}) collective-permute-start(bf16[24,2176]{1,0:T(8,128)(2,1)S(1)} %maximum_select_fusion.1), channel_id=1, source_target_pairs={{0,1},{1,0},{2,3},{3,2},{4,5},{5,4},{6,7},{7,6},{8,9},{9,8},{10,11... | collective-permute-start | bytes 313352 | tf_op jit(solution)/shard_map/ppermute | solution.py:40
  58.8 28.4 %copy-start.16 = (bf16[2,24,2176]{2,1,0:T(8,128)(2,1)}, bf16[2,24,2176]{2,1,0:T(8,128)(2,1)S(1)}, u32[]{:S(2)}) copy-start(bf16[2,24,2176]{2,1,0:T(8,128)(2,1)S(1)} %maximum_select_fusion) | copy-start | bytes 626692
  58.9 16.3 %collective-permute-start.5 = (bf16[48,2176]{1,0:T(8,128)(2,1)S(1)}, bf16[48,2176]{1,0:T(8,128)(2,1)S(1)}, u32[]{:S(2)}, u32[]{:S(2)}) collective-permute-start(bf16[48,2176]{1,0:T(8,128)(2,1)S(1)} %bitcast.41), channel_id=1, source_target_pairs={{0,2},{2,4},{4,6},{6,8},{8,10},{10,12},{12,14},{14,0},{1,3},{3,5},... | collective-permute-start | bytes 626696 | tf_op jit(solution)/shard_map/ppermute | solution.py:238
  60.8 32.7 %copy-start.15 = (bf16[576,512]{1,0:T(8,128)(2,1)}, bf16[576,512]{1,0:T(8,128)(2,1)S(1)}, u32[]{:S(2)}) copy-start(bf16[576,512]{1,0:T(8,128)(2,1)S(1)} %constant_dynamic-update-slice_fusion.s0) | copy-start | bytes 1769476
  60.8 31.8 %collective-permute-start.13 = (bf16[576,512]{1,0:T(8,128)(2,1)S(1)}, bf16[576,512]{1,0:T(8,128)(2,1)S(1)}, u32[]{:S(2)}, u32[]{:S(2)}) collective-permute-start(bf16[576,512]{1,0:T(8,128)(2,1)S(1)} %constant_dynamic-update-slice_fusion.s0), channel_id=1, source_target_pairs={{96,0},{0,32},{32,64},{64,96},{97,1},{1,33},{33,65},{65,97},{98,2}... | collective-permute-start | bytes 1769480 | tf_op jit(solution)/shard_map/ppermute | solution.py:243
  62.7 32.6 %collective-permute-start.12 = (bf16[576,512]{1,0:T(8,128)(2,1)S(1)}, bf16[576,512]{1,0:T(8,128)(2,1)S(1)}, u32[]{:S(2)}, u32[]{:S(2)}) collective-permute-start(bf16[576,512]{1,0:T(8,128)(2,1)S(1)} %constant_dynamic-update-slice_fusion.s0), channel_id=1, source_target_pairs={{32,0},{64,32},{96,64},{0,96},{33,1},{65,33},{97,65},{1,97},{34,2}... | collective-permute-start | bytes 1769480 | tf_op jit(solution)/shard_map/ppermute | solution.py:243
  67.3 11.5 %collective-permute-start.6 = (bf16[48,2176]{1,0:T(8,128)(2,1)S(1)}, bf16[48,2176]{1,0:T(8,128)(2,1)}, u32[]{:S(2)}, u32[]{:S(2)}) collective-permute-start(bf16[48,2176]{1,0:T(8,128)(2,1)S(1)} %bitcast.42), channel_id=1, source_target_pairs={{0,14},{2,0},{4,2},{6,4},{8,6},{10,8},{12,10},{14,12},{1,15},{3,1}... | collective-permute-start | bytes 626696 | tf_op jit(solution)/shard_map/ppermute | solution.py:238
  75.2 11.7 %copy-start.19 = (bf16[48,2176]{1,0:T(8,128)(2,1)}, bf16[48,2176]{1,0:T(8,128)(2,1)S(1)}, u32[]{:S(2)}) copy-start(bf16[48,2176]{1,0:T(8,128)(2,1)S(1)} %collective-permute-done.5.r1) | copy-start | bytes 626692
  75.2 9.1 %collective-permute-start.7 = (bf16[48,2176]{1,0:T(8,128)(2,1)S(1)}, bf16[48,2176]{1,0:T(8,128)(2,1)}, u32[]{:S(2)}, u32[]{:S(2)}) collective-permute-start(bf16[48,2176]{1,0:T(8,128)(2,1)S(1)} %collective-permute-done.5.r1), channel_id=1, source_target_pairs={{0,2},{2,4},{4,6},{6,8},{8,10},{10,12},{12,14},{14,0},{1,3},{3,5},... | collective-permute-start | bytes 626696 | tf_op jit(solution)/shard_map/ppermute | solution.py:238
  78.8 8.5 %collective-permute-start.8 = (bf16[48,2176]{1,0:T(8,128)(2,1)}, bf16[48,2176]{1,0:T(8,128)(2,1)}, u32[]{:S(2)}, u32[]{:S(2)}) collective-permute-start(bf16[48,2176]{1,0:T(8,128)(2,1)} %collective-permute-done.6.l1), channel_id=1, source_target_pairs={{0,14},{2,0},{4,2},{6,4},{8,6},{10,8},{12,10},{14,12},{1,15},{3,1}... | collective-permute-start | bytes 626696 | tf_op jit(solution)/shard_map/ppermute | solution.py:238
  84.3 15.7 %collective-permute-start.9 = (bf16[48,2176]{1,0:T(8,128)(2,1)}, bf16[48,2176]{1,0:T(8,128)(2,1)}, u32[]{:S(2)}, u32[]{:S(2)}) collective-permute-start(bf16[48,2176]{1,0:T(8,128)(2,1)} %collective-permute-done.7.r2), channel_id=1, source_target_pairs={{0,2},{2,4},{4,6},{6,8},{8,10},{10,12},{12,14},{14,0},{1,3},{3,5},... | collective-permute-start | bytes 626696 | tf_op jit(solution)/shard_map/ppermute | solution.py:238
  87.3 16.3 %collective-permute-start.10 = (bf16[48,2176]{1,0:T(8,128)(2,1)}, bf16[48,2176]{1,0:T(8,128)(2,1)S(1)}, u32[]{:S(2)}, u32[]{:S(2)}) collective-permute-start(bf16[48,2176]{1,0:T(8,128)(2,1)} %collective-permute-done.8.l2), channel_id=1, source_target_pairs={{0,14},{2,0},{4,2},{6,4},{8,6},{10,8},{12,10},{14,12},{1,15},{3,1}... | collective-permute-start | bytes 626696 | tf_op jit(solution)/shard_map/ppermute | solution.py:238
  92.6 10.3 %copy-start.13 = (bf16[576,512]{1,0:T(8,128)(2,1)}, bf16[576,512]{1,0:T(8,128)(2,1)S(1)}, u32[]{:S(2)}) copy-start(bf16[576,512]{1,0:T(8,128)(2,1)S(1)} %collective-permute-done.13.s3) | copy-start | bytes 1769476
  93.5 14.9 %collective-permute-start.14 = (bf16[288,512]{1,0:T(8,128)(2,1)}, bf16[288,512]{1,0:T(8,128)(2,1)}, u32[]{:S(2)}, u32[]{:S(2)}) collective-permute-start(bf16[288,512]{1,0:T(8,128)(2,1)} %slice.76), channel_id=1, source_target_pairs={{96,0},{0,32},{32,64},{64,96},{97,1},{1,33},{33,65},{65,97},{98,2}... | collective-permute-start | bytes 884744 | tf_op jit(solution)/shard_map/ppermute | solution.py:243
  95.4 14.9 %copy-start.14 = (bf16[576,512]{1,0:T(8,128)(2,1)}, bf16[576,512]{1,0:T(8,128)(2,1)S(1)}, u32[]{:S(2)}) copy-start(bf16[576,512]{1,0:T(8,128)(2,1)S(1)} %collective-permute-done.12.s1) | copy-start | bytes 1769476
  95.4 14.9 %collective-permute-start.15 = (bf16[288,512]{1,0:T(8,128)(2,1)S(1)}, bf16[288,512]{1,0:T(8,128)(2,1)S(1)}, u32[]{:S(2)}, u32[]{:S(2)}) collective-permute-start(bf16[288,512]{1,0:T(8,128)(2,1)S(1)} %slice.77), channel_id=1, source_target_pairs={{32,0},{64,32},{96,64},{0,96},{33,1},{65,33},{97,65},{1,97},{34,2}... | collective-permute-start | bytes 884744 | tf_op jit(solution)/shard_map/ppermute | solution.py:243
  100.0 10.3 %collective-permute-start.11 = (bf16[48,2176]{1,0:T(8,128)(2,1)}, bf16[48,2176]{1,0:T(8,128)(2,1)}, u32[]{:S(2)}, u32[]{:S(2)}) collective-permute-start(bf16[48,2176]{1,0:T(8,128)(2,1)} %collective-permute-done.9.r3), channel_id=1, source_target_pairs={{0,2},{2,4},{4,6},{6,8},{8,10},{10,12},{12,14},{14,0},{1,3},{3,5},... | collective-permute-start | bytes 626696 | tf_op jit(solution)/shard_map/ppermute | solution.py:238
  103.6 18.0 %copy-start.22 = (bf16[32,896]{1,0:T(8,128)(2,1)S(1)}, bf16[32,896]{1,0:T(8,128)(2,1)}, u32[]{:S(2)}) copy-start(bf16[32,896]{1,0:T(8,128)(2,1)} %param.12) | copy-start | bytes 172036
  103.6 19.4 %copy-start.23 = (bf16[896]{0:T(1024)(128)(2,1)S(1)}, bf16[896]{0:T(1024)(128)(2,1)}, u32[]{:S(2)}) copy-start(bf16[896]{0:T(1024)(128)(2,1)} %param.13) | copy-start | bytes 5380
  116.6 6.6 %collective-permute-start.16 = (f32[192,640]{1,0:T(8,128)}, f32[192,640]{1,0:T(8,128)S(1)}, u32[]{:S(2)}, u32[]{:S(2)}) collective-permute-start(f32[192,640]{1,0:T(8,128)} %get-tuple-element.32), channel_id=1, source_target_pairs={{0,16},{16,0},{1,17},{17,1},{2,18},{18,2},{3,19},{19,3},{4,20},{20... | collective-permute-start | bytes 1474568 | tf_op jit(solution)/shard_map/ppermute | solution.py:294
  124.3 11.7 %copy-start.11 = (s32[4]{0:T(128)S(1)}, s32[4]{0:T(128)}, u32[]{:S(2)}) copy-start(s32[4]{0:T(128)} %pad_add_fusion.place) | copy-start | bytes 52
  124.3 11.7 %copy-start.12 = (f32[1,128]{1,0:T(1,128)S(1)}, f32[1,128]{1,0:T(1,128)}, u32[]{:S(2)}) copy-start(f32[1,128]{1,0:T(1,128)} %get-tuple-element.41.count) | copy-start | bytes 1540
  130.4 4.7 %collective-permute-start.17 = (f32[192,1280]{1,0:T(8,128)}, f32[192,1280]{1,0:T(8,128)S(1)}, u32[]{:S(2)}, u32[]{:S(2)}) collective-permute-start(f32[192,1280]{1,0:T(8,128)} %get-tuple-element.36), channel_id=1, source_target_pairs={{0,16},{16,0},{1,17},{17,1},{2,18},{18,2},{3,19},{19,3},{4,20},{20... | collective-permute-start | bytes 2949128 | tf_op jit(solution)/shard_map/ppermute | solution.py:313
  134.0 10.2 %copy-start.1 = (bf16[2,128,192]{2,1,0:T(8,128)(2,1)}, bf16[2,128,192]{2,1,0:T(8,128)(2,1)S(1)}, u32[]{:S(2)}) copy-start(bf16[2,128,192]{2,1,0:T(8,128)(2,1)S(1)} %fusion.7.signs) | copy-start | bytes 294916
  145.4 15.7 %all-to-all-start = ((f32[32,1,512]{2,1,0:T(1,128)}), f32[32,1,512]{2,1,0:T(1,128)S(1)}, u32[]{:S(2)}, u32[]{:S(2)}) async-start(f32[32,1,512]{2,1,0:T(1,128)} %copy-done.8), calls=%async_computation | async-start | bytes 131072 | tf_op jit(solution)/shard_map/all_to_all | solution.py:322
  184.6 10.8 %all-to-all-start.2 = ((f32[16,2,128]{2,1,0:T(2,128)}), f32[16,2,128]{2,1,0:T(2,128)S(1)}, u32[]{:S(2)}, u32[]{:S(2)}) async-start(f32[16,2,128]{2,1,0:T(2,128)} %broadcast_in_dim.10), calls=%async_computation.2 | async-start | bytes 32768 | tf_op jit(solution)/shard_map/all_to_all | solution.py:338
  (13 other events, 27.5 us)
Sparse Core Ops, SparseCore 0:
  11.0 101.7 all-gather.1
